TPU v7x, 32 devices: a whole 2x2x4 slice. The times are simulated.
32 devices in a mesh: blk: 16 (over z, y, x), rep: 2 (over core).
Axes of the slice: x: 2, y: 2, z: 4, core: 2. Of those that a mesh axis runs over, the one named last changes fastest.
Arguments:
- hidden_pre: bfloat16 [2048, 1024], P('blk'), may hold values from -6 to 6
- adj_vals: bfloat16 [16, 16, 128, 128], P('blk', 'rep'), may hold values from -0.125 to 0.125
- adj_cols: int32 [16, 16], P('blk', 'rep'), may hold values from 0 to 15, as said below
- w_out: bfloat16 [1024, 1024], replicated, may hold values from -0.1875 to 0.1875
- cotangent: bfloat16 [2048, 1024], P('blk'), may hold values from -6 to 6
Outputs:
- aggregated: bfloat16 [2048, 1024], P('blk', 'rep')
- grad_weight: float32 [1024, 1024], P('blk', 'rep')
- grad_pre: bfloat16 [2048, 1024], P('blk', 'rep')
Inputs may be any that keep to these rules, and one draw needn't show every extreme that they name: For block-row i, let b = i // 1 and, for slot k, s = (b - adj_cols[i, k]) mod (16). Then s // 8 == k // 8, and the slots of one block-row with equal k // 8 have distinct s.
All inputs are finite; a program needn't handle non-finite values.
Results may differ from a plain program's by a relative error of at most 0.014.
Values may be sent and summed in bfloat16 or wider, within the bound.
No kernel may reach another device: no remote copies, remote signals or barrier semaphores. Data moves between devices by JAX's collectives and lax.ppermute only.
A program may use at most 64 MiB of HBM per device.

v0:
```python
import jax
import jax.numpy as jnp
from jax import lax
from jax.sharding import PartitionSpec as P


def passed_along(value, axis, steps):
    count = lax.axis_size(axis)
    pairs = [(source, (source + steps) % count) for source in range(count)]
    return lax.ppermute(value, axis, pairs)


def spread_into(matches, contribution):
    return jnp.sum(
        jnp.where(matches[:, :, :, None, None], contribution[:, :, None], 0.0), axis=(0, 1)
    )


def shards(hidden_pre, adj_vals, adj_cols, w_out, cotangent):
    row_count, feature_width = hidden_pre.shape
    row_blocks = adj_vals.shape[0]
    tile_size = adj_vals.shape[2]
    blk_count = lax.axis_size("blk")
    rep_count = lax.axis_size("rep")
    section_span = blk_count // rep_count
    bit_total = (rep_count - 1).bit_length()
    blk_pos = lax.axis_index("blk")
    rep_pos = lax.axis_index("rep")
    cols_here = feature_width // rep_count
    owners = adj_cols // row_blocks
    within = jnp.mod(blk_pos - owners, blk_count) - rep_pos * section_span
    inside = adj_cols % row_blocks
    block_range = jnp.arange(row_blocks, dtype=jnp.int32)
    zero_out = jnp.zeros((row_blocks, tile_size, feature_width), jnp.float32)
    w_columns = lax.dynamic_slice_in_dim(w_out, rep_pos * cols_here, cols_here, 1)

    def pick_mask(turn_index):
        return (within == turn_index)[:, :, None] & (
            inside[:, :, None] == block_range[None, None, :]
        )

    hidden_act = jnp.maximum(hidden_pre, 0)
    partial_value = jnp.dot(hidden_act, w_columns, preferred_element_type=jnp.float32).astype(
        jnp.bfloat16
    )
    projected = lax.all_gather(partial_value, "rep", axis=1, tiled=True)
    visiting = projected
    for bit_index in range(bit_total):
        shifted = passed_along(visiting, "blk", section_span << bit_index)
        visiting = jnp.where(rep_pos >> bit_index & 1 == 1, shifted, visiting)

    def forward_turn(current, turn_index):
        selector = pick_mask(turn_index).astype(jnp.bfloat16)
        blocks = current.reshape(row_blocks, tile_size, feature_width)
        picked = jnp.einsum(
            "jkq,qtd->jktd", selector, blocks, preferred_element_type=jnp.float32
        ).astype(jnp.bfloat16)
        return jnp.einsum("jkab,jkbd->jad", adj_vals, picked, preferred_element_type=jnp.float32)

    def forward_step(carry, turn_index):
        current, output_sum = carry
        output_sum = output_sum + forward_turn(current, turn_index)
        kept_rows = None
        current = passed_along(current, "blk", 1)
        return ((current, output_sum), kept_rows)

    (final_rows, output_sum), kept_rows = lax.scan(
        forward_step, (visiting, zero_out), jnp.arange(section_span - 1, dtype=jnp.int32)
    )
    output_sum = output_sum + forward_turn(final_rows, section_span - 1)
    out_part = lax.psum_scatter(
        output_sum.reshape(row_count, feature_width).astype(jnp.bfloat16),
        "rep",
        scatter_dimension=1,
        tiled=True,
    )
    grad_block = cotangent.reshape(row_blocks, tile_size, feature_width)
    contribution = jnp.einsum(
        "jkab,jad->jkbd", adj_vals, grad_block, preferred_element_type=jnp.float32
    )

    def carry_step(carried, turn_index):
        carried = carried + spread_into(pick_mask(section_span - 1 - turn_index), contribution)
        return (passed_along(carried, "blk", -1), None)

    carried, ignored = lax.scan(carry_step, zero_out, jnp.arange(section_span - 1, dtype=jnp.int32))
    carried = carried + spread_into(pick_mask(0), contribution)
    for bit_index in range(bit_total):
        shifted = passed_along(
            carried.astype(jnp.bfloat16), "blk", -(section_span << bit_index)
        ).astype(carried.dtype)
        carried = jnp.where(rep_pos >> bit_index & 1 == 1, shifted, carried)
    back_part = lax.psum_scatter(
        carried.reshape(row_count, feature_width), "rep", scatter_dimension=1, tiled=True
    )
    back_grad = back_part.astype(jnp.bfloat16)
    grad_weight = lax.psum_scatter(
        lax.dot_general(
            hidden_act, back_grad, (((0,), (0,)), ((), ())), preferred_element_type=jnp.float32
        ),
        "blk",
        scatter_dimension=0,
        tiled=True,
    )
    back_full = lax.all_gather(back_grad, "rep", axis=1, tiled=True)
    w_rows = lax.dynamic_slice_in_dim(w_out, rep_pos * cols_here, cols_here, 0)
    grad_in = lax.dot_general(
        back_full, w_rows, (((1,), (1,)), ((), ())), preferred_element_type=jnp.float32
    )
    pre_part = lax.dynamic_slice_in_dim(hidden_pre, rep_pos * cols_here, cols_here, 1)
    grad_pre = jnp.where(pre_part > 0, grad_in, 0.0).astype(jnp.bfloat16)
    return (out_part, grad_weight, grad_pre)


def solution(mesh):
    placed = (P("blk", None), P("blk", "rep", None, None), P("blk", "rep"), P(), P("blk", None))
    return jax.shard_map(
        shards,
        mesh=mesh,
        in_specs=placed,
        out_specs=(P("blk", "rep"), P("blk", "rep"), P("blk", "rep")),
        check_vma=False,
    )
```

profile of v0, /device:TPU:0, one launch (start us, length us, event | category | flops | bytes accessed | tf_op | source)
XLA Modules:
  0.0 335.0 jit_solution(15477481968386906016)
XLA Ops:
  12.1 3.9 %collective-permute-start.2 = (bf16[128,1024]{1,0:T(8,128)(2,1)S(1)}, bf16[128,1024]{1,0:T(8,128)(2,1)}, u32[]{:S(2)}, u32[]{:S(2)}) collective-permute-start(bf16[128,1024]{1,0:T(8,128)(2,1)S(1)} %all_gather.6), channel_id=1, source_target_pairs={{0,16},{2,18},{4,20},{6,22},{8,24},{10,26},{12,28},{14,30},{16,0},... | collective-permute-start | bytes 786440 | tf_op jit(solution)/shard_map/ppermute | solution.py:10
  16.7 4.6 %select_reduce_fusion.1 = (f32[128,1024]{1,0:T(8,128)}, f32[8,128,1024]{2,1,0:T(8,128)}) fusion(pred[8]{0:T(512)(128)(4,1)S(1)} %get-tuple-element.161, bf16[128,1024]{1,0:T(8,128)(2,1)} %param.13, bf16[1,8,128,128]{3,2,1,0:T(8,128)(2,1)} %param.10), kind=kOutput, calls=%fused_computation.12 | convolution fusion | flops 270401536 | bytes 5242888 | tf_op jit(solution)/shard_map/jkab,jad->jkbd/dot_general | solution.py:78
  21.3 132.4 %while.25 = (s32[]{:T(128)}, f32[1,128,1024]{2,1,0:T(8,128)S(1)}, s32[7]{0:T(128)S(1)}, s32[1,8]{1,0:T(1,128)S(1)}, f32[1,8,128,1024]{3,2,1,0:T(8,128)}, /*index=5*/s32[]{:T(128)}, s32[1]{0:T(128)}) while((s32[]{:T(128)}, f32[1,128,1024]{2,1,0:T(8,128)S(1)}, s32[7]{0:T(128)S(1)}, s32[1,8]{1,0:T(1,128)S(1)}, f32[1,8,128,1024]{3,2,1,0:T(8,128)}, ...), condition=%wide.region_5.6_spmd, body=%wide.region_3.5_spmd.sunk | while | flops 2097163 | bytes 8388801 | solution.py:86
  22.6 2.8 select_reduce_fusion.3
  25.5 3.3 collective-permute-start
  28.8 11.2 %collective-permute-done = f32[1,128,1024]{2,1,0:T(8,128)S(1)} collective-permute-done((f32[1,128,1024]{2,1,0:T(8,128)S(1)}, f32[1,128,1024]{2,1,0:T(8,128)S(1)}, u32[]{:S(2)}, u32[]{:S(2)}) %collective-permute-start) | collective-permute-done | bytes 524320 | tf_op jit(solution)/shard_map/while/body/eval_jaxpr/ppermute | solution.py:10
  41.2 2.8 select_reduce_fusion.3
  44.1 6.1 %collective-permute-start = (f32[1,128,1024]{2,1,0:T(8,128)S(1)}, f32[1,128,1024]{2,1,0:T(8,128)S(1)}, u32[]{:S(2)}, u32[]{:S(2)}) collective-permute-start(f32[1,128,1024]{2,1,0:T(8,128)S(1)} %bitcast_add_fusion.3), channel_id=1, source_target_pairs={{0,30},{2,0},{4,2},{6,4},{8,6},{10,8},{12,10},{14,12},{16,14},{18,... | collective-permute-start | bytes 1572872 | tf_op jit(solution)/shard_map/while/body/eval_jaxpr/ppermute | solution.py:10
  50.3 10.3 %collective-permute-done = f32[1,128,1024]{2,1,0:T(8,128)S(1)} collective-permute-done((f32[1,128,1024]{2,1,0:T(8,128)S(1)}, f32[1,128,1024]{2,1,0:T(8,128)S(1)}, u32[]{:S(2)}, u32[]{:S(2)}) %collective-permute-start) | collective-permute-done | bytes 524320 | tf_op jit(solution)/shard_map/while/body/eval_jaxpr/ppermute | solution.py:10
  61.9 2.8 select_reduce_fusion.3
  64.7 6.1 %collective-permute-start = (f32[1,128,1024]{2,1,0:T(8,128)S(1)}, f32[1,128,1024]{2,1,0:T(8,128)S(1)}, u32[]{:S(2)}, u32[]{:S(2)}) collective-permute-start(f32[1,128,1024]{2,1,0:T(8,128)S(1)} %bitcast_add_fusion.3), channel_id=1, source_target_pairs={{0,30},{2,0},{4,2},{6,4},{8,6},{10,8},{12,10},{14,12},{16,14},{18,... | collective-permute-start | bytes 1572872 | tf_op jit(solution)/shard_map/while/body/eval_jaxpr/ppermute | solution.py:10
  70.9 9.4 %collective-permute-done = f32[1,128,1024]{2,1,0:T(8,128)S(1)} collective-permute-done((f32[1,128,1024]{2,1,0:T(8,128)S(1)}, f32[1,128,1024]{2,1,0:T(8,128)S(1)}, u32[]{:S(2)}, u32[]{:S(2)}) %collective-permute-start) | collective-permute-done | bytes 524320 | tf_op jit(solution)/shard_map/while/body/eval_jaxpr/ppermute | solution.py:10
  81.6 2.8 select_reduce_fusion.3
  84.4 6.1 %collective-permute-start = (f32[1,128,1024]{2,1,0:T(8,128)S(1)}, f32[1,128,1024]{2,1,0:T(8,128)S(1)}, u32[]{:S(2)}, u32[]{:S(2)}) collective-permute-start(f32[1,128,1024]{2,1,0:T(8,128)S(1)} %bitcast_add_fusion.3), channel_id=1, source_target_pairs={{0,30},{2,0},{4,2},{6,4},{8,6},{10,8},{12,10},{14,12},{16,14},{18,... | collective-permute-start | bytes 1572872 | tf_op jit(solution)/shard_map/while/body/eval_jaxpr/ppermute | solution.py:10
  90.6 8.5 %collective-permute-done = f32[1,128,1024]{2,1,0:T(8,128)S(1)} collective-permute-done((f32[1,128,1024]{2,1,0:T(8,128)S(1)}, f32[1,128,1024]{2,1,0:T(8,128)S(1)}, u32[]{:S(2)}, u32[]{:S(2)}) %collective-permute-start) | collective-permute-done | bytes 524320 | tf_op jit(solution)/shard_map/while/body/eval_jaxpr/ppermute | solution.py:10
  103.2 6.1 %collective-permute-start = (f32[1,128,1024]{2,1,0:T(8,128)S(1)}, f32[1,128,1024]{2,1,0:T(8,128)S(1)}, u32[]{:S(2)}, u32[]{:S(2)}) collective-permute-start(f32[1,128,1024]{2,1,0:T(8,128)S(1)} %bitcast_add_fusion.3), channel_id=1, source_target_pairs={{0,30},{2,0},{4,2},{6,4},{8,6},{10,8},{12,10},{14,12},{16,14},{18,... | collective-permute-start | bytes 1572872 | tf_op jit(solution)/shard_map/while/body/eval_jaxpr/ppermute | solution.py:10
  109.4 7.6 %collective-permute-done = f32[1,128,1024]{2,1,0:T(8,128)S(1)} collective-permute-done((f32[1,128,1024]{2,1,0:T(8,128)S(1)}, f32[1,128,1024]{2,1,0:T(8,128)S(1)}, u32[]{:S(2)}, u32[]{:S(2)}) %collective-permute-start) | collective-permute-done | bytes 524320 | tf_op jit(solution)/shard_map/while/body/eval_jaxpr/ppermute | solution.py:10
  121.1 6.1 %collective-permute-start = (f32[1,128,1024]{2,1,0:T(8,128)S(1)}, f32[1,128,1024]{2,1,0:T(8,128)S(1)}, u32[]{:S(2)}, u32[]{:S(2)}) collective-permute-start(f32[1,128,1024]{2,1,0:T(8,128)S(1)} %bitcast_add_fusion.3), channel_id=1, source_target_pairs={{0,30},{2,0},{4,2},{6,4},{8,6},{10,8},{12,10},{14,12},{16,14},{18,... | collective-permute-start | bytes 1572872 | tf_op jit(solution)/shard_map/while/body/eval_jaxpr/ppermute | solution.py:10
  127.2 6.7 %collective-permute-done = f32[1,128,1024]{2,1,0:T(8,128)S(1)} collective-permute-done((f32[1,128,1024]{2,1,0:T(8,128)S(1)}, f32[1,128,1024]{2,1,0:T(8,128)S(1)}, u32[]{:S(2)}, u32[]{:S(2)}) %collective-permute-start) | collective-permute-done | bytes 524320 | tf_op jit(solution)/shard_map/while/body/eval_jaxpr/ppermute | solution.py:10
  135.2 2.8 select_reduce_fusion.3
  138.0 6.1 %collective-permute-start = (f32[1,128,1024]{2,1,0:T(8,128)S(1)}, f32[1,128,1024]{2,1,0:T(8,128)S(1)}, u32[]{:S(2)}, u32[]{:S(2)}) collective-permute-start(f32[1,128,1024]{2,1,0:T(8,128)S(1)} %bitcast_add_fusion.3), channel_id=1, source_target_pairs={{0,30},{2,0},{4,2},{6,4},{8,6},{10,8},{12,10},{14,12},{16,14},{18,... | collective-permute-start | bytes 1572872 | tf_op jit(solution)/shard_map/while/body/eval_jaxpr/ppermute | solution.py:10
  144.2 9.6 %collective-permute-done = f32[1,128,1024]{2,1,0:T(8,128)S(1)} collective-permute-done((f32[1,128,1024]{2,1,0:T(8,128)S(1)}, f32[1,128,1024]{2,1,0:T(8,128)S(1)}, u32[]{:S(2)}, u32[]{:S(2)}) %collective-permute-start) | collective-permute-done | bytes 524320 | tf_op jit(solution)/shard_map/while/body/eval_jaxpr/ppermute | solution.py:10
  155.2 7.1 %collective-permute-done.3 = bf16[1,128,1024]{2,1,0:T(8,128)(2,1)} collective-permute-done((bf16[1,128,1024]{2,1,0:T(8,128)(2,1)S(1)}, bf16[1,128,1024]{2,1,0:T(8,128)(2,1)}, u32[]{:S(2)}, u32[]{:S(2)}) %collective-permute-start.3) | collective-permute-done | bytes 262176 | tf_op jit(solution)/shard_map/ppermute | solution.py:10
  164.4 72.1 %while.26 = (s32[]{:T(128)}, bf16[128,1024]{0,1:T(8,128)(2,1)S(1)}, f32[1,128,1024]{1,2,0:T(8,128)}, s32[7]{0:T(128)S(1)}, s32[1,8]{1,0:T(1,128)S(1)}, /*index=5...) while((s32[]{:T(128)}, bf16[128,1024]{0,1:T(8,128)(2,1)S(1)}, f32[1,128,1024]{1,2,0:T(8,128)}, ...), condition=%wide.region_1.2_spmd.clone, body=%wide.region_0.1_spmd.clone.sunk | while | flops 270925856 | bytes 4194559 | solution.py:67
  168.3 7.8 %collective-permute-done.1 = bf16[128,1024]{0,1:T(8,128)(2,1)S(1)} collective-permute-done((bf16[128,1024]{0,1:T(8,128)(2,1)S(1)}, bf16[128,1024]{0,1:T(8,128)(2,1)S(1)}, u32[]{:S(2)}, u32[]{:S(2)}) %collective-permute-start.1) | collective-permute-done | bytes 262176 | tf_op jit(solution)/shard_map/while/body/eval_jaxpr/ppermute | solution.py:10
  180.1 6.2 %collective-permute-done.1 = bf16[128,1024]{0,1:T(8,128)(2,1)S(1)} collective-permute-done((bf16[128,1024]{0,1:T(8,128)(2,1)S(1)}, bf16[128,1024]{0,1:T(8,128)(2,1)S(1)}, u32[]{:S(2)}, u32[]{:S(2)}) %collective-permute-start.1) | collective-permute-done | bytes 262176 | tf_op jit(solution)/shard_map/while/body/eval_jaxpr/ppermute | solution.py:10
  190.3 6.0 %collective-permute-done.1 = bf16[128,1024]{0,1:T(8,128)(2,1)S(1)} collective-permute-done((bf16[128,1024]{0,1:T(8,128)(2,1)S(1)}, bf16[128,1024]{0,1:T(8,128)(2,1)S(1)}, u32[]{:S(2)}, u32[]{:S(2)}) %collective-permute-start.1) | collective-permute-done | bytes 262176 | tf_op jit(solution)/shard_map/while/body/eval_jaxpr/ppermute | solution.py:10
  200.4 6.0 %collective-permute-done.1 = bf16[128,1024]{0,1:T(8,128)(2,1)S(1)} collective-permute-done((bf16[128,1024]{0,1:T(8,128)(2,1)S(1)}, bf16[128,1024]{0,1:T(8,128)(2,1)S(1)}, u32[]{:S(2)}, u32[]{:S(2)}) %collective-permute-start.1) | collective-permute-done | bytes 262176 | tf_op jit(solution)/shard_map/while/body/eval_jaxpr/ppermute | solution.py:10
  210.4 6.0 %collective-permute-done.1 = bf16[128,1024]{0,1:T(8,128)(2,1)S(1)} collective-permute-done((bf16[128,1024]{0,1:T(8,128)(2,1)S(1)}, bf16[128,1024]{0,1:T(8,128)(2,1)S(1)}, u32[]{:S(2)}, u32[]{:S(2)}) %collective-permute-start.1) | collective-permute-done | bytes 262176 | tf_op jit(solution)/shard_map/while/body/eval_jaxpr/ppermute | solution.py:10
  220.5 6.0 %collective-permute-done.1 = bf16[128,1024]{0,1:T(8,128)(2,1)S(1)} collective-permute-done((bf16[128,1024]{0,1:T(8,128)(2,1)S(1)}, bf16[128,1024]{0,1:T(8,128)(2,1)S(1)}, u32[]{:S(2)}, u32[]{:S(2)}) %collective-permute-start.1) | collective-permute-done | bytes 262176 | tf_op jit(solution)/shard_map/while/body/eval_jaxpr/ppermute | solution.py:10
  230.5 6.0 %collective-permute-done.1 = bf16[128,1024]{0,1:T(8,128)(2,1)S(1)} collective-permute-done((bf16[128,1024]{0,1:T(8,128)(2,1)S(1)}, bf16[128,1024]{0,1:T(8,128)(2,1)S(1)}, u32[]{:S(2)}, u32[]{:S(2)}) %collective-permute-start.1) | collective-permute-done | bytes 262176 | tf_op jit(solution)/shard_map/while/body/eval_jaxpr/ppermute | solution.py:10
  248.6 79.9 %reduce-scatter.8.cloned.1.call-done = f32[64,512]{1,0:T(8,128)} async-done(((f32[1024,512]{1,0:T(8,128)}), f32[64,512]{1,0:T(8,128)}) %reduce-scatter.8.cloned.1.call-update) | async-done | bytes 131088 | tf_op jit(solution)/shard_map/reduce_scatter | solution.py:97
  (99 shorter events, 59.4 us)
Async XLA Ops:
  7.2 1.6 copy-start
  7.2 233.0 %reduce-scatter.6.cloned.1.call-start = ((), (), s32[]{:S(2)}) async-start(), calls=%async_computation.4 | async-start | bytes 786432 | tf_op jit(solution)/shard_map/reduce_scatter | solution.py:93
  12.1 142.8 %collective-permute-start.2 = (bf16[128,1024]{1,0:T(8,128)(2,1)S(1)}, bf16[128,1024]{1,0:T(8,128)(2,1)}, u32[]{:S(2)}, u32[]{:S(2)}) collective-permute-start(bf16[128,1024]{1,0:T(8,128)(2,1)S(1)} %all_gather.6), channel_id=1, source_target_pairs={{0,16},{2,18},{4,20},{6,22},{8,24},{10,26},{12,28},{14,30},{16,0},... | collective-permute-start | bytes 786440 | tf_op jit(solution)/shard_map/ppermute | solution.py:10
  25.5 14.5 %collective-permute-start = (f32[1,128,1024]{2,1,0:T(8,128)S(1)}, f32[1,128,1024]{2,1,0:T(8,128)S(1)}, u32[]{:S(2)}, u32[]{:S(2)}) collective-permute-start(f32[1,128,1024]{2,1,0:T(8,128)S(1)} %bitcast_add_fusion.3), channel_id=1, source_target_pairs={{0,30},{2,0},{4,2},{6,4},{8,6},{10,8},{12,10},{14,12},{16,14},{18,... | collective-permute-start | bytes 1572872 | tf_op jit(solution)/shard_map/while/body/eval_jaxpr/ppermute | solution.py:10
  44.1 16.5 %collective-permute-start = (f32[1,128,1024]{2,1,0:T(8,128)S(1)}, f32[1,128,1024]{2,1,0:T(8,128)S(1)}, u32[]{:S(2)}, u32[]{:S(2)}) collective-permute-start(f32[1,128,1024]{2,1,0:T(8,128)S(1)} %bitcast_add_fusion.3), channel_id=1, source_target_pairs={{0,30},{2,0},{4,2},{6,4},{8,6},{10,8},{12,10},{14,12},{16,14},{18,... | collective-permute-start | bytes 1572872 | tf_op jit(solution)/shard_map/while/body/eval_jaxpr/ppermute | solution.py:10
  64.7 15.6 %collective-permute-start = (f32[1,128,1024]{2,1,0:T(8,128)S(1)}, f32[1,128,1024]{2,1,0:T(8,128)S(1)}, u32[]{:S(2)}, u32[]{:S(2)}) collective-permute-start(f32[1,128,1024]{2,1,0:T(8,128)S(1)} %bitcast_add_fusion.3), channel_id=1, source_target_pairs={{0,30},{2,0},{4,2},{6,4},{8,6},{10,8},{12,10},{14,12},{16,14},{18,... | collective-permute-start | bytes 1572872 | tf_op jit(solution)/shard_map/while/body/eval_jaxpr/ppermute | solution.py:10
  84.4 14.6 %collective-permute-start = (f32[1,128,1024]{2,1,0:T(8,128)S(1)}, f32[1,128,1024]{2,1,0:T(8,128)S(1)}, u32[]{:S(2)}, u32[]{:S(2)}) collective-permute-start(f32[1,128,1024]{2,1,0:T(8,128)S(1)} %bitcast_add_fusion.3), channel_id=1, source_target_pairs={{0,30},{2,0},{4,2},{6,4},{8,6},{10,8},{12,10},{14,12},{16,14},{18,... | collective-permute-start | bytes 1572872 | tf_op jit(solution)/shard_map/while/body/eval_jaxpr/ppermute | solution.py:10
  103.2 13.7 %collective-permute-start = (f32[1,128,1024]{2,1,0:T(8,128)S(1)}, f32[1,128,1024]{2,1,0:T(8,128)S(1)}, u32[]{:S(2)}, u32[]{:S(2)}) collective-permute-start(f32[1,128,1024]{2,1,0:T(8,128)S(1)} %bitcast_add_fusion.3), channel_id=1, source_target_pairs={{0,30},{2,0},{4,2},{6,4},{8,6},{10,8},{12,10},{14,12},{16,14},{18,... | collective-permute-start | bytes 1572872 | tf_op jit(solution)/shard_map/while/body/eval_jaxpr/ppermute | solution.py:10
  121.1 12.8 %collective-permute-start = (f32[1,128,1024]{2,1,0:T(8,128)S(1)}, f32[1,128,1024]{2,1,0:T(8,128)S(1)}, u32[]{:S(2)}, u32[]{:S(2)}) collective-permute-start(f32[1,128,1024]{2,1,0:T(8,128)S(1)} %bitcast_add_fusion.3), channel_id=1, source_target_pairs={{0,30},{2,0},{4,2},{6,4},{8,6},{10,8},{12,10},{14,12},{16,14},{18,... | collective-permute-start | bytes 1572872 | tf_op jit(solution)/shard_map/while/body/eval_jaxpr/ppermute | solution.py:10
  138.0 15.7 %collective-permute-start = (f32[1,128,1024]{2,1,0:T(8,128)S(1)}, f32[1,128,1024]{2,1,0:T(8,128)S(1)}, u32[]{:S(2)}, u32[]{:S(2)}) collective-permute-start(f32[1,128,1024]{2,1,0:T(8,128)S(1)} %bitcast_add_fusion.3), channel_id=1, source_target_pairs={{0,30},{2,0},{4,2},{6,4},{8,6},{10,8},{12,10},{14,12},{16,14},{18,... | collective-permute-start | bytes 1572872 | tf_op jit(solution)/shard_map/while/body/eval_jaxpr/ppermute | solution.py:10
  154.8 7.4 %collective-permute-start.3 = (bf16[1,128,1024]{2,1,0:T(8,128)(2,1)S(1)}, bf16[1,128,1024]{2,1,0:T(8,128)(2,1)}, u32[]{:S(2)}, u32[]{:S(2)}) collective-permute-start(bf16[1,128,1024]{2,1,0:T(8,128)(2,1)S(1)} %fusion.19), channel_id=1, source_target_pairs={{0,16},{2,18},{4,20},{6,22},{8,24},{10,26},{12,28},{14,30},{16,0},... | collective-permute-start | bytes 786440 | tf_op jit(solution)/shard_map/ppermute | solution.py:10
  164.3 79.5 %reduce-scatter.4.cloned.1.call-start = ((), (), s32[]{:S(2)}) async-start(), calls=%async_computation.3 | async-start | bytes 393216 | tf_op jit(solution)/shard_map/reduce_scatter | solution.py:71
  164.4 11.6 %collective-permute-start.1 = (bf16[128,1024]{0,1:T(8,128)(2,1)S(1)}, bf16[128,1024]{0,1:T(8,128)(2,1)S(1)}, u32[]{:S(2)}, u32[]{:S(2)}) collective-permute-start(bf16[128,1024]{0,1:T(8,128)(2,1)S(1)} %copy.16), channel_id=1, source_target_pairs={{0,2},{2,4},{4,6},{6,8},{8,10},{10,12},{12,14},{14,16},{16,18},{18... | collective-permute-start | bytes 786440 | tf_op jit(solution)/shard_map/while/body/eval_jaxpr/ppermute | solution.py:10
  176.1 10.2 %collective-permute-start.1 = (bf16[128,1024]{0,1:T(8,128)(2,1)S(1)}, bf16[128,1024]{0,1:T(8,128)(2,1)S(1)}, u32[]{:S(2)}, u32[]{:S(2)}) collective-permute-start(bf16[128,1024]{0,1:T(8,128)(2,1)S(1)} %copy.16), channel_id=1, source_target_pairs={{0,2},{2,4},{4,6},{6,8},{8,10},{10,12},{12,14},{14,16},{16,18},{18... | collective-permute-start | bytes 786440 | tf_op jit(solution)/shard_map/while/body/eval_jaxpr/ppermute | solution.py:10
  186.3 10.0 %collective-permute-start.1 = (bf16[128,1024]{0,1:T(8,128)(2,1)S(1)}, bf16[128,1024]{0,1:T(8,128)(2,1)S(1)}, u32[]{:S(2)}, u32[]{:S(2)}) collective-permute-start(bf16[128,1024]{0,1:T(8,128)(2,1)S(1)} %copy.16), channel_id=1, source_target_pairs={{0,2},{2,4},{4,6},{6,8},{8,10},{10,12},{12,14},{14,16},{16,18},{18... | collective-permute-start | bytes 786440 | tf_op jit(solution)/shard_map/while/body/eval_jaxpr/ppermute | solution.py:10
  196.3 10.0 %collective-permute-start.1 = (bf16[128,1024]{0,1:T(8,128)(2,1)S(1)}, bf16[128,1024]{0,1:T(8,128)(2,1)S(1)}, u32[]{:S(2)}, u32[]{:S(2)}) collective-permute-start(bf16[128,1024]{0,1:T(8,128)(2,1)S(1)} %copy.16), channel_id=1, source_target_pairs={{0,2},{2,4},{4,6},{6,8},{8,10},{10,12},{12,14},{14,16},{16,18},{18... | collective-permute-start | bytes 786440 | tf_op jit(solution)/shard_map/while/body/eval_jaxpr/ppermute | solution.py:10
  206.4 10.0 %collective-permute-start.1 = (bf16[128,1024]{0,1:T(8,128)(2,1)S(1)}, bf16[128,1024]{0,1:T(8,128)(2,1)S(1)}, u32[]{:S(2)}, u32[]{:S(2)}) collective-permute-start(bf16[128,1024]{0,1:T(8,128)(2,1)S(1)} %copy.16), channel_id=1, source_target_pairs={{0,2},{2,4},{4,6},{6,8},{8,10},{10,12},{12,14},{14,16},{16,18},{18... | collective-permute-start | bytes 786440 | tf_op jit(solution)/shard_map/while/body/eval_jaxpr/ppermute | solution.py:10
  216.4 10.0 %collective-permute-start.1 = (bf16[128,1024]{0,1:T(8,128)(2,1)S(1)}, bf16[128,1024]{0,1:T(8,128)(2,1)S(1)}, u32[]{:S(2)}, u32[]{:S(2)}) collective-permute-start(bf16[128,1024]{0,1:T(8,128)(2,1)S(1)} %copy.16), channel_id=1, source_target_pairs={{0,2},{2,4},{4,6},{6,8},{8,10},{10,12},{12,14},{14,16},{16,18},{18... | collective-permute-start | bytes 786440 | tf_op jit(solution)/shard_map/while/body/eval_jaxpr/ppermute | solution.py:10
  226.5 10.0 %collective-permute-start.1 = (bf16[128,1024]{0,1:T(8,128)(2,1)S(1)}, bf16[128,1024]{0,1:T(8,128)(2,1)S(1)}, u32[]{:S(2)}, u32[]{:S(2)}) collective-permute-start(bf16[128,1024]{0,1:T(8,128)(2,1)S(1)} %copy.16), channel_id=1, source_target_pairs={{0,2},{2,4},{4,6},{6,8},{8,10},{10,12},{12,14},{14,16},{16,18},{18... | collective-permute-start | bytes 786440 | tf_op jit(solution)/shard_map/while/body/eval_jaxpr/ppermute | solution.py:10
  236.5 4.7 %copy-start.1 = (bf16[128,1024]{1,0:T(8,128)(2,1)S(1)}, bf16[128,1024]{1,0:T(8,128)(2,1)}, u32[]{:S(2)}) copy-start(bf16[128,1024]{1,0:T(8,128)(2,1)} %param.9) | copy-start | bytes 786436
  240.1 88.3 %reduce-scatter.8.cloned.1.call-start = ((), (), s32[]{:S(2)}) async-start(), calls=%async_computation.5 | async-start | bytes 2228224 | tf_op jit(solution)/shard_map/reduce_scatter | solution.py:97
Sparse Core Ops, SparseCore 0:
  164.4 9.8 reduce-scatter.5
  240.2 3.5 reduce-scatter.3
  246.6 81.7 reduce-scatter.7
where the time goes:
time: 336 us; the launch traced here: 335 us
  waiting for transfers between devices  195 us (58%)
  starting transfers between devices  44.6 us (13%)
  other arithmetic  31.7 us (9%)
  matrix products  29 us (9%)
  between operations  13.9 us (4%)
  local copies, waits for them, and re-layouts  11.7 us (3%)
  loops' own time  4.93 us (1%)
  blocking collectives  4.07 us (1%)
    ppermute x16, waiting for transfers between devices, passed_along(): return lax.ppermute(value, axis, pairs)  114 us
    reduce_scatter x1, waiting for transfers between devices, shards(): lax.psum_scatter(lax.dot_general(hidden_act, back_grad, (((0,), (0,)), ((...  79.9 us
    ppermute x16, starting transfers between devices, passed_along(): return lax.ppermute(value, axis, pairs)  44.5 us
    dot_general x8, matrix products, forward_turn(): jnp.einsum('jkab,jkbd->jad', adj_vals, picked, preferred_element_type=jnp...  20.3 us
    reduce_sum x7, other arithmetic, spread_into(): jnp.sum(jnp.where(matches[:, :, :, None, None], contribution[:, :, None],...  19.7 us
    dynamic_slice x14, local copies, waits for them, and re-layouts, shards(): lax.scan(forward_step, (visiting, zero_out), jnp.arange(section_span - 1,...  8.18 us
  transfers between devices with their start and end apart: 19, of which 17 were waited for; matrix products, arithmetic and copies ran while one was open for 20% of the time, Pallas kernels for 0%

commit v1 on v0

v1 whole, which is shorter than its diff:
```python
import jax
import jax.numpy as jnp
from jax import lax
from jax.sharding import PartitionSpec as P


def grid_of(blk_count, section_span):
    inner = 1 << ((blk_count.bit_length() - 1) // 2)
    while section_span % inner:
        inner //= 2
    return blk_count // inner, inner


def shards(hidden_pre, adj_vals, adj_cols, w_out, cotangent):
    feature_width = hidden_pre.shape[1]
    tile_size = adj_vals.shape[2]
    blk_count = lax.axis_size("blk")
    rep_count = lax.axis_size("rep")
    section_span = blk_count // rep_count
    outer, inner = grid_of(blk_count, section_span)
    per_core = section_span // inner
    blk_pos = lax.axis_index("blk")
    rep_pos = lax.axis_index("rep")
    outer_pos = blk_pos // inner
    inner_pos = blk_pos % inner
    cols_here = feature_width // rep_count
    rows_here = feature_width // blk_count
    bf16 = jnp.bfloat16

    def along_inner(value, steps):
        if steps % inner == 0:
            return value
        pairs = [
            (o * inner + i, o * inner + (i + steps) % inner)
            for o in range(outer)
            for i in range(inner)
        ]
        return lax.ppermute(value, "blk", pairs)

    def along_outer(value, steps):
        if steps % outer == 0:
            return value
        pairs = [
            (o * inner + i, (o + steps) % outer * inner + i)
            for o in range(outer)
            for i in range(inner)
        ]
        return lax.ppermute(value, "blk", pairs)

    def dot(lhs, rhs, dims):
        return lax.dot_general(lhs, rhs, (dims, ((), ())), preferred_element_type=jnp.float32)

    hidden_part = jnp.maximum(
        lax.dynamic_slice_in_dim(hidden_pre, rep_pos * cols_here, cols_here, 1), 0
    )
    grad_part = lax.dynamic_slice_in_dim(cotangent, rep_pos * cols_here, cols_here, 1)
    hidden_stack = jnp.concatenate([along_outer(hidden_part, e) for e in range(outer)], 0)

    within = jnp.mod(blk_pos - adj_cols[0], blk_count) - rep_pos * section_span
    hit = within[None, :] == jnp.arange(section_span, dtype=jnp.int32)[:, None]
    ordered = jnp.sum(
        jnp.where(hit[:, :, None, None], adj_vals[0][None].astype(jnp.float32), 0.0), axis=1
    ).astype(bf16)
    ordered = ordered.reshape(per_core, inner, tile_size, tile_size)
    received = jnp.stack([along_inner(ordered[:, t], -t) for t in range(inner)])
    grad_stack = jnp.concatenate([along_inner(grad_part, -t) for t in range(inner)], 0)
    everyone = lax.all_gather(received, "rep", axis=1)
    everyone = everyone.reshape(inner, outer, tile_size, tile_size)
    wrapped = (inner_pos + jnp.arange(inner, dtype=jnp.int32)) >= inner
    block = jnp.where(wrapped[:, None, None, None], jnp.roll(everyone, 1, 1), everyone)
    block = block.transpose(0, 2, 1, 3).reshape(inner * tile_size, outer * tile_size)

    mixed_t = dot(hidden_stack, block, ((0,), (1,))).astype(bf16)
    by_group = mixed_t.reshape(per_core, inner, rows_here, inner * tile_size)
    mixed_cols = 0.0
    for d in range(inner):
        piece = lax.dynamic_index_in_dim(by_group, (inner_pos + d) % inner, 1, keepdims=False)
        piece = jnp.roll(piece, -d * tile_size, 2)
        mixed_cols = mixed_cols + along_inner(piece, d).astype(jnp.float32)
    mixed_cols = mixed_cols.astype(bf16)
    mixed_rows = 0.0
    for t in range(inner):
        piece = mixed_t[:, t * tile_size : (t + 1) * tile_size]
        mixed_rows = mixed_rows + along_inner(piece, t).astype(jnp.float32)
    mixed_rows = mixed_rows.astype(bf16)

    back_stack = dot(block, grad_stack, ((0,), (0,))).astype(bf16)
    back_part = 0.0
    for e in range(outer):
        piece = back_stack[e * tile_size : (e + 1) * tile_size]
        back_part = back_part + along_outer(piece, -e).astype(jnp.float32)
    back_part = back_part.astype(bf16)

    mixed_cols = lax.all_gather(mixed_cols, "rep", axis=0, tiled=True)
    weight_part = dot(
        mixed_cols.reshape(outer * rows_here, inner * tile_size), grad_stack, ((1,), (0,))
    ).astype(bf16)
    weight_part = weight_part.reshape(outer, rows_here, cols_here)
    grad_weight = 0.0
    for e in range(outer):
        piece = lax.dynamic_index_in_dim(weight_part, (outer_pos + e) % outer, 0, keepdims=False)
        grad_weight = grad_weight + along_outer(piece, e).astype(jnp.float32)

    mixed_rows = lax.all_gather(mixed_rows, "rep", axis=0, tiled=True)
    w_columns = lax.dynamic_slice_in_dim(w_out, rep_pos * cols_here, cols_here, 1)
    out_part = dot(mixed_rows, w_columns, ((0,), (0,))).astype(bf16)

    back_full = lax.all_gather(back_part, "rep", axis=1, tiled=True)
    w_rows = lax.dynamic_slice_in_dim(w_out, rep_pos * cols_here, cols_here, 0)
    grad_in = dot(back_full, w_rows, ((1,), (1,)))
    pre_part = lax.dynamic_slice_in_dim(hidden_pre, rep_pos * cols_here, cols_here, 1)
    grad_pre = jnp.where(pre_part > 0, grad_in, 0.0).astype(bf16)
    return (out_part, grad_weight, grad_pre)


def solution(mesh):
    placed = (P("blk", None), P("blk", "rep", None, None), P("blk", "rep"), P(), P("blk", None))
    return jax.shard_map(
        shards,
        mesh=mesh,
        in_specs=placed,
        out_specs=(P("blk", "rep"), P("blk", "rep"), P("blk", "rep")),
        check_vma=False,
    )
```

time: 336 us -> 60.9 us (0.18)
  the two profiles are of different devices: /device:TPU:0 before, /device:TPU:27 now
where the time goes in v1:
time: 60.9 us; the launch traced here: 60.7 us
  starting transfers between devices  21.1 us (35%)
  waiting for transfers between devices  15.7 us (26%)
  blocking collectives  14.5 us (24%)
  other arithmetic  4.4 us (7%)
  matrix products  3.4 us (6%)
  between operations  0.94 us (2%)
  local copies, waits for them, and re-layouts  0.7 us (1%)
    ppermute x12, starting transfers between devices, along_inner(): return lax.ppermute(value, 'blk', pairs)  11.1 us
    ppermute x12, waiting for transfers between devices, along_inner(): return lax.ppermute(value, 'blk', pairs)  11 us
    ppermute x9, starting transfers between devices, along_outer(): return lax.ppermute(value, 'blk', pairs)  9.98 us
    all_gather x1, blocking collectives, shards(): everyone = lax.all_gather(received, 'rep', axis=1)  5.08 us
    ppermute x9, waiting for transfers between devices, along_outer(): return lax.ppermute(value, 'blk', pairs)  4.71 us
    all_gather x1, blocking collectives, shards(): back_full = lax.all_gather(back_part, 'rep', axis=1, tiled=True)  3.91 us
    dot_general x5, matrix products, dot(): lax.dot_general(lhs, rhs, (dims, ((), ())), preferred_element_type=jnp.fl...  3.4 us
    all_gather x1, blocking collectives, shards(): mixed_rows = lax.all_gather(mixed_rows, 'rep', axis=0, tiled=True)  2.83 us
  transfers between devices with their start and end apart: 21, of which 5 were waited for; matrix products, arithmetic and copies ran while one was open for 11% of the time, Pallas kernels for 0%

profile of v1, /device:TPU:27, one launch (start us, length us, event | category | flops | bytes accessed | tf_op | source)
XLA Modules:
  0.0 60.7 jit_solution(11437501079384219857)
XLA Ops:
  0.7 1.1 %dynamic-slice_maximum_fusion = bf16[128,512]{1,0:T(8,128)(2,1)S(1)} fusion(bf16[128,1024]{1,0:T(8,128)(2,1)} %param.5, s32[]{:T(128)S(6)} %select_n.95), kind=kLoop, calls=%fused_computation.40 | loop fusion | flops 262144 | bytes 262148 | tf_op jit(solution)/shard_map/max | solution.py:53
  2.0 1.0 %bitcast_convert_fusion = f32[8,128,128]{2,1,0:T(8,128)S(1)} fusion(bf16[1,8,128,128]{3,2,1,0:T(8,128)(2,1)} %param.6), kind=kLoop, calls=%fused_computation.28 | loop fusion | flops 131072 | bytes 786432 | tf_op jit(solution)/shard_map/jit(_where)/broadcast_in_dim | solution.py:62
  3.0 0.7 %fusion.23 = s32[8]{0:T(128)S(1)} fusion(s32[1,8]{1,0:T(1,128)} %param.7, s32[]{:T(128)S(6)} %mul.5, s32[]{:T(128)S(6)} %axis_index.25), kind=kLoop, calls=%fused_computation.56 | loop fusion | flops 104 | bytes 72 | tf_op jit(solution)/shard_map/eq | solution.py:60
  3.7 0.5 select_reduce_fusion
  4.3 1.3 %collective-permute-start.5 = (bf16[2,128,128]{2,1,0:T(8,128)(2,1)S(1)}, bf16[2,128,128]{2,1,0:T(8,128)(2,1)S(1)}, u32[]{:S(2)}, u32[]{:S(2)}) collective-permute-start(bf16[2,128,128]{2,1,0:T(8,128)(2,1)S(1)} %get-tuple-element.17), channel_id=1, source_target_pairs={{0,2},{2,4},{4,6},{6,0},{8,10},{10,12},{12,14},{14,8},{16,18},{18,... | collective-permute-start | bytes 196616 | tf_op jit(solution)/shard_map/ppermute | solution.py:38
  5.7 1.3 %collective-permute-start.3 = (bf16[2,128,128]{2,1,0:T(8,128)(2,1)S(1)}, bf16[2,128,128]{2,1,0:T(8,128)(2,1)S(1)}, u32[]{:S(2)}, u32[]{:S(2)}) collective-permute-start(bf16[2,128,128]{2,1,0:T(8,128)(2,1)S(1)} %get-tuple-element.16), channel_id=1, source_target_pairs={{0,6},{2,0},{4,2},{6,4},{8,14},{10,8},{12,10},{14,12},{16,22},{18,... | collective-permute-start | bytes 196616 | tf_op jit(solution)/shard_map/ppermute | solution.py:38
  7.1 0.6 %collective-permute-done.5 = bf16[2,128,128]{2,1,0:T(8,128)(2,1)S(1)} collective-permute-done((bf16[2,128,128]{2,1,0:T(8,128)(2,1)S(1)}, bf16[2,128,128]{2,1,0:T(8,128)(2,1)S(1)}, u32[]{:S(2)}, u32[]{:S(2)}) %collective-permute-start.5) | collective-permute-done | bytes 65568 | tf_op jit(solution)/shard_map/ppermute | solution.py:38
  7.7 3.0 %collective-permute-start = (bf16[128,512]{1,0:T(8,128)(2,1)S(1)}, bf16[128,512]{1,0:T(8,128)(2,1)S(1)}, u32[]{:S(2)}, u32[]{:S(2)}) collective-permute-start(bf16[128,512]{1,0:T(8,128)(2,1)S(1)} %dynamic-slice_maximum_fusion), channel_id=1, source_target_pairs={{0,8},{2,10},{4,12},{6,14},{8,16},{10,18},{12,20},{14,22},{16,24},... | collective-permute-start | bytes 393224 | tf_op jit(solution)/shard_map/ppermute | solution.py:48
  10.8 2.1 %collective-permute-start.14 = (bf16[128,512]{1,0:T(8,128)(2,1)S(1)}, bf16[128,512]{1,0:T(8,128)(2,1)S(1)}, u32[]{:S(2)}, u32[]{:S(2)}) collective-permute-start(bf16[128,512]{1,0:T(8,128)(2,1)S(1)} %constant_dynamic-slice_fusion), channel_id=1, source_target_pairs={{0,2},{2,4},{4,6},{6,0},{8,10},{10,12},{12,14},{14,8},{16,18},{18,... | collective-permute-start | bytes 393224 | tf_op jit(solution)/shard_map/ppermute | solution.py:38
  13.2 5.1 %all-gather = bf16[4,4,128,128]{3,2,1,0:T(8,128)(2,1)S(1)} all-gather(bf16[4,2,128,128]{3,2,1,0:T(8,128)(2,1)S(1)} %pad_maximum_fusion.1), channel_id=2, replica_groups=mesh['blk'=16,'rep'=2] {'rep'}, dimensions={1}, use_global_device_ids=true | all-gather | bytes 786432 | tf_op jit(solution)/shard_map/all_gather | solution.py:67
  18.4 0.4 copy.20
  18.8 0.5 collective-permute-start.12
  19.3 0.5 convolution_convert_fusion.1
  20.0 2.1 %collective-permute-start.8 = (bf16[512,128]{1,0:T(8,128)(2,1)S(1)}, bf16[512,128]{1,0:T(8,128)(2,1)S(1)}, u32[]{:S(2)}, u32[]{:S(2)}) collective-permute-start(bf16[512,128]{1,0:T(8,128)(2,1)S(1)} %get-tuple-element.10), channel_id=1, source_target_pairs={{0,6},{2,0},{4,2},{6,4},{8,14},{10,8},{12,10},{14,12},{16,22},{18,... | collective-permute-start | bytes 393224 | tf_op jit(solution)/shard_map/ppermute | solution.py:38
  22.4 0.5 collective-permute-start.11
  22.8 0.9 %collective-permute-start.10 = (bf16[2,64,512]{2,1,0:T(8,128)(2,1)S(1)}, bf16[2,64,512]{2,1,0:T(8,128)(2,1)S(1)}, u32[]{:S(2)}, u32[]{:S(2)}) collective-permute-start(bf16[2,64,512]{2,1,0:T(8,128)(2,1)S(1)} %pad_maximum_fusion.3), channel_id=1, source_target_pairs={{0,4},{2,6},{4,0},{6,2},{8,12},{10,14},{12,8},{14,10},{16,20},{18,... | collective-permute-start | bytes 393224 | tf_op jit(solution)/shard_map/ppermute | solution.py:38
  23.8 0.7 %collective-permute-done.12 = bf16[128,512]{1,0:T(8,128)(2,1)S(1)} collective-permute-done((bf16[128,512]{1,0:T(8,128)(2,1)S(1)}, bf16[128,512]{1,0:T(8,128)(2,1)S(1)}, u32[]{:S(2)}, u32[]{:S(2)}) %collective-permute-start.12) | collective-permute-done | bytes 131104 | tf_op jit(solution)/shard_map/ppermute | solution.py:38
  24.5 1.5 %collective-permute-start.9 = (bf16[2,64,512]{2,1,0:T(8,128)(2,1)S(1)}, bf16[2,64,512]{2,1,0:T(8,128)(2,1)S(1)}, u32[]{:S(2)}, u32[]{:S(2)}) collective-permute-start(bf16[2,64,512]{2,1,0:T(8,128)(2,1)S(1)} %pad_maximum_fusion.2), channel_id=1, source_target_pairs={{0,2},{2,4},{4,6},{6,0},{8,10},{10,12},{12,14},{14,8},{16,18},{18,... | collective-permute-start | bytes 393224 | tf_op jit(solution)/shard_map/ppermute | solution.py:38
  26.0 0.5 convolution_convert_fusion
  26.6 3.6 %collective-permute-done.11 = bf16[2,64,512]{2,1,0:T(8,128)(2,1)S(1)} collective-permute-done((bf16[2,64,512]{2,1,0:T(8,128)(2,1)S(1)}, bf16[2,64,512]{2,1,0:T(8,128)(2,1)S(1)}, u32[]{:S(2)}, u32[]{:S(2)}) %collective-permute-start.11) | collective-permute-done | bytes 131104 | tf_op jit(solution)/shard_map/ppermute | solution.py:38
  30.5 5.9 %collective-permute-done.10 = bf16[2,64,512]{2,1,0:T(8,128)(2,1)S(1)} collective-permute-done((bf16[2,64,512]{2,1,0:T(8,128)(2,1)S(1)}, bf16[2,64,512]{2,1,0:T(8,128)(2,1)S(1)}, u32[]{:S(2)}, u32[]{:S(2)}) %collective-permute-start.10) | collective-permute-done | bytes 131104 | tf_op jit(solution)/shard_map/ppermute | solution.py:38
  36.4 1.1 %collective-permute-start.20 = (bf16[128,512]{1,0:T(8,128)(2,1)S(1)}, bf16[128,512]{1,0:T(8,128)(2,1)S(1)}, u32[]{:S(2)}, u32[]{:S(2)}) collective-permute-start(bf16[128,512]{1,0:T(8,128)(2,1)S(1)} %get-tuple-element.4), channel_id=1, source_target_pairs={{0,8},{2,10},{4,12},{6,14},{8,16},{10,18},{12,20},{14,22},{16,24},... | collective-permute-start | bytes 393224 | tf_op jit(solution)/shard_map/ppermute | solution.py:48
  37.5 2.0 %collective-permute-start.19 = (bf16[128,512]{1,0:T(8,128)(2,1)S(1)}, bf16[128,512]{1,0:T(8,128)(2,1)S(1)}, u32[]{:S(2)}, u32[]{:S(2)}) collective-permute-start(bf16[128,512]{1,0:T(8,128)(2,1)S(1)} %get-tuple-element.5), channel_id=1, source_target_pairs={{0,16},{2,18},{4,20},{6,22},{8,24},{10,26},{12,28},{14,30},{16,0},... | collective-permute-start | bytes 393224 | tf_op jit(solution)/shard_map/ppermute | solution.py:48
  39.6 2.7 %all_gather.18 = bf16[4,64,512]{2,1,0:T(8,128)(2,1)S(1)} all-gather(bf16[2,64,512]{2,1,0:T(8,128)(2,1)S(1)} %fusion.17), channel_id=1, replica_groups=mesh['blk'=16,'rep'=2] {'rep'}, dimensions={0}, use_global_device_ids=true | all-gather | bytes 393216 | tf_op jit(solution)/shard_map/all_gather | solution.py:94
  42.8 0.5 collective-permute-start.17
  43.3 2.9 %collective-permute-start.16 = (bf16[64,512]{1,0:T(8,128)(2,1)S(1)}, bf16[64,512]{1,0:T(8,128)(2,1)S(1)}, u32[]{:S(2)}, u32[]{:S(2)}) collective-permute-start(bf16[64,512]{1,0:T(8,128)(2,1)S(1)} %get-tuple-element.14), channel_id=1, source_target_pairs={{0,16},{2,18},{4,20},{6,22},{8,24},{10,26},{12,28},{14,30},{16,0},... | collective-permute-start | bytes 196616 | tf_op jit(solution)/shard_map/ppermute | solution.py:48
  46.3 2.8 %all_gather.17 = bf16[1024,128]{1,0:T(8,128)(2,1)S(1)} all-gather(bf16[512,128]{1,0:T(8,128)(2,1)S(1)} %add_convert_fusion.1), channel_id=1, replica_groups=mesh['blk'=16,'rep'=2] {'rep'}, dimensions={0}, use_global_device_ids=true | all-gather | bytes 393216 | tf_op jit(solution)/shard_map/all_gather | solution.py:104
  49.2 4.7 %collective-permute-done.19 = bf16[128,512]{1,0:T(8,128)(2,1)S(1)} collective-permute-done((bf16[128,512]{1,0:T(8,128)(2,1)S(1)}, bf16[128,512]{1,0:T(8,128)(2,1)S(1)}, u32[]{:S(2)}, u32[]{:S(2)}) %collective-permute-start.19) | collective-permute-done | bytes 131104 | tf_op jit(solution)/shard_map/ppermute | solution.py:48
  53.9 3.9 %all_gather.19 = bf16[128,1024]{1,0:T(8,128)(2,1)S(1)} all-gather(bf16[128,512]{1,0:T(8,128)(2,1)S(1)} %add_convert_fusion), channel_id=1, replica_groups=mesh['blk'=16,'rep'=2] {'rep'}, dimensions={1}, use_global_device_ids=true | all-gather | bytes 393216 | tf_op jit(solution)/shard_map/all_gather | solution.py:108
  57.8 1.0 %convolution_convert_fusion.3 = bf16[128,512]{1,0:T(8,128)(2,1)} fusion(bf16[1024,128]{1,0:T(8,128)(2,1)S(1)} %all_gather.17, bf16[1024,1024]{1,0:T(8,128)(2,1)S(1)} %copy-done, s32[]{:T(128)S(6)} %select_n.95), kind=kOutput, calls=%fused_computation.5 | convolution fusion | flops 134283264 | bytes 1441796 | tf_op jit(solution)/shard_map/dot_general | solution.py:51
  58.8 1.1 %fusion = bf16[128,512]{1,0:T(8,128)(2,1)} fusion(bf16[128,1024]{1,0:T(8,128)(2,1)S(1)} %all_gather.19, bf16[1024,1024]{1,0:T(8,128)(2,1)S(1)} %copy-done, s32[]{:T(128)S(6)} %select_n.95, bf16[128,1024]{1,0:T(8,128)(2,1)S(1)} %copy-done.1), kind=kOutput, calls=%fused_computation.6 | convolution fusion | flops 134545408 | bytes 1573888 | tf_op jit(solution)/shard_map/dot_general | solution.py:51
  60.0 0.7 %fusion.19 = f32[64,512]{1,0:T(8,128)} fusion(bf16[64,512]{1,0:T(8,128)(2,1)S(1)} %collective-permute-done.17, bf16[64,512]{1,0:T(8,128)(2,1)S(1)} %collective-permute-done.16, bf16[64,512]{1,0:T(8,128)(2,1)S(1)} %collective-permute-done.15, bf16[4,64,512]{2,1,0:T(8,128)(2,1)S(1)} %bitcast.65, s32[]{:T(128)S(6)} %select_n.110), kind=kLoop, calls=%fused_computation.36 | loop fusion | flops 229376 | bytes 393220 | tf_op jit(solution)/shard_map/add | solution.py:102
  (54 shorter events, 2.5 us)
Async XLA Ops:
  0.6 57.2 %copy-start = (bf16[1024,1024]{1,0:T(8,128)(2,1)S(1)}, bf16[1024,1024]{1,0:T(8,128)(2,1)}, u32[]{:S(2)}) copy-start(bf16[1024,1024]{1,0:T(8,128)(2,1)} %param.8) | copy-start | bytes 6291460
  0.6 6.4 %copy-start.2 = (bf16[128,1024]{1,0:T(8,128)(2,1)S(1)}, bf16[128,1024]{1,0:T(8,128)(2,1)}, u32[]{:S(2)}) copy-start(bf16[128,1024]{1,0:T(8,128)(2,1)} %param.9) | copy-start | bytes 786436
  1.8 17.1 %collective-permute-start.2 = (bf16[128,512]{1,0:T(8,128)(2,1)S(1)}, bf16[128,512]{1,0:T(8,128)(2,1)S(1)}, u32[]{:S(2)}, u32[]{:S(2)}) collective-permute-start(bf16[128,512]{1,0:T(8,128)(2,1)S(1)} %dynamic-slice_maximum_fusion), channel_id=1, source_target_pairs={{0,24},{2,26},{4,28},{6,30},{8,0},{10,2},{12,4},{14,6},{16,8},{18,... | collective-permute-start | bytes 393224 | tf_op jit(solution)/shard_map/ppermute | solution.py:48
  2.0 17.3 %collective-permute-start.1 = (bf16[128,512]{1,0:T(8,128)(2,1)S(1)}, bf16[128,512]{1,0:T(8,128)(2,1)S(1)}, u32[]{:S(2)}, u32[]{:S(2)}) collective-permute-start(bf16[128,512]{1,0:T(8,128)(2,1)S(1)} %dynamic-slice_maximum_fusion), channel_id=1, source_target_pairs={{0,16},{2,18},{4,20},{6,22},{8,24},{10,26},{12,28},{14,30},{16,0},... | collective-permute-start | bytes 393224 | tf_op jit(solution)/shard_map/ppermute | solution.py:48
  4.3 3.5 %collective-permute-start.5 = (bf16[2,128,128]{2,1,0:T(8,128)(2,1)S(1)}, bf16[2,128,128]{2,1,0:T(8,128)(2,1)S(1)}, u32[]{:S(2)}, u32[]{:S(2)}) collective-permute-start(bf16[2,128,128]{2,1,0:T(8,128)(2,1)S(1)} %get-tuple-element.17), channel_id=1, source_target_pairs={{0,2},{2,4},{4,6},{6,0},{8,10},{10,12},{12,14},{14,8},{16,18},{18,... | collective-permute-start | bytes 196616 | tf_op jit(solution)/shard_map/ppermute | solution.py:38
  5.5 5.2 %collective-permute-start.4 = (bf16[2,128,128]{2,1,0:T(8,128)(2,1)S(1)}, bf16[2,128,128]{2,1,0:T(8,128)(2,1)S(1)}, u32[]{:S(2)}, u32[]{:S(2)}) collective-permute-start(bf16[2,128,128]{2,1,0:T(8,128)(2,1)S(1)} %get-tuple-element.18), channel_id=1, source_target_pairs={{0,4},{2,6},{4,0},{6,2},{8,12},{10,14},{12,8},{14,10},{16,20},{18,... | collective-permute-start | bytes 196616 | tf_op jit(solution)/shard_map/ppermute | solution.py:38
  5.7 7.2 %collective-permute-start.3 = (bf16[2,128,128]{2,1,0:T(8,128)(2,1)S(1)}, bf16[2,128,128]{2,1,0:T(8,128)(2,1)S(1)}, u32[]{:S(2)}, u32[]{:S(2)}) collective-permute-start(bf16[2,128,128]{2,1,0:T(8,128)(2,1)S(1)} %get-tuple-element.16), channel_id=1, source_target_pairs={{0,6},{2,0},{4,2},{6,4},{8,14},{10,8},{12,10},{14,12},{16,22},{18,... | collective-permute-start | bytes 196616 | tf_op jit(solution)/shard_map/ppermute | solution.py:38
  7.7 11.6 %collective-permute-start = (bf16[128,512]{1,0:T(8,128)(2,1)S(1)}, bf16[128,512]{1,0:T(8,128)(2,1)S(1)}, u32[]{:S(2)}, u32[]{:S(2)}) collective-permute-start(bf16[128,512]{1,0:T(8,128)(2,1)S(1)} %dynamic-slice_maximum_fusion), channel_id=1, source_target_pairs={{0,8},{2,10},{4,12},{6,14},{8,16},{10,18},{12,20},{14,22},{16,24},... | collective-permute-start | bytes 393224 | tf_op jit(solution)/shard_map/ppermute | solution.py:48
  10.8 11.6 %collective-permute-start.14 = (bf16[128,512]{1,0:T(8,128)(2,1)S(1)}, bf16[128,512]{1,0:T(8,128)(2,1)S(1)}, u32[]{:S(2)}, u32[]{:S(2)}) collective-permute-start(bf16[128,512]{1,0:T(8,128)(2,1)S(1)} %constant_dynamic-slice_fusion), channel_id=1, source_target_pairs={{0,2},{2,4},{4,6},{6,0},{8,10},{10,12},{12,14},{14,8},{16,18},{18,... | collective-permute-start | bytes 393224 | tf_op jit(solution)/shard_map/ppermute | solution.py:38
  12.9 10.0 %collective-permute-start.13 = (bf16[128,512]{1,0:T(8,128)(2,1)S(1)}, bf16[128,512]{1,0:T(8,128)(2,1)S(1)}, u32[]{:S(2)}, u32[]{:S(2)}) collective-permute-start(bf16[128,512]{1,0:T(8,128)(2,1)S(1)} %constant_dynamic-slice_fusion), channel_id=1, source_target_pairs={{0,4},{2,6},{4,0},{6,2},{8,12},{10,14},{12,8},{14,10},{16,20},{18,... | collective-permute-start | bytes 393224 | tf_op jit(solution)/shard_map/ppermute | solution.py:38
  18.8 5.7 %collective-permute-start.12 = (bf16[128,512]{1,0:T(8,128)(2,1)S(1)}, bf16[128,512]{1,0:T(8,128)(2,1)S(1)}, u32[]{:S(2)}, u32[]{:S(2)}) collective-permute-start(bf16[128,512]{1,0:T(8,128)(2,1)S(1)} %constant_dynamic-slice_fusion), channel_id=1, source_target_pairs={{0,6},{2,0},{4,2},{6,4},{8,14},{10,8},{12,10},{14,12},{16,22},{18,... | collective-permute-start | bytes 393224 | tf_op jit(solution)/shard_map/ppermute | solution.py:38
  20.0 22.7 %collective-permute-start.8 = (bf16[512,128]{1,0:T(8,128)(2,1)S(1)}, bf16[512,128]{1,0:T(8,128)(2,1)S(1)}, u32[]{:S(2)}, u32[]{:S(2)}) collective-permute-start(bf16[512,128]{1,0:T(8,128)(2,1)S(1)} %get-tuple-element.10), channel_id=1, source_target_pairs={{0,6},{2,0},{4,2},{6,4},{8,14},{10,8},{12,10},{14,12},{16,22},{18,... | collective-permute-start | bytes 393224 | tf_op jit(solution)/shard_map/ppermute | solution.py:38
  22.0 20.8 %collective-permute-start.7 = (bf16[512,128]{1,0:T(8,128)(2,1)S(1)}, bf16[512,128]{1,0:T(8,128)(2,1)S(1)}, u32[]{:S(2)}, u32[]{:S(2)}) collective-permute-start(bf16[512,128]{1,0:T(8,128)(2,1)S(1)} %get-tuple-element.11), channel_id=1, source_target_pairs={{0,4},{2,6},{4,0},{6,2},{8,12},{10,14},{12,8},{14,10},{16,20},{18,... | collective-permute-start | bytes 393224 | tf_op jit(solution)/shard_map/ppermute | solution.py:38
  22.4 7.8 %collective-permute-start.11 = (bf16[2,64,512]{2,1,0:T(8,128)(2,1)S(1)}, bf16[2,64,512]{2,1,0:T(8,128)(2,1)S(1)}, u32[]{:S(2)}, u32[]{:S(2)}) collective-permute-start(bf16[2,64,512]{2,1,0:T(8,128)(2,1)S(1)} %pad_maximum_fusion.4), channel_id=1, source_target_pairs={{0,6},{2,0},{4,2},{6,4},{8,14},{10,8},{12,10},{14,12},{16,22},{18,... | collective-permute-start | bytes 393224 | tf_op jit(solution)/shard_map/ppermute | solution.py:38
  22.8 13.6 %collective-permute-start.10 = (bf16[2,64,512]{2,1,0:T(8,128)(2,1)S(1)}, bf16[2,64,512]{2,1,0:T(8,128)(2,1)S(1)}, u32[]{:S(2)}, u32[]{:S(2)}) collective-permute-start(bf16[2,64,512]{2,1,0:T(8,128)(2,1)S(1)} %pad_maximum_fusion.3), channel_id=1, source_target_pairs={{0,4},{2,6},{4,0},{6,2},{8,12},{10,14},{12,8},{14,10},{16,20},{18,... | collective-permute-start | bytes 393224 | tf_op jit(solution)/shard_map/ppermute | solution.py:38
  24.5 13.0 %collective-permute-start.9 = (bf16[2,64,512]{2,1,0:T(8,128)(2,1)S(1)}, bf16[2,64,512]{2,1,0:T(8,128)(2,1)S(1)}, u32[]{:S(2)}, u32[]{:S(2)}) collective-permute-start(bf16[2,64,512]{2,1,0:T(8,128)(2,1)S(1)} %pad_maximum_fusion.2), channel_id=1, source_target_pairs={{0,2},{2,4},{4,6},{6,0},{8,10},{10,12},{12,14},{14,8},{16,18},{18,... | collective-permute-start | bytes 393224 | tf_op jit(solution)/shard_map/ppermute | solution.py:38
  30.2 13.2 %collective-permute-start.6 = (bf16[512,128]{1,0:T(8,128)(2,1)S(1)}, bf16[512,128]{1,0:T(8,128)(2,1)S(1)}, u32[]{:S(2)}, u32[]{:S(2)}) collective-permute-start(bf16[512,128]{1,0:T(8,128)(2,1)S(1)} %get-tuple-element.9), channel_id=1, source_target_pairs={{0,2},{2,4},{4,6},{6,0},{8,10},{10,12},{12,14},{14,8},{16,18},{18,... | collective-permute-start | bytes 393224 | tf_op jit(solution)/shard_map/ppermute | solution.py:38
  36.4 12.7 %collective-permute-start.20 = (bf16[128,512]{1,0:T(8,128)(2,1)S(1)}, bf16[128,512]{1,0:T(8,128)(2,1)S(1)}, u32[]{:S(2)}, u32[]{:S(2)}) collective-permute-start(bf16[128,512]{1,0:T(8,128)(2,1)S(1)} %get-tuple-element.4), channel_id=1, source_target_pairs={{0,8},{2,10},{4,12},{6,14},{8,16},{10,18},{12,20},{14,22},{16,24},... | collective-permute-start | bytes 393224 | tf_op jit(solution)/shard_map/ppermute | solution.py:48
  37.5 16.3 %collective-permute-start.19 = (bf16[128,512]{1,0:T(8,128)(2,1)S(1)}, bf16[128,512]{1,0:T(8,128)(2,1)S(1)}, u32[]{:S(2)}, u32[]{:S(2)}) collective-permute-start(bf16[128,512]{1,0:T(8,128)(2,1)S(1)} %get-tuple-element.5), channel_id=1, source_target_pairs={{0,16},{2,18},{4,20},{6,22},{8,24},{10,26},{12,28},{14,30},{16,0},... | collective-permute-start | bytes 393224 | tf_op jit(solution)/shard_map/ppermute | solution.py:48
  42.6 16.3 %copy-start.1 = (bf16[128,1024]{1,0:T(8,128)(2,1)S(1)}, bf16[128,1024]{1,0:T(8,128)(2,1)}, u32[]{:S(2)}) copy-start(bf16[128,1024]{1,0:T(8,128)(2,1)} %param.5) | copy-start | bytes 786436
  42.6 11.2 %collective-permute-start.18 = (bf16[128,512]{1,0:T(8,128)(2,1)S(1)}, bf16[128,512]{1,0:T(8,128)(2,1)S(1)}, u32[]{:S(2)}, u32[]{:S(2)}) collective-permute-start(bf16[128,512]{1,0:T(8,128)(2,1)S(1)} %get-tuple-element.3), channel_id=1, source_target_pairs={{0,24},{2,26},{4,28},{6,30},{8,0},{10,2},{12,4},{14,6},{16,8},{18,... | collective-permute-start | bytes 393224 | tf_op jit(solution)/shard_map/ppermute | solution.py:48
  42.8 17.2 %collective-permute-start.17 = (bf16[64,512]{1,0:T(8,128)(2,1)S(1)}, bf16[64,512]{1,0:T(8,128)(2,1)S(1)}, u32[]{:S(2)}, u32[]{:S(2)}) collective-permute-start(bf16[64,512]{1,0:T(8,128)(2,1)S(1)} %get-tuple-element.13), channel_id=1, source_target_pairs={{0,24},{2,26},{4,28},{6,30},{8,0},{10,2},{12,4},{14,6},{16,8},{18,... | collective-permute-start | bytes 196616 | tf_op jit(solution)/shard_map/ppermute | solution.py:48
  43.3 16.7 %collective-permute-start.16 = (bf16[64,512]{1,0:T(8,128)(2,1)S(1)}, bf16[64,512]{1,0:T(8,128)(2,1)S(1)}, u32[]{:S(2)}, u32[]{:S(2)}) collective-permute-start(bf16[64,512]{1,0:T(8,128)(2,1)S(1)} %get-tuple-element.14), channel_id=1, source_target_pairs={{0,16},{2,18},{4,20},{6,22},{8,24},{10,26},{12,28},{14,30},{16,0},... | collective-permute-start | bytes 196616 | tf_op jit(solution)/shard_map/ppermute | solution.py:48
  49.2 10.8 %collective-permute-start.15 = (bf16[64,512]{1,0:T(8,128)(2,1)S(1)}, bf16[64,512]{1,0:T(8,128)(2,1)S(1)}, u32[]{:S(2)}, u32[]{:S(2)}) collective-permute-start(bf16[64,512]{1,0:T(8,128)(2,1)S(1)} %get-tuple-element.12), channel_id=1, source_target_pairs={{0,8},{2,10},{4,12},{6,14},{8,16},{10,18},{12,20},{14,22},{16,24},... | collective-permute-start | bytes 196616 | tf_op jit(solution)/shard_map/ppermute | solution.py:48

commit v2 on v1

v2 whole, which is shorter than its diff:
```python
import jax
import jax.numpy as jnp
from jax import lax
from jax.sharding import PartitionSpec as P


def grid_of(blk_count, section_span):
    inner = 1 << ((blk_count.bit_length() - 1) // 2)
    while section_span % inner:
        inner //= 2
    return blk_count // inner, inner


def shards(hidden_pre, adj_vals, adj_cols, w_out, cotangent):
    feature_width = hidden_pre.shape[1]
    tile_size = adj_vals.shape[2]
    blk_count = lax.axis_size("blk")
    rep_count = lax.axis_size("rep")
    section_span = blk_count // rep_count
    outer, inner = grid_of(blk_count, section_span)
    per_core = section_span // inner
    blk_pos = lax.axis_index("blk")
    rep_pos = lax.axis_index("rep")
    outer_pos = blk_pos // inner
    inner_pos = blk_pos % inner
    cols_here = feature_width // rep_count
    rows_here = feature_width // blk_count
    bf16 = jnp.bfloat16
    inner_groups = [[o * inner + i for i in range(inner)] for o in range(outer)]
    outer_groups = [[o * inner + i for o in range(outer)] for i in range(inner)]

    def swap_all(value, groups):
        return lax.all_to_all(value, "blk", 0, 0, axis_index_groups=groups)

    def dot(lhs, rhs, dims):
        return lax.dot_general(lhs, rhs, (dims, ((), ())), preferred_element_type=jnp.float32)

    hidden_part = jnp.maximum(
        lax.dynamic_slice_in_dim(hidden_pre, rep_pos * cols_here, cols_here, 1), 0
    )
    hidden_stack = swap_all(
        jnp.broadcast_to(hidden_part[None], (outer, tile_size, cols_here)), outer_groups
    ).reshape(outer * tile_size, cols_here)

    order = jnp.arange(section_span, dtype=jnp.int32).reshape(per_core, inner).T.reshape(-1)
    hit = (adj_cols[0] % section_span)[None, :] == order[:, None]
    ordered = jnp.sum(
        jnp.where(hit[:, :, None, None], adj_vals[0][None].astype(jnp.float32), 0.0), axis=1
    ).astype(bf16)
    ordered = ordered.reshape(inner, per_core, tile_size, tile_size).transpose(0, 2, 1, 3)
    ordered = ordered.reshape(inner, tile_size, per_core * tile_size)
    grad_part = lax.dynamic_slice_in_dim(cotangent, rep_pos * cols_here, cols_here, 1)
    grad_copies = jnp.broadcast_to(grad_part[None], (inner, tile_size, cols_here))
    arrived = swap_all(jnp.concatenate([ordered, grad_copies], 2), inner_groups)
    arrived = arrived.reshape(inner * tile_size, per_core * tile_size + cols_here)
    grad_stack = arrived[:, per_core * tile_size :]
    everyone = lax.all_gather(arrived[:, : per_core * tile_size], "rep", axis=0)

    row_block = outer_pos * inner + jnp.repeat(jnp.arange(inner, dtype=jnp.int32), tile_size)
    pieces = []
    for o in range(outer):
        column = o * inner + inner_pos
        group = jnp.mod(row_block - column, blk_count) // section_span
        m = o % per_core
        piece = everyone[0, :, m * tile_size : (m + 1) * tile_size]
        for r in range(1, rep_count):
            other = everyone[r, :, m * tile_size : (m + 1) * tile_size]
            piece = jnp.where((group == r)[:, None], other, piece)
        pieces.append(piece)
    block = jnp.concatenate(pieces, 1)

    back_stack = dot(block, grad_stack, ((0,), (0,))).astype(bf16)
    back_arrived = swap_all(back_stack.reshape(outer, tile_size, cols_here), outer_groups)

    mixed = dot(block, hidden_stack, ((1,), (0,))).astype(bf16)
    mixed_t = dot(hidden_stack, block, ((0,), (1,))).astype(bf16)
    by_group = mixed_t.reshape(per_core, inner, rows_here, inner * tile_size)
    by_group = by_group.transpose(1, 0, 2, 3).reshape(
        inner, per_core * rows_here, inner * tile_size
    )
    mixed_rows = swap_all(mixed.reshape(inner, tile_size, cols_here), inner_groups)
    mixed_cols = swap_all(by_group, inner_groups)
    mixed_rows = jnp.sum(mixed_rows.astype(jnp.float32), 0).astype(bf16)
    mixed_cols = jnp.sum(mixed_cols.astype(jnp.float32), 0).astype(bf16)

    mixed_cols = lax.all_gather(mixed_cols, "rep", axis=0, tiled=True)
    weight_part = dot(mixed_cols, grad_stack, ((1,), (0,))).astype(bf16)
    weight_arrived = swap_all(weight_part.reshape(outer, rows_here, cols_here), outer_groups)
    grad_weight = jnp.sum(weight_arrived.astype(jnp.float32), 0)

    mixed_rows = lax.all_gather(mixed_rows, "rep", axis=1, tiled=True)
    w_columns = lax.dynamic_slice_in_dim(w_out, rep_pos * cols_here, cols_here, 1)
    out_part = dot(mixed_rows, w_columns, ((1,), (0,))).astype(bf16)

    back_part = jnp.sum(back_arrived.astype(jnp.float32), 0).astype(bf16)
    back_full = lax.all_gather(back_part, "rep", axis=1, tiled=True)
    w_rows = lax.dynamic_slice_in_dim(w_out, rep_pos * cols_here, cols_here, 0)
    grad_in = dot(back_full, w_rows, ((1,), (1,)))
    pre_part = lax.dynamic_slice_in_dim(hidden_pre, rep_pos * cols_here, cols_here, 1)
    grad_pre = jnp.where(pre_part > 0, grad_in, 0.0).astype(bf16)
    return (out_part, grad_weight, grad_pre)


def solution(mesh):
    placed = (P("blk", None), P("blk", "rep", None, None), P("blk", "rep"), P(), P("blk", None))
    return jax.shard_map(
        shards,
        mesh=mesh,
        in_specs=placed,
        out_specs=(P("blk", "rep"), P("blk", "rep"), P("blk", "rep")),
        check_vma=False,
    )
```

time: 60.9 us -> 91.4 us (1.50)
  the two profiles are of different devices: /device:TPU:27 before, /device:TPU:0 now
where the time goes in v2:
time: 91.4 us; the launch traced here: 90.8 us
  waiting for transfers between devices  37.9 us (41%)
  starting transfers between devices  23.9 us (26%)
  matrix products  10.5 us (11%)
  blocking collectives  8.15 us (9%)
  other arithmetic  6.48 us (7%)
  local copies, waits for them, and re-layouts  3.02 us (3%)
    all_to_all x6, waiting for transfers between devices, swap_all(): return lax.all_to_all(value, 'blk', 0, 0, axis_index_groups=groups)  37.9 us
    all_to_all x6, starting transfers between devices, swap_all(): return lax.all_to_all(value, 'blk', 0, 0, axis_index_groups=groups)  23.9 us
    dot_general x6, matrix products, dot(): lax.dot_general(lhs, rhs, (dims, ((), ())), preferred_element_type=jnp.fl...  10.5 us
    all_gather x1, blocking collectives, shards(): everyone = lax.all_gather(arrived[:, :per_core * tile_size], 'rep', axis=0)  2.18 us
    all_gather x1, blocking collectives, shards(): back_full = lax.all_gather(back_part, 'rep', axis=1, tiled=True)  1.99 us
    all_gather x1, blocking collectives, shards(): mixed_rows = lax.all_gather(mixed_rows, 'rep', axis=1, tiled=True)  1.99 us
    all_gather x1, blocking collectives, shards(): mixed_cols = lax.all_gather(mixed_cols, 'rep', axis=0, tiled=True)  1.98 us
  transfers between devices with their start and end apart: 6, of which 6 were waited for; matrix products, arithmetic and copies ran while one was open for 13% of the time, Pallas kernels for 0%

profile of v2, /device:TPU:0, one launch (start us, length us, event | category | flops | bytes accessed | tf_op | source)
XLA Modules:
  0.0 90.8 jit_solution(9735475198447295182)
XLA Ops:
  0.7 0.8 fusion.23
  1.6 1.0 %bitcast_convert_fusion = f32[8,128,128]{2,1,0:T(8,128)S(1)} fusion(bf16[1,8,128,128]{3,2,1,0:T(8,128)(2,1)} %param.6), kind=kLoop, calls=%fused_computation.15 | loop fusion | flops 131072 | bytes 786432 | tf_op jit(solution)/shard_map/jit(_where)/broadcast_in_dim | solution.py:48
  2.7 0.5 select_reduce_fusion
  3.6 0.9 %pad_maximum_fusion = bf16[4,128,768]{2,1,0:T(8,128)(2,1)} fusion(bf16[4,128,512]{2,1,0:T(8,128)(2,1)S(1)} %broadcast_in_dim.80, bf16[4,128,256]{2,1,0:T(8,128)(2,1)S(1)} %copy.13), kind=kLoop, calls=%fused_computation.10 | loop fusion | flops 1572864 | bytes 1572864 | tf_op jit(solution)/shard_map/concatenate | solution.py:54
  4.6 5.2 %all-to-all-start = ((bf16[4,128,768]{2,1,0:T(8,128)(2,1)}), bf16[4,128,768]{2,1,0:T(8,128)(2,1)S(1)}, u32[]{:S(2)}, u32[]{:S(2)}) async-start(bf16[4,128,768]{2,1,0:T(8,128)(2,1)} %pad_maximum_fusion), calls=%async_computation | async-start | bytes 1572864 | tf_op jit(solution)/shard_map/all_to_all | solution.py:33
  9.8 10.8 %all-to-all-done = bf16[4,128,768]{2,1,0:T(8,128)(2,1)S(1)} async-done(((bf16[4,128,768]{2,1,0:T(8,128)(2,1)}), bf16[4,128,768]{2,1,0:T(8,128)(2,1)S(1)}, u32[]{:S(2)}, u32[]{:S(2)}) %all-to-all-start) | async-done | bytes 786464 | tf_op jit(solution)/shard_map/all_to_all | solution.py:33
  20.6 0.9 broadcast_in_dim.84
  21.5 4.9 %all-to-all-start.1 = ((bf16[4,128,512]{2,1,0:T(8,128)(2,1)}), bf16[4,128,512]{2,1,0:T(8,128)(2,1)S(1)}, u32[]{:S(2)}, u32[]{:S(2)}) async-start(bf16[4,128,512]{2,1,0:T(8,128)(2,1)} %broadcast_in_dim.84), calls=%async_computation.1 | async-start | bytes 1048576 | tf_op jit(solution)/shard_map/all_to_all | solution.py:33
  26.4 2.2 %all-gather = bf16[1024,256]{1,0:T(8,128)(2,1)S(1)} all-gather(bf16[512,256]{1,0:T(8,128)(2,1)S(1)} %slice.28), channel_id=2, replica_groups=mesh['blk'=16,'rep'=2] {'rep'}, dimensions={0}, use_global_device_ids=true | all-gather | bytes 786432 | tf_op jit(solution)/shard_map/all_gather | solution.py:57
  28.6 1.1 %broadcast_select_fusion.3 = (bf16[512,128]{1,0:T(8,128)(2,1)S(1)}, bf16[512,128]{1,0:T(8,128)(2,1)}, bf16[512,128]{1,0:T(8,128)(2,1)}, bf16[512,128]{1,0:T(8,128)(2,1)}) fusion(pred[512]{0:T(512)(128)(4,1)S(1)} %get-tuple-element.7, bf16[2,512,256]{2,1,0:T(8,128)(2,1)S(1)} %bitcast.72, pred[512]{0:T(512)(128)(4,1)S(1)} %get-tuple-element.10, ...), kind=kLoop, calls=%fused_computation.23 | loop fusion | flops 262144 | bytes 1050624 | tf_op jit(solution)/shard_map/jit(_where)/select_n | solution.py:68
  29.7 10.4 %all-to-all-done.1 = bf16[4,128,512]{2,1,0:T(8,128)(2,1)S(1)} async-done(((bf16[4,128,512]{2,1,0:T(8,128)(2,1)}), bf16[4,128,512]{2,1,0:T(8,128)(2,1)S(1)}, u32[]{:S(2)}, u32[]{:S(2)}) %all-to-all-start.1) | async-done | bytes 524320 | tf_op jit(solution)/shard_map/all_to_all | solution.py:33
  40.0 1.5 %convolution_convert_fusion.1 = bf16[512,512]{1,0:T(8,128)(2,1)S(1)} fusion(bf16[512,512]{1,0:T(8,128)(2,1)S(1)} %bitcast.78, bf16[512,128]{1,0:T(8,128)(2,1)} %get-tuple-element.4, bf16[512,128]{1,0:T(8,128)(2,1)} %get-tuple-element.6, bf16[512,128]{1,0:T(8,128)(2,1)} %get-tuple-element.5, bf16[512,128]{1,0:T(8,128)(2,1)S(1)} %get-tuple-element.3), kind=kOutput, calls=%fused_computation.2 | convolution fusion | flops 270794752 | bytes 1572864 | tf_op jit(solution)/shard_map/dot_general | solution.py:36
  41.6 0.8 copy.14
  42.4 3.5 %all-to-all-start.3 = ((bf16[4,128,512]{2,1,0:T(8,128)(2,1)}), bf16[4,128,512]{2,1,0:T(8,128)(2,1)S(1)}, u32[]{:S(2)}, u32[]{:S(2)}) async-start(bf16[4,128,512]{2,1,0:T(8,128)(2,1)} %bitcast.19), calls=%async_computation.3 | async-start | bytes 1048576 | tf_op jit(solution)/shard_map/all_to_all | solution.py:33
  45.9 2.3 %convolution_convert_fusion.2 = bf16[512,512]{1,0:T(8,128)(2,1)} fusion(bf16[512,512]{1,0:T(8,128)(2,1)S(1)} %bitcast.79, bf16[512,128]{1,0:T(8,128)(2,1)} %get-tuple-element.4, bf16[512,128]{1,0:T(8,128)(2,1)} %get-tuple-element.6, bf16[512,128]{1,0:T(8,128)(2,1)} %get-tuple-element.5, bf16[512,128]{1,0:T(8,128)(2,1)S(1)} %get-tuple-element.3), kind=kOutput, calls=%fused_computation.3 | convolution fusion | flops 270794752 | bytes 1572864 | tf_op jit(solution)/shard_map/dot_general | solution.py:36
  48.1 5.2 %all-to-all-done.3 = bf16[4,128,512]{2,1,0:T(8,128)(2,1)S(1)} async-done(((bf16[4,128,512]{2,1,0:T(8,128)(2,1)}), bf16[4,128,512]{2,1,0:T(8,128)(2,1)S(1)}, u32[]{:S(2)}, u32[]{:S(2)}) %all-to-all-start.3) | async-done | bytes 524320 | tf_op jit(solution)/shard_map/all_to_all | solution.py:33
  53.3 3.5 %all-to-all-start.2 = ((bf16[4,128,512]{2,1,0:T(8,128)(2,1)}), bf16[4,128,512]{2,1,0:T(8,128)(2,1)S(1)}, u32[]{:S(2)}, u32[]{:S(2)}) async-start(bf16[4,128,512]{2,1,0:T(8,128)(2,1)} %bitcast.81), calls=%async_computation.2 | async-start | bytes 1048576 | tf_op jit(solution)/shard_map/all_to_all | solution.py:33
  56.8 2.5 %convolution_convert_fusion = bf16[512,512]{1,0:T(8,128)(2,1)} fusion(bf16[512,768]{1,0:T(8,128)(2,1)} %bitcast.74, bf16[512,128]{1,0:T(8,128)(2,1)} %get-tuple-element.4, bf16[512,128]{1,0:T(8,128)(2,1)} %get-tuple-element.6, bf16[512,128]{1,0:T(8,128)(2,1)} %get-tuple-element.5, bf16[512,128]{1,0:T(8,128)(2,1)S(1)} %get-tuple-element.3), kind=kOutput, calls=%fused_computation.1 | convolution fusion | flops 270794752 | bytes 1572864 | tf_op jit(solution)/shard_map/dot_general | solution.py:36
  59.3 4.1 %all-to-all-done.2 = bf16[4,128,512]{2,1,0:T(8,128)(2,1)S(1)} async-done(((bf16[4,128,512]{2,1,0:T(8,128)(2,1)}), bf16[4,128,512]{2,1,0:T(8,128)(2,1)S(1)}, u32[]{:S(2)}, u32[]{:S(2)}) %all-to-all-start.2) | async-done | bytes 524320 | tf_op jit(solution)/shard_map/all_to_all | solution.py:33
  63.5 0.8 copy-done.1
  64.3 3.5 %all-to-all-start.5 = ((bf16[4,128,512]{2,1,0:T(8,128)(2,1)}), bf16[4,128,512]{2,1,0:T(8,128)(2,1)S(1)}, u32[]{:S(2)}, u32[]{:S(2)}) async-start(bf16[4,128,512]{2,1,0:T(8,128)(2,1)} %bitcast.80), calls=%async_computation.5 | async-start | bytes 1048576 | tf_op jit(solution)/shard_map/all_to_all | solution.py:33
  67.8 1.1 %reduce_sum.55 = bf16[128,512]{1,0:T(8,128)(2,1)S(1)} reduce(bf16[4,128,512]{2,1,0:T(8,128)(2,1)} %copy-done.1, bf16[]{:T(256)} %constant.123.clone.1), dimensions={0}, to_apply=%region_1.2 | reduce | flops 196608 | bytes 655362 | tf_op jit(solution)/shard_map/reduce_sum | solution.py:83
  69.0 2.0 %all_gather.17 = bf16[128,1024]{1,0:T(8,128)(2,1)S(1)} all-gather(bf16[128,512]{1,0:T(8,128)(2,1)S(1)} %reduce_sum.55), channel_id=1, replica_groups=mesh['blk'=16,'rep'=2] {'rep'}, dimensions={1}, use_global_device_ids=true | all-gather | bytes 393216 | tf_op jit(solution)/shard_map/all_gather | solution.py:91
  71.0 2.0 %all_gather.18 = bf16[256,512]{1,0:T(8,128)(2,1)S(1)} all-gather(bf16[128,512]{1,0:T(8,128)(2,1)S(1)} %reduce_sum.56), channel_id=1, replica_groups=mesh['blk'=16,'rep'=2] {'rep'}, dimensions={0}, use_global_device_ids=true | all-gather | bytes 393216 | tf_op jit(solution)/shard_map/all_gather | solution.py:86
  72.9 2.1 %convolution_convert_fusion.3 = bf16[256,512]{1,0:T(8,128)(2,1)} fusion(bf16[256,512]{1,0:T(8,128)(2,1)S(1)} %all_gather.18, bf16[512,768]{1,0:T(8,128)(2,1)} %bitcast.75), kind=kOutput, calls=%fused_computation.4 | convolution fusion | flops 134348800 | bytes 1048576 | tf_op jit(solution)/shard_map/dot_general | solution.py:36
  75.0 4.9 %all-to-all-done.5 = bf16[4,128,512]{2,1,0:T(8,128)(2,1)S(1)} async-done(((bf16[4,128,512]{2,1,0:T(8,128)(2,1)}), bf16[4,128,512]{2,1,0:T(8,128)(2,1)S(1)}, u32[]{:S(2)}, u32[]{:S(2)}) %all-to-all-start.5) | async-done | bytes 524320 | tf_op jit(solution)/shard_map/all_to_all | solution.py:33
  79.9 3.4 %all-to-all-start.4 = ((bf16[4,64,512]{2,1,0:T(8,128)(2,1)}), bf16[4,64,512]{2,1,0:T(8,128)(2,1)S(1)}, u32[]{:S(2)}, u32[]{:S(2)}) async-start(bf16[4,64,512]{2,1,0:T(8,128)(2,1)} %bitcast.20), calls=%async_computation.4 | async-start | bytes 524288 | tf_op jit(solution)/shard_map/all_to_all | solution.py:33
  83.3 1.0 %convolution_convert_fusion.4 = bf16[128,512]{1,0:T(8,128)(2,1)} fusion(bf16[128,1024]{1,0:T(8,128)(2,1)S(1)} %all_gather.17, bf16[1024,1024]{1,0:T(8,128)(2,1)S(1)} %copy-done, s32[]{:T(128)S(6)} %select_n.116), kind=kOutput, calls=%fused_computation.6 | convolution fusion | flops 134283264 | bytes 1441796 | tf_op jit(solution)/shard_map/dot_general | solution.py:36
  84.4 2.0 %all_gather.19 = bf16[128,1024]{1,0:T(8,128)(2,1)S(1)} all-gather(bf16[128,512]{1,0:T(8,128)(2,1)S(1)} %reduce_sum.58), channel_id=1, replica_groups=mesh['blk'=16,'rep'=2] {'rep'}, dimensions={1}, use_global_device_ids=true | all-gather | bytes 393216 | tf_op jit(solution)/shard_map/all_gather | solution.py:96
  86.4 1.1 %fusion = bf16[128,512]{1,0:T(8,128)(2,1)} fusion(bf16[128,1024]{1,0:T(8,128)(2,1)S(1)} %all_gather.19, bf16[1024,1024]{1,0:T(8,128)(2,1)S(1)} %copy-done, s32[]{:T(128)S(6)} %select_n.116, bf16[128,1024]{1,0:T(8,128)(2,1)S(1)} %copy-done.4), kind=kOutput, calls=%fused_computation.7 | convolution fusion | flops 134545408 | bytes 1573888 | tf_op jit(solution)/shard_map/dot_general | solution.py:36
  87.5 2.5 %all-to-all-done.4 = bf16[4,64,512]{2,1,0:T(8,128)(2,1)S(1)} async-done(((bf16[4,64,512]{2,1,0:T(8,128)(2,1)}), bf16[4,64,512]{2,1,0:T(8,128)(2,1)S(1)}, u32[]{:S(2)}, u32[]{:S(2)}) %all-to-all-start.4) | async-done | bytes 262176 | tf_op jit(solution)/shard_map/all_to_all | solution.py:33
  90.1 0.7 convert_reduce_fusion
  (24 shorter events, 0.8 us)
Async XLA Ops:
  0.6 82.7 %copy-start = (bf16[1024,1024]{1,0:T(8,128)(2,1)S(1)}, bf16[1024,1024]{1,0:T(8,128)(2,1)}, u32[]{:S(2)}) copy-start(bf16[1024,1024]{1,0:T(8,128)(2,1)} %param.8) | copy-start | bytes 6291460
  0.6 2.9 %copy-start.5 = (bf16[128,1024]{1,0:T(8,128)(2,1)S(1)}, bf16[128,1024]{1,0:T(8,128)(2,1)}, u32[]{:S(2)}) copy-start(bf16[128,1024]{1,0:T(8,128)(2,1)} %param.9) | copy-start | bytes 786436
  3.5 6.2 %copy-start.3 = (bf16[128,1024]{1,0:T(8,128)(2,1)S(1)}, bf16[128,1024]{1,0:T(8,128)(2,1)}, u32[]{:S(2)}) copy-start(bf16[128,1024]{1,0:T(8,128)(2,1)} %param.5) | copy-start | bytes 786436
  4.6 16.0 %all-to-all-start = ((bf16[4,128,768]{2,1,0:T(8,128)(2,1)}), bf16[4,128,768]{2,1,0:T(8,128)(2,1)S(1)}, u32[]{:S(2)}, u32[]{:S(2)}) async-start(bf16[4,128,768]{2,1,0:T(8,128)(2,1)} %pad_maximum_fusion), calls=%async_computation | async-start | bytes 1572864 | tf_op jit(solution)/shard_map/all_to_all | solution.py:33
  20.6 21.0 %copy-start.2 = (bf16[4,128,768]{2,1,0:T(8,128)(2,1)}, bf16[4,128,768]{2,1,0:T(8,128)(2,1)S(1)}, u32[]{:S(2)}) copy-start(bf16[4,128,768]{2,1,0:T(8,128)(2,1)S(1)} %all-to-all-done) | copy-start | bytes 2359300
  21.5 18.6 %all-to-all-start.1 = ((bf16[4,128,512]{2,1,0:T(8,128)(2,1)}), bf16[4,128,512]{2,1,0:T(8,128)(2,1)S(1)}, u32[]{:S(2)}, u32[]{:S(2)}) async-start(bf16[4,128,512]{2,1,0:T(8,128)(2,1)} %broadcast_in_dim.84), calls=%async_computation.1 | async-start | bytes 1048576 | tf_op jit(solution)/shard_map/all_to_all | solution.py:33
  42.4 11.0 %all-to-all-start.3 = ((bf16[4,128,512]{2,1,0:T(8,128)(2,1)}), bf16[4,128,512]{2,1,0:T(8,128)(2,1)S(1)}, u32[]{:S(2)}, u32[]{:S(2)}) async-start(bf16[4,128,512]{2,1,0:T(8,128)(2,1)} %bitcast.19), calls=%async_computation.3 | async-start | bytes 1048576 | tf_op jit(solution)/shard_map/all_to_all | solution.py:33
  53.3 10.1 %all-to-all-start.2 = ((bf16[4,128,512]{2,1,0:T(8,128)(2,1)}), bf16[4,128,512]{2,1,0:T(8,128)(2,1)S(1)}, u32[]{:S(2)}, u32[]{:S(2)}) async-start(bf16[4,128,512]{2,1,0:T(8,128)(2,1)} %bitcast.81), calls=%async_computation.2 | async-start | bytes 1048576 | tf_op jit(solution)/shard_map/all_to_all | solution.py:33
  63.5 0.8 copy-start.1
  64.3 15.6 %all-to-all-start.5 = ((bf16[4,128,512]{2,1,0:T(8,128)(2,1)}), bf16[4,128,512]{2,1,0:T(8,128)(2,1)S(1)}, u32[]{:S(2)}, u32[]{:S(2)}) async-start(bf16[4,128,512]{2,1,0:T(8,128)(2,1)} %bitcast.80), calls=%async_computation.5 | async-start | bytes 1048576 | tf_op jit(solution)/shard_map/all_to_all | solution.py:33
  72.9 13.4 %copy-start.4 = (bf16[128,1024]{1,0:T(8,128)(2,1)S(1)}, bf16[128,1024]{1,0:T(8,128)(2,1)}, u32[]{:S(2)}) copy-start(bf16[128,1024]{1,0:T(8,128)(2,1)} %param.5) | copy-start | bytes 786436
  79.9 10.2 %all-to-all-start.4 = ((bf16[4,64,512]{2,1,0:T(8,128)(2,1)}), bf16[4,64,512]{2,1,0:T(8,128)(2,1)S(1)}, u32[]{:S(2)}, u32[]{:S(2)}) async-start(bf16[4,64,512]{2,1,0:T(8,128)(2,1)} %bitcast.20), calls=%async_computation.4 | async-start | bytes 524288 | tf_op jit(solution)/shard_map/all_to_all | solution.py:33

commit v3 on v2

--- a/solution.py
+++ b/solution.py
@@ -29,8 +29,23 @@
     inner_groups = [[o * inner + i for i in range(inner)] for o in range(outer)]
     outer_groups = [[o * inner + i for o in range(outer)] for i in range(inner)]
 
-    def swap_all(value, groups):
-        return lax.all_to_all(value, "blk", 0, 0, axis_index_groups=groups)
+    def along_inner(value, turn):
+        pairs = [
+            (o * inner + i, o * inner + (i ^ turn)) for o in range(outer) for i in range(inner)
+        ]
+        return lax.ppermute(value, "blk", pairs) if turn else value
+
+    def along_outer(value, turn):
+        pairs = [
+            (o * inner + i, (o ^ turn) * inner + i) for o in range(outer) for i in range(inner)
+        ]
+        return lax.ppermute(value, "blk", pairs) if turn else value
+
+    def pick(value, index):
+        return lax.dynamic_index_in_dim(value, index, 0, keepdims=False)
+
+    def summed(arrived):
+        return sum(part.astype(jnp.float32) for part in arrived)
 
     def dot(lhs, rhs, dims):
         return lax.dot_general(lhs, rhs, (dims, ((), ())), preferred_element_type=jnp.float32)
@@ -38,23 +53,34 @@
     hidden_part = jnp.maximum(
         lax.dynamic_slice_in_dim(hidden_pre, rep_pos * cols_here, cols_here, 1), 0
     )
-    hidden_stack = swap_all(
-        jnp.broadcast_to(hidden_part[None], (outer, tile_size, cols_here)), outer_groups
-    ).reshape(outer * tile_size, cols_here)
+    hidden_stack = lax.all_gather(
+        hidden_part, "blk", axis=0, axis_index_groups=outer_groups, tiled=True
+    )
+    grad_part = lax.dynamic_slice_in_dim(cotangent, rep_pos * cols_here, cols_here, 1)
+    grad_stack = lax.all_gather(
+        grad_part, "blk", axis=0, axis_index_groups=inner_groups, tiled=True
+    )
 
     order = jnp.arange(section_span, dtype=jnp.int32).reshape(per_core, inner).T.reshape(-1)
     hit = (adj_cols[0] % section_span)[None, :] == order[:, None]
     ordered = jnp.sum(
         jnp.where(hit[:, :, None, None], adj_vals[0][None].astype(jnp.float32), 0.0), axis=1
     ).astype(bf16)
-    ordered = ordered.reshape(inner, per_core, tile_size, tile_size).transpose(0, 2, 1, 3)
-    ordered = ordered.reshape(inner, tile_size, per_core * tile_size)
-    grad_part = lax.dynamic_slice_in_dim(cotangent, rep_pos * cols_here, cols_here, 1)
-    grad_copies = jnp.broadcast_to(grad_part[None], (inner, tile_size, cols_here))
-    arrived = swap_all(jnp.concatenate([ordered, grad_copies], 2), inner_groups)
-    arrived = arrived.reshape(inner * tile_size, per_core * tile_size + cols_here)
-    grad_stack = arrived[:, per_core * tile_size :]
-    everyone = lax.all_gather(arrived[:, : per_core * tile_size], "rep", axis=0)
+    ordered = ordered.reshape(inner, per_core, tile_size, tile_size)
+    arrived = jnp.stack(
+        [along_inner(pick(ordered, inner_pos ^ t), t) for t in range(inner)]
+    )
+    everyone = lax.all_gather(arrived, "rep", axis=0)
+    everyone = jnp.stack(
+        [
+            lax.dynamic_index_in_dim(everyone, inner_pos ^ i, 1, keepdims=False)
+            for i in range(inner)
+        ],
+        1,
+    )
+    everyone = everyone.transpose(0, 1, 3, 2, 4).reshape(
+        rep_count, inner * tile_size, per_core * tile_size
+    )
 
     row_block = outer_pos * inner + jnp.repeat(jnp.arange(inner, dtype=jnp.int32), tile_size)
     pieces = []
@@ -70,29 +96,31 @@
     block = jnp.concatenate(pieces, 1)
 
     back_stack = dot(block, grad_stack, ((0,), (0,))).astype(bf16)
-    back_arrived = swap_all(back_stack.reshape(outer, tile_size, cols_here), outer_groups)
+    back_part = lax.psum_scatter(
+        back_stack, "blk", scatter_dimension=0, axis_index_groups=outer_groups, tiled=True
+    )
 
-    mixed = dot(block, hidden_stack, ((1,), (0,))).astype(bf16)
     mixed_t = dot(hidden_stack, block, ((0,), (1,))).astype(bf16)
     by_group = mixed_t.reshape(per_core, inner, rows_here, inner * tile_size)
     by_group = by_group.transpose(1, 0, 2, 3).reshape(
         inner, per_core * rows_here, inner * tile_size
     )
-    mixed_rows = swap_all(mixed.reshape(inner, tile_size, cols_here), inner_groups)
-    mixed_cols = swap_all(by_group, inner_groups)
-    mixed_rows = jnp.sum(mixed_rows.astype(jnp.float32), 0).astype(bf16)
-    mixed_cols = jnp.sum(mixed_cols.astype(jnp.float32), 0).astype(bf16)
+    mixed = dot(block, hidden_stack, ((1,), (0,))).astype(bf16)
+    mixed = mixed.reshape(inner, tile_size, cols_here)
+    mixed_cols = summed([along_inner(pick(by_group, inner_pos ^ t), t) for t in range(inner)])
+    mixed_cols = mixed_cols.astype(bf16)
+    mixed_rows = summed([along_inner(pick(mixed, inner_pos ^ t), t) for t in range(inner)])
+    mixed_rows = mixed_rows.astype(bf16)
 
     mixed_cols = lax.all_gather(mixed_cols, "rep", axis=0, tiled=True)
     weight_part = dot(mixed_cols, grad_stack, ((1,), (0,))).astype(bf16)
-    weight_arrived = swap_all(weight_part.reshape(outer, rows_here, cols_here), outer_groups)
-    grad_weight = jnp.sum(weight_arrived.astype(jnp.float32), 0)
+    weight_part = weight_part.reshape(outer, rows_here, cols_here)
+    grad_weight = summed([along_outer(pick(weight_part, outer_pos ^ t), t) for t in range(outer)])
 
     mixed_rows = lax.all_gather(mixed_rows, "rep", axis=1, tiled=True)
     w_columns = lax.dynamic_slice_in_dim(w_out, rep_pos * cols_here, cols_here, 1)
     out_part = dot(mixed_rows, w_columns, ((1,), (0,))).astype(bf16)
 
-    back_part = jnp.sum(back_arrived.astype(jnp.float32), 0).astype(bf16)
     back_full = lax.all_gather(back_part, "rep", axis=1, tiled=True)
     w_rows = lax.dynamic_slice_in_dim(w_out, rep_pos * cols_here, cols_here, 0)
     grad_in = dot(back_full, w_rows, ((1,), (1,)))

time: 91.4 us -> 96.3 us (1.054)
  blocking collectives: 8.15 us -> 35.6 us
  waiting for transfers between devices: 37.9 us -> 11.8 us
  between operations: 0.82 us -> 14.4 us
  starting transfers between devices: 23.9 us -> 15.8 us
  matrix products: 10.5 us -> 5.63 us
  other arithmetic: 6.48 us -> 8.31 us
  local copies, waits for them, and re-layouts: 3.02 us -> 4.37 us
    all_to_all x6 -> x0, waiting for transfers between devices: 37.9 us -> none  [swap_all(): return lax.all_to_all(value, 'blk', 0, 0, axis_index_groups=groups)]
    all_gather x1 -> x3, blocking collectives: 2.18 us -> 29.4 us  [the longest x1 16.5 us: shards(): lax.all_gather(hidden_part, 'blk', axis=0, axis_index_groups=outer_groups...]
    all_to_all x6 -> x0, starting transfers between devices: 23.9 us -> none  [swap_all(): return lax.all_to_all(value, 'blk', 0, 0, axis_index_groups=groups)]
    ppermute x0 -> x12, starting transfers between devices: none -> 15.8 us  [the longest x9 11.3 us: along_inner(): return lax.ppermute(value, 'blk', pairs) if turn else value]
    ppermute x0 -> x12, waiting for transfers between devices: none -> 11.7 us  [the longest x9 6.21 us: along_inner(): return lax.ppermute(value, 'blk', pairs) if turn else value]
    dot_general x6, matrix products: 10.5 us -> 5.63 us  [dot(): lax.dot_general(lhs, rhs, (dims, ((), ())), preferred_element_type=jnp.fl...]
    convert_element_type x0 -> x2, other arithmetic: none -> 2.14 us  [the longest x1 1.1 us: shards(): mixed_cols = mixed_cols.astype(bf16)]
    reduce_sum x4 -> x0, other arithmetic: 1.97 us -> none  [the longest x1 1.13 us: shards(): mixed_rows = jnp.sum(mixed_rows.astype(jnp.float32), 0).astype(bf16)]
  transfers between devices with their start and end apart: 6 -> 13, of which waited for: 6 -> 3; matrix products, arithmetic and copies ran while one was open for 13% -> 7% of each run, Pallas kernels for 0% -> 0%
where the time goes in v3:
time: 96.3 us; the launch traced here: 95.9 us
  blocking collectives  35.6 us (37%)
  starting transfers between devices  15.8 us (16%)
  between operations  14.4 us (15%)
  waiting for transfers between devices  11.8 us (12%)
  other arithmetic  8.31 us (9%)
  matrix products  5.63 us (6%)
  local copies, waits for them, and re-layouts  4.37 us (5%)
    all_gather x1, blocking collectives, shards(): lax.all_gather(hidden_part, 'blk', axis=0, axis_index_groups=outer_groups...  16.5 us
    ppermute x9, starting transfers between devices, along_inner(): return lax.ppermute(value, 'blk', pairs) if turn else value  11.3 us
    all_gather x1, blocking collectives, shards(): lax.all_gather(grad_part, 'blk', axis=0, axis_index_groups=inner_groups,...  10.7 us
    ppermute x9, waiting for transfers between devices, along_inner(): return lax.ppermute(value, 'blk', pairs) if turn else value  6.21 us
    dot_general x6, matrix products, dot(): lax.dot_general(lhs, rhs, (dims, ((), ())), preferred_element_type=jnp.fl...  5.63 us
    ppermute x3, waiting for transfers between devices, along_outer(): return lax.ppermute(value, 'blk', pairs) if turn else value  5.53 us
    ppermute x3, starting transfers between devices, along_outer(): return lax.ppermute(value, 'blk', pairs) if turn else value  4.45 us
    all_gather x1, blocking collectives, shards(): back_full = lax.all_gather(back_part, 'rep', axis=1, tiled=True)  2.29 us
  transfers between devices with their start and end apart: 13, of which 3 were waited for; matrix products, arithmetic and copies ran while one was open for 7% of the time, Pallas kernels for 0%

profile of v3, /device:TPU:0, one launch (start us, length us, event | category | flops | bytes accessed | tf_op | source)
XLA Modules:
  0.0 95.9 jit_solution(3241244813946363269)
XLA Ops:
  7.3 1.1 %bitcast_convert_fusion = f32[8,128,128]{2,1,0:T(8,128)S(1)} fusion(bf16[1,8,128,128]{3,2,1,0:T(8,128)(2,1)} %param.6), kind=kLoop, calls=%fused_computation.21 | loop fusion | flops 131072 | bytes 786432 | tf_op jit(solution)/shard_map/jit(_where)/broadcast_in_dim | solution.py:67
  8.4 0.7 fusion.29
  10.5 3.9 %collective-permute-start.2 = (bf16[2,128,128]{2,1,0:T(8,128)(2,1)}, bf16[2,128,128]{2,1,0:T(8,128)(2,1)S(1)}, u32[]{:S(2)}, u32[]{:S(2)}) collective-permute-start(bf16[2,128,128]{2,1,0:T(8,128)(2,1)} %get-tuple-element.21), channel_id=1, source_target_pairs={{0,6},{2,4},{4,2},{6,0},{8,14},{10,12},{12,10},{14,8},{16,22},{18,... | collective-permute-start | bytes 196616 | tf_op jit(solution)/shard_map/ppermute | solution.py:36
  15.0 16.5 %all_gather.23 = bf16[512,512]{1,0:T(8,128)(2,1)} all-gather(bf16[128,512]{1,0:T(8,128)(2,1)S(1)} %dynamic-slice_maximum_fusion), channel_id=1, replica_groups={{0,8,16,24},{2,10,18,26},{4,12,20,28},{6,14,22,30},{1,9,17,25},{3,11,19..., dimensions={0}, use_global_device_ids=true | all-gather | bytes 655360 | tf_op jit(solution)/shard_map/all_gather | solution.py:56
  31.6 10.7 %all_gather.26 = bf16[512,512]{1,0:T(8,128)(2,1)S(1)} all-gather(bf16[128,512]{1,0:T(8,128)(2,1)S(1)} %constant_dynamic-slice_fusion), channel_id=1, replica_groups={{0,2,4,6},{8,10,12,14},{16,18,20,22},{24,26,28,30},{1,3,5,7},{9,11,13,1..., dimensions={0}, use_global_device_ids=true | all-gather | bytes 655360 | tf_op jit(solution)/shard_map/all_gather | solution.py:60
  42.3 0.9 pad_maximum_fusion.1
  43.2 2.2 %all-gather = bf16[8,2,128,128]{3,2,1,0:T(8,128)(2,1)S(1)} all-gather(bf16[4,2,128,128]{3,2,1,0:T(8,128)(2,1)S(1)} %pad_maximum_fusion.1), channel_id=2, replica_groups=mesh['blk'=16,'rep'=2] {'rep'}, dimensions={0}, use_global_device_ids=true | all-gather | bytes 786432 | tf_op jit(solution)/shard_map/all_gather | solution.py:73
  46.1 1.7 %maximum_bitcast_fusion = bf16[2,4,128,2,128]{4,3,2,1,0:T(2,128)(2,1)} fusion(bf16[2,1,2,128,128]{4,2,3,1,0:T(2,128)(2,1)S(1)} %copy.27, bf16[2,1,2,128,128]{4,2,3,1,0:T(2,128)(2,1)S(1)} %copy.26, bf16[2,1,2,128,128]{4,2,3,1,0:T(2,128)(2,1)S(1)} %copy.25, bf16[2,1,2,128,128]{4,2,3,1,0:T(2,128)(2,1)S(1)} %copy.24), kind=kLoop, calls=%fused_computation.10 | loop fusion | flops 786432 | bytes 1048576 | tf_op jit(solution)/shard_map/transpose | solution.py:81
  47.8 1.4 %reshape.225 = bf16[2,512,256]{2,1,0:T(8,128)(2,1)S(1)} reshape(bf16[2,4,128,2,128]{4,3,2,1,0:T(2,128)(2,1)} %maximum_bitcast_fusion) | data formatting | bytes 1048576 | tf_op jit(solution)/shard_map/reshape | solution.py:81
  49.5 1.5 %convolution_convert_fusion.2 = bf16[512,512]{1,0:T(8,128)(2,1)S(1)} fusion(bf16[512,512]{1,0:T(8,128)(2,1)} %all_gather.23, bf16[512,128]{1,0:T(8,128)(2,1)S(1)} %get-tuple-element.10, bf16[512,128]{1,0:T(8,128)(2,1)S(1)} %get-tuple-element.12, bf16[512,128]{1,0:T(8,128)(2,1)S(1)} %get-tuple-element.11, bf16[512,128]{1,0:T(8,128)(2,1)S(1)} %get-tuple-element.9), kind=kOutput, calls=%fused_computation.3 | convolution fusion | flops 270794752 | bytes 1572864 | tf_op jit(solution)/shard_map/dot_general | solution.py:51
  51.5 0.8 dynamic-slice_bitcast_fusion.5
  52.3 1.5 %collective-permute-start.5 = (bf16[128,512]{1,0:T(8,128)(2,1)}, bf16[128,512]{1,0:T(8,128)(2,1)S(1)}, u32[]{:S(2)}, u32[]{:S(2)}) collective-permute-start(bf16[128,512]{1,0:T(8,128)(2,1)} %get-tuple-element.7), channel_id=1, source_target_pairs={{0,6},{2,4},{4,2},{6,0},{8,14},{10,12},{12,10},{14,8},{16,22},{18,... | collective-permute-start | bytes 393224 | tf_op jit(solution)/shard_map/ppermute | solution.py:36
  53.7 0.9 collective-permute-start.4
  54.7 0.8 dynamic-slice_bitcast_fusion.2
  55.4 1.5 %collective-permute-start.8 = (bf16[128,512]{1,0:T(8,128)(2,1)}, bf16[128,512]{1,0:T(8,128)(2,1)}, u32[]{:S(2)}, u32[]{:S(2)}) collective-permute-start(bf16[128,512]{1,0:T(8,128)(2,1)} %get-tuple-element.4), channel_id=1, source_target_pairs={{0,6},{2,4},{4,2},{6,0},{8,14},{10,12},{12,10},{14,8},{16,22},{18,... | collective-permute-start | bytes 393224 | tf_op jit(solution)/shard_map/ppermute | solution.py:36
  56.9 1.2 %collective-permute-start.7 = (bf16[128,512]{1,0:T(8,128)(2,1)}, bf16[128,512]{1,0:T(8,128)(2,1)}, u32[]{:S(2)}, u32[]{:S(2)}) collective-permute-start(bf16[128,512]{1,0:T(8,128)(2,1)} %get-tuple-element.5), channel_id=1, source_target_pairs={{0,4},{2,6},{4,0},{6,2},{8,12},{10,14},{12,8},{14,10},{16,20},{18,... | collective-permute-start | bytes 393224 | tf_op jit(solution)/shard_map/ppermute | solution.py:36
  58.1 0.9 collective-permute-start.6
  58.9 1.2 %convolution_convert_fusion = bf16[512,512]{1,0:T(8,128)(2,1)} fusion(bf16[512,512]{1,0:T(8,128)(2,1)S(1)} %all_gather.26, bf16[512,128]{1,0:T(8,128)(2,1)S(1)} %get-tuple-element.10, bf16[512,128]{1,0:T(8,128)(2,1)S(1)} %get-tuple-element.12, bf16[512,128]{1,0:T(8,128)(2,1)S(1)} %get-tuple-element.11, bf16[512,128]{1,0:T(8,128)(2,1)S(1)} %get-tuple-element.9), kind=kOutput, calls=%fused_computation.1 | convolution fusion | flops 270794752 | bytes 1572864 | tf_op jit(solution)/shard_map/dot_general | solution.py:51
  60.2 2.9 %collective-permute-done.8 = bf16[128,512]{1,0:T(8,128)(2,1)} collective-permute-done((bf16[128,512]{1,0:T(8,128)(2,1)}, bf16[128,512]{1,0:T(8,128)(2,1)}, u32[]{:S(2)}, u32[]{:S(2)}) %collective-permute-start.8) | collective-permute-done | bytes 131104 | tf_op jit(solution)/shard_map/ppermute | solution.py:36
  63.1 1.1 %collective-permute-start.3 = (bf16[128,512]{1,0:T(8,128)(2,1)}, bf16[128,512]{1,0:T(8,128)(2,1)S(1)}, u32[]{:S(2)}, u32[]{:S(2)}) collective-permute-start(bf16[128,512]{1,0:T(8,128)(2,1)} %get-tuple-element.6), channel_id=1, source_target_pairs={{0,2},{2,0},{4,6},{6,4},{8,10},{10,8},{12,14},{14,12},{16,18},{18,... | collective-permute-start | bytes 393224 | tf_op jit(solution)/shard_map/ppermute | solution.py:36
  64.1 3.3 %collective-permute-done.7 = bf16[128,512]{1,0:T(8,128)(2,1)} collective-permute-done((bf16[128,512]{1,0:T(8,128)(2,1)}, bf16[128,512]{1,0:T(8,128)(2,1)}, u32[]{:S(2)}, u32[]{:S(2)}) %collective-permute-start.7) | collective-permute-done | bytes 131104 | tf_op jit(solution)/shard_map/ppermute | solution.py:36
  67.5 1.1 %fusion.5 = bf16[128,512]{1,0:T(8,128)(2,1)S(1)} fusion(bf16[128,512]{1,0:T(8,128)(2,1)} %collective-permute-done.8, bf16[128,512]{1,0:T(8,128)(2,1)} %collective-permute-done.7, bf16[128,512]{1,0:T(8,128)(2,1)} %collective-permute-done.6, bf16[4,128,512]{2,1,0:T(8,128)(2,1)S(1)} %bitcast.107, s32[]{:T(128)S(6)} %select_n.156), kind=kLoop, calls=%fused_computation.16 | loop fusion | flops 524288 | bytes 655364 | tf_op jit(solution)/shard_map/convert_element_type | solution.py:111
  68.6 2.0 %all_gather.25 = bf16[256,512]{1,0:T(8,128)(2,1)S(1)} all-gather(bf16[128,512]{1,0:T(8,128)(2,1)S(1)} %fusion.5), channel_id=1, replica_groups=mesh['blk'=16,'rep'=2] {'rep'}, dimensions={0}, use_global_device_ids=true | all-gather | bytes 393216 | tf_op jit(solution)/shard_map/all_gather | solution.py:115
  70.9 3.7 %collective-permute-start.11 = (bf16[64,512]{1,0:T(8,128)(2,1)S(1)}, bf16[64,512]{1,0:T(8,128)(2,1)S(1)}, u32[]{:S(2)}, u32[]{:S(2)}) collective-permute-start(bf16[64,512]{1,0:T(8,128)(2,1)S(1)} %get-tuple-element.18), channel_id=1, source_target_pairs={{0,24},{2,26},{4,28},{6,30},{8,16},{10,18},{12,20},{14,22},{16,8},... | collective-permute-start | bytes 196616 | tf_op jit(solution)/shard_map/ppermute | solution.py:42
  74.6 0.8 collective-permute-start.9
  75.4 1.0 %fusion.8 = bf16[128,512]{1,0:T(8,128)(2,1)S(1)} fusion(bf16[128,512]{1,0:T(8,128)(2,1)S(1)} %collective-permute-done.5, bf16[128,512]{1,0:T(8,128)(2,1)} %collective-permute-done.4, bf16[128,512]{1,0:T(8,128)(2,1)S(1)} %collective-permute-done.3, bf16[4,128,512]{2,1,0:T(8,128)(2,1)} %bitcast.114, s32[]{:T(128)S(6)} %select_n.156), kind=kLoop, calls=%fused_computation.20 | loop fusion | flops 524288 | bytes 655364 | tf_op jit(solution)/shard_map/convert_element_type | solution.py:113
  76.4 2.0 %all_gather.24 = bf16[128,1024]{1,0:T(8,128)(2,1)S(1)} all-gather(bf16[128,512]{1,0:T(8,128)(2,1)S(1)} %fusion.8), channel_id=1, replica_groups=mesh['blk'=16,'rep'=2] {'rep'}, dimensions={1}, use_global_device_ids=true | all-gather | bytes 393216 | tf_op jit(solution)/shard_map/all_gather | solution.py:120
  78.4 1.0 %convolution_convert_fusion.4 = bf16[128,512]{1,0:T(8,128)(2,1)} fusion(bf16[128,1024]{1,0:T(8,128)(2,1)S(1)} %all_gather.24, bf16[1024,1024]{1,0:T(8,128)(2,1)S(1)} %copy-done, s32[]{:T(128)S(6)} %select_n.170), kind=kOutput, calls=%fused_computation.6 | convolution fusion | flops 134283264 | bytes 1441796 | tf_op jit(solution)/shard_map/dot_general | solution.py:51
  79.4 5.5 %collective-permute-done.10 = bf16[64,512]{1,0:T(8,128)(2,1)S(1)} collective-permute-done((bf16[64,512]{1,0:T(8,128)(2,1)S(1)}, bf16[64,512]{1,0:T(8,128)(2,1)S(1)}, u32[]{:S(2)}, u32[]{:S(2)}) %collective-permute-start.10) | collective-permute-done | bytes 65568 | tf_op jit(solution)/shard_map/ppermute | solution.py:42
  84.9 0.7 fusion.10
  85.6 2.3 %all_gather.27 = bf16[128,1024]{1,0:T(8,128)(2,1)S(1)} all-gather(bf16[128,512]{1,0:T(8,128)(2,1)} %reduce-scatter.2.cloned.1.call-done), channel_id=1, replica_groups=mesh['blk'=16,'rep'=2] {'rep'}, dimensions={1}, use_global_device_ids=true | all-gather | bytes 393216 | tf_op jit(solution)/shard_map/all_gather | solution.py:124
  87.9 1.1 %fusion = bf16[128,512]{1,0:T(8,128)(2,1)} fusion(bf16[128,1024]{1,0:T(8,128)(2,1)S(1)} %all_gather.27, bf16[1024,1024]{1,0:T(8,128)(2,1)S(1)} %copy-done, s32[]{:T(128)S(6)} %select_n.170, bf16[128,1024]{1,0:T(8,128)(2,1)S(1)} %copy-done.3), kind=kOutput, calls=%fused_computation.7 | convolution fusion | flops 134545408 | bytes 1573888 | tf_op jit(solution)/shard_map/dot_general | solution.py:51
  (45 shorter events, 3.9 us)
Async XLA Ops:
  7.2 71.2 %copy-start = (bf16[1024,1024]{1,0:T(8,128)(2,1)S(1)}, bf16[1024,1024]{1,0:T(8,128)(2,1)}, u32[]{:S(2)}) copy-start(bf16[1024,1024]{1,0:T(8,128)(2,1)} %param.8) | copy-start | bytes 6291460
  7.2 7.8 %copy-start.3 = (bf16[128,1024]{1,0:T(8,128)(2,1)S(1)}, bf16[128,1024]{1,0:T(8,128)(2,1)}, u32[]{:S(2)}) copy-start(bf16[128,1024]{1,0:T(8,128)(2,1)} %param.5) | copy-start | bytes 786436
  7.2 24.4 %copy-start.4 = (bf16[128,1024]{1,0:T(8,128)(2,1)S(1)}, bf16[128,1024]{1,0:T(8,128)(2,1)}, u32[]{:S(2)}) copy-start(bf16[128,1024]{1,0:T(8,128)(2,1)} %param.9) | copy-start | bytes 786436
  7.2 78.4 %reduce-scatter.2.cloned.1.call-start = ((), (), s32[]{:S(2)}) async-start(), calls=%async_computation.1 | async-start | bytes 655360 | tf_op jit(solution)/shard_map/reduce_scatter | solution.py:99
  10.5 31.8 %collective-permute-start.2 = (bf16[2,128,128]{2,1,0:T(8,128)(2,1)}, bf16[2,128,128]{2,1,0:T(8,128)(2,1)S(1)}, u32[]{:S(2)}, u32[]{:S(2)}) collective-permute-start(bf16[2,128,128]{2,1,0:T(8,128)(2,1)} %get-tuple-element.21), channel_id=1, source_target_pairs={{0,6},{2,4},{4,2},{6,0},{8,14},{10,12},{12,10},{14,8},{16,22},{18,... | collective-permute-start | bytes 196616 | tf_op jit(solution)/shard_map/ppermute | solution.py:36
  14.4 27.9 %collective-permute-start.1 = (bf16[2,128,128]{2,1,0:T(8,128)(2,1)S(1)}, bf16[2,128,128]{2,1,0:T(8,128)(2,1)}, u32[]{:S(2)}, u32[]{:S(2)}) collective-permute-start(bf16[2,128,128]{2,1,0:T(8,128)(2,1)S(1)} %get-tuple-element.22), channel_id=1, source_target_pairs={{0,4},{2,6},{4,0},{6,2},{8,12},{10,14},{12,8},{14,10},{16,20},{18,... | collective-permute-start | bytes 196616 | tf_op jit(solution)/shard_map/ppermute | solution.py:36
  14.9 27.4 %collective-permute-start = (bf16[2,128,128]{2,1,0:T(8,128)(2,1)S(1)}, bf16[2,128,128]{2,1,0:T(8,128)(2,1)}, u32[]{:S(2)}, u32[]{:S(2)}) collective-permute-start(bf16[2,128,128]{2,1,0:T(8,128)(2,1)S(1)} %get-tuple-element.23), channel_id=1, source_target_pairs={{0,2},{2,0},{4,6},{6,4},{8,10},{10,8},{12,14},{14,12},{16,18},{18,... | collective-permute-start | bytes 196616 | tf_op jit(solution)/shard_map/ppermute | solution.py:36
  49.2 1.8 %copy-start.1 = (bf16[512,512]{1,0:T(8,128)(2,1)S(1)}, bf16[512,512]{1,0:T(8,128)(2,1)}, u32[]{:S(2)}) copy-start(bf16[512,512]{1,0:T(8,128)(2,1)} %all_gather.23) | copy-start | bytes 1572868
  51.0 3.6 %copy-start.2 = (bf16[512,512]{1,0:T(8,128)(2,1)}, bf16[512,512]{1,0:T(8,128)(2,1)S(1)}, u32[]{:S(2)}) copy-start(bf16[512,512]{1,0:T(8,128)(2,1)S(1)} %convolution_convert_fusion.2) | copy-start | bytes 1572868
  52.3 22.3 %collective-permute-start.5 = (bf16[128,512]{1,0:T(8,128)(2,1)}, bf16[128,512]{1,0:T(8,128)(2,1)S(1)}, u32[]{:S(2)}, u32[]{:S(2)}) collective-permute-start(bf16[128,512]{1,0:T(8,128)(2,1)} %get-tuple-element.7), channel_id=1, source_target_pairs={{0,6},{2,4},{4,2},{6,0},{8,14},{10,12},{12,10},{14,8},{16,22},{18,... | collective-permute-start | bytes 393224 | tf_op jit(solution)/shard_map/ppermute | solution.py:36
  53.7 21.6 %collective-permute-start.4 = (bf16[128,512]{1,0:T(8,128)(2,1)}, bf16[128,512]{1,0:T(8,128)(2,1)}, u32[]{:S(2)}, u32[]{:S(2)}) collective-permute-start(bf16[128,512]{1,0:T(8,128)(2,1)} %get-tuple-element.8), channel_id=1, source_target_pairs={{0,4},{2,6},{4,0},{6,2},{8,12},{10,14},{12,8},{14,10},{16,20},{18,... | collective-permute-start | bytes 393224 | tf_op jit(solution)/shard_map/ppermute | solution.py:36
  55.4 7.6 %collective-permute-start.8 = (bf16[128,512]{1,0:T(8,128)(2,1)}, bf16[128,512]{1,0:T(8,128)(2,1)}, u32[]{:S(2)}, u32[]{:S(2)}) collective-permute-start(bf16[128,512]{1,0:T(8,128)(2,1)} %get-tuple-element.4), channel_id=1, source_target_pairs={{0,6},{2,4},{4,2},{6,0},{8,14},{10,12},{12,10},{14,8},{16,22},{18,... | collective-permute-start | bytes 393224 | tf_op jit(solution)/shard_map/ppermute | solution.py:36
  56.9 10.5 %collective-permute-start.7 = (bf16[128,512]{1,0:T(8,128)(2,1)}, bf16[128,512]{1,0:T(8,128)(2,1)}, u32[]{:S(2)}, u32[]{:S(2)}) collective-permute-start(bf16[128,512]{1,0:T(8,128)(2,1)} %get-tuple-element.5), channel_id=1, source_target_pairs={{0,4},{2,6},{4,0},{6,2},{8,12},{10,14},{12,8},{14,10},{16,20},{18,... | collective-permute-start | bytes 393224 | tf_op jit(solution)/shard_map/ppermute | solution.py:36
  58.1 9.4 %collective-permute-start.6 = (bf16[128,512]{1,0:T(8,128)(2,1)}, bf16[128,512]{1,0:T(8,128)(2,1)}, u32[]{:S(2)}, u32[]{:S(2)}) collective-permute-start(bf16[128,512]{1,0:T(8,128)(2,1)} %get-tuple-element.3), channel_id=1, source_target_pairs={{0,2},{2,0},{4,6},{6,4},{8,10},{10,8},{12,14},{14,12},{16,18},{18,... | collective-permute-start | bytes 393224 | tf_op jit(solution)/shard_map/ppermute | solution.py:36
  63.1 12.3 %collective-permute-start.3 = (bf16[128,512]{1,0:T(8,128)(2,1)}, bf16[128,512]{1,0:T(8,128)(2,1)S(1)}, u32[]{:S(2)}, u32[]{:S(2)}) collective-permute-start(bf16[128,512]{1,0:T(8,128)(2,1)} %get-tuple-element.6), channel_id=1, source_target_pairs={{0,2},{2,0},{4,6},{6,4},{8,10},{10,8},{12,14},{14,12},{16,18},{18,... | collective-permute-start | bytes 393224 | tf_op jit(solution)/shard_map/ppermute | solution.py:36
  70.9 8.5 %collective-permute-start.11 = (bf16[64,512]{1,0:T(8,128)(2,1)S(1)}, bf16[64,512]{1,0:T(8,128)(2,1)S(1)}, u32[]{:S(2)}, u32[]{:S(2)}) collective-permute-start(bf16[64,512]{1,0:T(8,128)(2,1)S(1)} %get-tuple-element.18), channel_id=1, source_target_pairs={{0,24},{2,26},{4,28},{6,30},{8,16},{10,18},{12,20},{14,22},{16,8},... | collective-permute-start | bytes 196616 | tf_op jit(solution)/shard_map/ppermute | solution.py:42
  74.6 10.3 %collective-permute-start.10 = (bf16[64,512]{1,0:T(8,128)(2,1)S(1)}, bf16[64,512]{1,0:T(8,128)(2,1)S(1)}, u32[]{:S(2)}, u32[]{:S(2)}) collective-permute-start(bf16[64,512]{1,0:T(8,128)(2,1)S(1)} %get-tuple-element.19), channel_id=1, source_target_pairs={{0,16},{2,18},{4,20},{6,22},{8,24},{10,26},{12,28},{14,30},{16,0},... | collective-permute-start | bytes 196616 | tf_op jit(solution)/shard_map/ppermute | solution.py:42
  74.6 10.3 %collective-permute-start.9 = (bf16[64,512]{1,0:T(8,128)(2,1)S(1)}, bf16[64,512]{1,0:T(8,128)(2,1)S(1)}, u32[]{:S(2)}, u32[]{:S(2)}) collective-permute-start(bf16[64,512]{1,0:T(8,128)(2,1)S(1)} %get-tuple-element.17), channel_id=1, source_target_pairs={{0,8},{2,10},{4,12},{6,14},{8,0},{10,2},{12,4},{14,6},{16,24},{18,... | collective-permute-start | bytes 196616 | tf_op jit(solution)/shard_map/ppermute | solution.py:42
Sparse Core Ops, SparseCore 0:
  60.3 24.9 reduce-scatter.1

commit v4 on v2

v4 whole, which is shorter than its diff:
```python
import jax
import jax.numpy as jnp
from jax import lax
from jax.sharding import PartitionSpec as P


def shards(hidden_pre, adj_vals, adj_cols, w_out, cotangent):
    feature_width = hidden_pre.shape[1]
    tile_size = adj_vals.shape[2]
    blk_count = lax.axis_size("blk")
    rep_count = lax.axis_size("rep")
    section_span = blk_count // rep_count
    side = 1 << ((blk_count.bit_length() - 1) // 2)
    per_core = section_span // side
    groups = rep_count // 2
    wide = feature_width // groups
    rows_here = feature_width // blk_count
    half = wide // 2
    blk_pos = lax.axis_index("blk")
    rep_pos = lax.axis_index("rep")
    outer_pos, inner_pos = blk_pos // side, blk_pos % side
    role, group = rep_pos % 2, rep_pos // 2
    first_role = role == 0
    mates = [[g * 2 + r for g in range(groups)] for r in range(2)]
    bf16 = jnp.bfloat16
    turns = range(side)

    def routed(value, *routes):
        pairs = []
        for source_role, target in routes:
            for o in turns:
                for i in turns:
                    to_o, to_i, to_role = target(o, i)
                    for g in range(groups):
                        pairs.append(
                            (
                                (o * side + i) * rep_count + g * 2 + source_role,
                                (to_o * side + to_i) * rep_count + g * 2 + to_role,
                            )
                        )
        return lax.ppermute(value, ("blk", "rep"), pairs)

    def dot(lhs, rhs, dims):
        return lax.dot_general(lhs, rhs, (dims, ((), ())), preferred_element_type=jnp.float32)

    def summed(parts):
        return sum(part.astype(jnp.float32) for part in parts)

    def group_part(value, axis):
        if groups == 1:
            return value
        return lax.dynamic_slice_in_dim(value, group * wide, wide, axis)

    def all_groups(value):
        if groups == 1:
            return value
        return lax.all_gather(value, "rep", axis=0, tiled=True, axis_index_groups=mates)

    hidden_part = group_part(hidden_pre, 1)
    own = jnp.where(first_role, jnp.maximum(hidden_part, 0), group_part(cotangent, 1))
    stack = [own]
    for t in turns[1:]:
        stack.append(
            routed(own, (0, lambda o, i: (o ^ t, i, 0)), (1, lambda o, i: (o, i ^ t, 1)))
        )
    stack = jnp.concatenate(stack, 0)

    columns = adj_cols[0]
    place = ((columns % side) ^ inner_pos) * per_core + ((columns // side) ^ outer_pos) % per_core
    hit = place[None, :] == jnp.arange(section_span, dtype=jnp.int32)[:, None]
    ordered = jnp.sum(
        jnp.where(hit[:, :, None, None], adj_vals[0][None].astype(jnp.float32), 0.0), axis=1
    ).astype(bf16)
    ordered = ordered.reshape(side, per_core, tile_size, tile_size).transpose(0, 2, 1, 3)
    ordered = ordered.reshape(side, tile_size, per_core * tile_size)
    arrived = [ordered[0]]
    for t in turns[1:]:
        arrived.append(
            routed(ordered[t], *[(r, lambda o, i, r=r: (o, i ^ t, r)) for r in range(2)])
        )
    everyone = lax.all_gather(jnp.concatenate(arrived, 0), "rep", axis=0)

    turn_of_row = jnp.repeat(jnp.arange(side, dtype=jnp.int32), tile_size)
    row_block = outer_pos * side + (inner_pos ^ turn_of_row)
    pieces = []
    for e in turns:
        holder = jnp.mod(row_block - (outer_pos ^ e) * side - inner_pos, blk_count) // section_span
        m = e % per_core
        piece = everyone[0, :, m * tile_size : (m + 1) * tile_size]
        for r in range(1, rep_count):
            other = everyone[r, :, m * tile_size : (m + 1) * tile_size]
            piece = jnp.where((holder == r)[:, None], other, piece)
        pieces.append(piece)
    block = jnp.concatenate(pieces, 1)
    block = jnp.where(first_role, block, block.T)

    product = dot(stack, block, ((0,), (1,))).astype(bf16)
    parts = [product[:, t * tile_size : (t + 1) * tile_size] for t in turns]
    outer_share = side // groups
    by_owner = product.reshape(outer_share, side, rows_here, side * tile_size)
    sums = []
    for t in turns:
        chosen = lax.dynamic_index_in_dim(by_owner, inner_pos ^ t, 1, keepdims=False)
        chosen = chosen.reshape(outer_share * rows_here, side * tile_size)
        chosen = jnp.concatenate(
            [chosen[:, (u ^ t) * tile_size : ((u ^ t) + 1) * tile_size] for u in turns], 0
        )
        sums.append(
            routed(
                jnp.where(first_role, chosen, parts[t]),
                (0, lambda o, i: (o, i ^ t, 1)),
                (1, lambda o, i: (o ^ t, i, 0)),
            )
        )
    crossed = summed(sums).astype(bf16)
    rows_sum = summed(
        [parts[0]] + [routed(parts[t], (0, lambda o, i: (o, i ^ t, 0))) for t in turns[1:]]
    ).astype(bf16)

    share = outer_share * rows_here
    mixed = jnp.concatenate([crossed[u * share : (u + 1) * share] for u in turns], 1)
    weight_part = dot(all_groups(mixed), stack, ((1,), (0,))).astype(bf16)
    weight_part = weight_part.reshape(side, rows_here, wide)
    weight_sum = []
    for t in turns:
        chosen = lax.dynamic_index_in_dim(weight_part, outer_pos ^ t, 0, keepdims=False)
        weight_sum.append(routed(chosen, (1, lambda o, i: (o ^ t, i, 1))) if t else chosen)
    weight_sum = summed(weight_sum)

    out_wide = dot(all_groups(rows_sum), group_part(w_out, 1), ((0,), (0,))).astype(bf16)
    grad_in = dot(all_groups(crossed), group_part(w_out, 0), ((0,), (1,)))
    pre_wide = jnp.where(hidden_part > 0, grad_in, 0.0).astype(bf16)
    both = jnp.concatenate([out_wide, pre_wide], 0)
    both = jnp.where(
        first_role, both[:, :half], routed(both[:, half:], (0, lambda o, i: (o, i, 1)))
    )
    grad_weight = jnp.where(
        first_role,
        routed(weight_sum[:, :half], (1, lambda o, i: (o, i, 0))),
        weight_sum[:, half:],
    )
    return (both[:tile_size], grad_weight, both[tile_size:])


def solution(mesh):
    placed = (P("blk", None), P("blk", "rep", None, None), P("blk", "rep"), P(), P("blk", None))
    return jax.shard_map(
        shards,
        mesh=mesh,
        in_specs=placed,
        out_specs=(P("blk", "rep"), P("blk", "rep"), P("blk", "rep")),
        check_vma=False,
    )
```

time: 91.4 us -> 66.4 us (0.73)
  waiting for transfers between devices: 37.9 us -> 6.26 us
  starting transfers between devices: 23.9 us -> 36.2 us
  blocking collectives: 8.15 us -> 2.18 us
  matrix products: 10.5 us -> 5.22 us
  other arithmetic: 6.48 us -> 10.7 us
  local copies, waits for them, and re-layouts: 3.02 us -> 4 us
    all_to_all x6 -> x0, waiting for transfers between devices: 37.9 us -> none  [swap_all(): return lax.all_to_all(value, 'blk', 0, 0, axis_index_groups=groups)]
    ppermute x0 -> x18, starting transfers between devices: none -> 36.2 us  [routed(): return lax.ppermute(value, ('blk', 'rep'), pairs)]
    all_to_all x6 -> x0, starting transfers between devices: 23.9 us -> none  [swap_all(): return lax.all_to_all(value, 'blk', 0, 0, axis_index_groups=groups)]
    ppermute x0 -> x18, waiting for transfers between devices: none -> 6.26 us  [routed(): return lax.ppermute(value, ('blk', 'rep'), pairs)]
    all_gather x4 -> x1, blocking collectives: 8.15 us -> 2.18 us  [shards(): everyone = lax.all_gather(jnp.concatenate(arrived, 0), 'rep', axis=0)]
    dot_general x6 -> x4, matrix products: 10.5 us -> 5.22 us  [dot(): lax.dot_general(lhs, rhs, (dims, ((), ())), preferred_element_type=jnp.fl...]
    select_n x1 -> x5, other arithmetic: 1.05 us -> 4.62 us  [the longest x1 1.85 us: shards(): jnp.where(first_role, jnp.maximum(hidden_part, 0), group_part(cotangent, 1))]
    reduce_sum x4 -> x0, other arithmetic: 1.97 us -> none  [the longest x1 1.13 us: shards(): mixed_rows = jnp.sum(mixed_rows.astype(jnp.float32), 0).astype(bf16)]
  transfers between devices with their start and end apart: 6 -> 18, of which waited for: 6 -> 6; matrix products, arithmetic and copies ran while one was open for 13% -> 21% of each run, Pallas kernels for 0% -> 0%
where the time goes in v4:
time: 66.4 us; the launch traced here: 65.5 us
  starting transfers between devices  36.2 us (55%)
  other arithmetic  10.7 us (16%)
  waiting for transfers between devices  6.26 us (9%)
  matrix products  5.22 us (8%)
  local copies, waits for them, and re-layouts  4 us (6%)
  blocking collectives  2.18 us (3%)
  between operations  0.96 us (1%)
    ppermute x18, starting transfers between devices, routed(): return lax.ppermute(value, ('blk', 'rep'), pairs)  36.2 us
    ppermute x18, waiting for transfers between devices, routed(): return lax.ppermute(value, ('blk', 'rep'), pairs)  6.26 us
    dot_general x4, matrix products, dot(): lax.dot_general(lhs, rhs, (dims, ((), ())), preferred_element_type=jnp.fl...  5.22 us
    all_gather x1, blocking collectives, shards(): everyone = lax.all_gather(jnp.concatenate(arrived, 0), 'rep', axis=0)  2.18 us
    select_n x1, other arithmetic, shards(): jnp.where(first_role, jnp.maximum(hidden_part, 0), group_part(cotangent, 1))  1.85 us
  transfers between devices with their start and end apart: 18, of which 6 were waited for; matrix products, arithmetic and copies ran while one was open for 21% of the time, Pallas kernels for 0%

profile of v4, /device:TPU:0, one launch (start us, length us, event | category | flops | bytes accessed | tf_op | source)
XLA Modules:
  0.0 65.5 jit_solution(14485397455430271769)
XLA Ops:
  0.7 1.9 %maximum_select_fusion.4 = bf16[128,1024]{1,0:T(8,128)(2,1)} fusion(bf16[128,1024]{1,0:T(8,128)(2,1)} %param.9, bf16[128,1024]{1,0:T(8,128)(2,1)} %param.5, pred[]{:T(512)S(6)} %eq.61), kind=kLoop, calls=%fused_computation.33 | loop fusion | flops 262144 | bytes 786433 | tf_op jit(solution)/shard_map/jit(_where)/select_n | solution.py:60
  2.5 5.0 %collective-permute-start.2 = (bf16[128,1024]{1,0:T(8,128)(2,1)}, bf16[128,1024]{1,0:T(8,128)(2,1)}, u32[]{:S(2)}, u32[]{:S(2)}) collective-permute-start(bf16[128,1024]{1,0:T(8,128)(2,1)} %maximum_select_fusion.4), channel_id=1, source_target_pairs={{0,24},{2,26},{4,28},{6,30},{8,16},{10,18},{12,20},{14,22},{16,8},... | collective-permute-start | bytes 786440 | tf_op jit(solution)/shard_map/ppermute | solution.py:41
  8.2 1.0 %bitcast_convert_fusion = f32[8,128,128]{2,1,0:T(8,128)S(1)} fusion(bf16[1,8,128,128]{3,2,1,0:T(8,128)(2,1)} %param.6), kind=kLoop, calls=%fused_computation.32 | loop fusion | flops 131072 | bytes 786432 | tf_op jit(solution)/shard_map/jit(_where)/broadcast_in_dim | solution.py:72
  10.0 2.5 %collective-permute-start.5 = (bf16[128,256]{0,1:T(8,128)(2,1)S(1)}, bf16[128,256]{0,1:T(8,128)(2,1)S(1)}, u32[]{:S(2)}, u32[]{:S(2)}) collective-permute-start(bf16[128,256]{0,1:T(8,128)(2,1)S(1)} %bitcast.94), channel_id=1, source_target_pairs={{0,6},{2,4},{4,2},{6,0},{8,14},{10,12},{12,10},{14,8},{16,22},{18,... | collective-permute-start | bytes 196616 | tf_op jit(solution)/shard_map/ppermute | solution.py:41
  13.6 1.6 %collective-permute-done.5 = bf16[128,256]{0,1:T(8,128)(2,1)S(1)} collective-permute-done((bf16[128,256]{0,1:T(8,128)(2,1)S(1)}, bf16[128,256]{0,1:T(8,128)(2,1)S(1)}, u32[]{:S(2)}, u32[]{:S(2)}) %collective-permute-start.5) | collective-permute-done | bytes 65568 | tf_op jit(solution)/shard_map/ppermute | solution.py:41
  15.2 1.0 %collective-permute-start = (bf16[128,1024]{1,0:T(8,128)(2,1)}, bf16[128,1024]{1,0:T(8,128)(2,1)}, u32[]{:S(2)}, u32[]{:S(2)}) collective-permute-start(bf16[128,1024]{1,0:T(8,128)(2,1)} %maximum_select_fusion.4), channel_id=1, source_target_pairs={{0,8},{2,10},{4,12},{6,14},{8,0},{10,2},{12,4},{14,6},{16,24},{18,... | collective-permute-start | bytes 786440 | tf_op jit(solution)/shard_map/ppermute | solution.py:41
  16.8 1.2 %collective-permute-done.3 = bf16[128,256]{0,1:T(8,128)(2,1)S(1)} collective-permute-done((bf16[128,256]{0,1:T(8,128)(2,1)S(1)}, bf16[128,256]{0,1:T(8,128)(2,1)S(1)}, u32[]{:S(2)}, u32[]{:S(2)}) %collective-permute-start.3) | collective-permute-done | bytes 65568 | tf_op jit(solution)/shard_map/ppermute | solution.py:41
  18.0 2.2 %all-gather = bf16[1024,256]{0,1:T(8,128)(2,1)S(1)} all-gather(bf16[512,256]{0,1:T(8,128)(2,1)S(1)} %pad_maximum_fusion.3), channel_id=2, replica_groups=mesh['blk'=16,'rep'=2] {'rep'}, dimensions={0}, use_global_device_ids=true | all-gather | bytes 786432 | tf_op jit(solution)/shard_map/all_gather | solution.py:81
  20.8 1.0 %copy.13 = bf16[512,512]{0,1:T(8,128)(2,1)} copy(bf16[512,512]{1,0:T(8,128)(2,1)S(1)} %pad_maximum_fusion.1) | data formatting | bytes 1048576 | tf_op jit(solution)/shard_map/concatenate | solution.py:94
  21.8 1.1 %collective-permute-done = bf16[128,1024]{1,0:T(8,128)(2,1)} collective-permute-done((bf16[128,1024]{1,0:T(8,128)(2,1)}, bf16[128,1024]{1,0:T(8,128)(2,1)}, u32[]{:S(2)}, u32[]{:S(2)}) %collective-permute-start) | collective-permute-done | bytes 262176 | tf_op jit(solution)/shard_map/ppermute | solution.py:41
  22.9 2.1 %convolution_convert_fusion = bf16[1024,512]{1,0:T(8,128)(2,1)S(1)} fusion(bf16[512,512]{0,1:T(8,128)(2,1)} %copy.13, pred[]{:T(512)S(6)} %eq.61, bf16[128,1024]{1,0:T(8,128)(2,1)} %collective-permute-done.2, bf16[128,1024]{1,0:T(8,128)(2,1)} %collective-permute-done.1, bf16[128,1024]{1,0:T(8,128)(2,1)} %collective-permute-done, ...), kind=kOutput, calls=%fused_computation.1 | convolution fusion | flops 543948800 | bytes 3145729 | tf_op jit(solution)/shard_map/dot_general | solution.py:44
  25.4 0.8 %maximum_select_fusion = bf16[1024,128]{1,0:T(8,128)(2,1)} fusion(bf16[256,128]{1,0:T(8,128)(2,1)S(1)} %get-tuple-element.27, bf16[256,128]{1,0:T(8,128)(2,1)S(1)} %get-tuple-element.28, bf16[256,128]{1,0:T(8,128)(2,1)S(1)} %get-tuple-element.29, bf16[256,128]{1,0:T(8,128)(2,1)S(1)} %get-tuple-element.26, pred[]{:T(512)S(6)} %eq.61, ...), kind=kLoop, calls=%fused_computation.18 | loop fusion | flops 1179648 | bytes 786433 | tf_op jit(solution)/shard_map/jit(_where)/select_n | solution.py:110
  26.2 1.3 %fusion.38 = (bf16[1024,128]{1,0:T(8,128)(2,1)}, bf16[1024,128]{1,0:T(8,128)(2,1)}, bf16[1024,128]{1,0:T(8,128)(2,1)}, bf16[1024,128]{1,0:T(8,128)(2,1)}, bf16[1...) fusion(bf16[1024,512]{1,0:T(8,128)(2,1)S(1)} %convolution_convert_fusion, bf16[256,128]{1,0:T(8,128)(2,1)S(1)} %get-tuple-element.31, ...), kind=kLoop, calls=%fused_computation.117 | loop fusion | flops 3538944 | bytes 3145729 | tf_op jit(solution)/shard_map/slice | solution.py:98
  27.4 1.6 %collective-permute-start.10 = (bf16[1024,128]{1,0:T(8,128)(2,1)}, bf16[1024,128]{1,0:T(8,128)(2,1)}, u32[]{:S(2)}, u32[]{:S(2)}) collective-permute-start(bf16[1024,128]{1,0:T(8,128)(2,1)} %get-tuple-element.4), channel_id=1, source_target_pairs={{0,3},{2,1},{4,7},{6,5},{8,11},{10,9},{12,15},{14,13},{16,19},{18,... | collective-permute-start | bytes 786440 | tf_op jit(solution)/shard_map/ppermute | solution.py:41
  29.1 3.2 %collective-permute-start.12 = (bf16[1024,128]{1,0:T(8,128)(2,1)}, bf16[1024,128]{1,0:T(8,128)(2,1)}, u32[]{:S(2)}, u32[]{:S(2)}) collective-permute-start(bf16[1024,128]{1,0:T(8,128)(2,1)} %get-tuple-element.6), channel_id=1, source_target_pairs={{0,7},{2,5},{4,3},{6,1},{8,15},{10,13},{12,11},{14,9},{16,23},{18,... | collective-permute-start | bytes 786440 | tf_op jit(solution)/shard_map/ppermute | solution.py:41
  32.2 4.0 %collective-permute-start.6 = (bf16[1024,128]{1,0:T(8,128)(2,1)}, bf16[1024,128]{1,0:T(8,128)(2,1)S(1)}, u32[]{:S(2)}, u32[]{:S(2)}) collective-permute-start(bf16[1024,128]{1,0:T(8,128)(2,1)} %get-tuple-element.3), channel_id=1, source_target_pairs={{0,2},{2,0},{4,6},{6,4},{8,10},{10,8},{12,14},{14,12},{16,18},{18,... | collective-permute-start | bytes 786440 | tf_op jit(solution)/shard_map/ppermute | solution.py:41
  36.3 1.9 %collective-permute-start.8 = (bf16[1024,128]{1,0:T(8,128)(2,1)}, bf16[1024,128]{1,0:T(8,128)(2,1)S(1)}, u32[]{:S(2)}, u32[]{:S(2)}) collective-permute-start(bf16[1024,128]{1,0:T(8,128)(2,1)} %get-tuple-element.7), channel_id=1, source_target_pairs={{0,6},{2,4},{4,2},{6,0},{8,14},{10,12},{12,10},{14,8},{16,22},{18,... | collective-permute-start | bytes 786440 | tf_op jit(solution)/shard_map/ppermute | solution.py:41
  38.2 3.4 %collective-permute-start.7 = (bf16[1024,128]{1,0:T(8,128)(2,1)}, bf16[1024,128]{1,0:T(8,128)(2,1)S(1)}, u32[]{:S(2)}, u32[]{:S(2)}) collective-permute-start(bf16[1024,128]{1,0:T(8,128)(2,1)} %get-tuple-element.8), channel_id=1, source_target_pairs={{0,4},{2,6},{4,0},{6,2},{8,12},{10,14},{12,8},{14,10},{16,20},{18,... | collective-permute-start | bytes 786440 | tf_op jit(solution)/shard_map/ppermute | solution.py:41
  41.7 1.2 %add_convert_fusion = bf16[1024,128]{1,0:T(8,128)(2,1)S(1)} fusion(bf16[1024,128]{1,0:T(8,128)(2,1)} %collective-permute-done.12, bf16[1024,128]{1,0:T(8,128)(2,1)} %collective-permute-done.11, bf16[1024,128]{1,0:T(8,128)(2,1)} %collective-permute-done.10, bf16[1024,128]{1,0:T(8,128)(2,1)S(1)} %collective-permute-done.9), kind=kLoop, calls=%fused_computation.11 | loop fusion | flops 1048576 | bytes 1310720 | tf_op jit(solution)/shard_map/convert_element_type | solution.py:115
  43.0 1.7 %convolution_convert_fusion.1 = bf16[256,1024]{1,0:T(8,128)(2,1)S(1)} fusion(bf16[256,128]{1,0:T(8,128)(2,1)S(1)} %get-tuple-element.23, bf16[256,128]{1,0:T(8,128)(2,1)S(1)} %get-tuple-element.24, bf16[256,128]{1,0:T(8,128)(2,1)S(1)} %get-tuple-element.25, bf16[256,128]{1,0:T(8,128)(2,1)S(1)} %get-tuple-element.22, ...), kind=kOutput, calls=%fused_computation.2 | convolution fusion | flops 273940480 | bytes 1835008 | tf_op jit(solution)/shard_map/dot_general | solution.py:44
  44.7 0.8 %dynamic-slice_bitcast_fusion.2 = (bf16[64,1024]{1,0:T(8,128)(2,1)}, bf16[64,1024]{1,0:T(8,128)(2,1)}, bf16[64,1024]{1,0:T(8,128)(2,1)S(1)}) fusion(bf16[4,64,1024]{2,1,0:T(8,128)(2,1)S(1)} %bitcast.89, s32[]{:T(128)S(6)} %select_n.233, s32[]{:T(128)S(6)} %select_n.235, s32[]{:T(128)S(6)} %select_n.234), kind=kLoop, calls=%fused_computation.42 | loop fusion | bytes 786444 | tf_op jit(solution)/shard_map/jit(dynamic_index_in_dim)/squeeze | solution.py:126
  45.5 1.3 %collective-permute-start.14 = (bf16[64,1024]{1,0:T(8,128)(2,1)}, bf16[64,1024]{1,0:T(8,128)(2,1)}, u32[]{:S(2)}, u32[]{:S(2)}) collective-permute-start(bf16[64,1024]{1,0:T(8,128)(2,1)} %get-tuple-element.13), channel_id=1, source_target_pairs={{1,9},{3,11},{5,13},{7,15},{9,1},{11,3},{13,5},{15,7},{17,25},{19,... | collective-permute-start | bytes 393224 | tf_op jit(solution)/shard_map/ppermute | solution.py:41
  46.8 1.3 %collective-permute-start.16 = (bf16[64,1024]{1,0:T(8,128)(2,1)}, bf16[64,1024]{1,0:T(8,128)(2,1)}, u32[]{:S(2)}, u32[]{:S(2)}) collective-permute-start(bf16[64,1024]{1,0:T(8,128)(2,1)} %get-tuple-element.14), channel_id=1, source_target_pairs={{1,25},{3,27},{5,29},{7,31},{9,17},{11,19},{13,21},{15,23},{17,9},... | collective-permute-start | bytes 393224 | tf_op jit(solution)/shard_map/ppermute | solution.py:41
  48.2 0.8 %fusion = bf16[128,1024]{1,0:T(8,128)(2,1)S(1)} fusion(bf16[1024,128]{1,0:T(8,128)(2,1)S(1)} %add_convert_fusion, bf16[1024,1024]{1,0:T(8,128)(2,1)S(1)} %copy-done, bf16[128,1024]{1,0:T(8,128)(2,1)S(1)} %copy-done.2), kind=kOutput, calls=%fused_computation.5 | convolution fusion | flops 268828672 | bytes 2883584 | tf_op jit(solution)/shard_map/dot_general | solution.py:44
  49.0 1.3 %collective-permute-start.15 = (bf16[64,1024]{1,0:T(8,128)(2,1)S(1)}, bf16[64,1024]{1,0:T(8,128)(2,1)}, u32[]{:S(2)}, u32[]{:S(2)}) collective-permute-start(bf16[64,1024]{1,0:T(8,128)(2,1)S(1)} %get-tuple-element.15), channel_id=1, source_target_pairs={{1,17},{3,19},{5,21},{7,23},{9,25},{11,27},{13,29},{15,31},{17,1},... | collective-permute-start | bytes 393224 | tf_op jit(solution)/shard_map/ppermute | solution.py:41
  50.9 0.7 %copy-done.1 = bf16[128,1024]{1,0:T(8,128)(2,1)} copy-done((bf16[128,1024]{1,0:T(8,128)(2,1)}, bf16[128,1024]{1,0:T(8,128)(2,1)S(1)}, u32[]{:S(2)}) %copy-start.1) | copy-done | bytes 262168
  51.7 7.2 %collective-permute-start.13 = (bf16[256,512]{1,0:T(8,128)(2,1)S(1)}, bf16[256,512]{1,0:T(8,128)(2,1)S(1)}, u32[]{:S(2)}, u32[]{:S(2)}) collective-permute-start(bf16[256,512]{1,0:T(8,128)(2,1)S(1)} %pad_maximum_fusion.2), channel_id=1, source_target_pairs={{0,1},{2,3},{4,5},{6,7},{8,9},{10,11},{12,13},{14,15},{16,17},{18,... | collective-permute-start | bytes 786440 | tf_op jit(solution)/shard_map/ppermute | solution.py:41
  58.9 1.2 %fusion.12 = f32[64,1024]{1,0:T(8,128)S(1)} fusion(bf16[64,1024]{1,0:T(8,128)(2,1)} %collective-permute-done.16, bf16[64,1024]{1,0:T(8,128)(2,1)} %collective-permute-done.15, bf16[64,1024]{1,0:T(8,128)(2,1)} %collective-permute-done.14, bf16[4,64,1024]{2,1,0:T(8,128)(2,1)} %bitcast.90, s32[]{:T(128)S(6)} %select_n.232), kind=kLoop, calls=%fused_computation.31 | loop fusion | flops 458752 | bytes 786436 | tf_op jit(solution)/shard_map/add | solution.py:47
  60.1 1.3 %collective-permute-start.17 = (f32[64,512]{1,0:T(8,128)S(1)}, f32[64,512]{1,0:T(8,128)S(1)}, u32[]{:S(2)}, u32[]{:S(2)}) collective-permute-start(f32[64,512]{1,0:T(8,128)S(1)} %slice.195), channel_id=1, source_target_pairs={{1,0},{3,2},{5,4},{7,6},{9,8},{11,10},{13,12},{15,14},{17,16},{19,... | collective-permute-start | bytes 393224 | tf_op jit(solution)/shard_map/ppermute | solution.py:41
  61.4 1.0 %fusion.3 = bf16[256,512]{1,0:T(8,128)(2,1)S(1)} fusion(bf16[256,512]{1,0:T(8,128)(2,1)S(1)} %collective-permute-done.13, bf16[128,1024]{1,0:T(8,128)(2,1)} %copy-done.1, bf16[128,1024]{1,0:T(8,128)(2,1)S(1)} %fusion, pred[]{:T(512)S(6)} %eq.61), kind=kLoop, calls=%fused_computation.15 | loop fusion | flops 655360 | bytes 1048577 | tf_op jit(solution)/shard_map/jit(_where)/select_n | solution.py:134
  62.4 0.7 %fusion.39 = (bf16[128,512]{1,0:T(8,128)(2,1)}, bf16[128,512]{1,0:T(8,128)(2,1)}) fusion(bf16[256,512]{1,0:T(8,128)(2,1)S(1)} %fusion.3), kind=kLoop, calls=%fused_computation.118 | loop fusion | bytes 524288 | tf_op jit(solution)/shard_map/slice | solution.py:142
  63.1 1.7 %collective-permute-done.17 = f32[64,512]{1,0:T(8,128)S(1)} collective-permute-done((f32[64,512]{1,0:T(8,128)S(1)}, f32[64,512]{1,0:T(8,128)S(1)}, u32[]{:S(2)}, u32[]{:S(2)}) %collective-permute-start.17) | collective-permute-done | bytes 131104 | tf_op jit(solution)/shard_map/ppermute | solution.py:41
  (49 shorter events, 5.5 us)
Async XLA Ops:
  0.6 47.5 %copy-start = (bf16[1024,1024]{1,0:T(8,128)(2,1)S(1)}, bf16[1024,1024]{1,0:T(8,128)(2,1)}, u32[]{:S(2)}) copy-start(bf16[1024,1024]{1,0:T(8,128)(2,1)} %param.8) | copy-start | bytes 6291460
  2.5 19.3 %collective-permute-start.2 = (bf16[128,1024]{1,0:T(8,128)(2,1)}, bf16[128,1024]{1,0:T(8,128)(2,1)}, u32[]{:S(2)}, u32[]{:S(2)}) collective-permute-start(bf16[128,1024]{1,0:T(8,128)(2,1)} %maximum_select_fusion.4), channel_id=1, source_target_pairs={{0,24},{2,26},{4,28},{6,30},{8,16},{10,18},{12,20},{14,22},{16,8},... | collective-permute-start | bytes 786440 | tf_op jit(solution)/shard_map/ppermute | solution.py:41
  7.6 14.3 %collective-permute-start.1 = (bf16[128,1024]{1,0:T(8,128)(2,1)}, bf16[128,1024]{1,0:T(8,128)(2,1)}, u32[]{:S(2)}, u32[]{:S(2)}) collective-permute-start(bf16[128,1024]{1,0:T(8,128)(2,1)} %maximum_select_fusion.4), channel_id=1, source_target_pairs={{0,16},{2,18},{4,20},{6,22},{8,24},{10,26},{12,28},{14,30},{16,0},... | collective-permute-start | bytes 786440 | tf_op jit(solution)/shard_map/ppermute | solution.py:41
  10.0 5.2 %collective-permute-start.5 = (bf16[128,256]{0,1:T(8,128)(2,1)S(1)}, bf16[128,256]{0,1:T(8,128)(2,1)S(1)}, u32[]{:S(2)}, u32[]{:S(2)}) collective-permute-start(bf16[128,256]{0,1:T(8,128)(2,1)S(1)} %bitcast.94), channel_id=1, source_target_pairs={{0,6},{2,4},{4,2},{6,0},{8,14},{10,12},{12,10},{14,8},{16,22},{18,... | collective-permute-start | bytes 196616 | tf_op jit(solution)/shard_map/ppermute | solution.py:41
  12.5 4.3 %collective-permute-start.4 = (bf16[128,256]{0,1:T(8,128)(2,1)S(1)}, bf16[128,256]{0,1:T(8,128)(2,1)S(1)}, u32[]{:S(2)}, u32[]{:S(2)}) collective-permute-start(bf16[128,256]{0,1:T(8,128)(2,1)S(1)} %bitcast.93), channel_id=1, source_target_pairs={{0,4},{2,6},{4,0},{6,2},{8,12},{10,14},{12,8},{14,10},{16,20},{18,... | collective-permute-start | bytes 196616 | tf_op jit(solution)/shard_map/ppermute | solution.py:41
  13.0 4.9 %collective-permute-start.3 = (bf16[128,256]{0,1:T(8,128)(2,1)S(1)}, bf16[128,256]{0,1:T(8,128)(2,1)S(1)}, u32[]{:S(2)}, u32[]{:S(2)}) collective-permute-start(bf16[128,256]{0,1:T(8,128)(2,1)S(1)} %bitcast.92), channel_id=1, source_target_pairs={{0,2},{2,0},{4,6},{6,4},{8,10},{10,8},{12,14},{14,12},{16,18},{18,... | collective-permute-start | bytes 196616 | tf_op jit(solution)/shard_map/ppermute | solution.py:41
  15.2 7.7 %collective-permute-start = (bf16[128,1024]{1,0:T(8,128)(2,1)}, bf16[128,1024]{1,0:T(8,128)(2,1)}, u32[]{:S(2)}, u32[]{:S(2)}) collective-permute-start(bf16[128,1024]{1,0:T(8,128)(2,1)} %maximum_select_fusion.4), channel_id=1, source_target_pairs={{0,8},{2,10},{4,12},{6,14},{8,0},{10,2},{12,4},{14,6},{16,24},{18,... | collective-permute-start | bytes 786440 | tf_op jit(solution)/shard_map/ppermute | solution.py:41
  20.7 1.1 %copy-start.4 = (bf16[512,128]{1,0:T(8,128)(2,1)}, bf16[512,128]{1,0:T(8,128)(2,1)S(1)}, u32[]{:S(2)}) copy-start(bf16[512,128]{1,0:T(8,128)(2,1)S(1)} %get-tuple-element.19) | copy-start | bytes 393220
  26.1 10.1 %collective-permute-start.9 = (bf16[1024,128]{1,0:T(8,128)(2,1)}, bf16[1024,128]{1,0:T(8,128)(2,1)S(1)}, u32[]{:S(2)}, u32[]{:S(2)}) collective-permute-start(bf16[1024,128]{1,0:T(8,128)(2,1)} %maximum_select_fusion), channel_id=1, source_target_pairs={{0,1},{2,3},{4,5},{6,7},{8,9},{10,11},{12,13},{14,15},{16,17},{18,... | collective-permute-start | bytes 786440 | tf_op jit(solution)/shard_map/ppermute | solution.py:41
  27.4 10.8 %collective-permute-start.10 = (bf16[1024,128]{1,0:T(8,128)(2,1)}, bf16[1024,128]{1,0:T(8,128)(2,1)}, u32[]{:S(2)}, u32[]{:S(2)}) collective-permute-start(bf16[1024,128]{1,0:T(8,128)(2,1)} %get-tuple-element.4), channel_id=1, source_target_pairs={{0,3},{2,1},{4,7},{6,5},{8,11},{10,9},{12,15},{14,13},{16,19},{18,... | collective-permute-start | bytes 786440 | tf_op jit(solution)/shard_map/ppermute | solution.py:41
  29.0 12.7 %collective-permute-start.11 = (bf16[1024,128]{1,0:T(8,128)(2,1)}, bf16[1024,128]{1,0:T(8,128)(2,1)}, u32[]{:S(2)}, u32[]{:S(2)}) collective-permute-start(bf16[1024,128]{1,0:T(8,128)(2,1)} %get-tuple-element.5), channel_id=1, source_target_pairs={{0,5},{2,7},{4,1},{6,3},{8,13},{10,15},{12,9},{14,11},{16,21},{18,... | collective-permute-start | bytes 786440 | tf_op jit(solution)/shard_map/ppermute | solution.py:41
  29.1 12.6 %collective-permute-start.12 = (bf16[1024,128]{1,0:T(8,128)(2,1)}, bf16[1024,128]{1,0:T(8,128)(2,1)}, u32[]{:S(2)}, u32[]{:S(2)}) collective-permute-start(bf16[1024,128]{1,0:T(8,128)(2,1)} %get-tuple-element.6), channel_id=1, source_target_pairs={{0,7},{2,5},{4,3},{6,1},{8,15},{10,13},{12,11},{14,9},{16,23},{18,... | collective-permute-start | bytes 786440 | tf_op jit(solution)/shard_map/ppermute | solution.py:41
  32.2 16.8 %collective-permute-start.6 = (bf16[1024,128]{1,0:T(8,128)(2,1)}, bf16[1024,128]{1,0:T(8,128)(2,1)S(1)}, u32[]{:S(2)}, u32[]{:S(2)}) collective-permute-start(bf16[1024,128]{1,0:T(8,128)(2,1)} %get-tuple-element.3), channel_id=1, source_target_pairs={{0,2},{2,0},{4,6},{6,4},{8,10},{10,8},{12,14},{14,12},{16,18},{18,... | collective-permute-start | bytes 786440 | tf_op jit(solution)/shard_map/ppermute | solution.py:41
  36.3 14.0 %collective-permute-start.8 = (bf16[1024,128]{1,0:T(8,128)(2,1)}, bf16[1024,128]{1,0:T(8,128)(2,1)S(1)}, u32[]{:S(2)}, u32[]{:S(2)}) collective-permute-start(bf16[1024,128]{1,0:T(8,128)(2,1)} %get-tuple-element.7), channel_id=1, source_target_pairs={{0,6},{2,4},{4,2},{6,0},{8,14},{10,12},{12,10},{14,8},{16,22},{18,... | collective-permute-start | bytes 786440 | tf_op jit(solution)/shard_map/ppermute | solution.py:41
  38.2 12.1 %collective-permute-start.7 = (bf16[1024,128]{1,0:T(8,128)(2,1)}, bf16[1024,128]{1,0:T(8,128)(2,1)S(1)}, u32[]{:S(2)}, u32[]{:S(2)}) collective-permute-start(bf16[1024,128]{1,0:T(8,128)(2,1)} %get-tuple-element.8), channel_id=1, source_target_pairs={{0,4},{2,6},{4,0},{6,2},{8,12},{10,14},{12,8},{14,10},{16,20},{18,... | collective-permute-start | bytes 786440 | tf_op jit(solution)/shard_map/ppermute | solution.py:41
  43.0 5.1 %copy-start.2 = (bf16[128,1024]{1,0:T(8,128)(2,1)S(1)}, bf16[128,1024]{1,0:T(8,128)(2,1)}, u32[]{:S(2)}) copy-start(bf16[128,1024]{1,0:T(8,128)(2,1)} %param.5) | copy-start | bytes 786436
  44.7 2.1 %copy-start.3 = (bf16[256,1024]{1,0:T(8,128)(2,1)}, bf16[256,1024]{1,0:T(8,128)(2,1)S(1)}, u32[]{:S(2)}) copy-start(bf16[256,1024]{1,0:T(8,128)(2,1)S(1)} %convolution_convert_fusion.1) | copy-start | bytes 1572868
  45.5 13.4 %collective-permute-start.14 = (bf16[64,1024]{1,0:T(8,128)(2,1)}, bf16[64,1024]{1,0:T(8,128)(2,1)}, u32[]{:S(2)}, u32[]{:S(2)}) collective-permute-start(bf16[64,1024]{1,0:T(8,128)(2,1)} %get-tuple-element.13), channel_id=1, source_target_pairs={{1,9},{3,11},{5,13},{7,15},{9,1},{11,3},{13,5},{15,7},{17,25},{19,... | collective-permute-start | bytes 393224 | tf_op jit(solution)/shard_map/ppermute | solution.py:41
  46.8 12.1 %collective-permute-start.16 = (bf16[64,1024]{1,0:T(8,128)(2,1)}, bf16[64,1024]{1,0:T(8,128)(2,1)}, u32[]{:S(2)}, u32[]{:S(2)}) collective-permute-start(bf16[64,1024]{1,0:T(8,128)(2,1)} %get-tuple-element.14), channel_id=1, source_target_pairs={{1,25},{3,27},{5,29},{7,31},{9,17},{11,19},{13,21},{15,23},{17,9},... | collective-permute-start | bytes 393224 | tf_op jit(solution)/shard_map/ppermute | solution.py:41
  49.0 9.9 %collective-permute-start.15 = (bf16[64,1024]{1,0:T(8,128)(2,1)S(1)}, bf16[64,1024]{1,0:T(8,128)(2,1)}, u32[]{:S(2)}, u32[]{:S(2)}) collective-permute-start(bf16[64,1024]{1,0:T(8,128)(2,1)S(1)} %get-tuple-element.15), channel_id=1, source_target_pairs={{1,17},{3,19},{5,21},{7,23},{9,25},{11,27},{13,29},{15,31},{17,1},... | collective-permute-start | bytes 393224 | tf_op jit(solution)/shard_map/ppermute | solution.py:41
  50.9 0.7 %copy-start.1 = (bf16[128,1024]{1,0:T(8,128)(2,1)}, bf16[128,1024]{1,0:T(8,128)(2,1)S(1)}, u32[]{:S(2)}) copy-start(bf16[128,1024]{1,0:T(8,128)(2,1)S(1)} %convolution_convert_fusion.2) | copy-start | bytes 786436
  51.7 9.7 %collective-permute-start.13 = (bf16[256,512]{1,0:T(8,128)(2,1)S(1)}, bf16[256,512]{1,0:T(8,128)(2,1)S(1)}, u32[]{:S(2)}, u32[]{:S(2)}) collective-permute-start(bf16[256,512]{1,0:T(8,128)(2,1)S(1)} %pad_maximum_fusion.2), channel_id=1, source_target_pairs={{0,1},{2,3},{4,5},{6,7},{8,9},{10,11},{12,13},{14,15},{16,17},{18,... | collective-permute-start | bytes 786440 | tf_op jit(solution)/shard_map/ppermute | solution.py:41
  60.1 4.7 %collective-permute-start.17 = (f32[64,512]{1,0:T(8,128)S(1)}, f32[64,512]{1,0:T(8,128)S(1)}, u32[]{:S(2)}, u32[]{:S(2)}) collective-permute-start(f32[64,512]{1,0:T(8,128)S(1)} %slice.195), channel_id=1, source_target_pairs={{1,0},{3,2},{5,4},{7,6},{9,8},{11,10},{13,12},{15,14},{17,16},{19,... | collective-permute-start | bytes 393224 | tf_op jit(solution)/shard_map/ppermute | solution.py:41

commit v5 on v2

v5 whole, which is shorter than its diff:
```python
import jax
import jax.numpy as jnp
from jax import lax
from jax.sharding import PartitionSpec as P


def shards(hidden_pre, adj_vals, adj_cols, w_out, cotangent):
    feature_width = hidden_pre.shape[1]
    tile_size = adj_vals.shape[2]
    blk_count = lax.axis_size("blk")
    rep_count = lax.axis_size("rep")
    section_span = blk_count // rep_count
    side = 1 << ((blk_count.bit_length() - 1) // 2)
    per_core = section_span // side
    blk_pos = lax.axis_index("blk")
    rep_pos = lax.axis_index("rep")
    outer_pos, inner_pos = blk_pos // side, blk_pos % side
    cols_here = feature_width // rep_count
    rows_here = feature_width // blk_count
    bf16 = jnp.bfloat16
    turns = range(side)

    def along_inner(value, turn):
        pairs = [(o * side + i, o * side + (i ^ turn)) for o in turns for i in turns]
        return lax.ppermute(value, "blk", pairs) if turn else value

    def along_outer(value, turn):
        pairs = [(o * side + i, (o ^ turn) * side + i) for o in turns for i in turns]
        return lax.ppermute(value, "blk", pairs) if turn else value

    def dot(lhs, rhs, dims):
        return lax.dot_general(lhs, rhs, (dims, ((), ())), preferred_element_type=jnp.float32)

    def summed(parts):
        return sum(part.astype(jnp.float32) for part in parts)

    def lanes(value, index):
        return value[:, index * tile_size : (index + 1) * tile_size]

    hidden_part = jnp.maximum(
        lax.dynamic_slice_in_dim(hidden_pre, rep_pos * cols_here, cols_here, 1), 0
    )
    hidden_stack = jnp.concatenate([along_outer(hidden_part, e) for e in turns], 0)

    columns = adj_cols[0]
    place = ((columns % side) ^ inner_pos) * per_core + ((columns // side) ^ outer_pos) % per_core
    hit = place[None, :] == jnp.arange(section_span, dtype=jnp.int32)[:, None]
    ordered = jnp.sum(
        jnp.where(hit[:, :, None, None], adj_vals[0][None].astype(jnp.float32), 0.0), axis=1
    ).astype(bf16)
    grad_part = lax.dynamic_slice_in_dim(cotangent, rep_pos * cols_here, cols_here, 1)
    arrived = []
    for t in turns:
        message = [ordered[t * per_core + m] for m in range(per_core)] + [grad_part]
        arrived.append(along_inner(jnp.concatenate(message, 1), t))
    arrived = jnp.concatenate(arrived, 0)
    held = per_core * tile_size
    grad_stack = arrived[:, held:]
    everyone = lax.all_gather(arrived[:, :held], "rep", axis=0)

    turn_of_row = jnp.repeat(jnp.arange(side, dtype=jnp.int32), tile_size)
    row_block = outer_pos * side + (inner_pos ^ turn_of_row)
    pieces = []
    for e in turns:
        holder = jnp.mod(row_block - (outer_pos ^ e) * side - inner_pos, blk_count) // section_span
        piece = lanes(everyone[0], e % per_core)
        for r in range(1, rep_count):
            piece = jnp.where((holder == r)[:, None], lanes(everyone[r], e % per_core), piece)
        pieces.append(piece)
    block = jnp.concatenate(pieces, 1)

    back_stack = dot(block, grad_stack, ((0,), (0,))).astype(bf16)
    back_part = summed(
        [along_outer(back_stack[e * tile_size : (e + 1) * tile_size], e) for e in turns]
    ).astype(bf16)

    mixed = dot(hidden_stack, block, ((0,), (1,))).astype(bf16)
    share = cols_here // side
    by_owner = mixed.reshape(share // rows_here, side, rows_here, side * tile_size)
    exchanged = []
    for t in turns:
        chosen = lax.dynamic_index_in_dim(by_owner, inner_pos ^ t, 1, keepdims=False)
        chosen = chosen.reshape(share, side * tile_size)
        message = [lanes(mixed, t)] + [lanes(chosen, u ^ t) for u in turns]
        exchanged.append(along_inner(jnp.concatenate(message, 0), t))
    exchanged = summed(exchanged).astype(bf16)
    exchanged = lax.all_gather(exchanged, "rep", axis=0)
    mixed_rows = exchanged[:, :cols_here].reshape(feature_width, tile_size)
    mixed_cols = exchanged[:, cols_here:].reshape(rep_count, side, share, tile_size)
    mixed_cols = mixed_cols.transpose(0, 2, 1, 3).reshape(rep_count * share, side * tile_size)

    weight_part = dot(mixed_cols, grad_stack, ((1,), (0,))).astype(bf16)
    weight_part = weight_part.reshape(side, rows_here, cols_here)
    grad_weight = summed(
        [
            along_outer(
                lax.dynamic_index_in_dim(weight_part, outer_pos ^ t, 0, keepdims=False), t
            )
            for t in turns
        ]
    )

    w_columns = lax.dynamic_slice_in_dim(w_out, rep_pos * cols_here, cols_here, 1)
    out_part = dot(mixed_rows, w_columns, ((0,), (0,))).astype(bf16)

    back_full = lax.all_gather(back_part, "rep", axis=1, tiled=True)
    w_rows = lax.dynamic_slice_in_dim(w_out, rep_pos * cols_here, cols_here, 0)
    grad_in = dot(back_full, w_rows, ((1,), (1,)))
    pre_part = lax.dynamic_slice_in_dim(hidden_pre, rep_pos * cols_here, cols_here, 1)
    grad_pre = jnp.where(pre_part > 0, grad_in, 0.0).astype(bf16)
    return (out_part, grad_weight, grad_pre)


def solution(mesh):
    placed = (P("blk", None), P("blk", "rep", None, None), P("blk", "rep"), P(), P("blk", None))
    return jax.shard_map(
        shards,
        mesh=mesh,
        in_specs=placed,
        out_specs=(P("blk", "rep"), P("blk", "rep"), P("blk", "rep")),
        check_vma=False,
    )
```

time: 91.4 us -> 60.5 us (0.66)
  waiting for transfers between devices: 37.9 us -> 20.6 us
  matrix products: 10.5 us -> 4.42 us
  starting transfers between devices: 23.9 us -> 21.1 us
  blocking collectives: 8.15 us -> 6.36 us
  local copies, waits for them, and re-layouts: 3.02 us -> 1.62 us
  other arithmetic: 6.48 us -> 5.29 us
    all_to_all x6 -> x0, waiting for transfers between devices: 37.9 us -> none  [swap_all(): return lax.all_to_all(value, 'blk', 0, 0, axis_index_groups=groups)]
    all_to_all x6 -> x0, starting transfers between devices: 23.9 us -> none  [swap_all(): return lax.all_to_all(value, 'blk', 0, 0, axis_index_groups=groups)]
    ppermute x0 -> x15, starting transfers between devices: none -> 21.1 us  [the longest x9 13.9 us: along_outer(): return lax.ppermute(value, 'blk', pairs) if turn else value]
    ppermute x0 -> x15, waiting for transfers between devices: none -> 20.6 us  [the longest x9 11 us: along_outer(): return lax.ppermute(value, 'blk', pairs) if turn else value]
    dot_general x6 -> x5, matrix products: 10.5 us -> 4.42 us  [dot(): lax.dot_general(lhs, rhs, (dims, ((), ())), preferred_element_type=jnp.fl...]
    reduce_sum x4 -> x0, other arithmetic: 1.97 us -> none  [the longest x1 1.13 us: shards(): mixed_rows = jnp.sum(mixed_rows.astype(jnp.float32), 0).astype(bf16)]
    all_gather x3 -> x2, blocking collectives: 6.16 us -> 4.36 us  [the longest x1 2.18 us: shards(): everyone = lax.all_gather(arrived[:, :held], 'rep', axis=0)]
    max x1, other arithmetic: 0.02 us -> 1.73 us  [shards(): jnp.maximum(lax.dynamic_slice_in_dim(hidden_pre, rep_pos * cols_here, col...]
  transfers between devices with their start and end apart: 6 -> 15, of which waited for: 6 -> 8; matrix products, arithmetic and copies ran while one was open for 13% -> 14% of each run, Pallas kernels for 0% -> 0%
where the time goes in v5:
time: 60.5 us; the launch traced here: 60.3 us
  starting transfers between devices  21.1 us (35%)
  waiting for transfers between devices  20.6 us (34%)
  blocking collectives  6.36 us (11%)
  other arithmetic  5.29 us (9%)
  matrix products  4.42 us (7%)
  local copies, waits for them, and re-layouts  1.62 us (3%)
  between operations  0.88 us (1%)
    ppermute x9, starting transfers between devices, along_outer(): return lax.ppermute(value, 'blk', pairs) if turn else value  13.9 us
    ppermute x9, waiting for transfers between devices, along_outer(): return lax.ppermute(value, 'blk', pairs) if turn else value  11 us
    ppermute x6, waiting for transfers between devices, along_inner(): return lax.ppermute(value, 'blk', pairs) if turn else value  9.57 us
    ppermute x6, starting transfers between devices, along_inner(): return lax.ppermute(value, 'blk', pairs) if turn else value  7.17 us
    dot_general x5, matrix products, dot(): lax.dot_general(lhs, rhs, (dims, ((), ())), preferred_element_type=jnp.fl...  4.42 us
    all_gather x1, blocking collectives, shards(): everyone = lax.all_gather(arrived[:, :held], 'rep', axis=0)  2.18 us
    all_gather x1, blocking collectives, shards(): exchanged = lax.all_gather(exchanged, 'rep', axis=0)  2.18 us
    all_gather x1, blocking collectives, shards(): back_full = lax.all_gather(back_part, 'rep', axis=1, tiled=True)  1.99 us
  transfers between devices with their start and end apart: 15, of which 8 were waited for; matrix products, arithmetic and copies ran while one was open for 14% of the time, Pallas kernels for 0%

profile of v5, /device:TPU:0, one launch (start us, length us, event | category | flops | bytes accessed | tf_op | source)
XLA Modules:
  0.0 60.3 jit_solution(339374860438006428)
XLA Ops:
  0.7 1.7 %dynamic-slice_maximum_fusion = bf16[128,512]{1,0:T(8,128)(2,1)} fusion(bf16[128,1024]{1,0:T(8,128)(2,1)} %param.5, s32[]{:T(128)S(6)} %select_n.147), kind=kLoop, calls=%fused_computation.42 | loop fusion | flops 262144 | bytes 262148 | tf_op jit(solution)/shard_map/max | solution.py:40
  2.4 5.0 %collective-permute-start.2 = (bf16[128,512]{1,0:T(8,128)(2,1)}, bf16[128,512]{1,0:T(8,128)(2,1)}, u32[]{:S(2)}, u32[]{:S(2)}) collective-permute-start(bf16[128,512]{1,0:T(8,128)(2,1)} %dynamic-slice_maximum_fusion), channel_id=1, source_target_pairs={{0,24},{2,26},{4,28},{6,30},{8,16},{10,18},{12,20},{14,22},{16,8},... | collective-permute-start | bytes 393224 | tf_op jit(solution)/shard_map/ppermute | solution.py:29
  7.4 0.7 %fusion.37 = s32[8]{0:T(128)S(1)} fusion(s32[1,8]{1,0:T(1,128)} %param.7, s32[]{:T(128)S(6)} %select_n.153, s32[]{:T(128)S(6)} %select_n.148), kind=kLoop, calls=%fused_computation.140 | loop fusion | flops 272 | bytes 72 | tf_op jit(solution)/shard_map/eq | solution.py:47
  8.1 0.9 %constant_dynamic-slice_fusion.4 = bf16[128,512]{1,0:T(8,128)(2,1)S(1)} fusion(bf16[128,1024]{1,0:T(8,128)(2,1)} %param.9, s32[]{:T(128)S(6)} %select_n.147), kind=kLoop, calls=%fused_computation.105 | loop fusion | bytes 262148 | tf_op jit(solution)/shard_map/dynamic_slice | solution.py:51
  9.0 1.0 %bitcast_convert_fusion = f32[8,128,128]{2,1,0:T(8,128)S(1)} fusion(bf16[1,8,128,128]{3,2,1,0:T(8,128)(2,1)} %param.6), kind=kLoop, calls=%fused_computation.26 | loop fusion | flops 131072 | bytes 786432 | tf_op jit(solution)/shard_map/jit(_where)/broadcast_in_dim | solution.py:49
  10.0 0.5 select_reduce_fusion
  10.7 1.6 %collective-permute-start.3 = (bf16[128,768]{1,0:T(8,128)(2,1)S(1)}, bf16[128,768]{1,0:T(8,128)(2,1)S(1)}, u32[]{:S(2)}, u32[]{:S(2)}) collective-permute-start(bf16[128,768]{1,0:T(8,128)(2,1)S(1)} %get-tuple-element.31), channel_id=1, source_target_pairs={{0,2},{2,0},{4,6},{6,4},{8,10},{10,8},{12,14},{14,12},{16,18},{18,... | collective-permute-start | bytes 589832 | tf_op jit(solution)/shard_map/ppermute | solution.py:25
  12.2 1.5 %collective-permute-start.4 = (bf16[128,768]{1,0:T(8,128)(2,1)S(1)}, bf16[128,768]{1,0:T(8,128)(2,1)S(1)}, u32[]{:S(2)}, u32[]{:S(2)}) collective-permute-start(bf16[128,768]{1,0:T(8,128)(2,1)S(1)} %get-tuple-element.32), channel_id=1, source_target_pairs={{0,4},{2,6},{4,0},{6,2},{8,12},{10,14},{12,8},{14,10},{16,20},{18,... | collective-permute-start | bytes 589832 | tf_op jit(solution)/shard_map/ppermute | solution.py:25
  13.7 0.5 collective-permute-start.5
  14.3 4.3 %collective-permute-done.3 = bf16[128,768]{1,0:T(8,128)(2,1)S(1)} collective-permute-done((bf16[128,768]{1,0:T(8,128)(2,1)S(1)}, bf16[128,768]{1,0:T(8,128)(2,1)S(1)}, u32[]{:S(2)}, u32[]{:S(2)}) %collective-permute-start.3) | collective-permute-done | bytes 196640 | tf_op jit(solution)/shard_map/ppermute | solution.py:25
  18.6 0.6 collective-permute-start
  19.1 3.4 %collective-permute-done.4 = bf16[128,768]{1,0:T(8,128)(2,1)S(1)} collective-permute-done((bf16[128,768]{1,0:T(8,128)(2,1)S(1)}, bf16[128,768]{1,0:T(8,128)(2,1)S(1)}, u32[]{:S(2)}, u32[]{:S(2)}) %collective-permute-start.4) | collective-permute-done | bytes 196640 | tf_op jit(solution)/shard_map/ppermute | solution.py:25
  22.5 2.2 %all-gather = bf16[1024,256]{1,0:T(8,128)(2,1)S(1)} all-gather(bf16[512,256]{1,0:T(8,128)(2,1)S(1)} %pad_maximum_fusion.6), channel_id=2, replica_groups=mesh['blk'=16,'rep'=2] {'rep'}, dimensions={0}, use_global_device_ids=true | all-gather | bytes 786432 | tf_op jit(solution)/shard_map/all_gather | solution.py:59
  25.1 0.5 convolution_convert_fusion
  25.6 0.6 %collective-permute-start.12 = (bf16[128,512]{1,0:T(8,128)(2,1)S(1)}, bf16[128,512]{1,0:T(8,128)(2,1)S(1)}, u32[]{:S(2)}, u32[]{:S(2)}) collective-permute-start(bf16[128,512]{1,0:T(8,128)(2,1)S(1)} %get-tuple-element.3), channel_id=1, source_target_pairs={{0,8},{2,10},{4,12},{6,14},{8,0},{10,2},{12,4},{14,6},{16,24},{18,... | collective-permute-start | bytes 393224 | tf_op jit(solution)/shard_map/ppermute | solution.py:29
  26.2 3.5 %collective-permute-start.14 = (bf16[128,512]{1,0:T(8,128)(2,1)S(1)}, bf16[128,512]{1,0:T(8,128)(2,1)S(1)}, u32[]{:S(2)}, u32[]{:S(2)}) collective-permute-start(bf16[128,512]{1,0:T(8,128)(2,1)S(1)} %get-tuple-element.4), channel_id=1, source_target_pairs={{0,24},{2,26},{4,28},{6,30},{8,16},{10,18},{12,20},{14,22},{16,8},... | collective-permute-start | bytes 393224 | tf_op jit(solution)/shard_map/ppermute | solution.py:29
  29.8 1.5 %convolution_convert_fusion.1 = bf16[512,512]{1,0:T(8,128)(2,1)S(1)} fusion(bf16[128,512]{1,0:T(8,128)(2,1)} %collective-permute-done.2, bf16[128,512]{1,0:T(8,128)(2,1)} %collective-permute-done.1, bf16[128,512]{1,0:T(8,128)(2,1)S(1)} %collective-permute-done, bf16[128,512]{1,0:T(8,128)(2,1)} %dynamic-slice_maximum_fusion, ...), kind=kOutput, calls=%fused_computation.2 | convolution fusion | flops 272891904 | bytes 1572864 | tf_op jit(solution)/shard_map/dot_general | solution.py:32
  31.8 1.3 %collective-permute-start.6 = (bf16[1024,128]{1,0:T(8,128)(2,1)S(1)}, bf16[1024,128]{1,0:T(8,128)(2,1)S(1)}, u32[]{:S(2)}, u32[]{:S(2)}) collective-permute-start(bf16[1024,128]{1,0:T(8,128)(2,1)S(1)} %constant_dynamic-update-slice_fusion.4), channel_id=1, source_target_pairs={{0,2},{2,0},{4,6},{6,4},{8,10},{10,8},{12,14},{14,12},{16,18},{18,... | collective-permute-start | bytes 786440 | tf_op jit(solution)/shard_map/ppermute | solution.py:25
  33.1 0.8 %collective-permute-start.7 = (bf16[1024,128]{1,0:T(8,128)(2,1)S(1)}, bf16[1024,128]{1,0:T(8,128)(2,1)S(1)}, u32[]{:S(2)}, u32[]{:S(2)}) collective-permute-start(bf16[1024,128]{1,0:T(8,128)(2,1)S(1)} %constant_dynamic-update-slice_fusion.8), channel_id=1, source_target_pairs={{0,4},{2,6},{4,0},{6,2},{8,12},{10,14},{12,8},{14,10},{16,20},{18,... | collective-permute-start | bytes 786440 | tf_op jit(solution)/shard_map/ppermute | solution.py:25
  33.9 1.5 %collective-permute-start.8 = (bf16[1024,128]{1,0:T(8,128)(2,1)S(1)}, bf16[1024,128]{1,0:T(8,128)(2,1)S(1)}, u32[]{:S(2)}, u32[]{:S(2)}) collective-permute-start(bf16[1024,128]{1,0:T(8,128)(2,1)S(1)} %constant_dynamic-update-slice_fusion.12), channel_id=1, source_target_pairs={{0,6},{2,4},{4,2},{6,0},{8,14},{10,12},{12,10},{14,8},{16,22},{18,... | collective-permute-start | bytes 786440 | tf_op jit(solution)/shard_map/ppermute | solution.py:25
  35.4 1.6 %collective-permute-done.14 = bf16[128,512]{1,0:T(8,128)(2,1)S(1)} collective-permute-done((bf16[128,512]{1,0:T(8,128)(2,1)S(1)}, bf16[128,512]{1,0:T(8,128)(2,1)S(1)}, u32[]{:S(2)}, u32[]{:S(2)}) %collective-permute-start.14) | collective-permute-done | bytes 131104 | tf_op jit(solution)/shard_map/ppermute | solution.py:29
  37.0 4.1 %collective-permute-done.13 = bf16[128,512]{1,0:T(8,128)(2,1)S(1)} collective-permute-done((bf16[128,512]{1,0:T(8,128)(2,1)S(1)}, bf16[128,512]{1,0:T(8,128)(2,1)S(1)}, u32[]{:S(2)}, u32[]{:S(2)}) %collective-permute-start.13) | collective-permute-done | bytes 131104 | tf_op jit(solution)/shard_map/ppermute | solution.py:29
  41.1 2.0 %all_gather.19 = bf16[128,1024]{1,0:T(8,128)(2,1)S(1)} all-gather(bf16[128,512]{1,0:T(8,128)(2,1)S(1)} %add_convert_fusion.1), channel_id=1, replica_groups=mesh['blk'=16,'rep'=2] {'rep'}, dimensions={1}, use_global_device_ids=true | all-gather | bytes 393216 | tf_op jit(solution)/shard_map/all_gather | solution.py:106
  43.1 1.1 %fusion = bf16[128,512]{1,0:T(8,128)(2,1)} fusion(bf16[128,1024]{1,0:T(8,128)(2,1)S(1)} %all_gather.19, bf16[1024,1024]{1,0:T(8,128)(2,1)S(1)} %copy-done, s32[]{:T(128)S(6)} %select_n.147, bf16[128,1024]{1,0:T(8,128)(2,1)S(1)} %copy-done.1), kind=kOutput, calls=%fused_computation.6 | convolution fusion | flops 134545408 | bytes 1573888 | tf_op jit(solution)/shard_map/dot_general | solution.py:32
  44.6 1.6 %collective-permute-done.8 = bf16[1024,128]{1,0:T(8,128)(2,1)S(1)} collective-permute-done((bf16[1024,128]{1,0:T(8,128)(2,1)S(1)}, bf16[1024,128]{1,0:T(8,128)(2,1)S(1)}, u32[]{:S(2)}, u32[]{:S(2)}) %collective-permute-start.8) | collective-permute-done | bytes 262176 | tf_op jit(solution)/shard_map/ppermute | solution.py:25
  46.3 2.2 %all-gather.1 = bf16[2048,128]{1,0:T(8,128)(2,1)S(1)} all-gather(bf16[1024,128]{1,0:T(8,128)(2,1)S(1)} %add_convert_fusion), channel_id=3, replica_groups=mesh['blk'=16,'rep'=2] {'rep'}, dimensions={0}, use_global_device_ids=true | all-gather | bytes 786432 | tf_op jit(solution)/shard_map/all_gather | solution.py:87
  49.1 0.6 %collective-permute-start.9 = (bf16[64,512]{1,0:T(8,128)(2,1)S(1)}, bf16[64,512]{1,0:T(8,128)(2,1)S(1)}, u32[]{:S(2)}, u32[]{:S(2)}) collective-permute-start(bf16[64,512]{1,0:T(8,128)(2,1)S(1)} %get-tuple-element.20), channel_id=1, source_target_pairs={{0,8},{2,10},{4,12},{6,14},{8,0},{10,2},{12,4},{14,6},{16,24},{18,... | collective-permute-start | bytes 196616 | tf_op jit(solution)/shard_map/ppermute | solution.py:29
  49.7 3.5 %collective-permute-start.11 = (bf16[64,512]{1,0:T(8,128)(2,1)S(1)}, bf16[64,512]{1,0:T(8,128)(2,1)S(1)}, u32[]{:S(2)}, u32[]{:S(2)}) collective-permute-start(bf16[64,512]{1,0:T(8,128)(2,1)S(1)} %get-tuple-element.21), channel_id=1, source_target_pairs={{0,24},{2,26},{4,28},{6,30},{8,16},{10,18},{12,20},{14,22},{16,8},... | collective-permute-start | bytes 196616 | tf_op jit(solution)/shard_map/ppermute | solution.py:29
  53.3 1.0 %convolution_convert_fusion.3 = bf16[128,512]{1,0:T(8,128)(2,1)} fusion(bf16[1024,128]{1,0:T(8,128)(2,1)S(1)} %bitcast.83, bf16[1024,1024]{1,0:T(8,128)(2,1)S(1)} %copy-done, s32[]{:T(128)S(6)} %select_n.147), kind=kOutput, calls=%fused_computation.5 | convolution fusion | flops 134283264 | bytes 1441796 | tf_op jit(solution)/shard_map/dot_general | solution.py:32
  54.3 3.2 %collective-permute-done.11 = bf16[64,512]{1,0:T(8,128)(2,1)S(1)} collective-permute-done((bf16[64,512]{1,0:T(8,128)(2,1)S(1)}, bf16[64,512]{1,0:T(8,128)(2,1)S(1)}, u32[]{:S(2)}, u32[]{:S(2)}) %collective-permute-start.11) | collective-permute-done | bytes 65568 | tf_op jit(solution)/shard_map/ppermute | solution.py:29
  57.5 2.1 %collective-permute-done.10 = bf16[64,512]{1,0:T(8,128)(2,1)S(1)} collective-permute-done((bf16[64,512]{1,0:T(8,128)(2,1)S(1)}, bf16[64,512]{1,0:T(8,128)(2,1)S(1)}, u32[]{:S(2)}, u32[]{:S(2)}) %collective-permute-start.10) | collective-permute-done | bytes 65568 | tf_op jit(solution)/shard_map/ppermute | solution.py:29
  59.6 0.7 %fusion.13 = f32[64,512]{1,0:T(8,128)} fusion(bf16[64,512]{1,0:T(8,128)(2,1)S(1)} %collective-permute-done.11, bf16[64,512]{1,0:T(8,128)(2,1)S(1)} %collective-permute-done.10, bf16[64,512]{1,0:T(8,128)(2,1)S(1)} %collective-permute-done.9, bf16[4,64,512]{2,1,0:T(8,128)(2,1)S(1)} %bitcast.101, s32[]{:T(128)S(6)} %select_n.170), kind=kLoop, calls=%fused_computation.37 | loop fusion | flops 229376 | bytes 393220 | tf_op jit(solution)/shard_map/add | solution.py:35
  (47 shorter events, 2.0 us)
Async XLA Ops:
  0.6 42.5 %copy-start = (bf16[1024,1024]{1,0:T(8,128)(2,1)S(1)}, bf16[1024,1024]{1,0:T(8,128)(2,1)}, u32[]{:S(2)}) copy-start(bf16[1024,1024]{1,0:T(8,128)(2,1)} %param.8) | copy-start | bytes 6291460
  2.4 27.4 %collective-permute-start.2 = (bf16[128,512]{1,0:T(8,128)(2,1)}, bf16[128,512]{1,0:T(8,128)(2,1)}, u32[]{:S(2)}, u32[]{:S(2)}) collective-permute-start(bf16[128,512]{1,0:T(8,128)(2,1)} %dynamic-slice_maximum_fusion), channel_id=1, source_target_pairs={{0,24},{2,26},{4,28},{6,30},{8,16},{10,18},{12,20},{14,22},{16,8},... | collective-permute-start | bytes 393224 | tf_op jit(solution)/shard_map/ppermute | solution.py:29
  7.4 22.3 %collective-permute-start.1 = (bf16[128,512]{1,0:T(8,128)(2,1)}, bf16[128,512]{1,0:T(8,128)(2,1)}, u32[]{:S(2)}, u32[]{:S(2)}) collective-permute-start(bf16[128,512]{1,0:T(8,128)(2,1)} %dynamic-slice_maximum_fusion), channel_id=1, source_target_pairs={{0,16},{2,18},{4,20},{6,22},{8,24},{10,26},{12,28},{14,30},{16,0},... | collective-permute-start | bytes 393224 | tf_op jit(solution)/shard_map/ppermute | solution.py:29
  10.7 7.9 %collective-permute-start.3 = (bf16[128,768]{1,0:T(8,128)(2,1)S(1)}, bf16[128,768]{1,0:T(8,128)(2,1)S(1)}, u32[]{:S(2)}, u32[]{:S(2)}) collective-permute-start(bf16[128,768]{1,0:T(8,128)(2,1)S(1)} %get-tuple-element.31), channel_id=1, source_target_pairs={{0,2},{2,0},{4,6},{6,4},{8,10},{10,8},{12,14},{14,12},{16,18},{18,... | collective-permute-start | bytes 589832 | tf_op jit(solution)/shard_map/ppermute | solution.py:25
  12.2 10.3 %collective-permute-start.4 = (bf16[128,768]{1,0:T(8,128)(2,1)S(1)}, bf16[128,768]{1,0:T(8,128)(2,1)S(1)}, u32[]{:S(2)}, u32[]{:S(2)}) collective-permute-start(bf16[128,768]{1,0:T(8,128)(2,1)S(1)} %get-tuple-element.32), channel_id=1, source_target_pairs={{0,4},{2,6},{4,0},{6,2},{8,12},{10,14},{12,8},{14,10},{16,20},{18,... | collective-permute-start | bytes 589832 | tf_op jit(solution)/shard_map/ppermute | solution.py:25
  13.7 8.8 %collective-permute-start.5 = (bf16[128,768]{1,0:T(8,128)(2,1)S(1)}, bf16[128,768]{1,0:T(8,128)(2,1)S(1)}, u32[]{:S(2)}, u32[]{:S(2)}) collective-permute-start(bf16[128,768]{1,0:T(8,128)(2,1)S(1)} %get-tuple-element.33), channel_id=1, source_target_pairs={{0,6},{2,4},{4,2},{6,0},{8,14},{10,12},{12,10},{14,8},{16,22},{18,... | collective-permute-start | bytes 589832 | tf_op jit(solution)/shard_map/ppermute | solution.py:25
  18.6 11.2 %collective-permute-start = (bf16[128,512]{1,0:T(8,128)(2,1)}, bf16[128,512]{1,0:T(8,128)(2,1)S(1)}, u32[]{:S(2)}, u32[]{:S(2)}) collective-permute-start(bf16[128,512]{1,0:T(8,128)(2,1)} %dynamic-slice_maximum_fusion), channel_id=1, source_target_pairs={{0,8},{2,10},{4,12},{6,14},{8,0},{10,2},{12,4},{14,6},{16,24},{18,... | collective-permute-start | bytes 393224 | tf_op jit(solution)/shard_map/ppermute | solution.py:29
  25.6 8.3 %collective-permute-start.12 = (bf16[128,512]{1,0:T(8,128)(2,1)S(1)}, bf16[128,512]{1,0:T(8,128)(2,1)S(1)}, u32[]{:S(2)}, u32[]{:S(2)}) collective-permute-start(bf16[128,512]{1,0:T(8,128)(2,1)S(1)} %get-tuple-element.3), channel_id=1, source_target_pairs={{0,8},{2,10},{4,12},{6,14},{8,0},{10,2},{12,4},{14,6},{16,24},{18,... | collective-permute-start | bytes 393224 | tf_op jit(solution)/shard_map/ppermute | solution.py:29
  26.2 10.8 %collective-permute-start.14 = (bf16[128,512]{1,0:T(8,128)(2,1)S(1)}, bf16[128,512]{1,0:T(8,128)(2,1)S(1)}, u32[]{:S(2)}, u32[]{:S(2)}) collective-permute-start(bf16[128,512]{1,0:T(8,128)(2,1)S(1)} %get-tuple-element.4), channel_id=1, source_target_pairs={{0,24},{2,26},{4,28},{6,30},{8,16},{10,18},{12,20},{14,22},{16,8},... | collective-permute-start | bytes 393224 | tf_op jit(solution)/shard_map/ppermute | solution.py:29
  29.8 11.3 %collective-permute-start.13 = (bf16[128,512]{1,0:T(8,128)(2,1)S(1)}, bf16[128,512]{1,0:T(8,128)(2,1)S(1)}, u32[]{:S(2)}, u32[]{:S(2)}) collective-permute-start(bf16[128,512]{1,0:T(8,128)(2,1)S(1)} %get-tuple-element.5), channel_id=1, source_target_pairs={{0,16},{2,18},{4,20},{6,22},{8,24},{10,26},{12,28},{14,30},{16,0},... | collective-permute-start | bytes 393224 | tf_op jit(solution)/shard_map/ppermute | solution.py:29
  31.3 11.8 %copy-start.1 = (bf16[128,1024]{1,0:T(8,128)(2,1)S(1)}, bf16[128,1024]{1,0:T(8,128)(2,1)}, u32[]{:S(2)}) copy-start(bf16[128,1024]{1,0:T(8,128)(2,1)} %param.5) | copy-start | bytes 786436
  31.8 12.5 %collective-permute-start.6 = (bf16[1024,128]{1,0:T(8,128)(2,1)S(1)}, bf16[1024,128]{1,0:T(8,128)(2,1)S(1)}, u32[]{:S(2)}, u32[]{:S(2)}) collective-permute-start(bf16[1024,128]{1,0:T(8,128)(2,1)S(1)} %constant_dynamic-update-slice_fusion.4), channel_id=1, source_target_pairs={{0,2},{2,0},{4,6},{6,4},{8,10},{10,8},{12,14},{14,12},{16,18},{18,... | collective-permute-start | bytes 786440 | tf_op jit(solution)/shard_map/ppermute | solution.py:25
  33.1 11.5 %collective-permute-start.7 = (bf16[1024,128]{1,0:T(8,128)(2,1)S(1)}, bf16[1024,128]{1,0:T(8,128)(2,1)S(1)}, u32[]{:S(2)}, u32[]{:S(2)}) collective-permute-start(bf16[1024,128]{1,0:T(8,128)(2,1)S(1)} %constant_dynamic-update-slice_fusion.8), channel_id=1, source_target_pairs={{0,4},{2,6},{4,0},{6,2},{8,12},{10,14},{12,8},{14,10},{16,20},{18,... | collective-permute-start | bytes 786440 | tf_op jit(solution)/shard_map/ppermute | solution.py:25
  33.9 12.3 %collective-permute-start.8 = (bf16[1024,128]{1,0:T(8,128)(2,1)S(1)}, bf16[1024,128]{1,0:T(8,128)(2,1)S(1)}, u32[]{:S(2)}, u32[]{:S(2)}) collective-permute-start(bf16[1024,128]{1,0:T(8,128)(2,1)S(1)} %constant_dynamic-update-slice_fusion.12), channel_id=1, source_target_pairs={{0,6},{2,4},{4,2},{6,0},{8,14},{10,12},{12,10},{14,8},{16,22},{18,... | collective-permute-start | bytes 786440 | tf_op jit(solution)/shard_map/ppermute | solution.py:25
  49.1 5.2 %collective-permute-start.9 = (bf16[64,512]{1,0:T(8,128)(2,1)S(1)}, bf16[64,512]{1,0:T(8,128)(2,1)S(1)}, u32[]{:S(2)}, u32[]{:S(2)}) collective-permute-start(bf16[64,512]{1,0:T(8,128)(2,1)S(1)} %get-tuple-element.20), channel_id=1, source_target_pairs={{0,8},{2,10},{4,12},{6,14},{8,0},{10,2},{12,4},{14,6},{16,24},{18,... | collective-permute-start | bytes 196616 | tf_op jit(solution)/shard_map/ppermute | solution.py:29
  49.7 7.8 %collective-permute-start.11 = (bf16[64,512]{1,0:T(8,128)(2,1)S(1)}, bf16[64,512]{1,0:T(8,128)(2,1)S(1)}, u32[]{:S(2)}, u32[]{:S(2)}) collective-permute-start(bf16[64,512]{1,0:T(8,128)(2,1)S(1)} %get-tuple-element.21), channel_id=1, source_target_pairs={{0,24},{2,26},{4,28},{6,30},{8,16},{10,18},{12,20},{14,22},{16,8},... | collective-permute-start | bytes 196616 | tf_op jit(solution)/shard_map/ppermute | solution.py:29
  53.3 6.3 %collective-permute-start.10 = (bf16[64,512]{1,0:T(8,128)(2,1)S(1)}, bf16[64,512]{1,0:T(8,128)(2,1)S(1)}, u32[]{:S(2)}, u32[]{:S(2)}) collective-permute-start(bf16[64,512]{1,0:T(8,128)(2,1)S(1)} %get-tuple-element.22), channel_id=1, source_target_pairs={{0,16},{2,18},{4,20},{6,22},{8,24},{10,26},{12,28},{14,30},{16,0},... | collective-permute-start | bytes 196616 | tf_op jit(solution)/shard_map/ppermute | solution.py:29

commit v6 on v5

v6 whole, which is shorter than its diff:
```python
import functools

import jax
import jax.numpy as jnp
from jax import lax
from jax.experimental import pallas as pl
from jax.experimental.pallas import tpu as pltpu
from jax.sharding import PartitionSpec as P


def prepare_kernel(side, per_core, place_ref, cols_ref, hidden_ref, cot_ref, vals_ref, *outs):
    hidden_out, cot_out, blocks_out = outs
    hidden_out[...] = jnp.maximum(hidden_ref[...], 0)
    cot_out[...] = cot_ref[...]
    slots, spans = vals_ref.shape[1], blocks_out.shape[0]
    if slots < spans:
        blocks_out[...] = jnp.zeros_like(blocks_out)
    for k in range(slots):
        column = cols_ref[0, k]
        turn = (column % side) ^ place_ref[1]
        level = (column // side) ^ place_ref[2]
        blocks_out[turn * per_core + level % per_core] = vals_ref[0, k]


def prepared(hidden_pre, cotangent, adj_vals, adj_cols, place, side, per_core, cols_here):
    tile_size = hidden_pre.shape[0]
    part = pl.BlockSpec((tile_size, cols_here), lambda i, place, cols: (0, place[0]))
    whole = pl.BlockSpec((tile_size, cols_here), lambda i, place, cols: (0, 0))
    spans = side * per_core
    return pl.pallas_call(
        functools.partial(prepare_kernel, side, per_core),
        grid_spec=pltpu.PrefetchScalarGridSpec(
            num_scalar_prefetch=2,
            grid=(1,),
            in_specs=[
                part,
                part,
                pl.BlockSpec(adj_vals.shape, lambda i, place, cols: (0, 0, 0, 0)),
            ],
            out_specs=[
                whole,
                whole,
                pl.BlockSpec((spans, tile_size, tile_size), lambda i, place, cols: (0, 0, 0)),
            ],
        ),
        out_shape=[
            jax.ShapeDtypeStruct((tile_size, cols_here), jnp.bfloat16),
            jax.ShapeDtypeStruct((tile_size, cols_here), jnp.bfloat16),
            jax.ShapeDtypeStruct((spans, tile_size, tile_size), jnp.bfloat16),
        ],
    )(place, adj_cols, hidden_pre, cotangent, adj_vals)


def shards(hidden_pre, adj_vals, adj_cols, w_out, cotangent):
    feature_width = hidden_pre.shape[1]
    tile_size = adj_vals.shape[2]
    blk_count = lax.axis_size("blk")
    rep_count = lax.axis_size("rep")
    section_span = blk_count // rep_count
    bits = (blk_count.bit_length() - 1) // 2
    side = 1 << bits
    per_core = section_span // side
    blk_pos = lax.axis_index("blk")
    rep_pos = lax.axis_index("rep")
    outer_pos, inner_pos = blk_pos // side, blk_pos % side
    cols_here = feature_width // rep_count
    rows_here = feature_width // blk_count
    bf16 = jnp.bfloat16
    turns = range(side)
    rising = [1 << b for b in range(bits)]
    falling = rising[::-1]

    def along_inner(value, turn):
        pairs = [(o * side + i, o * side + (i ^ turn)) for o in turns for i in turns]
        return lax.ppermute(value, "blk", pairs) if turn else value

    def along_outer(value, turn):
        pairs = [(o * side + i, (o ^ turn) * side + i) for o in turns for i in turns]
        return lax.ppermute(value, "blk", pairs) if turn else value

    def doubled(value, move, order):
        held = {0: value}
        for bit in order:
            keys = list(held)
            size = held[keys[0]].shape[0]
            got = move(jnp.concatenate([held[k] for k in keys], 0), bit)
            for n, k in enumerate(keys):
                held[k ^ bit] = got[n * size : (n + 1) * size]
        return jnp.concatenate([held[k] for k in turns], 0)

    def halved(parts, move, order):
        parts = dict(enumerate(parts))
        size = parts[0].shape[0]
        for bit in order:
            keys = [k for k in parts if not k & bit]
            sent = jnp.concatenate([parts[k ^ bit].astype(bf16) for k in keys], 0)
            got = move(sent, bit)
            parts = {
                k: parts[k].astype(jnp.float32)
                + got[n * size : (n + 1) * size].astype(jnp.float32)
                for n, k in enumerate(keys)
            }
        return parts[0]

    def dealt(parts, move, order):
        held = {(0, k): part for k, part in enumerate(parts)}
        size = parts[0].shape[0]
        for bit in order:
            keys = [key for key in held if not key[1] & bit]
            got = move(jnp.concatenate([held[s, k ^ bit] for s, k in keys], 0), bit)
            kept = {key: held[key] for key in keys}
            for n, (s, k) in enumerate(keys):
                kept[s ^ bit, k] = got[n * size : (n + 1) * size]
            held = kept
        return [held[s, 0] for s in turns]

    def dot(lhs, rhs, dims):
        return lax.dot_general(lhs, rhs, (dims, ((), ())), preferred_element_type=jnp.float32)

    def after(value, other):
        return lax.optimization_barrier((value, other))[0]

    def lanes(value, index):
        return value[:, index * tile_size : (index + 1) * tile_size]

    place = jnp.stack([rep_pos, inner_pos, outer_pos]).astype(jnp.int32)
    hidden_part, grad_part, ordered = prepared(
        hidden_pre, cotangent, adj_vals, adj_cols, place, side, per_core, cols_here
    )
    hidden_stack = doubled(hidden_part, along_outer, falling)
    arrived = dealt(
        [ordered[t * per_core : (t + 1) * per_core] for t in turns], along_inner, rising
    )
    grad_stack = doubled(grad_part, along_inner, falling)
    everyone = lax.all_gather(jnp.concatenate(arrived, 0), "rep", axis=0)

    rows = []
    for t in turns:
        row_block = outer_pos * side + (inner_pos ^ t)
        row = []
        for e in turns:
            column_block = (outer_pos ^ e) * side + inner_pos
            holder = jnp.mod(row_block - column_block, blk_count) // section_span
            index = t * per_core + e % per_core
            piece = everyone[0, index]
            for r in range(1, rep_count):
                piece = jnp.where(holder == r, everyone[r, index], piece)
            row.append(piece)
        rows.append(jnp.concatenate(row, 1))
    block = jnp.concatenate(rows, 0)

    mixed = dot(hidden_stack, block, ((0,), (1,))).astype(bf16)
    share = cols_here // side
    by_owner = mixed.reshape(share // rows_here, side, rows_here, side * tile_size)
    mixed_cols = 0.0
    for t in turns:
        chosen = lax.dynamic_index_in_dim(by_owner, inner_pos ^ t, 1, keepdims=False)
        chosen = chosen.reshape(share, side * tile_size)
        chosen = jnp.concatenate([lanes(chosen, u ^ t) for u in turns], 1)
        mixed_cols = mixed_cols + along_inner(chosen, t).astype(jnp.float32)
    mixed_cols = lax.all_gather(mixed_cols.astype(bf16), "rep", axis=0, tiled=True)
    weight_part = dot(mixed_cols, grad_stack, ((1,), (0,)))
    weight_part = weight_part.reshape(side, rows_here, cols_here)
    weight_part = [
        lax.dynamic_index_in_dim(weight_part, outer_pos ^ t, 0, keepdims=False) for t in turns
    ]
    grad_weight = halved(weight_part, along_outer, rising)

    back_stack = dot(after(block, mixed), grad_stack, ((0,), (0,)))
    back_part = halved(
        [back_stack[e * tile_size : (e + 1) * tile_size] for e in turns], along_outer, rising
    ).astype(bf16)

    mixed_rows = halved([lanes(mixed, t) for t in turns], along_inner, rising).astype(bf16)
    mixed_rows = lax.all_gather(after(mixed_rows, weight_part[0]), "rep", axis=0, tiled=True)
    w_columns = lax.dynamic_slice_in_dim(w_out, rep_pos * cols_here, cols_here, 1)
    out_part = dot(mixed_rows, w_columns, ((0,), (0,))).astype(bf16)

    back_full = lax.all_gather(after(back_part, weight_part[0]), "rep", axis=1, tiled=True)
    w_rows = lax.dynamic_slice_in_dim(w_out, rep_pos * cols_here, cols_here, 0)
    grad_in = dot(back_full, w_rows, ((1,), (1,)))
    pre_part = lax.dynamic_slice_in_dim(hidden_pre, rep_pos * cols_here, cols_here, 1)
    grad_pre = jnp.where(pre_part > 0, grad_in, 0.0).astype(bf16)
    return (out_part, grad_weight, grad_pre)


def solution(mesh):
    placed = (P("blk", None), P("blk", "rep", None, None), P("blk", "rep"), P(), P("blk", None))
    return jax.shard_map(
        shards,
        mesh=mesh,
        in_specs=placed,
        out_specs=(P("blk", "rep"), P("blk", "rep"), P("blk", "rep")),
        check_vma=False,
    )
```

time: 60.5 us -> 63.6 us (1.051)
  other arithmetic: 5.29 us -> 1.9 us
  Pallas kernels: 0 us -> 2.6 us
  waiting for transfers between devices: 20.6 us -> 22.5 us
  blocking collectives: 6.36 us -> 8.16 us
  starting transfers between devices: 21.1 us -> 22.7 us
  matrix products: 4.42 us -> 3.39 us
    ppermute x9 -> x6, waiting for transfers between devices: 11 us -> 16.1 us  [along_outer(): return lax.ppermute(value, 'blk', pairs) if turn else value]
    ppermute x6 -> x9, starting transfers between devices: 7.17 us -> 11.2 us  [along_inner(): return lax.ppermute(value, 'blk', pairs) if turn else value]
    ppermute x6 -> x9, waiting for transfers between devices: 9.57 us -> 6.46 us  [along_inner(): return lax.ppermute(value, 'blk', pairs) if turn else value]
    pallas_call x0 -> x1, Pallas kernels: none -> 2.6 us  [prepared(): pl.pallas_call(functools.partial(prepare_kernel, side, per_core), grid_sp...]
    ppermute x9 -> x6, starting transfers between devices: 13.9 us -> 11.5 us  [along_outer(): return lax.ppermute(value, 'blk', pairs) if turn else value]
    all_gather x3 -> x4, blocking collectives: 6.36 us -> 8.16 us  [the longest x1 2.18 us: shards(): everyone = lax.all_gather(jnp.concatenate(arrived, 0), 'rep', axis=0)]
    max x1 -> x0, other arithmetic: 1.73 us -> none  [shards(): jnp.maximum(lax.dynamic_slice_in_dim(hidden_pre, rep_pos * cols_here, col...]
    slice x1 -> x8, local copies, waits for them, and re-layouts: 0.03 us -> 1.12 us  [the longest x1 1 us: shards(): ordered[t * per_core:(t + 1) * per_core]]
  transfers between devices with their start and end apart: 15 -> 15, of which waited for: 8 -> 7; matrix products, arithmetic and copies ran while one was open for 14% -> 4% of each run, Pallas kernels for 0% -> 0%
where the time goes in v6:
time: 63.6 us; the launch traced here: 63.4 us
  starting transfers between devices  22.7 us (36%)
  waiting for transfers between devices  22.5 us (35%)
  blocking collectives  8.16 us (13%)
  matrix products  3.39 us (5%)
  Pallas kernels  2.6 us (4%)
  other arithmetic  1.9 us (3%)
  local copies, waits for them, and re-layouts  1.23 us (2%)
  between operations  0.9 us (1%)
    ppermute x6, waiting for transfers between devices, along_outer(): return lax.ppermute(value, 'blk', pairs) if turn else value  16.1 us
    ppermute x6, starting transfers between devices, along_outer(): return lax.ppermute(value, 'blk', pairs) if turn else value  11.5 us
    ppermute x9, starting transfers between devices, along_inner(): return lax.ppermute(value, 'blk', pairs) if turn else value  11.2 us
    ppermute x9, waiting for transfers between devices, along_inner(): return lax.ppermute(value, 'blk', pairs) if turn else value  6.46 us
    dot_general x5, matrix products, dot(): lax.dot_general(lhs, rhs, (dims, ((), ())), preferred_element_type=jnp.fl...  3.39 us
    pallas_call x1, Pallas kernels, prepared(): pl.pallas_call(functools.partial(prepare_kernel, side, per_core), grid_sp...  2.6 us
    all_gather x1, blocking collectives, shards(): everyone = lax.all_gather(jnp.concatenate(arrived, 0), 'rep', axis=0)  2.18 us
    all_gather x1, blocking collectives, shards(): lax.all_gather(mixed_cols.astype(bf16), 'rep', axis=0, tiled=True)  1.99 us
  transfers between devices with their start and end apart: 15, of which 7 were waited for; matrix products, arithmetic and copies ran while one was open for 4% of the time, Pallas kernels for 0%

profile of v6, /device:TPU:0, one launch (start us, length us, event | category | flops | bytes accessed | tf_op | source)
XLA Modules:
  0.0 63.4 jit_solution(1715535189751342745)
XLA Ops:
  0.7 0.6 %pad_add_fusion.place_ref = s32[3]{0:T(128)} fusion(s32[1]{0:T(128)} %bitcast.2, s32[1]{0:T(128)} %bitcast.1, s32[1]{0:T(128)} %bitcast), kind=kLoop, calls=%fused_computation.70 | loop fusion | flops 6 | bytes 24 | tf_op jit(solution)/shard_map/stack | solution.py:126
  1.3 2.6 %shard_map.76 = (bf16[128,512]{1,0:T(8,128)(2,1)}, bf16[128,512]{1,0:T(8,128)(2,1)}, bf16[8,128,128]{2,1,0:T(8,128)(2,1)}) custom-call(s32[3]{0:T(128)} %pad_add_fusion.place_ref, s32[1,8]{1,0:T(1,128)} %cols_ref.1, bf16[128,1024]{1,0:T(8,128)(2,1)} %hidden_ref.1, bf16[128,1024]{1,0:T(8,128)(2,1)} %cot_ref.1, bf16[1,8,128,128]{3,2,1,0:T(8,128)(2,1)} %vals_ref.1), custom_call_target="tpu_custom_call" | custom-call | tf_op jit(solution)/shard_map/pallas_call | solution.py:30
  3.9 1.0 %fusion.31 = (bf16[2,128,128]{2,1,0:T(8,128)(2,1)S(1)}, bf16[2,128,128]{2,1,0:T(8,128)(2,1)S(1)}, bf16[2,128,128]{2,1,0:T(8,128)(2,1)S(1)}, bf16[2,128,128]{2,1,0:T(8,128)(2,1)S(1)}) fusion(bf16[8,128,128]{2,1,0:T(8,128)(2,1)} %get-tuple-element.10), kind=kLoop, calls=%fused_computation.78 | loop fusion | bytes 524288 | tf_op jit(solution)/shard_map/slice | solution.py:132
  4.9 3.0 %collective-permute-start.2 = (bf16[4,128,128]{2,1,0:T(8,128)(2,1)S(1)}, bf16[4,128,128]{2,1,0:T(8,128)(2,1)S(1)}, u32[]{:S(2)}, u32[]{:S(2)}) collective-permute-start(bf16[4,128,128]{2,1,0:T(8,128)(2,1)S(1)} %pad_maximum_fusion.6), channel_id=1, source_target_pairs={{0,2},{2,0},{4,6},{6,4},{8,10},{10,8},{12,14},{14,12},{16,18},{18,... | collective-permute-start | bytes 393224 | tf_op jit(solution)/shard_map/ppermute | solution.py:75
  7.9 2.6 %collective-permute-start = (bf16[128,512]{1,0:T(8,128)(2,1)}, bf16[128,512]{1,0:T(8,128)(2,1)S(1)}, u32[]{:S(2)}, u32[]{:S(2)}) collective-permute-start(bf16[128,512]{1,0:T(8,128)(2,1)} %get-tuple-element.9), channel_id=1, source_target_pairs={{0,16},{2,18},{4,20},{6,22},{8,24},{10,26},{12,28},{14,30},{16,0},... | collective-permute-start | bytes 393224 | tf_op jit(solution)/shard_map/ppermute | solution.py:79
  10.5 1.5 %collective-permute-start.9 = (bf16[128,512]{1,0:T(8,128)(2,1)}, bf16[128,512]{1,0:T(8,128)(2,1)S(1)}, u32[]{:S(2)}, u32[]{:S(2)}) collective-permute-start(bf16[128,512]{1,0:T(8,128)(2,1)} %get-tuple-element.11), channel_id=1, source_target_pairs={{0,4},{2,6},{4,0},{6,2},{8,12},{10,14},{12,8},{14,10},{16,20},{18,... | collective-permute-start | bytes 393224 | tf_op jit(solution)/shard_map/ppermute | solution.py:75
  12.1 1.2 %collective-permute-start.3 = (bf16[4,128,128]{2,1,0:T(8,128)(2,1)S(1)}, bf16[4,128,128]{2,1,0:T(8,128)(2,1)S(1)}, u32[]{:S(2)}, u32[]{:S(2)}) collective-permute-start(bf16[4,128,128]{2,1,0:T(8,128)(2,1)S(1)} %pad_maximum_fusion.7), channel_id=1, source_target_pairs={{0,4},{2,6},{4,0},{6,2},{8,12},{10,14},{12,8},{14,10},{16,20},{18,... | collective-permute-start | bytes 393224 | tf_op jit(solution)/shard_map/ppermute | solution.py:75
  13.3 3.5 %collective-permute-done = bf16[128,512]{1,0:T(8,128)(2,1)S(1)} collective-permute-done((bf16[128,512]{1,0:T(8,128)(2,1)}, bf16[128,512]{1,0:T(8,128)(2,1)S(1)}, u32[]{:S(2)}, u32[]{:S(2)}) %collective-permute-start) | collective-permute-done | bytes 131104 | tf_op jit(solution)/shard_map/ppermute | solution.py:79
  16.8 0.8 %collective-permute-start.1 = (bf16[256,512]{1,0:T(8,128)(2,1)S(1)}, bf16[256,512]{1,0:T(8,128)(2,1)S(1)}, u32[]{:S(2)}, u32[]{:S(2)}) collective-permute-start(bf16[256,512]{1,0:T(8,128)(2,1)S(1)} %pad_maximum_fusion.1), channel_id=1, source_target_pairs={{0,8},{2,10},{4,12},{6,14},{8,0},{10,2},{12,4},{14,6},{16,24},{18,... | collective-permute-start | bytes 786440 | tf_op jit(solution)/shard_map/ppermute | solution.py:79
  17.7 0.6 collective-permute-start.10
  18.4 2.2 %all-gather = bf16[16,128,128]{2,1,0:T(8,128)(2,1)S(1)} all-gather(bf16[8,128,128]{2,1,0:T(8,128)(2,1)S(1)} %pad_maximum_fusion.2), channel_id=2, replica_groups=mesh['blk'=16,'rep'=2] {'rep'}, dimensions={0}, use_global_device_ids=true | all-gather | bytes 786432 | tf_op jit(solution)/shard_map/all_gather | solution.py:135
  20.7 3.5 %collective-permute-done.1 = bf16[256,512]{1,0:T(8,128)(2,1)S(1)} collective-permute-done((bf16[256,512]{1,0:T(8,128)(2,1)S(1)}, bf16[256,512]{1,0:T(8,128)(2,1)S(1)}, u32[]{:S(2)}, u32[]{:S(2)}) %collective-permute-start.1) | collective-permute-done | bytes 262176 | tf_op jit(solution)/shard_map/ppermute | solution.py:79
  24.2 0.5 convolution_convert_fusion
  24.7 0.6 collective-permute-start.4
  25.5 1.6 %collective-permute-start.7 = (bf16[128,512]{1,0:T(8,128)(2,1)S(1)}, bf16[128,512]{1,0:T(8,128)(2,1)S(1)}, u32[]{:S(2)}, u32[]{:S(2)}) collective-permute-start(bf16[128,512]{1,0:T(8,128)(2,1)S(1)} %pad_maximum_fusion.9), channel_id=1, source_target_pairs={{0,4},{2,6},{4,0},{6,2},{8,12},{10,14},{12,8},{14,10},{16,20},{18,... | collective-permute-start | bytes 393224 | tf_op jit(solution)/shard_map/ppermute | solution.py:75
  27.1 1.6 %collective-permute-start.6 = (bf16[128,512]{1,0:T(8,128)(2,1)S(1)}, bf16[128,512]{1,0:T(8,128)(2,1)S(1)}, u32[]{:S(2)}, u32[]{:S(2)}) collective-permute-start(bf16[128,512]{1,0:T(8,128)(2,1)S(1)} %pad_maximum_fusion.8), channel_id=1, source_target_pairs={{0,2},{2,0},{4,6},{6,4},{8,10},{10,8},{12,14},{14,12},{16,18},{18,... | collective-permute-start | bytes 393224 | tf_op jit(solution)/shard_map/ppermute | solution.py:75
  28.7 0.5 collective-permute-start.8
  29.8 1.8 %collective-permute-start.13 = (bf16[256,512]{1,0:T(8,128)(2,1)S(1)}, bf16[256,512]{1,0:T(8,128)(2,1)S(1)}, u32[]{:S(2)}, u32[]{:S(2)}) collective-permute-start(bf16[256,512]{1,0:T(8,128)(2,1)S(1)} %pad_maximum_fusion.5), channel_id=1, source_target_pairs={{0,8},{2,10},{4,12},{6,14},{8,0},{10,2},{12,4},{14,6},{16,24},{18,... | collective-permute-start | bytes 786440 | tf_op jit(solution)/shard_map/ppermute | solution.py:79
  31.6 4.1 %collective-permute-done.6 = bf16[128,512]{1,0:T(8,128)(2,1)S(1)} collective-permute-done((bf16[128,512]{1,0:T(8,128)(2,1)S(1)}, bf16[128,512]{1,0:T(8,128)(2,1)S(1)}, u32[]{:S(2)}, u32[]{:S(2)}) %collective-permute-start.6) | collective-permute-done | bytes 131104 | tf_op jit(solution)/shard_map/ppermute | solution.py:75
  35.7 2.4 %collective-permute-done.8 = bf16[128,512]{1,0:T(8,128)(2,1)S(1)} collective-permute-done((bf16[128,512]{1,0:T(8,128)(2,1)S(1)}, bf16[128,512]{1,0:T(8,128)(2,1)S(1)}, u32[]{:S(2)}, u32[]{:S(2)}) %collective-permute-start.8) | collective-permute-done | bytes 131104 | tf_op jit(solution)/shard_map/ppermute | solution.py:75
  38.1 2.0 %all_gather.17 = bf16[256,512]{1,0:T(8,128)(2,1)S(1)} all-gather(bf16[128,512]{1,0:T(8,128)(2,1)S(1)} %fusion.15), channel_id=1, replica_groups=mesh['blk'=16,'rep'=2] {'rep'}, dimensions={0}, use_global_device_ids=true | all-gather | bytes 393216 | tf_op jit(solution)/shard_map/all_gather | solution.py:161
  40.5 2.5 %collective-permute-start.11 = (bf16[128,512]{1,0:T(8,128)(2,1)S(1)}, bf16[128,512]{1,0:T(8,128)(2,1)S(1)}, u32[]{:S(2)}, u32[]{:S(2)}) collective-permute-start(bf16[128,512]{1,0:T(8,128)(2,1)S(1)} %pad_maximum_fusion.11), channel_id=1, source_target_pairs={{0,8},{2,10},{4,12},{6,14},{8,0},{10,2},{12,4},{14,6},{16,24},{18,... | collective-permute-start | bytes 393224 | tf_op jit(solution)/shard_map/ppermute | solution.py:79
  43.0 0.6 collective-permute-start.5
  43.6 3.2 %collective-permute-done.11 = bf16[128,512]{1,0:T(8,128)(2,1)S(1)} collective-permute-done((bf16[128,512]{1,0:T(8,128)(2,1)S(1)}, bf16[128,512]{1,0:T(8,128)(2,1)S(1)}, u32[]{:S(2)}, u32[]{:S(2)}) %collective-permute-start.11) | collective-permute-done | bytes 131104 | tf_op jit(solution)/shard_map/ppermute | solution.py:79
  46.8 3.7 %collective-permute-start.12 = (bf16[64,512]{1,0:T(8,128)(2,1)S(1)}, bf16[64,512]{1,0:T(8,128)(2,1)S(1)}, u32[]{:S(2)}, u32[]{:S(2)}) collective-permute-start(bf16[64,512]{1,0:T(8,128)(2,1)S(1)} %fusion.16), channel_id=1, source_target_pairs={{0,16},{2,18},{4,20},{6,22},{8,24},{10,26},{12,28},{14,30},{16,0},... | collective-permute-start | bytes 196616 | tf_op jit(solution)/shard_map/ppermute | solution.py:79
  50.6 2.3 %collective-permute-done.12 = bf16[64,512]{1,0:T(8,128)(2,1)S(1)} collective-permute-done((bf16[64,512]{1,0:T(8,128)(2,1)S(1)}, bf16[64,512]{1,0:T(8,128)(2,1)S(1)}, u32[]{:S(2)}, u32[]{:S(2)}) %collective-permute-start.12) | collective-permute-done | bytes 65568 | tf_op jit(solution)/shard_map/ppermute | solution.py:79
  52.9 0.7 %convert_add_fusion.1 = f32[64,512]{1,0:T(8,128)} fusion(bf16[64,512]{1,0:T(8,128)(2,1)S(1)} %collective-permute-done.12, bf16[128,512]{1,0:T(8,128)(2,1)S(1)} %collective-permute-done.11, f32[4,64,512]{2,1,0:T(8,128)S(1)} %bitcast.74, s32[]{:T(128)S(6)} %select_n.370), kind=kLoop, calls=%fused_computation.39 | loop fusion | flops 131072 | bytes 393220 | tf_op jit(solution)/shard_map/add | solution.py:99
  53.7 2.0 %all_gather.18 = bf16[1024,128]{1,0:T(8,128)(2,1)S(1)} all-gather(bf16[512,128]{1,0:T(8,128)(2,1)S(1)} %add_convert_fusion), channel_id=1, replica_groups=mesh['blk'=16,'rep'=2] {'rep'}, dimensions={0}, use_global_device_ids=true | all-gather | bytes 393216 | tf_op jit(solution)/shard_map/all_gather | solution.py:175
  55.7 3.6 %collective-permute-done.14 = bf16[128,512]{1,0:T(8,128)(2,1)S(1)} collective-permute-done((bf16[128,512]{1,0:T(8,128)(2,1)S(1)}, bf16[128,512]{1,0:T(8,128)(2,1)S(1)}, u32[]{:S(2)}, u32[]{:S(2)}) %collective-permute-start.14) | collective-permute-done | bytes 131104 | tf_op jit(solution)/shard_map/ppermute | solution.py:79
  59.3 2.0 %all_gather.19 = bf16[128,1024]{1,0:T(8,128)(2,1)S(1)} all-gather(bf16[128,512]{1,0:T(8,128)(2,1)S(1)} %fusion.12), channel_id=1, replica_groups=mesh['blk'=16,'rep'=2] {'rep'}, dimensions={1}, use_global_device_ids=true | all-gather | bytes 393216 | tf_op jit(solution)/shard_map/all_gather | solution.py:179
  61.3 1.0 %convolution_convert_fusion.1 = bf16[128,512]{1,0:T(8,128)(2,1)} fusion(bf16[1024,128]{1,0:T(8,128)(2,1)S(1)} %all_gather.18, bf16[1024,1024]{1,0:T(8,128)(2,1)S(1)} %copy-done, s32[]{:T(128)S(6)} %select_n.371), kind=kOutput, calls=%fused_computation.2 | convolution fusion | flops 134283264 | bytes 1441796 | tf_op jit(solution)/shard_map/dot_general | solution.py:118
  62.3 1.1 %fusion = bf16[128,512]{1,0:T(8,128)(2,1)} fusion(bf16[128,1024]{1,0:T(8,128)(2,1)S(1)} %all_gather.19, bf16[1024,1024]{1,0:T(8,128)(2,1)S(1)} %copy-done, s32[]{:T(128)S(6)} %select_n.371, bf16[128,1024]{1,0:T(8,128)(2,1)S(1)} %copy-done.1), kind=kOutput, calls=%fused_computation.3 | convolution fusion | flops 134545408 | bytes 1573888 | tf_op jit(solution)/shard_map/dot_general | solution.py:118
  (51 shorter events, 1.7 us)
Async XLA Ops:
  0.6 60.7 %copy-start = (bf16[1024,1024]{1,0:T(8,128)(2,1)S(1)}, bf16[1024,1024]{1,0:T(8,128)(2,1)}, u32[]{:S(2)}) copy-start(bf16[1024,1024]{1,0:T(8,128)(2,1)} %param.8) | copy-start | bytes 6291460
  3.9 12.9 %copy-start.3 = (bf16[128,512]{1,0:T(8,128)(2,1)S(1)}, bf16[128,512]{1,0:T(8,128)(2,1)}, u32[]{:S(2)}) copy-start(bf16[128,512]{1,0:T(8,128)(2,1)} %get-tuple-element.9) | copy-start | bytes 393220
  3.9 13.8 %copy-start.2 = (bf16[128,512]{1,0:T(8,128)(2,1)S(1)}, bf16[128,512]{1,0:T(8,128)(2,1)}, u32[]{:S(2)}) copy-start(bf16[128,512]{1,0:T(8,128)(2,1)} %get-tuple-element.11) | copy-start | bytes 393220
  4.9 7.1 %collective-permute-start.2 = (bf16[4,128,128]{2,1,0:T(8,128)(2,1)S(1)}, bf16[4,128,128]{2,1,0:T(8,128)(2,1)S(1)}, u32[]{:S(2)}, u32[]{:S(2)}) collective-permute-start(bf16[4,128,128]{2,1,0:T(8,128)(2,1)S(1)} %pad_maximum_fusion.6), channel_id=1, source_target_pairs={{0,2},{2,0},{4,6},{6,4},{8,10},{10,8},{12,14},{14,12},{16,18},{18,... | collective-permute-start | bytes 393224 | tf_op jit(solution)/shard_map/ppermute | solution.py:75
  7.9 8.9 %collective-permute-start = (bf16[128,512]{1,0:T(8,128)(2,1)}, bf16[128,512]{1,0:T(8,128)(2,1)S(1)}, u32[]{:S(2)}, u32[]{:S(2)}) collective-permute-start(bf16[128,512]{1,0:T(8,128)(2,1)} %get-tuple-element.9), channel_id=1, source_target_pairs={{0,16},{2,18},{4,20},{6,22},{8,24},{10,26},{12,28},{14,30},{16,0},... | collective-permute-start | bytes 393224 | tf_op jit(solution)/shard_map/ppermute | solution.py:79
  10.5 7.2 %collective-permute-start.9 = (bf16[128,512]{1,0:T(8,128)(2,1)}, bf16[128,512]{1,0:T(8,128)(2,1)S(1)}, u32[]{:S(2)}, u32[]{:S(2)}) collective-permute-start(bf16[128,512]{1,0:T(8,128)(2,1)} %get-tuple-element.11), channel_id=1, source_target_pairs={{0,4},{2,6},{4,0},{6,2},{8,12},{10,14},{12,8},{14,10},{16,20},{18,... | collective-permute-start | bytes 393224 | tf_op jit(solution)/shard_map/ppermute | solution.py:75
  12.1 6.2 %collective-permute-start.3 = (bf16[4,128,128]{2,1,0:T(8,128)(2,1)S(1)}, bf16[4,128,128]{2,1,0:T(8,128)(2,1)S(1)}, u32[]{:S(2)}, u32[]{:S(2)}) collective-permute-start(bf16[4,128,128]{2,1,0:T(8,128)(2,1)S(1)} %pad_maximum_fusion.7), channel_id=1, source_target_pairs={{0,4},{2,6},{4,0},{6,2},{8,12},{10,14},{12,8},{14,10},{16,20},{18,... | collective-permute-start | bytes 393224 | tf_op jit(solution)/shard_map/ppermute | solution.py:75
  16.8 7.3 %collective-permute-start.1 = (bf16[256,512]{1,0:T(8,128)(2,1)S(1)}, bf16[256,512]{1,0:T(8,128)(2,1)S(1)}, u32[]{:S(2)}, u32[]{:S(2)}) collective-permute-start(bf16[256,512]{1,0:T(8,128)(2,1)S(1)} %pad_maximum_fusion.1), channel_id=1, source_target_pairs={{0,8},{2,10},{4,12},{6,14},{8,0},{10,2},{12,4},{14,6},{16,24},{18,... | collective-permute-start | bytes 786440 | tf_op jit(solution)/shard_map/ppermute | solution.py:79
  17.7 11.5 %collective-permute-start.10 = (bf16[256,512]{1,0:T(8,128)(2,1)S(1)}, bf16[256,512]{1,0:T(8,128)(2,1)S(1)}, u32[]{:S(2)}, u32[]{:S(2)}) collective-permute-start(bf16[256,512]{1,0:T(8,128)(2,1)S(1)} %pad_maximum_fusion.4), channel_id=1, source_target_pairs={{0,2},{2,0},{4,6},{6,4},{8,10},{10,8},{12,14},{14,12},{16,18},{18,... | collective-permute-start | bytes 786440 | tf_op jit(solution)/shard_map/ppermute | solution.py:75
  24.7 18.3 %collective-permute-start.4 = (bf16[1024,128]{1,0:T(8,128)(2,1)S(1)}, bf16[1024,128]{1,0:T(8,128)(2,1)S(1)}, u32[]{:S(2)}, u32[]{:S(2)}) collective-permute-start(bf16[1024,128]{1,0:T(8,128)(2,1)S(1)} %pad_maximum_fusion.3), channel_id=1, source_target_pairs={{0,2},{2,0},{4,6},{6,4},{8,10},{10,8},{12,14},{14,12},{16,18},{18,... | collective-permute-start | bytes 786440 | tf_op jit(solution)/shard_map/ppermute | solution.py:75
  25.5 6.1 %collective-permute-start.7 = (bf16[128,512]{1,0:T(8,128)(2,1)S(1)}, bf16[128,512]{1,0:T(8,128)(2,1)S(1)}, u32[]{:S(2)}, u32[]{:S(2)}) collective-permute-start(bf16[128,512]{1,0:T(8,128)(2,1)S(1)} %pad_maximum_fusion.9), channel_id=1, source_target_pairs={{0,4},{2,6},{4,0},{6,2},{8,12},{10,14},{12,8},{14,10},{16,20},{18,... | collective-permute-start | bytes 393224 | tf_op jit(solution)/shard_map/ppermute | solution.py:75
  27.1 8.6 %collective-permute-start.6 = (bf16[128,512]{1,0:T(8,128)(2,1)S(1)}, bf16[128,512]{1,0:T(8,128)(2,1)S(1)}, u32[]{:S(2)}, u32[]{:S(2)}) collective-permute-start(bf16[128,512]{1,0:T(8,128)(2,1)S(1)} %pad_maximum_fusion.8), channel_id=1, source_target_pairs={{0,2},{2,0},{4,6},{6,4},{8,10},{10,8},{12,14},{14,12},{16,18},{18,... | collective-permute-start | bytes 393224 | tf_op jit(solution)/shard_map/ppermute | solution.py:75
  28.7 9.3 %collective-permute-start.8 = (bf16[128,512]{1,0:T(8,128)(2,1)S(1)}, bf16[128,512]{1,0:T(8,128)(2,1)S(1)}, u32[]{:S(2)}, u32[]{:S(2)}) collective-permute-start(bf16[128,512]{1,0:T(8,128)(2,1)S(1)} %pad_maximum_fusion.10), channel_id=1, source_target_pairs={{0,6},{2,4},{4,2},{6,0},{8,14},{10,12},{12,10},{14,8},{16,22},{18,... | collective-permute-start | bytes 393224 | tf_op jit(solution)/shard_map/ppermute | solution.py:75
  29.8 20.7 %collective-permute-start.13 = (bf16[256,512]{1,0:T(8,128)(2,1)S(1)}, bf16[256,512]{1,0:T(8,128)(2,1)S(1)}, u32[]{:S(2)}, u32[]{:S(2)}) collective-permute-start(bf16[256,512]{1,0:T(8,128)(2,1)S(1)} %pad_maximum_fusion.5), channel_id=1, source_target_pairs={{0,8},{2,10},{4,12},{6,14},{8,0},{10,2},{12,4},{14,6},{16,24},{18,... | collective-permute-start | bytes 786440 | tf_op jit(solution)/shard_map/ppermute | solution.py:79
  40.5 6.4 %collective-permute-start.11 = (bf16[128,512]{1,0:T(8,128)(2,1)S(1)}, bf16[128,512]{1,0:T(8,128)(2,1)S(1)}, u32[]{:S(2)}, u32[]{:S(2)}) collective-permute-start(bf16[128,512]{1,0:T(8,128)(2,1)S(1)} %pad_maximum_fusion.11), channel_id=1, source_target_pairs={{0,8},{2,10},{4,12},{6,14},{8,0},{10,2},{12,4},{14,6},{16,24},{18,... | collective-permute-start | bytes 393224 | tf_op jit(solution)/shard_map/ppermute | solution.py:79
  43.0 10.6 %collective-permute-start.5 = (bf16[512,128]{1,0:T(8,128)(2,1)S(1)}, bf16[512,128]{1,0:T(8,128)(2,1)S(1)}, u32[]{:S(2)}, u32[]{:S(2)}) collective-permute-start(bf16[512,128]{1,0:T(8,128)(2,1)S(1)} %add_convert_fusion.1), channel_id=1, source_target_pairs={{0,4},{2,6},{4,0},{6,2},{8,12},{10,14},{12,8},{14,10},{16,20},{18,... | collective-permute-start | bytes 393224 | tf_op jit(solution)/shard_map/ppermute | solution.py:75
  46.8 6.1 %collective-permute-start.12 = (bf16[64,512]{1,0:T(8,128)(2,1)S(1)}, bf16[64,512]{1,0:T(8,128)(2,1)S(1)}, u32[]{:S(2)}, u32[]{:S(2)}) collective-permute-start(bf16[64,512]{1,0:T(8,128)(2,1)S(1)} %fusion.16), channel_id=1, source_target_pairs={{0,16},{2,18},{4,20},{6,22},{8,24},{10,26},{12,28},{14,30},{16,0},... | collective-permute-start | bytes 196616 | tf_op jit(solution)/shard_map/ppermute | solution.py:79
  50.5 11.8 %copy-start.1 = (bf16[128,1024]{1,0:T(8,128)(2,1)S(1)}, bf16[128,1024]{1,0:T(8,128)(2,1)}, u32[]{:S(2)}) copy-start(bf16[128,1024]{1,0:T(8,128)(2,1)} %hidden_ref.1) | copy-start | bytes 786436
  50.5 8.7 %collective-permute-start.14 = (bf16[128,512]{1,0:T(8,128)(2,1)S(1)}, bf16[128,512]{1,0:T(8,128)(2,1)S(1)}, u32[]{:S(2)}, u32[]{:S(2)}) collective-permute-start(bf16[128,512]{1,0:T(8,128)(2,1)S(1)} %fusion.10), channel_id=1, source_target_pairs={{0,16},{2,18},{4,20},{6,22},{8,24},{10,26},{12,28},{14,30},{16,0},... | collective-permute-start | bytes 393224 | tf_op jit(solution)/shard_map/ppermute | solution.py:79

commit v7 on v5

v7 whole, which is shorter than its diff:
```python
import jax
import jax.numpy as jnp
from jax import lax
from jax.sharding import PartitionSpec as P


def shards(hidden_pre, adj_vals, adj_cols, w_out, cotangent):
    feature_width = hidden_pre.shape[1]
    slots, tile_size = adj_vals.shape[1:3]
    blk_count = lax.axis_size("blk")
    rep_count = lax.axis_size("rep")
    section_span = blk_count // rep_count
    bits = (blk_count.bit_length() - 1) // 2
    side = 1 << bits
    per_core = section_span // side
    blk_pos = lax.axis_index("blk")
    rep_pos = lax.axis_index("rep")
    outer_pos, inner_pos = blk_pos >> bits, blk_pos & (side - 1)
    span_bits = section_span.bit_length() - 1
    cols_here = feature_width // rep_count
    rows_here = feature_width // blk_count
    bf16 = jnp.bfloat16
    turns = range(side)
    rising = [1 << b for b in range(bits)]

    def along_inner(value, turn):
        pairs = [(o * side + i, o * side + (i ^ turn)) for o in turns for i in turns]
        return lax.ppermute(value, "blk", pairs) if turn else value

    def along_outer(value, turn):
        pairs = [(o * side + i, (o ^ turn) * side + i) for o in turns for i in turns]
        return lax.ppermute(value, "blk", pairs) if turn else value

    def halved(parts, move, order, last_after):
        parts = dict(enumerate(parts))
        size = parts[0].shape[0]
        for bit in order:
            keys = [k for k in parts if not k & bit]
            sent = jnp.concatenate([parts[k ^ bit].astype(bf16) for k in keys], 0)
            got = move(after(sent, last_after) if bit == order[-1] else sent, bit)
            parts = {
                k: parts[k].astype(jnp.float32)
                + got[n * size : (n + 1) * size].astype(jnp.float32)
                for n, k in enumerate(keys)
            }
        return parts[0]

    def dot(lhs, rhs, dims):
        return lax.dot_general(lhs, rhs, (dims, ((), ())), preferred_element_type=jnp.float32)

    def after(value, *others):
        return lax.optimization_barrier((value,) + others)[0]

    def lanes(value, index):
        return value[:, index * tile_size : (index + 1) * tile_size]

    hidden_part = jnp.maximum(
        lax.dynamic_slice_in_dim(hidden_pre, rep_pos * cols_here, cols_here, 1), 0
    )
    hidden_stack = jnp.concatenate([along_outer(hidden_part, e) for e in turns], 0)

    columns = adj_cols[0]
    turn_of = (columns & (side - 1)) ^ inner_pos
    level_of = (columns >> bits) ^ outer_pos
    place = turn_of * per_core + (level_of & (per_core - 1))
    hit = place[None, :] == jnp.arange(section_span, dtype=jnp.int32)[:, None]
    ordered = jnp.zeros((section_span, tile_size, tile_size), bf16)
    for k in range(slots):
        ordered = jnp.where(hit[:, k, None, None], adj_vals[0, k][None], ordered)
    arrived = []
    for t in turns:
        message = ordered[t * per_core : (t + 1) * per_core]
        if t > 2:
            message = after(message, arrived[t - 2])
        arrived.append(along_inner(message, t))
    grad_part = lax.dynamic_slice_in_dim(cotangent, rep_pos * cols_here, cols_here, 1)
    grad_part = after(grad_part, arrived[2])
    grad_stack = jnp.concatenate([along_inner(grad_part, t) for t in turns], 0)
    everyone = lax.all_gather(jnp.concatenate(arrived, 0), "rep", axis=0)

    rows = []
    for t in turns:
        row_block = outer_pos * side + (inner_pos ^ t)
        row = []
        for e in turns:
            column_block = (outer_pos ^ e) * side + inner_pos
            holder = ((row_block - column_block) & (blk_count - 1)) >> span_bits
            index = t * per_core + e % per_core
            piece = everyone[0, index]
            for r in range(1, rep_count):
                piece = jnp.where(holder == r, everyone[r, index], piece)
            row.append(piece)
        rows.append(jnp.concatenate(row, 1))
    block = jnp.concatenate(rows, 0)

    mixed = dot(hidden_stack, block, ((0,), (1,))).astype(bf16)
    share = cols_here // side
    by_owner = mixed.reshape(share // rows_here, side, rows_here, side * tile_size)
    mixed_cols = []
    for t in turns:
        chosen = lax.dynamic_index_in_dim(by_owner, inner_pos ^ t, 1, keepdims=False)
        chosen = chosen.reshape(share, side * tile_size)
        chosen = jnp.concatenate([lanes(chosen, u ^ t) for u in turns], 1)
        mixed_cols.append(along_inner(chosen, t))
    first_col = mixed_cols[1]
    mixed_cols = sum(part.astype(jnp.float32) for part in mixed_cols).astype(bf16)
    mixed_cols = lax.all_gather(mixed_cols, "rep", axis=0, tiled=True)
    weight_part = dot(mixed_cols, grad_stack, ((1,), (0,))).astype(bf16)
    by_outer = weight_part.reshape(side, rows_here, cols_here)
    weight_got = [
        along_outer(lax.dynamic_index_in_dim(by_outer, outer_pos ^ t, 0, keepdims=False), t)
        for t in turns
    ]

    back = dot(after(grad_stack, mixed), block, ((0,), (0,)))
    back = halved([lanes(back, e) for e in turns], along_outer, rising, weight_part)
    rows_sum = halved(
        [lanes(after(mixed, first_col), t) for t in turns], along_inner, rising, weight_part
    )
    both = jnp.concatenate([rows_sum, back], 0).astype(bf16)
    both = lax.all_gather(both, "rep", axis=0)
    mixed_rows = both[:, :cols_here].reshape(feature_width, tile_size)
    back_full = both[:, cols_here:].reshape(feature_width, tile_size)

    w_columns = lax.dynamic_slice_in_dim(w_out, rep_pos * cols_here, cols_here, 1)
    out_part = dot(mixed_rows, w_columns, ((0,), (0,))).astype(bf16)
    w_rows = lax.dynamic_slice_in_dim(w_out, rep_pos * cols_here, cols_here, 0)
    grad_in = dot(back_full, w_rows, ((0,), (1,)))
    pre_part = lax.dynamic_slice_in_dim(hidden_pre, rep_pos * cols_here, cols_here, 1)
    grad_pre = jnp.where(pre_part > 0, grad_in, 0.0).astype(bf16)

    weight_got[1:], out_part, grad_pre = lax.optimization_barrier(
        (weight_got[1:], out_part, grad_pre)
    )
    grad_weight = sum(part.astype(jnp.float32) for part in weight_got)
    return (out_part, grad_weight, grad_pre)


def solution(mesh):
    placed = (P("blk", None), P("blk", "rep", None, None), P("blk", "rep"), P(), P("blk", None))
    return jax.shard_map(
        shards,
        mesh=mesh,
        in_specs=placed,
        out_specs=(P("blk", "rep"), P("blk", "rep"), P("blk", "rep")),
        check_vma=False,
    )
```

time: 60.5 us -> 60 us (level)
  starting transfers between devices: 21.1 us -> 30.1 us
  waiting for transfers between devices: 20.6 us -> 14.5 us
  other arithmetic: 5.29 us -> 3.26 us
  matrix products: 4.42 us -> 3.38 us
    ppermute x6 -> x11, starting transfers between devices: 7.17 us -> 16.3 us  [along_inner(): return lax.ppermute(value, 'blk', pairs) if turn else value]
    ppermute x9 -> x8, waiting for transfers between devices: 11 us -> 6.37 us  [along_outer(): return lax.ppermute(value, 'blk', pairs) if turn else value]
    ppermute x6 -> x11, waiting for transfers between devices: 9.57 us -> 8.18 us  [along_inner(): return lax.ppermute(value, 'blk', pairs) if turn else value]
    dot_general x5, matrix products: 4.42 us -> 3.38 us  [dot(): lax.dot_general(lhs, rhs, (dims, ((), ())), preferred_element_type=jnp.fl...]
    broadcast_in_dim x1 -> x0, other arithmetic: 0.99 us -> none  [shards(): jnp.where(hit[:, :, None, None], adj_vals[0][None].astype(jnp.float32), 0.0)]
    dynamic_slice x1, local copies, waits for them, and re-layouts: 0.92 us -> 0.01 us  [shards(): lax.dynamic_slice_in_dim(cotangent, rep_pos * cols_here, cols_here, 1)]
    broadcast_in_dim x0 -> x2, local copies, waits for them, and re-layouts: none -> 0.91 us  [shards(): ordered = jnp.where(hit[:, k, None, None], adj_vals[0, k][None], ordered)]
    max x1, other arithmetic: 1.73 us -> 1.09 us  [shards(): jnp.maximum(lax.dynamic_slice_in_dim(hidden_pre, rep_pos * cols_here, col...]
  transfers between devices with their start and end apart: 15 -> 19, of which waited for: 8 -> 6; matrix products, arithmetic and copies ran while one was open for 14% -> 10% of each run, Pallas kernels for 0% -> 0%
where the time goes in v7:
time: 60 us; the launch traced here: 59.8 us
  starting transfers between devices  30.1 us (50%)
  waiting for transfers between devices  14.5 us (24%)
  blocking collectives  6.36 us (11%)
  matrix products  3.38 us (6%)
  other arithmetic  3.26 us (5%)
  local copies, waits for them, and re-layouts  1.2 us (2%)
  between operations  0.95 us (2%)
    ppermute x11, starting transfers between devices, along_inner(): return lax.ppermute(value, 'blk', pairs) if turn else value  16.3 us
    ppermute x8, starting transfers between devices, along_outer(): return lax.ppermute(value, 'blk', pairs) if turn else value  13.8 us
    ppermute x11, waiting for transfers between devices, along_inner(): return lax.ppermute(value, 'blk', pairs) if turn else value  8.18 us
    ppermute x8, waiting for transfers between devices, along_outer(): return lax.ppermute(value, 'blk', pairs) if turn else value  6.37 us
    dot_general x5, matrix products, dot(): lax.dot_general(lhs, rhs, (dims, ((), ())), preferred_element_type=jnp.fl...  3.38 us
    all_gather x1, blocking collectives, shards(): everyone = lax.all_gather(jnp.concatenate(arrived, 0), 'rep', axis=0)  2.18 us
    all_gather x1, blocking collectives, shards(): both = lax.all_gather(both, 'rep', axis=0)  2.18 us
    all_gather x1, blocking collectives, shards(): mixed_cols = lax.all_gather(mixed_cols, 'rep', axis=0, tiled=True)  1.99 us
  transfers between devices with their start and end apart: 19, of which 6 were waited for; matrix products, arithmetic and copies ran while one was open for 10% of the time, Pallas kernels for 0%

profile of v7, /device:TPU:0, one launch (start us, length us, event | category | flops | bytes accessed | tf_op | source)
XLA Modules:
  0.0 59.8 jit_solution(15718205677575311775)
XLA Ops:
  0.7 1.1 %dynamic-slice_maximum_fusion = bf16[128,512]{1,0:T(8,128)(2,1)S(1)} fusion(bf16[128,1024]{1,0:T(8,128)(2,1)} %param.5, s32[]{:T(128)S(6)} %select_n.198), kind=kLoop, calls=%fused_computation.39 | loop fusion | flops 262144 | bytes 262148 | tf_op jit(solution)/shard_map/max | solution.py:57
  1.8 5.1 %collective-permute-start.2 = (bf16[128,512]{1,0:T(8,128)(2,1)S(1)}, bf16[128,512]{1,0:T(8,128)(2,1)S(1)}, u32[]{:S(2)}, u32[]{:S(2)}) collective-permute-start(bf16[128,512]{1,0:T(8,128)(2,1)S(1)} %dynamic-slice_maximum_fusion), channel_id=1, source_target_pairs={{0,24},{2,26},{4,28},{6,30},{8,16},{10,18},{12,20},{14,22},{16,8},... | collective-permute-start | bytes 393224 | tf_op jit(solution)/shard_map/ppermute | solution.py:32
  6.9 0.6 %collective-permute-start = (bf16[128,512]{1,0:T(8,128)(2,1)S(1)}, bf16[128,512]{1,0:T(8,128)(2,1)S(1)}, u32[]{:S(2)}, u32[]{:S(2)}) collective-permute-start(bf16[128,512]{1,0:T(8,128)(2,1)S(1)} %dynamic-slice_maximum_fusion), channel_id=1, source_target_pairs={{0,8},{2,10},{4,12},{6,14},{8,0},{10,2},{12,4},{14,6},{16,24},{18,... | collective-permute-start | bytes 393224 | tf_op jit(solution)/shard_map/ppermute | solution.py:32
  7.5 0.7 %add_bitcast_fusion = s32[8]{0:T(128)S(1)} fusion(s32[1,8]{1,0:T(1,128)} %param.7, s32[]{:T(128)S(6)} %shift_right_arithmetic.54, s32[]{:T(128)S(6)} %and.60), kind=kLoop, calls=%fused_computation.88 | loop fusion | flops 56 | bytes 72 | tf_op jit(solution)/shard_map/eq | solution.py:66
  8.3 0.9 %slice_bitcast_fusion.9 = (bf16[128,128]{1,0:T(8,128)(2,1)S(1)}, bf16[128,128]{1,0:T(8,128)(2,1)S(1)}, bf16[128,128]{1,0:T(8,128)(2,1)S(1)}, bf16[128,128]{1,0:T...) fusion(bf16[1,8,128,128]{3,2,1,0:T(8,128)(2,1)} %param.6), kind=kLoop, calls=%fused_computation.67 | loop fusion | bytes 524288 | tf_op jit(solution)/shard_map/jit(_where)/broadcast_in_dim | solution.py:69
  9.4 1.7 %collective-permute-start.4 = (bf16[2,128,128]{2,1,0:T(8,128)(2,1)S(1)}, bf16[2,128,128]{2,1,0:T(8,128)(2,1)S(1)}, u32[]{:S(2)}, u32[]{:S(2)}) collective-permute-start(bf16[2,128,128]{2,1,0:T(8,128)(2,1)S(1)} %get-tuple-element.55), channel_id=1, source_target_pairs={{0,4},{2,6},{4,0},{6,2},{8,12},{10,14},{12,8},{14,10},{16,20},{18,... | collective-permute-start | bytes 196616 | tf_op jit(solution)/shard_map/ppermute | solution.py:28
  11.1 1.5 %collective-permute-start.3 = (bf16[2,128,128]{2,1,0:T(8,128)(2,1)S(1)}, bf16[2,128,128]{2,1,0:T(8,128)(2,1)S(1)}, u32[]{:S(2)}, u32[]{:S(2)}) collective-permute-start(bf16[2,128,128]{2,1,0:T(8,128)(2,1)S(1)} %get-tuple-element.56), channel_id=1, source_target_pairs={{0,2},{2,0},{4,6},{6,4},{8,10},{10,8},{12,14},{14,12},{16,18},{18,... | collective-permute-start | bytes 196616 | tf_op jit(solution)/shard_map/ppermute | solution.py:28
  12.6 1.1 %collective-permute-done.4 = bf16[2,128,128]{2,1,0:T(8,128)(2,1)S(1)} collective-permute-done((bf16[2,128,128]{2,1,0:T(8,128)(2,1)S(1)}, bf16[2,128,128]{2,1,0:T(8,128)(2,1)S(1)}, u32[]{:S(2)}, u32[]{:S(2)}) %collective-permute-start.4) | collective-permute-done | bytes 65568 | tf_op jit(solution)/shard_map/ppermute | solution.py:28
  13.7 1.7 %collective-permute-done.3 = bf16[2,128,128]{2,1,0:T(8,128)(2,1)S(1)} collective-permute-done((bf16[2,128,128]{2,1,0:T(8,128)(2,1)S(1)}, bf16[2,128,128]{2,1,0:T(8,128)(2,1)S(1)}, u32[]{:S(2)}, u32[]{:S(2)}) %collective-permute-start.3) | collective-permute-done | bytes 65568 | tf_op jit(solution)/shard_map/ppermute | solution.py:28
  15.4 1.4 %collective-permute-start.5 = (bf16[2,128,128]{2,1,0:T(8,128)(2,1)S(1)}, bf16[2,128,128]{2,1,0:T(8,128)(2,1)S(1)}, u32[]{:S(2)}, u32[]{:S(2)}) collective-permute-start(bf16[2,128,128]{2,1,0:T(8,128)(2,1)S(1)} %get-tuple-element.14), channel_id=1, source_target_pairs={{0,6},{2,4},{4,2},{6,0},{8,14},{10,12},{12,10},{14,8},{16,22},{18,... | collective-permute-start | bytes 196616 | tf_op jit(solution)/shard_map/ppermute | solution.py:28
  16.8 1.5 %collective-permute-start.11 = (bf16[128,512]{1,0:T(8,128)(2,1)S(1)}, bf16[128,512]{1,0:T(8,128)(2,1)S(1)}, u32[]{:S(2)}, u32[]{:S(2)}) collective-permute-start(bf16[128,512]{1,0:T(8,128)(2,1)S(1)} %constant_dynamic-slice_fusion), channel_id=1, source_target_pairs={{0,6},{2,4},{4,2},{6,0},{8,14},{10,12},{12,10},{14,8},{16,22},{18,... | collective-permute-start | bytes 393224 | tf_op jit(solution)/shard_map/ppermute | solution.py:28
  18.3 2.3 %collective-permute-done.5 = bf16[2,128,128]{2,1,0:T(8,128)(2,1)S(1)} collective-permute-done((bf16[2,128,128]{2,1,0:T(8,128)(2,1)S(1)}, bf16[2,128,128]{2,1,0:T(8,128)(2,1)S(1)}, u32[]{:S(2)}, u32[]{:S(2)}) %collective-permute-start.5) | collective-permute-done | bytes 65568 | tf_op jit(solution)/shard_map/ppermute | solution.py:28
  20.6 1.1 %collective-permute-start.10 = (bf16[128,512]{1,0:T(8,128)(2,1)S(1)}, bf16[128,512]{1,0:T(8,128)(2,1)S(1)}, u32[]{:S(2)}, u32[]{:S(2)}) collective-permute-start(bf16[128,512]{1,0:T(8,128)(2,1)S(1)} %constant_dynamic-slice_fusion), channel_id=1, source_target_pairs={{0,4},{2,6},{4,0},{6,2},{8,12},{10,14},{12,8},{14,10},{16,20},{18,... | collective-permute-start | bytes 393224 | tf_op jit(solution)/shard_map/ppermute | solution.py:28
  21.7 2.2 %all-gather = bf16[16,128,128]{2,1,0:T(8,128)(2,1)S(1)} all-gather(bf16[8,128,128]{2,1,0:T(8,128)(2,1)S(1)} %pad_maximum_fusion), channel_id=2, replica_groups=mesh['blk'=16,'rep'=2] {'rep'}, dimensions={0}, use_global_device_ids=true | all-gather | bytes 786432 | tf_op jit(solution)/shard_map/all_gather | solution.py:79
  24.0 1.0 %collective-permute-start.9 = (bf16[128,512]{1,0:T(8,128)(2,1)S(1)}, bf16[128,512]{1,0:T(8,128)(2,1)S(1)}, u32[]{:S(2)}, u32[]{:S(2)}) collective-permute-start(bf16[128,512]{1,0:T(8,128)(2,1)S(1)} %constant_dynamic-slice_fusion), channel_id=1, source_target_pairs={{0,2},{2,0},{4,6},{6,4},{8,10},{10,8},{12,14},{14,12},{16,18},{18,... | collective-permute-start | bytes 393224 | tf_op jit(solution)/shard_map/ppermute | solution.py:28
  25.7 1.6 %collective-permute-start.7 = (bf16[128,512]{1,0:T(8,128)(2,1)S(1)}, bf16[128,512]{1,0:T(8,128)(2,1)S(1)}, u32[]{:S(2)}, u32[]{:S(2)}) collective-permute-start(bf16[128,512]{1,0:T(8,128)(2,1)S(1)} %pad_maximum_fusion.5), channel_id=1, source_target_pairs={{0,4},{2,6},{4,0},{6,2},{8,12},{10,14},{12,8},{14,10},{16,20},{18,... | collective-permute-start | bytes 393224 | tf_op jit(solution)/shard_map/ppermute | solution.py:28
  27.3 0.6 %collective-permute-start.6 = (bf16[128,512]{1,0:T(8,128)(2,1)S(1)}, bf16[128,512]{1,0:T(8,128)(2,1)S(1)}, u32[]{:S(2)}, u32[]{:S(2)}) collective-permute-start(bf16[128,512]{1,0:T(8,128)(2,1)S(1)} %pad_maximum_fusion.4), channel_id=1, source_target_pairs={{0,2},{2,0},{4,6},{6,4},{8,10},{10,8},{12,14},{14,12},{16,18},{18,... | collective-permute-start | bytes 393224 | tf_op jit(solution)/shard_map/ppermute | solution.py:28
  27.9 1.8 %collective-permute-done.9 = bf16[128,512]{1,0:T(8,128)(2,1)S(1)} collective-permute-done((bf16[128,512]{1,0:T(8,128)(2,1)S(1)}, bf16[128,512]{1,0:T(8,128)(2,1)S(1)}, u32[]{:S(2)}, u32[]{:S(2)}) %collective-permute-start.9) | collective-permute-done | bytes 131104 | tf_op jit(solution)/shard_map/ppermute | solution.py:28
  29.7 2.7 %collective-permute-start.8 = (bf16[128,512]{1,0:T(8,128)(2,1)S(1)}, bf16[128,512]{1,0:T(8,128)(2,1)S(1)}, u32[]{:S(2)}, u32[]{:S(2)}) collective-permute-start(bf16[128,512]{1,0:T(8,128)(2,1)S(1)} %pad_maximum_fusion.6), channel_id=1, source_target_pairs={{0,6},{2,4},{4,2},{6,0},{8,14},{10,12},{12,10},{14,8},{16,22},{18,... | collective-permute-start | bytes 393224 | tf_op jit(solution)/shard_map/ppermute | solution.py:28
  32.9 1.3 %collective-permute-start.17 = (bf16[1024,128]{1,0:T(8,128)(2,1)S(1)}, bf16[1024,128]{1,0:T(8,128)(2,1)S(1)}, u32[]{:S(2)}, u32[]{:S(2)}) collective-permute-start(bf16[1024,128]{1,0:T(8,128)(2,1)S(1)} %pad_maximum_fusion.2), channel_id=1, source_target_pairs={{0,8},{2,10},{4,12},{6,14},{8,0},{10,2},{12,4},{14,6},{16,24},{18,... | collective-permute-start | bytes 786440 | tf_op jit(solution)/shard_map/ppermute | solution.py:32
  34.3 1.4 %collective-permute-done.8 = bf16[128,512]{1,0:T(8,128)(2,1)S(1)} collective-permute-done((bf16[128,512]{1,0:T(8,128)(2,1)S(1)}, bf16[128,512]{1,0:T(8,128)(2,1)S(1)}, u32[]{:S(2)}, u32[]{:S(2)}) %collective-permute-start.8) | collective-permute-done | bytes 131104 | tf_op jit(solution)/shard_map/ppermute | solution.py:28
  35.7 2.0 %all_gather.15 = bf16[256,512]{1,0:T(8,128)(2,1)S(1)} all-gather(bf16[128,512]{1,0:T(8,128)(2,1)S(1)} %fusion.15), channel_id=1, replica_groups=mesh['blk'=16,'rep'=2] {'rep'}, dimensions={0}, use_global_device_ids=true | all-gather | bytes 393216 | tf_op jit(solution)/shard_map/all_gather | solution.py:107
  37.8 1.6 %collective-permute-start.15 = (bf16[1024,128]{1,0:T(8,128)(2,1)S(1)}, bf16[1024,128]{1,0:T(8,128)(2,1)S(1)}, u32[]{:S(2)}, u32[]{:S(2)}) collective-permute-start(bf16[1024,128]{1,0:T(8,128)(2,1)S(1)} %pad_maximum_fusion.1), channel_id=1, source_target_pairs={{0,2},{2,0},{4,6},{6,4},{8,10},{10,8},{12,14},{14,12},{16,18},{18,... | collective-permute-start | bytes 786440 | tf_op jit(solution)/shard_map/ppermute | solution.py:28
  39.7 3.7 %collective-permute-start.14 = (bf16[64,512]{1,0:T(8,128)(2,1)S(1)}, bf16[64,512]{1,0:T(8,128)(2,1)S(1)}, u32[]{:S(2)}, u32[]{:S(2)}) collective-permute-start(bf16[64,512]{1,0:T(8,128)(2,1)S(1)} %get-tuple-element.50), channel_id=1, source_target_pairs={{0,24},{2,26},{4,28},{6,30},{8,16},{10,18},{12,20},{14,22},{16,8},... | collective-permute-start | bytes 196616 | tf_op jit(solution)/shard_map/ppermute | solution.py:32
  43.4 0.7 %collective-permute-start.12 = (bf16[64,512]{1,0:T(8,128)(2,1)S(1)}, bf16[64,512]{1,0:T(8,128)(2,1)S(1)}, u32[]{:S(2)}, u32[]{:S(2)}) collective-permute-start(bf16[64,512]{1,0:T(8,128)(2,1)S(1)} %get-tuple-element.52), channel_id=1, source_target_pairs={{0,8},{2,10},{4,12},{6,14},{8,0},{10,2},{12,4},{14,6},{16,24},{18,... | collective-permute-start | bytes 196616 | tf_op jit(solution)/shard_map/ppermute | solution.py:32
  44.2 2.2 %collective-permute-start.18 = (bf16[512,128]{1,0:T(8,128)(2,1)S(1)}, bf16[512,128]{1,0:T(8,128)(2,1)S(1)}, u32[]{:S(2)}, u32[]{:S(2)}) collective-permute-start(bf16[512,128]{1,0:T(8,128)(2,1)S(1)} %fusion.10), channel_id=1, source_target_pairs={{0,16},{2,18},{4,20},{6,22},{8,24},{10,26},{12,28},{14,30},{16,0},... | collective-permute-start | bytes 393224 | tf_op jit(solution)/shard_map/ppermute | solution.py:32
  46.5 1.7 %collective-permute-start.16 = (bf16[512,128]{1,0:T(8,128)(2,1)S(1)}, bf16[512,128]{1,0:T(8,128)(2,1)S(1)}, u32[]{:S(2)}, u32[]{:S(2)}) collective-permute-start(bf16[512,128]{1,0:T(8,128)(2,1)S(1)} %add_convert_fusion.1), channel_id=1, source_target_pairs={{0,4},{2,6},{4,0},{6,2},{8,12},{10,14},{12,8},{14,10},{16,20},{18,... | collective-permute-start | bytes 393224 | tf_op jit(solution)/shard_map/ppermute | solution.py:28
  48.2 6.4 %collective-permute-done.18 = bf16[512,128]{1,0:T(8,128)(2,1)S(1)} collective-permute-done((bf16[512,128]{1,0:T(8,128)(2,1)S(1)}, bf16[512,128]{1,0:T(8,128)(2,1)S(1)}, u32[]{:S(2)}, u32[]{:S(2)}) %collective-permute-start.18) | collective-permute-done | bytes 131104 | tf_op jit(solution)/shard_map/ppermute | solution.py:32
  54.7 2.2 %all_gather.16 = bf16[2,1024,128]{2,1,0:T(8,128)(2,1)S(1)} all-gather(bf16[1,1024,128]{2,1,0:T(8,128)(2,1)S(1)} %pad_maximum_fusion.3), channel_id=1, replica_groups=mesh['blk'=16,'rep'=2] {'rep'}, dimensions={0}, use_global_device_ids=true | all-gather | bytes 786432 | tf_op jit(solution)/shard_map/all_gather | solution.py:121
  56.9 1.2 %fusion = bf16[128,512]{1,0:T(8,128)(2,1)} fusion(bf16[1024,128]{1,0:T(8,128)(2,1)S(1)} %bitcast.109, bf16[1024,1024]{1,0:T(8,128)(2,1)S(1)} %copy-done, s32[]{:T(128)S(6)} %select_n.198, bf16[128,1024]{1,0:T(8,128)(2,1)S(1)} %copy-done.1), kind=kOutput, calls=%fused_computation.4 | convolution fusion | flops 134545408 | bytes 1573888 | tf_op jit(solution)/shard_map/dot_general | solution.py:49
  58.1 1.0 %convolution_convert_fusion.2 = bf16[128,512]{1,0:T(8,128)(2,1)} fusion(bf16[1024,128]{1,0:T(8,128)(2,1)S(1)} %bitcast.108, bf16[1024,1024]{1,0:T(8,128)(2,1)S(1)} %copy-done, s32[]{:T(128)S(6)} %select_n.198), kind=kOutput, calls=%fused_computation.3 | convolution fusion | flops 134283264 | bytes 1441796 | tf_op jit(solution)/shard_map/dot_general | solution.py:49
  59.1 0.7 %fusion.19 = f32[64,512]{1,0:T(8,128)} fusion(bf16[64,512]{1,0:T(8,128)(2,1)S(1)} %collective-permute-done.14, bf16[64,512]{1,0:T(8,128)(2,1)S(1)} %collective-permute-done.13, bf16[64,512]{1,0:T(8,128)(2,1)S(1)} %collective-permute-done.12, bf16[4,64,512]{2,1,0:T(8,128)(2,1)S(1)} %bitcast.107, s32[]{:T(128)S(6)} %select_n.259), kind=kLoop, calls=%fused_computation.38 | loop fusion | flops 229376 | bytes 393220 | tf_op jit(solution)/shard_map/add | solution.py:135
  (58 shorter events, 2.4 us)
Async XLA Ops:
  0.6 56.3 %copy-start = (bf16[1024,1024]{1,0:T(8,128)(2,1)S(1)}, bf16[1024,1024]{1,0:T(8,128)(2,1)}, u32[]{:S(2)}) copy-start(bf16[1024,1024]{1,0:T(8,128)(2,1)} %param.8) | copy-start | bytes 6291460
  0.6 12.0 %copy-start.2 = (bf16[128,1024]{1,0:T(8,128)(2,1)S(1)}, bf16[128,1024]{1,0:T(8,128)(2,1)}, u32[]{:S(2)}) copy-start(bf16[128,1024]{1,0:T(8,128)(2,1)} %param.9) | copy-start | bytes 786436
  1.8 22.3 %collective-permute-start.2 = (bf16[128,512]{1,0:T(8,128)(2,1)S(1)}, bf16[128,512]{1,0:T(8,128)(2,1)S(1)}, u32[]{:S(2)}, u32[]{:S(2)}) collective-permute-start(bf16[128,512]{1,0:T(8,128)(2,1)S(1)} %dynamic-slice_maximum_fusion), channel_id=1, source_target_pairs={{0,24},{2,26},{4,28},{6,30},{8,16},{10,18},{12,20},{14,22},{16,8},... | collective-permute-start | bytes 393224 | tf_op jit(solution)/shard_map/ppermute | solution.py:32
  6.9 18.2 %collective-permute-start.1 = (bf16[128,512]{1,0:T(8,128)(2,1)S(1)}, bf16[128,512]{1,0:T(8,128)(2,1)S(1)}, u32[]{:S(2)}, u32[]{:S(2)}) collective-permute-start(bf16[128,512]{1,0:T(8,128)(2,1)S(1)} %dynamic-slice_maximum_fusion), channel_id=1, source_target_pairs={{0,16},{2,18},{4,20},{6,22},{8,24},{10,26},{12,28},{14,30},{16,0},... | collective-permute-start | bytes 393224 | tf_op jit(solution)/shard_map/ppermute | solution.py:32
  6.9 18.2 %collective-permute-start = (bf16[128,512]{1,0:T(8,128)(2,1)S(1)}, bf16[128,512]{1,0:T(8,128)(2,1)S(1)}, u32[]{:S(2)}, u32[]{:S(2)}) collective-permute-start(bf16[128,512]{1,0:T(8,128)(2,1)S(1)} %dynamic-slice_maximum_fusion), channel_id=1, source_target_pairs={{0,8},{2,10},{4,12},{6,14},{8,0},{10,2},{12,4},{14,6},{16,24},{18,... | collective-permute-start | bytes 393224 | tf_op jit(solution)/shard_map/ppermute | solution.py:32
  9.4 4.3 %collective-permute-start.4 = (bf16[2,128,128]{2,1,0:T(8,128)(2,1)S(1)}, bf16[2,128,128]{2,1,0:T(8,128)(2,1)S(1)}, u32[]{:S(2)}, u32[]{:S(2)}) collective-permute-start(bf16[2,128,128]{2,1,0:T(8,128)(2,1)S(1)} %get-tuple-element.55), channel_id=1, source_target_pairs={{0,4},{2,6},{4,0},{6,2},{8,12},{10,14},{12,8},{14,10},{16,20},{18,... | collective-permute-start | bytes 196616 | tf_op jit(solution)/shard_map/ppermute | solution.py:28
  11.1 4.3 %collective-permute-start.3 = (bf16[2,128,128]{2,1,0:T(8,128)(2,1)S(1)}, bf16[2,128,128]{2,1,0:T(8,128)(2,1)S(1)}, u32[]{:S(2)}, u32[]{:S(2)}) collective-permute-start(bf16[2,128,128]{2,1,0:T(8,128)(2,1)S(1)} %get-tuple-element.56), channel_id=1, source_target_pairs={{0,2},{2,0},{4,6},{6,4},{8,10},{10,8},{12,14},{14,12},{16,18},{18,... | collective-permute-start | bytes 196616 | tf_op jit(solution)/shard_map/ppermute | solution.py:28
  15.4 5.2 %collective-permute-start.5 = (bf16[2,128,128]{2,1,0:T(8,128)(2,1)S(1)}, bf16[2,128,128]{2,1,0:T(8,128)(2,1)S(1)}, u32[]{:S(2)}, u32[]{:S(2)}) collective-permute-start(bf16[2,128,128]{2,1,0:T(8,128)(2,1)S(1)} %get-tuple-element.14), channel_id=1, source_target_pairs={{0,6},{2,4},{4,2},{6,0},{8,14},{10,12},{12,10},{14,8},{16,22},{18,... | collective-permute-start | bytes 196616 | tf_op jit(solution)/shard_map/ppermute | solution.py:28
  16.8 15.6 %collective-permute-start.11 = (bf16[128,512]{1,0:T(8,128)(2,1)S(1)}, bf16[128,512]{1,0:T(8,128)(2,1)S(1)}, u32[]{:S(2)}, u32[]{:S(2)}) collective-permute-start(bf16[128,512]{1,0:T(8,128)(2,1)S(1)} %constant_dynamic-slice_fusion), channel_id=1, source_target_pairs={{0,6},{2,4},{4,2},{6,0},{8,14},{10,12},{12,10},{14,8},{16,22},{18,... | collective-permute-start | bytes 393224 | tf_op jit(solution)/shard_map/ppermute | solution.py:28
  20.6 11.8 %collective-permute-start.10 = (bf16[128,512]{1,0:T(8,128)(2,1)S(1)}, bf16[128,512]{1,0:T(8,128)(2,1)S(1)}, u32[]{:S(2)}, u32[]{:S(2)}) collective-permute-start(bf16[128,512]{1,0:T(8,128)(2,1)S(1)} %constant_dynamic-slice_fusion), channel_id=1, source_target_pairs={{0,4},{2,6},{4,0},{6,2},{8,12},{10,14},{12,8},{14,10},{16,20},{18,... | collective-permute-start | bytes 393224 | tf_op jit(solution)/shard_map/ppermute | solution.py:28
  24.0 5.6 %collective-permute-start.9 = (bf16[128,512]{1,0:T(8,128)(2,1)S(1)}, bf16[128,512]{1,0:T(8,128)(2,1)S(1)}, u32[]{:S(2)}, u32[]{:S(2)}) collective-permute-start(bf16[128,512]{1,0:T(8,128)(2,1)S(1)} %constant_dynamic-slice_fusion), channel_id=1, source_target_pairs={{0,2},{2,0},{4,6},{6,4},{8,10},{10,8},{12,14},{14,12},{16,18},{18,... | collective-permute-start | bytes 393224 | tf_op jit(solution)/shard_map/ppermute | solution.py:28
  25.7 8.6 %collective-permute-start.7 = (bf16[128,512]{1,0:T(8,128)(2,1)S(1)}, bf16[128,512]{1,0:T(8,128)(2,1)S(1)}, u32[]{:S(2)}, u32[]{:S(2)}) collective-permute-start(bf16[128,512]{1,0:T(8,128)(2,1)S(1)} %pad_maximum_fusion.5), channel_id=1, source_target_pairs={{0,4},{2,6},{4,0},{6,2},{8,12},{10,14},{12,8},{14,10},{16,20},{18,... | collective-permute-start | bytes 393224 | tf_op jit(solution)/shard_map/ppermute | solution.py:28
  27.3 7.0 %collective-permute-start.6 = (bf16[128,512]{1,0:T(8,128)(2,1)S(1)}, bf16[128,512]{1,0:T(8,128)(2,1)S(1)}, u32[]{:S(2)}, u32[]{:S(2)}) collective-permute-start(bf16[128,512]{1,0:T(8,128)(2,1)S(1)} %pad_maximum_fusion.4), channel_id=1, source_target_pairs={{0,2},{2,0},{4,6},{6,4},{8,10},{10,8},{12,14},{14,12},{16,18},{18,... | collective-permute-start | bytes 393224 | tf_op jit(solution)/shard_map/ppermute | solution.py:28
  29.7 6.0 %collective-permute-start.8 = (bf16[128,512]{1,0:T(8,128)(2,1)S(1)}, bf16[128,512]{1,0:T(8,128)(2,1)S(1)}, u32[]{:S(2)}, u32[]{:S(2)}) collective-permute-start(bf16[128,512]{1,0:T(8,128)(2,1)S(1)} %pad_maximum_fusion.6), channel_id=1, source_target_pairs={{0,6},{2,4},{4,2},{6,0},{8,14},{10,12},{12,10},{14,8},{16,22},{18,... | collective-permute-start | bytes 393224 | tf_op jit(solution)/shard_map/ppermute | solution.py:28
  32.9 11.2 %collective-permute-start.17 = (bf16[1024,128]{1,0:T(8,128)(2,1)S(1)}, bf16[1024,128]{1,0:T(8,128)(2,1)S(1)}, u32[]{:S(2)}, u32[]{:S(2)}) collective-permute-start(bf16[1024,128]{1,0:T(8,128)(2,1)S(1)} %pad_maximum_fusion.2), channel_id=1, source_target_pairs={{0,8},{2,10},{4,12},{6,14},{8,0},{10,2},{12,4},{14,6},{16,24},{18,... | collective-permute-start | bytes 786440 | tf_op jit(solution)/shard_map/ppermute | solution.py:32
  37.8 8.7 %collective-permute-start.15 = (bf16[1024,128]{1,0:T(8,128)(2,1)S(1)}, bf16[1024,128]{1,0:T(8,128)(2,1)S(1)}, u32[]{:S(2)}, u32[]{:S(2)}) collective-permute-start(bf16[1024,128]{1,0:T(8,128)(2,1)S(1)} %pad_maximum_fusion.1), channel_id=1, source_target_pairs={{0,2},{2,0},{4,6},{6,4},{8,10},{10,8},{12,14},{14,12},{16,18},{18,... | collective-permute-start | bytes 786440 | tf_op jit(solution)/shard_map/ppermute | solution.py:28
  39.7 19.4 %collective-permute-start.14 = (bf16[64,512]{1,0:T(8,128)(2,1)S(1)}, bf16[64,512]{1,0:T(8,128)(2,1)S(1)}, u32[]{:S(2)}, u32[]{:S(2)}) collective-permute-start(bf16[64,512]{1,0:T(8,128)(2,1)S(1)} %get-tuple-element.50), channel_id=1, source_target_pairs={{0,24},{2,26},{4,28},{6,30},{8,16},{10,18},{12,20},{14,22},{16,8},... | collective-permute-start | bytes 196616 | tf_op jit(solution)/shard_map/ppermute | solution.py:32
  43.4 15.7 %collective-permute-start.13 = (bf16[64,512]{1,0:T(8,128)(2,1)S(1)}, bf16[64,512]{1,0:T(8,128)(2,1)S(1)}, u32[]{:S(2)}, u32[]{:S(2)}) collective-permute-start(bf16[64,512]{1,0:T(8,128)(2,1)S(1)} %get-tuple-element.51), channel_id=1, source_target_pairs={{0,16},{2,18},{4,20},{6,22},{8,24},{10,26},{12,28},{14,30},{16,0},... | collective-permute-start | bytes 196616 | tf_op jit(solution)/shard_map/ppermute | solution.py:32
  43.4 15.7 %collective-permute-start.12 = (bf16[64,512]{1,0:T(8,128)(2,1)S(1)}, bf16[64,512]{1,0:T(8,128)(2,1)S(1)}, u32[]{:S(2)}, u32[]{:S(2)}) collective-permute-start(bf16[64,512]{1,0:T(8,128)(2,1)S(1)} %get-tuple-element.52), channel_id=1, source_target_pairs={{0,8},{2,10},{4,12},{6,14},{8,0},{10,2},{12,4},{14,6},{16,24},{18,... | collective-permute-start | bytes 196616 | tf_op jit(solution)/shard_map/ppermute | solution.py:32
  44.2 12.7 %copy-start.1 = (bf16[128,1024]{1,0:T(8,128)(2,1)S(1)}, bf16[128,1024]{1,0:T(8,128)(2,1)}, u32[]{:S(2)}) copy-start(bf16[128,1024]{1,0:T(8,128)(2,1)} %param.5) | copy-start | bytes 786436
  44.2 10.3 %collective-permute-start.18 = (bf16[512,128]{1,0:T(8,128)(2,1)S(1)}, bf16[512,128]{1,0:T(8,128)(2,1)S(1)}, u32[]{:S(2)}, u32[]{:S(2)}) collective-permute-start(bf16[512,128]{1,0:T(8,128)(2,1)S(1)} %fusion.10), channel_id=1, source_target_pairs={{0,16},{2,18},{4,20},{6,22},{8,24},{10,26},{12,28},{14,30},{16,0},... | collective-permute-start | bytes 393224 | tf_op jit(solution)/shard_map/ppermute | solution.py:32
  46.5 8.1 %collective-permute-start.16 = (bf16[512,128]{1,0:T(8,128)(2,1)S(1)}, bf16[512,128]{1,0:T(8,128)(2,1)S(1)}, u32[]{:S(2)}, u32[]{:S(2)}) collective-permute-start(bf16[512,128]{1,0:T(8,128)(2,1)S(1)} %add_convert_fusion.1), channel_id=1, source_target_pairs={{0,4},{2,6},{4,0},{6,2},{8,12},{10,14},{12,8},{14,10},{16,20},{18,... | collective-permute-start | bytes 393224 | tf_op jit(solution)/shard_map/ppermute | solution.py:28

commit v8 on v7

--- a/solution.py
+++ b/solution.py
@@ -31,19 +31,19 @@
         pairs = [(o * side + i, (o ^ turn) * side + i) for o in turns for i in turns]
         return lax.ppermute(value, "blk", pairs) if turn else value
 
-    def halved(parts, move, order, last_after):
+    def halved(parts, move, order):
         parts = dict(enumerate(parts))
         size = parts[0].shape[0]
         for bit in order:
             keys = [k for k in parts if not k & bit]
             sent = jnp.concatenate([parts[k ^ bit].astype(bf16) for k in keys], 0)
-            got = move(after(sent, last_after) if bit == order[-1] else sent, bit)
+            got = move(sent, bit)
             parts = {
                 k: parts[k].astype(jnp.float32)
                 + got[n * size : (n + 1) * size].astype(jnp.float32)
                 for n, k in enumerate(keys)
             }
-        return parts[0]
+        return parts
 
     def dot(lhs, rhs, dims):
         return lax.dot_general(lhs, rhs, (dims, ((), ())), preferred_element_type=jnp.float32)
@@ -57,9 +57,15 @@
     hidden_part = jnp.maximum(
         lax.dynamic_slice_in_dim(hidden_pre, rep_pos * cols_here, cols_here, 1), 0
     )
-    hidden_stack = jnp.concatenate([along_outer(hidden_part, e) for e in turns], 0)
+    held = {0: hidden_part}
+    for bit in rising[::-1]:
+        keys = list(held)
+        got = along_outer(jnp.concatenate([held[k] for k in keys], 0), bit)
+        for n, k in enumerate(keys):
+            held[k ^ bit] = got[n * tile_size : (n + 1) * tile_size]
+    hidden_stack = jnp.concatenate([held[e] for e in turns], 0)
 
-    columns = adj_cols[0]
+    columns = after(adj_cols, hidden_part)[0]
     turn_of = (columns & (side - 1)) ^ inner_pos
     level_of = (columns >> bits) ^ outer_pos
     place = turn_of * per_core + (level_of & (per_core - 1))
@@ -70,11 +76,9 @@
     arrived = []
     for t in turns:
         message = ordered[t * per_core : (t + 1) * per_core]
-        if t > 2:
-            message = after(message, arrived[t - 2])
         arrived.append(along_inner(message, t))
     grad_part = lax.dynamic_slice_in_dim(cotangent, rep_pos * cols_here, cols_here, 1)
-    grad_part = after(grad_part, arrived[2])
+    grad_part = after(grad_part, *arrived[1:])
     grad_stack = jnp.concatenate([along_inner(grad_part, t) for t in turns], 0)
     everyone = lax.all_gather(jnp.concatenate(arrived, 0), "rep", axis=0)
 
@@ -102,9 +106,14 @@
         chosen = chosen.reshape(share, side * tile_size)
         chosen = jnp.concatenate([lanes(chosen, u ^ t) for u in turns], 1)
         mixed_cols.append(along_inner(chosen, t))
-    first_col = mixed_cols[1]
     mixed_cols = sum(part.astype(jnp.float32) for part in mixed_cols).astype(bf16)
     mixed_cols = lax.all_gather(mixed_cols, "rep", axis=0, tiled=True)
+    back = dot(after(grad_stack, mixed), block, ((0,), (0,)))
+    rows = after(mixed, back)
+    back = halved([lanes(back, e) for e in turns], along_outer, rising[:-1])
+    rows = halved([lanes(rows, t) for t in turns], along_inner, rising[:-1])
+
+    mixed_cols, back[0] = lax.optimization_barrier((mixed_cols, back[0]))
     weight_part = dot(mixed_cols, grad_stack, ((1,), (0,))).astype(bf16)
     by_outer = weight_part.reshape(side, rows_here, cols_here)
     weight_got = [
@@ -112,11 +121,11 @@
         for t in turns
     ]
 
-    back = dot(after(grad_stack, mixed), block, ((0,), (0,)))
-    back = halved([lanes(back, e) for e in turns], along_outer, rising, weight_part)
-    rows_sum = halved(
-        [lanes(after(mixed, first_col), t) for t in turns], along_inner, rising, weight_part
-    )
+    last = rising[-1]
+    back_got = along_outer(back[last].astype(bf16), last).astype(jnp.float32)
+    rows_got = after(rows[last].astype(bf16), weight_part)
+    rows_got = along_inner(rows_got, last).astype(jnp.float32)
+    rows_sum, back = rows[0] + rows_got, back[0] + back_got
     both = jnp.concatenate([rows_sum, back], 0).astype(bf16)
     both = lax.all_gather(both, "rep", axis=0)
     mixed_rows = both[:, :cols_here].reshape(feature_width, tile_size)

time: 60 us -> 67.5 us (1.12)
  waiting for transfers between devices: 14.5 us -> 25.5 us
  starting transfers between devices: 30.1 us -> 25 us
  other arithmetic: 3.26 us -> 4.83 us
    ppermute x8 -> x7, waiting for transfers between devices: 6.37 us -> 13.8 us  [along_outer(): return lax.ppermute(value, 'blk', pairs) if turn else value]
    ppermute x11, waiting for transfers between devices: 8.18 us -> 11.7 us  [along_inner(): return lax.ppermute(value, 'blk', pairs) if turn else value]
    ppermute x11, starting transfers between devices: 16.3 us -> 12.8 us  [along_inner(): return lax.ppermute(value, 'blk', pairs) if turn else value]
    ppermute x8 -> x7, starting transfers between devices: 13.8 us -> 12.2 us  [along_outer(): return lax.ppermute(value, 'blk', pairs) if turn else value]
    concatenate x3, other arithmetic: 0.13 us -> 1.01 us  [shards(): both = jnp.concatenate([rows_sum, back], 0).astype(bf16)]
  transfers between devices with their start and end apart: 19 -> 18, of which waited for: 6 -> 7; matrix products, arithmetic and copies ran while one was open for 10% -> 9% of each run, Pallas kernels for 0% -> 0%
where the time goes in v8:
time: 67.5 us; the launch traced here: 67.2 us
  waiting for transfers between devices  25.5 us (38%)
  starting transfers between devices  25 us (37%)
  blocking collectives  6.36 us (9%)
  other arithmetic  4.83 us (7%)
  matrix products  3.39 us (5%)
  local copies, waits for them, and re-layouts  1.19 us (2%)
  between operations  0.94 us (1%)
    ppermute x7, waiting for transfers between devices, along_outer(): return lax.ppermute(value, 'blk', pairs) if turn else value  13.8 us
    ppermute x11, starting transfers between devices, along_inner(): return lax.ppermute(value, 'blk', pairs) if turn else value  12.8 us
    ppermute x7, starting transfers between devices, along_outer(): return lax.ppermute(value, 'blk', pairs) if turn else value  12.2 us
    ppermute x11, waiting for transfers between devices, along_inner(): return lax.ppermute(value, 'blk', pairs) if turn else value  11.7 us
    dot_general x5, matrix products, dot(): lax.dot_general(lhs, rhs, (dims, ((), ())), preferred_element_type=jnp.fl...  3.39 us
    all_gather x1, blocking collectives, shards(): everyone = lax.all_gather(jnp.concatenate(arrived, 0), 'rep', axis=0)  2.18 us
    all_gather x1, blocking collectives, shards(): both = lax.all_gather(both, 'rep', axis=0)  2.18 us
    all_gather x1, blocking collectives, shards(): mixed_cols = lax.all_gather(mixed_cols, 'rep', axis=0, tiled=True)  1.99 us
  transfers between devices with their start and end apart: 18, of which 7 were waited for; matrix products, arithmetic and copies ran while one was open for 9% of the time, Pallas kernels for 0%

profile of v8, /device:TPU:0, one launch (start us, length us, event | category | flops | bytes accessed | tf_op | source)
XLA Modules:
  0.0 67.2 jit_solution(14359521719274575916)
XLA Ops:
  0.7 1.1 %dynamic-slice_maximum_fusion = bf16[128,512]{1,0:T(8,128)(2,1)S(1)} fusion(bf16[128,1024]{1,0:T(8,128)(2,1)} %param.5, s32[]{:T(128)S(6)} %select_n.198), kind=kLoop, calls=%fused_computation.39 | loop fusion | flops 262144 | bytes 262148 | tf_op jit(solution)/shard_map/max | solution.py:57
  1.8 4.1 %collective-permute-start = (bf16[128,512]{1,0:T(8,128)(2,1)S(1)}, bf16[128,512]{1,0:T(8,128)(2,1)S(1)}, u32[]{:S(2)}, u32[]{:S(2)}) collective-permute-start(bf16[128,512]{1,0:T(8,128)(2,1)S(1)} %dynamic-slice_maximum_fusion), channel_id=1, source_target_pairs={{0,16},{2,18},{4,20},{6,22},{8,24},{10,26},{12,28},{14,30},{16,0},... | collective-permute-start | bytes 393224 | tf_op jit(solution)/shard_map/ppermute | solution.py:32
  5.9 0.7 add_bitcast_fusion
  6.6 0.9 %slice_bitcast_fusion.9 = (bf16[128,128]{1,0:T(8,128)(2,1)S(1)}, bf16[128,128]{1,0:T(8,128)(2,1)S(1)}, bf16[128,128]{1,0:T(8,128)(2,1)S(1)}, bf16[128,128]{1,0:T...) fusion(bf16[1,8,128,128]{3,2,1,0:T(8,128)(2,1)} %param.6), kind=kLoop, calls=%fused_computation.67 | loop fusion | bytes 524288 | tf_op jit(solution)/shard_map/jit(_where)/broadcast_in_dim | solution.py:75
  7.7 1.6 %collective-permute-start.2 = (bf16[2,128,128]{2,1,0:T(8,128)(2,1)S(1)}, bf16[2,128,128]{2,1,0:T(8,128)(2,1)S(1)}, u32[]{:S(2)}, u32[]{:S(2)}) collective-permute-start(bf16[2,128,128]{2,1,0:T(8,128)(2,1)S(1)} %get-tuple-element.62), channel_id=1, source_target_pairs={{0,2},{2,0},{4,6},{6,4},{8,10},{10,8},{12,14},{14,12},{16,18},{18,... | collective-permute-start | bytes 196616 | tf_op jit(solution)/shard_map/ppermute | solution.py:28
  9.3 1.5 %collective-permute-start.3 = (bf16[2,128,128]{2,1,0:T(8,128)(2,1)S(1)}, bf16[2,128,128]{2,1,0:T(8,128)(2,1)S(1)}, u32[]{:S(2)}, u32[]{:S(2)}) collective-permute-start(bf16[2,128,128]{2,1,0:T(8,128)(2,1)S(1)} %get-tuple-element.61), channel_id=1, source_target_pairs={{0,4},{2,6},{4,0},{6,2},{8,12},{10,14},{12,8},{14,10},{16,20},{18,... | collective-permute-start | bytes 196616 | tf_op jit(solution)/shard_map/ppermute | solution.py:28
  11.3 0.8 %collective-permute-done.2 = bf16[2,128,128]{2,1,0:T(8,128)(2,1)S(1)} collective-permute-done((bf16[2,128,128]{2,1,0:T(8,128)(2,1)S(1)}, bf16[2,128,128]{2,1,0:T(8,128)(2,1)S(1)}, u32[]{:S(2)}, u32[]{:S(2)}) %collective-permute-start.2) | collective-permute-done | bytes 65568 | tf_op jit(solution)/shard_map/ppermute | solution.py:28
  12.1 2.2 %collective-permute-done.3 = bf16[2,128,128]{2,1,0:T(8,128)(2,1)S(1)} collective-permute-done((bf16[2,128,128]{2,1,0:T(8,128)(2,1)S(1)}, bf16[2,128,128]{2,1,0:T(8,128)(2,1)S(1)}, u32[]{:S(2)}, u32[]{:S(2)}) %collective-permute-start.3) | collective-permute-done | bytes 65568 | tf_op jit(solution)/shard_map/ppermute | solution.py:28
  14.2 1.7 %collective-permute-done.4 = bf16[2,128,128]{2,1,0:T(8,128)(2,1)S(1)} collective-permute-done((bf16[2,128,128]{2,1,0:T(8,128)(2,1)S(1)}, bf16[2,128,128]{2,1,0:T(8,128)(2,1)S(1)}, u32[]{:S(2)}, u32[]{:S(2)}) %collective-permute-start.4) | collective-permute-done | bytes 65568 | tf_op jit(solution)/shard_map/ppermute | solution.py:28
  16.0 0.5 collective-permute-start.8
  17.0 2.4 %collective-permute-start.10 = (bf16[128,512]{1,0:T(8,128)(2,1)S(1)}, bf16[128,512]{1,0:T(8,128)(2,1)S(1)}, u32[]{:S(2)}, u32[]{:S(2)}) collective-permute-start(bf16[128,512]{1,0:T(8,128)(2,1)S(1)} %constant_dynamic-slice_fusion), channel_id=1, source_target_pairs={{0,6},{2,4},{4,2},{6,0},{8,14},{10,12},{12,10},{14,8},{16,22},{18,... | collective-permute-start | bytes 393224 | tf_op jit(solution)/shard_map/ppermute | solution.py:28
  19.5 2.2 %all-gather = bf16[16,128,128]{2,1,0:T(8,128)(2,1)S(1)} all-gather(bf16[8,128,128]{2,1,0:T(8,128)(2,1)S(1)} %pad_maximum_fusion.1), channel_id=2, replica_groups=mesh['blk'=16,'rep'=2] {'rep'}, dimensions={0}, use_global_device_ids=true | all-gather | bytes 786432 | tf_op jit(solution)/shard_map/all_gather | solution.py:83
  21.9 1.6 %collective-permute-start.1 = (bf16[256,512]{1,0:T(8,128)(2,1)S(1)}, bf16[256,512]{1,0:T(8,128)(2,1)S(1)}, u32[]{:S(2)}, u32[]{:S(2)}) collective-permute-start(bf16[256,512]{1,0:T(8,128)(2,1)S(1)} %pad_maximum_fusion), channel_id=1, source_target_pairs={{0,8},{2,10},{4,12},{6,14},{8,0},{10,2},{12,4},{14,6},{16,24},{18,... | collective-permute-start | bytes 786440 | tf_op jit(solution)/shard_map/ppermute | solution.py:32
  23.6 6.7 %collective-permute-done.1 = bf16[256,512]{1,0:T(8,128)(2,1)S(1)} collective-permute-done((bf16[256,512]{1,0:T(8,128)(2,1)S(1)}, bf16[256,512]{1,0:T(8,128)(2,1)S(1)}, u32[]{:S(2)}, u32[]{:S(2)}) %collective-permute-start.1) | collective-permute-done | bytes 262176 | tf_op jit(solution)/shard_map/ppermute | solution.py:32
  31.4 0.6 collective-permute-start.15
  32.0 1.6 %collective-permute-start.5 = (bf16[128,512]{1,0:T(8,128)(2,1)S(1)}, bf16[128,512]{1,0:T(8,128)(2,1)S(1)}, u32[]{:S(2)}, u32[]{:S(2)}) collective-permute-start(bf16[128,512]{1,0:T(8,128)(2,1)S(1)} %pad_maximum_fusion.5), channel_id=1, source_target_pairs={{0,2},{2,0},{4,6},{6,4},{8,10},{10,8},{12,14},{14,12},{16,18},{18,... | collective-permute-start | bytes 393224 | tf_op jit(solution)/shard_map/ppermute | solution.py:28
  33.6 0.6 collective-permute-start.6
  34.3 1.6 %collective-permute-start.7 = (bf16[128,512]{1,0:T(8,128)(2,1)S(1)}, bf16[128,512]{1,0:T(8,128)(2,1)S(1)}, u32[]{:S(2)}, u32[]{:S(2)}) collective-permute-start(bf16[128,512]{1,0:T(8,128)(2,1)S(1)} %pad_maximum_fusion.7), channel_id=1, source_target_pairs={{0,6},{2,4},{4,2},{6,0},{8,14},{10,12},{12,10},{14,8},{16,22},{18,... | collective-permute-start | bytes 393224 | tf_op jit(solution)/shard_map/ppermute | solution.py:28
  35.9 1.6 %collective-permute-start.11 = (bf16[1024,128]{1,0:T(8,128)(2,1)S(1)}, bf16[1024,128]{1,0:T(8,128)(2,1)S(1)}, u32[]{:S(2)}, u32[]{:S(2)}) collective-permute-start(bf16[1024,128]{1,0:T(8,128)(2,1)S(1)} %pad_maximum_fusion.2), channel_id=1, source_target_pairs={{0,8},{2,10},{4,12},{6,14},{8,0},{10,2},{12,4},{14,6},{16,24},{18,... | collective-permute-start | bytes 786440 | tf_op jit(solution)/shard_map/ppermute | solution.py:32
  37.5 5.6 %collective-permute-done.5 = bf16[128,512]{1,0:T(8,128)(2,1)S(1)} collective-permute-done((bf16[128,512]{1,0:T(8,128)(2,1)S(1)}, bf16[128,512]{1,0:T(8,128)(2,1)S(1)}, u32[]{:S(2)}, u32[]{:S(2)}) %collective-permute-start.5) | collective-permute-done | bytes 131104 | tf_op jit(solution)/shard_map/ppermute | solution.py:28
  43.1 1.3 %collective-permute-done.7 = bf16[128,512]{1,0:T(8,128)(2,1)S(1)} collective-permute-done((bf16[128,512]{1,0:T(8,128)(2,1)S(1)}, bf16[128,512]{1,0:T(8,128)(2,1)S(1)}, u32[]{:S(2)}, u32[]{:S(2)}) %collective-permute-start.7) | collective-permute-done | bytes 131104 | tf_op jit(solution)/shard_map/ppermute | solution.py:28
  44.6 2.0 %all_gather.15 = bf16[256,512]{1,0:T(8,128)(2,1)S(1)} all-gather(bf16[128,512]{1,0:T(8,128)(2,1)S(1)} %fusion.13), channel_id=1, replica_groups=mesh['blk'=16,'rep'=2] {'rep'}, dimensions={0}, use_global_device_ids=true | all-gather | bytes 393216 | tf_op jit(solution)/shard_map/all_gather | solution.py:110
  46.9 0.7 %add_convert_fusion.2 = bf16[512,128]{1,0:T(8,128)(2,1)} fusion(bf16[1024,128]{1,0:T(8,128)(2,1)S(1)} %collective-permute-done.15, bf16[512,512]{1,0:T(8,128)(2,1)S(1)} %convolution_convert_fusion), kind=kLoop, calls=%fused_computation.29 | loop fusion | flops 262144 | bytes 393216 | tf_op jit(solution)/shard_map/convert_element_type | solution.py:126
  47.6 1.5 %collective-permute-start.16 = (bf16[512,128]{1,0:T(8,128)(2,1)}, bf16[512,128]{1,0:T(8,128)(2,1)}, u32[]{:S(2)}, u32[]{:S(2)}) collective-permute-start(bf16[512,128]{1,0:T(8,128)(2,1)} %add_convert_fusion.2), channel_id=1, source_target_pairs={{0,4},{2,6},{4,0},{6,2},{8,12},{10,14},{12,8},{14,10},{16,20},{18,... | collective-permute-start | bytes 393224 | tf_op jit(solution)/shard_map/ppermute | solution.py:28
  49.5 1.6 %collective-permute-start.12 = (bf16[64,512]{1,0:T(8,128)(2,1)S(1)}, bf16[64,512]{1,0:T(8,128)(2,1)S(1)}, u32[]{:S(2)}, u32[]{:S(2)}) collective-permute-start(bf16[64,512]{1,0:T(8,128)(2,1)S(1)} %get-tuple-element.56), channel_id=1, source_target_pairs={{0,8},{2,10},{4,12},{6,14},{8,0},{10,2},{12,4},{14,6},{16,24},{18,... | collective-permute-start | bytes 196616 | tf_op jit(solution)/shard_map/ppermute | solution.py:32
  51.2 2.6 %collective-permute-start.13 = (bf16[64,512]{1,0:T(8,128)(2,1)S(1)}, bf16[64,512]{1,0:T(8,128)(2,1)S(1)}, u32[]{:S(2)}, u32[]{:S(2)}) collective-permute-start(bf16[64,512]{1,0:T(8,128)(2,1)S(1)} %get-tuple-element.55), channel_id=1, source_target_pairs={{0,16},{2,18},{4,20},{6,22},{8,24},{10,26},{12,28},{14,30},{16,0},... | collective-permute-start | bytes 196616 | tf_op jit(solution)/shard_map/ppermute | solution.py:32
  54.0 1.0 %fusion.14 = bf16[1,512,128]{2,1,0:T(8,128)(2,1)S(1)} fusion(bf16[512,128]{1,0:T(8,128)(2,1)} %collective-permute-done.16, bf16[1024,128]{1,0:T(8,128)(2,1)S(1)} %collective-permute-done.15, bf16[512,512]{1,0:T(8,128)(2,1)S(1)} %convolution_convert_fusion), kind=kLoop, calls=%fused_computation.31 | loop fusion | flops 393216 | bytes 524288 | tf_op jit(solution)/shard_map/concatenate | solution.py:129
  54.9 7.1 %collective-permute-done.17 = bf16[512,128]{1,0:T(8,128)(2,1)S(1)} collective-permute-done((bf16[512,128]{1,0:T(8,128)(2,1)S(1)}, bf16[512,128]{1,0:T(8,128)(2,1)S(1)}, u32[]{:S(2)}, u32[]{:S(2)}) %collective-permute-start.17) | collective-permute-done | bytes 131104 | tf_op jit(solution)/shard_map/ppermute | solution.py:32
  62.1 2.2 %all_gather.16 = bf16[2,1024,128]{2,1,0:T(8,128)(2,1)S(1)} all-gather(bf16[1,1024,128]{2,1,0:T(8,128)(2,1)S(1)} %pad_maximum_fusion.4), channel_id=1, replica_groups=mesh['blk'=16,'rep'=2] {'rep'}, dimensions={0}, use_global_device_ids=true | all-gather | bytes 786432 | tf_op jit(solution)/shard_map/all_gather | solution.py:130
  64.3 1.1 %fusion = bf16[128,512]{1,0:T(8,128)(2,1)} fusion(bf16[1024,128]{1,0:T(8,128)(2,1)S(1)} %bitcast.109, bf16[1024,1024]{1,0:T(8,128)(2,1)S(1)} %copy-done, s32[]{:T(128)S(6)} %select_n.198, bf16[128,1024]{1,0:T(8,128)(2,1)S(1)} %copy-done.1), kind=kOutput, calls=%fused_computation.4 | convolution fusion | flops 134545408 | bytes 1573888 | tf_op jit(solution)/shard_map/dot_general | solution.py:49
  65.5 1.0 %convolution_convert_fusion.2 = bf16[128,512]{1,0:T(8,128)(2,1)} fusion(bf16[1024,128]{1,0:T(8,128)(2,1)S(1)} %bitcast.108, bf16[1024,1024]{1,0:T(8,128)(2,1)S(1)} %copy-done, s32[]{:T(128)S(6)} %select_n.198), kind=kOutput, calls=%fused_computation.3 | convolution fusion | flops 134283264 | bytes 1441796 | tf_op jit(solution)/shard_map/dot_general | solution.py:49
  66.5 0.7 %fusion.17 = f32[64,512]{1,0:T(8,128)} fusion(bf16[64,512]{1,0:T(8,128)(2,1)S(1)} %collective-permute-done.14, bf16[64,512]{1,0:T(8,128)(2,1)S(1)} %collective-permute-done.13, bf16[64,512]{1,0:T(8,128)(2,1)S(1)} %collective-permute-done.12, bf16[4,64,512]{2,1,0:T(8,128)(2,1)S(1)} %bitcast.107, s32[]{:T(128)S(6)} %select_n.259), kind=kLoop, calls=%fused_computation.38 | loop fusion | flops 229376 | bytes 393220 | tf_op jit(solution)/shard_map/add | solution.py:144
  (58 shorter events, 3.8 us)
Async XLA Ops:
  0.6 63.7 %copy-start = (bf16[1024,1024]{1,0:T(8,128)(2,1)S(1)}, bf16[1024,1024]{1,0:T(8,128)(2,1)}, u32[]{:S(2)}) copy-start(bf16[1024,1024]{1,0:T(8,128)(2,1)} %param.8) | copy-start | bytes 6291460
  0.6 10.6 %copy-start.2 = (bf16[128,1024]{1,0:T(8,128)(2,1)S(1)}, bf16[128,1024]{1,0:T(8,128)(2,1)}, u32[]{:S(2)}) copy-start(bf16[128,1024]{1,0:T(8,128)(2,1)} %param.9) | copy-start | bytes 786436
  1.8 20.1 %collective-permute-start = (bf16[128,512]{1,0:T(8,128)(2,1)S(1)}, bf16[128,512]{1,0:T(8,128)(2,1)S(1)}, u32[]{:S(2)}, u32[]{:S(2)}) collective-permute-start(bf16[128,512]{1,0:T(8,128)(2,1)S(1)} %dynamic-slice_maximum_fusion), channel_id=1, source_target_pairs={{0,16},{2,18},{4,20},{6,22},{8,24},{10,26},{12,28},{14,30},{16,0},... | collective-permute-start | bytes 393224 | tf_op jit(solution)/shard_map/ppermute | solution.py:32
  7.7 4.3 %collective-permute-start.2 = (bf16[2,128,128]{2,1,0:T(8,128)(2,1)S(1)}, bf16[2,128,128]{2,1,0:T(8,128)(2,1)S(1)}, u32[]{:S(2)}, u32[]{:S(2)}) collective-permute-start(bf16[2,128,128]{2,1,0:T(8,128)(2,1)S(1)} %get-tuple-element.62), channel_id=1, source_target_pairs={{0,2},{2,0},{4,6},{6,4},{8,10},{10,8},{12,14},{14,12},{16,18},{18,... | collective-permute-start | bytes 196616 | tf_op jit(solution)/shard_map/ppermute | solution.py:28
  9.3 5.0 %collective-permute-start.3 = (bf16[2,128,128]{2,1,0:T(8,128)(2,1)S(1)}, bf16[2,128,128]{2,1,0:T(8,128)(2,1)S(1)}, u32[]{:S(2)}, u32[]{:S(2)}) collective-permute-start(bf16[2,128,128]{2,1,0:T(8,128)(2,1)S(1)} %get-tuple-element.61), channel_id=1, source_target_pairs={{0,4},{2,6},{4,0},{6,2},{8,12},{10,14},{12,8},{14,10},{16,20},{18,... | collective-permute-start | bytes 196616 | tf_op jit(solution)/shard_map/ppermute | solution.py:28
  10.8 5.2 %collective-permute-start.4 = (bf16[2,128,128]{2,1,0:T(8,128)(2,1)S(1)}, bf16[2,128,128]{2,1,0:T(8,128)(2,1)S(1)}, u32[]{:S(2)}, u32[]{:S(2)}) collective-permute-start(bf16[2,128,128]{2,1,0:T(8,128)(2,1)S(1)} %get-tuple-element.60), channel_id=1, source_target_pairs={{0,6},{2,4},{4,2},{6,0},{8,14},{10,12},{12,10},{14,8},{16,22},{18,... | collective-permute-start | bytes 196616 | tf_op jit(solution)/shard_map/ppermute | solution.py:28
  16.0 7.6 %collective-permute-start.8 = (bf16[128,512]{1,0:T(8,128)(2,1)S(1)}, bf16[128,512]{1,0:T(8,128)(2,1)S(1)}, u32[]{:S(2)}, u32[]{:S(2)}) collective-permute-start(bf16[128,512]{1,0:T(8,128)(2,1)S(1)} %constant_dynamic-slice_fusion), channel_id=1, source_target_pairs={{0,2},{2,0},{4,6},{6,4},{8,10},{10,8},{12,14},{14,12},{16,18},{18,... | collective-permute-start | bytes 393224 | tf_op jit(solution)/shard_map/ppermute | solution.py:28
  16.5 7.1 %collective-permute-start.9 = (bf16[128,512]{1,0:T(8,128)(2,1)S(1)}, bf16[128,512]{1,0:T(8,128)(2,1)S(1)}, u32[]{:S(2)}, u32[]{:S(2)}) collective-permute-start(bf16[128,512]{1,0:T(8,128)(2,1)S(1)} %constant_dynamic-slice_fusion), channel_id=1, source_target_pairs={{0,4},{2,6},{4,0},{6,2},{8,12},{10,14},{12,8},{14,10},{16,20},{18,... | collective-permute-start | bytes 393224 | tf_op jit(solution)/shard_map/ppermute | solution.py:28
  17.0 6.6 %collective-permute-start.10 = (bf16[128,512]{1,0:T(8,128)(2,1)S(1)}, bf16[128,512]{1,0:T(8,128)(2,1)S(1)}, u32[]{:S(2)}, u32[]{:S(2)}) collective-permute-start(bf16[128,512]{1,0:T(8,128)(2,1)S(1)} %constant_dynamic-slice_fusion), channel_id=1, source_target_pairs={{0,6},{2,4},{4,2},{6,0},{8,14},{10,12},{12,10},{14,8},{16,22},{18,... | collective-permute-start | bytes 393224 | tf_op jit(solution)/shard_map/ppermute | solution.py:28
  21.9 8.4 %collective-permute-start.1 = (bf16[256,512]{1,0:T(8,128)(2,1)S(1)}, bf16[256,512]{1,0:T(8,128)(2,1)S(1)}, u32[]{:S(2)}, u32[]{:S(2)}) collective-permute-start(bf16[256,512]{1,0:T(8,128)(2,1)S(1)} %pad_maximum_fusion), channel_id=1, source_target_pairs={{0,8},{2,10},{4,12},{6,14},{8,0},{10,2},{12,4},{14,6},{16,24},{18,... | collective-permute-start | bytes 786440 | tf_op jit(solution)/shard_map/ppermute | solution.py:32
  31.4 15.6 %collective-permute-start.15 = (bf16[1024,128]{1,0:T(8,128)(2,1)S(1)}, bf16[1024,128]{1,0:T(8,128)(2,1)S(1)}, u32[]{:S(2)}, u32[]{:S(2)}) collective-permute-start(bf16[1024,128]{1,0:T(8,128)(2,1)S(1)} %pad_maximum_fusion.3), channel_id=1, source_target_pairs={{0,2},{2,0},{4,6},{6,4},{8,10},{10,8},{12,14},{14,12},{16,18},{18,... | collective-permute-start | bytes 786440 | tf_op jit(solution)/shard_map/ppermute | solution.py:28
  32.0 11.1 %collective-permute-start.5 = (bf16[128,512]{1,0:T(8,128)(2,1)S(1)}, bf16[128,512]{1,0:T(8,128)(2,1)S(1)}, u32[]{:S(2)}, u32[]{:S(2)}) collective-permute-start(bf16[128,512]{1,0:T(8,128)(2,1)S(1)} %pad_maximum_fusion.5), channel_id=1, source_target_pairs={{0,2},{2,0},{4,6},{6,4},{8,10},{10,8},{12,14},{14,12},{16,18},{18,... | collective-permute-start | bytes 393224 | tf_op jit(solution)/shard_map/ppermute | solution.py:28
  33.6 9.5 %collective-permute-start.6 = (bf16[128,512]{1,0:T(8,128)(2,1)S(1)}, bf16[128,512]{1,0:T(8,128)(2,1)S(1)}, u32[]{:S(2)}, u32[]{:S(2)}) collective-permute-start(bf16[128,512]{1,0:T(8,128)(2,1)S(1)} %pad_maximum_fusion.6), channel_id=1, source_target_pairs={{0,4},{2,6},{4,0},{6,2},{8,12},{10,14},{12,8},{14,10},{16,20},{18,... | collective-permute-start | bytes 393224 | tf_op jit(solution)/shard_map/ppermute | solution.py:28
  34.3 10.2 %collective-permute-start.7 = (bf16[128,512]{1,0:T(8,128)(2,1)S(1)}, bf16[128,512]{1,0:T(8,128)(2,1)S(1)}, u32[]{:S(2)}, u32[]{:S(2)}) collective-permute-start(bf16[128,512]{1,0:T(8,128)(2,1)S(1)} %pad_maximum_fusion.7), channel_id=1, source_target_pairs={{0,6},{2,4},{4,2},{6,0},{8,14},{10,12},{12,10},{14,8},{16,22},{18,... | collective-permute-start | bytes 393224 | tf_op jit(solution)/shard_map/ppermute | solution.py:28
  35.9 10.7 %collective-permute-start.11 = (bf16[1024,128]{1,0:T(8,128)(2,1)S(1)}, bf16[1024,128]{1,0:T(8,128)(2,1)S(1)}, u32[]{:S(2)}, u32[]{:S(2)}) collective-permute-start(bf16[1024,128]{1,0:T(8,128)(2,1)S(1)} %pad_maximum_fusion.2), channel_id=1, source_target_pairs={{0,8},{2,10},{4,12},{6,14},{8,0},{10,2},{12,4},{14,6},{16,24},{18,... | collective-permute-start | bytes 786440 | tf_op jit(solution)/shard_map/ppermute | solution.py:32
  47.6 6.3 %collective-permute-start.16 = (bf16[512,128]{1,0:T(8,128)(2,1)}, bf16[512,128]{1,0:T(8,128)(2,1)}, u32[]{:S(2)}, u32[]{:S(2)}) collective-permute-start(bf16[512,128]{1,0:T(8,128)(2,1)} %add_convert_fusion.2), channel_id=1, source_target_pairs={{0,4},{2,6},{4,0},{6,2},{8,12},{10,14},{12,8},{14,10},{16,20},{18,... | collective-permute-start | bytes 393224 | tf_op jit(solution)/shard_map/ppermute | solution.py:28
  49.2 15.2 %copy-start.1 = (bf16[128,1024]{1,0:T(8,128)(2,1)S(1)}, bf16[128,1024]{1,0:T(8,128)(2,1)}, u32[]{:S(2)}) copy-start(bf16[128,1024]{1,0:T(8,128)(2,1)} %param.5) | copy-start | bytes 786436
  49.2 12.9 %collective-permute-start.17 = (bf16[512,128]{1,0:T(8,128)(2,1)S(1)}, bf16[512,128]{1,0:T(8,128)(2,1)S(1)}, u32[]{:S(2)}, u32[]{:S(2)}) collective-permute-start(bf16[512,128]{1,0:T(8,128)(2,1)S(1)} %get-tuple-element.27), channel_id=1, source_target_pairs={{0,16},{2,18},{4,20},{6,22},{8,24},{10,26},{12,28},{14,30},{16,0},... | collective-permute-start | bytes 393224 | tf_op jit(solution)/shard_map/ppermute | solution.py:32
  49.5 17.0 %collective-permute-start.12 = (bf16[64,512]{1,0:T(8,128)(2,1)S(1)}, bf16[64,512]{1,0:T(8,128)(2,1)S(1)}, u32[]{:S(2)}, u32[]{:S(2)}) collective-permute-start(bf16[64,512]{1,0:T(8,128)(2,1)S(1)} %get-tuple-element.56), channel_id=1, source_target_pairs={{0,8},{2,10},{4,12},{6,14},{8,0},{10,2},{12,4},{14,6},{16,24},{18,... | collective-permute-start | bytes 196616 | tf_op jit(solution)/shard_map/ppermute | solution.py:32
  51.2 15.3 %collective-permute-start.13 = (bf16[64,512]{1,0:T(8,128)(2,1)S(1)}, bf16[64,512]{1,0:T(8,128)(2,1)S(1)}, u32[]{:S(2)}, u32[]{:S(2)}) collective-permute-start(bf16[64,512]{1,0:T(8,128)(2,1)S(1)} %get-tuple-element.55), channel_id=1, source_target_pairs={{0,16},{2,18},{4,20},{6,22},{8,24},{10,26},{12,28},{14,30},{16,0},... | collective-permute-start | bytes 196616 | tf_op jit(solution)/shard_map/ppermute | solution.py:32
  53.7 12.8 %collective-permute-start.14 = (bf16[64,512]{1,0:T(8,128)(2,1)S(1)}, bf16[64,512]{1,0:T(8,128)(2,1)S(1)}, u32[]{:S(2)}, u32[]{:S(2)}) collective-permute-start(bf16[64,512]{1,0:T(8,128)(2,1)S(1)} %get-tuple-element.54), channel_id=1, source_target_pairs={{0,24},{2,26},{4,28},{6,30},{8,16},{10,18},{12,20},{14,22},{16,8},... | collective-permute-start | bytes 196616 | tf_op jit(solution)/shard_map/ppermute | solution.py:32

commit v9 on v8

--- a/solution.py
+++ b/solution.py
@@ -57,13 +57,7 @@
     hidden_part = jnp.maximum(
         lax.dynamic_slice_in_dim(hidden_pre, rep_pos * cols_here, cols_here, 1), 0
     )
-    held = {0: hidden_part}
-    for bit in rising[::-1]:
-        keys = list(held)
-        got = along_outer(jnp.concatenate([held[k] for k in keys], 0), bit)
-        for n, k in enumerate(keys):
-            held[k ^ bit] = got[n * tile_size : (n + 1) * tile_size]
-    hidden_stack = jnp.concatenate([held[e] for e in turns], 0)
+    hidden_stack = jnp.concatenate([along_outer(hidden_part, e) for e in turns], 0)
 
     columns = after(adj_cols, hidden_part)[0]
     turn_of = (columns & (side - 1)) ^ inner_pos
@@ -73,29 +67,25 @@
     ordered = jnp.zeros((section_span, tile_size, tile_size), bf16)
     for k in range(slots):
         ordered = jnp.where(hit[:, k, None, None], adj_vals[0, k][None], ordered)
-    arrived = []
-    for t in turns:
-        message = ordered[t * per_core : (t + 1) * per_core]
-        arrived.append(along_inner(message, t))
-    grad_part = lax.dynamic_slice_in_dim(cotangent, rep_pos * cols_here, cols_here, 1)
-    grad_part = after(grad_part, *arrived[1:])
-    grad_stack = jnp.concatenate([along_inner(grad_part, t) for t in turns], 0)
-    everyone = lax.all_gather(jnp.concatenate(arrived, 0), "rep", axis=0)
-
+    everyone = lax.all_gather(ordered, "rep", axis=0)
+    row_block = outer_pos * side + inner_pos
     rows = []
     for t in turns:
-        row_block = outer_pos * side + (inner_pos ^ t)
         row = []
         for e in turns:
-            column_block = (outer_pos ^ e) * side + inner_pos
+            column_block = (outer_pos ^ e) * side + (inner_pos ^ t)
             holder = ((row_block - column_block) & (blk_count - 1)) >> span_bits
             index = t * per_core + e % per_core
             piece = everyone[0, index]
             for r in range(1, rep_count):
                 piece = jnp.where(holder == r, everyone[r, index], piece)
             row.append(piece)
-        rows.append(jnp.concatenate(row, 1))
+        rows.append(along_inner(jnp.concatenate(row, 1), t))
     block = jnp.concatenate(rows, 0)
+
+    grad_part = lax.dynamic_slice_in_dim(cotangent, rep_pos * cols_here, cols_here, 1)
+    grad_part = after(grad_part, rows[1])
+    grad_stack = jnp.concatenate([along_inner(grad_part, t) for t in turns], 0)
 
     mixed = dot(hidden_stack, block, ((0,), (1,))).astype(bf16)
     share = cols_here // side
@@ -107,12 +97,12 @@
         chosen = jnp.concatenate([lanes(chosen, u ^ t) for u in turns], 1)
         mixed_cols.append(along_inner(chosen, t))
     mixed_cols = sum(part.astype(jnp.float32) for part in mixed_cols).astype(bf16)
+    back = dot(after(grad_stack, mixed), block, ((0,), (0,)))
+    back = halved([lanes(back, e) for e in turns], along_outer, rising[:-1])
+    rows = [lanes(after(mixed, mixed_cols), t) for t in turns]
+    rows = halved(rows, along_inner, rising[:-1])
+
     mixed_cols = lax.all_gather(mixed_cols, "rep", axis=0, tiled=True)
-    back = dot(after(grad_stack, mixed), block, ((0,), (0,)))
-    rows = after(mixed, back)
-    back = halved([lanes(back, e) for e in turns], along_outer, rising[:-1])
-    rows = halved([lanes(rows, t) for t in turns], along_inner, rising[:-1])
-
     mixed_cols, back[0] = lax.optimization_barrier((mixed_cols, back[0]))
     weight_part = dot(mixed_cols, grad_stack, ((1,), (0,))).astype(bf16)
     by_outer = weight_part.reshape(side, rows_here, cols_here)

time: 67.5 us -> 69.4 us (1.028)
  waiting for transfers between devices: 25.5 us -> 21.4 us
  starting transfers between devices: 25 us -> 28.9 us
  matrix products: 3.39 us -> 5.52 us
    ppermute x7 -> x8, waiting for transfers between devices: 13.8 us -> 7.11 us  [along_outer(): return lax.ppermute(value, 'blk', pairs) if turn else value]
    ppermute x11, starting transfers between devices: 12.8 us -> 16.1 us  [along_inner(): return lax.ppermute(value, 'blk', pairs) if turn else value]
    ppermute x11, waiting for transfers between devices: 11.7 us -> 14.3 us  [along_inner(): return lax.ppermute(value, 'blk', pairs) if turn else value]
    dot_general x5, matrix products: 3.39 us -> 5.52 us  [dot(): lax.dot_general(lhs, rhs, (dims, ((), ())), preferred_element_type=jnp.fl...]
    ppermute x7 -> x8, starting transfers between devices: 12.2 us -> 12.8 us  [along_outer(): return lax.ppermute(value, 'blk', pairs) if turn else value]
  transfers between devices with their start and end apart: 18 -> 19, of which waited for: 7 -> 7; matrix products, arithmetic and copies ran while one was open for 9% -> 13% of each run, Pallas kernels for 0% -> 0%
where the time goes in v9:
time: 69.4 us; the launch traced here: 69 us
  starting transfers between devices  28.9 us (42%)
  waiting for transfers between devices  21.4 us (31%)
  blocking collectives  6.34 us (9%)
  matrix products  5.52 us (8%)
  other arithmetic  4.72 us (7%)
  local copies, waits for them, and re-layouts  1.18 us (2%)
  between operations  0.97 us (1%)
    ppermute x11, starting transfers between devices, along_inner(): return lax.ppermute(value, 'blk', pairs) if turn else value  16.1 us
    ppermute x11, waiting for transfers between devices, along_inner(): return lax.ppermute(value, 'blk', pairs) if turn else value  14.3 us
    ppermute x8, starting transfers between devices, along_outer(): return lax.ppermute(value, 'blk', pairs) if turn else value  12.8 us
    ppermute x8, waiting for transfers between devices, along_outer(): return lax.ppermute(value, 'blk', pairs) if turn else value  7.11 us
    dot_general x5, matrix products, dot(): lax.dot_general(lhs, rhs, (dims, ((), ())), preferred_element_type=jnp.fl...  5.52 us
    all_gather x1, blocking collectives, shards(): everyone = lax.all_gather(ordered, 'rep', axis=0)  2.18 us
    all_gather x1, blocking collectives, shards(): both = lax.all_gather(both, 'rep', axis=0)  2.18 us
    all_gather x1, blocking collectives, shards(): mixed_cols = lax.all_gather(mixed_cols, 'rep', axis=0, tiled=True)  1.98 us
  transfers between devices with their start and end apart: 19, of which 7 were waited for; matrix products, arithmetic and copies ran while one was open for 13% of the time, Pallas kernels for 0%

profile of v9, /device:TPU:0, one launch (start us, length us, event | category | flops | bytes accessed | tf_op | source)
XLA Modules:
  0.0 69.0 jit_solution(9924677000535468794)
XLA Ops:
  0.7 1.1 %dynamic-slice_maximum_fusion = bf16[128,512]{1,0:T(8,128)(2,1)S(1)} fusion(bf16[128,1024]{1,0:T(8,128)(2,1)} %param.5, s32[]{:T(128)S(6)} %select_n.254), kind=kLoop, calls=%fused_computation.40 | loop fusion | flops 262144 | bytes 262148 | tf_op jit(solution)/shard_map/max | solution.py:57
  1.7 5.1 %collective-permute-start.2 = (bf16[128,512]{1,0:T(8,128)(2,1)S(1)}, bf16[128,512]{1,0:T(8,128)(2,1)}, u32[]{:S(2)}, u32[]{:S(2)}) collective-permute-start(bf16[128,512]{1,0:T(8,128)(2,1)S(1)} %dynamic-slice_maximum_fusion), channel_id=1, source_target_pairs={{0,24},{2,26},{4,28},{6,30},{8,16},{10,18},{12,20},{14,22},{16,8},... | collective-permute-start | bytes 393224 | tf_op jit(solution)/shard_map/ppermute | solution.py:32
  6.9 0.6 collective-permute-start
  7.5 0.7 add_bitcast_fusion
  8.3 0.9 %slice_bitcast_fusion.9 = (bf16[128,128]{1,0:T(8,128)(2,1)S(1)}, bf16[128,128]{1,0:T(8,128)(2,1)S(1)}, bf16[128,128]{1,0:T(8,128)(2,1)S(1)}, bf16[128,128]{1,0:T...) fusion(bf16[1,8,128,128]{3,2,1,0:T(8,128)(2,1)} %param.6), kind=kLoop, calls=%fused_computation.68 | loop fusion | bytes 524288 | tf_op jit(solution)/shard_map/jit(_where)/broadcast_in_dim | solution.py:69
  9.3 2.2 %all_gather.11 = bf16[2,8,128,128]{3,2,1,0:T(8,128)(2,1)S(1)} all-gather(bf16[1,8,128,128]{3,2,1,0:T(8,128)(2,1)S(1)} %select_select_fusion), channel_id=1, replica_groups=mesh['blk'=16,'rep'=2] {'rep'}, dimensions={0}, use_global_device_ids=true | all-gather | bytes 786432 | tf_op jit(solution)/shard_map/all_gather | solution.py:70
  11.6 2.7 %collective-permute-start.5 = (bf16[128,512]{1,0:T(8,128)(2,1)S(1)}, bf16[128,512]{1,0:T(8,128)(2,1)}, u32[]{:S(2)}, u32[]{:S(2)}) collective-permute-start(bf16[128,512]{1,0:T(8,128)(2,1)S(1)} %pad_maximum_fusion.6), channel_id=1, source_target_pairs={{0,6},{2,4},{4,2},{6,0},{8,14},{10,12},{12,10},{14,8},{16,22},{18,... | collective-permute-start | bytes 393224 | tf_op jit(solution)/shard_map/ppermute | solution.py:28
  14.9 6.3 %collective-permute-done.3 = bf16[128,512]{1,0:T(8,128)(2,1)} collective-permute-done((bf16[128,512]{1,0:T(8,128)(2,1)S(1)}, bf16[128,512]{1,0:T(8,128)(2,1)}, u32[]{:S(2)}, u32[]{:S(2)}) %collective-permute-start.3) | collective-permute-done | bytes 131104 | tf_op jit(solution)/shard_map/ppermute | solution.py:28
  21.6 1.7 %collective-permute-start.9 = (bf16[128,512]{1,0:T(8,128)(2,1)S(1)}, bf16[128,512]{1,0:T(8,128)(2,1)S(1)}, u32[]{:S(2)}, u32[]{:S(2)}) collective-permute-start(bf16[128,512]{1,0:T(8,128)(2,1)S(1)} %constant_dynamic-slice_fusion), channel_id=1, source_target_pairs={{0,2},{2,0},{4,6},{6,4},{8,10},{10,8},{12,14},{14,12},{16,18},{18,... | collective-permute-start | bytes 393224 | tf_op jit(solution)/shard_map/ppermute | solution.py:28
  23.3 1.5 %collective-permute-start.10 = (bf16[128,512]{1,0:T(8,128)(2,1)S(1)}, bf16[128,512]{1,0:T(8,128)(2,1)S(1)}, u32[]{:S(2)}, u32[]{:S(2)}) collective-permute-start(bf16[128,512]{1,0:T(8,128)(2,1)S(1)} %constant_dynamic-slice_fusion), channel_id=1, source_target_pairs={{0,4},{2,6},{4,0},{6,2},{8,12},{10,14},{12,8},{14,10},{16,20},{18,... | collective-permute-start | bytes 393224 | tf_op jit(solution)/shard_map/ppermute | solution.py:28
  25.2 3.0 %collective-permute-done.4 = bf16[128,512]{1,0:T(8,128)(2,1)S(1)} collective-permute-done((bf16[128,512]{1,0:T(8,128)(2,1)S(1)}, bf16[128,512]{1,0:T(8,128)(2,1)S(1)}, u32[]{:S(2)}, u32[]{:S(2)}) %collective-permute-start.4) | collective-permute-done | bytes 131104 | tf_op jit(solution)/shard_map/ppermute | solution.py:28
  28.2 1.6 %convolution_convert_fusion = bf16[512,512]{1,0:T(8,128)(2,1)S(1)} fusion(bf16[128,512]{1,0:T(8,128)(2,1)} %collective-permute-done.2, bf16[128,512]{1,0:T(8,128)(2,1)} %collective-permute-done.1, bf16[128,512]{1,0:T(8,128)(2,1)} %collective-permute-done, bf16[128,512]{1,0:T(8,128)(2,1)S(1)} %dynamic-slice_maximum_fusion, ...), kind=kOutput, calls=%fused_computation | convolution fusion | flops 274464768 | bytes 1572864 | tf_op jit(solution)/shard_map/dot_general | solution.py:49
  30.0 5.1 %collective-permute-start.8 = (bf16[128,512]{1,0:T(8,128)(2,1)S(1)}, bf16[128,512]{1,0:T(8,128)(2,1)S(1)}, u32[]{:S(2)}, u32[]{:S(2)}) collective-permute-start(bf16[128,512]{1,0:T(8,128)(2,1)S(1)} %pad_maximum_fusion.9), channel_id=1, source_target_pairs={{0,6},{2,4},{4,2},{6,0},{8,14},{10,12},{12,10},{14,8},{16,22},{18,... | collective-permute-start | bytes 393224 | tf_op jit(solution)/shard_map/ppermute | solution.py:28
  35.2 0.6 collective-permute-start.6
  35.9 1.4 %fusion.29 = (bf16[512,512]{1,0:T(8,128)(2,1)S(1)}, f32[512,512]{1,0:T(8,128)S(1)}) fusion(bf16[512,512]{1,0:T(8,128)(2,1)S(1)} %constant_dynamic-update-slice_fusion, bf16[128,512]{1,0:T(8,128)(2,1)} %collective-permute-done.5, bf16[128,512]{1,0:T(8,128)(2,1)S(1)} %collective-permute-done.4, bf16[128,512]{1,0:T(8,128)(2,1)} %collective-permute-done.3, ...), kind=kOutput, calls=%fused_computation.98 | convolution fusion | flops 272367616 | bytes 2621440 | tf_op jit(solution)/shard_map/dot_general | solution.py:49
  37.4 1.3 %collective-permute-start.12 = (bf16[1024,128]{1,0:T(8,128)(2,1)S(1)}, bf16[1024,128]{1,0:T(8,128)(2,1)S(1)}, u32[]{:S(2)}, u32[]{:S(2)}) collective-permute-start(bf16[1024,128]{1,0:T(8,128)(2,1)S(1)} %pad_maximum_fusion.1), channel_id=1, source_target_pairs={{0,8},{2,10},{4,12},{6,14},{8,0},{10,2},{12,4},{14,6},{16,24},{18,... | collective-permute-start | bytes 786440 | tf_op jit(solution)/shard_map/ppermute | solution.py:32
  38.9 1.3 %collective-permute-done.7 = bf16[128,512]{1,0:T(8,128)(2,1)S(1)} collective-permute-done((bf16[128,512]{1,0:T(8,128)(2,1)S(1)}, bf16[128,512]{1,0:T(8,128)(2,1)S(1)}, u32[]{:S(2)}, u32[]{:S(2)}) %collective-permute-start.7) | collective-permute-done | bytes 131104 | tf_op jit(solution)/shard_map/ppermute | solution.py:28
  40.2 1.5 %collective-permute-done.6 = bf16[128,512]{1,0:T(8,128)(2,1)S(1)} collective-permute-done((bf16[128,512]{1,0:T(8,128)(2,1)S(1)}, bf16[128,512]{1,0:T(8,128)(2,1)S(1)}, u32[]{:S(2)}, u32[]{:S(2)}) %collective-permute-start.6) | collective-permute-done | bytes 131104 | tf_op jit(solution)/shard_map/ppermute | solution.py:28
  41.8 2.5 %collective-permute-start.16 = (bf16[1024,128]{1,0:T(8,128)(2,1)S(1)}, bf16[1024,128]{1,0:T(8,128)(2,1)S(1)}, u32[]{:S(2)}, u32[]{:S(2)}) collective-permute-start(bf16[1024,128]{1,0:T(8,128)(2,1)S(1)} %pad_maximum_fusion.2), channel_id=1, source_target_pairs={{0,2},{2,0},{4,6},{6,4},{8,10},{10,8},{12,14},{14,12},{16,18},{18,... | collective-permute-start | bytes 786440 | tf_op jit(solution)/shard_map/ppermute | solution.py:28
  44.4 2.0 %all_gather.12 = bf16[256,512]{1,0:T(8,128)(2,1)S(1)} all-gather(bf16[128,512]{1,0:T(8,128)(2,1)S(1)} %fusion.13), channel_id=1, replica_groups=mesh['blk'=16,'rep'=2] {'rep'}, dimensions={0}, use_global_device_ids=true | all-gather | bytes 393216 | tf_op jit(solution)/shard_map/all_gather | solution.py:105
  46.7 2.0 %collective-permute-done.16 = bf16[1024,128]{1,0:T(8,128)(2,1)S(1)} collective-permute-done((bf16[1024,128]{1,0:T(8,128)(2,1)S(1)}, bf16[1024,128]{1,0:T(8,128)(2,1)S(1)}, u32[]{:S(2)}, u32[]{:S(2)}) %collective-permute-start.16) | collective-permute-done | bytes 262176 | tf_op jit(solution)/shard_map/ppermute | solution.py:28
  48.7 0.7 %add_convert_fusion.2 = bf16[512,128]{1,0:T(8,128)(2,1)} fusion(bf16[1024,128]{1,0:T(8,128)(2,1)S(1)} %collective-permute-done.16, bf16[512,512]{1,0:T(8,128)(2,1)S(1)} %convolution_convert_fusion), kind=kLoop, calls=%fused_computation.27 | loop fusion | flops 262144 | bytes 393216 | tf_op jit(solution)/shard_map/convert_element_type | solution.py:116
  49.4 0.6 collective-permute-start.17
  50.1 1.3 %collective-permute-start.13 = (bf16[64,512]{1,0:T(8,128)(2,1)S(1)}, bf16[64,512]{1,0:T(8,128)(2,1)S(1)}, u32[]{:S(2)}, u32[]{:S(2)}) collective-permute-start(bf16[64,512]{1,0:T(8,128)(2,1)S(1)} %get-tuple-element.56), channel_id=1, source_target_pairs={{0,8},{2,10},{4,12},{6,14},{8,0},{10,2},{12,4},{14,6},{16,24},{18,... | collective-permute-start | bytes 196616 | tf_op jit(solution)/shard_map/ppermute | solution.py:32
  51.4 2.9 %collective-permute-start.14 = (bf16[64,512]{1,0:T(8,128)(2,1)S(1)}, bf16[64,512]{1,0:T(8,128)(2,1)S(1)}, u32[]{:S(2)}, u32[]{:S(2)}) collective-permute-start(bf16[64,512]{1,0:T(8,128)(2,1)S(1)} %get-tuple-element.55), channel_id=1, source_target_pairs={{0,16},{2,18},{4,20},{6,22},{8,24},{10,26},{12,28},{14,30},{16,0},... | collective-permute-start | bytes 196616 | tf_op jit(solution)/shard_map/ppermute | solution.py:32
  54.5 1.3 %collective-permute-start.18 = (bf16[512,128]{1,0:T(8,128)(2,1)S(1)}, bf16[512,128]{1,0:T(8,128)(2,1)S(1)}, u32[]{:S(2)}, u32[]{:S(2)}) collective-permute-start(bf16[512,128]{1,0:T(8,128)(2,1)S(1)} %get-tuple-element.27), channel_id=1, source_target_pairs={{0,16},{2,18},{4,20},{6,22},{8,24},{10,26},{12,28},{14,30},{16,0},... | collective-permute-start | bytes 393224 | tf_op jit(solution)/shard_map/ppermute | solution.py:32
  55.8 1.0 %fusion.14 = bf16[1,512,128]{2,1,0:T(8,128)(2,1)S(1)} fusion(bf16[512,128]{1,0:T(8,128)(2,1)} %collective-permute-done.17, bf16[1024,128]{1,0:T(8,128)(2,1)S(1)} %collective-permute-done.16, bf16[512,512]{1,0:T(8,128)(2,1)S(1)} %convolution_convert_fusion), kind=kLoop, calls=%fused_computation.29 | loop fusion | flops 393216 | bytes 524288 | tf_op jit(solution)/shard_map/concatenate | solution.py:119
  56.8 7.1 %collective-permute-done.18 = bf16[512,128]{1,0:T(8,128)(2,1)S(1)} collective-permute-done((bf16[512,128]{1,0:T(8,128)(2,1)S(1)}, bf16[512,128]{1,0:T(8,128)(2,1)S(1)}, u32[]{:S(2)}, u32[]{:S(2)}) %collective-permute-start.18) | collective-permute-done | bytes 131104 | tf_op jit(solution)/shard_map/ppermute | solution.py:32
  64.0 2.2 %all_gather.13 = bf16[2,1024,128]{2,1,0:T(8,128)(2,1)S(1)} all-gather(bf16[1,1024,128]{2,1,0:T(8,128)(2,1)S(1)} %pad_maximum_fusion.3), channel_id=1, replica_groups=mesh['blk'=16,'rep'=2] {'rep'}, dimensions={0}, use_global_device_ids=true | all-gather | bytes 786432 | tf_op jit(solution)/shard_map/all_gather | solution.py:120
  66.2 1.0 %convolution_convert_fusion.2 = bf16[128,512]{1,0:T(8,128)(2,1)} fusion(bf16[1024,128]{1,0:T(8,128)(2,1)S(1)} %bitcast.102, bf16[1024,1024]{1,0:T(8,128)(2,1)S(1)} %copy-done, s32[]{:T(128)S(6)} %select_n.254), kind=kOutput, calls=%fused_computation.3 | convolution fusion | flops 134283264 | bytes 1441796 | tf_op jit(solution)/shard_map/dot_general | solution.py:49
  67.2 1.1 %fusion = bf16[128,512]{1,0:T(8,128)(2,1)} fusion(bf16[1024,128]{1,0:T(8,128)(2,1)S(1)} %bitcast.101, bf16[1024,1024]{1,0:T(8,128)(2,1)S(1)} %copy-done, s32[]{:T(128)S(6)} %select_n.254, bf16[128,1024]{1,0:T(8,128)(2,1)S(1)} %copy-done.1), kind=kOutput, calls=%fused_computation.4 | convolution fusion | flops 134545408 | bytes 1573888 | tf_op jit(solution)/shard_map/dot_general | solution.py:49
  68.4 0.7 %fusion.17 = f32[64,512]{1,0:T(8,128)} fusion(bf16[64,512]{1,0:T(8,128)(2,1)S(1)} %collective-permute-done.15, bf16[64,512]{1,0:T(8,128)(2,1)S(1)} %collective-permute-done.14, bf16[64,512]{1,0:T(8,128)(2,1)S(1)} %collective-permute-done.13, bf16[4,64,512]{2,1,0:T(8,128)(2,1)S(1)} %bitcast.100, s32[]{:T(128)S(6)} %select_n.315), kind=kLoop, calls=%fused_computation.39 | loop fusion | flops 229376 | bytes 393220 | tf_op jit(solution)/shard_map/add | solution.py:134
  (58 shorter events, 3.0 us)
Async XLA Ops:
  0.6 65.6 %copy-start = (bf16[1024,1024]{1,0:T(8,128)(2,1)S(1)}, bf16[1024,1024]{1,0:T(8,128)(2,1)}, u32[]{:S(2)}) copy-start(bf16[1024,1024]{1,0:T(8,128)(2,1)} %param.8) | copy-start | bytes 6291460
  1.7 19.8 %copy-start.2 = (bf16[128,1024]{1,0:T(8,128)(2,1)S(1)}, bf16[128,1024]{1,0:T(8,128)(2,1)}, u32[]{:S(2)}) copy-start(bf16[128,1024]{1,0:T(8,128)(2,1)} %param.9) | copy-start | bytes 786436
  1.7 19.9 %collective-permute-start.2 = (bf16[128,512]{1,0:T(8,128)(2,1)S(1)}, bf16[128,512]{1,0:T(8,128)(2,1)}, u32[]{:S(2)}, u32[]{:S(2)}) collective-permute-start(bf16[128,512]{1,0:T(8,128)(2,1)S(1)} %dynamic-slice_maximum_fusion), channel_id=1, source_target_pairs={{0,24},{2,26},{4,28},{6,30},{8,16},{10,18},{12,20},{14,22},{16,8},... | collective-permute-start | bytes 393224 | tf_op jit(solution)/shard_map/ppermute | solution.py:32
  6.9 16.5 %collective-permute-start.1 = (bf16[128,512]{1,0:T(8,128)(2,1)S(1)}, bf16[128,512]{1,0:T(8,128)(2,1)}, u32[]{:S(2)}, u32[]{:S(2)}) collective-permute-start(bf16[128,512]{1,0:T(8,128)(2,1)S(1)} %dynamic-slice_maximum_fusion), channel_id=1, source_target_pairs={{0,16},{2,18},{4,20},{6,22},{8,24},{10,26},{12,28},{14,30},{16,0},... | collective-permute-start | bytes 393224 | tf_op jit(solution)/shard_map/ppermute | solution.py:32
  6.9 18.0 %collective-permute-start = (bf16[128,512]{1,0:T(8,128)(2,1)S(1)}, bf16[128,512]{1,0:T(8,128)(2,1)}, u32[]{:S(2)}, u32[]{:S(2)}) collective-permute-start(bf16[128,512]{1,0:T(8,128)(2,1)S(1)} %dynamic-slice_maximum_fusion), channel_id=1, source_target_pairs={{0,8},{2,10},{4,12},{6,14},{8,0},{10,2},{12,4},{14,6},{16,24},{18,... | collective-permute-start | bytes 393224 | tf_op jit(solution)/shard_map/ppermute | solution.py:32
  11.6 13.6 %collective-permute-start.5 = (bf16[128,512]{1,0:T(8,128)(2,1)S(1)}, bf16[128,512]{1,0:T(8,128)(2,1)}, u32[]{:S(2)}, u32[]{:S(2)}) collective-permute-start(bf16[128,512]{1,0:T(8,128)(2,1)S(1)} %pad_maximum_fusion.6), channel_id=1, source_target_pairs={{0,6},{2,4},{4,2},{6,0},{8,14},{10,12},{12,10},{14,8},{16,22},{18,... | collective-permute-start | bytes 393224 | tf_op jit(solution)/shard_map/ppermute | solution.py:28
  14.3 6.9 %collective-permute-start.3 = (bf16[128,512]{1,0:T(8,128)(2,1)S(1)}, bf16[128,512]{1,0:T(8,128)(2,1)}, u32[]{:S(2)}, u32[]{:S(2)}) collective-permute-start(bf16[128,512]{1,0:T(8,128)(2,1)S(1)} %pad_maximum_fusion.4), channel_id=1, source_target_pairs={{0,2},{2,0},{4,6},{6,4},{8,10},{10,8},{12,14},{14,12},{16,18},{18,... | collective-permute-start | bytes 393224 | tf_op jit(solution)/shard_map/ppermute | solution.py:28
  21.2 7.0 %collective-permute-start.4 = (bf16[128,512]{1,0:T(8,128)(2,1)S(1)}, bf16[128,512]{1,0:T(8,128)(2,1)S(1)}, u32[]{:S(2)}, u32[]{:S(2)}) collective-permute-start(bf16[128,512]{1,0:T(8,128)(2,1)S(1)} %pad_maximum_fusion.5), channel_id=1, source_target_pairs={{0,4},{2,6},{4,0},{6,2},{8,12},{10,14},{12,8},{14,10},{16,20},{18,... | collective-permute-start | bytes 393224 | tf_op jit(solution)/shard_map/ppermute | solution.py:28
  21.6 13.6 %collective-permute-start.9 = (bf16[128,512]{1,0:T(8,128)(2,1)S(1)}, bf16[128,512]{1,0:T(8,128)(2,1)S(1)}, u32[]{:S(2)}, u32[]{:S(2)}) collective-permute-start(bf16[128,512]{1,0:T(8,128)(2,1)S(1)} %constant_dynamic-slice_fusion), channel_id=1, source_target_pairs={{0,2},{2,0},{4,6},{6,4},{8,10},{10,8},{12,14},{14,12},{16,18},{18,... | collective-permute-start | bytes 393224 | tf_op jit(solution)/shard_map/ppermute | solution.py:28
  23.3 12.6 %collective-permute-start.10 = (bf16[128,512]{1,0:T(8,128)(2,1)S(1)}, bf16[128,512]{1,0:T(8,128)(2,1)S(1)}, u32[]{:S(2)}, u32[]{:S(2)}) collective-permute-start(bf16[128,512]{1,0:T(8,128)(2,1)S(1)} %constant_dynamic-slice_fusion), channel_id=1, source_target_pairs={{0,4},{2,6},{4,0},{6,2},{8,12},{10,14},{12,8},{14,10},{16,20},{18,... | collective-permute-start | bytes 393224 | tf_op jit(solution)/shard_map/ppermute | solution.py:28
  24.9 11.1 %collective-permute-start.11 = (bf16[128,512]{1,0:T(8,128)(2,1)S(1)}, bf16[128,512]{1,0:T(8,128)(2,1)S(1)}, u32[]{:S(2)}, u32[]{:S(2)}) collective-permute-start(bf16[128,512]{1,0:T(8,128)(2,1)S(1)} %constant_dynamic-slice_fusion), channel_id=1, source_target_pairs={{0,6},{2,4},{4,2},{6,0},{8,14},{10,12},{12,10},{14,8},{16,22},{18,... | collective-permute-start | bytes 393224 | tf_op jit(solution)/shard_map/ppermute | solution.py:28
  30.0 8.9 %collective-permute-start.8 = (bf16[128,512]{1,0:T(8,128)(2,1)S(1)}, bf16[128,512]{1,0:T(8,128)(2,1)S(1)}, u32[]{:S(2)}, u32[]{:S(2)}) collective-permute-start(bf16[128,512]{1,0:T(8,128)(2,1)S(1)} %pad_maximum_fusion.9), channel_id=1, source_target_pairs={{0,6},{2,4},{4,2},{6,0},{8,14},{10,12},{12,10},{14,8},{16,22},{18,... | collective-permute-start | bytes 393224 | tf_op jit(solution)/shard_map/ppermute | solution.py:28
  35.1 5.1 %collective-permute-start.7 = (bf16[128,512]{1,0:T(8,128)(2,1)S(1)}, bf16[128,512]{1,0:T(8,128)(2,1)S(1)}, u32[]{:S(2)}, u32[]{:S(2)}) collective-permute-start(bf16[128,512]{1,0:T(8,128)(2,1)S(1)} %pad_maximum_fusion.8), channel_id=1, source_target_pairs={{0,4},{2,6},{4,0},{6,2},{8,12},{10,14},{12,8},{14,10},{16,20},{18,... | collective-permute-start | bytes 393224 | tf_op jit(solution)/shard_map/ppermute | solution.py:28
  35.2 6.5 %collective-permute-start.6 = (bf16[128,512]{1,0:T(8,128)(2,1)S(1)}, bf16[128,512]{1,0:T(8,128)(2,1)S(1)}, u32[]{:S(2)}, u32[]{:S(2)}) collective-permute-start(bf16[128,512]{1,0:T(8,128)(2,1)S(1)} %pad_maximum_fusion.7), channel_id=1, source_target_pairs={{0,2},{2,0},{4,6},{6,4},{8,10},{10,8},{12,14},{14,12},{16,18},{18,... | collective-permute-start | bytes 393224 | tf_op jit(solution)/shard_map/ppermute | solution.py:28
  37.4 8.9 %collective-permute-start.12 = (bf16[1024,128]{1,0:T(8,128)(2,1)S(1)}, bf16[1024,128]{1,0:T(8,128)(2,1)S(1)}, u32[]{:S(2)}, u32[]{:S(2)}) collective-permute-start(bf16[1024,128]{1,0:T(8,128)(2,1)S(1)} %pad_maximum_fusion.1), channel_id=1, source_target_pairs={{0,8},{2,10},{4,12},{6,14},{8,0},{10,2},{12,4},{14,6},{16,24},{18,... | collective-permute-start | bytes 786440 | tf_op jit(solution)/shard_map/ppermute | solution.py:32
  41.8 6.9 %collective-permute-start.16 = (bf16[1024,128]{1,0:T(8,128)(2,1)S(1)}, bf16[1024,128]{1,0:T(8,128)(2,1)S(1)}, u32[]{:S(2)}, u32[]{:S(2)}) collective-permute-start(bf16[1024,128]{1,0:T(8,128)(2,1)S(1)} %pad_maximum_fusion.2), channel_id=1, source_target_pairs={{0,2},{2,0},{4,6},{6,4},{8,10},{10,8},{12,14},{14,12},{16,18},{18,... | collective-permute-start | bytes 786440 | tf_op jit(solution)/shard_map/ppermute | solution.py:28
  49.4 6.4 %collective-permute-start.17 = (bf16[512,128]{1,0:T(8,128)(2,1)}, bf16[512,128]{1,0:T(8,128)(2,1)}, u32[]{:S(2)}, u32[]{:S(2)}) collective-permute-start(bf16[512,128]{1,0:T(8,128)(2,1)} %add_convert_fusion.2), channel_id=1, source_target_pairs={{0,4},{2,6},{4,0},{6,2},{8,12},{10,14},{12,8},{14,10},{16,20},{18,... | collective-permute-start | bytes 393224 | tf_op jit(solution)/shard_map/ppermute | solution.py:28
  50.1 18.3 %collective-permute-start.13 = (bf16[64,512]{1,0:T(8,128)(2,1)S(1)}, bf16[64,512]{1,0:T(8,128)(2,1)S(1)}, u32[]{:S(2)}, u32[]{:S(2)}) collective-permute-start(bf16[64,512]{1,0:T(8,128)(2,1)S(1)} %get-tuple-element.56), channel_id=1, source_target_pairs={{0,8},{2,10},{4,12},{6,14},{8,0},{10,2},{12,4},{14,6},{16,24},{18,... | collective-permute-start | bytes 196616 | tf_op jit(solution)/shard_map/ppermute | solution.py:32
  51.4 17.0 %collective-permute-start.14 = (bf16[64,512]{1,0:T(8,128)(2,1)S(1)}, bf16[64,512]{1,0:T(8,128)(2,1)S(1)}, u32[]{:S(2)}, u32[]{:S(2)}) collective-permute-start(bf16[64,512]{1,0:T(8,128)(2,1)S(1)} %get-tuple-element.55), channel_id=1, source_target_pairs={{0,16},{2,18},{4,20},{6,22},{8,24},{10,26},{12,28},{14,30},{16,0},... | collective-permute-start | bytes 196616 | tf_op jit(solution)/shard_map/ppermute | solution.py:32
  54.3 14.1 %collective-permute-start.15 = (bf16[64,512]{1,0:T(8,128)(2,1)S(1)}, bf16[64,512]{1,0:T(8,128)(2,1)S(1)}, u32[]{:S(2)}, u32[]{:S(2)}) collective-permute-start(bf16[64,512]{1,0:T(8,128)(2,1)S(1)} %get-tuple-element.54), channel_id=1, source_target_pairs={{0,24},{2,26},{4,28},{6,30},{8,16},{10,18},{12,20},{14,22},{16,8},... | collective-permute-start | bytes 196616 | tf_op jit(solution)/shard_map/ppermute | solution.py:32
  54.5 9.4 %collective-permute-start.18 = (bf16[512,128]{1,0:T(8,128)(2,1)S(1)}, bf16[512,128]{1,0:T(8,128)(2,1)S(1)}, u32[]{:S(2)}, u32[]{:S(2)}) collective-permute-start(bf16[512,128]{1,0:T(8,128)(2,1)S(1)} %get-tuple-element.27), channel_id=1, source_target_pairs={{0,16},{2,18},{4,20},{6,22},{8,24},{10,26},{12,28},{14,30},{16,0},... | collective-permute-start | bytes 393224 | tf_op jit(solution)/shard_map/ppermute | solution.py:32
  56.8 10.4 %copy-start.1 = (bf16[128,1024]{1,0:T(8,128)(2,1)S(1)}, bf16[128,1024]{1,0:T(8,128)(2,1)}, u32[]{:S(2)}) copy-start(bf16[128,1024]{1,0:T(8,128)(2,1)} %param.5) | copy-start | bytes 786436

commit v10 on v9

--- a/solution.py
+++ b/solution.py
@@ -49,7 +49,9 @@
         return lax.dot_general(lhs, rhs, (dims, ((), ())), preferred_element_type=jnp.float32)
 
     def after(value, *others):
-        return lax.optimization_barrier((value,) + others)[0]
+        firsts = [lax.slice(other, (0,) * other.ndim, (1,) * other.ndim) for other in others]
+        zero = sum(first.astype(jnp.float32).reshape(()) * 0 for first in firsts)
+        return value + zero.astype(value.dtype)
 
     def lanes(value, index):
         return value[:, index * tile_size : (index + 1) * tile_size]
@@ -57,9 +59,7 @@
     hidden_part = jnp.maximum(
         lax.dynamic_slice_in_dim(hidden_pre, rep_pos * cols_here, cols_here, 1), 0
     )
-    hidden_stack = jnp.concatenate([along_outer(hidden_part, e) for e in turns], 0)
-
-    columns = after(adj_cols, hidden_part)[0]
+    columns = adj_cols[0]
     turn_of = (columns & (side - 1)) ^ inner_pos
     level_of = (columns >> bits) ^ outer_pos
     place = turn_of * per_core + (level_of & (per_core - 1))
@@ -67,25 +67,40 @@
     ordered = jnp.zeros((section_span, tile_size, tile_size), bf16)
     for k in range(slots):
         ordered = jnp.where(hit[:, k, None, None], adj_vals[0, k][None], ordered)
-    everyone = lax.all_gather(ordered, "rep", axis=0)
-    row_block = outer_pos * side + inner_pos
+    arrived = []
+    for t in turns:
+        message = ordered[t * per_core : (t + 1) * per_core]
+        arrived.append(along_inner(message, t))
+    held = {0: hidden_part}
+    for bit in rising[::-1]:
+        keys = list(held)
+        sent = jnp.concatenate([held[k] for k in keys], 0)
+        got = along_outer(after(sent, *arrived[1:]) if len(keys) > 1 else sent, bit)
+        for n, k in enumerate(keys):
+            held[k ^ bit] = got[n * tile_size : (n + 1) * tile_size]
+    hidden_stack = jnp.concatenate([held[e] for e in turns], 0)
+
+    grad_part = lax.dynamic_slice_in_dim(cotangent, rep_pos * cols_here, cols_here, 1)
+    grad_part = after(grad_part, *arrived[1:], held[rising[-1]])
+    grad_stack = [along_inner(grad_part, t) for t in turns]
+    everyone = after(jnp.concatenate(arrived, 0), held[side - 1], *grad_stack[1:])
+    everyone = lax.all_gather(everyone, "rep", axis=0)
+    grad_stack = jnp.concatenate(grad_stack, 0)
+
     rows = []
     for t in turns:
+        row_block = outer_pos * side + (inner_pos ^ t)
         row = []
         for e in turns:
-            column_block = (outer_pos ^ e) * side + (inner_pos ^ t)
+            column_block = (outer_pos ^ e) * side + inner_pos
             holder = ((row_block - column_block) & (blk_count - 1)) >> span_bits
             index = t * per_core + e % per_core
             piece = everyone[0, index]
             for r in range(1, rep_count):
                 piece = jnp.where(holder == r, everyone[r, index], piece)
             row.append(piece)
-        rows.append(along_inner(jnp.concatenate(row, 1), t))
+        rows.append(jnp.concatenate(row, 1))
     block = jnp.concatenate(rows, 0)
-
-    grad_part = lax.dynamic_slice_in_dim(cotangent, rep_pos * cols_here, cols_here, 1)
-    grad_part = after(grad_part, rows[1])
-    grad_stack = jnp.concatenate([along_inner(grad_part, t) for t in turns], 0)
 
     mixed = dot(hidden_stack, block, ((0,), (1,))).astype(bf16)
     share = cols_here // side
@@ -97,14 +112,13 @@
         chosen = jnp.concatenate([lanes(chosen, u ^ t) for u in turns], 1)
         mixed_cols.append(along_inner(chosen, t))
     mixed_cols = sum(part.astype(jnp.float32) for part in mixed_cols).astype(bf16)
-    back = dot(after(grad_stack, mixed), block, ((0,), (0,)))
+    back = after(dot(grad_stack, block, ((0,), (0,))), mixed)
     back = halved([lanes(back, e) for e in turns], along_outer, rising[:-1])
     rows = [lanes(after(mixed, mixed_cols), t) for t in turns]
     rows = halved(rows, along_inner, rising[:-1])
 
     mixed_cols = lax.all_gather(mixed_cols, "rep", axis=0, tiled=True)
-    mixed_cols, back[0] = lax.optimization_barrier((mixed_cols, back[0]))
-    weight_part = dot(mixed_cols, grad_stack, ((1,), (0,))).astype(bf16)
+    weight_part = after(dot(mixed_cols, grad_stack, ((1,), (0,))), back[0]).astype(bf16)
     by_outer = weight_part.reshape(side, rows_here, cols_here)
     weight_got = [
         along_outer(lax.dynamic_index_in_dim(by_outer, outer_pos ^ t, 0, keepdims=False), t)
@@ -128,10 +142,7 @@
     pre_part = lax.dynamic_slice_in_dim(hidden_pre, rep_pos * cols_here, cols_here, 1)
     grad_pre = jnp.where(pre_part > 0, grad_in, 0.0).astype(bf16)
 
-    weight_got[1:], out_part, grad_pre = lax.optimization_barrier(
-        (weight_got[1:], out_part, grad_pre)
-    )
-    grad_weight = sum(part.astype(jnp.float32) for part in weight_got)
+    grad_weight = after(sum(part.astype(jnp.float32) for part in weight_got), out_part)
     return (out_part, grad_weight, grad_pre)
 
 

time: 69.4 us -> 71.8 us (1.035)
  between operations: 0.97 us -> 9.42 us
  local copies, waits for them, and re-layouts: 1.18 us -> 8.54 us
  waiting for transfers between devices: 21.4 us -> 15.6 us
  starting transfers between devices: 28.9 us -> 23.5 us
  other arithmetic: 4.72 us -> 3.39 us
  matrix products: 5.52 us -> 4.55 us
    slice x0 -> x14, local copies, waits for them, and re-layouts: none -> 7.38 us  [the longest x13 7.36 us: after(): lax.slice(other, (0,) * other.ndim, (1,) * other.ndim)]
    ppermute x11, waiting for transfers between devices: 14.3 us -> 9.5 us  [along_inner(): return lax.ppermute(value, 'blk', pairs) if turn else value]
    ppermute x11, starting transfers between devices: 16.1 us -> 12.4 us  [along_inner(): return lax.ppermute(value, 'blk', pairs) if turn else value]
    ppermute x8 -> x7, starting transfers between devices: 12.8 us -> 11.1 us  [along_outer(): return lax.ppermute(value, 'blk', pairs) if turn else value]
    ppermute x8 -> x7, waiting for transfers between devices: 7.11 us -> 6.13 us  [along_outer(): return lax.ppermute(value, 'blk', pairs) if turn else value]
    dot_general x5, matrix products: 5.52 us -> 4.55 us  [dot(): lax.dot_general(lhs, rhs, (dims, ((), ())), preferred_element_type=jnp.fl...]
    concatenate x3, other arithmetic: 1.01 us -> 0.12 us  [shards(): both = jnp.concatenate([rows_sum, back], 0).astype(bf16)]
  transfers between devices with their start and end apart: 19 -> 18, of which waited for: 7 -> 8; matrix products, arithmetic and copies ran while one was open for 13% -> 18% of each run, Pallas kernels for 0% -> 0%
where the time goes in v10:
time: 71.8 us; the launch traced here: 71.4 us
  starting transfers between devices  23.5 us (33%)
  waiting for transfers between devices  15.6 us (22%)
  between operations  9.42 us (13%)
  local copies, waits for them, and re-layouts  8.54 us (12%)
  blocking collectives  6.34 us (9%)
  matrix products  4.55 us (6%)
  other arithmetic  3.39 us (5%)
    ppermute x11, starting transfers between devices, along_inner(): return lax.ppermute(value, 'blk', pairs) if turn else value  12.4 us
    ppermute x7, starting transfers between devices, along_outer(): return lax.ppermute(value, 'blk', pairs) if turn else value  11.1 us
    ppermute x11, waiting for transfers between devices, along_inner(): return lax.ppermute(value, 'blk', pairs) if turn else value  9.5 us
    slice x13, local copies, waits for them, and re-layouts, after(): lax.slice(other, (0,) * other.ndim, (1,) * other.ndim)  7.36 us
    ppermute x7, waiting for transfers between devices, along_outer(): return lax.ppermute(value, 'blk', pairs) if turn else value  6.13 us
    dot_general x5, matrix products, dot(): lax.dot_general(lhs, rhs, (dims, ((), ())), preferred_element_type=jnp.fl...  4.55 us
    all_gather x1, blocking collectives, shards(): everyone = lax.all_gather(everyone, 'rep', axis=0)  2.18 us
    all_gather x1, blocking collectives, shards(): both = lax.all_gather(both, 'rep', axis=0)  2.18 us
  transfers between devices with their start and end apart: 18, of which 8 were waited for; matrix products, arithmetic and copies ran while one was open for 18% of the time, Pallas kernels for 0%

profile of v10, /device:TPU:0, one launch (start us, length us, event | category | flops | bytes accessed | tf_op | source)
XLA Modules:
  0.0 71.4 jit_solution(17902986568511932651)
XLA Ops:
  0.7 1.1 %dynamic-slice_maximum_fusion = bf16[128,512]{1,0:T(8,128)(2,1)S(1)} fusion(bf16[128,1024]{1,0:T(8,128)(2,1)} %param.5, s32[]{:T(128)S(6)} %select_n.198), kind=kLoop, calls=%fused_computation.46 | loop fusion | flops 262144 | bytes 262148 | tf_op jit(solution)/shard_map/max | solution.py:59
  1.8 4.1 %collective-permute-start = (bf16[128,512]{1,0:T(8,128)(2,1)S(1)}, bf16[128,512]{1,0:T(8,128)(2,1)S(1)}, u32[]{:S(2)}, u32[]{:S(2)}) collective-permute-start(bf16[128,512]{1,0:T(8,128)(2,1)S(1)} %dynamic-slice_maximum_fusion), channel_id=1, source_target_pairs={{0,16},{2,18},{4,20},{6,22},{8,24},{10,26},{12,28},{14,30},{16,0},... | collective-permute-start | bytes 393224 | tf_op jit(solution)/shard_map/ppermute | solution.py:32
  5.9 0.7 add_bitcast_fusion
  6.6 0.9 %slice_bitcast_fusion.10 = (bf16[128,128]{1,0:T(8,128)(2,1)S(1)}, bf16[128,128]{1,0:T(8,128)(2,1)S(1)}, bf16[128,128]{1,0:T(8,128)(2,1)S(1)}, bf16[128,128]{1,0:...) fusion(bf16[1,8,128,128]{3,2,1,0:T(8,128)(2,1)} %param.6), kind=kLoop, calls=%fused_computation.75 | loop fusion | bytes 524288 | tf_op jit(solution)/shard_map/jit(_where)/broadcast_in_dim | solution.py:69
  7.7 1.6 %collective-permute-start.1 = (bf16[2,128,128]{2,1,0:T(8,128)(2,1)S(1)}, bf16[2,128,128]{2,1,0:T(8,128)(2,1)S(1)}, u32[]{:S(2)}, u32[]{:S(2)}) collective-permute-start(bf16[2,128,128]{2,1,0:T(8,128)(2,1)S(1)} %get-tuple-element.38), channel_id=1, source_target_pairs={{0,2},{2,0},{4,6},{6,4},{8,10},{10,8},{12,14},{14,12},{16,18},{18,... | collective-permute-start | bytes 196616 | tf_op jit(solution)/shard_map/ppermute | solution.py:28
  9.3 1.5 %collective-permute-start.2 = (bf16[2,128,128]{2,1,0:T(8,128)(2,1)S(1)}, bf16[2,128,128]{2,1,0:T(8,128)(2,1)S(1)}, u32[]{:S(2)}, u32[]{:S(2)}) collective-permute-start(bf16[2,128,128]{2,1,0:T(8,128)(2,1)S(1)} %get-tuple-element.37), channel_id=1, source_target_pairs={{0,4},{2,6},{4,0},{6,2},{8,12},{10,14},{12,8},{14,10},{16,20},{18,... | collective-permute-start | bytes 196616 | tf_op jit(solution)/shard_map/ppermute | solution.py:28
  11.3 0.8 %collective-permute-done.1 = bf16[2,128,128]{2,1,0:T(8,128)(2,1)S(1)} collective-permute-done((bf16[2,128,128]{2,1,0:T(8,128)(2,1)S(1)}, bf16[2,128,128]{2,1,0:T(8,128)(2,1)S(1)}, u32[]{:S(2)}, u32[]{:S(2)}) %collective-permute-start.1) | collective-permute-done | bytes 65568 | tf_op jit(solution)/shard_map/ppermute | solution.py:28
  12.6 1.7 %collective-permute-done.2 = bf16[2,128,128]{2,1,0:T(8,128)(2,1)S(1)} collective-permute-done((bf16[2,128,128]{2,1,0:T(8,128)(2,1)S(1)}, bf16[2,128,128]{2,1,0:T(8,128)(2,1)S(1)}, u32[]{:S(2)}, u32[]{:S(2)}) %collective-permute-start.2) | collective-permute-done | bytes 65568 | tf_op jit(solution)/shard_map/ppermute | solution.py:28
  17.3 1.6 %collective-permute-start.4 = (bf16[256,512]{1,0:T(8,128)(2,1)S(1)}, bf16[256,512]{1,0:T(8,128)(2,1)S(1)}, u32[]{:S(2)}, u32[]{:S(2)}) collective-permute-start(bf16[256,512]{1,0:T(8,128)(2,1)S(1)} %maximum_add_fusion), channel_id=1, source_target_pairs={{0,8},{2,10},{4,12},{6,14},{8,0},{10,2},{12,4},{14,6},{16,24},{18,... | collective-permute-start | bytes 786440 | tf_op jit(solution)/shard_map/ppermute | solution.py:32
  20.2 0.6 collective-permute-start.5
  20.7 1.5 %collective-permute-start.6 = (bf16[128,512]{1,0:T(8,128)(2,1)S(1)}, bf16[128,512]{1,0:T(8,128)(2,1)S(1)}, u32[]{:S(2)}, u32[]{:S(2)}) collective-permute-start(bf16[128,512]{1,0:T(8,128)(2,1)S(1)} %dynamic-slice_add_fusion), channel_id=1, source_target_pairs={{0,4},{2,6},{4,0},{6,2},{8,12},{10,14},{12,8},{14,10},{16,20},{18,... | collective-permute-start | bytes 393224 | tf_op jit(solution)/shard_map/ppermute | solution.py:28
  22.3 1.5 %collective-permute-start.7 = (bf16[128,512]{1,0:T(8,128)(2,1)S(1)}, bf16[128,512]{1,0:T(8,128)(2,1)}, u32[]{:S(2)}, u32[]{:S(2)}) collective-permute-start(bf16[128,512]{1,0:T(8,128)(2,1)S(1)} %dynamic-slice_add_fusion), channel_id=1, source_target_pairs={{0,6},{2,4},{4,2},{6,0},{8,14},{10,12},{12,10},{14,8},{16,22},{18,... | collective-permute-start | bytes 393224 | tf_op jit(solution)/shard_map/ppermute | solution.py:28
  23.7 1.5 %collective-permute-done.5 = bf16[128,512]{1,0:T(8,128)(2,1)S(1)} collective-permute-done((bf16[128,512]{1,0:T(8,128)(2,1)S(1)}, bf16[128,512]{1,0:T(8,128)(2,1)S(1)}, u32[]{:S(2)}, u32[]{:S(2)}) %collective-permute-start.5) | collective-permute-done | bytes 131104 | tf_op jit(solution)/shard_map/ppermute | solution.py:28
  26.3 2.0 %collective-permute-done.7 = bf16[128,512]{1,0:T(8,128)(2,1)} collective-permute-done((bf16[128,512]{1,0:T(8,128)(2,1)S(1)}, bf16[128,512]{1,0:T(8,128)(2,1)}, u32[]{:S(2)}, u32[]{:S(2)}) %collective-permute-start.7) | collective-permute-done | bytes 131104 | tf_op jit(solution)/shard_map/ppermute | solution.py:28
  28.2 1.2 %slice.347 = bf16[1,1]{1,0:T(2,128)(2,1)} slice(bf16[128,512]{1,0:T(8,128)(2,1)} %collective-permute-done.7), slice={[0:1], [0:1]} | slice | bytes 4 | tf_op jit(solution)/shard_map/slice | solution.py:52
  32.5 2.2 %all_gather.11 = bf16[2,8,128,128]{3,2,1,0:T(8,128)(2,1)S(1)} all-gather(bf16[1,8,128,128]{3,2,1,0:T(8,128)(2,1)S(1)} %maximum_add_fusion.1), channel_id=1, replica_groups=mesh['blk'=16,'rep'=2] {'rep'}, dimensions={0}, use_global_device_ids=true | all-gather | bytes 786432 | tf_op jit(solution)/shard_map/all_gather | solution.py:87
  36.7 1.5 %collective-permute-start.10 = (bf16[128,512]{1,0:T(8,128)(2,1)S(1)}, bf16[128,512]{1,0:T(8,128)(2,1)S(1)}, u32[]{:S(2)}, u32[]{:S(2)}) collective-permute-start(bf16[128,512]{1,0:T(8,128)(2,1)S(1)} %pad_maximum_fusion.6), channel_id=1, source_target_pairs={{0,6},{2,4},{4,2},{6,0},{8,14},{10,12},{12,10},{14,8},{16,22},{18,... | collective-permute-start | bytes 393224 | tf_op jit(solution)/shard_map/ppermute | solution.py:28
  38.2 1.0 %collective-permute-start.9 = (bf16[128,512]{1,0:T(8,128)(2,1)S(1)}, bf16[128,512]{1,0:T(8,128)(2,1)S(1)}, u32[]{:S(2)}, u32[]{:S(2)}) collective-permute-start(bf16[128,512]{1,0:T(8,128)(2,1)S(1)} %pad_maximum_fusion.5), channel_id=1, source_target_pairs={{0,4},{2,6},{4,0},{6,2},{8,12},{10,14},{12,8},{14,10},{16,20},{18,... | collective-permute-start | bytes 393224 | tf_op jit(solution)/shard_map/ppermute | solution.py:28
  39.3 1.1 %collective-permute-start.8 = (bf16[128,512]{1,0:T(8,128)(2,1)S(1)}, bf16[128,512]{1,0:T(8,128)(2,1)S(1)}, u32[]{:S(2)}, u32[]{:S(2)}) collective-permute-start(bf16[128,512]{1,0:T(8,128)(2,1)S(1)} %pad_maximum_fusion.4), channel_id=1, source_target_pairs={{0,2},{2,0},{4,6},{6,4},{8,10},{10,8},{12,14},{14,12},{16,18},{18,... | collective-permute-start | bytes 393224 | tf_op jit(solution)/shard_map/ppermute | solution.py:28
  40.4 1.4 %fusion.34 = (bf16[512,512]{1,0:T(8,128)(2,1)S(1)}, f32[512,512]{1,0:T(8,128)S(1)}) fusion(f32[]{:T(128)} %bitcast.46, bf16[512,512]{1,0:T(8,128)(2,1)S(1)} %maximum_maximum_fusion, bf16[128,512]{1,0:T(8,128)(2,1)} %collective-permute-done.7, bf16[128,512]{1,0:T(8,128)(2,1)S(1)} %collective-permute-done.6, ...), kind=kOutput, calls=%fused_computation.102 | convolution fusion | flops 271056896 | bytes 2621444 | tf_op jit(solution)/shard_map/dot_general | solution.py:49
  42.4 1.6 %collective-permute-done.10 = bf16[128,512]{1,0:T(8,128)(2,1)S(1)} collective-permute-done((bf16[128,512]{1,0:T(8,128)(2,1)S(1)}, bf16[128,512]{1,0:T(8,128)(2,1)S(1)}, u32[]{:S(2)}, u32[]{:S(2)}) %collective-permute-start.10) | collective-permute-done | bytes 131104 | tf_op jit(solution)/shard_map/ppermute | solution.py:28
  44.0 2.0 %collective-permute-done.9 = bf16[128,512]{1,0:T(8,128)(2,1)S(1)} collective-permute-done((bf16[128,512]{1,0:T(8,128)(2,1)S(1)}, bf16[128,512]{1,0:T(8,128)(2,1)S(1)}, u32[]{:S(2)}, u32[]{:S(2)}) %collective-permute-start.9) | collective-permute-done | bytes 131104 | tf_op jit(solution)/shard_map/ppermute | solution.py:28
  47.3 2.1 %collective-permute-done.12 = bf16[1024,128]{1,0:T(8,128)(2,1)S(1)} collective-permute-done((bf16[1024,128]{1,0:T(8,128)(2,1)S(1)}, bf16[1024,128]{1,0:T(8,128)(2,1)S(1)}, u32[]{:S(2)}, u32[]{:S(2)}) %collective-permute-start.12) | collective-permute-done | bytes 262176 | tf_op jit(solution)/shard_map/ppermute | solution.py:32
  49.9 1.0 %collective-permute-start.11 = (bf16[1024,128]{1,0:T(8,128)(2,1)S(1)}, bf16[1024,128]{1,0:T(8,128)(2,1)S(1)}, u32[]{:S(2)}, u32[]{:S(2)}) collective-permute-start(bf16[1024,128]{1,0:T(8,128)(2,1)S(1)} %pad_maximum_fusion.1), channel_id=1, source_target_pairs={{0,2},{2,0},{4,6},{6,4},{8,10},{10,8},{12,14},{14,12},{16,18},{18,... | collective-permute-start | bytes 786440 | tf_op jit(solution)/shard_map/ppermute | solution.py:28
  50.9 2.0 %all_gather.12 = bf16[256,512]{1,0:T(8,128)(2,1)S(1)} all-gather(bf16[128,512]{1,0:T(8,128)(2,1)S(1)} %fusion.14), channel_id=1, replica_groups=mesh['blk'=16,'rep'=2] {'rep'}, dimensions={0}, use_global_device_ids=true | all-gather | bytes 393216 | tf_op jit(solution)/shard_map/all_gather | solution.py:120
  52.9 4.0 %collective-permute-done.14 = bf16[512,128]{1,0:T(8,128)(2,1)S(1)} collective-permute-done((bf16[512,128]{1,0:T(8,128)(2,1)S(1)}, bf16[512,128]{1,0:T(8,128)(2,1)S(1)}, u32[]{:S(2)}, u32[]{:S(2)}) %collective-permute-start.14) | collective-permute-done | bytes 131104 | tf_op jit(solution)/shard_map/ppermute | solution.py:32
  58.1 1.2 %fusion = bf16[256,512]{1,0:T(8,128)(2,1)S(1)} fusion(bf16[256,512]{1,0:T(8,128)(2,1)S(1)} %all_gather.12, f32[]{:T(128)} %bitcast.47, bf16[128,512]{1,0:T(8,128)(2,1)} %collective-permute-done.7, bf16[128,512]{1,0:T(8,128)(2,1)S(1)} %copy-done.5, bf16[128,512]{1,0:T(8,128)(2,1)S(1)} %collective-permute-done.5, bf16[128,512]{1,0:T(8,128)(2,1)S(1)} %dynamic-slice_add_fusion), kind=kOutput, calls=%fused_computation.3 | convolution fusion | flops 136577024 | bytes 1048580 | tf_op jit(solution)/shard_map/dot_general | solution.py:49
  60.6 0.6 collective-permute-start.13
  61.8 3.9 %collective-permute-start.15 = (bf16[64,512]{1,0:T(8,128)(2,1)S(1)}, bf16[64,512]{1,0:T(8,128)(2,1)S(1)}, u32[]{:S(2)}, u32[]{:S(2)}) collective-permute-start(bf16[64,512]{1,0:T(8,128)(2,1)S(1)} %get-tuple-element.30), channel_id=1, source_target_pairs={{0,8},{2,10},{4,12},{6,14},{8,0},{10,2},{12,4},{14,6},{16,24},{18,... | collective-permute-start | bytes 196616 | tf_op jit(solution)/shard_map/ppermute | solution.py:32
  65.7 2.2 %all_gather.13 = bf16[2,1024,128]{2,1,0:T(8,128)(2,1)S(1)} all-gather(bf16[1,1024,128]{2,1,0:T(8,128)(2,1)S(1)} %pad_maximum_fusion.3), channel_id=1, replica_groups=mesh['blk'=16,'rep'=2] {'rep'}, dimensions={0}, use_global_device_ids=true | all-gather | bytes 786432 | tf_op jit(solution)/shard_map/all_gather | solution.py:134
  68.3 1.2 %fusion.1 = bf16[128,512]{1,0:T(8,128)(2,1)} fusion(bf16[1024,128]{1,0:T(8,128)(2,1)S(1)} %bitcast.120, bf16[1024,1024]{1,0:T(8,128)(2,1)S(1)} %copy-done, s32[]{:T(128)S(6)} %select_n.198, bf16[128,1024]{1,0:T(8,128)(2,1)S(1)} %copy-done.1), kind=kOutput, calls=%fused_computation.6 | convolution fusion | flops 134545408 | bytes 1573888 | tf_op jit(solution)/shard_map/dot_general | solution.py:49
  70.7 0.7 fusion.20
  (74 shorter events, 10.2 us)
Async XLA Ops:
  0.6 67.3 %copy-start = (bf16[1024,1024]{1,0:T(8,128)(2,1)S(1)}, bf16[1024,1024]{1,0:T(8,128)(2,1)}, u32[]{:S(2)}) copy-start(bf16[1024,1024]{1,0:T(8,128)(2,1)} %param.8) | copy-start | bytes 6291460
  0.6 19.5 %copy-start.3 = (bf16[128,1024]{1,0:T(8,128)(2,1)S(1)}, bf16[128,1024]{1,0:T(8,128)(2,1)}, u32[]{:S(2)}) copy-start(bf16[128,1024]{1,0:T(8,128)(2,1)} %param.9) | copy-start | bytes 786436
  1.8 15.5 %collective-permute-start = (bf16[128,512]{1,0:T(8,128)(2,1)S(1)}, bf16[128,512]{1,0:T(8,128)(2,1)S(1)}, u32[]{:S(2)}, u32[]{:S(2)}) collective-permute-start(bf16[128,512]{1,0:T(8,128)(2,1)S(1)} %dynamic-slice_maximum_fusion), channel_id=1, source_target_pairs={{0,16},{2,18},{4,20},{6,22},{8,24},{10,26},{12,28},{14,30},{16,0},... | collective-permute-start | bytes 393224 | tf_op jit(solution)/shard_map/ppermute | solution.py:32
  7.7 4.3 %collective-permute-start.1 = (bf16[2,128,128]{2,1,0:T(8,128)(2,1)S(1)}, bf16[2,128,128]{2,1,0:T(8,128)(2,1)S(1)}, u32[]{:S(2)}, u32[]{:S(2)}) collective-permute-start(bf16[2,128,128]{2,1,0:T(8,128)(2,1)S(1)} %get-tuple-element.38), channel_id=1, source_target_pairs={{0,2},{2,0},{4,6},{6,4},{8,10},{10,8},{12,14},{14,12},{16,18},{18,... | collective-permute-start | bytes 196616 | tf_op jit(solution)/shard_map/ppermute | solution.py:28
  9.3 5.0 %collective-permute-start.2 = (bf16[2,128,128]{2,1,0:T(8,128)(2,1)S(1)}, bf16[2,128,128]{2,1,0:T(8,128)(2,1)S(1)}, u32[]{:S(2)}, u32[]{:S(2)}) collective-permute-start(bf16[2,128,128]{2,1,0:T(8,128)(2,1)S(1)} %get-tuple-element.37), channel_id=1, source_target_pairs={{0,4},{2,6},{4,0},{6,2},{8,12},{10,14},{12,8},{14,10},{16,20},{18,... | collective-permute-start | bytes 196616 | tf_op jit(solution)/shard_map/ppermute | solution.py:28
  10.8 5.3 %collective-permute-start.3 = (bf16[2,128,128]{2,1,0:T(8,128)(2,1)S(1)}, bf16[2,128,128]{2,1,0:T(8,128)(2,1)S(1)}, u32[]{:S(2)}, u32[]{:S(2)}) collective-permute-start(bf16[2,128,128]{2,1,0:T(8,128)(2,1)S(1)} %get-tuple-element.36), channel_id=1, source_target_pairs={{0,6},{2,4},{4,2},{6,0},{8,14},{10,12},{12,10},{14,8},{16,22},{18,... | collective-permute-start | bytes 196616 | tf_op jit(solution)/shard_map/ppermute | solution.py:28
  17.3 12.1 %collective-permute-start.4 = (bf16[256,512]{1,0:T(8,128)(2,1)S(1)}, bf16[256,512]{1,0:T(8,128)(2,1)S(1)}, u32[]{:S(2)}, u32[]{:S(2)}) collective-permute-start(bf16[256,512]{1,0:T(8,128)(2,1)S(1)} %maximum_add_fusion), channel_id=1, source_target_pairs={{0,8},{2,10},{4,12},{6,14},{8,0},{10,2},{12,4},{14,6},{16,24},{18,... | collective-permute-start | bytes 786440 | tf_op jit(solution)/shard_map/ppermute | solution.py:32
  20.2 5.0 %collective-permute-start.5 = (bf16[128,512]{1,0:T(8,128)(2,1)S(1)}, bf16[128,512]{1,0:T(8,128)(2,1)S(1)}, u32[]{:S(2)}, u32[]{:S(2)}) collective-permute-start(bf16[128,512]{1,0:T(8,128)(2,1)S(1)} %dynamic-slice_add_fusion), channel_id=1, source_target_pairs={{0,2},{2,0},{4,6},{6,4},{8,10},{10,8},{12,14},{14,12},{16,18},{18,... | collective-permute-start | bytes 393224 | tf_op jit(solution)/shard_map/ppermute | solution.py:28
  20.7 5.0 %collective-permute-start.6 = (bf16[128,512]{1,0:T(8,128)(2,1)S(1)}, bf16[128,512]{1,0:T(8,128)(2,1)S(1)}, u32[]{:S(2)}, u32[]{:S(2)}) collective-permute-start(bf16[128,512]{1,0:T(8,128)(2,1)S(1)} %dynamic-slice_add_fusion), channel_id=1, source_target_pairs={{0,4},{2,6},{4,0},{6,2},{8,12},{10,14},{12,8},{14,10},{16,20},{18,... | collective-permute-start | bytes 393224 | tf_op jit(solution)/shard_map/ppermute | solution.py:28
  22.3 6.0 %collective-permute-start.7 = (bf16[128,512]{1,0:T(8,128)(2,1)S(1)}, bf16[128,512]{1,0:T(8,128)(2,1)}, u32[]{:S(2)}, u32[]{:S(2)}) collective-permute-start(bf16[128,512]{1,0:T(8,128)(2,1)S(1)} %dynamic-slice_add_fusion), channel_id=1, source_target_pairs={{0,6},{2,4},{4,2},{6,0},{8,14},{10,12},{12,10},{14,8},{16,22},{18,... | collective-permute-start | bytes 393224 | tf_op jit(solution)/shard_map/ppermute | solution.py:28
  25.7 14.7 %copy-start.4 = (bf16[128,512]{1,0:T(8,128)(2,1)}, bf16[128,512]{1,0:T(8,128)(2,1)S(1)}, u32[]{:S(2)}) copy-start(bf16[128,512]{1,0:T(8,128)(2,1)S(1)} %collective-permute-done.6) | copy-start | bytes 393220
  36.7 7.3 %collective-permute-start.10 = (bf16[128,512]{1,0:T(8,128)(2,1)S(1)}, bf16[128,512]{1,0:T(8,128)(2,1)S(1)}, u32[]{:S(2)}, u32[]{:S(2)}) collective-permute-start(bf16[128,512]{1,0:T(8,128)(2,1)S(1)} %pad_maximum_fusion.6), channel_id=1, source_target_pairs={{0,6},{2,4},{4,2},{6,0},{8,14},{10,12},{12,10},{14,8},{16,22},{18,... | collective-permute-start | bytes 393224 | tf_op jit(solution)/shard_map/ppermute | solution.py:28
  38.2 7.7 %collective-permute-start.9 = (bf16[128,512]{1,0:T(8,128)(2,1)S(1)}, bf16[128,512]{1,0:T(8,128)(2,1)S(1)}, u32[]{:S(2)}, u32[]{:S(2)}) collective-permute-start(bf16[128,512]{1,0:T(8,128)(2,1)S(1)} %pad_maximum_fusion.5), channel_id=1, source_target_pairs={{0,4},{2,6},{4,0},{6,2},{8,12},{10,14},{12,8},{14,10},{16,20},{18,... | collective-permute-start | bytes 393224 | tf_op jit(solution)/shard_map/ppermute | solution.py:28
  39.3 6.7 %collective-permute-start.8 = (bf16[128,512]{1,0:T(8,128)(2,1)S(1)}, bf16[128,512]{1,0:T(8,128)(2,1)S(1)}, u32[]{:S(2)}, u32[]{:S(2)}) collective-permute-start(bf16[128,512]{1,0:T(8,128)(2,1)S(1)} %pad_maximum_fusion.4), channel_id=1, source_target_pairs={{0,2},{2,0},{4,6},{6,4},{8,10},{10,8},{12,14},{14,12},{16,18},{18,... | collective-permute-start | bytes 393224 | tf_op jit(solution)/shard_map/ppermute | solution.py:28
  41.9 7.6 %collective-permute-start.12 = (bf16[1024,128]{1,0:T(8,128)(2,1)S(1)}, bf16[1024,128]{1,0:T(8,128)(2,1)S(1)}, u32[]{:S(2)}, u32[]{:S(2)}) collective-permute-start(bf16[1024,128]{1,0:T(8,128)(2,1)S(1)} %pad_maximum_fusion.2), channel_id=1, source_target_pairs={{0,8},{2,10},{4,12},{6,14},{8,0},{10,2},{12,4},{14,6},{16,24},{18,... | collective-permute-start | bytes 786440 | tf_op jit(solution)/shard_map/ppermute | solution.py:32
  46.1 12.1 %copy-start.5 = (bf16[128,512]{1,0:T(8,128)(2,1)S(1)}, bf16[128,512]{1,0:T(8,128)(2,1)}, u32[]{:S(2)}) copy-start(bf16[128,512]{1,0:T(8,128)(2,1)} %copy-done.4) | copy-start | bytes 393220
  49.5 7.4 %collective-permute-start.14 = (bf16[512,128]{1,0:T(8,128)(2,1)S(1)}, bf16[512,128]{1,0:T(8,128)(2,1)S(1)}, u32[]{:S(2)}, u32[]{:S(2)}) collective-permute-start(bf16[512,128]{1,0:T(8,128)(2,1)S(1)} %fusion.11), channel_id=1, source_target_pairs={{0,16},{2,18},{4,20},{6,22},{8,24},{10,26},{12,28},{14,30},{16,0},... | collective-permute-start | bytes 393224 | tf_op jit(solution)/shard_map/ppermute | solution.py:32
  49.9 10.6 %collective-permute-start.11 = (bf16[1024,128]{1,0:T(8,128)(2,1)S(1)}, bf16[1024,128]{1,0:T(8,128)(2,1)S(1)}, u32[]{:S(2)}, u32[]{:S(2)}) collective-permute-start(bf16[1024,128]{1,0:T(8,128)(2,1)S(1)} %pad_maximum_fusion.1), channel_id=1, source_target_pairs={{0,2},{2,0},{4,6},{6,4},{8,10},{10,8},{12,14},{14,12},{16,18},{18,... | collective-permute-start | bytes 786440 | tf_op jit(solution)/shard_map/ppermute | solution.py:28
  60.6 5.1 %collective-permute-start.13 = (bf16[512,128]{1,0:T(8,128)(2,1)S(1)}, bf16[512,128]{1,0:T(8,128)(2,1)S(1)}, u32[]{:S(2)}, u32[]{:S(2)}) collective-permute-start(bf16[512,128]{1,0:T(8,128)(2,1)S(1)} %fusion.15), channel_id=1, source_target_pairs={{0,4},{2,6},{4,0},{6,2},{8,12},{10,14},{12,8},{14,10},{16,20},{18,... | collective-permute-start | bytes 393224 | tf_op jit(solution)/shard_map/ppermute | solution.py:28
  61.2 9.5 %collective-permute-start.17 = (bf16[64,512]{1,0:T(8,128)(2,1)S(1)}, bf16[64,512]{1,0:T(8,128)(2,1)S(1)}, u32[]{:S(2)}, u32[]{:S(2)}) collective-permute-start(bf16[64,512]{1,0:T(8,128)(2,1)S(1)} %get-tuple-element.31), channel_id=1, source_target_pairs={{0,24},{2,26},{4,28},{6,30},{8,16},{10,18},{12,20},{14,22},{16,8},... | collective-permute-start | bytes 196616 | tf_op jit(solution)/shard_map/ppermute | solution.py:32
  61.6 9.1 %collective-permute-start.16 = (bf16[64,512]{1,0:T(8,128)(2,1)S(1)}, bf16[64,512]{1,0:T(8,128)(2,1)S(1)}, u32[]{:S(2)}, u32[]{:S(2)}) collective-permute-start(bf16[64,512]{1,0:T(8,128)(2,1)S(1)} %get-tuple-element.32), channel_id=1, source_target_pairs={{0,16},{2,18},{4,20},{6,22},{8,24},{10,26},{12,28},{14,30},{16,0},... | collective-permute-start | bytes 196616 | tf_op jit(solution)/shard_map/ppermute | solution.py:32
  61.8 6.6 %copy-start.1 = (bf16[128,1024]{1,0:T(8,128)(2,1)S(1)}, bf16[128,1024]{1,0:T(8,128)(2,1)}, u32[]{:S(2)}) copy-start(bf16[128,1024]{1,0:T(8,128)(2,1)} %param.5) | copy-start | bytes 786436
  61.8 8.9 %collective-permute-start.15 = (bf16[64,512]{1,0:T(8,128)(2,1)S(1)}, bf16[64,512]{1,0:T(8,128)(2,1)S(1)}, u32[]{:S(2)}, u32[]{:S(2)}) collective-permute-start(bf16[64,512]{1,0:T(8,128)(2,1)S(1)} %get-tuple-element.30), channel_id=1, source_target_pairs={{0,8},{2,10},{4,12},{6,14},{8,0},{10,2},{12,4},{14,6},{16,24},{18,... | collective-permute-start | bytes 196616 | tf_op jit(solution)/shard_map/ppermute | solution.py:32
  68.3 3.1 %copy-start.2 = (bf16[128,512]{1,0:T(8,128)(2,1)}, bf16[128,512]{1,0:T(8,128)(2,1)S(1)}, u32[]{:S(2)}) copy-start(bf16[128,512]{1,0:T(8,128)(2,1)S(1)} %convolution_convert_fusion.1) | copy-start | bytes 393220

commit v11 on v10

--- a/solution.py
+++ b/solution.py
@@ -49,9 +49,12 @@
         return lax.dot_general(lhs, rhs, (dims, ((), ())), preferred_element_type=jnp.float32)
 
     def after(value, *others):
-        firsts = [lax.slice(other, (0,) * other.ndim, (1,) * other.ndim) for other in others]
-        zero = sum(first.astype(jnp.float32).reshape(()) * 0 for first in firsts)
-        return value + zero.astype(value.dtype)
+        row = 0.0
+        for other in others:
+            flat = other[0] if other.ndim == 3 else other
+            row = row + flat[:1, :tile_size].astype(jnp.float32) * 0
+        row = jnp.concatenate([row.astype(value.dtype)] * (value.shape[-1] // tile_size), 1)
+        return value + row
 
     def lanes(value, index):
         return value[:, index * tile_size : (index + 1) * tile_size]
@@ -112,7 +115,7 @@
         chosen = jnp.concatenate([lanes(chosen, u ^ t) for u in turns], 1)
         mixed_cols.append(along_inner(chosen, t))
     mixed_cols = sum(part.astype(jnp.float32) for part in mixed_cols).astype(bf16)
-    back = after(dot(grad_stack, block, ((0,), (0,))), mixed)
+    back = dot(grad_stack, block, ((0,), (0,)))
     back = halved([lanes(back, e) for e in turns], along_outer, rising[:-1])
     rows = [lanes(after(mixed, mixed_cols), t) for t in turns]
     rows = halved(rows, along_inner, rising[:-1])

time: 71.8 us -> 63.5 us (0.88)
  between operations: 9.42 us -> 0.98 us
  local copies, waits for them, and re-layouts: 8.54 us -> 1.18 us
  starting transfers between devices: 23.5 us -> 27.8 us
  waiting for transfers between devices: 15.6 us -> 18.2 us
  other arithmetic: 3.39 us -> 4.18 us
    slice x13 -> x0, local copies, waits for them, and re-layouts: 7.36 us -> none  [after(): lax.slice(other, (0,) * other.ndim, (1,) * other.ndim)]
    ppermute x7, waiting for transfers between devices: 6.13 us -> 9.45 us  [along_outer(): return lax.ppermute(value, 'blk', pairs) if turn else value]
    ppermute x11, starting transfers between devices: 12.4 us -> 14.7 us  [along_inner(): return lax.ppermute(value, 'blk', pairs) if turn else value]
    ppermute x7, starting transfers between devices: 11.1 us -> 13.1 us  [along_outer(): return lax.ppermute(value, 'blk', pairs) if turn else value]
    add x6 -> x8, other arithmetic: 0.91 us -> 1.59 us  [after(): return value + row]
  transfers between devices with their start and end apart: 18 -> 18, of which waited for: 8 -> 10; matrix products, arithmetic and copies ran while one was open for 18% -> 9% of each run, Pallas kernels for 0% -> 0%
where the time goes in v11:
time: 63.5 us; the launch traced here: 63.2 us
  starting transfers between devices  27.8 us (44%)
  waiting for transfers between devices  18.2 us (29%)
  blocking collectives  6.34 us (10%)
  matrix products  4.54 us (7%)
  other arithmetic  4.18 us (7%)
  local copies, waits for them, and re-layouts  1.18 us (2%)
  between operations  0.98 us (2%)
    ppermute x11, starting transfers between devices, along_inner(): return lax.ppermute(value, 'blk', pairs) if turn else value  14.7 us
    ppermute x7, starting transfers between devices, along_outer(): return lax.ppermute(value, 'blk', pairs) if turn else value  13.1 us
    ppermute x7, waiting for transfers between devices, along_outer(): return lax.ppermute(value, 'blk', pairs) if turn else value  9.45 us
    ppermute x11, waiting for transfers between devices, along_inner(): return lax.ppermute(value, 'blk', pairs) if turn else value  8.8 us
    dot_general x5, matrix products, dot(): lax.dot_general(lhs, rhs, (dims, ((), ())), preferred_element_type=jnp.fl...  4.54 us
    all_gather x1, blocking collectives, shards(): everyone = lax.all_gather(everyone, 'rep', axis=0)  2.18 us
    all_gather x1, blocking collectives, shards(): both = lax.all_gather(both, 'rep', axis=0)  2.18 us
    all_gather x1, blocking collectives, shards(): mixed_cols = lax.all_gather(mixed_cols, 'rep', axis=0, tiled=True)  1.98 us
  transfers between devices with their start and end apart: 18, of which 10 were waited for; matrix products, arithmetic and copies ran while one was open for 9% of the time, Pallas kernels for 0%

profile of v11, /device:TPU:0, one launch (start us, length us, event | category | flops | bytes accessed | tf_op | source)
XLA Modules:
  0.0 63.2 jit_solution(7112033498565722124)
XLA Ops:
  0.7 0.8 %add_bitcast_fusion = s32[8]{0:T(128)S(1)} fusion(s32[1,8]{1,0:T(1,128)} %param.7, s32[]{:T(128)S(6)} %shift_right_arithmetic.54, s32[]{:T(128)S(6)} %and.60), kind=kLoop, calls=%fused_computation.125 | loop fusion | flops 56 | bytes 72 | tf_op jit(solution)/shard_map/eq | solution.py:69
  1.6 0.9 %slice_bitcast_fusion.10 = (bf16[128,128]{1,0:T(8,128)(2,1)S(1)}, bf16[128,128]{1,0:T(8,128)(2,1)S(1)}, bf16[128,128]{1,0:T(8,128)(2,1)S(1)}, bf16[128,128]{1,0:...) fusion(bf16[1,8,128,128]{3,2,1,0:T(8,128)(2,1)} %param.6), kind=kLoop, calls=%fused_computation.75 | loop fusion | bytes 524288 | tf_op jit(solution)/shard_map/jit(_where)/broadcast_in_dim | solution.py:72
  2.7 4.0 %collective-permute-start.3 = (bf16[2,128,128]{2,1,0:T(8,128)(2,1)S(1)}, bf16[2,128,128]{2,1,0:T(8,128)(2,1)S(1)}, u32[]{:S(2)}, u32[]{:S(2)}) collective-permute-start(bf16[2,128,128]{2,1,0:T(8,128)(2,1)S(1)} %get-tuple-element.38), channel_id=1, source_target_pairs={{0,6},{2,4},{4,2},{6,0},{8,14},{10,12},{12,10},{14,8},{16,22},{18,... | collective-permute-start | bytes 196616 | tf_op jit(solution)/shard_map/ppermute | solution.py:28
  7.3 0.9 %dynamic-slice_maximum_fusion = bf16[128,512]{1,0:T(8,128)(2,1)S(1)} fusion(bf16[128,1024]{1,0:T(8,128)(2,1)} %param.5, s32[]{:T(128)S(6)} %select_n.198), kind=kLoop, calls=%fused_computation.45 | loop fusion | flops 262144 | bytes 262148 | tf_op jit(solution)/shard_map/max | solution.py:62
  8.2 3.1 %collective-permute-start = (bf16[128,512]{1,0:T(8,128)(2,1)S(1)}, bf16[128,512]{1,0:T(8,128)(2,1)S(1)}, u32[]{:S(2)}, u32[]{:S(2)}) collective-permute-start(bf16[128,512]{1,0:T(8,128)(2,1)S(1)} %dynamic-slice_maximum_fusion), channel_id=1, source_target_pairs={{0,16},{2,18},{4,20},{6,22},{8,24},{10,26},{12,28},{14,30},{16,0},... | collective-permute-start | bytes 393224 | tf_op jit(solution)/shard_map/ppermute | solution.py:32
  11.5 5.3 %collective-permute-done = bf16[128,512]{1,0:T(8,128)(2,1)S(1)} collective-permute-done((bf16[128,512]{1,0:T(8,128)(2,1)S(1)}, bf16[128,512]{1,0:T(8,128)(2,1)S(1)}, u32[]{:S(2)}, u32[]{:S(2)}) %collective-permute-start) | collective-permute-done | bytes 131104 | tf_op jit(solution)/shard_map/ppermute | solution.py:32
  16.8 0.8 %collective-permute-start.4 = (bf16[256,512]{1,0:T(8,128)(2,1)S(1)}, bf16[256,512]{1,0:T(8,128)(2,1)S(1)}, u32[]{:S(2)}, u32[]{:S(2)}) collective-permute-start(bf16[256,512]{1,0:T(8,128)(2,1)S(1)} %maximum_add_fusion), channel_id=1, source_target_pairs={{0,8},{2,10},{4,12},{6,14},{8,0},{10,2},{12,4},{14,6},{16,24},{18,... | collective-permute-start | bytes 786440 | tf_op jit(solution)/shard_map/ppermute | solution.py:32
  17.7 2.5 %collective-permute-start.7 = (bf16[128,512]{1,0:T(8,128)(2,1)S(1)}, bf16[128,512]{1,0:T(8,128)(2,1)S(1)}, u32[]{:S(2)}, u32[]{:S(2)}) collective-permute-start(bf16[128,512]{1,0:T(8,128)(2,1)S(1)} %dynamic-slice_add_fusion), channel_id=1, source_target_pairs={{0,6},{2,4},{4,2},{6,0},{8,14},{10,12},{12,10},{14,8},{16,22},{18,... | collective-permute-start | bytes 393224 | tf_op jit(solution)/shard_map/ppermute | solution.py:28
  21.2 3.3 %collective-permute-done.7 = bf16[128,512]{1,0:T(8,128)(2,1)S(1)} collective-permute-done((bf16[128,512]{1,0:T(8,128)(2,1)S(1)}, bf16[128,512]{1,0:T(8,128)(2,1)S(1)}, u32[]{:S(2)}, u32[]{:S(2)}) %collective-permute-start.7) | collective-permute-done | bytes 131104 | tf_op jit(solution)/shard_map/ppermute | solution.py:28
  24.5 1.5 %collective-permute-done.6 = bf16[128,512]{1,0:T(8,128)(2,1)S(1)} collective-permute-done((bf16[128,512]{1,0:T(8,128)(2,1)S(1)}, bf16[128,512]{1,0:T(8,128)(2,1)S(1)}, u32[]{:S(2)}, u32[]{:S(2)}) %collective-permute-start.6) | collective-permute-done | bytes 131104 | tf_op jit(solution)/shard_map/ppermute | solution.py:28
  26.1 0.7 %convert_bitcast_fusion = bf16[128]{0:T(256)(128)(2,1)S(1)} fusion(bf16[128,512]{1,0:T(8,128)(2,1)S(1)} %collective-permute-done.7, bf16[128,512]{1,0:T(8,128)(2,1)S(1)} %collective-permute-done.6, bf16[128,512]{1,0:T(8,128)(2,1)} %collective-permute-done.5, bf16[256,512]{1,0:T(8,128)(2,1)S(1)} %collective-permute-done.4), kind=kLoop, calls=%fused_computation.124 | loop fusion | flops 1152 | bytes 1280 | tf_op jit(solution)/shard_map/add | solution.py:57
  26.8 2.2 %all_gather.11 = bf16[2,8,128,128]{3,2,1,0:T(8,128)(2,1)S(1)} all-gather(bf16[1,8,128,128]{3,2,1,0:T(8,128)(2,1)S(1)} %maximum_add_fusion.1), channel_id=1, replica_groups=mesh['blk'=16,'rep'=2] {'rep'}, dimensions={0}, use_global_device_ids=true | all-gather | bytes 786432 | tf_op jit(solution)/shard_map/all_gather | solution.py:90
  29.8 1.6 %collective-permute-start.10 = (bf16[128,512]{1,0:T(8,128)(2,1)S(1)}, bf16[128,512]{1,0:T(8,128)(2,1)S(1)}, u32[]{:S(2)}, u32[]{:S(2)}) collective-permute-start(bf16[128,512]{1,0:T(8,128)(2,1)S(1)} %pad_maximum_fusion.6), channel_id=1, source_target_pairs={{0,6},{2,4},{4,2},{6,0},{8,14},{10,12},{12,10},{14,8},{16,22},{18,... | collective-permute-start | bytes 393224 | tf_op jit(solution)/shard_map/ppermute | solution.py:28
  31.5 1.5 %collective-permute-start.9 = (bf16[128,512]{1,0:T(8,128)(2,1)S(1)}, bf16[128,512]{1,0:T(8,128)(2,1)S(1)}, u32[]{:S(2)}, u32[]{:S(2)}) collective-permute-start(bf16[128,512]{1,0:T(8,128)(2,1)S(1)} %pad_maximum_fusion.5), channel_id=1, source_target_pairs={{0,4},{2,6},{4,0},{6,2},{8,12},{10,14},{12,8},{14,10},{16,20},{18,... | collective-permute-start | bytes 393224 | tf_op jit(solution)/shard_map/ppermute | solution.py:28
  33.0 0.6 collective-permute-start.8
  33.6 1.4 %fusion.52 = (bf16[512,512]{1,0:T(8,128)(2,1)S(1)}, f32[512,512]{1,0:T(8,128)S(1)}) fusion(bf16[512,512]{1,0:T(8,128)(2,1)S(1)} %maximum_maximum_fusion, bf16[128,512]{1,0:T(8,128)(2,1)S(1)} %collective-permute-done.7, bf16[128,512]{1,0:T(8,128)(2,1)S(1)} %collective-permute-done.6, bf16[128,512]{1,0:T(8,128)(2,1)} %collective-permute-done.5, ...), kind=kOutput, calls=%fused_computation.137 | convolution fusion | flops 270794752 | bytes 2621440 | tf_op jit(solution)/shard_map/dot_general | solution.py:49
  35.0 1.1 %collective-permute-start.12 = (bf16[1024,128]{1,0:T(8,128)(2,1)S(1)}, bf16[1024,128]{1,0:T(8,128)(2,1)S(1)}, u32[]{:S(2)}, u32[]{:S(2)}) collective-permute-start(bf16[1024,128]{1,0:T(8,128)(2,1)S(1)} %pad_maximum_fusion.2), channel_id=1, source_target_pairs={{0,8},{2,10},{4,12},{6,14},{8,0},{10,2},{12,4},{14,6},{16,24},{18,... | collective-permute-start | bytes 786440 | tf_op jit(solution)/shard_map/ppermute | solution.py:32
  36.1 1.0 %collective-permute-done.10 = bf16[128,512]{1,0:T(8,128)(2,1)S(1)} collective-permute-done((bf16[128,512]{1,0:T(8,128)(2,1)S(1)}, bf16[128,512]{1,0:T(8,128)(2,1)S(1)}, u32[]{:S(2)}, u32[]{:S(2)}) %collective-permute-start.10) | collective-permute-done | bytes 131104 | tf_op jit(solution)/shard_map/ppermute | solution.py:28
  37.2 2.0 %collective-permute-done.9 = bf16[128,512]{1,0:T(8,128)(2,1)S(1)} collective-permute-done((bf16[128,512]{1,0:T(8,128)(2,1)S(1)}, bf16[128,512]{1,0:T(8,128)(2,1)S(1)}, u32[]{:S(2)}, u32[]{:S(2)}) %collective-permute-start.9) | collective-permute-done | bytes 131104 | tf_op jit(solution)/shard_map/ppermute | solution.py:28
  39.4 3.3 %collective-permute-done.12 = bf16[1024,128]{1,0:T(8,128)(2,1)S(1)} collective-permute-done((bf16[1024,128]{1,0:T(8,128)(2,1)S(1)}, bf16[1024,128]{1,0:T(8,128)(2,1)S(1)}, u32[]{:S(2)}, u32[]{:S(2)}) %collective-permute-start.12) | collective-permute-done | bytes 262176 | tf_op jit(solution)/shard_map/ppermute | solution.py:32
  42.7 3.7 %collective-permute-start.14 = (bf16[512,128]{1,0:T(8,128)(2,1)S(1)}, bf16[512,128]{1,0:T(8,128)(2,1)S(1)}, u32[]{:S(2)}, u32[]{:S(2)}) collective-permute-start(bf16[512,128]{1,0:T(8,128)(2,1)S(1)} %fusion.11), channel_id=1, source_target_pairs={{0,16},{2,18},{4,20},{6,22},{8,24},{10,26},{12,28},{14,30},{16,0},... | collective-permute-start | bytes 393224 | tf_op jit(solution)/shard_map/ppermute | solution.py:32
  46.4 1.6 %collective-permute-start.11 = (bf16[1024,128]{1,0:T(8,128)(2,1)S(1)}, bf16[1024,128]{1,0:T(8,128)(2,1)S(1)}, u32[]{:S(2)}, u32[]{:S(2)}) collective-permute-start(bf16[1024,128]{1,0:T(8,128)(2,1)S(1)} %pad_maximum_fusion.1), channel_id=1, source_target_pairs={{0,2},{2,0},{4,6},{6,4},{8,10},{10,8},{12,14},{14,12},{16,18},{18,... | collective-permute-start | bytes 786440 | tf_op jit(solution)/shard_map/ppermute | solution.py:28
  48.0 2.0 %all_gather.12 = bf16[256,512]{1,0:T(8,128)(2,1)S(1)} all-gather(bf16[128,512]{1,0:T(8,128)(2,1)S(1)} %fusion.14), channel_id=1, replica_groups=mesh['blk'=16,'rep'=2] {'rep'}, dimensions={0}, use_global_device_ids=true | all-gather | bytes 393216 | tf_op jit(solution)/shard_map/all_gather | solution.py:123
  50.0 0.9 %collective-permute-done.14 = bf16[512,128]{1,0:T(8,128)(2,1)S(1)} collective-permute-done((bf16[512,128]{1,0:T(8,128)(2,1)S(1)}, bf16[512,128]{1,0:T(8,128)(2,1)S(1)}, u32[]{:S(2)}, u32[]{:S(2)}) %collective-permute-start.14) | collective-permute-done | bytes 131104 | tf_op jit(solution)/shard_map/ppermute | solution.py:32
  50.9 1.2 %fusion = bf16[256,512]{1,0:T(8,128)(2,1)S(1)} fusion(bf16[256,512]{1,0:T(8,128)(2,1)S(1)} %all_gather.12, f32[512]{0:T(512)S(1)} %bitcast.134, bf16[128,512]{1,0:T(8,128)(2,1)S(1)} %collective-permute-done.7, bf16[128,512]{1,0:T(8,128)(2,1)S(1)} %copy-done.5, bf16[128,512]{1,0:T(8,128)(2,1)} %collective-permute-done.5, ...), kind=kOutput, calls=%fused_computation.2 | convolution fusion | flops 136577024 | bytes 1050624 | tf_op jit(solution)/shard_map/dot_general | solution.py:49
  52.2 0.7 %collective-permute-done.11 = bf16[1024,128]{1,0:T(8,128)(2,1)S(1)} collective-permute-done((bf16[1024,128]{1,0:T(8,128)(2,1)S(1)}, bf16[1024,128]{1,0:T(8,128)(2,1)S(1)}, u32[]{:S(2)}, u32[]{:S(2)}) %collective-permute-start.11) | collective-permute-done | bytes 262176 | tf_op jit(solution)/shard_map/ppermute | solution.py:28
  52.9 1.3 %collective-permute-start.13 = (bf16[512,128]{1,0:T(8,128)(2,1)S(1)}, bf16[512,128]{1,0:T(8,128)(2,1)S(1)}, u32[]{:S(2)}, u32[]{:S(2)}) collective-permute-start(bf16[512,128]{1,0:T(8,128)(2,1)S(1)} %fusion.15), channel_id=1, source_target_pairs={{0,4},{2,6},{4,0},{6,2},{8,12},{10,14},{12,8},{14,10},{16,20},{18,... | collective-permute-start | bytes 393224 | tf_op jit(solution)/shard_map/ppermute | solution.py:28
  54.2 2.0 %collective-permute-start.17 = (bf16[64,512]{1,0:T(8,128)(2,1)S(1)}, bf16[64,512]{1,0:T(8,128)(2,1)S(1)}, u32[]{:S(2)}, u32[]{:S(2)}) collective-permute-start(bf16[64,512]{1,0:T(8,128)(2,1)S(1)} %get-tuple-element.33), channel_id=1, source_target_pairs={{0,24},{2,26},{4,28},{6,30},{8,16},{10,18},{12,20},{14,22},{16,8},... | collective-permute-start | bytes 196616 | tf_op jit(solution)/shard_map/ppermute | solution.py:32
  56.2 2.5 %collective-permute-start.15 = (bf16[64,512]{1,0:T(8,128)(2,1)S(1)}, bf16[64,512]{1,0:T(8,128)(2,1)S(1)}, u32[]{:S(2)}, u32[]{:S(2)}) collective-permute-start(bf16[64,512]{1,0:T(8,128)(2,1)S(1)} %get-tuple-element.32), channel_id=1, source_target_pairs={{0,8},{2,10},{4,12},{6,14},{8,0},{10,2},{12,4},{14,6},{16,24},{18,... | collective-permute-start | bytes 196616 | tf_op jit(solution)/shard_map/ppermute | solution.py:32
  58.8 2.2 %all_gather.13 = bf16[2,1024,128]{2,1,0:T(8,128)(2,1)S(1)} all-gather(bf16[1,1024,128]{2,1,0:T(8,128)(2,1)S(1)} %pad_maximum_fusion.3), channel_id=1, replica_groups=mesh['blk'=16,'rep'=2] {'rep'}, dimensions={0}, use_global_device_ids=true | all-gather | bytes 786432 | tf_op jit(solution)/shard_map/all_gather | solution.py:137
  61.4 1.2 %fusion.1 = bf16[128,512]{1,0:T(8,128)(2,1)} fusion(bf16[1024,128]{1,0:T(8,128)(2,1)S(1)} %bitcast.123, bf16[1024,1024]{1,0:T(8,128)(2,1)S(1)} %copy-done, s32[]{:T(128)S(6)} %select_n.198, bf16[128,1024]{1,0:T(8,128)(2,1)S(1)} %copy-done.1), kind=kOutput, calls=%fused_computation.5 | convolution fusion | flops 134545408 | bytes 1573888 | tf_op jit(solution)/shard_map/dot_general | solution.py:49
  62.5 0.7 %fusion.20 = f32[64,512]{1,0:T(8,128)} fusion(bf16[64,512]{1,0:T(8,128)(2,1)S(1)} %collective-permute-done.17, bf16[64,512]{1,0:T(8,128)(2,1)S(1)} %collective-permute-done.16, bf16[64,512]{1,0:T(8,128)(2,1)S(1)} %collective-permute-done.15, f32[512]{0:T(512)S(1)} %bitcast.133, bf16[4,64,512]{2,1,0:T(8,128)(2,1)S(1)} %bitcast.129, s32[]{:T(128)S(6)} %select_n.255), kind=kLoop, calls=%fused_computation.43 | loop fusion | flops 262144 | bytes 395268 | tf_op jit(solution)/shard_map/add | solution.py:57
  (73 shorter events, 4.2 us)
Async XLA Ops:
  0.6 60.3 %copy-start = (bf16[1024,1024]{1,0:T(8,128)(2,1)S(1)}, bf16[1024,1024]{1,0:T(8,128)(2,1)}, u32[]{:S(2)}) copy-start(bf16[1024,1024]{1,0:T(8,128)(2,1)} %param.8) | copy-start | bytes 6291460
  0.6 17.0 %copy-start.3 = (bf16[128,1024]{1,0:T(8,128)(2,1)S(1)}, bf16[128,1024]{1,0:T(8,128)(2,1)}, u32[]{:S(2)}) copy-start(bf16[128,1024]{1,0:T(8,128)(2,1)} %param.9) | copy-start | bytes 786436
  2.7 8.6 %collective-permute-start.3 = (bf16[2,128,128]{2,1,0:T(8,128)(2,1)S(1)}, bf16[2,128,128]{2,1,0:T(8,128)(2,1)S(1)}, u32[]{:S(2)}, u32[]{:S(2)}) collective-permute-start(bf16[2,128,128]{2,1,0:T(8,128)(2,1)S(1)} %get-tuple-element.38), channel_id=1, source_target_pairs={{0,6},{2,4},{4,2},{6,0},{8,14},{10,12},{12,10},{14,8},{16,22},{18,... | collective-permute-start | bytes 196616 | tf_op jit(solution)/shard_map/ppermute | solution.py:28
  6.7 4.6 %collective-permute-start.2 = (bf16[2,128,128]{2,1,0:T(8,128)(2,1)S(1)}, bf16[2,128,128]{2,1,0:T(8,128)(2,1)S(1)}, u32[]{:S(2)}, u32[]{:S(2)}) collective-permute-start(bf16[2,128,128]{2,1,0:T(8,128)(2,1)S(1)} %get-tuple-element.39), channel_id=1, source_target_pairs={{0,4},{2,6},{4,0},{6,2},{8,12},{10,14},{12,8},{14,10},{16,20},{18,... | collective-permute-start | bytes 196616 | tf_op jit(solution)/shard_map/ppermute | solution.py:28
  7.2 4.3 %collective-permute-start.1 = (bf16[2,128,128]{2,1,0:T(8,128)(2,1)S(1)}, bf16[2,128,128]{2,1,0:T(8,128)(2,1)S(1)}, u32[]{:S(2)}, u32[]{:S(2)}) collective-permute-start(bf16[2,128,128]{2,1,0:T(8,128)(2,1)S(1)} %get-tuple-element.40), channel_id=1, source_target_pairs={{0,2},{2,0},{4,6},{6,4},{8,10},{10,8},{12,14},{14,12},{16,18},{18,... | collective-permute-start | bytes 196616 | tf_op jit(solution)/shard_map/ppermute | solution.py:28
  8.2 8.5 %collective-permute-start = (bf16[128,512]{1,0:T(8,128)(2,1)S(1)}, bf16[128,512]{1,0:T(8,128)(2,1)S(1)}, u32[]{:S(2)}, u32[]{:S(2)}) collective-permute-start(bf16[128,512]{1,0:T(8,128)(2,1)S(1)} %dynamic-slice_maximum_fusion), channel_id=1, source_target_pairs={{0,16},{2,18},{4,20},{6,22},{8,24},{10,26},{12,28},{14,30},{16,0},... | collective-permute-start | bytes 393224 | tf_op jit(solution)/shard_map/ppermute | solution.py:32
  16.8 9.3 %collective-permute-start.4 = (bf16[256,512]{1,0:T(8,128)(2,1)S(1)}, bf16[256,512]{1,0:T(8,128)(2,1)S(1)}, u32[]{:S(2)}, u32[]{:S(2)}) collective-permute-start(bf16[256,512]{1,0:T(8,128)(2,1)S(1)} %maximum_add_fusion), channel_id=1, source_target_pairs={{0,8},{2,10},{4,12},{6,14},{8,0},{10,2},{12,4},{14,6},{16,24},{18,... | collective-permute-start | bytes 786440 | tf_op jit(solution)/shard_map/ppermute | solution.py:32
  17.7 6.8 %collective-permute-start.7 = (bf16[128,512]{1,0:T(8,128)(2,1)S(1)}, bf16[128,512]{1,0:T(8,128)(2,1)S(1)}, u32[]{:S(2)}, u32[]{:S(2)}) collective-permute-start(bf16[128,512]{1,0:T(8,128)(2,1)S(1)} %dynamic-slice_add_fusion), channel_id=1, source_target_pairs={{0,6},{2,4},{4,2},{6,0},{8,14},{10,12},{12,10},{14,8},{16,22},{18,... | collective-permute-start | bytes 393224 | tf_op jit(solution)/shard_map/ppermute | solution.py:28
  20.2 5.8 %collective-permute-start.6 = (bf16[128,512]{1,0:T(8,128)(2,1)S(1)}, bf16[128,512]{1,0:T(8,128)(2,1)S(1)}, u32[]{:S(2)}, u32[]{:S(2)}) collective-permute-start(bf16[128,512]{1,0:T(8,128)(2,1)S(1)} %dynamic-slice_add_fusion), channel_id=1, source_target_pairs={{0,4},{2,6},{4,0},{6,2},{8,12},{10,14},{12,8},{14,10},{16,20},{18,... | collective-permute-start | bytes 393224 | tf_op jit(solution)/shard_map/ppermute | solution.py:28
  20.7 5.4 %collective-permute-start.5 = (bf16[128,512]{1,0:T(8,128)(2,1)S(1)}, bf16[128,512]{1,0:T(8,128)(2,1)}, u32[]{:S(2)}, u32[]{:S(2)}) collective-permute-start(bf16[128,512]{1,0:T(8,128)(2,1)S(1)} %dynamic-slice_add_fusion), channel_id=1, source_target_pairs={{0,2},{2,0},{4,6},{6,4},{8,10},{10,8},{12,14},{14,12},{16,18},{18,... | collective-permute-start | bytes 393224 | tf_op jit(solution)/shard_map/ppermute | solution.py:28
  25.9 7.7 %copy-start.4 = (bf16[128,512]{1,0:T(8,128)(2,1)}, bf16[128,512]{1,0:T(8,128)(2,1)S(1)}, u32[]{:S(2)}) copy-start(bf16[128,512]{1,0:T(8,128)(2,1)S(1)} %collective-permute-done.6) | copy-start | bytes 393220
  29.8 7.3 %collective-permute-start.10 = (bf16[128,512]{1,0:T(8,128)(2,1)S(1)}, bf16[128,512]{1,0:T(8,128)(2,1)S(1)}, u32[]{:S(2)}, u32[]{:S(2)}) collective-permute-start(bf16[128,512]{1,0:T(8,128)(2,1)S(1)} %pad_maximum_fusion.6), channel_id=1, source_target_pairs={{0,6},{2,4},{4,2},{6,0},{8,14},{10,12},{12,10},{14,8},{16,22},{18,... | collective-permute-start | bytes 393224 | tf_op jit(solution)/shard_map/ppermute | solution.py:28
  31.5 7.6 %collective-permute-start.9 = (bf16[128,512]{1,0:T(8,128)(2,1)S(1)}, bf16[128,512]{1,0:T(8,128)(2,1)S(1)}, u32[]{:S(2)}, u32[]{:S(2)}) collective-permute-start(bf16[128,512]{1,0:T(8,128)(2,1)S(1)} %pad_maximum_fusion.5), channel_id=1, source_target_pairs={{0,4},{2,6},{4,0},{6,2},{8,12},{10,14},{12,8},{14,10},{16,20},{18,... | collective-permute-start | bytes 393224 | tf_op jit(solution)/shard_map/ppermute | solution.py:28
  33.0 6.1 %collective-permute-start.8 = (bf16[128,512]{1,0:T(8,128)(2,1)S(1)}, bf16[128,512]{1,0:T(8,128)(2,1)S(1)}, u32[]{:S(2)}, u32[]{:S(2)}) collective-permute-start(bf16[128,512]{1,0:T(8,128)(2,1)S(1)} %pad_maximum_fusion.4), channel_id=1, source_target_pairs={{0,2},{2,0},{4,6},{6,4},{8,10},{10,8},{12,14},{14,12},{16,18},{18,... | collective-permute-start | bytes 393224 | tf_op jit(solution)/shard_map/ppermute | solution.py:28
  35.0 7.6 %collective-permute-start.12 = (bf16[1024,128]{1,0:T(8,128)(2,1)S(1)}, bf16[1024,128]{1,0:T(8,128)(2,1)S(1)}, u32[]{:S(2)}, u32[]{:S(2)}) collective-permute-start(bf16[1024,128]{1,0:T(8,128)(2,1)S(1)} %pad_maximum_fusion.2), channel_id=1, source_target_pairs={{0,8},{2,10},{4,12},{6,14},{8,0},{10,2},{12,4},{14,6},{16,24},{18,... | collective-permute-start | bytes 786440 | tf_op jit(solution)/shard_map/ppermute | solution.py:32
  39.2 11.7 %copy-start.5 = (bf16[128,512]{1,0:T(8,128)(2,1)S(1)}, bf16[128,512]{1,0:T(8,128)(2,1)}, u32[]{:S(2)}) copy-start(bf16[128,512]{1,0:T(8,128)(2,1)} %copy-done.4) | copy-start | bytes 393220
  42.7 8.2 %collective-permute-start.14 = (bf16[512,128]{1,0:T(8,128)(2,1)S(1)}, bf16[512,128]{1,0:T(8,128)(2,1)S(1)}, u32[]{:S(2)}, u32[]{:S(2)}) collective-permute-start(bf16[512,128]{1,0:T(8,128)(2,1)S(1)} %fusion.11), channel_id=1, source_target_pairs={{0,16},{2,18},{4,20},{6,22},{8,24},{10,26},{12,28},{14,30},{16,0},... | collective-permute-start | bytes 393224 | tf_op jit(solution)/shard_map/ppermute | solution.py:32
  46.4 6.4 %collective-permute-start.11 = (bf16[1024,128]{1,0:T(8,128)(2,1)S(1)}, bf16[1024,128]{1,0:T(8,128)(2,1)S(1)}, u32[]{:S(2)}, u32[]{:S(2)}) collective-permute-start(bf16[1024,128]{1,0:T(8,128)(2,1)S(1)} %pad_maximum_fusion.1), channel_id=1, source_target_pairs={{0,2},{2,0},{4,6},{6,4},{8,10},{10,8},{12,14},{14,12},{16,18},{18,... | collective-permute-start | bytes 786440 | tf_op jit(solution)/shard_map/ppermute | solution.py:28
  52.9 5.8 %collective-permute-start.13 = (bf16[512,128]{1,0:T(8,128)(2,1)S(1)}, bf16[512,128]{1,0:T(8,128)(2,1)S(1)}, u32[]{:S(2)}, u32[]{:S(2)}) collective-permute-start(bf16[512,128]{1,0:T(8,128)(2,1)S(1)} %fusion.15), channel_id=1, source_target_pairs={{0,4},{2,6},{4,0},{6,2},{8,12},{10,14},{12,8},{14,10},{16,20},{18,... | collective-permute-start | bytes 393224 | tf_op jit(solution)/shard_map/ppermute | solution.py:28
  54.2 8.3 %collective-permute-start.17 = (bf16[64,512]{1,0:T(8,128)(2,1)S(1)}, bf16[64,512]{1,0:T(8,128)(2,1)S(1)}, u32[]{:S(2)}, u32[]{:S(2)}) collective-permute-start(bf16[64,512]{1,0:T(8,128)(2,1)S(1)} %get-tuple-element.33), channel_id=1, source_target_pairs={{0,24},{2,26},{4,28},{6,30},{8,16},{10,18},{12,20},{14,22},{16,8},... | collective-permute-start | bytes 196616 | tf_op jit(solution)/shard_map/ppermute | solution.py:32
  56.2 6.4 %collective-permute-start.16 = (bf16[64,512]{1,0:T(8,128)(2,1)S(1)}, bf16[64,512]{1,0:T(8,128)(2,1)S(1)}, u32[]{:S(2)}, u32[]{:S(2)}) collective-permute-start(bf16[64,512]{1,0:T(8,128)(2,1)S(1)} %get-tuple-element.34), channel_id=1, source_target_pairs={{0,16},{2,18},{4,20},{6,22},{8,24},{10,26},{12,28},{14,30},{16,0},... | collective-permute-start | bytes 196616 | tf_op jit(solution)/shard_map/ppermute | solution.py:32
  56.2 5.2 %copy-start.1 = (bf16[128,1024]{1,0:T(8,128)(2,1)S(1)}, bf16[128,1024]{1,0:T(8,128)(2,1)}, u32[]{:S(2)}) copy-start(bf16[128,1024]{1,0:T(8,128)(2,1)} %param.5) | copy-start | bytes 786436
  56.2 6.4 %collective-permute-start.15 = (bf16[64,512]{1,0:T(8,128)(2,1)S(1)}, bf16[64,512]{1,0:T(8,128)(2,1)S(1)}, u32[]{:S(2)}, u32[]{:S(2)}) collective-permute-start(bf16[64,512]{1,0:T(8,128)(2,1)S(1)} %get-tuple-element.32), channel_id=1, source_target_pairs={{0,8},{2,10},{4,12},{6,14},{8,0},{10,2},{12,4},{14,6},{16,24},{18,... | collective-permute-start | bytes 196616 | tf_op jit(solution)/shard_map/ppermute | solution.py:32
  61.3 1.9 %copy-start.2 = (bf16[128,512]{1,0:T(8,128)(2,1)}, bf16[128,512]{1,0:T(8,128)(2,1)S(1)}, u32[]{:S(2)}) copy-start(bf16[128,512]{1,0:T(8,128)(2,1)S(1)} %convolution_convert_fusion.1) | copy-start | bytes 393220

commit v12 on v11

--- a/solution.py
+++ b/solution.py
@@ -62,6 +62,8 @@
     hidden_part = jnp.maximum(
         lax.dynamic_slice_in_dim(hidden_pre, rep_pos * cols_here, cols_here, 1), 0
     )
+    hidden_stack = [along_outer(hidden_part, e) for e in turns]
+
     columns = adj_cols[0]
     turn_of = (columns & (side - 1)) ^ inner_pos
     level_of = (columns >> bits) ^ outer_pos
@@ -73,22 +75,13 @@
     arrived = []
     for t in turns:
         message = ordered[t * per_core : (t + 1) * per_core]
+        if t > 2:
+            message = after(message, hidden_stack[1])
         arrived.append(along_inner(message, t))
-    held = {0: hidden_part}
-    for bit in rising[::-1]:
-        keys = list(held)
-        sent = jnp.concatenate([held[k] for k in keys], 0)
-        got = along_outer(after(sent, *arrived[1:]) if len(keys) > 1 else sent, bit)
-        for n, k in enumerate(keys):
-            held[k ^ bit] = got[n * tile_size : (n + 1) * tile_size]
-    hidden_stack = jnp.concatenate([held[e] for e in turns], 0)
-
+    hidden_stack = jnp.concatenate(hidden_stack, 0)
+    everyone = lax.all_gather(jnp.concatenate(arrived, 0), "rep", axis=0)
     grad_part = lax.dynamic_slice_in_dim(cotangent, rep_pos * cols_here, cols_here, 1)
-    grad_part = after(grad_part, *arrived[1:], held[rising[-1]])
-    grad_stack = [along_inner(grad_part, t) for t in turns]
-    everyone = after(jnp.concatenate(arrived, 0), held[side - 1], *grad_stack[1:])
-    everyone = lax.all_gather(everyone, "rep", axis=0)
-    grad_stack = jnp.concatenate(grad_stack, 0)
+    grad_stack = jnp.concatenate([along_inner(grad_part, t) for t in turns], 0)
 
     rows = []
     for t in turns:
@@ -115,13 +108,13 @@
         chosen = jnp.concatenate([lanes(chosen, u ^ t) for u in turns], 1)
         mixed_cols.append(along_inner(chosen, t))
     mixed_cols = sum(part.astype(jnp.float32) for part in mixed_cols).astype(bf16)
-    back = dot(grad_stack, block, ((0,), (0,)))
-    back = halved([lanes(back, e) for e in turns], along_outer, rising[:-1])
+    back = dot(grad_stack, block, ((0,), (0,))).astype(bf16)
+    back = sum(along_outer(lanes(back, e), e).astype(jnp.float32) for e in turns)
     rows = [lanes(after(mixed, mixed_cols), t) for t in turns]
     rows = halved(rows, along_inner, rising[:-1])
 
     mixed_cols = lax.all_gather(mixed_cols, "rep", axis=0, tiled=True)
-    weight_part = after(dot(mixed_cols, grad_stack, ((1,), (0,))), back[0]).astype(bf16)
+    weight_part = dot(mixed_cols, grad_stack, ((1,), (0,))).astype(bf16)
     by_outer = weight_part.reshape(side, rows_here, cols_here)
     weight_got = [
         along_outer(lax.dynamic_index_in_dim(by_outer, outer_pos ^ t, 0, keepdims=False), t)
@@ -129,10 +122,8 @@
     ]
 
     last = rising[-1]
-    back_got = along_outer(back[last].astype(bf16), last).astype(jnp.float32)
     rows_got = after(rows[last].astype(bf16), weight_part)
-    rows_got = along_inner(rows_got, last).astype(jnp.float32)
-    rows_sum, back = rows[0] + rows_got, back[0] + back_got
+    rows_sum = rows[0] + along_inner(rows_got, last).astype(jnp.float32)
     both = jnp.concatenate([rows_sum, back], 0).astype(bf16)
     both = lax.all_gather(both, "rep", axis=0)
     mixed_rows = both[:, :cols_here].reshape(feature_width, tile_size)
@@ -145,7 +136,7 @@
     pre_part = lax.dynamic_slice_in_dim(hidden_pre, rep_pos * cols_here, cols_here, 1)
     grad_pre = jnp.where(pre_part > 0, grad_in, 0.0).astype(bf16)
 
-    grad_weight = after(sum(part.astype(jnp.float32) for part in weight_got), out_part)
+    grad_weight = sum(part.astype(jnp.float32) for part in weight_got)
     return (out_part, grad_weight, grad_pre)
 
 

time: 63.5 us -> 60.7 us (0.956)
  matrix products: 4.54 us -> 3.39 us
  other arithmetic: 4.18 us -> 3.32 us
    ppermute x11, waiting for transfers between devices: 8.8 us -> 6.14 us  [along_inner(): return lax.ppermute(value, 'blk', pairs) if turn else value]
    ppermute x7 -> x9, waiting for transfers between devices: 9.45 us -> 11.5 us  [along_outer(): return lax.ppermute(value, 'blk', pairs) if turn else value]
    add x8 -> x4, other arithmetic: 1.59 us -> 0.1 us  [after(): return value + row]
    dot_general x5, matrix products: 4.54 us -> 3.39 us  [dot(): lax.dot_general(lhs, rhs, (dims, ((), ())), preferred_element_type=jnp.fl...]
    ppermute x11, starting transfers between devices: 14.7 us -> 13.6 us  [along_inner(): return lax.ppermute(value, 'blk', pairs) if turn else value]
    ppermute x7 -> x9, starting transfers between devices: 13.1 us -> 13.9 us  [along_outer(): return lax.ppermute(value, 'blk', pairs) if turn else value]
    add x0 -> x1, other arithmetic: none -> 0.69 us  [shards(): grad_weight = sum((part.astype(jnp.float32) for part in weight_got))]
  transfers between devices with their start and end apart: 18 -> 20, of which waited for: 10 -> 7; matrix products, arithmetic and copies ran while one was open for 9% -> 7% of each run, Pallas kernels for 0% -> 0%
where the time goes in v12:
time: 60.7 us; the launch traced here: 60.5 us
  starting transfers between devices  27.6 us (45%)
  waiting for transfers between devices  17.6 us (29%)
  blocking collectives  6.36 us (10%)
  matrix products  3.39 us (6%)
  other arithmetic  3.32 us (5%)
  local copies, waits for them, and re-layouts  1.19 us (2%)
  between operations  0.95 us (2%)
    ppermute x9, starting transfers between devices, along_outer(): return lax.ppermute(value, 'blk', pairs) if turn else value  13.9 us
    ppermute x11, starting transfers between devices, along_inner(): return lax.ppermute(value, 'blk', pairs) if turn else value  13.6 us
    ppermute x9, waiting for transfers between devices, along_outer(): return lax.ppermute(value, 'blk', pairs) if turn else value  11.5 us
    ppermute x11, waiting for transfers between devices, along_inner(): return lax.ppermute(value, 'blk', pairs) if turn else value  6.14 us
    dot_general x5, matrix products, dot(): lax.dot_general(lhs, rhs, (dims, ((), ())), preferred_element_type=jnp.fl...  3.39 us
    all_gather x1, blocking collectives, shards(): everyone = lax.all_gather(jnp.concatenate(arrived, 0), 'rep', axis=0)  2.18 us
    all_gather x1, blocking collectives, shards(): both = lax.all_gather(both, 'rep', axis=0)  2.18 us
    all_gather x1, blocking collectives, shards(): mixed_cols = lax.all_gather(mixed_cols, 'rep', axis=0, tiled=True)  1.99 us
  transfers between devices with their start and end apart: 20, of which 7 were waited for; matrix products, arithmetic and copies ran while one was open for 7% of the time, Pallas kernels for 0%

profile of v12, /device:TPU:0, one launch (start us, length us, event | category | flops | bytes accessed | tf_op | source)
XLA Modules:
  0.0 60.5 jit_solution(10270294427671471700)
XLA Ops:
  0.7 1.1 %dynamic-slice_maximum_fusion = bf16[128,512]{1,0:T(8,128)(2,1)S(1)} fusion(bf16[128,1024]{1,0:T(8,128)(2,1)} %param.5, s32[]{:T(128)S(6)} %select_n.198), kind=kLoop, calls=%fused_computation.38 | loop fusion | flops 262144 | bytes 262148 | tf_op jit(solution)/shard_map/max | solution.py:62
  1.8 5.1 %collective-permute-start.2 = (bf16[128,512]{1,0:T(8,128)(2,1)S(1)}, bf16[128,512]{1,0:T(8,128)(2,1)S(1)}, u32[]{:S(2)}, u32[]{:S(2)}) collective-permute-start(bf16[128,512]{1,0:T(8,128)(2,1)S(1)} %dynamic-slice_maximum_fusion), channel_id=1, source_target_pairs={{0,24},{2,26},{4,28},{6,30},{8,16},{10,18},{12,20},{14,22},{16,8},... | collective-permute-start | bytes 393224 | tf_op jit(solution)/shard_map/ppermute | solution.py:32
  6.9 0.6 %collective-permute-start = (bf16[128,512]{1,0:T(8,128)(2,1)S(1)}, bf16[128,512]{1,0:T(8,128)(2,1)S(1)}, u32[]{:S(2)}, u32[]{:S(2)}) collective-permute-start(bf16[128,512]{1,0:T(8,128)(2,1)S(1)} %dynamic-slice_maximum_fusion), channel_id=1, source_target_pairs={{0,8},{2,10},{4,12},{6,14},{8,0},{10,2},{12,4},{14,6},{16,24},{18,... | collective-permute-start | bytes 393224 | tf_op jit(solution)/shard_map/ppermute | solution.py:32
  7.5 0.7 %add_bitcast_fusion = s32[8]{0:T(128)S(1)} fusion(s32[1,8]{1,0:T(1,128)} %param.7, s32[]{:T(128)S(6)} %shift_right_arithmetic.54, s32[]{:T(128)S(6)} %and.60), kind=kLoop, calls=%fused_computation.96 | loop fusion | flops 56 | bytes 72 | tf_op jit(solution)/shard_map/eq | solution.py:71
  8.3 0.9 %slice_bitcast_fusion.9 = (bf16[128,128]{1,0:T(8,128)(2,1)S(1)}, bf16[128,128]{1,0:T(8,128)(2,1)S(1)}, bf16[128,128]{1,0:T(8,128)(2,1)S(1)}, bf16[128,128]{1,0:T...) fusion(bf16[1,8,128,128]{3,2,1,0:T(8,128)(2,1)} %param.6), kind=kLoop, calls=%fused_computation.67 | loop fusion | bytes 524288 | tf_op jit(solution)/shard_map/jit(_where)/broadcast_in_dim | solution.py:74
  9.4 5.9 %collective-permute-done = bf16[128,512]{1,0:T(8,128)(2,1)S(1)} collective-permute-done((bf16[128,512]{1,0:T(8,128)(2,1)S(1)}, bf16[128,512]{1,0:T(8,128)(2,1)S(1)}, u32[]{:S(2)}, u32[]{:S(2)}) %collective-permute-start) | collective-permute-done | bytes 131104 | tf_op jit(solution)/shard_map/ppermute | solution.py:32
  15.3 2.5 %collective-permute-start.5 = (bf16[2,128,128]{2,1,0:T(8,128)(2,1)S(1)}, bf16[2,128,128]{2,1,0:T(8,128)(2,1)S(1)}, u32[]{:S(2)}, u32[]{:S(2)}) collective-permute-start(bf16[2,128,128]{2,1,0:T(8,128)(2,1)S(1)} %get-tuple-element.33), channel_id=1, source_target_pairs={{0,6},{2,4},{4,2},{6,0},{8,14},{10,12},{12,10},{14,8},{16,22},{18,... | collective-permute-start | bytes 196616 | tf_op jit(solution)/shard_map/ppermute | solution.py:28
  17.8 0.5 collective-permute-start.4
  18.3 0.5 collective-permute-start.3
  18.9 1.9 %collective-permute-done.5 = bf16[2,128,128]{2,1,0:T(8,128)(2,1)S(1)} collective-permute-done((bf16[2,128,128]{2,1,0:T(8,128)(2,1)S(1)}, bf16[2,128,128]{2,1,0:T(8,128)(2,1)S(1)}, u32[]{:S(2)}, u32[]{:S(2)}) %collective-permute-start.5) | collective-permute-done | bytes 65568 | tf_op jit(solution)/shard_map/ppermute | solution.py:28
  20.8 2.3 %collective-permute-start.12 = (bf16[128,512]{1,0:T(8,128)(2,1)S(1)}, bf16[128,512]{1,0:T(8,128)(2,1)S(1)}, u32[]{:S(2)}, u32[]{:S(2)}) collective-permute-start(bf16[128,512]{1,0:T(8,128)(2,1)S(1)} %constant_dynamic-slice_fusion), channel_id=1, source_target_pairs={{0,6},{2,4},{4,2},{6,0},{8,14},{10,12},{12,10},{14,8},{16,22},{18,... | collective-permute-start | bytes 393224 | tf_op jit(solution)/shard_map/ppermute | solution.py:28
  23.2 0.6 collective-permute-start.11
  23.8 0.5 collective-permute-start.10
  24.4 2.2 %all-gather = bf16[16,128,128]{2,1,0:T(8,128)(2,1)S(1)} all-gather(bf16[8,128,128]{2,1,0:T(8,128)(2,1)S(1)} %pad_maximum_fusion.1), channel_id=2, replica_groups=mesh['blk'=16,'rep'=2] {'rep'}, dimensions={0}, use_global_device_ids=true | all-gather | bytes 786432 | tf_op jit(solution)/shard_map/all_gather | solution.py:82
  26.8 0.5 convolution_convert_fusion.1
  27.4 1.5 %collective-permute-start.7 = (bf16[128,512]{1,0:T(8,128)(2,1)S(1)}, bf16[128,512]{1,0:T(8,128)(2,1)S(1)}, u32[]{:S(2)}, u32[]{:S(2)}) collective-permute-start(bf16[128,512]{1,0:T(8,128)(2,1)S(1)} %pad_maximum_fusion.5), channel_id=1, source_target_pairs={{0,4},{2,6},{4,0},{6,2},{8,12},{10,14},{12,8},{14,10},{16,20},{18,... | collective-permute-start | bytes 393224 | tf_op jit(solution)/shard_map/ppermute | solution.py:28
  28.9 1.6 %collective-permute-start.6 = (bf16[128,512]{1,0:T(8,128)(2,1)S(1)}, bf16[128,512]{1,0:T(8,128)(2,1)S(1)}, u32[]{:S(2)}, u32[]{:S(2)}) collective-permute-start(bf16[128,512]{1,0:T(8,128)(2,1)S(1)} %pad_maximum_fusion.4), channel_id=1, source_target_pairs={{0,2},{2,0},{4,6},{6,4},{8,10},{10,8},{12,14},{14,12},{16,18},{18,... | collective-permute-start | bytes 393224 | tf_op jit(solution)/shard_map/ppermute | solution.py:28
  30.5 0.6 %collective-permute-start.8 = (bf16[128,512]{1,0:T(8,128)(2,1)S(1)}, bf16[128,512]{1,0:T(8,128)(2,1)S(1)}, u32[]{:S(2)}, u32[]{:S(2)}) collective-permute-start(bf16[128,512]{1,0:T(8,128)(2,1)S(1)} %pad_maximum_fusion.6), channel_id=1, source_target_pairs={{0,6},{2,4},{4,2},{6,0},{8,14},{10,12},{12,10},{14,8},{16,22},{18,... | collective-permute-start | bytes 393224 | tf_op jit(solution)/shard_map/ppermute | solution.py:28
  31.7 2.6 %collective-permute-start.14 = (bf16[512,128]{1,0:T(8,128)(2,1)S(1)}, bf16[512,128]{1,0:T(8,128)(2,1)S(1)}, u32[]{:S(2)}, u32[]{:S(2)}) collective-permute-start(bf16[512,128]{1,0:T(8,128)(2,1)S(1)} %get-tuple-element.11), channel_id=1, source_target_pairs={{0,8},{2,10},{4,12},{6,14},{8,0},{10,2},{12,4},{14,6},{16,24},{18,... | collective-permute-start | bytes 393224 | tf_op jit(solution)/shard_map/ppermute | solution.py:32
  34.5 1.3 %collective-permute-start.15 = (bf16[512,128]{1,0:T(8,128)(2,1)S(1)}, bf16[512,128]{1,0:T(8,128)(2,1)S(1)}, u32[]{:S(2)}, u32[]{:S(2)}) collective-permute-start(bf16[512,128]{1,0:T(8,128)(2,1)S(1)} %get-tuple-element.13), channel_id=1, source_target_pairs={{0,16},{2,18},{4,20},{6,22},{8,24},{10,26},{12,28},{14,30},{16,0},... | collective-permute-start | bytes 393224 | tf_op jit(solution)/shard_map/ppermute | solution.py:32
  35.8 1.3 %collective-permute-done.8 = bf16[128,512]{1,0:T(8,128)(2,1)S(1)} collective-permute-done((bf16[128,512]{1,0:T(8,128)(2,1)S(1)}, bf16[128,512]{1,0:T(8,128)(2,1)S(1)}, u32[]{:S(2)}, u32[]{:S(2)}) %collective-permute-start.8) | collective-permute-done | bytes 131104 | tf_op jit(solution)/shard_map/ppermute | solution.py:28
  37.2 2.0 %all_gather.15 = bf16[256,512]{1,0:T(8,128)(2,1)S(1)} all-gather(bf16[128,512]{1,0:T(8,128)(2,1)S(1)} %fusion.12), channel_id=1, replica_groups=mesh['blk'=16,'rep'=2] {'rep'}, dimensions={0}, use_global_device_ids=true | all-gather | bytes 393216 | tf_op jit(solution)/shard_map/all_gather | solution.py:116
  39.6 1.5 %collective-permute-start.9 = (bf16[1024,128]{1,0:T(8,128)(2,1)S(1)}, bf16[1024,128]{1,0:T(8,128)(2,1)S(1)}, u32[]{:S(2)}, u32[]{:S(2)}) collective-permute-start(bf16[1024,128]{1,0:T(8,128)(2,1)S(1)} %pad_maximum_fusion.2), channel_id=1, source_target_pairs={{0,2},{2,0},{4,6},{6,4},{8,10},{10,8},{12,14},{14,12},{16,18},{18,... | collective-permute-start | bytes 786440 | tf_op jit(solution)/shard_map/ppermute | solution.py:28
  41.2 2.6 %collective-permute-start.17 = (bf16[64,512]{1,0:T(8,128)(2,1)S(1)}, bf16[64,512]{1,0:T(8,128)(2,1)S(1)}, u32[]{:S(2)}, u32[]{:S(2)}) collective-permute-start(bf16[64,512]{1,0:T(8,128)(2,1)S(1)} %get-tuple-element.29), channel_id=1, source_target_pairs={{0,8},{2,10},{4,12},{6,14},{8,0},{10,2},{12,4},{14,6},{16,24},{18,... | collective-permute-start | bytes 196616 | tf_op jit(solution)/shard_map/ppermute | solution.py:32
  44.2 1.1 %collective-permute-start.18 = (bf16[64,512]{1,0:T(8,128)(2,1)S(1)}, bf16[64,512]{1,0:T(8,128)(2,1)S(1)}, u32[]{:S(2)}, u32[]{:S(2)}) collective-permute-start(bf16[64,512]{1,0:T(8,128)(2,1)S(1)} %get-tuple-element.31), channel_id=1, source_target_pairs={{0,16},{2,18},{4,20},{6,22},{8,24},{10,26},{12,28},{14,30},{16,0},... | collective-permute-start | bytes 196616 | tf_op jit(solution)/shard_map/ppermute | solution.py:32
  45.3 5.5 %collective-permute-done.15 = bf16[512,128]{1,0:T(8,128)(2,1)S(1)} collective-permute-done((bf16[512,128]{1,0:T(8,128)(2,1)S(1)}, bf16[512,128]{1,0:T(8,128)(2,1)S(1)}, u32[]{:S(2)}, u32[]{:S(2)}) %collective-permute-start.15) | collective-permute-done | bytes 131104 | tf_op jit(solution)/shard_map/ppermute | solution.py:32
  50.9 1.5 %collective-permute-start.13 = (bf16[512,128]{1,0:T(8,128)(2,1)S(1)}, bf16[512,128]{1,0:T(8,128)(2,1)S(1)}, u32[]{:S(2)}, u32[]{:S(2)}) collective-permute-start(bf16[512,128]{1,0:T(8,128)(2,1)S(1)} %fusion.13), channel_id=1, source_target_pairs={{0,4},{2,6},{4,0},{6,2},{8,12},{10,14},{12,8},{14,10},{16,20},{18,... | collective-permute-start | bytes 393224 | tf_op jit(solution)/shard_map/ppermute | solution.py:28
  52.5 0.7 %fusion.17 = f32[64,512]{1,0:T(8,128)} fusion(bf16[64,512]{1,0:T(8,128)(2,1)S(1)} %collective-permute-done.19, bf16[64,512]{1,0:T(8,128)(2,1)S(1)} %collective-permute-done.18, bf16[64,512]{1,0:T(8,128)(2,1)S(1)} %collective-permute-done.17, bf16[4,64,512]{2,1,0:T(8,128)(2,1)S(1)} %bitcast.114, s32[]{:T(128)S(6)} %select_n.255), kind=kLoop, calls=%fused_computation.37 | loop fusion | flops 229376 | bytes 393220 | tf_op jit(solution)/shard_map/add | solution.py:139
  53.2 2.8 %collective-permute-done.13 = bf16[512,128]{1,0:T(8,128)(2,1)S(1)} collective-permute-done((bf16[512,128]{1,0:T(8,128)(2,1)S(1)}, bf16[512,128]{1,0:T(8,128)(2,1)S(1)}, u32[]{:S(2)}, u32[]{:S(2)}) %collective-permute-start.13) | collective-permute-done | bytes 131104 | tf_op jit(solution)/shard_map/ppermute | solution.py:28
  56.1 2.2 %all_gather.16 = bf16[2,1024,128]{2,1,0:T(8,128)(2,1)S(1)} all-gather(bf16[1,1024,128]{2,1,0:T(8,128)(2,1)S(1)} %pad_maximum_fusion.3), channel_id=1, replica_groups=mesh['blk'=16,'rep'=2] {'rep'}, dimensions={0}, use_global_device_ids=true | all-gather | bytes 786432 | tf_op jit(solution)/shard_map/all_gather | solution.py:128
  58.3 1.2 %fusion = bf16[128,512]{1,0:T(8,128)(2,1)} fusion(bf16[1024,128]{1,0:T(8,128)(2,1)S(1)} %bitcast.109, bf16[1024,1024]{1,0:T(8,128)(2,1)S(1)} %copy-done, s32[]{:T(128)S(6)} %select_n.198, bf16[128,1024]{1,0:T(8,128)(2,1)S(1)} %copy-done.1), kind=kOutput, calls=%fused_computation.5 | convolution fusion | flops 134545408 | bytes 1573888 | tf_op jit(solution)/shard_map/dot_general | solution.py:49
  59.5 1.0 %convolution_convert_fusion.3 = bf16[128,512]{1,0:T(8,128)(2,1)} fusion(bf16[1024,128]{1,0:T(8,128)(2,1)S(1)} %bitcast.108, bf16[1024,1024]{1,0:T(8,128)(2,1)S(1)} %copy-done, s32[]{:T(128)S(6)} %select_n.198), kind=kOutput, calls=%fused_computation.4 | convolution fusion | flops 134283264 | bytes 1441796 | tf_op jit(solution)/shard_map/dot_general | solution.py:49
  (59 shorter events, 2.8 us)
Async XLA Ops:
  0.6 57.7 %copy-start = (bf16[1024,1024]{1,0:T(8,128)(2,1)S(1)}, bf16[1024,1024]{1,0:T(8,128)(2,1)}, u32[]{:S(2)}) copy-start(bf16[1024,1024]{1,0:T(8,128)(2,1)} %param.8) | copy-start | bytes 6291460
  0.6 18.2 %copy-start.2 = (bf16[128,1024]{1,0:T(8,128)(2,1)S(1)}, bf16[128,1024]{1,0:T(8,128)(2,1)}, u32[]{:S(2)}) copy-start(bf16[128,1024]{1,0:T(8,128)(2,1)} %param.9) | copy-start | bytes 786436
  1.8 25.0 %collective-permute-start.2 = (bf16[128,512]{1,0:T(8,128)(2,1)S(1)}, bf16[128,512]{1,0:T(8,128)(2,1)S(1)}, u32[]{:S(2)}, u32[]{:S(2)}) collective-permute-start(bf16[128,512]{1,0:T(8,128)(2,1)S(1)} %dynamic-slice_maximum_fusion), channel_id=1, source_target_pairs={{0,24},{2,26},{4,28},{6,30},{8,16},{10,18},{12,20},{14,22},{16,8},... | collective-permute-start | bytes 393224 | tf_op jit(solution)/shard_map/ppermute | solution.py:32
  6.9 19.9 %collective-permute-start.1 = (bf16[128,512]{1,0:T(8,128)(2,1)S(1)}, bf16[128,512]{1,0:T(8,128)(2,1)S(1)}, u32[]{:S(2)}, u32[]{:S(2)}) collective-permute-start(bf16[128,512]{1,0:T(8,128)(2,1)S(1)} %dynamic-slice_maximum_fusion), channel_id=1, source_target_pairs={{0,16},{2,18},{4,20},{6,22},{8,24},{10,26},{12,28},{14,30},{16,0},... | collective-permute-start | bytes 393224 | tf_op jit(solution)/shard_map/ppermute | solution.py:32
  6.9 8.4 %collective-permute-start = (bf16[128,512]{1,0:T(8,128)(2,1)S(1)}, bf16[128,512]{1,0:T(8,128)(2,1)S(1)}, u32[]{:S(2)}, u32[]{:S(2)}) collective-permute-start(bf16[128,512]{1,0:T(8,128)(2,1)S(1)} %dynamic-slice_maximum_fusion), channel_id=1, source_target_pairs={{0,8},{2,10},{4,12},{6,14},{8,0},{10,2},{12,4},{14,6},{16,24},{18,... | collective-permute-start | bytes 393224 | tf_op jit(solution)/shard_map/ppermute | solution.py:32
  15.3 5.5 %collective-permute-start.5 = (bf16[2,128,128]{2,1,0:T(8,128)(2,1)S(1)}, bf16[2,128,128]{2,1,0:T(8,128)(2,1)S(1)}, u32[]{:S(2)}, u32[]{:S(2)}) collective-permute-start(bf16[2,128,128]{2,1,0:T(8,128)(2,1)S(1)} %get-tuple-element.33), channel_id=1, source_target_pairs={{0,6},{2,4},{4,2},{6,0},{8,14},{10,12},{12,10},{14,8},{16,22},{18,... | collective-permute-start | bytes 196616 | tf_op jit(solution)/shard_map/ppermute | solution.py:28
  17.8 5.4 %collective-permute-start.4 = (bf16[2,128,128]{2,1,0:T(8,128)(2,1)S(1)}, bf16[2,128,128]{2,1,0:T(8,128)(2,1)S(1)}, u32[]{:S(2)}, u32[]{:S(2)}) collective-permute-start(bf16[2,128,128]{2,1,0:T(8,128)(2,1)S(1)} %get-tuple-element.34), channel_id=1, source_target_pairs={{0,4},{2,6},{4,0},{6,2},{8,12},{10,14},{12,8},{14,10},{16,20},{18,... | collective-permute-start | bytes 196616 | tf_op jit(solution)/shard_map/ppermute | solution.py:28
  18.3 5.4 %collective-permute-start.3 = (bf16[2,128,128]{2,1,0:T(8,128)(2,1)S(1)}, bf16[2,128,128]{2,1,0:T(8,128)(2,1)S(1)}, u32[]{:S(2)}, u32[]{:S(2)}) collective-permute-start(bf16[2,128,128]{2,1,0:T(8,128)(2,1)S(1)} %get-tuple-element.35), channel_id=1, source_target_pairs={{0,2},{2,0},{4,6},{6,4},{8,10},{10,8},{12,14},{14,12},{16,18},{18,... | collective-permute-start | bytes 196616 | tf_op jit(solution)/shard_map/ppermute | solution.py:28
  20.8 9.7 %collective-permute-start.12 = (bf16[128,512]{1,0:T(8,128)(2,1)S(1)}, bf16[128,512]{1,0:T(8,128)(2,1)S(1)}, u32[]{:S(2)}, u32[]{:S(2)}) collective-permute-start(bf16[128,512]{1,0:T(8,128)(2,1)S(1)} %constant_dynamic-slice_fusion), channel_id=1, source_target_pairs={{0,6},{2,4},{4,2},{6,0},{8,14},{10,12},{12,10},{14,8},{16,22},{18,... | collective-permute-start | bytes 393224 | tf_op jit(solution)/shard_map/ppermute | solution.py:28
  23.2 7.9 %collective-permute-start.11 = (bf16[128,512]{1,0:T(8,128)(2,1)S(1)}, bf16[128,512]{1,0:T(8,128)(2,1)S(1)}, u32[]{:S(2)}, u32[]{:S(2)}) collective-permute-start(bf16[128,512]{1,0:T(8,128)(2,1)S(1)} %constant_dynamic-slice_fusion), channel_id=1, source_target_pairs={{0,4},{2,6},{4,0},{6,2},{8,12},{10,14},{12,8},{14,10},{16,20},{18,... | collective-permute-start | bytes 393224 | tf_op jit(solution)/shard_map/ppermute | solution.py:28
  23.8 7.4 %collective-permute-start.10 = (bf16[128,512]{1,0:T(8,128)(2,1)S(1)}, bf16[128,512]{1,0:T(8,128)(2,1)S(1)}, u32[]{:S(2)}, u32[]{:S(2)}) collective-permute-start(bf16[128,512]{1,0:T(8,128)(2,1)S(1)} %constant_dynamic-slice_fusion), channel_id=1, source_target_pairs={{0,2},{2,0},{4,6},{6,4},{8,10},{10,8},{12,14},{14,12},{16,18},{18,... | collective-permute-start | bytes 393224 | tf_op jit(solution)/shard_map/ppermute | solution.py:28
  27.4 7.0 %collective-permute-start.7 = (bf16[128,512]{1,0:T(8,128)(2,1)S(1)}, bf16[128,512]{1,0:T(8,128)(2,1)S(1)}, u32[]{:S(2)}, u32[]{:S(2)}) collective-permute-start(bf16[128,512]{1,0:T(8,128)(2,1)S(1)} %pad_maximum_fusion.5), channel_id=1, source_target_pairs={{0,4},{2,6},{4,0},{6,2},{8,12},{10,14},{12,8},{14,10},{16,20},{18,... | collective-permute-start | bytes 393224 | tf_op jit(solution)/shard_map/ppermute | solution.py:28
  28.9 6.9 %collective-permute-start.6 = (bf16[128,512]{1,0:T(8,128)(2,1)S(1)}, bf16[128,512]{1,0:T(8,128)(2,1)S(1)}, u32[]{:S(2)}, u32[]{:S(2)}) collective-permute-start(bf16[128,512]{1,0:T(8,128)(2,1)S(1)} %pad_maximum_fusion.4), channel_id=1, source_target_pairs={{0,2},{2,0},{4,6},{6,4},{8,10},{10,8},{12,14},{14,12},{16,18},{18,... | collective-permute-start | bytes 393224 | tf_op jit(solution)/shard_map/ppermute | solution.py:28
  30.5 6.6 %collective-permute-start.8 = (bf16[128,512]{1,0:T(8,128)(2,1)S(1)}, bf16[128,512]{1,0:T(8,128)(2,1)S(1)}, u32[]{:S(2)}, u32[]{:S(2)}) collective-permute-start(bf16[128,512]{1,0:T(8,128)(2,1)S(1)} %pad_maximum_fusion.6), channel_id=1, source_target_pairs={{0,6},{2,4},{4,2},{6,0},{8,14},{10,12},{12,10},{14,8},{16,22},{18,... | collective-permute-start | bytes 393224 | tf_op jit(solution)/shard_map/ppermute | solution.py:28
  31.7 12.0 %collective-permute-start.14 = (bf16[512,128]{1,0:T(8,128)(2,1)S(1)}, bf16[512,128]{1,0:T(8,128)(2,1)S(1)}, u32[]{:S(2)}, u32[]{:S(2)}) collective-permute-start(bf16[512,128]{1,0:T(8,128)(2,1)S(1)} %get-tuple-element.11), channel_id=1, source_target_pairs={{0,8},{2,10},{4,12},{6,14},{8,0},{10,2},{12,4},{14,6},{16,24},{18,... | collective-permute-start | bytes 393224 | tf_op jit(solution)/shard_map/ppermute | solution.py:32
  34.3 9.9 %collective-permute-start.16 = (bf16[512,128]{1,0:T(8,128)(2,1)S(1)}, bf16[512,128]{1,0:T(8,128)(2,1)S(1)}, u32[]{:S(2)}, u32[]{:S(2)}) collective-permute-start(bf16[512,128]{1,0:T(8,128)(2,1)S(1)} %get-tuple-element.12), channel_id=1, source_target_pairs={{0,24},{2,26},{4,28},{6,30},{8,16},{10,18},{12,20},{14,22},{16,8},... | collective-permute-start | bytes 393224 | tf_op jit(solution)/shard_map/ppermute | solution.py:32
  34.5 16.3 %collective-permute-start.15 = (bf16[512,128]{1,0:T(8,128)(2,1)S(1)}, bf16[512,128]{1,0:T(8,128)(2,1)S(1)}, u32[]{:S(2)}, u32[]{:S(2)}) collective-permute-start(bf16[512,128]{1,0:T(8,128)(2,1)S(1)} %get-tuple-element.13), channel_id=1, source_target_pairs={{0,16},{2,18},{4,20},{6,22},{8,24},{10,26},{12,28},{14,30},{16,0},... | collective-permute-start | bytes 393224 | tf_op jit(solution)/shard_map/ppermute | solution.py:32
  39.6 11.3 %collective-permute-start.9 = (bf16[1024,128]{1,0:T(8,128)(2,1)S(1)}, bf16[1024,128]{1,0:T(8,128)(2,1)S(1)}, u32[]{:S(2)}, u32[]{:S(2)}) collective-permute-start(bf16[1024,128]{1,0:T(8,128)(2,1)S(1)} %pad_maximum_fusion.2), channel_id=1, source_target_pairs={{0,2},{2,0},{4,6},{6,4},{8,10},{10,8},{12,14},{14,12},{16,18},{18,... | collective-permute-start | bytes 786440 | tf_op jit(solution)/shard_map/ppermute | solution.py:28
  41.2 11.3 %collective-permute-start.17 = (bf16[64,512]{1,0:T(8,128)(2,1)S(1)}, bf16[64,512]{1,0:T(8,128)(2,1)S(1)}, u32[]{:S(2)}, u32[]{:S(2)}) collective-permute-start(bf16[64,512]{1,0:T(8,128)(2,1)S(1)} %get-tuple-element.29), channel_id=1, source_target_pairs={{0,8},{2,10},{4,12},{6,14},{8,0},{10,2},{12,4},{14,6},{16,24},{18,... | collective-permute-start | bytes 196616 | tf_op jit(solution)/shard_map/ppermute | solution.py:32
  43.7 8.7 %collective-permute-start.19 = (bf16[64,512]{1,0:T(8,128)(2,1)S(1)}, bf16[64,512]{1,0:T(8,128)(2,1)S(1)}, u32[]{:S(2)}, u32[]{:S(2)}) collective-permute-start(bf16[64,512]{1,0:T(8,128)(2,1)S(1)} %get-tuple-element.30), channel_id=1, source_target_pairs={{0,24},{2,26},{4,28},{6,30},{8,16},{10,18},{12,20},{14,22},{16,8},... | collective-permute-start | bytes 196616 | tf_op jit(solution)/shard_map/ppermute | solution.py:32
  44.2 14.1 %copy-start.1 = (bf16[128,1024]{1,0:T(8,128)(2,1)S(1)}, bf16[128,1024]{1,0:T(8,128)(2,1)}, u32[]{:S(2)}) copy-start(bf16[128,1024]{1,0:T(8,128)(2,1)} %param.5) | copy-start | bytes 786436
  44.2 8.3 %collective-permute-start.18 = (bf16[64,512]{1,0:T(8,128)(2,1)S(1)}, bf16[64,512]{1,0:T(8,128)(2,1)S(1)}, u32[]{:S(2)}, u32[]{:S(2)}) collective-permute-start(bf16[64,512]{1,0:T(8,128)(2,1)S(1)} %get-tuple-element.31), channel_id=1, source_target_pairs={{0,16},{2,18},{4,20},{6,22},{8,24},{10,26},{12,28},{14,30},{16,0},... | collective-permute-start | bytes 196616 | tf_op jit(solution)/shard_map/ppermute | solution.py:32
  50.9 5.0 %collective-permute-start.13 = (bf16[512,128]{1,0:T(8,128)(2,1)S(1)}, bf16[512,128]{1,0:T(8,128)(2,1)S(1)}, u32[]{:S(2)}, u32[]{:S(2)}) collective-permute-start(bf16[512,128]{1,0:T(8,128)(2,1)S(1)} %fusion.13), channel_id=1, source_target_pairs={{0,4},{2,6},{4,0},{6,2},{8,12},{10,14},{12,8},{14,10},{16,20},{18,... | collective-permute-start | bytes 393224 | tf_op jit(solution)/shard_map/ppermute | solution.py:28

commit v13 on v7

v13 whole, which is shorter than its diff:
```python
import jax
import jax.numpy as jnp
from jax import lax
from jax.sharding import PartitionSpec as P


def shards(hidden_pre, adj_vals, adj_cols, w_out, cotangent):
    feature_width = hidden_pre.shape[1]
    slots, tile_size = adj_vals.shape[1:3]
    blk_count = lax.axis_size("blk")
    rep_count = lax.axis_size("rep")
    section_span = blk_count // rep_count
    bits = (blk_count.bit_length() - 1) // 2
    side = 1 << bits
    per_core = section_span // side
    blk_pos = lax.axis_index("blk")
    rep_pos = lax.axis_index("rep")
    outer_pos, inner_pos = blk_pos >> bits, blk_pos & (side - 1)
    span_bits = section_span.bit_length() - 1
    cols_here = feature_width // rep_count
    rows_here = feature_width // blk_count
    lane_blocks = cols_here // tile_size
    bf16 = jnp.bfloat16
    turns = range(side)
    rising = [1 << b for b in range(bits)]

    def along_inner(value, turn):
        pairs = [(o * side + i, o * side + (i ^ turn)) for o in turns for i in turns]
        return lax.ppermute(value, "blk", pairs) if turn else value

    def along_outer(value, turn):
        pairs = [(o * side + i, (o ^ turn) * side + i) for o in turns for i in turns]
        return lax.ppermute(value, "blk", pairs) if turn else value

    def from_two(value, turn, outer):
        pairs = []
        for o in turns:
            for i in turns:
                for r in range(2):
                    there = (o ^ (turn + r)) * side + i if outer else o * side + (i ^ (turn + r))
                    pairs.append(((o * side + i) * 2 + r, there * 2 + r))
        return lax.ppermute(value, ("blk", "rep"), pairs)

    def halved(parts, move):
        parts = dict(enumerate(parts))
        size = parts[0].shape[0]
        for bit in rising:
            keys = [k for k in parts if not k & bit]
            sent = jnp.concatenate([parts[k ^ bit].astype(bf16) for k in keys], 0)
            got = move(sent, bit)
            parts = {
                k: parts[k].astype(jnp.float32)
                + got[n * size : (n + 1) * size].astype(jnp.float32)
                for n, k in enumerate(keys)
            }
        return parts[0]

    def dot(lhs, rhs, dims):
        return lax.dot_general(lhs, rhs, (dims, ((), ())), preferred_element_type=jnp.float32)

    def lanes(value, index):
        return value[:, index * tile_size : (index + 1) * tile_size]

    def columns_of(value, index):
        return lax.dynamic_slice_in_dim(value, index * cols_here, cols_here, 1)

    pair_up = rep_count == 2
    direct = turns[1:2] if pair_up else turns[1:]
    hidden_far = [from_two(hidden_pre, t, True) for t in turns[2::2]] if pair_up else []
    hidden_part = jnp.maximum(columns_of(hidden_pre, rep_pos), 0)
    hidden_stack = [hidden_part] + [along_outer(hidden_part, t) for t in direct]

    columns = adj_cols[0]
    turn_of = (columns & (side - 1)) ^ inner_pos
    level_of = (columns >> bits) ^ outer_pos
    place = turn_of * per_core + (level_of & (per_core - 1))
    hit = place[None, :] == jnp.arange(section_span, dtype=jnp.int32)[:, None]
    ordered = jnp.zeros((section_span, tile_size, tile_size), bf16)
    for k in range(slots):
        ordered = jnp.where(hit[:, k, None, None], adj_vals[0, k][None], ordered)
    swapped = [
        along_inner(ordered[t * per_core : (t + 1) * per_core], t) for t in turns
    ]

    grad_far = [from_two(cotangent, t, False) for t in turns[2::2]] if pair_up else []
    grad_part = columns_of(cotangent, rep_pos)
    grad_stack = [grad_part] + [along_inner(grad_part, t) for t in direct]

    for far in hidden_far + grad_far:
        other = columns_of(far, 1 - rep_pos)
        swapped.append(jnp.stack([lanes(other, n) for n in range(lane_blocks)]))
    everyone = lax.all_gather(jnp.concatenate(swapped, 0), "rep", axis=0)

    for index, far in enumerate(hidden_far + grad_far):
        mine = columns_of(far, rep_pos)
        start = section_span + index * lane_blocks
        both = everyone[:, start : start + lane_blocks]
        other = jnp.where(rep_pos == 0, both[1], both[0])
        other = jnp.concatenate([other[n] for n in range(lane_blocks)], 1)
        blocks = [jnp.where(rep_pos == 0, mine, other), jnp.where(rep_pos == 0, other, mine)]
        if index < len(hidden_far):
            hidden_stack.extend(jnp.maximum(part, 0) for part in blocks)
        else:
            grad_stack.extend(blocks)
    hidden_stack = jnp.concatenate(hidden_stack, 0)
    grad_stack = jnp.concatenate(grad_stack, 0)

    rows = []
    for t in turns:
        row_block = outer_pos * side + (inner_pos ^ t)
        row = []
        for e in turns:
            column_block = (outer_pos ^ e) * side + inner_pos
            holder = ((row_block - column_block) & (blk_count - 1)) >> span_bits
            index = t * per_core + e % per_core
            piece = everyone[0, index]
            for r in range(1, rep_count):
                piece = jnp.where(holder == r, everyone[r, index], piece)
            row.append(piece)
        rows.append(jnp.concatenate(row, 1))
    block = jnp.concatenate(rows, 0)

    mixed = dot(hidden_stack, block, ((0,), (1,))).astype(bf16)
    share = cols_here // side
    by_owner = mixed.reshape(share // rows_here, side, rows_here, side * tile_size)
    mixed_cols = 0.0
    for t in turns:
        chosen = lax.dynamic_index_in_dim(by_owner, inner_pos ^ t, 1, keepdims=False)
        chosen = chosen.reshape(share, side * tile_size)
        chosen = jnp.concatenate([lanes(chosen, u ^ t) for u in turns], 1)
        mixed_cols = mixed_cols + along_inner(chosen, t).astype(jnp.float32)

    back = dot(grad_stack, block, ((0,), (0,)))
    back = halved([lanes(back, e) for e in turns], along_outer).astype(bf16)

    mixed_cols = lax.all_gather(mixed_cols.astype(bf16), "rep", axis=0, tiled=True)
    weight_part = dot(mixed_cols, grad_stack, ((1,), (0,))).astype(bf16)
    by_outer = weight_part.reshape(side, rows_here, cols_here)
    grad_weight = sum(
        along_outer(
            lax.dynamic_index_in_dim(by_outer, outer_pos ^ t, 0, keepdims=False), t
        ).astype(jnp.float32)
        for t in turns
    )

    w_share = w_out.reshape(side, side, rows_here, feature_width)
    w_share = lax.dynamic_index_in_dim(w_share, inner_pos, 1, keepdims=False)
    w_share = columns_of(w_share.reshape(side * rows_here, feature_width), rep_pos)
    out_part = dot(mixed_cols, w_share, ((0,), (0,)))
    out_part = halved(
        [out_part[t * tile_size : (t + 1) * tile_size] for t in turns], along_inner
    ).astype(bf16)

    back_full = lax.all_gather(back, "rep", axis=0, tiled=True)
    w_rows = lax.dynamic_slice_in_dim(w_out, rep_pos * cols_here, cols_here, 0)
    grad_in = dot(back_full, w_rows, ((0,), (1,)))
    pre_part = columns_of(hidden_pre, rep_pos)
    grad_pre = jnp.where(pre_part > 0, grad_in, 0.0).astype(bf16)
    return (out_part, grad_weight, grad_pre)


def solution(mesh):
    placed = (P("blk", None), P("blk", "rep", None, None), P("blk", "rep"), P(), P("blk", None))
    return jax.shard_map(
        shards,
        mesh=mesh,
        in_specs=placed,
        out_specs=(P("blk", "rep"), P("blk", "rep"), P("blk", "rep")),
        check_vma=False,
    )
```

time: 60 us -> 88.5 us (1.48)
  waiting for transfers between devices: 14.5 us -> 28.3 us
  between operations: 0.95 us -> 14.4 us
  starting transfers between devices: 30.1 us -> 24.8 us
  other arithmetic: 3.26 us -> 8.16 us
  local copies, waits for them, and re-layouts: 1.2 us -> 4.66 us
  blocking collectives: 6.36 us -> 3.99 us
    ppermute x0 -> x2, waiting for transfers between devices: none -> 9.02 us  [from_two(): return lax.ppermute(value, ('blk', 'rep'), pairs)]
    ppermute x8 -> x6, starting transfers between devices: 13.8 us -> 7.45 us  [along_outer(): return lax.ppermute(value, 'blk', pairs) if turn else value]
    all_gather x0 -> x1, waiting for transfers between devices: none -> 6.09 us  [shards(): everyone = lax.all_gather(jnp.concatenate(swapped, 0), 'rep', axis=0)]
    ppermute x0 -> x2, starting transfers between devices: none -> 4.58 us  [from_two(): return lax.ppermute(value, ('blk', 'rep'), pairs)]
    ppermute x11 -> x9, waiting for transfers between devices: 8.18 us -> 4.29 us  [along_inner(): return lax.ppermute(value, 'blk', pairs) if turn else value]
    ppermute x11 -> x9, starting transfers between devices: 16.3 us -> 12.7 us  [along_inner(): return lax.ppermute(value, 'blk', pairs) if turn else value]
    ppermute x8 -> x6, waiting for transfers between devices: 6.37 us -> 8.89 us  [along_outer(): return lax.ppermute(value, 'blk', pairs) if turn else value]
    select_n x3, other arithmetic: 0.05 us -> 2.51 us  [shards(): piece = jnp.where(holder == r, everyone[r, index], piece)]
  transfers between devices with their start and end apart: 19 -> 18, of which waited for: 6 -> 9; matrix products, arithmetic and copies ran while one was open for 10% -> 14% of each run, Pallas kernels for 0% -> 0%
where the time goes in v13:
time: 88.5 us; the launch traced here: 87.9 us
  waiting for transfers between devices  28.3 us (32%)
  starting transfers between devices  24.8 us (28%)
  between operations  14.4 us (16%)
  other arithmetic  8.16 us (9%)
  local copies, waits for them, and re-layouts  4.66 us (5%)
  blocking collectives  3.99 us (5%)
  matrix products  3.62 us (4%)
    ppermute x9, starting transfers between devices, along_inner(): return lax.ppermute(value, 'blk', pairs) if turn else value  12.7 us
    ppermute x2, waiting for transfers between devices, from_two(): return lax.ppermute(value, ('blk', 'rep'), pairs)  9.02 us
    ppermute x6, waiting for transfers between devices, along_outer(): return lax.ppermute(value, 'blk', pairs) if turn else value  8.89 us
    ppermute x6, starting transfers between devices, along_outer(): return lax.ppermute(value, 'blk', pairs) if turn else value  7.45 us
    all_gather x1, waiting for transfers between devices, shards(): everyone = lax.all_gather(jnp.concatenate(swapped, 0), 'rep', axis=0)  6.09 us
    ppermute x2, starting transfers between devices, from_two(): return lax.ppermute(value, ('blk', 'rep'), pairs)  4.58 us
    ppermute x9, waiting for transfers between devices, along_inner(): return lax.ppermute(value, 'blk', pairs) if turn else value  4.29 us
    dot_general x5, matrix products, dot(): lax.dot_general(lhs, rhs, (dims, ((), ())), preferred_element_type=jnp.fl...  3.62 us
  transfers between devices with their start and end apart: 18, of which 9 were waited for; matrix products, arithmetic and copies ran while one was open for 14% of the time, Pallas kernels for 0%

profile of v13, /device:TPU:0, one launch (start us, length us, event | category | flops | bytes accessed | tf_op | source)
XLA Modules:
  0.0 87.9 jit_solution(7931977018443519839)
XLA Ops:
  7.2 0.8 add_bitcast_fusion
  8.2 0.9 %slice_bitcast_fusion.17 = (bf16[128,128]{1,0:T(8,128)(2,1)S(1)}, bf16[128,128]{1,0:T(8,128)(2,1)S(1)}, bf16[128,128]{1,0:T(8,128)(2,1)S(1)}, bf16[128,128]{1,0:...) fusion(bf16[1,8,128,128]{3,2,1,0:T(8,128)(2,1)} %param.6), kind=kLoop, calls=%fused_computation.101 | loop fusion | bytes 524288 | tf_op jit(solution)/shard_map/jit(_where)/broadcast_in_dim | solution.py:80
  9.9 2.9 %collective-permute-start.2 = (bf16[2,128,128]{2,1,0:T(8,128)(2,1)}, bf16[2,128,128]{2,1,0:T(8,128)(2,1)}, u32[]{:S(2)}, u32[]{:S(2)}) collective-permute-start(bf16[2,128,128]{2,1,0:T(8,128)(2,1)} %get-tuple-element.37), channel_id=1, source_target_pairs={{0,2},{2,0},{4,6},{6,4},{8,10},{10,8},{12,14},{14,12},{16,18},{18,... | collective-permute-start | bytes 196616 | tf_op jit(solution)/shard_map/ppermute | solution.py:29
  12.9 1.5 %collective-permute-start.3 = (bf16[2,128,128]{2,1,0:T(8,128)(2,1)}, bf16[2,128,128]{2,1,0:T(8,128)(2,1)S(1)}, u32[]{:S(2)}, u32[]{:S(2)}) collective-permute-start(bf16[2,128,128]{2,1,0:T(8,128)(2,1)} %get-tuple-element.36), channel_id=1, source_target_pairs={{0,4},{2,6},{4,0},{6,2},{8,12},{10,14},{12,8},{14,10},{16,20},{18,... | collective-permute-start | bytes 196616 | tf_op jit(solution)/shard_map/ppermute | solution.py:29
  14.4 3.1 %collective-permute-start.1 = (bf16[128,1024]{1,0:T(8,128)(2,1)}, bf16[128,1024]{1,0:T(8,128)(2,1)S(1)}, u32[]{:S(2)}, u32[]{:S(2)}) collective-permute-start(bf16[128,1024]{1,0:T(8,128)(2,1)} %param.5), channel_id=1, source_target_pairs={{0,16},{1,25},{2,18},{3,27},{4,20},{5,29},{6,22},{7,31},{8,24},{9,... | collective-permute-start | bytes 786440 | tf_op jit(solution)/shard_map/ppermute | solution.py:42
  17.5 1.5 %collective-permute-start.5 = (bf16[128,1024]{1,0:T(8,128)(2,1)}, bf16[128,1024]{1,0:T(8,128)(2,1)S(1)}, u32[]{:S(2)}, u32[]{:S(2)}) collective-permute-start(bf16[128,1024]{1,0:T(8,128)(2,1)} %param.9), channel_id=1, source_target_pairs={{0,4},{1,7},{2,6},{3,5},{4,0},{5,3},{6,2},{7,1},{8,12},{9,15},{10,... | collective-permute-start | bytes 786440 | tf_op jit(solution)/shard_map/ppermute | solution.py:42
  19.0 0.9 constant_dynamic-update-slice_fusion.2
  19.9 9.0 %collective-permute-done.1 = bf16[128,1024]{1,0:T(8,128)(2,1)S(1)} collective-permute-done((bf16[128,1024]{1,0:T(8,128)(2,1)}, bf16[128,1024]{1,0:T(8,128)(2,1)S(1)}, u32[]{:S(2)}, u32[]{:S(2)}) %collective-permute-start.1) | collective-permute-done | bytes 262176 | tf_op jit(solution)/shard_map/ppermute | solution.py:42
  29.2 0.8 copy-done.1
  30.7 0.9 %constant_dynamic-slice_fusion = bf16[128,512]{1,0:T(8,128)(2,1)S(1)} fusion(bf16[128,1024]{1,0:T(8,128)(2,1)} %param.9, s32[]{:T(128)S(6)} %select_n.240), kind=kLoop, calls=%fused_computation.106 | loop fusion | bytes 262148 | tf_op jit(solution)/shard_map/dynamic_slice | solution.py:65
  31.6 1.6 %collective-permute-start.11 = (bf16[128,512]{1,0:T(8,128)(2,1)S(1)}, bf16[128,512]{1,0:T(8,128)(2,1)S(1)}, u32[]{:S(2)}, u32[]{:S(2)}) collective-permute-start(bf16[128,512]{1,0:T(8,128)(2,1)S(1)} %constant_dynamic-slice_fusion), channel_id=1, source_target_pairs={{0,2},{2,0},{4,6},{6,4},{8,10},{10,8},{12,14},{14,12},{16,18},{18,... | collective-permute-start | bytes 393224 | tf_op jit(solution)/shard_map/ppermute | solution.py:29
  33.2 6.1 %all-gather.3.cloned.1.call-done = bf16[32,128,128]{2,1,0:T(8,128)(2,1)} async-done(((bf16[16,128,128]{2,1,0:T(8,128)(2,1)}), bf16[32,128,128]{2,1,0:T(8,128)(2,1)}) %all-gather.3.cloned.1.call-update) | async-done | bytes 1048592 | tf_op jit(solution)/shard_map/all_gather | solution.py:92
  39.3 0.8 fusion.23
  40.1 1.1 %slice_select_fusion = (bf16[1,4,128,128]{3,2,1,0:T(8,128)(2,1)S(1)}, bf16[1,4,128,128]{3,2,1,0:T(8,128)(2,1)S(1)}) fusion(bf16[2,16,128,128]{3,2,1,0:T(8,128)(2,1)} %bitcast.145, pred[]{:T(512)S(6)} %eq.69), kind=kLoop, calls=%fused_computation.33 | loop fusion | flops 131072 | bytes 786433 | tf_op jit(solution)/shard_map/jit(_where)/select_n | solution.py:98
  41.2 0.8 select_bitcast_fusion.12
  42.1 0.9 %slice_bitcast_fusion.5 = (bf16[128,128]{1,0:T(8,128)(2,1)S(1)}, bf16[128,128]{1,0:T(8,128)(2,1)S(1)}, bf16[128,128]{1,0:T(8,128)(2,1)S(1)}, bf16[128,128]{1,0:T...) fusion(bf16[2,16,128,128]{3,2,1,0:T(8,128)(2,1)} %bitcast.147, ...), kind=kLoop, calls=%fused_computation.59 | loop fusion | flops 98304 | bytes 458758 | tf_op jit(solution)/shard_map/squeeze | solution.py:116
  43.0 0.9 %select_bitcast_fusion.13 = (bf16[128,128]{1,0:T(8,128)(2,1)S(1)}, bf16[128,128]{1,0:T(8,128)(2,1)S(1)}, bf16[128,128]{1,0:T(8,128)(2,1)S(1)}, bf16[128,128]{1,0...) fusion(pred[]{:T(512)S(6)} %eq.74, bf16[2,16,128,128]{3,2,1,0:T(8,128)(2,1)} %bitcast.148, ...), kind=kLoop, calls=%fused_computation.93 | loop fusion | flops 98304 | bytes 458758 | tf_op jit(solution)/shard_map/jit(_where)/select_n | solution.py:118
  44.1 1.4 %convolution_convert_fusion = bf16[512,512]{1,0:T(8,128)(2,1)S(1)} fusion(bf16[512,512]{1,0:T(8,128)(2,1)S(1)} %maximum_maximum_fusion, bf16[128,512]{1,0:T(8,128)(2,1)S(1)} %get-tuple-element.31, bf16[128,512]{1,0:T(8,128)(2,1)S(1)} %get-tuple-element.30, bf16[128,512]{1,0:T(8,128)(2,1)S(1)} %collective-permute-done, ...), kind=kOutput, calls=%fused_computation | convolution fusion | flops 270794752 | bytes 1572864 | tf_op jit(solution)/shard_map/dot_general | solution.py:59
  45.6 2.7 %collective-permute-start.8 = (bf16[128,512]{1,0:T(8,128)(2,1)S(1)}, bf16[128,512]{1,0:T(8,128)(2,1)S(1)}, u32[]{:S(2)}, u32[]{:S(2)}) collective-permute-start(bf16[128,512]{1,0:T(8,128)(2,1)S(1)} %pad_maximum_fusion.6), channel_id=1, source_target_pairs={{0,6},{2,4},{4,2},{6,0},{8,14},{10,12},{12,10},{14,8},{16,22},{18,... | collective-permute-start | bytes 393224 | tf_op jit(solution)/shard_map/ppermute | solution.py:29
  49.9 1.8 %collective-permute-start.15 = (bf16[1024,128]{1,0:T(8,128)(2,1)S(1)}, bf16[1024,128]{1,0:T(8,128)(2,1)S(1)}, u32[]{:S(2)}, u32[]{:S(2)}) collective-permute-start(bf16[1024,128]{1,0:T(8,128)(2,1)S(1)} %pad_maximum_fusion.2), channel_id=1, source_target_pairs={{0,8},{2,10},{4,12},{6,14},{8,0},{10,2},{12,4},{14,6},{16,24},{18,... | collective-permute-start | bytes 786440 | tf_op jit(solution)/shard_map/ppermute | solution.py:33
  52.4 2.7 %collective-permute-done.7 = bf16[128,512]{1,0:T(8,128)(2,1)S(1)} collective-permute-done((bf16[128,512]{1,0:T(8,128)(2,1)S(1)}, bf16[128,512]{1,0:T(8,128)(2,1)S(1)}, u32[]{:S(2)}, u32[]{:S(2)}) %collective-permute-start.7) | collective-permute-done | bytes 131104 | tf_op jit(solution)/shard_map/ppermute | solution.py:29
  55.4 2.0 %all_gather.14 = bf16[256,512]{1,0:T(8,128)(2,1)S(1)} all-gather(bf16[128,512]{1,0:T(8,128)(2,1)S(1)} %fusion.17), channel_id=1, replica_groups=mesh['blk'=16,'rep'=2] {'rep'}, dimensions={0}, use_global_device_ids=true | all-gather | bytes 393216 | tf_op jit(solution)/shard_map/all_gather | solution.py:136
  58.2 3.4 %collective-permute-start.14 = (bf16[64,512]{1,0:T(8,128)(2,1)S(1)}, bf16[64,512]{1,0:T(8,128)(2,1)S(1)}, u32[]{:S(2)}, u32[]{:S(2)}) collective-permute-start(bf16[64,512]{1,0:T(8,128)(2,1)S(1)} %get-tuple-element.33), channel_id=1, source_target_pairs={{0,24},{2,26},{4,28},{6,30},{8,16},{10,18},{12,20},{14,22},{16,8},... | collective-permute-start | bytes 196616 | tf_op jit(solution)/shard_map/ppermute | solution.py:33
  61.6 1.1 %collective-permute-start.12 = (bf16[64,512]{1,0:T(8,128)(2,1)S(1)}, bf16[64,512]{1,0:T(8,128)(2,1)S(1)}, u32[]{:S(2)}, u32[]{:S(2)}) collective-permute-start(bf16[64,512]{1,0:T(8,128)(2,1)S(1)} %get-tuple-element.32), channel_id=1, source_target_pairs={{0,8},{2,10},{4,12},{6,14},{8,0},{10,2},{12,4},{14,6},{16,24},{18,... | collective-permute-start | bytes 196616 | tf_op jit(solution)/shard_map/ppermute | solution.py:33
  62.6 1.5 %collective-permute-start.9 = (bf16[256,512]{1,0:T(8,128)(2,1)S(1)}, bf16[256,512]{1,0:T(8,128)(2,1)S(1)}, u32[]{:S(2)}, u32[]{:S(2)}) collective-permute-start(bf16[256,512]{1,0:T(8,128)(2,1)S(1)} %pad_maximum_fusion.1), channel_id=1, source_target_pairs={{0,2},{2,0},{4,6},{6,4},{8,10},{10,8},{12,14},{14,12},{16,18},{18,... | collective-permute-start | bytes 786440 | tf_op jit(solution)/shard_map/ppermute | solution.py:29
  64.7 2.9 %collective-permute-done.13 = bf16[64,512]{1,0:T(8,128)(2,1)S(1)} collective-permute-done((bf16[64,512]{1,0:T(8,128)(2,1)S(1)}, bf16[64,512]{1,0:T(8,128)(2,1)S(1)}, u32[]{:S(2)}, u32[]{:S(2)}) %collective-permute-start.13) | collective-permute-done | bytes 65568 | tf_op jit(solution)/shard_map/ppermute | solution.py:33
  68.4 1.2 %collective-permute-start.16 = (bf16[512,128]{1,0:T(8,128)(2,1)S(1)}, bf16[512,128]{1,0:T(8,128)(2,1)S(1)}, u32[]{:S(2)}, u32[]{:S(2)}) collective-permute-start(bf16[512,128]{1,0:T(8,128)(2,1)S(1)} %fusion.9), channel_id=1, source_target_pairs={{0,16},{2,18},{4,20},{6,22},{8,24},{10,26},{12,28},{14,30},{16,0},... | collective-permute-start | bytes 393224 | tf_op jit(solution)/shard_map/ppermute | solution.py:33
  70.2 1.5 %collective-permute-start.10 = (bf16[128,512]{1,0:T(8,128)(2,1)S(1)}, bf16[128,512]{1,0:T(8,128)(2,1)S(1)}, u32[]{:S(2)}, u32[]{:S(2)}) collective-permute-start(bf16[128,512]{1,0:T(8,128)(2,1)S(1)} %fusion.12), channel_id=1, source_target_pairs={{0,4},{2,6},{4,0},{6,2},{8,12},{10,14},{12,8},{14,10},{16,20},{18,... | collective-permute-start | bytes 393224 | tf_op jit(solution)/shard_map/ppermute | solution.py:29
  71.7 5.4 %collective-permute-done.16 = bf16[512,128]{1,0:T(8,128)(2,1)S(1)} collective-permute-done((bf16[512,128]{1,0:T(8,128)(2,1)S(1)}, bf16[512,128]{1,0:T(8,128)(2,1)S(1)}, u32[]{:S(2)}, u32[]{:S(2)}) %collective-permute-start.16) | collective-permute-done | bytes 131104 | tf_op jit(solution)/shard_map/ppermute | solution.py:33
  77.2 2.0 %all_gather.15 = bf16[1024,128]{1,0:T(8,128)(2,1)S(1)} all-gather(bf16[512,128]{1,0:T(8,128)(2,1)S(1)} %fusion.11), channel_id=1, replica_groups=mesh['blk'=16,'rep'=2] {'rep'}, dimensions={0}, use_global_device_ids=true | all-gather | bytes 393216 | tf_op jit(solution)/shard_map/all_gather | solution.py:154
  79.2 1.1 %fusion = bf16[128,512]{1,0:T(8,128)(2,1)} fusion(bf16[1024,128]{1,0:T(8,128)(2,1)S(1)} %all_gather.15, bf16[1024,1024]{1,0:T(8,128)(2,1)S(1)} %copy-done, s32[]{:T(128)S(6)} %select_n.240, bf16[128,1024]{1,0:T(8,128)(2,1)S(1)} %copy-done.5), kind=kOutput, calls=%fused_computation.3 | convolution fusion | flops 134545408 | bytes 1573888 | tf_op jit(solution)/shard_map/dot_general | solution.py:59
  80.4 0.7 fusion.14
  (71 shorter events, 7.6 us)
Async XLA Ops:
  7.2 26.0 %copy-start = (bf16[1024,1024]{1,0:T(8,128)(2,1)S(1)}, bf16[1024,1024]{1,0:T(8,128)(2,1)}, u32[]{:S(2)}) copy-start(bf16[1024,1024]{1,0:T(8,128)(2,1)} %param.8) | copy-start | bytes 6291460
  7.2 22.8 %copy-start.4 = (bf16[128,1024]{1,0:T(8,128)(2,1)S(1)}, bf16[128,1024]{1,0:T(8,128)(2,1)}, u32[]{:S(2)}) copy-start(bf16[128,1024]{1,0:T(8,128)(2,1)} %param.5) | copy-start | bytes 786436
  7.2 32.1 %all-gather.3.cloned.1.call-start = ((), (), s32[]{:S(2)}) async-start(), calls=%async_computation | async-start | bytes 1572864 | tf_op jit(solution)/shard_map/all_gather | solution.py:92
  9.9 9.0 %collective-permute-start.2 = (bf16[2,128,128]{2,1,0:T(8,128)(2,1)}, bf16[2,128,128]{2,1,0:T(8,128)(2,1)}, u32[]{:S(2)}, u32[]{:S(2)}) collective-permute-start(bf16[2,128,128]{2,1,0:T(8,128)(2,1)} %get-tuple-element.37), channel_id=1, source_target_pairs={{0,2},{2,0},{4,6},{6,4},{8,10},{10,8},{12,14},{14,12},{16,18},{18,... | collective-permute-start | bytes 196616 | tf_op jit(solution)/shard_map/ppermute | solution.py:29
  12.9 7.0 %collective-permute-start.3 = (bf16[2,128,128]{2,1,0:T(8,128)(2,1)}, bf16[2,128,128]{2,1,0:T(8,128)(2,1)S(1)}, u32[]{:S(2)}, u32[]{:S(2)}) collective-permute-start(bf16[2,128,128]{2,1,0:T(8,128)(2,1)} %get-tuple-element.36), channel_id=1, source_target_pairs={{0,4},{2,6},{4,0},{6,2},{8,12},{10,14},{12,8},{14,10},{16,20},{18,... | collective-permute-start | bytes 196616 | tf_op jit(solution)/shard_map/ppermute | solution.py:29
  14.4 5.5 %collective-permute-start.4 = (bf16[2,128,128]{2,1,0:T(8,128)(2,1)}, bf16[2,128,128]{2,1,0:T(8,128)(2,1)S(1)}, u32[]{:S(2)}, u32[]{:S(2)}) collective-permute-start(bf16[2,128,128]{2,1,0:T(8,128)(2,1)} %get-tuple-element.35), channel_id=1, source_target_pairs={{0,6},{2,4},{4,2},{6,0},{8,14},{10,12},{12,10},{14,8},{16,22},{18,... | collective-permute-start | bytes 196616 | tf_op jit(solution)/shard_map/ppermute | solution.py:29
  14.4 14.5 %collective-permute-start.1 = (bf16[128,1024]{1,0:T(8,128)(2,1)}, bf16[128,1024]{1,0:T(8,128)(2,1)S(1)}, u32[]{:S(2)}, u32[]{:S(2)}) collective-permute-start(bf16[128,1024]{1,0:T(8,128)(2,1)} %param.5), channel_id=1, source_target_pairs={{0,16},{1,25},{2,18},{3,27},{4,20},{5,29},{6,22},{7,31},{8,24},{9,... | collective-permute-start | bytes 786440 | tf_op jit(solution)/shard_map/ppermute | solution.py:42
  17.5 11.6 %collective-permute-start.5 = (bf16[128,1024]{1,0:T(8,128)(2,1)}, bf16[128,1024]{1,0:T(8,128)(2,1)S(1)}, u32[]{:S(2)}, u32[]{:S(2)}) collective-permute-start(bf16[128,1024]{1,0:T(8,128)(2,1)} %param.9), channel_id=1, source_target_pairs={{0,4},{1,7},{2,6},{3,5},{4,0},{5,3},{6,2},{7,1},{8,12},{9,15},{10,... | collective-permute-start | bytes 786440 | tf_op jit(solution)/shard_map/ppermute | solution.py:42
  28.9 4.3 %copy-start.2 = (bf16[128,1024]{1,0:T(8,128)(2,1)}, bf16[128,1024]{1,0:T(8,128)(2,1)S(1)}, u32[]{:S(2)}) copy-start(bf16[128,1024]{1,0:T(8,128)(2,1)S(1)} %collective-permute-done.1) | copy-start | bytes 786436
  29.2 0.8 copy-start.1
  30.7 13.4 %collective-permute-start = (bf16[128,512]{1,0:T(8,128)(2,1)}, bf16[128,512]{1,0:T(8,128)(2,1)S(1)}, u32[]{:S(2)}, u32[]{:S(2)}) collective-permute-start(bf16[128,512]{1,0:T(8,128)(2,1)} %dynamic-slice_maximum_fusion), channel_id=1, source_target_pairs={{0,8},{2,10},{4,12},{6,14},{8,0},{10,2},{12,4},{14,6},{16,24},{18,... | collective-permute-start | bytes 393224 | tf_op jit(solution)/shard_map/ppermute | solution.py:33
  31.6 17.8 %collective-permute-start.11 = (bf16[128,512]{1,0:T(8,128)(2,1)S(1)}, bf16[128,512]{1,0:T(8,128)(2,1)S(1)}, u32[]{:S(2)}, u32[]{:S(2)}) collective-permute-start(bf16[128,512]{1,0:T(8,128)(2,1)S(1)} %constant_dynamic-slice_fusion), channel_id=1, source_target_pairs={{0,2},{2,0},{4,6},{6,4},{8,10},{10,8},{12,14},{14,12},{16,18},{18,... | collective-permute-start | bytes 393224 | tf_op jit(solution)/shard_map/ppermute | solution.py:29
  33.2 10.8 %copy-start.3 = (bf16[128,1024]{1,0:T(8,128)(2,1)S(1)}, bf16[128,1024]{1,0:T(8,128)(2,1)}, u32[]{:S(2)}) copy-start(bf16[128,1024]{1,0:T(8,128)(2,1)} %copy-done.2) | copy-start | bytes 786436
  45.6 6.8 %collective-permute-start.8 = (bf16[128,512]{1,0:T(8,128)(2,1)S(1)}, bf16[128,512]{1,0:T(8,128)(2,1)S(1)}, u32[]{:S(2)}, u32[]{:S(2)}) collective-permute-start(bf16[128,512]{1,0:T(8,128)(2,1)S(1)} %pad_maximum_fusion.6), channel_id=1, source_target_pairs={{0,6},{2,4},{4,2},{6,0},{8,14},{10,12},{12,10},{14,8},{16,22},{18,... | collective-permute-start | bytes 393224 | tf_op jit(solution)/shard_map/ppermute | solution.py:29
  48.3 6.7 %collective-permute-start.7 = (bf16[128,512]{1,0:T(8,128)(2,1)S(1)}, bf16[128,512]{1,0:T(8,128)(2,1)S(1)}, u32[]{:S(2)}, u32[]{:S(2)}) collective-permute-start(bf16[128,512]{1,0:T(8,128)(2,1)S(1)} %pad_maximum_fusion.5), channel_id=1, source_target_pairs={{0,4},{2,6},{4,0},{6,2},{8,12},{10,14},{12,8},{14,10},{16,20},{18,... | collective-permute-start | bytes 393224 | tf_op jit(solution)/shard_map/ppermute | solution.py:29
  49.0 6.4 %collective-permute-start.6 = (bf16[128,512]{1,0:T(8,128)(2,1)S(1)}, bf16[128,512]{1,0:T(8,128)(2,1)S(1)}, u32[]{:S(2)}, u32[]{:S(2)}) collective-permute-start(bf16[128,512]{1,0:T(8,128)(2,1)S(1)} %pad_maximum_fusion.4), channel_id=1, source_target_pairs={{0,2},{2,0},{4,6},{6,4},{8,10},{10,8},{12,14},{14,12},{16,18},{18,... | collective-permute-start | bytes 393224 | tf_op jit(solution)/shard_map/ppermute | solution.py:29
  49.9 18.4 %collective-permute-start.15 = (bf16[1024,128]{1,0:T(8,128)(2,1)S(1)}, bf16[1024,128]{1,0:T(8,128)(2,1)S(1)}, u32[]{:S(2)}, u32[]{:S(2)}) collective-permute-start(bf16[1024,128]{1,0:T(8,128)(2,1)S(1)} %pad_maximum_fusion.2), channel_id=1, source_target_pairs={{0,8},{2,10},{4,12},{6,14},{8,0},{10,2},{12,4},{14,6},{16,24},{18,... | collective-permute-start | bytes 786440 | tf_op jit(solution)/shard_map/ppermute | solution.py:33
  58.1 21.1 %copy-start.5 = (bf16[128,1024]{1,0:T(8,128)(2,1)S(1)}, bf16[128,1024]{1,0:T(8,128)(2,1)}, u32[]{:S(2)}) copy-start(bf16[128,1024]{1,0:T(8,128)(2,1)} %param.5) | copy-start | bytes 786436
  58.2 6.6 %collective-permute-start.14 = (bf16[64,512]{1,0:T(8,128)(2,1)S(1)}, bf16[64,512]{1,0:T(8,128)(2,1)S(1)}, u32[]{:S(2)}, u32[]{:S(2)}) collective-permute-start(bf16[64,512]{1,0:T(8,128)(2,1)S(1)} %get-tuple-element.33), channel_id=1, source_target_pairs={{0,24},{2,26},{4,28},{6,30},{8,16},{10,18},{12,20},{14,22},{16,8},... | collective-permute-start | bytes 196616 | tf_op jit(solution)/shard_map/ppermute | solution.py:33
  61.6 6.1 %collective-permute-start.13 = (bf16[64,512]{1,0:T(8,128)(2,1)S(1)}, bf16[64,512]{1,0:T(8,128)(2,1)S(1)}, u32[]{:S(2)}, u32[]{:S(2)}) collective-permute-start(bf16[64,512]{1,0:T(8,128)(2,1)S(1)} %get-tuple-element.34), channel_id=1, source_target_pairs={{0,16},{2,18},{4,20},{6,22},{8,24},{10,26},{12,28},{14,30},{16,0},... | collective-permute-start | bytes 196616 | tf_op jit(solution)/shard_map/ppermute | solution.py:33
  61.6 6.1 %collective-permute-start.12 = (bf16[64,512]{1,0:T(8,128)(2,1)S(1)}, bf16[64,512]{1,0:T(8,128)(2,1)S(1)}, u32[]{:S(2)}, u32[]{:S(2)}) collective-permute-start(bf16[64,512]{1,0:T(8,128)(2,1)S(1)} %get-tuple-element.32), channel_id=1, source_target_pairs={{0,8},{2,10},{4,12},{6,14},{8,0},{10,2},{12,4},{14,6},{16,24},{18,... | collective-permute-start | bytes 196616 | tf_op jit(solution)/shard_map/ppermute | solution.py:33
  62.6 7.6 %collective-permute-start.9 = (bf16[256,512]{1,0:T(8,128)(2,1)S(1)}, bf16[256,512]{1,0:T(8,128)(2,1)S(1)}, u32[]{:S(2)}, u32[]{:S(2)}) collective-permute-start(bf16[256,512]{1,0:T(8,128)(2,1)S(1)} %pad_maximum_fusion.1), channel_id=1, source_target_pairs={{0,2},{2,0},{4,6},{6,4},{8,10},{10,8},{12,14},{14,12},{16,18},{18,... | collective-permute-start | bytes 786440 | tf_op jit(solution)/shard_map/ppermute | solution.py:29
  68.4 8.8 %collective-permute-start.16 = (bf16[512,128]{1,0:T(8,128)(2,1)S(1)}, bf16[512,128]{1,0:T(8,128)(2,1)S(1)}, u32[]{:S(2)}, u32[]{:S(2)}) collective-permute-start(bf16[512,128]{1,0:T(8,128)(2,1)S(1)} %fusion.9), channel_id=1, source_target_pairs={{0,16},{2,18},{4,20},{6,22},{8,24},{10,26},{12,28},{14,30},{16,0},... | collective-permute-start | bytes 393224 | tf_op jit(solution)/shard_map/ppermute | solution.py:33
  70.2 10.1 %collective-permute-start.10 = (bf16[128,512]{1,0:T(8,128)(2,1)S(1)}, bf16[128,512]{1,0:T(8,128)(2,1)S(1)}, u32[]{:S(2)}, u32[]{:S(2)}) collective-permute-start(bf16[128,512]{1,0:T(8,128)(2,1)S(1)} %fusion.12), channel_id=1, source_target_pairs={{0,4},{2,6},{4,0},{6,2},{8,12},{10,14},{12,8},{14,10},{16,20},{18,... | collective-permute-start | bytes 393224 | tf_op jit(solution)/shard_map/ppermute | solution.py:29
Sparse Core Ops, SparseCore 0:
  30.1 9.1 all-gather.2

commit v14 on v13

--- a/solution.py
+++ b/solution.py
@@ -19,7 +19,6 @@
     span_bits = section_span.bit_length() - 1
     cols_here = feature_width // rep_count
     rows_here = feature_width // blk_count
-    lane_blocks = cols_here // tile_size
     bf16 = jnp.bfloat16
     turns = range(side)
     rising = [1 << b for b in range(bits)]
@@ -31,15 +30,6 @@
     def along_outer(value, turn):
         pairs = [(o * side + i, (o ^ turn) * side + i) for o in turns for i in turns]
         return lax.ppermute(value, "blk", pairs) if turn else value
-
-    def from_two(value, turn, outer):
-        pairs = []
-        for o in turns:
-            for i in turns:
-                for r in range(2):
-                    there = (o ^ (turn + r)) * side + i if outer else o * side + (i ^ (turn + r))
-                    pairs.append(((o * side + i) * 2 + r, there * 2 + r))
-        return lax.ppermute(value, ("blk", "rep"), pairs)
 
     def halved(parts, move):
         parts = dict(enumerate(parts))
@@ -61,14 +51,14 @@
     def lanes(value, index):
         return value[:, index * tile_size : (index + 1) * tile_size]
 
+    def after(value, other):
+        row = other[:1, :tile_size] * 0
+        return value + jnp.concatenate([row] * (value.shape[1] // tile_size), 1)
+
     def columns_of(value, index):
         return lax.dynamic_slice_in_dim(value, index * cols_here, cols_here, 1)
 
-    pair_up = rep_count == 2
-    direct = turns[1:2] if pair_up else turns[1:]
-    hidden_far = [from_two(hidden_pre, t, True) for t in turns[2::2]] if pair_up else []
     hidden_part = jnp.maximum(columns_of(hidden_pre, rep_pos), 0)
-    hidden_stack = [hidden_part] + [along_outer(hidden_part, t) for t in direct]
 
     columns = adj_cols[0]
     turn_of = (columns & (side - 1)) ^ inner_pos
@@ -78,47 +68,29 @@
     ordered = jnp.zeros((section_span, tile_size, tile_size), bf16)
     for k in range(slots):
         ordered = jnp.where(hit[:, k, None, None], adj_vals[0, k][None], ordered)
-    swapped = [
-        along_inner(ordered[t * per_core : (t + 1) * per_core], t) for t in turns
-    ]
-
-    grad_far = [from_two(cotangent, t, False) for t in turns[2::2]] if pair_up else []
-    grad_part = columns_of(cotangent, rep_pos)
-    grad_stack = [grad_part] + [along_inner(grad_part, t) for t in direct]
-
-    for far in hidden_far + grad_far:
-        other = columns_of(far, 1 - rep_pos)
-        swapped.append(jnp.stack([lanes(other, n) for n in range(lane_blocks)]))
-    everyone = lax.all_gather(jnp.concatenate(swapped, 0), "rep", axis=0)
-
-    for index, far in enumerate(hidden_far + grad_far):
-        mine = columns_of(far, rep_pos)
-        start = section_span + index * lane_blocks
-        both = everyone[:, start : start + lane_blocks]
-        other = jnp.where(rep_pos == 0, both[1], both[0])
-        other = jnp.concatenate([other[n] for n in range(lane_blocks)], 1)
-        blocks = [jnp.where(rep_pos == 0, mine, other), jnp.where(rep_pos == 0, other, mine)]
-        if index < len(hidden_far):
-            hidden_stack.extend(jnp.maximum(part, 0) for part in blocks)
-        else:
-            grad_stack.extend(blocks)
-    hidden_stack = jnp.concatenate(hidden_stack, 0)
-    grad_stack = jnp.concatenate(grad_stack, 0)
-
+    everyone = lax.all_gather(ordered, "rep", axis=0)
+    row_block = outer_pos * side + inner_pos
     rows = []
     for t in turns:
-        row_block = outer_pos * side + (inner_pos ^ t)
         row = []
         for e in turns:
-            column_block = (outer_pos ^ e) * side + inner_pos
+            column_block = (outer_pos ^ e) * side + (inner_pos ^ t)
             holder = ((row_block - column_block) & (blk_count - 1)) >> span_bits
             index = t * per_core + e % per_core
             piece = everyone[0, index]
             for r in range(1, rep_count):
                 piece = jnp.where(holder == r, everyone[r, index], piece)
             row.append(piece)
-        rows.append(jnp.concatenate(row, 1))
+        rows.append(along_inner(jnp.concatenate(row, 1), t))
     block = jnp.concatenate(rows, 0)
+
+    hidden_stack = [hidden_part]
+    for t in turns[1:]:
+        message = after(hidden_part, rows[1]) if t == 1 else hidden_part
+        hidden_stack.append(along_outer(message, t))
+    hidden_stack = jnp.concatenate(hidden_stack, 0)
+    grad_part = columns_of(cotangent, rep_pos)
+    grad_stack = jnp.concatenate([along_inner(grad_part, t) for t in turns], 0)
 
     mixed = dot(hidden_stack, block, ((0,), (1,))).astype(bf16)
     share = cols_here // side
@@ -130,8 +102,8 @@
         chosen = jnp.concatenate([lanes(chosen, u ^ t) for u in turns], 1)
         mixed_cols = mixed_cols + along_inner(chosen, t).astype(jnp.float32)
 
-    back = dot(grad_stack, block, ((0,), (0,)))
-    back = halved([lanes(back, e) for e in turns], along_outer).astype(bf16)
+    back = dot(grad_stack, block, ((0,), (0,))).astype(bf16)
+    back = sum(along_outer(lanes(back, e), e).astype(jnp.float32) for e in turns).astype(bf16)
 
     mixed_cols = lax.all_gather(mixed_cols.astype(bf16), "rep", axis=0, tiled=True)
     weight_part = dot(mixed_cols, grad_stack, ((1,), (0,))).astype(bf16)

time: 88.5 us -> 66.1 us (0.75)
  between operations: 14.4 us -> 0.93 us
  waiting for transfers between devices: 28.3 us -> 17.5 us
  starting transfers between devices: 24.8 us -> 29 us
  other arithmetic: 8.16 us -> 4.01 us
  local copies, waits for them, and re-layouts: 4.66 us -> 2.26 us
  matrix products: 3.62 us -> 5.89 us
  blocking collectives: 3.99 us -> 6.17 us
    ppermute x2 -> x0, waiting for transfers between devices: 9.02 us -> none  [from_two(): return lax.ppermute(value, ('blk', 'rep'), pairs)]
    all_gather x1 -> x0, waiting for transfers between devices: 6.09 us -> none  [shards(): everyone = lax.all_gather(jnp.concatenate(swapped, 0), 'rep', axis=0)]
    ppermute x6 -> x9, starting transfers between devices: 7.45 us -> 13 us  [along_outer(): return lax.ppermute(value, 'blk', pairs) if turn else value]
    ppermute x2 -> x0, starting transfers between devices: 4.58 us -> none  [from_two(): return lax.ppermute(value, ('blk', 'rep'), pairs)]
    ppermute x9 -> x11, starting transfers between devices: 12.7 us -> 16 us  [along_inner(): return lax.ppermute(value, 'blk', pairs) if turn else value]
    ppermute x9 -> x11, waiting for transfers between devices: 4.29 us -> 6.7 us  [along_inner(): return lax.ppermute(value, 'blk', pairs) if turn else value]
    dot_general x5, matrix products: 3.62 us -> 5.89 us  [dot(): lax.dot_general(lhs, rhs, (dims, ((), ())), preferred_element_type=jnp.fl...]
    all_gather x0 -> x1, blocking collectives: none -> 2.18 us  [shards(): everyone = lax.all_gather(ordered, 'rep', axis=0)]
  transfers between devices with their start and end apart: 18 -> 20, of which waited for: 9 -> 8; matrix products, arithmetic and copies ran while one was open for 14% -> 15% of each run, Pallas kernels for 0% -> 0%
where the time goes in v14:
time: 66.1 us; the launch traced here: 65.8 us
  starting transfers between devices  29 us (44%)
  waiting for transfers between devices  17.5 us (26%)
  blocking collectives  6.17 us (9%)
  matrix products  5.89 us (9%)
  other arithmetic  4.01 us (6%)
  local copies, waits for them, and re-layouts  2.26 us (3%)
  between operations  0.93 us (1%)
    ppermute x11, starting transfers between devices, along_inner(): return lax.ppermute(value, 'blk', pairs) if turn else value  16 us
    ppermute x9, starting transfers between devices, along_outer(): return lax.ppermute(value, 'blk', pairs) if turn else value  13 us
    ppermute x9, waiting for transfers between devices, along_outer(): return lax.ppermute(value, 'blk', pairs) if turn else value  10.8 us
    ppermute x11, waiting for transfers between devices, along_inner(): return lax.ppermute(value, 'blk', pairs) if turn else value  6.7 us
    dot_general x5, matrix products, dot(): lax.dot_general(lhs, rhs, (dims, ((), ())), preferred_element_type=jnp.fl...  5.89 us
    all_gather x1, blocking collectives, shards(): everyone = lax.all_gather(ordered, 'rep', axis=0)  2.18 us
    all_gather x1, blocking collectives, shards(): back_full = lax.all_gather(back, 'rep', axis=0, tiled=True)  1.99 us
    all_gather x1, blocking collectives, shards(): lax.all_gather(mixed_cols.astype(bf16), 'rep', axis=0, tiled=True)  1.99 us
  transfers between devices with their start and end apart: 20, of which 8 were waited for; matrix products, arithmetic and copies ran while one was open for 15% of the time, Pallas kernels for 0%

profile of v14, /device:TPU:0, one launch (start us, length us, event | category | flops | bytes accessed | tf_op | source)
XLA Modules:
  0.0 65.8 jit_solution(5324175290900525079)
XLA Ops:
  0.7 1.1 %constant_dynamic-slice_fusion = bf16[128,512]{1,0:T(8,128)(2,1)S(1)} fusion(bf16[128,1024]{1,0:T(8,128)(2,1)} %param.9, s32[]{:T(128)S(6)} %select_n.256), kind=kLoop, calls=%fused_computation.70 | loop fusion | bytes 262148 | tf_op jit(solution)/shard_map/dynamic_slice | solution.py:59
  1.7 4.0 %collective-permute-start.13 = (bf16[128,512]{1,0:T(8,128)(2,1)S(1)}, bf16[128,512]{1,0:T(8,128)(2,1)}, u32[]{:S(2)}, u32[]{:S(2)}) collective-permute-start(bf16[128,512]{1,0:T(8,128)(2,1)S(1)} %constant_dynamic-slice_fusion), channel_id=1, source_target_pairs={{0,6},{2,4},{4,2},{6,0},{8,14},{10,12},{12,10},{14,8},{16,22},{18,... | collective-permute-start | bytes 393224 | tf_op jit(solution)/shard_map/ppermute | solution.py:28
  6.3 0.7 %add_bitcast_fusion = s32[8]{0:T(128)S(1)} fusion(s32[1,8]{1,0:T(1,128)} %param.7, s32[]{:T(128)S(6)} %shift_right_arithmetic.53, s32[]{:T(128)S(6)} %and.59), kind=kLoop, calls=%fused_computation.87 | loop fusion | flops 56 | bytes 72 | tf_op jit(solution)/shard_map/eq | solution.py:67
  7.1 0.9 %slice_bitcast_fusion.9 = (bf16[128,128]{1,0:T(8,128)(2,1)S(1)}, bf16[128,128]{1,0:T(8,128)(2,1)S(1)}, bf16[128,128]{1,0:T(8,128)(2,1)S(1)}, bf16[128,128]{1,0:T...) fusion(bf16[1,8,128,128]{3,2,1,0:T(8,128)(2,1)} %param.6), kind=kLoop, calls=%fused_computation.67 | loop fusion | bytes 524288 | tf_op jit(solution)/shard_map/jit(_where)/broadcast_in_dim | solution.py:70
  8.2 2.2 %all_gather.10 = bf16[2,8,128,128]{3,2,1,0:T(8,128)(2,1)S(1)} all-gather(bf16[1,8,128,128]{3,2,1,0:T(8,128)(2,1)S(1)} %select_select_fusion), channel_id=1, replica_groups=mesh['blk'=16,'rep'=2] {'rep'}, dimensions={0}, use_global_device_ids=true | all-gather | bytes 786432 | tf_op jit(solution)/shard_map/all_gather | solution.py:71
  11.0 2.0 %collective-permute-start = (bf16[128,512]{1,0:T(8,128)(2,1)S(1)}, bf16[128,512]{1,0:T(8,128)(2,1)}, u32[]{:S(2)}, u32[]{:S(2)}) collective-permute-start(bf16[128,512]{1,0:T(8,128)(2,1)S(1)} %pad_maximum_fusion.3), channel_id=1, source_target_pairs={{0,2},{2,0},{4,6},{6,4},{8,10},{10,8},{12,14},{14,12},{16,18},{18,... | collective-permute-start | bytes 393224 | tf_op jit(solution)/shard_map/ppermute | solution.py:28
  13.0 1.6 %collective-permute-start.4 = (bf16[128,512]{1,0:T(8,128)(2,1)S(1)}, bf16[128,512]{1,0:T(8,128)(2,1)}, u32[]{:S(2)}, u32[]{:S(2)}) collective-permute-start(bf16[128,512]{1,0:T(8,128)(2,1)S(1)} %pad_maximum_fusion.4), channel_id=1, source_target_pairs={{0,4},{2,6},{4,0},{6,2},{8,12},{10,14},{12,8},{14,10},{16,20},{18,... | collective-permute-start | bytes 393224 | tf_op jit(solution)/shard_map/ppermute | solution.py:28
  14.8 2.1 %collective-permute-done = bf16[128,512]{1,0:T(8,128)(2,1)} collective-permute-done((bf16[128,512]{1,0:T(8,128)(2,1)S(1)}, bf16[128,512]{1,0:T(8,128)(2,1)}, u32[]{:S(2)}, u32[]{:S(2)}) %collective-permute-start) | collective-permute-done | bytes 131104 | tf_op jit(solution)/shard_map/ppermute | solution.py:28
  16.9 2.7 %collective-permute-start.5 = (bf16[128,512]{1,0:T(8,128)(2,1)S(1)}, bf16[128,512]{1,0:T(8,128)(2,1)S(1)}, u32[]{:S(2)}, u32[]{:S(2)}) collective-permute-start(bf16[128,512]{1,0:T(8,128)(2,1)S(1)} %pad_maximum_fusion.5), channel_id=1, source_target_pairs={{0,6},{2,4},{4,2},{6,0},{8,14},{10,12},{12,10},{14,8},{16,22},{18,... | collective-permute-start | bytes 393224 | tf_op jit(solution)/shard_map/ppermute | solution.py:28
  20.3 3.7 %collective-permute-start.3 = (bf16[128,512]{1,0:T(8,128)(2,1)S(1)}, bf16[128,512]{1,0:T(8,128)(2,1)S(1)}, u32[]{:S(2)}, u32[]{:S(2)}) collective-permute-start(bf16[128,512]{1,0:T(8,128)(2,1)S(1)} %get-tuple-element.4), channel_id=1, source_target_pairs={{0,24},{2,26},{4,28},{6,30},{8,16},{10,18},{12,20},{14,22},{16,8},... | collective-permute-start | bytes 393224 | tf_op jit(solution)/shard_map/ppermute | solution.py:32
  24.0 0.8 %collective-permute-start.1 = (bf16[128,512]{1,0:T(8,128)(2,1)S(1)}, bf16[128,512]{1,0:T(8,128)(2,1)S(1)}, u32[]{:S(2)}, u32[]{:S(2)}) collective-permute-start(bf16[128,512]{1,0:T(8,128)(2,1)S(1)} %get-tuple-element.3), channel_id=1, source_target_pairs={{0,8},{2,10},{4,12},{6,14},{8,0},{10,2},{12,4},{14,6},{16,24},{18,... | collective-permute-start | bytes 393224 | tf_op jit(solution)/shard_map/ppermute | solution.py:32
  24.8 1.6 %convolution_convert_fusion = bf16[512,512]{1,0:T(8,128)(2,1)S(1)} fusion(bf16[128,512]{1,0:T(8,128)(2,1)} %collective-permute-done.13, bf16[128,512]{1,0:T(8,128)(2,1)} %collective-permute-done.12, bf16[128,512]{1,0:T(8,128)(2,1)} %collective-permute-done.11, bf16[128,512]{1,0:T(8,128)(2,1)S(1)} %constant_dynamic-slice_fusion, ...), kind=kOutput, calls=%fused_computation | convolution fusion | flops 274464768 | bytes 1572864 | tf_op jit(solution)/shard_map/dot_general | solution.py:49
  26.5 1.4 %collective-permute-start.17 = (bf16[512,128]{1,0:T(8,128)(2,1)S(1)}, bf16[512,128]{1,0:T(8,128)(2,1)S(1)}, u32[]{:S(2)}, u32[]{:S(2)}) collective-permute-start(bf16[512,128]{1,0:T(8,128)(2,1)S(1)} %get-tuple-element.5), channel_id=1, source_target_pairs={{0,8},{2,10},{4,12},{6,14},{8,0},{10,2},{12,4},{14,6},{16,24},{18,... | collective-permute-start | bytes 393224 | tf_op jit(solution)/shard_map/ppermute | solution.py:32
  27.9 2.4 %collective-permute-start.19 = (bf16[512,128]{1,0:T(8,128)(2,1)S(1)}, bf16[512,128]{1,0:T(8,128)(2,1)S(1)}, u32[]{:S(2)}, u32[]{:S(2)}) collective-permute-start(bf16[512,128]{1,0:T(8,128)(2,1)S(1)} %get-tuple-element.6), channel_id=1, source_target_pairs={{0,24},{2,26},{4,28},{6,30},{8,16},{10,18},{12,20},{14,22},{16,8},... | collective-permute-start | bytes 393224 | tf_op jit(solution)/shard_map/ppermute | solution.py:32
  30.3 3.3 %collective-permute-done.1 = bf16[128,512]{1,0:T(8,128)(2,1)S(1)} collective-permute-done((bf16[128,512]{1,0:T(8,128)(2,1)S(1)}, bf16[128,512]{1,0:T(8,128)(2,1)S(1)}, u32[]{:S(2)}, u32[]{:S(2)}) %collective-permute-start.1) | collective-permute-done | bytes 131104 | tf_op jit(solution)/shard_map/ppermute | solution.py:32
  33.6 1.2 %collective-permute-start.18 = (bf16[512,128]{1,0:T(8,128)(2,1)S(1)}, bf16[512,128]{1,0:T(8,128)(2,1)S(1)}, u32[]{:S(2)}, u32[]{:S(2)}) collective-permute-start(bf16[512,128]{1,0:T(8,128)(2,1)S(1)} %get-tuple-element.7), channel_id=1, source_target_pairs={{0,16},{2,18},{4,20},{6,22},{8,24},{10,26},{12,28},{14,30},{16,0},... | collective-permute-start | bytes 393224 | tf_op jit(solution)/shard_map/ppermute | solution.py:32
  34.8 4.7 %collective-permute-done.2 = bf16[128,512]{1,0:T(8,128)(2,1)S(1)} collective-permute-done((bf16[128,512]{1,0:T(8,128)(2,1)S(1)}, bf16[128,512]{1,0:T(8,128)(2,1)S(1)}, u32[]{:S(2)}, u32[]{:S(2)}) %collective-permute-start.2) | collective-permute-done | bytes 131104 | tf_op jit(solution)/shard_map/ppermute | solution.py:32
  39.5 1.5 %convolution_convert_fusion.1 = bf16[512,512]{1,0:T(8,128)(2,1)S(1)} fusion(bf16[128,512]{1,0:T(8,128)(2,1)S(1)} %collective-permute-done.3, bf16[128,512]{1,0:T(8,128)(2,1)S(1)} %collective-permute-done.2, bf16[128,512]{1,0:T(8,128)(2,1)S(1)} %collective-permute-done.1, bf16[128,512]{1,0:T(8,128)(2,1)S(1)} %get-tuple-element.4, ...), kind=kOutput, calls=%fused_computation.1 | convolution fusion | flops 274464768 | bytes 1572864 | tf_op jit(solution)/shard_map/dot_general | solution.py:49
  42.3 2.5 %collective-permute-start.8 = (bf16[128,512]{1,0:T(8,128)(2,1)S(1)}, bf16[128,512]{1,0:T(8,128)(2,1)S(1)}, u32[]{:S(2)}, u32[]{:S(2)}) collective-permute-start(bf16[128,512]{1,0:T(8,128)(2,1)S(1)} %pad_maximum_fusion.8), channel_id=1, source_target_pairs={{0,6},{2,4},{4,2},{6,0},{8,14},{10,12},{12,10},{14,8},{16,22},{18,... | collective-permute-start | bytes 393224 | tf_op jit(solution)/shard_map/ppermute | solution.py:28
  45.6 2.0 %all_gather.12 = bf16[1024,128]{1,0:T(8,128)(2,1)S(1)} all-gather(bf16[512,128]{1,0:T(8,128)(2,1)S(1)} %add_convert_fusion), channel_id=1, replica_groups=mesh['blk'=16,'rep'=2] {'rep'}, dimensions={0}, use_global_device_ids=true | all-gather | bytes 393216 | tf_op jit(solution)/shard_map/all_gather | solution.py:126
  47.6 1.1 %fusion = bf16[128,512]{1,0:T(8,128)(2,1)} fusion(bf16[1024,128]{1,0:T(8,128)(2,1)S(1)} %all_gather.12, bf16[1024,1024]{1,0:T(8,128)(2,1)S(1)} %copy-done, s32[]{:T(128)S(6)} %select_n.256, bf16[128,1024]{1,0:T(8,128)(2,1)S(1)} %copy-done.1), kind=kOutput, calls=%fused_computation.4 | convolution fusion | flops 134545408 | bytes 1573888 | tf_op jit(solution)/shard_map/dot_general | solution.py:49
  49.2 2.0 %all_gather.11 = bf16[256,512]{1,0:T(8,128)(2,1)S(1)} all-gather(bf16[128,512]{1,0:T(8,128)(2,1)S(1)} %fusion.14), channel_id=1, replica_groups=mesh['blk'=16,'rep'=2] {'rep'}, dimensions={0}, use_global_device_ids=true | all-gather | bytes 393216 | tf_op jit(solution)/shard_map/all_gather | solution.py:108
  51.6 0.7 %collective-permute-start.9 = (bf16[256,512]{1,0:T(8,128)(2,1)S(1)}, bf16[256,512]{1,0:T(8,128)(2,1)S(1)}, u32[]{:S(2)}, u32[]{:S(2)}) collective-permute-start(bf16[256,512]{1,0:T(8,128)(2,1)S(1)} %pad_maximum_fusion.2), channel_id=1, source_target_pairs={{0,2},{2,0},{4,6},{6,4},{8,10},{10,8},{12,14},{14,12},{16,18},{18,... | collective-permute-start | bytes 786440 | tf_op jit(solution)/shard_map/ppermute | solution.py:28
  52.3 1.3 %convolution_convert_fusion.2 = bf16[256,512]{1,0:T(8,128)(2,1)S(1)} fusion(bf16[256,512]{1,0:T(8,128)(2,1)S(1)} %all_gather.11, bf16[128,512]{1,0:T(8,128)(2,1)} %collective-permute-done.13, bf16[128,512]{1,0:T(8,128)(2,1)} %collective-permute-done.12, bf16[128,512]{1,0:T(8,128)(2,1)} %collective-permute-done.11, ...), kind=kOutput, calls=%fused_computation.2 | convolution fusion | flops 136445952 | bytes 1048576 | tf_op jit(solution)/shard_map/dot_general | solution.py:49
  53.7 2.0 %collective-permute-start.16 = (bf16[64,512]{1,0:T(8,128)(2,1)S(1)}, bf16[64,512]{1,0:T(8,128)(2,1)S(1)}, u32[]{:S(2)}, u32[]{:S(2)}) collective-permute-start(bf16[64,512]{1,0:T(8,128)(2,1)S(1)} %get-tuple-element.30), channel_id=1, source_target_pairs={{0,24},{2,26},{4,28},{6,30},{8,16},{10,18},{12,20},{14,22},{16,8},... | collective-permute-start | bytes 196616 | tf_op jit(solution)/shard_map/ppermute | solution.py:32
  55.8 1.4 %collective-permute-start.15 = (bf16[64,512]{1,0:T(8,128)(2,1)S(1)}, bf16[64,512]{1,0:T(8,128)(2,1)S(1)}, u32[]{:S(2)}, u32[]{:S(2)}) collective-permute-start(bf16[64,512]{1,0:T(8,128)(2,1)S(1)} %get-tuple-element.31), channel_id=1, source_target_pairs={{0,16},{2,18},{4,20},{6,22},{8,24},{10,26},{12,28},{14,30},{16,0},... | collective-permute-start | bytes 196616 | tf_op jit(solution)/shard_map/ppermute | solution.py:32
  57.2 2.8 %collective-permute-done.9 = bf16[256,512]{1,0:T(8,128)(2,1)S(1)} collective-permute-done((bf16[256,512]{1,0:T(8,128)(2,1)S(1)}, bf16[256,512]{1,0:T(8,128)(2,1)S(1)}, u32[]{:S(2)}, u32[]{:S(2)}) %collective-permute-start.9) | collective-permute-done | bytes 262176 | tf_op jit(solution)/shard_map/ppermute | solution.py:28
  60.0 0.8 %collective-permute-start.10 = (bf16[128,512]{1,0:T(8,128)(2,1)S(1)}, bf16[128,512]{1,0:T(8,128)(2,1)S(1)}, u32[]{:S(2)}, u32[]{:S(2)}) collective-permute-start(bf16[128,512]{1,0:T(8,128)(2,1)S(1)} %fusion.9), channel_id=1, source_target_pairs={{0,4},{2,6},{4,0},{6,2},{8,12},{10,14},{12,8},{14,10},{16,20},{18,... | collective-permute-start | bytes 393224 | tf_op jit(solution)/shard_map/ppermute | solution.py:28
  60.8 2.2 %collective-permute-done.15 = bf16[64,512]{1,0:T(8,128)(2,1)S(1)} collective-permute-done((bf16[64,512]{1,0:T(8,128)(2,1)S(1)}, bf16[64,512]{1,0:T(8,128)(2,1)S(1)}, u32[]{:S(2)}, u32[]{:S(2)}) %collective-permute-start.15) | collective-permute-done | bytes 65568 | tf_op jit(solution)/shard_map/ppermute | solution.py:32
  63.0 0.7 %fusion.18 = f32[64,512]{1,0:T(8,128)} fusion(bf16[64,512]{1,0:T(8,128)(2,1)S(1)} %collective-permute-done.16, bf16[64,512]{1,0:T(8,128)(2,1)S(1)} %collective-permute-done.15, bf16[64,512]{1,0:T(8,128)(2,1)S(1)} %collective-permute-done.14, bf16[4,64,512]{2,1,0:T(8,128)(2,1)S(1)} %bitcast.99, s32[]{:T(128)S(6)} %select_n.313), kind=kLoop, calls=%fused_computation.37 | loop fusion | flops 229376 | bytes 393220 | tf_op jit(solution)/shard_map/add | solution.py:111
  63.7 1.4 %collective-permute-done.10 = bf16[128,512]{1,0:T(8,128)(2,1)S(1)} collective-permute-done((bf16[128,512]{1,0:T(8,128)(2,1)S(1)}, bf16[128,512]{1,0:T(8,128)(2,1)S(1)}, u32[]{:S(2)}, u32[]{:S(2)}) %collective-permute-start.10) | collective-permute-done | bytes 131104 | tf_op jit(solution)/shard_map/ppermute | solution.py:28
  65.1 0.7 %fusion.11 = bf16[128,512]{1,0:T(8,128)(2,1)} fusion(f32[512,512]{1,0:T(8,128)S(1)} %get-tuple-element.59, bf16[128,512]{1,0:T(8,128)(2,1)S(1)} %collective-permute-done.10, bf16[256,512]{1,0:T(8,128)(2,1)S(1)} %collective-permute-done.9), kind=kLoop, calls=%fused_computation.19 | loop fusion | flops 327680 | bytes 655360 | tf_op jit(solution)/shard_map/convert_element_type | solution.py:124
  (55 shorter events, 5.5 us)
Async XLA Ops:
  0.6 14.1 %copy-start = (bf16[1024,1024]{1,0:T(8,128)(2,1)S(1)}, bf16[1024,1024]{1,0:T(8,128)(2,1)}, u32[]{:S(2)}) copy-start(bf16[1024,1024]{1,0:T(8,128)(2,1)} %param.8) | copy-start | bytes 6291460
  1.7 18.6 %collective-permute-start.13 = (bf16[128,512]{1,0:T(8,128)(2,1)S(1)}, bf16[128,512]{1,0:T(8,128)(2,1)}, u32[]{:S(2)}, u32[]{:S(2)}) collective-permute-start(bf16[128,512]{1,0:T(8,128)(2,1)S(1)} %constant_dynamic-slice_fusion), channel_id=1, source_target_pairs={{0,6},{2,4},{4,2},{6,0},{8,14},{10,12},{12,10},{14,8},{16,22},{18,... | collective-permute-start | bytes 393224 | tf_op jit(solution)/shard_map/ppermute | solution.py:28
  5.7 18.3 %collective-permute-start.12 = (bf16[128,512]{1,0:T(8,128)(2,1)S(1)}, bf16[128,512]{1,0:T(8,128)(2,1)}, u32[]{:S(2)}, u32[]{:S(2)}) collective-permute-start(bf16[128,512]{1,0:T(8,128)(2,1)S(1)} %constant_dynamic-slice_fusion), channel_id=1, source_target_pairs={{0,4},{2,6},{4,0},{6,2},{8,12},{10,14},{12,8},{14,10},{16,20},{18,... | collective-permute-start | bytes 393224 | tf_op jit(solution)/shard_map/ppermute | solution.py:28
  6.2 17.8 %collective-permute-start.11 = (bf16[128,512]{1,0:T(8,128)(2,1)S(1)}, bf16[128,512]{1,0:T(8,128)(2,1)}, u32[]{:S(2)}, u32[]{:S(2)}) collective-permute-start(bf16[128,512]{1,0:T(8,128)(2,1)S(1)} %constant_dynamic-slice_fusion), channel_id=1, source_target_pairs={{0,2},{2,0},{4,6},{6,4},{8,10},{10,8},{12,14},{14,12},{16,18},{18,... | collective-permute-start | bytes 393224 | tf_op jit(solution)/shard_map/ppermute | solution.py:28
  8.0 12.3 %copy-start.1 = (bf16[128,1024]{1,0:T(8,128)(2,1)S(1)}, bf16[128,1024]{1,0:T(8,128)(2,1)}, u32[]{:S(2)}) copy-start(bf16[128,1024]{1,0:T(8,128)(2,1)} %param.5) | copy-start | bytes 786436
  11.0 5.9 %collective-permute-start = (bf16[128,512]{1,0:T(8,128)(2,1)S(1)}, bf16[128,512]{1,0:T(8,128)(2,1)}, u32[]{:S(2)}, u32[]{:S(2)}) collective-permute-start(bf16[128,512]{1,0:T(8,128)(2,1)S(1)} %pad_maximum_fusion.3), channel_id=1, source_target_pairs={{0,2},{2,0},{4,6},{6,4},{8,10},{10,8},{12,14},{14,12},{16,18},{18,... | collective-permute-start | bytes 393224 | tf_op jit(solution)/shard_map/ppermute | solution.py:28
  13.0 11.8 %collective-permute-start.4 = (bf16[128,512]{1,0:T(8,128)(2,1)S(1)}, bf16[128,512]{1,0:T(8,128)(2,1)}, u32[]{:S(2)}, u32[]{:S(2)}) collective-permute-start(bf16[128,512]{1,0:T(8,128)(2,1)S(1)} %pad_maximum_fusion.4), channel_id=1, source_target_pairs={{0,4},{2,6},{4,0},{6,2},{8,12},{10,14},{12,8},{14,10},{16,20},{18,... | collective-permute-start | bytes 393224 | tf_op jit(solution)/shard_map/ppermute | solution.py:28
  16.9 7.9 %collective-permute-start.5 = (bf16[128,512]{1,0:T(8,128)(2,1)S(1)}, bf16[128,512]{1,0:T(8,128)(2,1)S(1)}, u32[]{:S(2)}, u32[]{:S(2)}) collective-permute-start(bf16[128,512]{1,0:T(8,128)(2,1)S(1)} %pad_maximum_fusion.5), channel_id=1, source_target_pairs={{0,6},{2,4},{4,2},{6,0},{8,14},{10,12},{12,10},{14,8},{16,22},{18,... | collective-permute-start | bytes 393224 | tf_op jit(solution)/shard_map/ppermute | solution.py:28
  20.3 14.5 %collective-permute-start.3 = (bf16[128,512]{1,0:T(8,128)(2,1)S(1)}, bf16[128,512]{1,0:T(8,128)(2,1)S(1)}, u32[]{:S(2)}, u32[]{:S(2)}) collective-permute-start(bf16[128,512]{1,0:T(8,128)(2,1)S(1)} %get-tuple-element.4), channel_id=1, source_target_pairs={{0,24},{2,26},{4,28},{6,30},{8,16},{10,18},{12,20},{14,22},{16,8},... | collective-permute-start | bytes 393224 | tf_op jit(solution)/shard_map/ppermute | solution.py:32
  24.0 15.5 %collective-permute-start.2 = (bf16[128,512]{1,0:T(8,128)(2,1)S(1)}, bf16[128,512]{1,0:T(8,128)(2,1)S(1)}, u32[]{:S(2)}, u32[]{:S(2)}) collective-permute-start(bf16[128,512]{1,0:T(8,128)(2,1)S(1)} %get-tuple-element.4), channel_id=1, source_target_pairs={{0,16},{2,18},{4,20},{6,22},{8,24},{10,26},{12,28},{14,30},{16,0},... | collective-permute-start | bytes 393224 | tf_op jit(solution)/shard_map/ppermute | solution.py:32
  24.0 9.6 %collective-permute-start.1 = (bf16[128,512]{1,0:T(8,128)(2,1)S(1)}, bf16[128,512]{1,0:T(8,128)(2,1)S(1)}, u32[]{:S(2)}, u32[]{:S(2)}) collective-permute-start(bf16[128,512]{1,0:T(8,128)(2,1)S(1)} %get-tuple-element.3), channel_id=1, source_target_pairs={{0,8},{2,10},{4,12},{6,14},{8,0},{10,2},{12,4},{14,6},{16,24},{18,... | collective-permute-start | bytes 393224 | tf_op jit(solution)/shard_map/ppermute | solution.py:32
  24.8 14.7 %copy-start.2 = (bf16[128,128]{1,0:T(8,128)(2,1)S(1)}, bf16[128,128]{1,0:T(8,128)(2,1)}, u32[]{:S(2)}) copy-start(bf16[128,128]{1,0:T(8,128)(2,1)} %get-tuple-element.24) | copy-start | bytes 98308
  26.5 15.8 %collective-permute-start.17 = (bf16[512,128]{1,0:T(8,128)(2,1)S(1)}, bf16[512,128]{1,0:T(8,128)(2,1)S(1)}, u32[]{:S(2)}, u32[]{:S(2)}) collective-permute-start(bf16[512,128]{1,0:T(8,128)(2,1)S(1)} %get-tuple-element.5), channel_id=1, source_target_pairs={{0,8},{2,10},{4,12},{6,14},{8,0},{10,2},{12,4},{14,6},{16,24},{18,... | collective-permute-start | bytes 393224 | tf_op jit(solution)/shard_map/ppermute | solution.py:32
  27.9 17.0 %collective-permute-start.19 = (bf16[512,128]{1,0:T(8,128)(2,1)S(1)}, bf16[512,128]{1,0:T(8,128)(2,1)S(1)}, u32[]{:S(2)}, u32[]{:S(2)}) collective-permute-start(bf16[512,128]{1,0:T(8,128)(2,1)S(1)} %get-tuple-element.6), channel_id=1, source_target_pairs={{0,24},{2,26},{4,28},{6,30},{8,16},{10,18},{12,20},{14,22},{16,8},... | collective-permute-start | bytes 393224 | tf_op jit(solution)/shard_map/ppermute | solution.py:32
  33.6 11.9 %collective-permute-start.18 = (bf16[512,128]{1,0:T(8,128)(2,1)S(1)}, bf16[512,128]{1,0:T(8,128)(2,1)S(1)}, u32[]{:S(2)}, u32[]{:S(2)}) collective-permute-start(bf16[512,128]{1,0:T(8,128)(2,1)S(1)} %get-tuple-element.7), channel_id=1, source_target_pairs={{0,16},{2,18},{4,20},{6,22},{8,24},{10,26},{12,28},{14,30},{16,0},... | collective-permute-start | bytes 393224 | tf_op jit(solution)/shard_map/ppermute | solution.py:32
  41.1 7.6 %collective-permute-start.7 = (bf16[128,512]{1,0:T(8,128)(2,1)S(1)}, bf16[128,512]{1,0:T(8,128)(2,1)S(1)}, u32[]{:S(2)}, u32[]{:S(2)}) collective-permute-start(bf16[128,512]{1,0:T(8,128)(2,1)S(1)} %pad_maximum_fusion.7), channel_id=1, source_target_pairs={{0,4},{2,6},{4,0},{6,2},{8,12},{10,14},{12,8},{14,10},{16,20},{18,... | collective-permute-start | bytes 393224 | tf_op jit(solution)/shard_map/ppermute | solution.py:28
  41.7 7.0 %collective-permute-start.6 = (bf16[128,512]{1,0:T(8,128)(2,1)S(1)}, bf16[128,512]{1,0:T(8,128)(2,1)S(1)}, u32[]{:S(2)}, u32[]{:S(2)}) collective-permute-start(bf16[128,512]{1,0:T(8,128)(2,1)S(1)} %pad_maximum_fusion.6), channel_id=1, source_target_pairs={{0,2},{2,0},{4,6},{6,4},{8,10},{10,8},{12,14},{14,12},{16,18},{18,... | collective-permute-start | bytes 393224 | tf_op jit(solution)/shard_map/ppermute | solution.py:28
  42.3 6.8 %collective-permute-start.8 = (bf16[128,512]{1,0:T(8,128)(2,1)S(1)}, bf16[128,512]{1,0:T(8,128)(2,1)S(1)}, u32[]{:S(2)}, u32[]{:S(2)}) collective-permute-start(bf16[128,512]{1,0:T(8,128)(2,1)S(1)} %pad_maximum_fusion.8), channel_id=1, source_target_pairs={{0,6},{2,4},{4,2},{6,0},{8,14},{10,12},{12,10},{14,8},{16,22},{18,... | collective-permute-start | bytes 393224 | tf_op jit(solution)/shard_map/ppermute | solution.py:28
  51.6 8.4 %collective-permute-start.9 = (bf16[256,512]{1,0:T(8,128)(2,1)S(1)}, bf16[256,512]{1,0:T(8,128)(2,1)S(1)}, u32[]{:S(2)}, u32[]{:S(2)}) collective-permute-start(bf16[256,512]{1,0:T(8,128)(2,1)S(1)} %pad_maximum_fusion.2), channel_id=1, source_target_pairs={{0,2},{2,0},{4,6},{6,4},{8,10},{10,8},{12,14},{14,12},{16,18},{18,... | collective-permute-start | bytes 786440 | tf_op jit(solution)/shard_map/ppermute | solution.py:28
  53.7 7.1 %collective-permute-start.14 = (bf16[64,512]{1,0:T(8,128)(2,1)S(1)}, bf16[64,512]{1,0:T(8,128)(2,1)S(1)}, u32[]{:S(2)}, u32[]{:S(2)}) collective-permute-start(bf16[64,512]{1,0:T(8,128)(2,1)S(1)} %get-tuple-element.29), channel_id=1, source_target_pairs={{0,8},{2,10},{4,12},{6,14},{8,0},{10,2},{12,4},{14,6},{16,24},{18,... | collective-permute-start | bytes 196616 | tf_op jit(solution)/shard_map/ppermute | solution.py:32
  53.7 7.1 %collective-permute-start.16 = (bf16[64,512]{1,0:T(8,128)(2,1)S(1)}, bf16[64,512]{1,0:T(8,128)(2,1)S(1)}, u32[]{:S(2)}, u32[]{:S(2)}) collective-permute-start(bf16[64,512]{1,0:T(8,128)(2,1)S(1)} %get-tuple-element.30), channel_id=1, source_target_pairs={{0,24},{2,26},{4,28},{6,30},{8,16},{10,18},{12,20},{14,22},{16,8},... | collective-permute-start | bytes 196616 | tf_op jit(solution)/shard_map/ppermute | solution.py:32
  55.8 7.2 %collective-permute-start.15 = (bf16[64,512]{1,0:T(8,128)(2,1)S(1)}, bf16[64,512]{1,0:T(8,128)(2,1)S(1)}, u32[]{:S(2)}, u32[]{:S(2)}) collective-permute-start(bf16[64,512]{1,0:T(8,128)(2,1)S(1)} %get-tuple-element.31), channel_id=1, source_target_pairs={{0,16},{2,18},{4,20},{6,22},{8,24},{10,26},{12,28},{14,30},{16,0},... | collective-permute-start | bytes 196616 | tf_op jit(solution)/shard_map/ppermute | solution.py:32
  60.0 5.0 %collective-permute-start.10 = (bf16[128,512]{1,0:T(8,128)(2,1)S(1)}, bf16[128,512]{1,0:T(8,128)(2,1)S(1)}, u32[]{:S(2)}, u32[]{:S(2)}) collective-permute-start(bf16[128,512]{1,0:T(8,128)(2,1)S(1)} %fusion.9), channel_id=1, source_target_pairs={{0,4},{2,6},{4,0},{6,2},{8,12},{10,14},{12,8},{14,10},{16,20},{18,... | collective-permute-start | bytes 393224 | tf_op jit(solution)/shard_map/ppermute | solution.py:28

commit v15 on v14

--- a/solution.py
+++ b/solution.py
@@ -52,8 +52,10 @@
         return value[:, index * tile_size : (index + 1) * tile_size]
 
     def after(value, other):
-        row = other[:1, :tile_size] * 0
-        return value + jnp.concatenate([row] * (value.shape[1] // tile_size), 1)
+        height, width = (min(a, b) for a, b in zip(value.shape, other.shape))
+        part = other[:height, :width].astype(value.dtype) * 0
+        part = jnp.concatenate([part] * (value.shape[1] // width), 1)
+        return value + jnp.concatenate([part] * (value.shape[0] // height), 0)
 
     def columns_of(value, index):
         return lax.dynamic_slice_in_dim(value, index * cols_here, cols_here, 1)
@@ -68,27 +70,26 @@
     ordered = jnp.zeros((section_span, tile_size, tile_size), bf16)
     for k in range(slots):
         ordered = jnp.where(hit[:, k, None, None], adj_vals[0, k][None], ordered)
-    everyone = lax.all_gather(ordered, "rep", axis=0)
-    row_block = outer_pos * side + inner_pos
+    arrived = [
+        along_inner(ordered[t * per_core : (t + 1) * per_core], t) for t in turns
+    ]
+    everyone = lax.all_gather(jnp.concatenate(arrived, 0), "rep", axis=0)
     rows = []
     for t in turns:
+        row_block = outer_pos * side + (inner_pos ^ t)
         row = []
         for e in turns:
-            column_block = (outer_pos ^ e) * side + (inner_pos ^ t)
+            column_block = (outer_pos ^ e) * side + inner_pos
             holder = ((row_block - column_block) & (blk_count - 1)) >> span_bits
             index = t * per_core + e % per_core
             piece = everyone[0, index]
             for r in range(1, rep_count):
                 piece = jnp.where(holder == r, everyone[r, index], piece)
             row.append(piece)
-        rows.append(along_inner(jnp.concatenate(row, 1), t))
+        rows.append(jnp.concatenate(row, 1))
     block = jnp.concatenate(rows, 0)
 
-    hidden_stack = [hidden_part]
-    for t in turns[1:]:
-        message = after(hidden_part, rows[1]) if t == 1 else hidden_part
-        hidden_stack.append(along_outer(message, t))
-    hidden_stack = jnp.concatenate(hidden_stack, 0)
+    hidden_stack = jnp.concatenate([along_outer(hidden_part, e) for e in turns], 0)
     grad_part = columns_of(cotangent, rep_pos)
     grad_stack = jnp.concatenate([along_inner(grad_part, t) for t in turns], 0)
 
@@ -102,8 +103,8 @@
         chosen = jnp.concatenate([lanes(chosen, u ^ t) for u in turns], 1)
         mixed_cols = mixed_cols + along_inner(chosen, t).astype(jnp.float32)
 
-    back = dot(grad_stack, block, ((0,), (0,))).astype(bf16)
-    back = sum(along_outer(lanes(back, e), e).astype(jnp.float32) for e in turns).astype(bf16)
+    back = after(dot(grad_stack, block, ((0,), (0,))), mixed).astype(bf16)
+    back = sum(along_outer(lanes(back, e), e).astype(jnp.float32) for e in turns)
 
     mixed_cols = lax.all_gather(mixed_cols.astype(bf16), "rep", axis=0, tiled=True)
     weight_part = dot(mixed_cols, grad_stack, ((1,), (0,))).astype(bf16)
@@ -123,6 +124,7 @@
         [out_part[t * tile_size : (t + 1) * tile_size] for t in turns], along_inner
     ).astype(bf16)
 
+    back = after(back, weight_part).astype(bf16)
     back_full = lax.all_gather(back, "rep", axis=0, tiled=True)
     w_rows = lax.dynamic_slice_in_dim(w_out, rep_pos * cols_here, cols_here, 0)
     grad_in = dot(back_full, w_rows, ((0,), (1,)))

time: 66.1 us -> 56.2 us (0.85)
  waiting for transfers between devices: 17.5 us -> 14.1 us
  matrix products: 5.89 us -> 2.71 us
  starting transfers between devices: 29 us -> 27 us
  local copies, waits for them, and re-layouts: 2.26 us -> 1.22 us
    ppermute x9, waiting for transfers between devices: 10.8 us -> 5.92 us  [along_outer(): return lax.ppermute(value, 'blk', pairs) if turn else value]
    dot_general x5, matrix products: 5.89 us -> 2.71 us  [dot(): lax.dot_general(lhs, rhs, (dims, ((), ())), preferred_element_type=jnp.fl...]
    ppermute x11, starting transfers between devices: 16 us -> 12.9 us  [along_inner(): return lax.ppermute(value, 'blk', pairs) if turn else value]
    ppermute x11, waiting for transfers between devices: 6.7 us -> 8.2 us  [along_inner(): return lax.ppermute(value, 'blk', pairs) if turn else value]
    ppermute x9, starting transfers between devices: 13 us -> 14.2 us  [along_outer(): return lax.ppermute(value, 'blk', pairs) if turn else value]
    max x0 -> x1, other arithmetic: none -> 1.08 us  [shards(): hidden_part = jnp.maximum(columns_of(hidden_pre, rep_pos), 0)]
    dynamic_slice x1, local copies, waits for them, and re-layouts: 1.06 us -> 0.02 us  [columns_of(): return lax.dynamic_slice_in_dim(value, index * cols_here, cols_here, 1)]
  transfers between devices with their start and end apart: 20 -> 20, of which waited for: 8 -> 6; matrix products, arithmetic and copies ran while one was open for 15% -> 11% of each run, Pallas kernels for 0% -> 0%
where the time goes in v15:
time: 56.2 us; the launch traced here: 56 us
  starting transfers between devices  27 us (48%)
  waiting for transfers between devices  14.1 us (25%)
  blocking collectives  6.17 us (11%)
  other arithmetic  3.85 us (7%)
  matrix products  2.71 us (5%)
  local copies, waits for them, and re-layouts  1.22 us (2%)
  between operations  0.9 us (2%)
    ppermute x9, starting transfers between devices, along_outer(): return lax.ppermute(value, 'blk', pairs) if turn else value  14.2 us
    ppermute x11, starting transfers between devices, along_inner(): return lax.ppermute(value, 'blk', pairs) if turn else value  12.9 us
    ppermute x11, waiting for transfers between devices, along_inner(): return lax.ppermute(value, 'blk', pairs) if turn else value  8.2 us
    ppermute x9, waiting for transfers between devices, along_outer(): return lax.ppermute(value, 'blk', pairs) if turn else value  5.92 us
    dot_general x5, matrix products, dot(): lax.dot_general(lhs, rhs, (dims, ((), ())), preferred_element_type=jnp.fl...  2.71 us
    all_gather x1, blocking collectives, shards(): everyone = lax.all_gather(jnp.concatenate(arrived, 0), 'rep', axis=0)  2.18 us
    all_gather x1, blocking collectives, shards(): lax.all_gather(mixed_cols.astype(bf16), 'rep', axis=0, tiled=True)  1.99 us
    all_gather x1, blocking collectives, shards(): back_full = lax.all_gather(back, 'rep', axis=0, tiled=True)  1.99 us
  transfers between devices with their start and end apart: 20, of which 6 were waited for; matrix products, arithmetic and copies ran while one was open for 11% of the time, Pallas kernels for 0%

profile of v15, /device:TPU:0, one launch (start us, length us, event | category | flops | bytes accessed | tf_op | source)
XLA Modules:
  0.0 56.0 jit_solution(5402225787021255515)
XLA Ops:
  0.7 1.1 %dynamic-slice_maximum_fusion = bf16[128,512]{1,0:T(8,128)(2,1)S(1)} fusion(bf16[128,1024]{1,0:T(8,128)(2,1)} %param.5, s32[]{:T(128)S(6)} %select_n.200), kind=kLoop, calls=%fused_computation.39 | loop fusion | flops 262144 | bytes 262148 | tf_op jit(solution)/shard_map/max | solution.py:63
  1.7 5.1 %collective-permute-start.2 = (bf16[128,512]{1,0:T(8,128)(2,1)S(1)}, bf16[128,512]{1,0:T(8,128)(2,1)S(1)}, u32[]{:S(2)}, u32[]{:S(2)}) collective-permute-start(bf16[128,512]{1,0:T(8,128)(2,1)S(1)} %dynamic-slice_maximum_fusion), channel_id=1, source_target_pairs={{0,24},{2,26},{4,28},{6,30},{8,16},{10,18},{12,20},{14,22},{16,8},... | collective-permute-start | bytes 393224 | tf_op jit(solution)/shard_map/ppermute | solution.py:32
  6.9 0.7 %add_bitcast_fusion = s32[8]{0:T(128)S(1)} fusion(s32[1,8]{1,0:T(1,128)} %param.7, s32[]{:T(128)S(6)} %shift_right_arithmetic.54, s32[]{:T(128)S(6)} %and.60), kind=kLoop, calls=%fused_computation.85 | loop fusion | flops 56 | bytes 72 | tf_op jit(solution)/shard_map/eq | solution.py:69
  7.6 0.9 %slice_bitcast_fusion.9 = (bf16[128,128]{1,0:T(8,128)(2,1)S(1)}, bf16[128,128]{1,0:T(8,128)(2,1)S(1)}, bf16[128,128]{1,0:T(8,128)(2,1)S(1)}, bf16[128,128]{1,0:T...) fusion(bf16[1,8,128,128]{3,2,1,0:T(8,128)(2,1)} %param.6), kind=kLoop, calls=%fused_computation.67 | loop fusion | bytes 524288 | tf_op jit(solution)/shard_map/jit(_where)/broadcast_in_dim | solution.py:72
  8.7 2.5 %collective-permute-start.5 = (bf16[2,128,128]{2,1,0:T(8,128)(2,1)S(1)}, bf16[2,128,128]{2,1,0:T(8,128)(2,1)S(1)}, u32[]{:S(2)}, u32[]{:S(2)}) collective-permute-start(bf16[2,128,128]{2,1,0:T(8,128)(2,1)S(1)} %get-tuple-element.31), channel_id=1, source_target_pairs={{0,6},{2,4},{4,2},{6,0},{8,14},{10,12},{12,10},{14,8},{16,22},{18,... | collective-permute-start | bytes 196616 | tf_op jit(solution)/shard_map/ppermute | solution.py:28
  11.2 0.5 collective-permute-start.4
  11.8 0.5 collective-permute-start.3
  12.4 1.7 %collective-permute-done.5 = bf16[2,128,128]{2,1,0:T(8,128)(2,1)S(1)} collective-permute-done((bf16[2,128,128]{2,1,0:T(8,128)(2,1)S(1)}, bf16[2,128,128]{2,1,0:T(8,128)(2,1)S(1)}, u32[]{:S(2)}, u32[]{:S(2)}) %collective-permute-start.5) | collective-permute-done | bytes 65568 | tf_op jit(solution)/shard_map/ppermute | solution.py:28
  14.1 0.6 %collective-permute-start = (bf16[128,512]{1,0:T(8,128)(2,1)S(1)}, bf16[128,512]{1,0:T(8,128)(2,1)S(1)}, u32[]{:S(2)}, u32[]{:S(2)}) collective-permute-start(bf16[128,512]{1,0:T(8,128)(2,1)S(1)} %dynamic-slice_maximum_fusion), channel_id=1, source_target_pairs={{0,8},{2,10},{4,12},{6,14},{8,0},{10,2},{12,4},{14,6},{16,24},{18,... | collective-permute-start | bytes 393224 | tf_op jit(solution)/shard_map/ppermute | solution.py:32
  14.7 0.8 %collective-permute-done.4 = bf16[2,128,128]{2,1,0:T(8,128)(2,1)S(1)} collective-permute-done((bf16[2,128,128]{2,1,0:T(8,128)(2,1)S(1)}, bf16[2,128,128]{2,1,0:T(8,128)(2,1)S(1)}, u32[]{:S(2)}, u32[]{:S(2)}) %collective-permute-start.4) | collective-permute-done | bytes 65568 | tf_op jit(solution)/shard_map/ppermute | solution.py:28
  15.5 1.8 %collective-permute-start.13 = (bf16[128,512]{1,0:T(8,128)(2,1)S(1)}, bf16[128,512]{1,0:T(8,128)(2,1)S(1)}, u32[]{:S(2)}, u32[]{:S(2)}) collective-permute-start(bf16[128,512]{1,0:T(8,128)(2,1)S(1)} %constant_dynamic-slice_fusion), channel_id=1, source_target_pairs={{0,6},{2,4},{4,2},{6,0},{8,14},{10,12},{12,10},{14,8},{16,22},{18,... | collective-permute-start | bytes 393224 | tf_op jit(solution)/shard_map/ppermute | solution.py:28
  17.3 1.1 %collective-permute-start.12 = (bf16[128,512]{1,0:T(8,128)(2,1)S(1)}, bf16[128,512]{1,0:T(8,128)(2,1)S(1)}, u32[]{:S(2)}, u32[]{:S(2)}) collective-permute-start(bf16[128,512]{1,0:T(8,128)(2,1)S(1)} %constant_dynamic-slice_fusion), channel_id=1, source_target_pairs={{0,4},{2,6},{4,0},{6,2},{8,12},{10,14},{12,8},{14,10},{16,20},{18,... | collective-permute-start | bytes 393224 | tf_op jit(solution)/shard_map/ppermute | solution.py:28
  18.5 2.2 %all-gather = bf16[16,128,128]{2,1,0:T(8,128)(2,1)S(1)} all-gather(bf16[8,128,128]{2,1,0:T(8,128)(2,1)S(1)} %pad_maximum_fusion.1), channel_id=2, replica_groups=mesh['blk'=16,'rep'=2] {'rep'}, dimensions={0}, use_global_device_ids=true | all-gather | bytes 786432 | tf_op jit(solution)/shard_map/all_gather | solution.py:76
  20.9 0.6 %collective-permute-start.11 = (bf16[128,512]{1,0:T(8,128)(2,1)S(1)}, bf16[128,512]{1,0:T(8,128)(2,1)S(1)}, u32[]{:S(2)}, u32[]{:S(2)}) collective-permute-start(bf16[128,512]{1,0:T(8,128)(2,1)S(1)} %constant_dynamic-slice_fusion), channel_id=1, source_target_pairs={{0,2},{2,0},{4,6},{6,4},{8,10},{10,8},{12,14},{14,12},{16,18},{18,... | collective-permute-start | bytes 393224 | tf_op jit(solution)/shard_map/ppermute | solution.py:28
  22.1 1.5 %collective-permute-start.7 = (bf16[128,512]{1,0:T(8,128)(2,1)S(1)}, bf16[128,512]{1,0:T(8,128)(2,1)S(1)}, u32[]{:S(2)}, u32[]{:S(2)}) collective-permute-start(bf16[128,512]{1,0:T(8,128)(2,1)S(1)} %pad_maximum_fusion.4), channel_id=1, source_target_pairs={{0,4},{2,6},{4,0},{6,2},{8,12},{10,14},{12,8},{14,10},{16,20},{18,... | collective-permute-start | bytes 393224 | tf_op jit(solution)/shard_map/ppermute | solution.py:28
  23.7 1.0 %collective-permute-start.6 = (bf16[128,512]{1,0:T(8,128)(2,1)S(1)}, bf16[128,512]{1,0:T(8,128)(2,1)S(1)}, u32[]{:S(2)}, u32[]{:S(2)}) collective-permute-start(bf16[128,512]{1,0:T(8,128)(2,1)S(1)} %pad_maximum_fusion.3), channel_id=1, source_target_pairs={{0,2},{2,0},{4,6},{6,4},{8,10},{10,8},{12,14},{14,12},{16,18},{18,... | collective-permute-start | bytes 393224 | tf_op jit(solution)/shard_map/ppermute | solution.py:28
  24.7 1.2 %collective-permute-start.8 = (bf16[128,512]{1,0:T(8,128)(2,1)S(1)}, bf16[128,512]{1,0:T(8,128)(2,1)S(1)}, u32[]{:S(2)}, u32[]{:S(2)}) collective-permute-start(bf16[128,512]{1,0:T(8,128)(2,1)S(1)} %pad_maximum_fusion.5), channel_id=1, source_target_pairs={{0,6},{2,4},{4,2},{6,0},{8,14},{10,12},{12,10},{14,8},{16,22},{18,... | collective-permute-start | bytes 393224 | tf_op jit(solution)/shard_map/ppermute | solution.py:28
  25.9 1.1 %collective-permute-done.11 = bf16[128,512]{1,0:T(8,128)(2,1)S(1)} collective-permute-done((bf16[128,512]{1,0:T(8,128)(2,1)S(1)}, bf16[128,512]{1,0:T(8,128)(2,1)S(1)}, u32[]{:S(2)}, u32[]{:S(2)}) %collective-permute-start.11) | collective-permute-done | bytes 131104 | tf_op jit(solution)/shard_map/ppermute | solution.py:28
  27.5 1.0 %collective-permute-start.17 = (bf16[512,128]{1,0:T(8,128)(2,1)S(1)}, bf16[512,128]{1,0:T(8,128)(2,1)S(1)}, u32[]{:S(2)}, u32[]{:S(2)}) collective-permute-start(bf16[512,128]{1,0:T(8,128)(2,1)S(1)} %get-tuple-element.3), channel_id=1, source_target_pairs={{0,8},{2,10},{4,12},{6,14},{8,0},{10,2},{12,4},{14,6},{16,24},{18,... | collective-permute-start | bytes 393224 | tf_op jit(solution)/shard_map/ppermute | solution.py:32
  28.6 2.8 %collective-permute-start.19 = (bf16[512,128]{1,0:T(8,128)(2,1)S(1)}, bf16[512,128]{1,0:T(8,128)(2,1)S(1)}, u32[]{:S(2)}, u32[]{:S(2)}) collective-permute-start(bf16[512,128]{1,0:T(8,128)(2,1)S(1)} %get-tuple-element.4), channel_id=1, source_target_pairs={{0,24},{2,26},{4,28},{6,30},{8,16},{10,18},{12,20},{14,22},{16,8},... | collective-permute-start | bytes 393224 | tf_op jit(solution)/shard_map/ppermute | solution.py:32
  31.6 0.8 %collective-permute-done.8 = bf16[128,512]{1,0:T(8,128)(2,1)S(1)} collective-permute-done((bf16[128,512]{1,0:T(8,128)(2,1)S(1)}, bf16[128,512]{1,0:T(8,128)(2,1)S(1)}, u32[]{:S(2)}, u32[]{:S(2)}) %collective-permute-start.8) | collective-permute-done | bytes 131104 | tf_op jit(solution)/shard_map/ppermute | solution.py:28
  32.5 2.0 %all_gather.14 = bf16[256,512]{1,0:T(8,128)(2,1)S(1)} all-gather(bf16[128,512]{1,0:T(8,128)(2,1)S(1)} %fusion.16), channel_id=1, replica_groups=mesh['blk'=16,'rep'=2] {'rep'}, dimensions={0}, use_global_device_ids=true | all-gather | bytes 393216 | tf_op jit(solution)/shard_map/all_gather | solution.py:109
  34.8 1.3 %collective-permute-start.14 = (bf16[64,512]{1,0:T(8,128)(2,1)S(1)}, bf16[64,512]{1,0:T(8,128)(2,1)S(1)}, u32[]{:S(2)}, u32[]{:S(2)}) collective-permute-start(bf16[64,512]{1,0:T(8,128)(2,1)S(1)} %get-tuple-element.27), channel_id=1, source_target_pairs={{0,8},{2,10},{4,12},{6,14},{8,0},{10,2},{12,4},{14,6},{16,24},{18,... | collective-permute-start | bytes 196616 | tf_op jit(solution)/shard_map/ppermute | solution.py:32
  36.1 2.5 %collective-permute-start.16 = (bf16[64,512]{1,0:T(8,128)(2,1)S(1)}, bf16[64,512]{1,0:T(8,128)(2,1)S(1)}, u32[]{:S(2)}, u32[]{:S(2)}) collective-permute-start(bf16[64,512]{1,0:T(8,128)(2,1)S(1)} %get-tuple-element.28), channel_id=1, source_target_pairs={{0,24},{2,26},{4,28},{6,30},{8,16},{10,18},{12,20},{14,22},{16,8},... | collective-permute-start | bytes 196616 | tf_op jit(solution)/shard_map/ppermute | solution.py:32
  39.5 1.0 %collective-permute-start.9 = (bf16[256,512]{1,0:T(8,128)(2,1)S(1)}, bf16[256,512]{1,0:T(8,128)(2,1)S(1)}, u32[]{:S(2)}, u32[]{:S(2)}) collective-permute-start(bf16[256,512]{1,0:T(8,128)(2,1)S(1)} %pad_maximum_fusion.2), channel_id=1, source_target_pairs={{0,2},{2,0},{4,6},{6,4},{8,10},{10,8},{12,14},{14,12},{16,18},{18,... | collective-permute-start | bytes 786440 | tf_op jit(solution)/shard_map/ppermute | solution.py:28
  40.5 5.9 %collective-permute-done.18 = bf16[512,128]{1,0:T(8,128)(2,1)S(1)} collective-permute-done((bf16[512,128]{1,0:T(8,128)(2,1)S(1)}, bf16[512,128]{1,0:T(8,128)(2,1)S(1)}, u32[]{:S(2)}, u32[]{:S(2)}) %collective-permute-start.18) | collective-permute-done | bytes 131104 | tf_op jit(solution)/shard_map/ppermute | solution.py:32
  46.5 2.0 %all_gather.15 = bf16[1024,128]{1,0:T(8,128)(2,1)S(1)} all-gather(bf16[512,128]{1,0:T(8,128)(2,1)S(1)} %fusion.13), channel_id=1, replica_groups=mesh['blk'=16,'rep'=2] {'rep'}, dimensions={0}, use_global_device_ids=true | all-gather | bytes 393216 | tf_op jit(solution)/shard_map/all_gather | solution.py:128
  48.5 1.1 %fusion.1 = bf16[128,512]{1,0:T(8,128)(2,1)} fusion(bf16[1024,128]{1,0:T(8,128)(2,1)S(1)} %all_gather.15, bf16[1024,1024]{1,0:T(8,128)(2,1)S(1)} %copy-done, s32[]{:T(128)S(6)} %select_n.200, bf16[128,1024]{1,0:T(8,128)(2,1)S(1)} %copy-done.1), kind=kOutput, calls=%fused_computation.5 | convolution fusion | flops 134545408 | bytes 1573888 | tf_op jit(solution)/shard_map/dot_general | solution.py:49
  49.7 1.1 %collective-permute-start.10 = (bf16[128,512]{1,0:T(8,128)(2,1)S(1)}, bf16[128,512]{1,0:T(8,128)(2,1)S(1)}, u32[]{:S(2)}, u32[]{:S(2)}) collective-permute-start(bf16[128,512]{1,0:T(8,128)(2,1)S(1)} %fusion.10), channel_id=1, source_target_pairs={{0,4},{2,6},{4,0},{6,2},{8,12},{10,14},{12,8},{14,10},{16,20},{18,... | collective-permute-start | bytes 393224 | tf_op jit(solution)/shard_map/ppermute | solution.py:28
  50.8 0.7 %fusion.20 = f32[64,512]{1,0:T(8,128)} fusion(bf16[64,512]{1,0:T(8,128)(2,1)S(1)} %collective-permute-done.16, bf16[64,512]{1,0:T(8,128)(2,1)S(1)} %collective-permute-done.15, bf16[64,512]{1,0:T(8,128)(2,1)S(1)} %collective-permute-done.14, bf16[4,64,512]{2,1,0:T(8,128)(2,1)S(1)} %bitcast.106, s32[]{:T(128)S(6)} %select_n.257), kind=kLoop, calls=%fused_computation.37 | loop fusion | flops 229376 | bytes 393220 | tf_op jit(solution)/shard_map/add | solution.py:112
  51.5 3.8 %collective-permute-done.10 = bf16[128,512]{1,0:T(8,128)(2,1)S(1)} collective-permute-done((bf16[128,512]{1,0:T(8,128)(2,1)S(1)}, bf16[128,512]{1,0:T(8,128)(2,1)S(1)}, u32[]{:S(2)}, u32[]{:S(2)}) %collective-permute-start.10) | collective-permute-done | bytes 131104 | tf_op jit(solution)/shard_map/ppermute | solution.py:28
  55.3 0.7 %fusion.12 = bf16[128,512]{1,0:T(8,128)(2,1)} fusion(f32[512,512]{1,0:T(8,128)S(1)} %get-tuple-element.61, bf16[128,512]{1,0:T(8,128)(2,1)S(1)} %collective-permute-done.10, bf16[256,512]{1,0:T(8,128)(2,1)S(1)} %collective-permute-done.9), kind=kLoop, calls=%fused_computation.20 | loop fusion | flops 327680 | bytes 655360 | tf_op jit(solution)/shard_map/convert_element_type | solution.py:125
  (54 shorter events, 3.3 us)
Async XLA Ops:
  0.6 11.7 %copy-start = (bf16[1024,1024]{1,0:T(8,128)(2,1)S(1)}, bf16[1024,1024]{1,0:T(8,128)(2,1)}, u32[]{:S(2)}) copy-start(bf16[1024,1024]{1,0:T(8,128)(2,1)} %param.8) | copy-start | bytes 6291460
  0.6 11.7 %copy-start.2 = (bf16[128,1024]{1,0:T(8,128)(2,1)S(1)}, bf16[128,1024]{1,0:T(8,128)(2,1)}, u32[]{:S(2)}) copy-start(bf16[128,1024]{1,0:T(8,128)(2,1)} %param.9) | copy-start | bytes 786436
  1.7 19.1 %collective-permute-start.2 = (bf16[128,512]{1,0:T(8,128)(2,1)S(1)}, bf16[128,512]{1,0:T(8,128)(2,1)S(1)}, u32[]{:S(2)}, u32[]{:S(2)}) collective-permute-start(bf16[128,512]{1,0:T(8,128)(2,1)S(1)} %dynamic-slice_maximum_fusion), channel_id=1, source_target_pairs={{0,24},{2,26},{4,28},{6,30},{8,16},{10,18},{12,20},{14,22},{16,8},... | collective-permute-start | bytes 393224 | tf_op jit(solution)/shard_map/ppermute | solution.py:32
  6.9 14.6 %collective-permute-start.1 = (bf16[128,512]{1,0:T(8,128)(2,1)S(1)}, bf16[128,512]{1,0:T(8,128)(2,1)S(1)}, u32[]{:S(2)}, u32[]{:S(2)}) collective-permute-start(bf16[128,512]{1,0:T(8,128)(2,1)S(1)} %dynamic-slice_maximum_fusion), channel_id=1, source_target_pairs={{0,16},{2,18},{4,20},{6,22},{8,24},{10,26},{12,28},{14,30},{16,0},... | collective-permute-start | bytes 393224 | tf_op jit(solution)/shard_map/ppermute | solution.py:32
  8.7 5.3 %collective-permute-start.5 = (bf16[2,128,128]{2,1,0:T(8,128)(2,1)S(1)}, bf16[2,128,128]{2,1,0:T(8,128)(2,1)S(1)}, u32[]{:S(2)}, u32[]{:S(2)}) collective-permute-start(bf16[2,128,128]{2,1,0:T(8,128)(2,1)S(1)} %get-tuple-element.31), channel_id=1, source_target_pairs={{0,6},{2,4},{4,2},{6,0},{8,14},{10,12},{12,10},{14,8},{16,22},{18,... | collective-permute-start | bytes 196616 | tf_op jit(solution)/shard_map/ppermute | solution.py:28
  11.2 4.3 %collective-permute-start.4 = (bf16[2,128,128]{2,1,0:T(8,128)(2,1)S(1)}, bf16[2,128,128]{2,1,0:T(8,128)(2,1)S(1)}, u32[]{:S(2)}, u32[]{:S(2)}) collective-permute-start(bf16[2,128,128]{2,1,0:T(8,128)(2,1)S(1)} %get-tuple-element.32), channel_id=1, source_target_pairs={{0,4},{2,6},{4,0},{6,2},{8,12},{10,14},{12,8},{14,10},{16,20},{18,... | collective-permute-start | bytes 196616 | tf_op jit(solution)/shard_map/ppermute | solution.py:28
  11.8 5.6 %collective-permute-start.3 = (bf16[2,128,128]{2,1,0:T(8,128)(2,1)S(1)}, bf16[2,128,128]{2,1,0:T(8,128)(2,1)S(1)}, u32[]{:S(2)}, u32[]{:S(2)}) collective-permute-start(bf16[2,128,128]{2,1,0:T(8,128)(2,1)S(1)} %get-tuple-element.33), channel_id=1, source_target_pairs={{0,2},{2,0},{4,6},{6,4},{8,10},{10,8},{12,14},{14,12},{16,18},{18,... | collective-permute-start | bytes 196616 | tf_op jit(solution)/shard_map/ppermute | solution.py:28
  14.1 7.4 %collective-permute-start = (bf16[128,512]{1,0:T(8,128)(2,1)S(1)}, bf16[128,512]{1,0:T(8,128)(2,1)S(1)}, u32[]{:S(2)}, u32[]{:S(2)}) collective-permute-start(bf16[128,512]{1,0:T(8,128)(2,1)S(1)} %dynamic-slice_maximum_fusion), channel_id=1, source_target_pairs={{0,8},{2,10},{4,12},{6,14},{8,0},{10,2},{12,4},{14,6},{16,24},{18,... | collective-permute-start | bytes 393224 | tf_op jit(solution)/shard_map/ppermute | solution.py:32
  15.5 9.1 %collective-permute-start.13 = (bf16[128,512]{1,0:T(8,128)(2,1)S(1)}, bf16[128,512]{1,0:T(8,128)(2,1)S(1)}, u32[]{:S(2)}, u32[]{:S(2)}) collective-permute-start(bf16[128,512]{1,0:T(8,128)(2,1)S(1)} %constant_dynamic-slice_fusion), channel_id=1, source_target_pairs={{0,6},{2,4},{4,2},{6,0},{8,14},{10,12},{12,10},{14,8},{16,22},{18,... | collective-permute-start | bytes 393224 | tf_op jit(solution)/shard_map/ppermute | solution.py:28
  17.3 8.6 %collective-permute-start.12 = (bf16[128,512]{1,0:T(8,128)(2,1)S(1)}, bf16[128,512]{1,0:T(8,128)(2,1)S(1)}, u32[]{:S(2)}, u32[]{:S(2)}) collective-permute-start(bf16[128,512]{1,0:T(8,128)(2,1)S(1)} %constant_dynamic-slice_fusion), channel_id=1, source_target_pairs={{0,4},{2,6},{4,0},{6,2},{8,12},{10,14},{12,8},{14,10},{16,20},{18,... | collective-permute-start | bytes 393224 | tf_op jit(solution)/shard_map/ppermute | solution.py:28
  20.9 6.1 %collective-permute-start.11 = (bf16[128,512]{1,0:T(8,128)(2,1)S(1)}, bf16[128,512]{1,0:T(8,128)(2,1)S(1)}, u32[]{:S(2)}, u32[]{:S(2)}) collective-permute-start(bf16[128,512]{1,0:T(8,128)(2,1)S(1)} %constant_dynamic-slice_fusion), channel_id=1, source_target_pairs={{0,2},{2,0},{4,6},{6,4},{8,10},{10,8},{12,14},{14,12},{16,18},{18,... | collective-permute-start | bytes 393224 | tf_op jit(solution)/shard_map/ppermute | solution.py:28
  22.1 9.3 %collective-permute-start.7 = (bf16[128,512]{1,0:T(8,128)(2,1)S(1)}, bf16[128,512]{1,0:T(8,128)(2,1)S(1)}, u32[]{:S(2)}, u32[]{:S(2)}) collective-permute-start(bf16[128,512]{1,0:T(8,128)(2,1)S(1)} %pad_maximum_fusion.4), channel_id=1, source_target_pairs={{0,4},{2,6},{4,0},{6,2},{8,12},{10,14},{12,8},{14,10},{16,20},{18,... | collective-permute-start | bytes 393224 | tf_op jit(solution)/shard_map/ppermute | solution.py:28
  23.7 8.0 %collective-permute-start.6 = (bf16[128,512]{1,0:T(8,128)(2,1)S(1)}, bf16[128,512]{1,0:T(8,128)(2,1)S(1)}, u32[]{:S(2)}, u32[]{:S(2)}) collective-permute-start(bf16[128,512]{1,0:T(8,128)(2,1)S(1)} %pad_maximum_fusion.3), channel_id=1, source_target_pairs={{0,2},{2,0},{4,6},{6,4},{8,10},{10,8},{12,14},{14,12},{16,18},{18,... | collective-permute-start | bytes 393224 | tf_op jit(solution)/shard_map/ppermute | solution.py:28
  24.7 7.7 %collective-permute-start.8 = (bf16[128,512]{1,0:T(8,128)(2,1)S(1)}, bf16[128,512]{1,0:T(8,128)(2,1)S(1)}, u32[]{:S(2)}, u32[]{:S(2)}) collective-permute-start(bf16[128,512]{1,0:T(8,128)(2,1)S(1)} %pad_maximum_fusion.5), channel_id=1, source_target_pairs={{0,6},{2,4},{4,2},{6,0},{8,14},{10,12},{12,10},{14,8},{16,22},{18,... | collective-permute-start | bytes 393224 | tf_op jit(solution)/shard_map/ppermute | solution.py:28
  27.5 11.5 %collective-permute-start.17 = (bf16[512,128]{1,0:T(8,128)(2,1)S(1)}, bf16[512,128]{1,0:T(8,128)(2,1)S(1)}, u32[]{:S(2)}, u32[]{:S(2)}) collective-permute-start(bf16[512,128]{1,0:T(8,128)(2,1)S(1)} %get-tuple-element.3), channel_id=1, source_target_pairs={{0,8},{2,10},{4,12},{6,14},{8,0},{10,2},{12,4},{14,6},{16,24},{18,... | collective-permute-start | bytes 393224 | tf_op jit(solution)/shard_map/ppermute | solution.py:32
  28.6 11.0 %collective-permute-start.19 = (bf16[512,128]{1,0:T(8,128)(2,1)S(1)}, bf16[512,128]{1,0:T(8,128)(2,1)S(1)}, u32[]{:S(2)}, u32[]{:S(2)}) collective-permute-start(bf16[512,128]{1,0:T(8,128)(2,1)S(1)} %get-tuple-element.4), channel_id=1, source_target_pairs={{0,24},{2,26},{4,28},{6,30},{8,16},{10,18},{12,20},{14,22},{16,8},... | collective-permute-start | bytes 393224 | tf_op jit(solution)/shard_map/ppermute | solution.py:32
  31.4 15.0 %collective-permute-start.18 = (bf16[512,128]{1,0:T(8,128)(2,1)S(1)}, bf16[512,128]{1,0:T(8,128)(2,1)S(1)}, u32[]{:S(2)}, u32[]{:S(2)}) collective-permute-start(bf16[512,128]{1,0:T(8,128)(2,1)S(1)} %get-tuple-element.5), channel_id=1, source_target_pairs={{0,16},{2,18},{4,20},{6,22},{8,24},{10,26},{12,28},{14,30},{16,0},... | collective-permute-start | bytes 393224 | tf_op jit(solution)/shard_map/ppermute | solution.py:32
  34.8 16.0 %collective-permute-start.14 = (bf16[64,512]{1,0:T(8,128)(2,1)S(1)}, bf16[64,512]{1,0:T(8,128)(2,1)S(1)}, u32[]{:S(2)}, u32[]{:S(2)}) collective-permute-start(bf16[64,512]{1,0:T(8,128)(2,1)S(1)} %get-tuple-element.27), channel_id=1, source_target_pairs={{0,8},{2,10},{4,12},{6,14},{8,0},{10,2},{12,4},{14,6},{16,24},{18,... | collective-permute-start | bytes 196616 | tf_op jit(solution)/shard_map/ppermute | solution.py:32
  36.1 14.6 %collective-permute-start.16 = (bf16[64,512]{1,0:T(8,128)(2,1)S(1)}, bf16[64,512]{1,0:T(8,128)(2,1)S(1)}, u32[]{:S(2)}, u32[]{:S(2)}) collective-permute-start(bf16[64,512]{1,0:T(8,128)(2,1)S(1)} %get-tuple-element.28), channel_id=1, source_target_pairs={{0,24},{2,26},{4,28},{6,30},{8,16},{10,18},{12,20},{14,22},{16,8},... | collective-permute-start | bytes 196616 | tf_op jit(solution)/shard_map/ppermute | solution.py:32
  38.7 9.8 %copy-start.1 = (bf16[128,1024]{1,0:T(8,128)(2,1)S(1)}, bf16[128,1024]{1,0:T(8,128)(2,1)}, u32[]{:S(2)}) copy-start(bf16[128,1024]{1,0:T(8,128)(2,1)} %param.5) | copy-start | bytes 786436
  39.1 11.7 %collective-permute-start.15 = (bf16[64,512]{1,0:T(8,128)(2,1)S(1)}, bf16[64,512]{1,0:T(8,128)(2,1)S(1)}, u32[]{:S(2)}, u32[]{:S(2)}) collective-permute-start(bf16[64,512]{1,0:T(8,128)(2,1)S(1)} %get-tuple-element.29), channel_id=1, source_target_pairs={{0,16},{2,18},{4,20},{6,22},{8,24},{10,26},{12,28},{14,30},{16,0},... | collective-permute-start | bytes 196616 | tf_op jit(solution)/shard_map/ppermute | solution.py:32
  39.5 10.1 %collective-permute-start.9 = (bf16[256,512]{1,0:T(8,128)(2,1)S(1)}, bf16[256,512]{1,0:T(8,128)(2,1)S(1)}, u32[]{:S(2)}, u32[]{:S(2)}) collective-permute-start(bf16[256,512]{1,0:T(8,128)(2,1)S(1)} %pad_maximum_fusion.2), channel_id=1, source_target_pairs={{0,2},{2,0},{4,6},{6,4},{8,10},{10,8},{12,14},{14,12},{16,18},{18,... | collective-permute-start | bytes 786440 | tf_op jit(solution)/shard_map/ppermute | solution.py:28
  49.7 5.6 %collective-permute-start.10 = (bf16[128,512]{1,0:T(8,128)(2,1)S(1)}, bf16[128,512]{1,0:T(8,128)(2,1)S(1)}, u32[]{:S(2)}, u32[]{:S(2)}) collective-permute-start(bf16[128,512]{1,0:T(8,128)(2,1)S(1)} %fusion.10), channel_id=1, source_target_pairs={{0,4},{2,6},{4,0},{6,2},{8,12},{10,14},{12,8},{14,10},{16,20},{18,... | collective-permute-start | bytes 393224 | tf_op jit(solution)/shard_map/ppermute | solution.py:28

commit v16 on v15

--- a/solution.py
+++ b/solution.py
@@ -21,7 +21,6 @@
     rows_here = feature_width // blk_count
     bf16 = jnp.bfloat16
     turns = range(side)
-    rising = [1 << b for b in range(bits)]
 
     def along_inner(value, turn):
         pairs = [(o * side + i, o * side + (i ^ turn)) for o in turns for i in turns]
@@ -30,20 +29,6 @@
     def along_outer(value, turn):
         pairs = [(o * side + i, (o ^ turn) * side + i) for o in turns for i in turns]
         return lax.ppermute(value, "blk", pairs) if turn else value
-
-    def halved(parts, move):
-        parts = dict(enumerate(parts))
-        size = parts[0].shape[0]
-        for bit in rising:
-            keys = [k for k in parts if not k & bit]
-            sent = jnp.concatenate([parts[k ^ bit].astype(bf16) for k in keys], 0)
-            got = move(sent, bit)
-            parts = {
-                k: parts[k].astype(jnp.float32)
-                + got[n * size : (n + 1) * size].astype(jnp.float32)
-                for n, k in enumerate(keys)
-            }
-        return parts[0]
 
     def dot(lhs, rhs, dims):
         return lax.dot_general(lhs, rhs, (dims, ((), ())), preferred_element_type=jnp.float32)
@@ -119,9 +104,10 @@
     w_share = w_out.reshape(side, side, rows_here, feature_width)
     w_share = lax.dynamic_index_in_dim(w_share, inner_pos, 1, keepdims=False)
     w_share = columns_of(w_share.reshape(side * rows_here, feature_width), rep_pos)
-    out_part = dot(mixed_cols, w_share, ((0,), (0,)))
-    out_part = halved(
-        [out_part[t * tile_size : (t + 1) * tile_size] for t in turns], along_inner
+    out_wide = dot(mixed_cols, w_share, ((0,), (0,))).astype(bf16)
+    out_part = sum(
+        along_inner(out_wide[t * tile_size : (t + 1) * tile_size], t).astype(jnp.float32)
+        for t in turns
     ).astype(bf16)
 
     back = after(back, weight_part).astype(bf16)

time: 56.2 us -> 61.3 us (1.091)
  waiting for transfers between devices: 14.1 us -> 17.8 us
  starting transfers between devices: 27 us -> 28.4 us
    ppermute x11 -> x12, waiting for transfers between devices: 8.2 us -> 10.5 us  [along_inner(): return lax.ppermute(value, 'blk', pairs) if turn else value]
    ppermute x11 -> x12, starting transfers between devices: 12.9 us -> 14.3 us  [along_inner(): return lax.ppermute(value, 'blk', pairs) if turn else value]
    ppermute x9, waiting for transfers between devices: 5.92 us -> 7.28 us  [along_outer(): return lax.ppermute(value, 'blk', pairs) if turn else value]
  transfers between devices with their start and end apart: 20 -> 21, of which waited for: 6 -> 8; matrix products, arithmetic and copies ran while one was open for 11% -> 10% of each run, Pallas kernels for 0% -> 0%
where the time goes in v16:
time: 61.3 us; the launch traced here: 61 us
  starting transfers between devices  28.4 us (46%)
  waiting for transfers between devices  17.8 us (29%)
  blocking collectives  6.17 us (10%)
  other arithmetic  3.81 us (6%)
  matrix products  2.71 us (4%)
  local copies, waits for them, and re-layouts  1.24 us (2%)
  between operations  0.9 us (1%)
    ppermute x12, starting transfers between devices, along_inner(): return lax.ppermute(value, 'blk', pairs) if turn else value  14.3 us
    ppermute x9, starting transfers between devices, along_outer(): return lax.ppermute(value, 'blk', pairs) if turn else value  14.1 us
    ppermute x12, waiting for transfers between devices, along_inner(): return lax.ppermute(value, 'blk', pairs) if turn else value  10.5 us
    ppermute x9, waiting for transfers between devices, along_outer(): return lax.ppermute(value, 'blk', pairs) if turn else value  7.28 us
    dot_general x5, matrix products, dot(): lax.dot_general(lhs, rhs, (dims, ((), ())), preferred_element_type=jnp.fl...  2.71 us
    all_gather x1, blocking collectives, shards(): everyone = lax.all_gather(jnp.concatenate(arrived, 0), 'rep', axis=0)  2.18 us
    all_gather x1, blocking collectives, shards(): lax.all_gather(mixed_cols.astype(bf16), 'rep', axis=0, tiled=True)  1.99 us
    all_gather x1, blocking collectives, shards(): back_full = lax.all_gather(back, 'rep', axis=0, tiled=True)  1.99 us
  transfers between devices with their start and end apart: 21, of which 8 were waited for; matrix products, arithmetic and copies ran while one was open for 10% of the time, Pallas kernels for 0%

profile of v16, /device:TPU:0, one launch (start us, length us, event | category | flops | bytes accessed | tf_op | source)
XLA Modules:
  0.0 61.0 jit_solution(14764437548127653311)
XLA Ops:
  0.7 1.1 %dynamic-slice_maximum_fusion = bf16[128,512]{1,0:T(8,128)(2,1)S(1)} fusion(bf16[128,1024]{1,0:T(8,128)(2,1)} %param.5, s32[]{:T(128)S(6)} %select_n.200), kind=kLoop, calls=%fused_computation.34 | loop fusion | flops 262144 | bytes 262148 | tf_op jit(solution)/shard_map/max | solution.py:48
  1.7 5.1 %collective-permute-start.2 = (bf16[128,512]{1,0:T(8,128)(2,1)S(1)}, bf16[128,512]{1,0:T(8,128)(2,1)S(1)}, u32[]{:S(2)}, u32[]{:S(2)}) collective-permute-start(bf16[128,512]{1,0:T(8,128)(2,1)S(1)} %dynamic-slice_maximum_fusion), channel_id=1, source_target_pairs={{0,24},{2,26},{4,28},{6,30},{8,16},{10,18},{12,20},{14,22},{16,8},... | collective-permute-start | bytes 393224 | tf_op jit(solution)/shard_map/ppermute | solution.py:31
  6.9 0.7 %add_bitcast_fusion = s32[8]{0:T(128)S(1)} fusion(s32[1,8]{1,0:T(1,128)} %param.7, s32[]{:T(128)S(6)} %shift_right_arithmetic.54, s32[]{:T(128)S(6)} %and.60), kind=kLoop, calls=%fused_computation.80 | loop fusion | flops 56 | bytes 72 | tf_op jit(solution)/shard_map/eq | solution.py:54
  7.6 0.9 %slice_bitcast_fusion.9 = (bf16[128,128]{1,0:T(8,128)(2,1)S(1)}, bf16[128,128]{1,0:T(8,128)(2,1)S(1)}, bf16[128,128]{1,0:T(8,128)(2,1)S(1)}, bf16[128,128]{1,0:T...) fusion(bf16[1,8,128,128]{3,2,1,0:T(8,128)(2,1)} %param.6), kind=kLoop, calls=%fused_computation.62 | loop fusion | bytes 524288 | tf_op jit(solution)/shard_map/jit(_where)/broadcast_in_dim | solution.py:57
  8.7 2.5 %collective-permute-start.5 = (bf16[2,128,128]{2,1,0:T(8,128)(2,1)S(1)}, bf16[2,128,128]{2,1,0:T(8,128)(2,1)S(1)}, u32[]{:S(2)}, u32[]{:S(2)}) collective-permute-start(bf16[2,128,128]{2,1,0:T(8,128)(2,1)S(1)} %get-tuple-element.32), channel_id=1, source_target_pairs={{0,6},{2,4},{4,2},{6,0},{8,14},{10,12},{12,10},{14,8},{16,22},{18,... | collective-permute-start | bytes 196616 | tf_op jit(solution)/shard_map/ppermute | solution.py:27
  12.4 1.7 %collective-permute-done.5 = bf16[2,128,128]{2,1,0:T(8,128)(2,1)S(1)} collective-permute-done((bf16[2,128,128]{2,1,0:T(8,128)(2,1)S(1)}, bf16[2,128,128]{2,1,0:T(8,128)(2,1)S(1)}, u32[]{:S(2)}, u32[]{:S(2)}) %collective-permute-start.5) | collective-permute-done | bytes 65568 | tf_op jit(solution)/shard_map/ppermute | solution.py:27
  14.1 0.6 %collective-permute-start = (bf16[128,512]{1,0:T(8,128)(2,1)S(1)}, bf16[128,512]{1,0:T(8,128)(2,1)S(1)}, u32[]{:S(2)}, u32[]{:S(2)}) collective-permute-start(bf16[128,512]{1,0:T(8,128)(2,1)S(1)} %dynamic-slice_maximum_fusion), channel_id=1, source_target_pairs={{0,8},{2,10},{4,12},{6,14},{8,0},{10,2},{12,4},{14,6},{16,24},{18,... | collective-permute-start | bytes 393224 | tf_op jit(solution)/shard_map/ppermute | solution.py:31
  14.7 0.8 %collective-permute-done.4 = bf16[2,128,128]{2,1,0:T(8,128)(2,1)S(1)} collective-permute-done((bf16[2,128,128]{2,1,0:T(8,128)(2,1)S(1)}, bf16[2,128,128]{2,1,0:T(8,128)(2,1)S(1)}, u32[]{:S(2)}, u32[]{:S(2)}) %collective-permute-start.4) | collective-permute-done | bytes 65568 | tf_op jit(solution)/shard_map/ppermute | solution.py:27
  15.5 1.8 %collective-permute-start.14 = (bf16[128,512]{1,0:T(8,128)(2,1)S(1)}, bf16[128,512]{1,0:T(8,128)(2,1)S(1)}, u32[]{:S(2)}, u32[]{:S(2)}) collective-permute-start(bf16[128,512]{1,0:T(8,128)(2,1)S(1)} %constant_dynamic-slice_fusion), channel_id=1, source_target_pairs={{0,6},{2,4},{4,2},{6,0},{8,14},{10,12},{12,10},{14,8},{16,22},{18,... | collective-permute-start | bytes 393224 | tf_op jit(solution)/shard_map/ppermute | solution.py:27
  17.3 1.1 %collective-permute-start.13 = (bf16[128,512]{1,0:T(8,128)(2,1)S(1)}, bf16[128,512]{1,0:T(8,128)(2,1)S(1)}, u32[]{:S(2)}, u32[]{:S(2)}) collective-permute-start(bf16[128,512]{1,0:T(8,128)(2,1)S(1)} %constant_dynamic-slice_fusion), channel_id=1, source_target_pairs={{0,4},{2,6},{4,0},{6,2},{8,12},{10,14},{12,8},{14,10},{16,20},{18,... | collective-permute-start | bytes 393224 | tf_op jit(solution)/shard_map/ppermute | solution.py:27
  18.5 2.2 %all-gather = bf16[16,128,128]{2,1,0:T(8,128)(2,1)S(1)} all-gather(bf16[8,128,128]{2,1,0:T(8,128)(2,1)S(1)} %pad_maximum_fusion.1), channel_id=2, replica_groups=mesh['blk'=16,'rep'=2] {'rep'}, dimensions={0}, use_global_device_ids=true | all-gather | bytes 786432 | tf_op jit(solution)/shard_map/all_gather | solution.py:61
  22.1 1.5 %collective-permute-start.7 = (bf16[128,512]{1,0:T(8,128)(2,1)S(1)}, bf16[128,512]{1,0:T(8,128)(2,1)S(1)}, u32[]{:S(2)}, u32[]{:S(2)}) collective-permute-start(bf16[128,512]{1,0:T(8,128)(2,1)S(1)} %pad_maximum_fusion.3), channel_id=1, source_target_pairs={{0,4},{2,6},{4,0},{6,2},{8,12},{10,14},{12,8},{14,10},{16,20},{18,... | collective-permute-start | bytes 393224 | tf_op jit(solution)/shard_map/ppermute | solution.py:27
  23.7 1.0 %collective-permute-start.6 = (bf16[128,512]{1,0:T(8,128)(2,1)S(1)}, bf16[128,512]{1,0:T(8,128)(2,1)S(1)}, u32[]{:S(2)}, u32[]{:S(2)}) collective-permute-start(bf16[128,512]{1,0:T(8,128)(2,1)S(1)} %pad_maximum_fusion.2), channel_id=1, source_target_pairs={{0,2},{2,0},{4,6},{6,4},{8,10},{10,8},{12,14},{14,12},{16,18},{18,... | collective-permute-start | bytes 393224 | tf_op jit(solution)/shard_map/ppermute | solution.py:27
  24.7 1.2 %collective-permute-start.8 = (bf16[128,512]{1,0:T(8,128)(2,1)S(1)}, bf16[128,512]{1,0:T(8,128)(2,1)S(1)}, u32[]{:S(2)}, u32[]{:S(2)}) collective-permute-start(bf16[128,512]{1,0:T(8,128)(2,1)S(1)} %pad_maximum_fusion.4), channel_id=1, source_target_pairs={{0,6},{2,4},{4,2},{6,0},{8,14},{10,12},{12,10},{14,8},{16,22},{18,... | collective-permute-start | bytes 393224 | tf_op jit(solution)/shard_map/ppermute | solution.py:27
  25.9 1.1 %collective-permute-done.12 = bf16[128,512]{1,0:T(8,128)(2,1)S(1)} collective-permute-done((bf16[128,512]{1,0:T(8,128)(2,1)S(1)}, bf16[128,512]{1,0:T(8,128)(2,1)S(1)}, u32[]{:S(2)}, u32[]{:S(2)}) %collective-permute-start.12) | collective-permute-done | bytes 131104 | tf_op jit(solution)/shard_map/ppermute | solution.py:27
  27.5 1.1 %collective-permute-start.18 = (bf16[512,128]{1,0:T(8,128)(2,1)S(1)}, bf16[512,128]{1,0:T(8,128)(2,1)S(1)}, u32[]{:S(2)}, u32[]{:S(2)}) collective-permute-start(bf16[512,128]{1,0:T(8,128)(2,1)S(1)} %get-tuple-element.3), channel_id=1, source_target_pairs={{0,8},{2,10},{4,12},{6,14},{8,0},{10,2},{12,4},{14,6},{16,24},{18,... | collective-permute-start | bytes 393224 | tf_op jit(solution)/shard_map/ppermute | solution.py:31
  28.6 2.8 %collective-permute-start.20 = (bf16[512,128]{1,0:T(8,128)(2,1)S(1)}, bf16[512,128]{1,0:T(8,128)(2,1)S(1)}, u32[]{:S(2)}, u32[]{:S(2)}) collective-permute-start(bf16[512,128]{1,0:T(8,128)(2,1)S(1)} %get-tuple-element.4), channel_id=1, source_target_pairs={{0,24},{2,26},{4,28},{6,30},{8,16},{10,18},{12,20},{14,22},{16,8},... | collective-permute-start | bytes 393224 | tf_op jit(solution)/shard_map/ppermute | solution.py:31
  31.6 0.8 %collective-permute-done.8 = bf16[128,512]{1,0:T(8,128)(2,1)S(1)} collective-permute-done((bf16[128,512]{1,0:T(8,128)(2,1)S(1)}, bf16[128,512]{1,0:T(8,128)(2,1)S(1)}, u32[]{:S(2)}, u32[]{:S(2)}) %collective-permute-start.8) | collective-permute-done | bytes 131104 | tf_op jit(solution)/shard_map/ppermute | solution.py:27
  32.5 2.0 %all_gather.14 = bf16[256,512]{1,0:T(8,128)(2,1)S(1)} all-gather(bf16[128,512]{1,0:T(8,128)(2,1)S(1)} %fusion.13), channel_id=1, replica_groups=mesh['blk'=16,'rep'=2] {'rep'}, dimensions={0}, use_global_device_ids=true | all-gather | bytes 393216 | tf_op jit(solution)/shard_map/all_gather | solution.py:94
  34.8 1.3 %collective-permute-start.15 = (bf16[64,512]{1,0:T(8,128)(2,1)S(1)}, bf16[64,512]{1,0:T(8,128)(2,1)S(1)}, u32[]{:S(2)}, u32[]{:S(2)}) collective-permute-start(bf16[64,512]{1,0:T(8,128)(2,1)S(1)} %get-tuple-element.28), channel_id=1, source_target_pairs={{0,8},{2,10},{4,12},{6,14},{8,0},{10,2},{12,4},{14,6},{16,24},{18,... | collective-permute-start | bytes 196616 | tf_op jit(solution)/shard_map/ppermute | solution.py:31
  36.1 2.5 %collective-permute-start.17 = (bf16[64,512]{1,0:T(8,128)(2,1)S(1)}, bf16[64,512]{1,0:T(8,128)(2,1)S(1)}, u32[]{:S(2)}, u32[]{:S(2)}) collective-permute-start(bf16[64,512]{1,0:T(8,128)(2,1)S(1)} %get-tuple-element.29), channel_id=1, source_target_pairs={{0,24},{2,26},{4,28},{6,30},{8,16},{10,18},{12,20},{14,22},{16,8},... | collective-permute-start | bytes 196616 | tf_op jit(solution)/shard_map/ppermute | solution.py:31
  39.1 7.3 %collective-permute-done.19 = bf16[512,128]{1,0:T(8,128)(2,1)S(1)} collective-permute-done((bf16[512,128]{1,0:T(8,128)(2,1)S(1)}, bf16[512,128]{1,0:T(8,128)(2,1)S(1)}, u32[]{:S(2)}, u32[]{:S(2)}) %collective-permute-start.19) | collective-permute-done | bytes 131104 | tf_op jit(solution)/shard_map/ppermute | solution.py:31
  46.5 2.0 %all_gather.15 = bf16[1024,128]{1,0:T(8,128)(2,1)S(1)} all-gather(bf16[512,128]{1,0:T(8,128)(2,1)S(1)} %fusion.10), channel_id=1, replica_groups=mesh['blk'=16,'rep'=2] {'rep'}, dimensions={0}, use_global_device_ids=true | all-gather | bytes 393216 | tf_op jit(solution)/shard_map/all_gather | solution.py:114
  48.9 1.2 %fusion.1 = bf16[128,512]{1,0:T(8,128)(2,1)} fusion(bf16[1024,128]{1,0:T(8,128)(2,1)S(1)} %all_gather.15, bf16[1024,1024]{1,0:T(8,128)(2,1)S(1)} %copy-done, s32[]{:T(128)S(6)} %select_n.200, bf16[128,1024]{1,0:T(8,128)(2,1)S(1)} %copy-done.1), kind=kOutput, calls=%fused_computation.6 | convolution fusion | flops 134545408 | bytes 1573888 | tf_op jit(solution)/shard_map/dot_general | solution.py:34
  50.0 0.9 %collective-permute-start.9 = (bf16[128,512]{1,0:T(8,128)(2,1)S(1)}, bf16[128,512]{1,0:T(8,128)(2,1)S(1)}, u32[]{:S(2)}, u32[]{:S(2)}) collective-permute-start(bf16[128,512]{1,0:T(8,128)(2,1)S(1)} %get-tuple-element.6), channel_id=1, source_target_pairs={{0,2},{2,0},{4,6},{6,4},{8,10},{10,8},{12,14},{14,12},{16,18},{18,... | collective-permute-start | bytes 393224 | tf_op jit(solution)/shard_map/ppermute | solution.py:27
  50.9 1.6 %collective-permute-start.11 = (bf16[128,512]{1,0:T(8,128)(2,1)S(1)}, bf16[128,512]{1,0:T(8,128)(2,1)S(1)}, u32[]{:S(2)}, u32[]{:S(2)}) collective-permute-start(bf16[128,512]{1,0:T(8,128)(2,1)S(1)} %get-tuple-element.7), channel_id=1, source_target_pairs={{0,6},{2,4},{4,2},{6,0},{8,14},{10,12},{12,10},{14,8},{16,22},{18,... | collective-permute-start | bytes 393224 | tf_op jit(solution)/shard_map/ppermute | solution.py:27
  52.5 1.0 %collective-permute-start.10 = (bf16[128,512]{1,0:T(8,128)(2,1)S(1)}, bf16[128,512]{1,0:T(8,128)(2,1)S(1)}, u32[]{:S(2)}, u32[]{:S(2)}) collective-permute-start(bf16[128,512]{1,0:T(8,128)(2,1)S(1)} %get-tuple-element.8), channel_id=1, source_target_pairs={{0,4},{2,6},{4,0},{6,2},{8,12},{10,14},{12,8},{14,10},{16,20},{18,... | collective-permute-start | bytes 393224 | tf_op jit(solution)/shard_map/ppermute | solution.py:27
  53.5 0.7 %fusion.16 = f32[64,512]{1,0:T(8,128)} fusion(bf16[64,512]{1,0:T(8,128)(2,1)S(1)} %collective-permute-done.17, bf16[64,512]{1,0:T(8,128)(2,1)S(1)} %collective-permute-done.16, bf16[64,512]{1,0:T(8,128)(2,1)S(1)} %collective-permute-done.15, bf16[4,64,512]{2,1,0:T(8,128)(2,1)S(1)} %bitcast.106, s32[]{:T(128)S(6)} %select_n.257), kind=kLoop, calls=%fused_computation.32 | loop fusion | flops 229376 | bytes 393220 | tf_op jit(solution)/shard_map/add | solution.py:97
  54.2 2.2 %collective-permute-done.9 = bf16[128,512]{1,0:T(8,128)(2,1)S(1)} collective-permute-done((bf16[128,512]{1,0:T(8,128)(2,1)S(1)}, bf16[128,512]{1,0:T(8,128)(2,1)S(1)}, u32[]{:S(2)}, u32[]{:S(2)}) %collective-permute-start.9) | collective-permute-done | bytes 131104 | tf_op jit(solution)/shard_map/ppermute | solution.py:27
  56.3 2.6 %collective-permute-done.11 = bf16[128,512]{1,0:T(8,128)(2,1)S(1)} collective-permute-done((bf16[128,512]{1,0:T(8,128)(2,1)S(1)}, bf16[128,512]{1,0:T(8,128)(2,1)S(1)}, u32[]{:S(2)}, u32[]{:S(2)}) %collective-permute-start.11) | collective-permute-done | bytes 131104 | tf_op jit(solution)/shard_map/ppermute | solution.py:27
  58.9 1.4 %collective-permute-done.10 = bf16[128,512]{1,0:T(8,128)(2,1)S(1)} collective-permute-done((bf16[128,512]{1,0:T(8,128)(2,1)S(1)}, bf16[128,512]{1,0:T(8,128)(2,1)S(1)}, u32[]{:S(2)}, u32[]{:S(2)}) %collective-permute-start.10) | collective-permute-done | bytes 131104 | tf_op jit(solution)/shard_map/ppermute | solution.py:27
  60.3 0.7 %add_convert_fusion = bf16[128,512]{1,0:T(8,128)(2,1)} fusion(bf16[128,512]{1,0:T(8,128)(2,1)S(1)} %collective-permute-done.11, bf16[128,512]{1,0:T(8,128)(2,1)S(1)} %collective-permute-done.10, bf16[128,512]{1,0:T(8,128)(2,1)S(1)} %collective-permute-done.9, bf16[512,512]{1,0:T(8,128)(2,1)S(1)} %convolution_convert_fusion.1), kind=kLoop, calls=%fused_computation.24 | loop fusion | flops 524288 | bytes 655360 | tf_op jit(solution)/shard_map/convert_element_type | solution.py:111
  (54 shorter events, 4.9 us)
Async XLA Ops:
  0.6 11.7 %copy-start = (bf16[1024,1024]{1,0:T(8,128)(2,1)S(1)}, bf16[1024,1024]{1,0:T(8,128)(2,1)}, u32[]{:S(2)}) copy-start(bf16[1024,1024]{1,0:T(8,128)(2,1)} %param.8) | copy-start | bytes 6291460
  0.6 11.7 %copy-start.2 = (bf16[128,1024]{1,0:T(8,128)(2,1)S(1)}, bf16[128,1024]{1,0:T(8,128)(2,1)}, u32[]{:S(2)}) copy-start(bf16[128,1024]{1,0:T(8,128)(2,1)} %param.9) | copy-start | bytes 786436
  1.7 19.1 %collective-permute-start.2 = (bf16[128,512]{1,0:T(8,128)(2,1)S(1)}, bf16[128,512]{1,0:T(8,128)(2,1)S(1)}, u32[]{:S(2)}, u32[]{:S(2)}) collective-permute-start(bf16[128,512]{1,0:T(8,128)(2,1)S(1)} %dynamic-slice_maximum_fusion), channel_id=1, source_target_pairs={{0,24},{2,26},{4,28},{6,30},{8,16},{10,18},{12,20},{14,22},{16,8},... | collective-permute-start | bytes 393224 | tf_op jit(solution)/shard_map/ppermute | solution.py:31
  6.9 14.6 %collective-permute-start.1 = (bf16[128,512]{1,0:T(8,128)(2,1)S(1)}, bf16[128,512]{1,0:T(8,128)(2,1)S(1)}, u32[]{:S(2)}, u32[]{:S(2)}) collective-permute-start(bf16[128,512]{1,0:T(8,128)(2,1)S(1)} %dynamic-slice_maximum_fusion), channel_id=1, source_target_pairs={{0,16},{2,18},{4,20},{6,22},{8,24},{10,26},{12,28},{14,30},{16,0},... | collective-permute-start | bytes 393224 | tf_op jit(solution)/shard_map/ppermute | solution.py:31
  8.7 5.3 %collective-permute-start.5 = (bf16[2,128,128]{2,1,0:T(8,128)(2,1)S(1)}, bf16[2,128,128]{2,1,0:T(8,128)(2,1)S(1)}, u32[]{:S(2)}, u32[]{:S(2)}) collective-permute-start(bf16[2,128,128]{2,1,0:T(8,128)(2,1)S(1)} %get-tuple-element.32), channel_id=1, source_target_pairs={{0,6},{2,4},{4,2},{6,0},{8,14},{10,12},{12,10},{14,8},{16,22},{18,... | collective-permute-start | bytes 196616 | tf_op jit(solution)/shard_map/ppermute | solution.py:27
  11.2 4.3 %collective-permute-start.4 = (bf16[2,128,128]{2,1,0:T(8,128)(2,1)S(1)}, bf16[2,128,128]{2,1,0:T(8,128)(2,1)S(1)}, u32[]{:S(2)}, u32[]{:S(2)}) collective-permute-start(bf16[2,128,128]{2,1,0:T(8,128)(2,1)S(1)} %get-tuple-element.33), channel_id=1, source_target_pairs={{0,4},{2,6},{4,0},{6,2},{8,12},{10,14},{12,8},{14,10},{16,20},{18,... | collective-permute-start | bytes 196616 | tf_op jit(solution)/shard_map/ppermute | solution.py:27
  11.8 5.6 %collective-permute-start.3 = (bf16[2,128,128]{2,1,0:T(8,128)(2,1)S(1)}, bf16[2,128,128]{2,1,0:T(8,128)(2,1)S(1)}, u32[]{:S(2)}, u32[]{:S(2)}) collective-permute-start(bf16[2,128,128]{2,1,0:T(8,128)(2,1)S(1)} %get-tuple-element.34), channel_id=1, source_target_pairs={{0,2},{2,0},{4,6},{6,4},{8,10},{10,8},{12,14},{14,12},{16,18},{18,... | collective-permute-start | bytes 196616 | tf_op jit(solution)/shard_map/ppermute | solution.py:27
  14.1 7.4 %collective-permute-start = (bf16[128,512]{1,0:T(8,128)(2,1)S(1)}, bf16[128,512]{1,0:T(8,128)(2,1)S(1)}, u32[]{:S(2)}, u32[]{:S(2)}) collective-permute-start(bf16[128,512]{1,0:T(8,128)(2,1)S(1)} %dynamic-slice_maximum_fusion), channel_id=1, source_target_pairs={{0,8},{2,10},{4,12},{6,14},{8,0},{10,2},{12,4},{14,6},{16,24},{18,... | collective-permute-start | bytes 393224 | tf_op jit(solution)/shard_map/ppermute | solution.py:31
  15.5 9.2 %collective-permute-start.14 = (bf16[128,512]{1,0:T(8,128)(2,1)S(1)}, bf16[128,512]{1,0:T(8,128)(2,1)S(1)}, u32[]{:S(2)}, u32[]{:S(2)}) collective-permute-start(bf16[128,512]{1,0:T(8,128)(2,1)S(1)} %constant_dynamic-slice_fusion), channel_id=1, source_target_pairs={{0,6},{2,4},{4,2},{6,0},{8,14},{10,12},{12,10},{14,8},{16,22},{18,... | collective-permute-start | bytes 393224 | tf_op jit(solution)/shard_map/ppermute | solution.py:27
  17.3 8.6 %collective-permute-start.13 = (bf16[128,512]{1,0:T(8,128)(2,1)S(1)}, bf16[128,512]{1,0:T(8,128)(2,1)S(1)}, u32[]{:S(2)}, u32[]{:S(2)}) collective-permute-start(bf16[128,512]{1,0:T(8,128)(2,1)S(1)} %constant_dynamic-slice_fusion), channel_id=1, source_target_pairs={{0,4},{2,6},{4,0},{6,2},{8,12},{10,14},{12,8},{14,10},{16,20},{18,... | collective-permute-start | bytes 393224 | tf_op jit(solution)/shard_map/ppermute | solution.py:27
  20.9 6.1 %collective-permute-start.12 = (bf16[128,512]{1,0:T(8,128)(2,1)S(1)}, bf16[128,512]{1,0:T(8,128)(2,1)S(1)}, u32[]{:S(2)}, u32[]{:S(2)}) collective-permute-start(bf16[128,512]{1,0:T(8,128)(2,1)S(1)} %constant_dynamic-slice_fusion), channel_id=1, source_target_pairs={{0,2},{2,0},{4,6},{6,4},{8,10},{10,8},{12,14},{14,12},{16,18},{18,... | collective-permute-start | bytes 393224 | tf_op jit(solution)/shard_map/ppermute | solution.py:27
  22.1 9.2 %collective-permute-start.7 = (bf16[128,512]{1,0:T(8,128)(2,1)S(1)}, bf16[128,512]{1,0:T(8,128)(2,1)S(1)}, u32[]{:S(2)}, u32[]{:S(2)}) collective-permute-start(bf16[128,512]{1,0:T(8,128)(2,1)S(1)} %pad_maximum_fusion.3), channel_id=1, source_target_pairs={{0,4},{2,6},{4,0},{6,2},{8,12},{10,14},{12,8},{14,10},{16,20},{18,... | collective-permute-start | bytes 393224 | tf_op jit(solution)/shard_map/ppermute | solution.py:27
  23.7 7.9 %collective-permute-start.6 = (bf16[128,512]{1,0:T(8,128)(2,1)S(1)}, bf16[128,512]{1,0:T(8,128)(2,1)S(1)}, u32[]{:S(2)}, u32[]{:S(2)}) collective-permute-start(bf16[128,512]{1,0:T(8,128)(2,1)S(1)} %pad_maximum_fusion.2), channel_id=1, source_target_pairs={{0,2},{2,0},{4,6},{6,4},{8,10},{10,8},{12,14},{14,12},{16,18},{18,... | collective-permute-start | bytes 393224 | tf_op jit(solution)/shard_map/ppermute | solution.py:27
  24.7 7.7 %collective-permute-start.8 = (bf16[128,512]{1,0:T(8,128)(2,1)S(1)}, bf16[128,512]{1,0:T(8,128)(2,1)S(1)}, u32[]{:S(2)}, u32[]{:S(2)}) collective-permute-start(bf16[128,512]{1,0:T(8,128)(2,1)S(1)} %pad_maximum_fusion.4), channel_id=1, source_target_pairs={{0,6},{2,4},{4,2},{6,0},{8,14},{10,12},{12,10},{14,8},{16,22},{18,... | collective-permute-start | bytes 393224 | tf_op jit(solution)/shard_map/ppermute | solution.py:27
  27.5 11.2 %collective-permute-start.18 = (bf16[512,128]{1,0:T(8,128)(2,1)S(1)}, bf16[512,128]{1,0:T(8,128)(2,1)S(1)}, u32[]{:S(2)}, u32[]{:S(2)}) collective-permute-start(bf16[512,128]{1,0:T(8,128)(2,1)S(1)} %get-tuple-element.3), channel_id=1, source_target_pairs={{0,8},{2,10},{4,12},{6,14},{8,0},{10,2},{12,4},{14,6},{16,24},{18,... | collective-permute-start | bytes 393224 | tf_op jit(solution)/shard_map/ppermute | solution.py:31
  28.6 10.6 %collective-permute-start.20 = (bf16[512,128]{1,0:T(8,128)(2,1)S(1)}, bf16[512,128]{1,0:T(8,128)(2,1)S(1)}, u32[]{:S(2)}, u32[]{:S(2)}) collective-permute-start(bf16[512,128]{1,0:T(8,128)(2,1)S(1)} %get-tuple-element.4), channel_id=1, source_target_pairs={{0,24},{2,26},{4,28},{6,30},{8,16},{10,18},{12,20},{14,22},{16,8},... | collective-permute-start | bytes 393224 | tf_op jit(solution)/shard_map/ppermute | solution.py:31
  31.4 15.0 %collective-permute-start.19 = (bf16[512,128]{1,0:T(8,128)(2,1)S(1)}, bf16[512,128]{1,0:T(8,128)(2,1)S(1)}, u32[]{:S(2)}, u32[]{:S(2)}) collective-permute-start(bf16[512,128]{1,0:T(8,128)(2,1)S(1)} %get-tuple-element.5), channel_id=1, source_target_pairs={{0,16},{2,18},{4,20},{6,22},{8,24},{10,26},{12,28},{14,30},{16,0},... | collective-permute-start | bytes 393224 | tf_op jit(solution)/shard_map/ppermute | solution.py:31
  34.8 14.1 %copy-start.1 = (bf16[128,1024]{1,0:T(8,128)(2,1)S(1)}, bf16[128,1024]{1,0:T(8,128)(2,1)}, u32[]{:S(2)}) copy-start(bf16[128,1024]{1,0:T(8,128)(2,1)} %param.5) | copy-start | bytes 786436
  34.8 17.7 %collective-permute-start.15 = (bf16[64,512]{1,0:T(8,128)(2,1)S(1)}, bf16[64,512]{1,0:T(8,128)(2,1)S(1)}, u32[]{:S(2)}, u32[]{:S(2)}) collective-permute-start(bf16[64,512]{1,0:T(8,128)(2,1)S(1)} %get-tuple-element.28), channel_id=1, source_target_pairs={{0,8},{2,10},{4,12},{6,14},{8,0},{10,2},{12,4},{14,6},{16,24},{18,... | collective-permute-start | bytes 196616 | tf_op jit(solution)/shard_map/ppermute | solution.py:31
  36.1 17.4 %collective-permute-start.17 = (bf16[64,512]{1,0:T(8,128)(2,1)S(1)}, bf16[64,512]{1,0:T(8,128)(2,1)S(1)}, u32[]{:S(2)}, u32[]{:S(2)}) collective-permute-start(bf16[64,512]{1,0:T(8,128)(2,1)S(1)} %get-tuple-element.29), channel_id=1, source_target_pairs={{0,24},{2,26},{4,28},{6,30},{8,16},{10,18},{12,20},{14,22},{16,8},... | collective-permute-start | bytes 196616 | tf_op jit(solution)/shard_map/ppermute | solution.py:31
  38.7 14.8 %collective-permute-start.16 = (bf16[64,512]{1,0:T(8,128)(2,1)S(1)}, bf16[64,512]{1,0:T(8,128)(2,1)S(1)}, u32[]{:S(2)}, u32[]{:S(2)}) collective-permute-start(bf16[64,512]{1,0:T(8,128)(2,1)S(1)} %get-tuple-element.30), channel_id=1, source_target_pairs={{0,16},{2,18},{4,20},{6,22},{8,24},{10,26},{12,28},{14,30},{16,0},... | collective-permute-start | bytes 196616 | tf_op jit(solution)/shard_map/ppermute | solution.py:31
  50.0 6.3 %collective-permute-start.9 = (bf16[128,512]{1,0:T(8,128)(2,1)S(1)}, bf16[128,512]{1,0:T(8,128)(2,1)S(1)}, u32[]{:S(2)}, u32[]{:S(2)}) collective-permute-start(bf16[128,512]{1,0:T(8,128)(2,1)S(1)} %get-tuple-element.6), channel_id=1, source_target_pairs={{0,2},{2,0},{4,6},{6,4},{8,10},{10,8},{12,14},{14,12},{16,18},{18,... | collective-permute-start | bytes 393224 | tf_op jit(solution)/shard_map/ppermute | solution.py:27
  50.9 8.1 %collective-permute-start.11 = (bf16[128,512]{1,0:T(8,128)(2,1)S(1)}, bf16[128,512]{1,0:T(8,128)(2,1)S(1)}, u32[]{:S(2)}, u32[]{:S(2)}) collective-permute-start(bf16[128,512]{1,0:T(8,128)(2,1)S(1)} %get-tuple-element.7), channel_id=1, source_target_pairs={{0,6},{2,4},{4,2},{6,0},{8,14},{10,12},{12,10},{14,8},{16,22},{18,... | collective-permute-start | bytes 393224 | tf_op jit(solution)/shard_map/ppermute | solution.py:27
  52.5 7.8 %collective-permute-start.10 = (bf16[128,512]{1,0:T(8,128)(2,1)S(1)}, bf16[128,512]{1,0:T(8,128)(2,1)S(1)}, u32[]{:S(2)}, u32[]{:S(2)}) collective-permute-start(bf16[128,512]{1,0:T(8,128)(2,1)S(1)} %get-tuple-element.8), channel_id=1, source_target_pairs={{0,4},{2,6},{4,0},{6,2},{8,12},{10,14},{12,8},{14,10},{16,20},{18,... | collective-permute-start | bytes 393224 | tf_op jit(solution)/shard_map/ppermute | solution.py:27

commit v17 on v16

--- a/solution.py
+++ b/solution.py
@@ -30,6 +30,9 @@
         pairs = [(o * side + i, (o ^ turn) * side + i) for o in turns for i in turns]
         return lax.ppermute(value, "blk", pairs) if turn else value
 
+    def to_other(value):
+        return lax.ppermute(value, "rep", [(0, 1), (1, 0)])
+
     def dot(lhs, rhs, dims):
         return lax.dot_general(lhs, rhs, (dims, ((), ())), preferred_element_type=jnp.float32)
 
@@ -58,7 +61,13 @@
     arrived = [
         along_inner(ordered[t * per_core : (t + 1) * per_core], t) for t in turns
     ]
-    everyone = lax.all_gather(jnp.concatenate(arrived, 0), "rep", axis=0)
+    arrived = jnp.concatenate(arrived, 0)
+    if rep_count == 2:
+        everyone = [arrived, to_other(arrived)]
+        first_holder = rep_pos
+    else:
+        everyone = lax.all_gather(arrived, "rep", axis=0)
+        first_holder = 0
     rows = []
     for t in turns:
         row_block = outer_pos * side + (inner_pos ^ t)
@@ -67,9 +76,9 @@
             column_block = (outer_pos ^ e) * side + inner_pos
             holder = ((row_block - column_block) & (blk_count - 1)) >> span_bits
             index = t * per_core + e % per_core
-            piece = everyone[0, index]
+            piece = everyone[0][index]
             for r in range(1, rep_count):
-                piece = jnp.where(holder == r, everyone[r, index], piece)
+                piece = jnp.where(holder ^ first_holder == r, everyone[r][index], piece)
             row.append(piece)
         rows.append(jnp.concatenate(row, 1))
     block = jnp.concatenate(rows, 0)
@@ -110,10 +119,19 @@
         for t in turns
     ).astype(bf16)
 
-    back = after(back, weight_part).astype(bf16)
-    back_full = lax.all_gather(back, "rep", axis=0, tiled=True)
-    w_rows = lax.dynamic_slice_in_dim(w_out, rep_pos * cols_here, cols_here, 0)
-    grad_in = dot(back_full, w_rows, ((0,), (1,)))
+    back = after(back, out_wide).astype(bf16)
+    w_rows = w_out.reshape(rep_count, cols_here, feature_width)
+    if rep_count == 2:
+        w_mine = columns_of(lax.dynamic_index_in_dim(w_rows, rep_pos, 0, keepdims=False), rep_pos)
+        w_other = columns_of(
+            lax.dynamic_index_in_dim(w_rows, 1 - rep_pos, 0, keepdims=False), rep_pos
+        )
+        grad_in = to_other(dot(back, w_other, ((0,), (1,))).astype(bf16)).astype(jnp.float32)
+        grad_in = grad_in + dot(back, w_mine, ((0,), (1,)))
+    else:
+        back_full = lax.all_gather(back, "rep", axis=0, tiled=True)
+        w_mine = lax.dynamic_index_in_dim(w_rows, rep_pos, 0, keepdims=False)
+        grad_in = dot(back_full, w_mine, ((0,), (1,)))
     pre_part = columns_of(hidden_pre, rep_pos)
     grad_pre = jnp.where(pre_part > 0, grad_in, 0.0).astype(bf16)
     return (out_part, grad_weight, grad_pre)

time: 61.3 us -> 65.7 us (1.072)
  waiting for transfers between devices: 17.8 us -> 24.6 us
  blocking collectives: 6.17 us -> 1.99 us
  matrix products: 2.71 us -> 5.99 us
  starting transfers between devices: 28.4 us -> 26.3 us
  local copies, waits for them, and re-layouts: 1.24 us -> 2.12 us
    ppermute x9, waiting for transfers between devices: 7.28 us -> 14.2 us  [along_outer(): return lax.ppermute(value, 'blk', pairs) if turn else value]
    all_gather x2 -> x0, blocking collectives: 4.18 us -> none  [the longest x1 2.18 us: shards(): everyone = lax.all_gather(jnp.concatenate(arrived, 0), 'rep', axis=0)]
    dot_general x5 -> x6, matrix products: 2.71 us -> 5.99 us  [dot(): lax.dot_general(lhs, rhs, (dims, ((), ())), preferred_element_type=jnp.fl...]
    ppermute x9, starting transfers between devices: 14.1 us -> 11.5 us  [along_outer(): return lax.ppermute(value, 'blk', pairs) if turn else value]
    dynamic_slice x1, local copies, waits for them, and re-layouts: 0.02 us -> 0.91 us  [columns_of(): return lax.dynamic_slice_in_dim(value, index * cols_here, cols_here, 1)]
  transfers between devices with their start and end apart: 21 -> 23, of which waited for: 8 -> 10; matrix products, arithmetic and copies ran while one was open for 10% -> 14% of each run, Pallas kernels for 0% -> 0%
where the time goes in v17:
time: 65.7 us; the launch traced here: 65.5 us
  starting transfers between devices  26.3 us (40%)
  waiting for transfers between devices  24.6 us (37%)
  matrix products  5.99 us (9%)
  other arithmetic  3.56 us (5%)
  local copies, waits for them, and re-layouts  2.12 us (3%)
  blocking collectives  1.99 us (3%)
  between operations  0.91 us (1%)
    ppermute x12, starting transfers between devices, along_inner(): return lax.ppermute(value, 'blk', pairs) if turn else value  14.6 us
    ppermute x9, waiting for transfers between devices, along_outer(): return lax.ppermute(value, 'blk', pairs) if turn else value  14.2 us
    ppermute x9, starting transfers between devices, along_outer(): return lax.ppermute(value, 'blk', pairs) if turn else value  11.5 us
    ppermute x12, waiting for transfers between devices, along_inner(): return lax.ppermute(value, 'blk', pairs) if turn else value  10.4 us
    dot_general x6, matrix products, dot(): lax.dot_general(lhs, rhs, (dims, ((), ())), preferred_element_type=jnp.fl...  5.99 us
    all_gather x1, blocking collectives, shards(): lax.all_gather(mixed_cols.astype(bf16), 'rep', axis=0, tiled=True)  1.99 us
  transfers between devices with their start and end apart: 23, of which 10 were waited for; matrix products, arithmetic and copies ran while one was open for 14% of the time, Pallas kernels for 0%

profile of v17, /device:TPU:0, one launch (start us, length us, event | category | flops | bytes accessed | tf_op | source)
XLA Modules:
  0.0 65.5 jit_solution(2230103887815277483)
XLA Ops:
  0.7 0.8 %add_bitcast_fusion = s32[8]{0:T(128)S(1)} fusion(s32[1,8]{1,0:T(1,128)} %param.7, s32[]{:T(128)S(6)} %shift_right_arithmetic.54, s32[]{:T(128)S(6)} %and.60), kind=kLoop, calls=%fused_computation.82 | loop fusion | flops 56 | bytes 72 | tf_op jit(solution)/shard_map/eq | solution.py:57
  1.6 0.9 %slice_bitcast_fusion.7 = (bf16[128,128]{1,0:T(8,128)(2,1)S(1)}, bf16[128,128]{1,0:T(8,128)(2,1)S(1)}, bf16[128,128]{1,0:T(8,128)(2,1)S(1)}, bf16[128,128]{1,0:T...) fusion(bf16[1,8,128,128]{3,2,1,0:T(8,128)(2,1)} %param.6), kind=kLoop, calls=%fused_computation.63 | loop fusion | bytes 524288 | tf_op jit(solution)/shard_map/jit(_where)/broadcast_in_dim | solution.py:60
  2.7 4.0 %collective-permute-start.5 = (bf16[2,128,128]{2,1,0:T(8,128)(2,1)S(1)}, bf16[2,128,128]{2,1,0:T(8,128)(2,1)S(1)}, u32[]{:S(2)}, u32[]{:S(2)}) collective-permute-start(bf16[2,128,128]{2,1,0:T(8,128)(2,1)S(1)} %get-tuple-element.33), channel_id=1, source_target_pairs={{0,6},{2,4},{4,2},{6,0},{8,14},{10,12},{12,10},{14,8},{16,22},{18,... | collective-permute-start | bytes 196616 | tf_op jit(solution)/shard_map/ppermute | solution.py:27
  7.3 1.6 %collective-permute-done.5 = bf16[2,128,128]{2,1,0:T(8,128)(2,1)S(1)} collective-permute-done((bf16[2,128,128]{2,1,0:T(8,128)(2,1)S(1)}, bf16[2,128,128]{2,1,0:T(8,128)(2,1)S(1)}, u32[]{:S(2)}, u32[]{:S(2)}) %collective-permute-start.5) | collective-permute-done | bytes 65568 | tf_op jit(solution)/shard_map/ppermute | solution.py:27
  8.9 2.0 %collective-permute-done.4 = bf16[2,128,128]{2,1,0:T(8,128)(2,1)S(1)} collective-permute-done((bf16[2,128,128]{2,1,0:T(8,128)(2,1)S(1)}, bf16[2,128,128]{2,1,0:T(8,128)(2,1)S(1)}, u32[]{:S(2)}, u32[]{:S(2)}) %collective-permute-start.4) | collective-permute-done | bytes 65568 | tf_op jit(solution)/shard_map/ppermute | solution.py:27
  11.6 0.7 %dynamic-slice_maximum_fusion = bf16[128,512]{1,0:T(8,128)(2,1)} fusion(bf16[128,1024]{1,0:T(8,128)(2,1)S(1)} %copy-done.1, s32[]{:T(128)S(6)} %select_n.224), kind=kLoop, calls=%fused_computation.36 | loop fusion | flops 262144 | bytes 262148 | tf_op jit(solution)/shard_map/max | solution.py:51
  12.2 3.6 %collective-permute-start.2 = (bf16[128,512]{1,0:T(8,128)(2,1)}, bf16[128,512]{1,0:T(8,128)(2,1)}, u32[]{:S(2)}, u32[]{:S(2)}) collective-permute-start(bf16[128,512]{1,0:T(8,128)(2,1)} %dynamic-slice_maximum_fusion), channel_id=1, source_target_pairs={{0,24},{2,26},{4,28},{6,30},{8,16},{10,18},{12,20},{14,22},{16,8},... | collective-permute-start | bytes 393224 | tf_op jit(solution)/shard_map/ppermute | solution.py:31
  15.8 0.8 %collective-permute-start = (bf16[128,512]{1,0:T(8,128)(2,1)}, bf16[128,512]{1,0:T(8,128)(2,1)}, u32[]{:S(2)}, u32[]{:S(2)}) collective-permute-start(bf16[128,512]{1,0:T(8,128)(2,1)} %dynamic-slice_maximum_fusion), channel_id=1, source_target_pairs={{0,8},{2,10},{4,12},{6,14},{8,0},{10,2},{12,4},{14,6},{16,24},{18,... | collective-permute-start | bytes 393224 | tf_op jit(solution)/shard_map/ppermute | solution.py:31
  16.6 0.9 %constant_dynamic-slice_fusion = bf16[128,512]{1,0:T(8,128)(2,1)S(1)} fusion(bf16[128,1024]{1,0:T(8,128)(2,1)} %param.9, s32[]{:T(128)S(6)} %select_n.224), kind=kLoop, calls=%fused_computation.67 | loop fusion | bytes 262148 | tf_op jit(solution)/shard_map/dynamic_slice | solution.py:49
  17.5 1.6 %collective-permute-start.15 = (bf16[128,512]{1,0:T(8,128)(2,1)S(1)}, bf16[128,512]{1,0:T(8,128)(2,1)}, u32[]{:S(2)}, u32[]{:S(2)}) collective-permute-start(bf16[128,512]{1,0:T(8,128)(2,1)S(1)} %constant_dynamic-slice_fusion), channel_id=1, source_target_pairs={{0,6},{2,4},{4,2},{6,0},{8,14},{10,12},{12,10},{14,8},{16,22},{18,... | collective-permute-start | bytes 393224 | tf_op jit(solution)/shard_map/ppermute | solution.py:27
  19.8 0.9 %collective-permute-done.2 = bf16[128,512]{1,0:T(8,128)(2,1)} collective-permute-done((bf16[128,512]{1,0:T(8,128)(2,1)}, bf16[128,512]{1,0:T(8,128)(2,1)}, u32[]{:S(2)}, u32[]{:S(2)}) %collective-permute-start.2) | collective-permute-done | bytes 131104 | tf_op jit(solution)/shard_map/ppermute | solution.py:31
  20.7 0.7 %collective-permute-start.13 = (bf16[128,512]{1,0:T(8,128)(2,1)S(1)}, bf16[128,512]{1,0:T(8,128)(2,1)S(1)}, u32[]{:S(2)}, u32[]{:S(2)}) collective-permute-start(bf16[128,512]{1,0:T(8,128)(2,1)S(1)} %constant_dynamic-slice_fusion), channel_id=1, source_target_pairs={{0,2},{2,0},{4,6},{6,4},{8,10},{10,8},{12,14},{14,12},{16,18},{18,... | collective-permute-start | bytes 393224 | tf_op jit(solution)/shard_map/ppermute | solution.py:27
  21.5 6.4 %collective-permute-done.1 = bf16[128,512]{1,0:T(8,128)(2,1)} collective-permute-done((bf16[128,512]{1,0:T(8,128)(2,1)}, bf16[128,512]{1,0:T(8,128)(2,1)}, u32[]{:S(2)}, u32[]{:S(2)}) %collective-permute-start.1) | collective-permute-done | bytes 131104 | tf_op jit(solution)/shard_map/ppermute | solution.py:31
  27.9 1.6 %convolution_convert_fusion = bf16[512,512]{1,0:T(8,128)(2,1)S(1)} fusion(bf16[512,512]{1,0:T(8,128)(2,1)S(1)} %maximum_maximum_fusion, bf16[128,512]{1,0:T(8,128)(2,1)} %collective-permute-done.2, bf16[128,512]{1,0:T(8,128)(2,1)} %collective-permute-done.1, bf16[128,512]{1,0:T(8,128)(2,1)} %collective-permute-done, ...), kind=kOutput, calls=%fused_computation.1 | convolution fusion | flops 270794752 | bytes 1572864 | tf_op jit(solution)/shard_map/dot_general | solution.py:37
  29.6 1.6 %collective-permute-start.8 = (bf16[128,512]{1,0:T(8,128)(2,1)S(1)}, bf16[128,512]{1,0:T(8,128)(2,1)S(1)}, u32[]{:S(2)}, u32[]{:S(2)}) collective-permute-start(bf16[128,512]{1,0:T(8,128)(2,1)S(1)} %pad_maximum_fusion.3), channel_id=1, source_target_pairs={{0,4},{2,6},{4,0},{6,2},{8,12},{10,14},{12,8},{14,10},{16,20},{18,... | collective-permute-start | bytes 393224 | tf_op jit(solution)/shard_map/ppermute | solution.py:27
  31.2 0.6 collective-permute-start.7
  31.9 1.5 %collective-permute-start.9 = (bf16[128,512]{1,0:T(8,128)(2,1)S(1)}, bf16[128,512]{1,0:T(8,128)(2,1)S(1)}, u32[]{:S(2)}, u32[]{:S(2)}) collective-permute-start(bf16[128,512]{1,0:T(8,128)(2,1)S(1)} %pad_maximum_fusion.4), channel_id=1, source_target_pairs={{0,6},{2,4},{4,2},{6,0},{8,14},{10,12},{12,10},{14,8},{16,22},{18,... | collective-permute-start | bytes 393224 | tf_op jit(solution)/shard_map/ppermute | solution.py:27
  33.4 1.4 %fusion = bf16[512,512]{1,0:T(8,128)(2,1)S(1)} fusion(bf16[512,512]{1,0:T(8,128)(2,1)S(1)} %maximum_maximum_fusion, bf16[512,512]{1,0:T(8,128)(2,1)S(1)} %convolution_convert_fusion, bf16[128,512]{1,0:T(8,128)(2,1)} %collective-permute-done.15, bf16[128,512]{1,0:T(8,128)(2,1)S(1)} %collective-permute-done.14, ...), kind=kOutput, calls=%fused_computation.3 | convolution fusion | flops 271581184 | bytes 2097152 | tf_op jit(solution)/shard_map/dot_general | solution.py:37
  34.9 2.5 %collective-permute-start.21 = (bf16[512,128]{1,0:T(8,128)(2,1)S(1)}, bf16[512,128]{1,0:T(8,128)(2,1)S(1)}, u32[]{:S(2)}, u32[]{:S(2)}) collective-permute-start(bf16[512,128]{1,0:T(8,128)(2,1)S(1)} %get-tuple-element.4), channel_id=1, source_target_pairs={{0,24},{2,26},{4,28},{6,30},{8,16},{10,18},{12,20},{14,22},{16,8},... | collective-permute-start | bytes 393224 | tf_op jit(solution)/shard_map/ppermute | solution.py:31
  37.5 0.9 %collective-permute-start.20 = (bf16[512,128]{1,0:T(8,128)(2,1)S(1)}, bf16[512,128]{1,0:T(8,128)(2,1)S(1)}, u32[]{:S(2)}, u32[]{:S(2)}) collective-permute-start(bf16[512,128]{1,0:T(8,128)(2,1)S(1)} %get-tuple-element.5), channel_id=1, source_target_pairs={{0,16},{2,18},{4,20},{6,22},{8,24},{10,26},{12,28},{14,30},{16,0},... | collective-permute-start | bytes 393224 | tf_op jit(solution)/shard_map/ppermute | solution.py:31
  39.0 2.0 %all_gather.3 = bf16[256,512]{1,0:T(8,128)(2,1)S(1)} all-gather(bf16[128,512]{1,0:T(8,128)(2,1)S(1)} %fusion.15), channel_id=1, replica_groups=mesh['blk'=16,'rep'=2] {'rep'}, dimensions={0}, use_global_device_ids=true | all-gather | bytes 393216 | tf_op jit(solution)/shard_map/all_gather | solution.py:103
  40.9 1.2 %convolution_convert_fusion.2 = bf16[256,512]{1,0:T(8,128)(2,1)S(1)} fusion(bf16[256,512]{1,0:T(8,128)(2,1)S(1)} %all_gather.3, bf16[128,512]{1,0:T(8,128)(2,1)} %collective-permute-done.15, bf16[128,512]{1,0:T(8,128)(2,1)S(1)} %collective-permute-done.14, bf16[128,512]{1,0:T(8,128)(2,1)S(1)} %collective-permute-done.13, ...), kind=kOutput, calls=%fused_computation.4 | convolution fusion | flops 136445952 | bytes 1048576 | tf_op jit(solution)/shard_map/dot_general | solution.py:37
  42.8 2.5 %collective-permute-start.18 = (bf16[64,512]{1,0:T(8,128)(2,1)S(1)}, bf16[64,512]{1,0:T(8,128)(2,1)S(1)}, u32[]{:S(2)}, u32[]{:S(2)}) collective-permute-start(bf16[64,512]{1,0:T(8,128)(2,1)S(1)} %get-tuple-element.30), channel_id=1, source_target_pairs={{0,24},{2,26},{4,28},{6,30},{8,16},{10,18},{12,20},{14,22},{16,8},... | collective-permute-start | bytes 196616 | tf_op jit(solution)/shard_map/ppermute | solution.py:31
  46.2 6.8 %collective-permute-done.20 = bf16[512,128]{1,0:T(8,128)(2,1)S(1)} collective-permute-done((bf16[512,128]{1,0:T(8,128)(2,1)S(1)}, bf16[512,128]{1,0:T(8,128)(2,1)S(1)}, u32[]{:S(2)}, u32[]{:S(2)}) %collective-permute-start.20) | collective-permute-done | bytes 131104 | tf_op jit(solution)/shard_map/ppermute | solution.py:31
  53.6 0.6 collective-permute-start.10
  54.2 2.4 %collective-permute-start.12 = (bf16[128,512]{1,0:T(8,128)(2,1)S(1)}, bf16[128,512]{1,0:T(8,128)(2,1)S(1)}, u32[]{:S(2)}, u32[]{:S(2)}) collective-permute-start(bf16[128,512]{1,0:T(8,128)(2,1)S(1)} %get-tuple-element.7), channel_id=1, source_target_pairs={{0,6},{2,4},{4,2},{6,0},{8,14},{10,12},{12,10},{14,8},{16,22},{18,... | collective-permute-start | bytes 393224 | tf_op jit(solution)/shard_map/ppermute | solution.py:27
  57.1 0.7 %fusion.18 = f32[64,512]{1,0:T(8,128)} fusion(bf16[64,512]{1,0:T(8,128)(2,1)S(1)} %collective-permute-done.18, bf16[64,512]{1,0:T(8,128)(2,1)S(1)} %collective-permute-done.17, bf16[64,512]{1,0:T(8,128)(2,1)S(1)} %collective-permute-done.16, bf16[4,64,512]{2,1,0:T(8,128)(2,1)S(1)} %bitcast.109, s32[]{:T(128)S(6)} %select_n.285), kind=kLoop, calls=%fused_computation.35 | loop fusion | flops 229376 | bytes 393220 | tf_op jit(solution)/shard_map/add | solution.py:106
  57.8 1.1 %select_convert_fusion = bf16[128,512]{1,0:T(8,128)(2,1)} fusion(bf16[128,512]{1,0:T(8,128)(2,1)S(1)} %collective-permute-done.22, bf16[128,1024]{1,0:T(8,128)(2,1)S(1)} %copy-done.1, s32[]{:T(128)S(6)} %select_n.224, bf16[512,128]{1,0:T(8,128)(2,1)S(1)} %add_convert_fusion, bf16[2,512,1024]{2,1,0:T(8,128)(2,1)S(1)} %bitcast.102, s32[]{:T(128)S(6)} %select_n.293, ...), kind=kOutput, calls=%fused_computation.25 | convolution fusion | flops 67567616 | bytes 1048588 | tf_op jit(solution)/shard_map/dot_general | solution.py:37
  58.9 1.0 %collective-permute-done.10 = bf16[128,512]{1,0:T(8,128)(2,1)S(1)} collective-permute-done((bf16[128,512]{1,0:T(8,128)(2,1)S(1)}, bf16[128,512]{1,0:T(8,128)(2,1)S(1)}, u32[]{:S(2)}, u32[]{:S(2)}) %collective-permute-start.10) | collective-permute-done | bytes 131104 | tf_op jit(solution)/shard_map/ppermute | solution.py:27
  59.9 3.4 %collective-permute-done.12 = bf16[128,512]{1,0:T(8,128)(2,1)S(1)} collective-permute-done((bf16[128,512]{1,0:T(8,128)(2,1)S(1)}, bf16[128,512]{1,0:T(8,128)(2,1)S(1)}, u32[]{:S(2)}, u32[]{:S(2)}) %collective-permute-start.12) | collective-permute-done | bytes 131104 | tf_op jit(solution)/shard_map/ppermute | solution.py:27
  63.4 1.4 %collective-permute-done.11 = bf16[128,512]{1,0:T(8,128)(2,1)S(1)} collective-permute-done((bf16[128,512]{1,0:T(8,128)(2,1)S(1)}, bf16[128,512]{1,0:T(8,128)(2,1)S(1)}, u32[]{:S(2)}, u32[]{:S(2)}) %collective-permute-start.11) | collective-permute-done | bytes 131104 | tf_op jit(solution)/shard_map/ppermute | solution.py:27
  64.7 0.7 %add_convert_fusion.1 = bf16[128,512]{1,0:T(8,128)(2,1)} fusion(bf16[128,512]{1,0:T(8,128)(2,1)S(1)} %collective-permute-done.12, bf16[128,512]{1,0:T(8,128)(2,1)S(1)} %collective-permute-done.11, bf16[128,512]{1,0:T(8,128)(2,1)S(1)} %collective-permute-done.10, bf16[512,512]{1,0:T(8,128)(2,1)S(1)} %convolution_convert_fusion.1), kind=kLoop, calls=%fused_computation.27 | loop fusion | flops 524288 | bytes 655360 | tf_op jit(solution)/shard_map/convert_element_type | solution.py:120
  (54 shorter events, 5.7 us)
Async XLA Ops:
  0.6 18.5 %copy-start = (bf16[1024,1024]{1,0:T(8,128)(2,1)S(1)}, bf16[1024,1024]{1,0:T(8,128)(2,1)}, u32[]{:S(2)}) copy-start(bf16[1024,1024]{1,0:T(8,128)(2,1)} %param.8) | copy-start | bytes 6291460
  0.6 10.9 %copy-start.1 = (bf16[128,1024]{1,0:T(8,128)(2,1)S(1)}, bf16[128,1024]{1,0:T(8,128)(2,1)}, u32[]{:S(2)}) copy-start(bf16[128,1024]{1,0:T(8,128)(2,1)} %param.5) | copy-start | bytes 786436
  2.7 6.2 %collective-permute-start.5 = (bf16[2,128,128]{2,1,0:T(8,128)(2,1)S(1)}, bf16[2,128,128]{2,1,0:T(8,128)(2,1)S(1)}, u32[]{:S(2)}, u32[]{:S(2)}) collective-permute-start(bf16[2,128,128]{2,1,0:T(8,128)(2,1)S(1)} %get-tuple-element.33), channel_id=1, source_target_pairs={{0,6},{2,4},{4,2},{6,0},{8,14},{10,12},{12,10},{14,8},{16,22},{18,... | collective-permute-start | bytes 196616 | tf_op jit(solution)/shard_map/ppermute | solution.py:27
  6.7 4.3 %collective-permute-start.4 = (bf16[2,128,128]{2,1,0:T(8,128)(2,1)S(1)}, bf16[2,128,128]{2,1,0:T(8,128)(2,1)S(1)}, u32[]{:S(2)}, u32[]{:S(2)}) collective-permute-start(bf16[2,128,128]{2,1,0:T(8,128)(2,1)S(1)} %get-tuple-element.34), channel_id=1, source_target_pairs={{0,4},{2,6},{4,0},{6,2},{8,12},{10,14},{12,8},{14,10},{16,20},{18,... | collective-permute-start | bytes 196616 | tf_op jit(solution)/shard_map/ppermute | solution.py:27
  7.2 4.3 %collective-permute-start.3 = (bf16[2,128,128]{2,1,0:T(8,128)(2,1)S(1)}, bf16[2,128,128]{2,1,0:T(8,128)(2,1)S(1)}, u32[]{:S(2)}, u32[]{:S(2)}) collective-permute-start(bf16[2,128,128]{2,1,0:T(8,128)(2,1)S(1)} %get-tuple-element.35), channel_id=1, source_target_pairs={{0,2},{2,0},{4,6},{6,4},{8,10},{10,8},{12,14},{14,12},{16,18},{18,... | collective-permute-start | bytes 196616 | tf_op jit(solution)/shard_map/ppermute | solution.py:27
  11.5 7.7 %collective-permute-start.6 = (bf16[8,128,128]{2,1,0:T(8,128)(2,1)S(1)}, bf16[8,128,128]{2,1,0:T(8,128)(2,1)S(1)}, u32[]{:S(2)}, u32[]{:S(2)}) collective-permute-start(bf16[8,128,128]{2,1,0:T(8,128)(2,1)S(1)} %pad_maximum_fusion.1), channel_id=1, source_target_pairs={{0,1},{1,0},{2,3},{3,2},{4,5},{5,4},{6,7},{7,6},{8,9},{9,8},{10,11... | collective-permute-start | bytes 786440 | tf_op jit(solution)/shard_map/ppermute | solution.py:34
  12.2 8.5 %collective-permute-start.2 = (bf16[128,512]{1,0:T(8,128)(2,1)}, bf16[128,512]{1,0:T(8,128)(2,1)}, u32[]{:S(2)}, u32[]{:S(2)}) collective-permute-start(bf16[128,512]{1,0:T(8,128)(2,1)} %dynamic-slice_maximum_fusion), channel_id=1, source_target_pairs={{0,24},{2,26},{4,28},{6,30},{8,16},{10,18},{12,20},{14,22},{16,8},... | collective-permute-start | bytes 393224 | tf_op jit(solution)/shard_map/ppermute | solution.py:31
  15.8 12.0 %collective-permute-start.1 = (bf16[128,512]{1,0:T(8,128)(2,1)}, bf16[128,512]{1,0:T(8,128)(2,1)}, u32[]{:S(2)}, u32[]{:S(2)}) collective-permute-start(bf16[128,512]{1,0:T(8,128)(2,1)} %dynamic-slice_maximum_fusion), channel_id=1, source_target_pairs={{0,16},{2,18},{4,20},{6,22},{8,24},{10,26},{12,28},{14,30},{16,0},... | collective-permute-start | bytes 393224 | tf_op jit(solution)/shard_map/ppermute | solution.py:31
  15.8 12.0 %collective-permute-start = (bf16[128,512]{1,0:T(8,128)(2,1)}, bf16[128,512]{1,0:T(8,128)(2,1)}, u32[]{:S(2)}, u32[]{:S(2)}) collective-permute-start(bf16[128,512]{1,0:T(8,128)(2,1)} %dynamic-slice_maximum_fusion), channel_id=1, source_target_pairs={{0,8},{2,10},{4,12},{6,14},{8,0},{10,2},{12,4},{14,6},{16,24},{18,... | collective-permute-start | bytes 393224 | tf_op jit(solution)/shard_map/ppermute | solution.py:31
  17.5 14.3 %collective-permute-start.15 = (bf16[128,512]{1,0:T(8,128)(2,1)S(1)}, bf16[128,512]{1,0:T(8,128)(2,1)}, u32[]{:S(2)}, u32[]{:S(2)}) collective-permute-start(bf16[128,512]{1,0:T(8,128)(2,1)S(1)} %constant_dynamic-slice_fusion), channel_id=1, source_target_pairs={{0,6},{2,4},{4,2},{6,0},{8,14},{10,12},{12,10},{14,8},{16,22},{18,... | collective-permute-start | bytes 393224 | tf_op jit(solution)/shard_map/ppermute | solution.py:27
  19.2 14.2 %collective-permute-start.14 = (bf16[128,512]{1,0:T(8,128)(2,1)S(1)}, bf16[128,512]{1,0:T(8,128)(2,1)S(1)}, u32[]{:S(2)}, u32[]{:S(2)}) collective-permute-start(bf16[128,512]{1,0:T(8,128)(2,1)S(1)} %constant_dynamic-slice_fusion), channel_id=1, source_target_pairs={{0,4},{2,6},{4,0},{6,2},{8,12},{10,14},{12,8},{14,10},{16,20},{18,... | collective-permute-start | bytes 393224 | tf_op jit(solution)/shard_map/ppermute | solution.py:27
  20.7 12.6 %collective-permute-start.13 = (bf16[128,512]{1,0:T(8,128)(2,1)S(1)}, bf16[128,512]{1,0:T(8,128)(2,1)S(1)}, u32[]{:S(2)}, u32[]{:S(2)}) collective-permute-start(bf16[128,512]{1,0:T(8,128)(2,1)S(1)} %constant_dynamic-slice_fusion), channel_id=1, source_target_pairs={{0,2},{2,0},{4,6},{6,4},{8,10},{10,8},{12,14},{14,12},{16,18},{18,... | collective-permute-start | bytes 393224 | tf_op jit(solution)/shard_map/ppermute | solution.py:27
  29.6 7.8 %collective-permute-start.8 = (bf16[128,512]{1,0:T(8,128)(2,1)S(1)}, bf16[128,512]{1,0:T(8,128)(2,1)S(1)}, u32[]{:S(2)}, u32[]{:S(2)}) collective-permute-start(bf16[128,512]{1,0:T(8,128)(2,1)S(1)} %pad_maximum_fusion.3), channel_id=1, source_target_pairs={{0,4},{2,6},{4,0},{6,2},{8,12},{10,14},{12,8},{14,10},{16,20},{18,... | collective-permute-start | bytes 393224 | tf_op jit(solution)/shard_map/ppermute | solution.py:27
  31.2 7.1 %collective-permute-start.7 = (bf16[128,512]{1,0:T(8,128)(2,1)S(1)}, bf16[128,512]{1,0:T(8,128)(2,1)S(1)}, u32[]{:S(2)}, u32[]{:S(2)}) collective-permute-start(bf16[128,512]{1,0:T(8,128)(2,1)S(1)} %pad_maximum_fusion.2), channel_id=1, source_target_pairs={{0,2},{2,0},{4,6},{6,4},{8,10},{10,8},{12,14},{14,12},{16,18},{18,... | collective-permute-start | bytes 393224 | tf_op jit(solution)/shard_map/ppermute | solution.py:27
  31.9 7.0 %collective-permute-start.9 = (bf16[128,512]{1,0:T(8,128)(2,1)S(1)}, bf16[128,512]{1,0:T(8,128)(2,1)S(1)}, u32[]{:S(2)}, u32[]{:S(2)}) collective-permute-start(bf16[128,512]{1,0:T(8,128)(2,1)S(1)} %pad_maximum_fusion.4), channel_id=1, source_target_pairs={{0,6},{2,4},{4,2},{6,0},{8,14},{10,12},{12,10},{14,8},{16,22},{18,... | collective-permute-start | bytes 393224 | tf_op jit(solution)/shard_map/ppermute | solution.py:27
  34.8 10.8 %collective-permute-start.19 = (bf16[512,128]{1,0:T(8,128)(2,1)S(1)}, bf16[512,128]{1,0:T(8,128)(2,1)S(1)}, u32[]{:S(2)}, u32[]{:S(2)}) collective-permute-start(bf16[512,128]{1,0:T(8,128)(2,1)S(1)} %get-tuple-element.3), channel_id=1, source_target_pairs={{0,8},{2,10},{4,12},{6,14},{8,0},{10,2},{12,4},{14,6},{16,24},{18,... | collective-permute-start | bytes 393224 | tf_op jit(solution)/shard_map/ppermute | solution.py:31
  34.9 11.3 %collective-permute-start.21 = (bf16[512,128]{1,0:T(8,128)(2,1)S(1)}, bf16[512,128]{1,0:T(8,128)(2,1)S(1)}, u32[]{:S(2)}, u32[]{:S(2)}) collective-permute-start(bf16[512,128]{1,0:T(8,128)(2,1)S(1)} %get-tuple-element.4), channel_id=1, source_target_pairs={{0,24},{2,26},{4,28},{6,30},{8,16},{10,18},{12,20},{14,22},{16,8},... | collective-permute-start | bytes 393224 | tf_op jit(solution)/shard_map/ppermute | solution.py:31
  37.5 15.5 %collective-permute-start.20 = (bf16[512,128]{1,0:T(8,128)(2,1)S(1)}, bf16[512,128]{1,0:T(8,128)(2,1)S(1)}, u32[]{:S(2)}, u32[]{:S(2)}) collective-permute-start(bf16[512,128]{1,0:T(8,128)(2,1)S(1)} %get-tuple-element.5), channel_id=1, source_target_pairs={{0,16},{2,18},{4,20},{6,22},{8,24},{10,26},{12,28},{14,30},{16,0},... | collective-permute-start | bytes 393224 | tf_op jit(solution)/shard_map/ppermute | solution.py:31
  42.2 12.0 %collective-permute-start.16 = (bf16[64,512]{1,0:T(8,128)(2,1)S(1)}, bf16[64,512]{1,0:T(8,128)(2,1)S(1)}, u32[]{:S(2)}, u32[]{:S(2)}) collective-permute-start(bf16[64,512]{1,0:T(8,128)(2,1)S(1)} %get-tuple-element.29), channel_id=1, source_target_pairs={{0,8},{2,10},{4,12},{6,14},{8,0},{10,2},{12,4},{14,6},{16,24},{18,... | collective-permute-start | bytes 196616 | tf_op jit(solution)/shard_map/ppermute | solution.py:31
  42.8 13.9 %collective-permute-start.18 = (bf16[64,512]{1,0:T(8,128)(2,1)S(1)}, bf16[64,512]{1,0:T(8,128)(2,1)S(1)}, u32[]{:S(2)}, u32[]{:S(2)}) collective-permute-start(bf16[64,512]{1,0:T(8,128)(2,1)S(1)} %get-tuple-element.30), channel_id=1, source_target_pairs={{0,24},{2,26},{4,28},{6,30},{8,16},{10,18},{12,20},{14,22},{16,8},... | collective-permute-start | bytes 196616 | tf_op jit(solution)/shard_map/ppermute | solution.py:31
  45.6 11.5 %collective-permute-start.17 = (bf16[64,512]{1,0:T(8,128)(2,1)S(1)}, bf16[64,512]{1,0:T(8,128)(2,1)S(1)}, u32[]{:S(2)}, u32[]{:S(2)}) collective-permute-start(bf16[64,512]{1,0:T(8,128)(2,1)S(1)} %get-tuple-element.31), channel_id=1, source_target_pairs={{0,16},{2,18},{4,20},{6,22},{8,24},{10,26},{12,28},{14,30},{16,0},... | collective-permute-start | bytes 196616 | tf_op jit(solution)/shard_map/ppermute | solution.py:31
  53.5 4.3 %collective-permute-start.22 = (bf16[128,512]{1,0:T(8,128)(2,1)S(1)}, bf16[128,512]{1,0:T(8,128)(2,1)S(1)}, u32[]{:S(2)}, u32[]{:S(2)}) collective-permute-start(bf16[128,512]{1,0:T(8,128)(2,1)S(1)} %convolution_convert_fusion.3), channel_id=1, source_target_pairs={{0,1},{1,0},{2,3},{3,2},{4,5},{5,4},{6,7},{7,6},{8,9},{9,8},{10,11... | collective-permute-start | bytes 393224 | tf_op jit(solution)/shard_map/ppermute | solution.py:34
  53.6 6.4 %collective-permute-start.10 = (bf16[128,512]{1,0:T(8,128)(2,1)S(1)}, bf16[128,512]{1,0:T(8,128)(2,1)S(1)}, u32[]{:S(2)}, u32[]{:S(2)}) collective-permute-start(bf16[128,512]{1,0:T(8,128)(2,1)S(1)} %get-tuple-element.6), channel_id=1, source_target_pairs={{0,2},{2,0},{4,6},{6,4},{8,10},{10,8},{12,14},{14,12},{16,18},{18,... | collective-permute-start | bytes 393224 | tf_op jit(solution)/shard_map/ppermute | solution.py:27
  54.2 9.2 %collective-permute-start.12 = (bf16[128,512]{1,0:T(8,128)(2,1)S(1)}, bf16[128,512]{1,0:T(8,128)(2,1)S(1)}, u32[]{:S(2)}, u32[]{:S(2)}) collective-permute-start(bf16[128,512]{1,0:T(8,128)(2,1)S(1)} %get-tuple-element.7), channel_id=1, source_target_pairs={{0,6},{2,4},{4,2},{6,0},{8,14},{10,12},{12,10},{14,8},{16,22},{18,... | collective-permute-start | bytes 393224 | tf_op jit(solution)/shard_map/ppermute | solution.py:27
  56.6 8.1 %collective-permute-start.11 = (bf16[128,512]{1,0:T(8,128)(2,1)S(1)}, bf16[128,512]{1,0:T(8,128)(2,1)S(1)}, u32[]{:S(2)}, u32[]{:S(2)}) collective-permute-start(bf16[128,512]{1,0:T(8,128)(2,1)S(1)} %get-tuple-element.8), channel_id=1, source_target_pairs={{0,4},{2,6},{4,0},{6,2},{8,12},{10,14},{12,8},{14,10},{16,20},{18,... | collective-permute-start | bytes 393224 | tf_op jit(solution)/shard_map/ppermute | solution.py:27

commit v18 on v15

--- a/solution.py
+++ b/solution.py
@@ -44,6 +44,9 @@
                 for n, k in enumerate(keys)
             }
         return parts[0]
+
+    def to_other(value):
+        return lax.ppermute(value, "rep", [(0, 1), (1, 0)])
 
     def dot(lhs, rhs, dims):
         return lax.dot_general(lhs, rhs, (dims, ((), ())), preferred_element_type=jnp.float32)
@@ -125,9 +128,18 @@
     ).astype(bf16)
 
     back = after(back, weight_part).astype(bf16)
-    back_full = lax.all_gather(back, "rep", axis=0, tiled=True)
-    w_rows = lax.dynamic_slice_in_dim(w_out, rep_pos * cols_here, cols_here, 0)
-    grad_in = dot(back_full, w_rows, ((0,), (1,)))
+    w_rows = w_out.reshape(rep_count, cols_here, feature_width)
+    if rep_count == 2:
+        w_mine = columns_of(lax.dynamic_index_in_dim(w_rows, rep_pos, 0, keepdims=False), rep_pos)
+        w_other = columns_of(
+            lax.dynamic_index_in_dim(w_rows, 1 - rep_pos, 0, keepdims=False), rep_pos
+        )
+        grad_in = to_other(dot(back, w_other, ((0,), (1,))).astype(bf16)).astype(jnp.float32)
+        grad_in = grad_in + dot(back, w_mine, ((0,), (1,)))
+    else:
+        back_full = lax.all_gather(back, "rep", axis=0, tiled=True)
+        w_mine = lax.dynamic_index_in_dim(w_rows, rep_pos, 0, keepdims=False)
+        grad_in = dot(back_full, w_mine, ((0,), (1,)))
     pre_part = columns_of(hidden_pre, rep_pos)
     grad_pre = jnp.where(pre_part > 0, grad_in, 0.0).astype(bf16)
     return (out_part, grad_weight, grad_pre)

time: 56.2 us -> 54.7 us (0.973)
  blocking collectives: 6.17 us -> 4.18 us
    all_gather x1 -> x0, blocking collectives: 1.99 us -> none  [shards(): back_full = lax.all_gather(back, 'rep', axis=0, tiled=True)]
    ppermute x11, waiting for transfers between devices: 8.2 us -> 7.39 us  [along_inner(): return lax.ppermute(value, 'blk', pairs) if turn else value]
    ppermute x9, waiting for transfers between devices: 5.92 us -> 6.69 us  [along_outer(): return lax.ppermute(value, 'blk', pairs) if turn else value]
    dot_general x5 -> x6, matrix products: 2.71 us -> 3.09 us  [dot(): lax.dot_general(lhs, rhs, (dims, ((), ())), preferred_element_type=jnp.fl...]
  transfers between devices with their start and end apart: 20 -> 21, of which waited for: 6 -> 7; matrix products, arithmetic and copies ran while one was open for 11% -> 12% of each run, Pallas kernels for 0% -> 0%
where the time goes in v18:
time: 54.7 us; the launch traced here: 54.4 us
  starting transfers between devices  27.1 us (50%)
  waiting for transfers between devices  14.1 us (26%)
  blocking collectives  4.18 us (8%)
  other arithmetic  3.84 us (7%)
  matrix products  3.09 us (6%)
  local copies, waits for them, and re-layouts  1.23 us (2%)
  between operations  0.94 us (2%)
    ppermute x9, starting transfers between devices, along_outer(): return lax.ppermute(value, 'blk', pairs) if turn else value  14.1 us
    ppermute x11, starting transfers between devices, along_inner(): return lax.ppermute(value, 'blk', pairs) if turn else value  12.9 us
    ppermute x11, waiting for transfers between devices, along_inner(): return lax.ppermute(value, 'blk', pairs) if turn else value  7.39 us
    ppermute x9, waiting for transfers between devices, along_outer(): return lax.ppermute(value, 'blk', pairs) if turn else value  6.69 us
    dot_general x6, matrix products, dot(): lax.dot_general(lhs, rhs, (dims, ((), ())), preferred_element_type=jnp.fl...  3.09 us
    all_gather x1, blocking collectives, shards(): everyone = lax.all_gather(jnp.concatenate(arrived, 0), 'rep', axis=0)  2.18 us
    all_gather x1, blocking collectives, shards(): lax.all_gather(mixed_cols.astype(bf16), 'rep', axis=0, tiled=True)  1.99 us
  transfers between devices with their start and end apart: 21, of which 7 were waited for; matrix products, arithmetic and copies ran while one was open for 12% of the time, Pallas kernels for 0%

profile of v18, /device:TPU:0, one launch (start us, length us, event | category | flops | bytes accessed | tf_op | source)
XLA Modules:
  0.0 54.4 jit_solution(3096477045793886843)
XLA Ops:
  0.7 1.1 %dynamic-slice_maximum_fusion = bf16[128,512]{1,0:T(8,128)(2,1)S(1)} fusion(bf16[128,1024]{1,0:T(8,128)(2,1)} %param.5, s32[]{:T(128)S(6)} %select_n.214), kind=kLoop, calls=%fused_computation.43 | loop fusion | flops 262144 | bytes 262148 | tf_op jit(solution)/shard_map/max | solution.py:66
  1.7 5.1 %collective-permute-start.2 = (bf16[128,512]{1,0:T(8,128)(2,1)S(1)}, bf16[128,512]{1,0:T(8,128)(2,1)S(1)}, u32[]{:S(2)}, u32[]{:S(2)}) collective-permute-start(bf16[128,512]{1,0:T(8,128)(2,1)S(1)} %dynamic-slice_maximum_fusion), channel_id=1, source_target_pairs={{0,24},{2,26},{4,28},{6,30},{8,16},{10,18},{12,20},{14,22},{16,8},... | collective-permute-start | bytes 393224 | tf_op jit(solution)/shard_map/ppermute | solution.py:32
  6.9 0.7 %add_bitcast_fusion = s32[8]{0:T(128)S(1)} fusion(s32[1,8]{1,0:T(1,128)} %param.7, s32[]{:T(128)S(6)} %shift_right_arithmetic.54, s32[]{:T(128)S(6)} %and.60), kind=kLoop, calls=%fused_computation.90 | loop fusion | flops 56 | bytes 72 | tf_op jit(solution)/shard_map/eq | solution.py:72
  7.6 0.9 %slice_bitcast_fusion.9 = (bf16[128,128]{1,0:T(8,128)(2,1)S(1)}, bf16[128,128]{1,0:T(8,128)(2,1)S(1)}, bf16[128,128]{1,0:T(8,128)(2,1)S(1)}, bf16[128,128]{1,0:T...) fusion(bf16[1,8,128,128]{3,2,1,0:T(8,128)(2,1)} %param.6), kind=kLoop, calls=%fused_computation.71 | loop fusion | bytes 524288 | tf_op jit(solution)/shard_map/jit(_where)/broadcast_in_dim | solution.py:75
  8.7 2.5 %collective-permute-start.5 = (bf16[2,128,128]{2,1,0:T(8,128)(2,1)S(1)}, bf16[2,128,128]{2,1,0:T(8,128)(2,1)S(1)}, u32[]{:S(2)}, u32[]{:S(2)}) collective-permute-start(bf16[2,128,128]{2,1,0:T(8,128)(2,1)S(1)} %get-tuple-element.31), channel_id=1, source_target_pairs={{0,6},{2,4},{4,2},{6,0},{8,14},{10,12},{12,10},{14,8},{16,22},{18,... | collective-permute-start | bytes 196616 | tf_op jit(solution)/shard_map/ppermute | solution.py:28
  11.2 0.5 collective-permute-start.4
  11.8 0.5 collective-permute-start.3
  12.4 1.7 %collective-permute-done.5 = bf16[2,128,128]{2,1,0:T(8,128)(2,1)S(1)} collective-permute-done((bf16[2,128,128]{2,1,0:T(8,128)(2,1)S(1)}, bf16[2,128,128]{2,1,0:T(8,128)(2,1)S(1)}, u32[]{:S(2)}, u32[]{:S(2)}) %collective-permute-start.5) | collective-permute-done | bytes 65568 | tf_op jit(solution)/shard_map/ppermute | solution.py:28
  14.1 0.6 %collective-permute-start = (bf16[128,512]{1,0:T(8,128)(2,1)S(1)}, bf16[128,512]{1,0:T(8,128)(2,1)S(1)}, u32[]{:S(2)}, u32[]{:S(2)}) collective-permute-start(bf16[128,512]{1,0:T(8,128)(2,1)S(1)} %dynamic-slice_maximum_fusion), channel_id=1, source_target_pairs={{0,8},{2,10},{4,12},{6,14},{8,0},{10,2},{12,4},{14,6},{16,24},{18,... | collective-permute-start | bytes 393224 | tf_op jit(solution)/shard_map/ppermute | solution.py:32
  14.7 0.8 %collective-permute-done.4 = bf16[2,128,128]{2,1,0:T(8,128)(2,1)S(1)} collective-permute-done((bf16[2,128,128]{2,1,0:T(8,128)(2,1)S(1)}, bf16[2,128,128]{2,1,0:T(8,128)(2,1)S(1)}, u32[]{:S(2)}, u32[]{:S(2)}) %collective-permute-start.4) | collective-permute-done | bytes 65568 | tf_op jit(solution)/shard_map/ppermute | solution.py:28
  15.5 1.8 %collective-permute-start.13 = (bf16[128,512]{1,0:T(8,128)(2,1)S(1)}, bf16[128,512]{1,0:T(8,128)(2,1)S(1)}, u32[]{:S(2)}, u32[]{:S(2)}) collective-permute-start(bf16[128,512]{1,0:T(8,128)(2,1)S(1)} %constant_dynamic-slice_fusion), channel_id=1, source_target_pairs={{0,6},{2,4},{4,2},{6,0},{8,14},{10,12},{12,10},{14,8},{16,22},{18,... | collective-permute-start | bytes 393224 | tf_op jit(solution)/shard_map/ppermute | solution.py:28
  17.3 1.1 %collective-permute-start.12 = (bf16[128,512]{1,0:T(8,128)(2,1)S(1)}, bf16[128,512]{1,0:T(8,128)(2,1)S(1)}, u32[]{:S(2)}, u32[]{:S(2)}) collective-permute-start(bf16[128,512]{1,0:T(8,128)(2,1)S(1)} %constant_dynamic-slice_fusion), channel_id=1, source_target_pairs={{0,4},{2,6},{4,0},{6,2},{8,12},{10,14},{12,8},{14,10},{16,20},{18,... | collective-permute-start | bytes 393224 | tf_op jit(solution)/shard_map/ppermute | solution.py:28
  18.5 2.2 %all-gather = bf16[16,128,128]{2,1,0:T(8,128)(2,1)S(1)} all-gather(bf16[8,128,128]{2,1,0:T(8,128)(2,1)S(1)} %pad_maximum_fusion.1), channel_id=2, replica_groups=mesh['blk'=16,'rep'=2] {'rep'}, dimensions={0}, use_global_device_ids=true | all-gather | bytes 786432 | tf_op jit(solution)/shard_map/all_gather | solution.py:79
  20.9 0.6 %collective-permute-start.11 = (bf16[128,512]{1,0:T(8,128)(2,1)S(1)}, bf16[128,512]{1,0:T(8,128)(2,1)S(1)}, u32[]{:S(2)}, u32[]{:S(2)}) collective-permute-start(bf16[128,512]{1,0:T(8,128)(2,1)S(1)} %constant_dynamic-slice_fusion), channel_id=1, source_target_pairs={{0,2},{2,0},{4,6},{6,4},{8,10},{10,8},{12,14},{14,12},{16,18},{18,... | collective-permute-start | bytes 393224 | tf_op jit(solution)/shard_map/ppermute | solution.py:28
  22.1 1.5 %collective-permute-start.7 = (bf16[128,512]{1,0:T(8,128)(2,1)S(1)}, bf16[128,512]{1,0:T(8,128)(2,1)S(1)}, u32[]{:S(2)}, u32[]{:S(2)}) collective-permute-start(bf16[128,512]{1,0:T(8,128)(2,1)S(1)} %pad_maximum_fusion.4), channel_id=1, source_target_pairs={{0,4},{2,6},{4,0},{6,2},{8,12},{10,14},{12,8},{14,10},{16,20},{18,... | collective-permute-start | bytes 393224 | tf_op jit(solution)/shard_map/ppermute | solution.py:28
  23.7 1.0 %collective-permute-start.6 = (bf16[128,512]{1,0:T(8,128)(2,1)S(1)}, bf16[128,512]{1,0:T(8,128)(2,1)S(1)}, u32[]{:S(2)}, u32[]{:S(2)}) collective-permute-start(bf16[128,512]{1,0:T(8,128)(2,1)S(1)} %pad_maximum_fusion.3), channel_id=1, source_target_pairs={{0,2},{2,0},{4,6},{6,4},{8,10},{10,8},{12,14},{14,12},{16,18},{18,... | collective-permute-start | bytes 393224 | tf_op jit(solution)/shard_map/ppermute | solution.py:28
  24.7 1.2 %collective-permute-start.8 = (bf16[128,512]{1,0:T(8,128)(2,1)S(1)}, bf16[128,512]{1,0:T(8,128)(2,1)S(1)}, u32[]{:S(2)}, u32[]{:S(2)}) collective-permute-start(bf16[128,512]{1,0:T(8,128)(2,1)S(1)} %pad_maximum_fusion.5), channel_id=1, source_target_pairs={{0,6},{2,4},{4,2},{6,0},{8,14},{10,12},{12,10},{14,8},{16,22},{18,... | collective-permute-start | bytes 393224 | tf_op jit(solution)/shard_map/ppermute | solution.py:28
  25.9 1.1 %collective-permute-done.11 = bf16[128,512]{1,0:T(8,128)(2,1)S(1)} collective-permute-done((bf16[128,512]{1,0:T(8,128)(2,1)S(1)}, bf16[128,512]{1,0:T(8,128)(2,1)S(1)}, u32[]{:S(2)}, u32[]{:S(2)}) %collective-permute-start.11) | collective-permute-done | bytes 131104 | tf_op jit(solution)/shard_map/ppermute | solution.py:28
  27.5 1.0 %collective-permute-start.17 = (bf16[512,128]{1,0:T(8,128)(2,1)S(1)}, bf16[512,128]{1,0:T(8,128)(2,1)S(1)}, u32[]{:S(2)}, u32[]{:S(2)}) collective-permute-start(bf16[512,128]{1,0:T(8,128)(2,1)S(1)} %get-tuple-element.3), channel_id=1, source_target_pairs={{0,8},{2,10},{4,12},{6,14},{8,0},{10,2},{12,4},{14,6},{16,24},{18,... | collective-permute-start | bytes 393224 | tf_op jit(solution)/shard_map/ppermute | solution.py:32
  28.6 2.8 %collective-permute-start.19 = (bf16[512,128]{1,0:T(8,128)(2,1)S(1)}, bf16[512,128]{1,0:T(8,128)(2,1)S(1)}, u32[]{:S(2)}, u32[]{:S(2)}) collective-permute-start(bf16[512,128]{1,0:T(8,128)(2,1)S(1)} %get-tuple-element.4), channel_id=1, source_target_pairs={{0,24},{2,26},{4,28},{6,30},{8,16},{10,18},{12,20},{14,22},{16,8},... | collective-permute-start | bytes 393224 | tf_op jit(solution)/shard_map/ppermute | solution.py:32
  31.6 0.8 %collective-permute-done.8 = bf16[128,512]{1,0:T(8,128)(2,1)S(1)} collective-permute-done((bf16[128,512]{1,0:T(8,128)(2,1)S(1)}, bf16[128,512]{1,0:T(8,128)(2,1)S(1)}, u32[]{:S(2)}, u32[]{:S(2)}) %collective-permute-start.8) | collective-permute-done | bytes 131104 | tf_op jit(solution)/shard_map/ppermute | solution.py:28
  32.5 2.0 %all_gather.11 = bf16[256,512]{1,0:T(8,128)(2,1)S(1)} all-gather(bf16[128,512]{1,0:T(8,128)(2,1)S(1)} %fusion.19), channel_id=1, replica_groups=mesh['blk'=16,'rep'=2] {'rep'}, dimensions={0}, use_global_device_ids=true | all-gather | bytes 393216 | tf_op jit(solution)/shard_map/all_gather | solution.py:112
  34.8 1.3 %collective-permute-start.14 = (bf16[64,512]{1,0:T(8,128)(2,1)S(1)}, bf16[64,512]{1,0:T(8,128)(2,1)S(1)}, u32[]{:S(2)}, u32[]{:S(2)}) collective-permute-start(bf16[64,512]{1,0:T(8,128)(2,1)S(1)} %get-tuple-element.27), channel_id=1, source_target_pairs={{0,8},{2,10},{4,12},{6,14},{8,0},{10,2},{12,4},{14,6},{16,24},{18,... | collective-permute-start | bytes 196616 | tf_op jit(solution)/shard_map/ppermute | solution.py:32
  36.1 2.5 %collective-permute-start.16 = (bf16[64,512]{1,0:T(8,128)(2,1)S(1)}, bf16[64,512]{1,0:T(8,128)(2,1)S(1)}, u32[]{:S(2)}, u32[]{:S(2)}) collective-permute-start(bf16[64,512]{1,0:T(8,128)(2,1)S(1)} %get-tuple-element.28), channel_id=1, source_target_pairs={{0,24},{2,26},{4,28},{6,30},{8,16},{10,18},{12,20},{14,22},{16,8},... | collective-permute-start | bytes 196616 | tf_op jit(solution)/shard_map/ppermute | solution.py:32
  39.5 1.0 %collective-permute-start.9 = (bf16[256,512]{1,0:T(8,128)(2,1)S(1)}, bf16[256,512]{1,0:T(8,128)(2,1)S(1)}, u32[]{:S(2)}, u32[]{:S(2)}) collective-permute-start(bf16[256,512]{1,0:T(8,128)(2,1)S(1)} %pad_maximum_fusion.2), channel_id=1, source_target_pairs={{0,2},{2,0},{4,6},{6,4},{8,10},{10,8},{12,14},{14,12},{16,18},{18,... | collective-permute-start | bytes 786440 | tf_op jit(solution)/shard_map/ppermute | solution.py:28
  40.5 5.9 %collective-permute-done.18 = bf16[512,128]{1,0:T(8,128)(2,1)S(1)} collective-permute-done((bf16[512,128]{1,0:T(8,128)(2,1)S(1)}, bf16[512,128]{1,0:T(8,128)(2,1)S(1)}, u32[]{:S(2)}, u32[]{:S(2)}) %collective-permute-start.18) | collective-permute-done | bytes 131104 | tf_op jit(solution)/shard_map/ppermute | solution.py:32
  47.0 0.8 %collective-permute-done.15 = bf16[64,512]{1,0:T(8,128)(2,1)S(1)} collective-permute-done((bf16[64,512]{1,0:T(8,128)(2,1)S(1)}, bf16[64,512]{1,0:T(8,128)(2,1)S(1)}, u32[]{:S(2)}, u32[]{:S(2)}) %collective-permute-start.15) | collective-permute-done | bytes 65568 | tf_op jit(solution)/shard_map/ppermute | solution.py:32
  47.8 0.7 %fusion.23 = f32[64,512]{1,0:T(8,128)} fusion(bf16[64,512]{1,0:T(8,128)(2,1)S(1)} %collective-permute-done.16, bf16[64,512]{1,0:T(8,128)(2,1)S(1)} %collective-permute-done.15, bf16[64,512]{1,0:T(8,128)(2,1)S(1)} %collective-permute-done.14, bf16[4,64,512]{2,1,0:T(8,128)(2,1)S(1)} %bitcast.118, s32[]{:T(128)S(6)} %select_n.271), kind=kLoop, calls=%fused_computation.41 | loop fusion | flops 229376 | bytes 393220 | tf_op jit(solution)/shard_map/add | solution.py:115
  48.5 1.1 %collective-permute-start.10 = (bf16[128,512]{1,0:T(8,128)(2,1)S(1)}, bf16[128,512]{1,0:T(8,128)(2,1)S(1)}, u32[]{:S(2)}, u32[]{:S(2)}) collective-permute-start(bf16[128,512]{1,0:T(8,128)(2,1)S(1)} %fusion.13), channel_id=1, source_target_pairs={{0,4},{2,6},{4,0},{6,2},{8,12},{10,14},{12,8},{14,10},{16,20},{18,... | collective-permute-start | bytes 393224 | tf_op jit(solution)/shard_map/ppermute | solution.py:28
  49.6 1.1 %select_convert_fusion = bf16[128,512]{1,0:T(8,128)(2,1)} fusion(bf16[128,512]{1,0:T(8,128)(2,1)S(1)} %collective-permute-done.20, bf16[128,1024]{1,0:T(8,128)(2,1)S(1)} %copy-done.1, s32[]{:T(128)S(6)} %select_n.214, bf16[512,128]{1,0:T(8,128)(2,1)S(1)} %fusion.16, bf16[2,512,1024]{2,1,0:T(8,128)(2,1)S(1)} %bitcast.107, s32[]{:T(128)S(6)} %select_n.279, ...), kind=kOutput, calls=%fused_computation.32 | convolution fusion | flops 67567616 | bytes 1048588 | tf_op jit(solution)/shard_map/dot_general | solution.py:52
  50.7 3.0 %collective-permute-done.10 = bf16[128,512]{1,0:T(8,128)(2,1)S(1)} collective-permute-done((bf16[128,512]{1,0:T(8,128)(2,1)S(1)}, bf16[128,512]{1,0:T(8,128)(2,1)S(1)}, u32[]{:S(2)}, u32[]{:S(2)}) %collective-permute-start.10) | collective-permute-done | bytes 131104 | tf_op jit(solution)/shard_map/ppermute | solution.py:28
  53.7 0.7 %fusion.15 = bf16[128,512]{1,0:T(8,128)(2,1)} fusion(f32[512,512]{1,0:T(8,128)S(1)} %get-tuple-element.61, bf16[128,512]{1,0:T(8,128)(2,1)S(1)} %collective-permute-done.10, bf16[256,512]{1,0:T(8,128)(2,1)S(1)} %collective-permute-done.9), kind=kLoop, calls=%fused_computation.23 | loop fusion | flops 327680 | bytes 655360 | tf_op jit(solution)/shard_map/convert_element_type | solution.py:128
  (56 shorter events, 3.8 us)
Async XLA Ops:
  0.6 11.7 %copy-start = (bf16[1024,1024]{1,0:T(8,128)(2,1)S(1)}, bf16[1024,1024]{1,0:T(8,128)(2,1)}, u32[]{:S(2)}) copy-start(bf16[1024,1024]{1,0:T(8,128)(2,1)} %param.8) | copy-start | bytes 6291460
  0.6 11.7 %copy-start.2 = (bf16[128,1024]{1,0:T(8,128)(2,1)S(1)}, bf16[128,1024]{1,0:T(8,128)(2,1)}, u32[]{:S(2)}) copy-start(bf16[128,1024]{1,0:T(8,128)(2,1)} %param.9) | copy-start | bytes 786436
  1.7 19.1 %collective-permute-start.2 = (bf16[128,512]{1,0:T(8,128)(2,1)S(1)}, bf16[128,512]{1,0:T(8,128)(2,1)S(1)}, u32[]{:S(2)}, u32[]{:S(2)}) collective-permute-start(bf16[128,512]{1,0:T(8,128)(2,1)S(1)} %dynamic-slice_maximum_fusion), channel_id=1, source_target_pairs={{0,24},{2,26},{4,28},{6,30},{8,16},{10,18},{12,20},{14,22},{16,8},... | collective-permute-start | bytes 393224 | tf_op jit(solution)/shard_map/ppermute | solution.py:32
  6.9 14.6 %collective-permute-start.1 = (bf16[128,512]{1,0:T(8,128)(2,1)S(1)}, bf16[128,512]{1,0:T(8,128)(2,1)S(1)}, u32[]{:S(2)}, u32[]{:S(2)}) collective-permute-start(bf16[128,512]{1,0:T(8,128)(2,1)S(1)} %dynamic-slice_maximum_fusion), channel_id=1, source_target_pairs={{0,16},{2,18},{4,20},{6,22},{8,24},{10,26},{12,28},{14,30},{16,0},... | collective-permute-start | bytes 393224 | tf_op jit(solution)/shard_map/ppermute | solution.py:32
  8.7 5.3 %collective-permute-start.5 = (bf16[2,128,128]{2,1,0:T(8,128)(2,1)S(1)}, bf16[2,128,128]{2,1,0:T(8,128)(2,1)S(1)}, u32[]{:S(2)}, u32[]{:S(2)}) collective-permute-start(bf16[2,128,128]{2,1,0:T(8,128)(2,1)S(1)} %get-tuple-element.31), channel_id=1, source_target_pairs={{0,6},{2,4},{4,2},{6,0},{8,14},{10,12},{12,10},{14,8},{16,22},{18,... | collective-permute-start | bytes 196616 | tf_op jit(solution)/shard_map/ppermute | solution.py:28
  11.2 4.3 %collective-permute-start.4 = (bf16[2,128,128]{2,1,0:T(8,128)(2,1)S(1)}, bf16[2,128,128]{2,1,0:T(8,128)(2,1)S(1)}, u32[]{:S(2)}, u32[]{:S(2)}) collective-permute-start(bf16[2,128,128]{2,1,0:T(8,128)(2,1)S(1)} %get-tuple-element.32), channel_id=1, source_target_pairs={{0,4},{2,6},{4,0},{6,2},{8,12},{10,14},{12,8},{14,10},{16,20},{18,... | collective-permute-start | bytes 196616 | tf_op jit(solution)/shard_map/ppermute | solution.py:28
  11.8 5.6 %collective-permute-start.3 = (bf16[2,128,128]{2,1,0:T(8,128)(2,1)S(1)}, bf16[2,128,128]{2,1,0:T(8,128)(2,1)S(1)}, u32[]{:S(2)}, u32[]{:S(2)}) collective-permute-start(bf16[2,128,128]{2,1,0:T(8,128)(2,1)S(1)} %get-tuple-element.33), channel_id=1, source_target_pairs={{0,2},{2,0},{4,6},{6,4},{8,10},{10,8},{12,14},{14,12},{16,18},{18,... | collective-permute-start | bytes 196616 | tf_op jit(solution)/shard_map/ppermute | solution.py:28
  14.1 7.4 %collective-permute-start = (bf16[128,512]{1,0:T(8,128)(2,1)S(1)}, bf16[128,512]{1,0:T(8,128)(2,1)S(1)}, u32[]{:S(2)}, u32[]{:S(2)}) collective-permute-start(bf16[128,512]{1,0:T(8,128)(2,1)S(1)} %dynamic-slice_maximum_fusion), channel_id=1, source_target_pairs={{0,8},{2,10},{4,12},{6,14},{8,0},{10,2},{12,4},{14,6},{16,24},{18,... | collective-permute-start | bytes 393224 | tf_op jit(solution)/shard_map/ppermute | solution.py:32
  15.5 9.2 %collective-permute-start.13 = (bf16[128,512]{1,0:T(8,128)(2,1)S(1)}, bf16[128,512]{1,0:T(8,128)(2,1)S(1)}, u32[]{:S(2)}, u32[]{:S(2)}) collective-permute-start(bf16[128,512]{1,0:T(8,128)(2,1)S(1)} %constant_dynamic-slice_fusion), channel_id=1, source_target_pairs={{0,6},{2,4},{4,2},{6,0},{8,14},{10,12},{12,10},{14,8},{16,22},{18,... | collective-permute-start | bytes 393224 | tf_op jit(solution)/shard_map/ppermute | solution.py:28
  17.3 8.6 %collective-permute-start.12 = (bf16[128,512]{1,0:T(8,128)(2,1)S(1)}, bf16[128,512]{1,0:T(8,128)(2,1)S(1)}, u32[]{:S(2)}, u32[]{:S(2)}) collective-permute-start(bf16[128,512]{1,0:T(8,128)(2,1)S(1)} %constant_dynamic-slice_fusion), channel_id=1, source_target_pairs={{0,4},{2,6},{4,0},{6,2},{8,12},{10,14},{12,8},{14,10},{16,20},{18,... | collective-permute-start | bytes 393224 | tf_op jit(solution)/shard_map/ppermute | solution.py:28
  20.9 6.1 %collective-permute-start.11 = (bf16[128,512]{1,0:T(8,128)(2,1)S(1)}, bf16[128,512]{1,0:T(8,128)(2,1)S(1)}, u32[]{:S(2)}, u32[]{:S(2)}) collective-permute-start(bf16[128,512]{1,0:T(8,128)(2,1)S(1)} %constant_dynamic-slice_fusion), channel_id=1, source_target_pairs={{0,2},{2,0},{4,6},{6,4},{8,10},{10,8},{12,14},{14,12},{16,18},{18,... | collective-permute-start | bytes 393224 | tf_op jit(solution)/shard_map/ppermute | solution.py:28
  22.1 9.2 %collective-permute-start.7 = (bf16[128,512]{1,0:T(8,128)(2,1)S(1)}, bf16[128,512]{1,0:T(8,128)(2,1)S(1)}, u32[]{:S(2)}, u32[]{:S(2)}) collective-permute-start(bf16[128,512]{1,0:T(8,128)(2,1)S(1)} %pad_maximum_fusion.4), channel_id=1, source_target_pairs={{0,4},{2,6},{4,0},{6,2},{8,12},{10,14},{12,8},{14,10},{16,20},{18,... | collective-permute-start | bytes 393224 | tf_op jit(solution)/shard_map/ppermute | solution.py:28
  23.7 7.9 %collective-permute-start.6 = (bf16[128,512]{1,0:T(8,128)(2,1)S(1)}, bf16[128,512]{1,0:T(8,128)(2,1)S(1)}, u32[]{:S(2)}, u32[]{:S(2)}) collective-permute-start(bf16[128,512]{1,0:T(8,128)(2,1)S(1)} %pad_maximum_fusion.3), channel_id=1, source_target_pairs={{0,2},{2,0},{4,6},{6,4},{8,10},{10,8},{12,14},{14,12},{16,18},{18,... | collective-permute-start | bytes 393224 | tf_op jit(solution)/shard_map/ppermute | solution.py:28
  24.7 7.7 %collective-permute-start.8 = (bf16[128,512]{1,0:T(8,128)(2,1)S(1)}, bf16[128,512]{1,0:T(8,128)(2,1)S(1)}, u32[]{:S(2)}, u32[]{:S(2)}) collective-permute-start(bf16[128,512]{1,0:T(8,128)(2,1)S(1)} %pad_maximum_fusion.5), channel_id=1, source_target_pairs={{0,6},{2,4},{4,2},{6,0},{8,14},{10,12},{12,10},{14,8},{16,22},{18,... | collective-permute-start | bytes 393224 | tf_op jit(solution)/shard_map/ppermute | solution.py:28
  27.5 11.6 %collective-permute-start.17 = (bf16[512,128]{1,0:T(8,128)(2,1)S(1)}, bf16[512,128]{1,0:T(8,128)(2,1)S(1)}, u32[]{:S(2)}, u32[]{:S(2)}) collective-permute-start(bf16[512,128]{1,0:T(8,128)(2,1)S(1)} %get-tuple-element.3), channel_id=1, source_target_pairs={{0,8},{2,10},{4,12},{6,14},{8,0},{10,2},{12,4},{14,6},{16,24},{18,... | collective-permute-start | bytes 393224 | tf_op jit(solution)/shard_map/ppermute | solution.py:32
  28.6 11.0 %collective-permute-start.19 = (bf16[512,128]{1,0:T(8,128)(2,1)S(1)}, bf16[512,128]{1,0:T(8,128)(2,1)S(1)}, u32[]{:S(2)}, u32[]{:S(2)}) collective-permute-start(bf16[512,128]{1,0:T(8,128)(2,1)S(1)} %get-tuple-element.4), channel_id=1, source_target_pairs={{0,24},{2,26},{4,28},{6,30},{8,16},{10,18},{12,20},{14,22},{16,8},... | collective-permute-start | bytes 393224 | tf_op jit(solution)/shard_map/ppermute | solution.py:32
  31.4 15.0 %collective-permute-start.18 = (bf16[512,128]{1,0:T(8,128)(2,1)S(1)}, bf16[512,128]{1,0:T(8,128)(2,1)S(1)}, u32[]{:S(2)}, u32[]{:S(2)}) collective-permute-start(bf16[512,128]{1,0:T(8,128)(2,1)S(1)} %get-tuple-element.5), channel_id=1, source_target_pairs={{0,16},{2,18},{4,20},{6,22},{8,24},{10,26},{12,28},{14,30},{16,0},... | collective-permute-start | bytes 393224 | tf_op jit(solution)/shard_map/ppermute | solution.py:32
  34.8 12.2 %collective-permute-start.14 = (bf16[64,512]{1,0:T(8,128)(2,1)S(1)}, bf16[64,512]{1,0:T(8,128)(2,1)S(1)}, u32[]{:S(2)}, u32[]{:S(2)}) collective-permute-start(bf16[64,512]{1,0:T(8,128)(2,1)S(1)} %get-tuple-element.27), channel_id=1, source_target_pairs={{0,8},{2,10},{4,12},{6,14},{8,0},{10,2},{12,4},{14,6},{16,24},{18,... | collective-permute-start | bytes 196616 | tf_op jit(solution)/shard_map/ppermute | solution.py:32
  36.1 10.9 %collective-permute-start.16 = (bf16[64,512]{1,0:T(8,128)(2,1)S(1)}, bf16[64,512]{1,0:T(8,128)(2,1)S(1)}, u32[]{:S(2)}, u32[]{:S(2)}) collective-permute-start(bf16[64,512]{1,0:T(8,128)(2,1)S(1)} %get-tuple-element.28), channel_id=1, source_target_pairs={{0,24},{2,26},{4,28},{6,30},{8,16},{10,18},{12,20},{14,22},{16,8},... | collective-permute-start | bytes 196616 | tf_op jit(solution)/shard_map/ppermute | solution.py:32
  39.0 10.6 %copy-start.1 = (bf16[128,1024]{1,0:T(8,128)(2,1)S(1)}, bf16[128,1024]{1,0:T(8,128)(2,1)}, u32[]{:S(2)}) copy-start(bf16[128,1024]{1,0:T(8,128)(2,1)} %param.5) | copy-start | bytes 786436
  39.1 8.7 %collective-permute-start.15 = (bf16[64,512]{1,0:T(8,128)(2,1)S(1)}, bf16[64,512]{1,0:T(8,128)(2,1)S(1)}, u32[]{:S(2)}, u32[]{:S(2)}) collective-permute-start(bf16[64,512]{1,0:T(8,128)(2,1)S(1)} %get-tuple-element.29), channel_id=1, source_target_pairs={{0,16},{2,18},{4,20},{6,22},{8,24},{10,26},{12,28},{14,30},{16,0},... | collective-permute-start | bytes 196616 | tf_op jit(solution)/shard_map/ppermute | solution.py:32
  39.5 9.0 %collective-permute-start.9 = (bf16[256,512]{1,0:T(8,128)(2,1)S(1)}, bf16[256,512]{1,0:T(8,128)(2,1)S(1)}, u32[]{:S(2)}, u32[]{:S(2)}) collective-permute-start(bf16[256,512]{1,0:T(8,128)(2,1)S(1)} %pad_maximum_fusion.2), channel_id=1, source_target_pairs={{0,2},{2,0},{4,6},{6,4},{8,10},{10,8},{12,14},{14,12},{16,18},{18,... | collective-permute-start | bytes 786440 | tf_op jit(solution)/shard_map/ppermute | solution.py:28
  46.9 2.7 %collective-permute-start.20 = (bf16[128,512]{1,0:T(8,128)(2,1)S(1)}, bf16[128,512]{1,0:T(8,128)(2,1)S(1)}, u32[]{:S(2)}, u32[]{:S(2)}) collective-permute-start(bf16[128,512]{1,0:T(8,128)(2,1)S(1)} %convolution_convert_fusion.2), channel_id=1, source_target_pairs={{0,1},{1,0},{2,3},{3,2},{4,5},{5,4},{6,7},{7,6},{8,9},{9,8},{10,11... | collective-permute-start | bytes 393224 | tf_op jit(solution)/shard_map/ppermute | solution.py:49
  48.5 5.2 %collective-permute-start.10 = (bf16[128,512]{1,0:T(8,128)(2,1)S(1)}, bf16[128,512]{1,0:T(8,128)(2,1)S(1)}, u32[]{:S(2)}, u32[]{:S(2)}) collective-permute-start(bf16[128,512]{1,0:T(8,128)(2,1)S(1)} %fusion.13), channel_id=1, source_target_pairs={{0,4},{2,6},{4,0},{6,2},{8,12},{10,14},{12,8},{14,10},{16,20},{18,... | collective-permute-start | bytes 393224 | tf_op jit(solution)/shard_map/ppermute | solution.py:28

commit v19 on v18

--- a/solution.py
+++ b/solution.py
@@ -34,16 +34,18 @@
     def halved(parts, move):
         parts = dict(enumerate(parts))
         size = parts[0].shape[0]
+        arrived = []
         for bit in rising:
             keys = [k for k in parts if not k & bit]
             sent = jnp.concatenate([parts[k ^ bit].astype(bf16) for k in keys], 0)
             got = move(sent, bit)
+            arrived.append(got)
             parts = {
                 k: parts[k].astype(jnp.float32)
                 + got[n * size : (n + 1) * size].astype(jnp.float32)
                 for n, k in enumerate(keys)
             }
-        return parts[0]
+        return parts[0], arrived[0]
 
     def to_other(value):
         return lax.ppermute(value, "rep", [(0, 1), (1, 0)])
@@ -110,7 +112,11 @@
     back = sum(along_outer(lanes(back, e), e).astype(jnp.float32) for e in turns)
 
     mixed_cols = lax.all_gather(mixed_cols.astype(bf16), "rep", axis=0, tiled=True)
-    weight_part = dot(mixed_cols, grad_stack, ((1,), (0,))).astype(bf16)
+    w_share = w_out.reshape(side, side, rows_here, feature_width)
+    w_share = lax.dynamic_index_in_dim(w_share, inner_pos, 1, keepdims=False)
+    w_share = columns_of(w_share.reshape(side * rows_here, feature_width), rep_pos)
+    out_wide = dot(mixed_cols, w_share, ((0,), (0,)))
+    weight_part = after(dot(mixed_cols, grad_stack, ((1,), (0,))), out_wide).astype(bf16)
     by_outer = weight_part.reshape(side, rows_here, cols_here)
     grad_weight = sum(
         along_outer(
@@ -119,15 +125,12 @@
         for t in turns
     )
 
-    w_share = w_out.reshape(side, side, rows_here, feature_width)
-    w_share = lax.dynamic_index_in_dim(w_share, inner_pos, 1, keepdims=False)
-    w_share = columns_of(w_share.reshape(side * rows_here, feature_width), rep_pos)
-    out_part = dot(mixed_cols, w_share, ((0,), (0,)))
-    out_part = halved(
-        [out_part[t * tile_size : (t + 1) * tile_size] for t in turns], along_inner
-    ).astype(bf16)
+    out_part, first_got = halved(
+        [out_wide[t * tile_size : (t + 1) * tile_size] for t in turns], along_inner
+    )
+    out_part = out_part.astype(bf16)
 
-    back = after(back, weight_part).astype(bf16)
+    back = after(back, first_got).astype(bf16)
     w_rows = w_out.reshape(rep_count, cols_here, feature_width)
     if rep_count == 2:
         w_mine = columns_of(lax.dynamic_index_in_dim(w_rows, rep_pos, 0, keepdims=False), rep_pos)

time: 54.7 us -> 58.9 us (1.077)
  waiting for transfers between devices: 14.1 us -> 19.3 us
  starting transfers between devices: 27.1 us -> 25.1 us
  matrix products: 3.09 us -> 4.05 us
    ppermute x11, waiting for transfers between devices: 7.39 us -> 10.1 us  [along_inner(): return lax.ppermute(value, 'blk', pairs) if turn else value]
    ppermute x9, waiting for transfers between devices: 6.69 us -> 8.67 us  [along_outer(): return lax.ppermute(value, 'blk', pairs) if turn else value]
    ppermute x11, starting transfers between devices: 12.9 us -> 11.1 us  [along_inner(): return lax.ppermute(value, 'blk', pairs) if turn else value]
    dot_general x6, matrix products: 3.09 us -> 4.05 us  [dot(): lax.dot_general(lhs, rhs, (dims, ((), ())), preferred_element_type=jnp.fl...]
    ppermute x1, waiting for transfers between devices: 0.01 us -> 0.62 us  [to_other(): return lax.ppermute(value, 'rep', [(0, 1), (1, 0)])]
  transfers between devices with their start and end apart: 21 -> 21, of which waited for: 7 -> 11; matrix products, arithmetic and copies ran while one was open for 12% -> 11% of each run, Pallas kernels for 0% -> 0%
where the time goes in v19:
time: 58.9 us; the launch traced here: 58.7 us
  starting transfers between devices  25.1 us (43%)
  waiting for transfers between devices  19.3 us (33%)
  blocking collectives  4.18 us (7%)
  matrix products  4.05 us (7%)
  other arithmetic  3.85 us (7%)
  local copies, waits for them, and re-layouts  1.21 us (2%)
  between operations  0.94 us (2%)
    ppermute x9, starting transfers between devices, along_outer(): return lax.ppermute(value, 'blk', pairs) if turn else value  14 us
    ppermute x11, starting transfers between devices, along_inner(): return lax.ppermute(value, 'blk', pairs) if turn else value  11.1 us
    ppermute x11, waiting for transfers between devices, along_inner(): return lax.ppermute(value, 'blk', pairs) if turn else value  10.1 us
    ppermute x9, waiting for transfers between devices, along_outer(): return lax.ppermute(value, 'blk', pairs) if turn else value  8.67 us
    dot_general x6, matrix products, dot(): lax.dot_general(lhs, rhs, (dims, ((), ())), preferred_element_type=jnp.fl...  4.05 us
    all_gather x1, blocking collectives, shards(): everyone = lax.all_gather(jnp.concatenate(arrived, 0), 'rep', axis=0)  2.18 us
    all_gather x1, blocking collectives, shards(): lax.all_gather(mixed_cols.astype(bf16), 'rep', axis=0, tiled=True)  1.99 us
  transfers between devices with their start and end apart: 21, of which 11 were waited for; matrix products, arithmetic and copies ran while one was open for 11% of the time, Pallas kernels for 0%

profile of v19, /device:TPU:0, one launch (start us, length us, event | category | flops | bytes accessed | tf_op | source)
XLA Modules:
  0.0 58.7 jit_solution(16804813648960471688)
XLA Ops:
  0.7 1.1 %dynamic-slice_maximum_fusion = bf16[128,512]{1,0:T(8,128)(2,1)S(1)} fusion(bf16[128,1024]{1,0:T(8,128)(2,1)} %param.5, s32[]{:T(128)S(6)} %select_n.214), kind=kLoop, calls=%fused_computation.45 | loop fusion | flops 262144 | bytes 262148 | tf_op jit(solution)/shard_map/max | solution.py:68
  1.7 3.1 %collective-permute-start = (bf16[128,512]{1,0:T(8,128)(2,1)S(1)}, bf16[128,512]{1,0:T(8,128)(2,1)}, u32[]{:S(2)}, u32[]{:S(2)}) collective-permute-start(bf16[128,512]{1,0:T(8,128)(2,1)S(1)} %dynamic-slice_maximum_fusion), channel_id=1, source_target_pairs={{0,8},{2,10},{4,12},{6,14},{8,0},{10,2},{12,4},{14,6},{16,24},{18,... | collective-permute-start | bytes 393224 | tf_op jit(solution)/shard_map/ppermute | solution.py:32
  4.8 2.6 %collective-permute-start.1 = (bf16[128,512]{1,0:T(8,128)(2,1)S(1)}, bf16[128,512]{1,0:T(8,128)(2,1)}, u32[]{:S(2)}, u32[]{:S(2)}) collective-permute-start(bf16[128,512]{1,0:T(8,128)(2,1)S(1)} %dynamic-slice_maximum_fusion), channel_id=1, source_target_pairs={{0,16},{2,18},{4,20},{6,22},{8,24},{10,26},{12,28},{14,30},{16,0},... | collective-permute-start | bytes 393224 | tf_op jit(solution)/shard_map/ppermute | solution.py:32
  7.4 0.7 %add_bitcast_fusion = s32[8]{0:T(128)S(1)} fusion(s32[1,8]{1,0:T(1,128)} %param.7, s32[]{:T(128)S(6)} %shift_right_arithmetic.54, s32[]{:T(128)S(6)} %and.60), kind=kLoop, calls=%fused_computation.92 | loop fusion | flops 56 | bytes 72 | tf_op jit(solution)/shard_map/eq | solution.py:74
  8.2 0.9 %slice_bitcast_fusion.9 = (bf16[128,128]{1,0:T(8,128)(2,1)S(1)}, bf16[128,128]{1,0:T(8,128)(2,1)S(1)}, bf16[128,128]{1,0:T(8,128)(2,1)S(1)}, bf16[128,128]{1,0:T...) fusion(bf16[1,8,128,128]{3,2,1,0:T(8,128)(2,1)} %param.6), kind=kLoop, calls=%fused_computation.73 | loop fusion | bytes 524288 | tf_op jit(solution)/shard_map/jit(_where)/broadcast_in_dim | solution.py:77
  9.3 1.6 %collective-permute-start.3 = (bf16[2,128,128]{2,1,0:T(8,128)(2,1)S(1)}, bf16[2,128,128]{2,1,0:T(8,128)(2,1)S(1)}, u32[]{:S(2)}, u32[]{:S(2)}) collective-permute-start(bf16[2,128,128]{2,1,0:T(8,128)(2,1)S(1)} %get-tuple-element.33), channel_id=1, source_target_pairs={{0,2},{2,0},{4,6},{6,4},{8,10},{10,8},{12,14},{14,12},{16,18},{18,... | collective-permute-start | bytes 196616 | tf_op jit(solution)/shard_map/ppermute | solution.py:28
  10.9 1.5 %collective-permute-start.4 = (bf16[2,128,128]{2,1,0:T(8,128)(2,1)S(1)}, bf16[2,128,128]{2,1,0:T(8,128)(2,1)S(1)}, u32[]{:S(2)}, u32[]{:S(2)}) collective-permute-start(bf16[2,128,128]{2,1,0:T(8,128)(2,1)S(1)} %get-tuple-element.32), channel_id=1, source_target_pairs={{0,4},{2,6},{4,0},{6,2},{8,12},{10,14},{12,8},{14,10},{16,20},{18,... | collective-permute-start | bytes 196616 | tf_op jit(solution)/shard_map/ppermute | solution.py:28
  12.9 0.7 %collective-permute-done.3 = bf16[2,128,128]{2,1,0:T(8,128)(2,1)S(1)} collective-permute-done((bf16[2,128,128]{2,1,0:T(8,128)(2,1)S(1)}, bf16[2,128,128]{2,1,0:T(8,128)(2,1)S(1)}, u32[]{:S(2)}, u32[]{:S(2)}) %collective-permute-start.3) | collective-permute-done | bytes 65568 | tf_op jit(solution)/shard_map/ppermute | solution.py:28
  13.6 2.2 %collective-permute-done.4 = bf16[2,128,128]{2,1,0:T(8,128)(2,1)S(1)} collective-permute-done((bf16[2,128,128]{2,1,0:T(8,128)(2,1)S(1)}, bf16[2,128,128]{2,1,0:T(8,128)(2,1)S(1)}, u32[]{:S(2)}, u32[]{:S(2)}) %collective-permute-start.4) | collective-permute-done | bytes 65568 | tf_op jit(solution)/shard_map/ppermute | solution.py:28
  15.8 0.5 collective-permute-start.11
  16.4 1.8 %collective-permute-done.5 = bf16[2,128,128]{2,1,0:T(8,128)(2,1)S(1)} collective-permute-done((bf16[2,128,128]{2,1,0:T(8,128)(2,1)S(1)}, bf16[2,128,128]{2,1,0:T(8,128)(2,1)S(1)}, u32[]{:S(2)}, u32[]{:S(2)}) %collective-permute-start.5) | collective-permute-done | bytes 65568 | tf_op jit(solution)/shard_map/ppermute | solution.py:28
  18.7 2.2 %all-gather = bf16[16,128,128]{2,1,0:T(8,128)(2,1)S(1)} all-gather(bf16[8,128,128]{2,1,0:T(8,128)(2,1)S(1)} %pad_maximum_fusion.1), channel_id=2, replica_groups=mesh['blk'=16,'rep'=2] {'rep'}, dimensions={0}, use_global_device_ids=true | all-gather | bytes 786432 | tf_op jit(solution)/shard_map/all_gather | solution.py:81
  21.1 1.6 %collective-permute-start.13 = (bf16[128,512]{1,0:T(8,128)(2,1)S(1)}, bf16[128,512]{1,0:T(8,128)(2,1)S(1)}, u32[]{:S(2)}, u32[]{:S(2)}) collective-permute-start(bf16[128,512]{1,0:T(8,128)(2,1)S(1)} %constant_dynamic-slice_fusion), channel_id=1, source_target_pairs={{0,6},{2,4},{4,2},{6,0},{8,14},{10,12},{12,10},{14,8},{16,22},{18,... | collective-permute-start | bytes 393224 | tf_op jit(solution)/shard_map/ppermute | solution.py:28
  22.6 1.5 %convolution_convert_fusion = bf16[512,512]{1,0:T(8,128)(2,1)S(1)} fusion(bf16[512,512]{1,0:T(8,128)(2,1)S(1)} %maximum_maximum_fusion, bf16[128,512]{1,0:T(8,128)(2,1)S(1)} %collective-permute-done.2, bf16[128,512]{1,0:T(8,128)(2,1)} %collective-permute-done.1, bf16[128,512]{1,0:T(8,128)(2,1)} %collective-permute-done, ...), kind=kOutput, calls=%fused_computation.1 | convolution fusion | flops 270794752 | bytes 1572864 | tf_op jit(solution)/shard_map/dot_general | solution.py:54
  24.2 1.6 %collective-permute-start.6 = (bf16[128,512]{1,0:T(8,128)(2,1)S(1)}, bf16[128,512]{1,0:T(8,128)(2,1)S(1)}, u32[]{:S(2)}, u32[]{:S(2)}) collective-permute-start(bf16[128,512]{1,0:T(8,128)(2,1)S(1)} %pad_maximum_fusion.3), channel_id=1, source_target_pairs={{0,2},{2,0},{4,6},{6,4},{8,10},{10,8},{12,14},{14,12},{16,18},{18,... | collective-permute-start | bytes 393224 | tf_op jit(solution)/shard_map/ppermute | solution.py:28
  25.8 0.6 collective-permute-start.7
  26.4 1.6 %collective-permute-start.8 = (bf16[128,512]{1,0:T(8,128)(2,1)S(1)}, bf16[128,512]{1,0:T(8,128)(2,1)S(1)}, u32[]{:S(2)}, u32[]{:S(2)}) collective-permute-start(bf16[128,512]{1,0:T(8,128)(2,1)S(1)} %pad_maximum_fusion.5), channel_id=1, source_target_pairs={{0,6},{2,4},{4,2},{6,0},{8,14},{10,12},{12,10},{14,8},{16,22},{18,... | collective-permute-start | bytes 393224 | tf_op jit(solution)/shard_map/ppermute | solution.py:28
  28.8 2.4 %collective-permute-done.6 = bf16[128,512]{1,0:T(8,128)(2,1)S(1)} collective-permute-done((bf16[128,512]{1,0:T(8,128)(2,1)S(1)}, bf16[128,512]{1,0:T(8,128)(2,1)S(1)}, u32[]{:S(2)}, u32[]{:S(2)}) %collective-permute-start.6) | collective-permute-done | bytes 131104 | tf_op jit(solution)/shard_map/ppermute | solution.py:28
  31.2 2.6 %collective-permute-done.7 = bf16[128,512]{1,0:T(8,128)(2,1)S(1)} collective-permute-done((bf16[128,512]{1,0:T(8,128)(2,1)S(1)}, bf16[128,512]{1,0:T(8,128)(2,1)S(1)}, u32[]{:S(2)}, u32[]{:S(2)}) %collective-permute-start.7) | collective-permute-done | bytes 131104 | tf_op jit(solution)/shard_map/ppermute | solution.py:28
  33.9 2.0 %all_gather.11 = bf16[256,512]{1,0:T(8,128)(2,1)S(1)} all-gather(bf16[128,512]{1,0:T(8,128)(2,1)S(1)} %fusion.20), channel_id=1, replica_groups=mesh['blk'=16,'rep'=2] {'rep'}, dimensions={0}, use_global_device_ids=true | all-gather | bytes 393216 | tf_op jit(solution)/shard_map/all_gather | solution.py:114
  37.6 2.0 %collective-permute-start.15 = (bf16[64,512]{1,0:T(8,128)(2,1)S(1)}, bf16[64,512]{1,0:T(8,128)(2,1)S(1)}, u32[]{:S(2)}, u32[]{:S(2)}) collective-permute-start(bf16[64,512]{1,0:T(8,128)(2,1)S(1)} %get-tuple-element.29), channel_id=1, source_target_pairs={{0,16},{2,18},{4,20},{6,22},{8,24},{10,26},{12,28},{14,30},{16,0},... | collective-permute-start | bytes 196616 | tf_op jit(solution)/shard_map/ppermute | solution.py:32
  39.5 2.0 %collective-permute-start.16 = (bf16[64,512]{1,0:T(8,128)(2,1)S(1)}, bf16[64,512]{1,0:T(8,128)(2,1)S(1)}, u32[]{:S(2)}, u32[]{:S(2)}) collective-permute-start(bf16[64,512]{1,0:T(8,128)(2,1)S(1)} %get-tuple-element.28), channel_id=1, source_target_pairs={{0,24},{2,26},{4,28},{6,30},{8,16},{10,18},{12,20},{14,22},{16,8},... | collective-permute-start | bytes 196616 | tf_op jit(solution)/shard_map/ppermute | solution.py:32
  42.1 2.0 %collective-permute-start.18 = (bf16[512,128]{1,0:T(8,128)(2,1)S(1)}, bf16[512,128]{1,0:T(8,128)(2,1)S(1)}, u32[]{:S(2)}, u32[]{:S(2)}) collective-permute-start(bf16[512,128]{1,0:T(8,128)(2,1)S(1)} %get-tuple-element.5), channel_id=1, source_target_pairs={{0,16},{2,18},{4,20},{6,22},{8,24},{10,26},{12,28},{14,30},{16,0},... | collective-permute-start | bytes 393224 | tf_op jit(solution)/shard_map/ppermute | solution.py:32
  44.0 1.3 %collective-permute-done.15 = bf16[64,512]{1,0:T(8,128)(2,1)S(1)} collective-permute-done((bf16[64,512]{1,0:T(8,128)(2,1)S(1)}, bf16[64,512]{1,0:T(8,128)(2,1)S(1)}, u32[]{:S(2)}, u32[]{:S(2)}) %collective-permute-start.15) | collective-permute-done | bytes 65568 | tf_op jit(solution)/shard_map/ppermute | solution.py:32
  45.4 1.8 %collective-permute-start.19 = (bf16[512,128]{1,0:T(8,128)(2,1)S(1)}, bf16[512,128]{1,0:T(8,128)(2,1)S(1)}, u32[]{:S(2)}, u32[]{:S(2)}) collective-permute-start(bf16[512,128]{1,0:T(8,128)(2,1)S(1)} %get-tuple-element.4), channel_id=1, source_target_pairs={{0,24},{2,26},{4,28},{6,30},{8,16},{10,18},{12,20},{14,22},{16,8},... | collective-permute-start | bytes 393224 | tf_op jit(solution)/shard_map/ppermute | solution.py:32
  47.1 0.7 %fusion.24 = f32[64,512]{1,0:T(8,128)} fusion(bf16[64,512]{1,0:T(8,128)(2,1)S(1)} %collective-permute-done.16, bf16[64,512]{1,0:T(8,128)(2,1)S(1)} %collective-permute-done.15, bf16[64,512]{1,0:T(8,128)(2,1)S(1)} %collective-permute-done.14, bf16[4,64,512]{2,1,0:T(8,128)(2,1)S(1)} %bitcast.118, s32[]{:T(128)S(6)} %select_n.271), kind=kLoop, calls=%fused_computation.43 | loop fusion | flops 229376 | bytes 393220 | tf_op jit(solution)/shard_map/add | solution.py:121
  47.8 0.8 %collective-permute-start.10 = (bf16[128,512]{1,0:T(8,128)(2,1)S(1)}, bf16[128,512]{1,0:T(8,128)(2,1)S(1)}, u32[]{:S(2)}, u32[]{:S(2)}) collective-permute-start(bf16[128,512]{1,0:T(8,128)(2,1)S(1)} %fusion.14), channel_id=1, source_target_pairs={{0,4},{2,6},{4,0},{6,2},{8,12},{10,14},{12,8},{14,10},{16,20},{18,... | collective-permute-start | bytes 393224 | tf_op jit(solution)/shard_map/ppermute | solution.py:28
  48.7 0.9 %collective-permute-done.17 = bf16[512,128]{1,0:T(8,128)(2,1)S(1)} collective-permute-done((bf16[512,128]{1,0:T(8,128)(2,1)S(1)}, bf16[512,128]{1,0:T(8,128)(2,1)S(1)}, u32[]{:S(2)}, u32[]{:S(2)}) %collective-permute-start.17) | collective-permute-done | bytes 131104 | tf_op jit(solution)/shard_map/ppermute | solution.py:32
  49.6 6.0 %collective-permute-done.18 = bf16[512,128]{1,0:T(8,128)(2,1)S(1)} collective-permute-done((bf16[512,128]{1,0:T(8,128)(2,1)S(1)}, bf16[512,128]{1,0:T(8,128)(2,1)S(1)}, u32[]{:S(2)}, u32[]{:S(2)}) %collective-permute-start.18) | collective-permute-done | bytes 131104 | tf_op jit(solution)/shard_map/ppermute | solution.py:32
  56.3 0.7 %fusion.16 = bf16[128,512]{1,0:T(8,128)(2,1)} fusion(f32[512,512]{1,0:T(8,128)S(1)} %get-tuple-element.61, bf16[128,512]{1,0:T(8,128)(2,1)S(1)} %collective-permute-done.10, bf16[256,512]{1,0:T(8,128)(2,1)S(1)} %collective-permute-done.9), kind=kLoop, calls=%fused_computation.25 | loop fusion | flops 327680 | bytes 655360 | tf_op jit(solution)/shard_map/convert_element_type | solution.py:131
  57.0 0.6 %collective-permute-done.20 = bf16[128,512]{1,0:T(8,128)(2,1)S(1)} collective-permute-done((bf16[128,512]{1,0:T(8,128)(2,1)S(1)}, bf16[128,512]{1,0:T(8,128)(2,1)S(1)}, u32[]{:S(2)}, u32[]{:S(2)}) %collective-permute-start.20) | collective-permute-done | bytes 131104 | tf_op jit(solution)/shard_map/ppermute | solution.py:51
  57.6 1.1 %select_convert_fusion = bf16[128,512]{1,0:T(8,128)(2,1)} fusion(bf16[128,512]{1,0:T(8,128)(2,1)S(1)} %collective-permute-done.20, bf16[128,1024]{1,0:T(8,128)(2,1)S(1)} %copy-done.1, s32[]{:T(128)S(6)} %select_n.214, bf16[512,128]{1,0:T(8,128)(2,1)S(1)} %fusion.17, bf16[2,512,1024]{2,1,0:T(8,128)(2,1)S(1)} %bitcast.107, s32[]{:T(128)S(6)} %select_n.279, ...), kind=kOutput, calls=%fused_computation.34 | convolution fusion | flops 67567616 | bytes 1048588 | tf_op jit(solution)/shard_map/dot_general | solution.py:54
  (56 shorter events, 5.4 us)
Async XLA Ops:
  0.6 12.2 %copy-start = (bf16[1024,1024]{1,0:T(8,128)(2,1)S(1)}, bf16[1024,1024]{1,0:T(8,128)(2,1)}, u32[]{:S(2)}) copy-start(bf16[1024,1024]{1,0:T(8,128)(2,1)} %param.8) | copy-start | bytes 6291460
  0.6 12.3 %copy-start.2 = (bf16[128,1024]{1,0:T(8,128)(2,1)S(1)}, bf16[128,1024]{1,0:T(8,128)(2,1)}, u32[]{:S(2)}) copy-start(bf16[128,1024]{1,0:T(8,128)(2,1)} %param.9) | copy-start | bytes 786436
  1.7 19.3 %collective-permute-start = (bf16[128,512]{1,0:T(8,128)(2,1)S(1)}, bf16[128,512]{1,0:T(8,128)(2,1)}, u32[]{:S(2)}, u32[]{:S(2)}) collective-permute-start(bf16[128,512]{1,0:T(8,128)(2,1)S(1)} %dynamic-slice_maximum_fusion), channel_id=1, source_target_pairs={{0,8},{2,10},{4,12},{6,14},{8,0},{10,2},{12,4},{14,6},{16,24},{18,... | collective-permute-start | bytes 393224 | tf_op jit(solution)/shard_map/ppermute | solution.py:32
  4.8 17.8 %collective-permute-start.1 = (bf16[128,512]{1,0:T(8,128)(2,1)S(1)}, bf16[128,512]{1,0:T(8,128)(2,1)}, u32[]{:S(2)}, u32[]{:S(2)}) collective-permute-start(bf16[128,512]{1,0:T(8,128)(2,1)S(1)} %dynamic-slice_maximum_fusion), channel_id=1, source_target_pairs={{0,16},{2,18},{4,20},{6,22},{8,24},{10,26},{12,28},{14,30},{16,0},... | collective-permute-start | bytes 393224 | tf_op jit(solution)/shard_map/ppermute | solution.py:32
  9.3 4.3 %collective-permute-start.3 = (bf16[2,128,128]{2,1,0:T(8,128)(2,1)S(1)}, bf16[2,128,128]{2,1,0:T(8,128)(2,1)S(1)}, u32[]{:S(2)}, u32[]{:S(2)}) collective-permute-start(bf16[2,128,128]{2,1,0:T(8,128)(2,1)S(1)} %get-tuple-element.33), channel_id=1, source_target_pairs={{0,2},{2,0},{4,6},{6,4},{8,10},{10,8},{12,14},{14,12},{16,18},{18,... | collective-permute-start | bytes 196616 | tf_op jit(solution)/shard_map/ppermute | solution.py:28
  10.9 5.0 %collective-permute-start.4 = (bf16[2,128,128]{2,1,0:T(8,128)(2,1)S(1)}, bf16[2,128,128]{2,1,0:T(8,128)(2,1)S(1)}, u32[]{:S(2)}, u32[]{:S(2)}) collective-permute-start(bf16[2,128,128]{2,1,0:T(8,128)(2,1)S(1)} %get-tuple-element.32), channel_id=1, source_target_pairs={{0,4},{2,6},{4,0},{6,2},{8,12},{10,14},{12,8},{14,10},{16,20},{18,... | collective-permute-start | bytes 196616 | tf_op jit(solution)/shard_map/ppermute | solution.py:28
  12.4 5.8 %collective-permute-start.5 = (bf16[2,128,128]{2,1,0:T(8,128)(2,1)S(1)}, bf16[2,128,128]{2,1,0:T(8,128)(2,1)S(1)}, u32[]{:S(2)}, u32[]{:S(2)}) collective-permute-start(bf16[2,128,128]{2,1,0:T(8,128)(2,1)S(1)} %get-tuple-element.31), channel_id=1, source_target_pairs={{0,6},{2,4},{4,2},{6,0},{8,14},{10,12},{12,10},{14,8},{16,22},{18,... | collective-permute-start | bytes 196616 | tf_op jit(solution)/shard_map/ppermute | solution.py:28
  13.6 9.0 %collective-permute-start.2 = (bf16[128,512]{1,0:T(8,128)(2,1)S(1)}, bf16[128,512]{1,0:T(8,128)(2,1)S(1)}, u32[]{:S(2)}, u32[]{:S(2)}) collective-permute-start(bf16[128,512]{1,0:T(8,128)(2,1)S(1)} %dynamic-slice_maximum_fusion), channel_id=1, source_target_pairs={{0,24},{2,26},{4,28},{6,30},{8,16},{10,18},{12,20},{14,22},{16,8},... | collective-permute-start | bytes 393224 | tf_op jit(solution)/shard_map/ppermute | solution.py:32
  15.8 10.6 %collective-permute-start.11 = (bf16[128,512]{1,0:T(8,128)(2,1)S(1)}, bf16[128,512]{1,0:T(8,128)(2,1)S(1)}, u32[]{:S(2)}, u32[]{:S(2)}) collective-permute-start(bf16[128,512]{1,0:T(8,128)(2,1)S(1)} %constant_dynamic-slice_fusion), channel_id=1, source_target_pairs={{0,2},{2,0},{4,6},{6,4},{8,10},{10,8},{12,14},{14,12},{16,18},{18,... | collective-permute-start | bytes 393224 | tf_op jit(solution)/shard_map/ppermute | solution.py:28
  18.2 9.8 %collective-permute-start.12 = (bf16[128,512]{1,0:T(8,128)(2,1)S(1)}, bf16[128,512]{1,0:T(8,128)(2,1)S(1)}, u32[]{:S(2)}, u32[]{:S(2)}) collective-permute-start(bf16[128,512]{1,0:T(8,128)(2,1)S(1)} %constant_dynamic-slice_fusion), channel_id=1, source_target_pairs={{0,4},{2,6},{4,0},{6,2},{8,12},{10,14},{12,8},{14,10},{16,20},{18,... | collective-permute-start | bytes 393224 | tf_op jit(solution)/shard_map/ppermute | solution.py:28
  21.1 7.3 %collective-permute-start.13 = (bf16[128,512]{1,0:T(8,128)(2,1)S(1)}, bf16[128,512]{1,0:T(8,128)(2,1)S(1)}, u32[]{:S(2)}, u32[]{:S(2)}) collective-permute-start(bf16[128,512]{1,0:T(8,128)(2,1)S(1)} %constant_dynamic-slice_fusion), channel_id=1, source_target_pairs={{0,6},{2,4},{4,2},{6,0},{8,14},{10,12},{12,10},{14,8},{16,22},{18,... | collective-permute-start | bytes 393224 | tf_op jit(solution)/shard_map/ppermute | solution.py:28
  24.2 7.0 %collective-permute-start.6 = (bf16[128,512]{1,0:T(8,128)(2,1)S(1)}, bf16[128,512]{1,0:T(8,128)(2,1)S(1)}, u32[]{:S(2)}, u32[]{:S(2)}) collective-permute-start(bf16[128,512]{1,0:T(8,128)(2,1)S(1)} %pad_maximum_fusion.3), channel_id=1, source_target_pairs={{0,2},{2,0},{4,6},{6,4},{8,10},{10,8},{12,14},{14,12},{16,18},{18,... | collective-permute-start | bytes 393224 | tf_op jit(solution)/shard_map/ppermute | solution.py:28
  25.8 8.0 %collective-permute-start.7 = (bf16[128,512]{1,0:T(8,128)(2,1)S(1)}, bf16[128,512]{1,0:T(8,128)(2,1)S(1)}, u32[]{:S(2)}, u32[]{:S(2)}) collective-permute-start(bf16[128,512]{1,0:T(8,128)(2,1)S(1)} %pad_maximum_fusion.4), channel_id=1, source_target_pairs={{0,4},{2,6},{4,0},{6,2},{8,12},{10,14},{12,8},{14,10},{16,20},{18,... | collective-permute-start | bytes 393224 | tf_op jit(solution)/shard_map/ppermute | solution.py:28
  26.4 7.4 %collective-permute-start.8 = (bf16[128,512]{1,0:T(8,128)(2,1)S(1)}, bf16[128,512]{1,0:T(8,128)(2,1)S(1)}, u32[]{:S(2)}, u32[]{:S(2)}) collective-permute-start(bf16[128,512]{1,0:T(8,128)(2,1)S(1)} %pad_maximum_fusion.5), channel_id=1, source_target_pairs={{0,6},{2,4},{4,2},{6,0},{8,14},{10,12},{12,10},{14,8},{16,22},{18,... | collective-permute-start | bytes 393224 | tf_op jit(solution)/shard_map/ppermute | solution.py:28
  36.3 11.5 %collective-permute-start.9 = (bf16[256,512]{1,0:T(8,128)(2,1)S(1)}, bf16[256,512]{1,0:T(8,128)(2,1)S(1)}, u32[]{:S(2)}, u32[]{:S(2)}) collective-permute-start(bf16[256,512]{1,0:T(8,128)(2,1)S(1)} %pad_maximum_fusion.2), channel_id=1, source_target_pairs={{0,2},{2,0},{4,6},{6,4},{8,10},{10,8},{12,14},{14,12},{16,18},{18,... | collective-permute-start | bytes 786440 | tf_op jit(solution)/shard_map/ppermute | solution.py:28
  37.0 20.6 %copy-start.1 = (bf16[128,1024]{1,0:T(8,128)(2,1)S(1)}, bf16[128,1024]{1,0:T(8,128)(2,1)}, u32[]{:S(2)}) copy-start(bf16[128,1024]{1,0:T(8,128)(2,1)} %param.5) | copy-start | bytes 786436
  37.1 5.0 %collective-permute-start.14 = (bf16[64,512]{1,0:T(8,128)(2,1)S(1)}, bf16[64,512]{1,0:T(8,128)(2,1)S(1)}, u32[]{:S(2)}, u32[]{:S(2)}) collective-permute-start(bf16[64,512]{1,0:T(8,128)(2,1)S(1)} %get-tuple-element.27), channel_id=1, source_target_pairs={{0,8},{2,10},{4,12},{6,14},{8,0},{10,2},{12,4},{14,6},{16,24},{18,... | collective-permute-start | bytes 196616 | tf_op jit(solution)/shard_map/ppermute | solution.py:32
  37.6 7.8 %collective-permute-start.15 = (bf16[64,512]{1,0:T(8,128)(2,1)S(1)}, bf16[64,512]{1,0:T(8,128)(2,1)S(1)}, u32[]{:S(2)}, u32[]{:S(2)}) collective-permute-start(bf16[64,512]{1,0:T(8,128)(2,1)S(1)} %get-tuple-element.29), channel_id=1, source_target_pairs={{0,16},{2,18},{4,20},{6,22},{8,24},{10,26},{12,28},{14,30},{16,0},... | collective-permute-start | bytes 196616 | tf_op jit(solution)/shard_map/ppermute | solution.py:32
  39.5 7.6 %collective-permute-start.16 = (bf16[64,512]{1,0:T(8,128)(2,1)S(1)}, bf16[64,512]{1,0:T(8,128)(2,1)S(1)}, u32[]{:S(2)}, u32[]{:S(2)}) collective-permute-start(bf16[64,512]{1,0:T(8,128)(2,1)S(1)} %get-tuple-element.28), channel_id=1, source_target_pairs={{0,24},{2,26},{4,28},{6,30},{8,16},{10,18},{12,20},{14,22},{16,8},... | collective-permute-start | bytes 196616 | tf_op jit(solution)/shard_map/ppermute | solution.py:32
  41.6 8.0 %collective-permute-start.17 = (bf16[512,128]{1,0:T(8,128)(2,1)S(1)}, bf16[512,128]{1,0:T(8,128)(2,1)S(1)}, u32[]{:S(2)}, u32[]{:S(2)}) collective-permute-start(bf16[512,128]{1,0:T(8,128)(2,1)S(1)} %get-tuple-element.3), channel_id=1, source_target_pairs={{0,8},{2,10},{4,12},{6,14},{8,0},{10,2},{12,4},{14,6},{16,24},{18,... | collective-permute-start | bytes 393224 | tf_op jit(solution)/shard_map/ppermute | solution.py:32
  42.1 13.6 %collective-permute-start.18 = (bf16[512,128]{1,0:T(8,128)(2,1)S(1)}, bf16[512,128]{1,0:T(8,128)(2,1)S(1)}, u32[]{:S(2)}, u32[]{:S(2)}) collective-permute-start(bf16[512,128]{1,0:T(8,128)(2,1)S(1)} %get-tuple-element.5), channel_id=1, source_target_pairs={{0,16},{2,18},{4,20},{6,22},{8,24},{10,26},{12,28},{14,30},{16,0},... | collective-permute-start | bytes 393224 | tf_op jit(solution)/shard_map/ppermute | solution.py:32
  45.4 10.3 %collective-permute-start.19 = (bf16[512,128]{1,0:T(8,128)(2,1)S(1)}, bf16[512,128]{1,0:T(8,128)(2,1)S(1)}, u32[]{:S(2)}, u32[]{:S(2)}) collective-permute-start(bf16[512,128]{1,0:T(8,128)(2,1)S(1)} %get-tuple-element.4), channel_id=1, source_target_pairs={{0,24},{2,26},{4,28},{6,30},{8,16},{10,18},{12,20},{14,22},{16,8},... | collective-permute-start | bytes 393224 | tf_op jit(solution)/shard_map/ppermute | solution.py:32
  47.8 8.4 %collective-permute-start.10 = (bf16[128,512]{1,0:T(8,128)(2,1)S(1)}, bf16[128,512]{1,0:T(8,128)(2,1)S(1)}, u32[]{:S(2)}, u32[]{:S(2)}) collective-permute-start(bf16[128,512]{1,0:T(8,128)(2,1)S(1)} %fusion.14), channel_id=1, source_target_pairs={{0,4},{2,6},{4,0},{6,2},{8,12},{10,14},{12,8},{14,10},{16,20},{18,... | collective-permute-start | bytes 393224 | tf_op jit(solution)/shard_map/ppermute | solution.py:28
  56.2 1.4 %collective-permute-start.20 = (bf16[128,512]{1,0:T(8,128)(2,1)S(1)}, bf16[128,512]{1,0:T(8,128)(2,1)S(1)}, u32[]{:S(2)}, u32[]{:S(2)}) collective-permute-start(bf16[128,512]{1,0:T(8,128)(2,1)S(1)} %convolution_convert_fusion.1), channel_id=1, source_target_pairs={{0,1},{1,0},{2,3},{3,2},{4,5},{5,4},{6,7},{7,6},{8,9},{9,8},{10,11... | collective-permute-start | bytes 393224 | tf_op jit(solution)/shard_map/ppermute | solution.py:51

commit v20 on v18

--- a/solution.py
+++ b/solution.py
@@ -110,19 +110,16 @@
     back = sum(along_outer(lanes(back, e), e).astype(jnp.float32) for e in turns)
 
     mixed_cols = lax.all_gather(mixed_cols.astype(bf16), "rep", axis=0, tiled=True)
-    weight_part = dot(mixed_cols, grad_stack, ((1,), (0,))).astype(bf16)
-    by_outer = weight_part.reshape(side, rows_here, cols_here)
-    grad_weight = sum(
-        along_outer(
-            lax.dynamic_index_in_dim(by_outer, outer_pos ^ t, 0, keepdims=False), t
-        ).astype(jnp.float32)
-        for t in turns
-    )
-
     w_share = w_out.reshape(side, side, rows_here, feature_width)
     w_share = lax.dynamic_index_in_dim(w_share, inner_pos, 1, keepdims=False)
     w_share = columns_of(w_share.reshape(side * rows_here, feature_width), rep_pos)
     out_part = dot(mixed_cols, w_share, ((0,), (0,)))
+    weight_part = after(dot(mixed_cols, grad_stack, ((1,), (0,))), out_part)
+    by_outer = weight_part.reshape(side, rows_here, cols_here)
+    grad_weight = halved(
+        [lax.dynamic_index_in_dim(by_outer, outer_pos ^ t, 0, keepdims=False) for t in turns],
+        along_outer,
+    )
     out_part = halved(
         [out_part[t * tile_size : (t + 1) * tile_size] for t in turns], along_inner
     ).astype(bf16)

time: 54.7 us -> 52.1 us (0.952)
  starting transfers between devices: 27.1 us -> 25.2 us
  waiting for transfers between devices: 14.1 us -> 12.4 us
  matrix products: 3.09 us -> 4.05 us
    ppermute x11, waiting for transfers between devices: 7.39 us -> 3.25 us  [along_inner(): return lax.ppermute(value, 'blk', pairs) if turn else value]
    ppermute x9 -> x8, waiting for transfers between devices: 6.69 us -> 9.14 us  [along_outer(): return lax.ppermute(value, 'blk', pairs) if turn else value]
    ppermute x9 -> x8, starting transfers between devices: 14.1 us -> 12.3 us  [along_outer(): return lax.ppermute(value, 'blk', pairs) if turn else value]
    dot_general x6, matrix products: 3.09 us -> 4.05 us  [dot(): lax.dot_general(lhs, rhs, (dims, ((), ())), preferred_element_type=jnp.fl...]
  transfers between devices with their start and end apart: 21 -> 20, of which waited for: 7 -> 7; matrix products, arithmetic and copies ran while one was open for 12% -> 14% of each run, Pallas kernels for 0% -> 0%
where the time goes in v20:
time: 52.1 us; the launch traced here: 51.8 us
  starting transfers between devices  25.2 us (48%)
  waiting for transfers between devices  12.4 us (24%)
  blocking collectives  4.18 us (8%)
  matrix products  4.05 us (8%)
  other arithmetic  3.86 us (7%)
  local copies, waits for them, and re-layouts  1.22 us (2%)
  between operations  0.94 us (2%)
    ppermute x11, starting transfers between devices, along_inner(): return lax.ppermute(value, 'blk', pairs) if turn else value  12.8 us
    ppermute x8, starting transfers between devices, along_outer(): return lax.ppermute(value, 'blk', pairs) if turn else value  12.3 us
    ppermute x8, waiting for transfers between devices, along_outer(): return lax.ppermute(value, 'blk', pairs) if turn else value  9.14 us
    dot_general x6, matrix products, dot(): lax.dot_general(lhs, rhs, (dims, ((), ())), preferred_element_type=jnp.fl...  4.05 us
    ppermute x11, waiting for transfers between devices, along_inner(): return lax.ppermute(value, 'blk', pairs) if turn else value  3.25 us
    all_gather x1, blocking collectives, shards(): everyone = lax.all_gather(jnp.concatenate(arrived, 0), 'rep', axis=0)  2.18 us
    all_gather x1, blocking collectives, shards(): lax.all_gather(mixed_cols.astype(bf16), 'rep', axis=0, tiled=True)  1.99 us
    max x1, other arithmetic, shards(): hidden_part = jnp.maximum(columns_of(hidden_pre, rep_pos), 0)  1.08 us
  transfers between devices with their start and end apart: 20, of which 7 were waited for; matrix products, arithmetic and copies ran while one was open for 14% of the time, Pallas kernels for 0%

profile of v20, /device:TPU:0, one launch (start us, length us, event | category | flops | bytes accessed | tf_op | source)
XLA Modules:
  0.0 51.8 jit_solution(14723425122822864719)
XLA Ops:
  0.7 1.1 %dynamic-slice_maximum_fusion = bf16[128,512]{1,0:T(8,128)(2,1)S(1)} fusion(bf16[128,1024]{1,0:T(8,128)(2,1)} %param.5, s32[]{:T(128)S(6)} %select_n.214), kind=kLoop, calls=%fused_computation.48 | loop fusion | flops 262144 | bytes 262148 | tf_op jit(solution)/shard_map/max | solution.py:66
  1.7 5.1 %collective-permute-start.2 = (bf16[128,512]{1,0:T(8,128)(2,1)S(1)}, bf16[128,512]{1,0:T(8,128)(2,1)}, u32[]{:S(2)}, u32[]{:S(2)}) collective-permute-start(bf16[128,512]{1,0:T(8,128)(2,1)S(1)} %dynamic-slice_maximum_fusion), channel_id=1, source_target_pairs={{0,24},{2,26},{4,28},{6,30},{8,16},{10,18},{12,20},{14,22},{16,8},... | collective-permute-start | bytes 393224 | tf_op jit(solution)/shard_map/ppermute | solution.py:32
  6.9 0.7 %add_bitcast_fusion = s32[8]{0:T(128)S(1)} fusion(s32[1,8]{1,0:T(1,128)} %param.7, s32[]{:T(128)S(6)} %shift_right_arithmetic.54, s32[]{:T(128)S(6)} %and.60), kind=kLoop, calls=%fused_computation.94 | loop fusion | flops 56 | bytes 72 | tf_op jit(solution)/shard_map/eq | solution.py:72
  7.6 0.9 %slice_bitcast_fusion.9 = (bf16[128,128]{1,0:T(8,128)(2,1)S(1)}, bf16[128,128]{1,0:T(8,128)(2,1)S(1)}, bf16[128,128]{1,0:T(8,128)(2,1)S(1)}, bf16[128,128]{1,0:T...) fusion(bf16[1,8,128,128]{3,2,1,0:T(8,128)(2,1)} %param.6), kind=kLoop, calls=%fused_computation.75 | loop fusion | bytes 524288 | tf_op jit(solution)/shard_map/jit(_where)/broadcast_in_dim | solution.py:75
  8.7 2.5 %collective-permute-start.5 = (bf16[2,128,128]{2,1,0:T(8,128)(2,1)S(1)}, bf16[2,128,128]{2,1,0:T(8,128)(2,1)S(1)}, u32[]{:S(2)}, u32[]{:S(2)}) collective-permute-start(bf16[2,128,128]{2,1,0:T(8,128)(2,1)S(1)} %get-tuple-element.30), channel_id=1, source_target_pairs={{0,6},{2,4},{4,2},{6,0},{8,14},{10,12},{12,10},{14,8},{16,22},{18,... | collective-permute-start | bytes 196616 | tf_op jit(solution)/shard_map/ppermute | solution.py:28
  11.2 0.5 collective-permute-start.4
  11.8 0.5 %collective-permute-start.3 = (bf16[2,128,128]{2,1,0:T(8,128)(2,1)S(1)}, bf16[2,128,128]{2,1,0:T(8,128)(2,1)S(1)}, u32[]{:S(2)}, u32[]{:S(2)}) collective-permute-start(bf16[2,128,128]{2,1,0:T(8,128)(2,1)S(1)} %get-tuple-element.32), channel_id=1, source_target_pairs={{0,2},{2,0},{4,6},{6,4},{8,10},{10,8},{12,14},{14,12},{16,18},{18,... | collective-permute-start | bytes 196616 | tf_op jit(solution)/shard_map/ppermute | solution.py:28
  12.4 1.7 %collective-permute-done.5 = bf16[2,128,128]{2,1,0:T(8,128)(2,1)S(1)} collective-permute-done((bf16[2,128,128]{2,1,0:T(8,128)(2,1)S(1)}, bf16[2,128,128]{2,1,0:T(8,128)(2,1)S(1)}, u32[]{:S(2)}, u32[]{:S(2)}) %collective-permute-start.5) | collective-permute-done | bytes 65568 | tf_op jit(solution)/shard_map/ppermute | solution.py:28
  14.1 0.6 %collective-permute-start = (bf16[128,512]{1,0:T(8,128)(2,1)S(1)}, bf16[128,512]{1,0:T(8,128)(2,1)S(1)}, u32[]{:S(2)}, u32[]{:S(2)}) collective-permute-start(bf16[128,512]{1,0:T(8,128)(2,1)S(1)} %dynamic-slice_maximum_fusion), channel_id=1, source_target_pairs={{0,8},{2,10},{4,12},{6,14},{8,0},{10,2},{12,4},{14,6},{16,24},{18,... | collective-permute-start | bytes 393224 | tf_op jit(solution)/shard_map/ppermute | solution.py:32
  14.7 0.8 %collective-permute-done.4 = bf16[2,128,128]{2,1,0:T(8,128)(2,1)S(1)} collective-permute-done((bf16[2,128,128]{2,1,0:T(8,128)(2,1)S(1)}, bf16[2,128,128]{2,1,0:T(8,128)(2,1)S(1)}, u32[]{:S(2)}, u32[]{:S(2)}) %collective-permute-start.4) | collective-permute-done | bytes 65568 | tf_op jit(solution)/shard_map/ppermute | solution.py:28
  15.5 1.8 %collective-permute-start.13 = (bf16[128,512]{1,0:T(8,128)(2,1)S(1)}, bf16[128,512]{1,0:T(8,128)(2,1)S(1)}, u32[]{:S(2)}, u32[]{:S(2)}) collective-permute-start(bf16[128,512]{1,0:T(8,128)(2,1)S(1)} %constant_dynamic-slice_fusion), channel_id=1, source_target_pairs={{0,6},{2,4},{4,2},{6,0},{8,14},{10,12},{12,10},{14,8},{16,22},{18,... | collective-permute-start | bytes 393224 | tf_op jit(solution)/shard_map/ppermute | solution.py:28
  17.3 1.1 %collective-permute-start.12 = (bf16[128,512]{1,0:T(8,128)(2,1)S(1)}, bf16[128,512]{1,0:T(8,128)(2,1)S(1)}, u32[]{:S(2)}, u32[]{:S(2)}) collective-permute-start(bf16[128,512]{1,0:T(8,128)(2,1)S(1)} %constant_dynamic-slice_fusion), channel_id=1, source_target_pairs={{0,4},{2,6},{4,0},{6,2},{8,12},{10,14},{12,8},{14,10},{16,20},{18,... | collective-permute-start | bytes 393224 | tf_op jit(solution)/shard_map/ppermute | solution.py:28
  18.5 2.2 %all-gather = bf16[16,128,128]{2,1,0:T(8,128)(2,1)S(1)} all-gather(bf16[8,128,128]{2,1,0:T(8,128)(2,1)S(1)} %pad_maximum_fusion.1), channel_id=2, replica_groups=mesh['blk'=16,'rep'=2] {'rep'}, dimensions={0}, use_global_device_ids=true | all-gather | bytes 786432 | tf_op jit(solution)/shard_map/all_gather | solution.py:79
  20.9 0.6 %collective-permute-start.11 = (bf16[128,512]{1,0:T(8,128)(2,1)S(1)}, bf16[128,512]{1,0:T(8,128)(2,1)S(1)}, u32[]{:S(2)}, u32[]{:S(2)}) collective-permute-start(bf16[128,512]{1,0:T(8,128)(2,1)S(1)} %constant_dynamic-slice_fusion), channel_id=1, source_target_pairs={{0,2},{2,0},{4,6},{6,4},{8,10},{10,8},{12,14},{14,12},{16,18},{18,... | collective-permute-start | bytes 393224 | tf_op jit(solution)/shard_map/ppermute | solution.py:28
  21.5 1.5 %convolution_convert_fusion = bf16[512,512]{1,0:T(8,128)(2,1)S(1)} fusion(bf16[512,512]{1,0:T(8,128)(2,1)S(1)} %maximum_maximum_fusion, bf16[128,512]{1,0:T(8,128)(2,1)} %collective-permute-done.2, bf16[128,512]{1,0:T(8,128)(2,1)} %collective-permute-done.1, bf16[128,512]{1,0:T(8,128)(2,1)S(1)} %collective-permute-done, ...), kind=kOutput, calls=%fused_computation.1 | convolution fusion | flops 270794752 | bytes 1572864 | tf_op jit(solution)/shard_map/dot_general | solution.py:52
  23.1 1.9 %collective-permute-start.8 = (bf16[128,512]{1,0:T(8,128)(2,1)S(1)}, bf16[128,512]{1,0:T(8,128)(2,1)S(1)}, u32[]{:S(2)}, u32[]{:S(2)}) collective-permute-start(bf16[128,512]{1,0:T(8,128)(2,1)S(1)} %pad_maximum_fusion.5), channel_id=1, source_target_pairs={{0,6},{2,4},{4,2},{6,0},{8,14},{10,12},{12,10},{14,8},{16,22},{18,... | collective-permute-start | bytes 393224 | tf_op jit(solution)/shard_map/ppermute | solution.py:28
  25.0 1.2 %collective-permute-start.7 = (bf16[128,512]{1,0:T(8,128)(2,1)S(1)}, bf16[128,512]{1,0:T(8,128)(2,1)S(1)}, u32[]{:S(2)}, u32[]{:S(2)}) collective-permute-start(bf16[128,512]{1,0:T(8,128)(2,1)S(1)} %pad_maximum_fusion.4), channel_id=1, source_target_pairs={{0,4},{2,6},{4,0},{6,2},{8,12},{10,14},{12,8},{14,10},{16,20},{18,... | collective-permute-start | bytes 393224 | tf_op jit(solution)/shard_map/ppermute | solution.py:28
  26.2 0.6 %collective-permute-start.6 = (bf16[128,512]{1,0:T(8,128)(2,1)S(1)}, bf16[128,512]{1,0:T(8,128)(2,1)S(1)}, u32[]{:S(2)}, u32[]{:S(2)}) collective-permute-start(bf16[128,512]{1,0:T(8,128)(2,1)S(1)} %pad_maximum_fusion.3), channel_id=1, source_target_pairs={{0,2},{2,0},{4,6},{6,4},{8,10},{10,8},{12,14},{14,12},{16,18},{18,... | collective-permute-start | bytes 393224 | tf_op jit(solution)/shard_map/ppermute | solution.py:28
  27.4 3.1 %collective-permute-start.18 = (bf16[512,128]{1,0:T(8,128)(2,1)S(1)}, bf16[512,128]{1,0:T(8,128)(2,1)S(1)}, u32[]{:S(2)}, u32[]{:S(2)}) collective-permute-start(bf16[512,128]{1,0:T(8,128)(2,1)S(1)} %get-tuple-element.4), channel_id=1, source_target_pairs={{0,24},{2,26},{4,28},{6,30},{8,16},{10,18},{12,20},{14,22},{16,8},... | collective-permute-start | bytes 393224 | tf_op jit(solution)/shard_map/ppermute | solution.py:32
  30.5 1.3 %collective-permute-start.16 = (bf16[512,128]{1,0:T(8,128)(2,1)S(1)}, bf16[512,128]{1,0:T(8,128)(2,1)S(1)}, u32[]{:S(2)}, u32[]{:S(2)}) collective-permute-start(bf16[512,128]{1,0:T(8,128)(2,1)S(1)} %get-tuple-element.3), channel_id=1, source_target_pairs={{0,8},{2,10},{4,12},{6,14},{8,0},{10,2},{12,4},{14,6},{16,24},{18,... | collective-permute-start | bytes 393224 | tf_op jit(solution)/shard_map/ppermute | solution.py:32
  31.9 0.5 %collective-permute-done.7 = bf16[128,512]{1,0:T(8,128)(2,1)S(1)} collective-permute-done((bf16[128,512]{1,0:T(8,128)(2,1)S(1)}, bf16[128,512]{1,0:T(8,128)(2,1)S(1)}, u32[]{:S(2)}, u32[]{:S(2)}) %collective-permute-start.7) | collective-permute-done | bytes 131104 | tf_op jit(solution)/shard_map/ppermute | solution.py:28
  32.5 2.0 %all_gather.11 = bf16[256,512]{1,0:T(8,128)(2,1)S(1)} all-gather(bf16[128,512]{1,0:T(8,128)(2,1)S(1)} %fusion.19), channel_id=1, replica_groups=mesh['blk'=16,'rep'=2] {'rep'}, dimensions={0}, use_global_device_ids=true | all-gather | bytes 393216 | tf_op jit(solution)/shard_map/all_gather | solution.py:112
  34.9 1.2 %collective-permute-start.9 = (bf16[256,512]{1,0:T(8,128)(2,1)S(1)}, bf16[256,512]{1,0:T(8,128)(2,1)S(1)}, u32[]{:S(2)}, u32[]{:S(2)}) collective-permute-start(bf16[256,512]{1,0:T(8,128)(2,1)S(1)} %pad_maximum_fusion.2), channel_id=1, source_target_pairs={{0,2},{2,0},{4,6},{6,4},{8,10},{10,8},{12,14},{14,12},{16,18},{18,... | collective-permute-start | bytes 786440 | tf_op jit(solution)/shard_map/ppermute | solution.py:28
  36.5 1.2 %collective-permute-start.14 = (bf16[128,512]{1,0:T(8,128)(2,1)S(1)}, bf16[128,512]{1,0:T(8,128)(2,1)S(1)}, u32[]{:S(2)}, u32[]{:S(2)}) collective-permute-start(bf16[128,512]{1,0:T(8,128)(2,1)S(1)} %pad_maximum_fusion.6), channel_id=1, source_target_pairs={{0,8},{2,10},{4,12},{6,14},{8,0},{10,2},{12,4},{14,6},{16,24},{18,... | collective-permute-start | bytes 393224 | tf_op jit(solution)/shard_map/ppermute | solution.py:32
  37.7 3.9 %collective-permute-done.17 = bf16[512,128]{1,0:T(8,128)(2,1)S(1)} collective-permute-done((bf16[512,128]{1,0:T(8,128)(2,1)S(1)}, bf16[512,128]{1,0:T(8,128)(2,1)S(1)}, u32[]{:S(2)}, u32[]{:S(2)}) %collective-permute-start.17) | collective-permute-done | bytes 131104 | tf_op jit(solution)/shard_map/ppermute | solution.py:32
  42.2 1.9 %collective-permute-done.14 = bf16[128,512]{1,0:T(8,128)(2,1)S(1)} collective-permute-done((bf16[128,512]{1,0:T(8,128)(2,1)S(1)}, bf16[128,512]{1,0:T(8,128)(2,1)S(1)}, u32[]{:S(2)}, u32[]{:S(2)}) %collective-permute-start.14) | collective-permute-done | bytes 131104 | tf_op jit(solution)/shard_map/ppermute | solution.py:32
  44.1 0.8 %collective-permute-start.15 = (bf16[64,512]{1,0:T(8,128)(2,1)S(1)}, bf16[64,512]{1,0:T(8,128)(2,1)S(1)}, u32[]{:S(2)}, u32[]{:S(2)}) collective-permute-start(bf16[64,512]{1,0:T(8,128)(2,1)S(1)} %fusion.22), channel_id=1, source_target_pairs={{0,16},{2,18},{4,20},{6,22},{8,24},{10,26},{12,28},{14,30},{16,0},... | collective-permute-start | bytes 196616 | tf_op jit(solution)/shard_map/ppermute | solution.py:32
  44.9 1.1 %select_convert_fusion = bf16[128,512]{1,0:T(8,128)(2,1)} fusion(bf16[128,512]{1,0:T(8,128)(2,1)S(1)} %collective-permute-done.19, bf16[128,1024]{1,0:T(8,128)(2,1)S(1)} %copy-done.1, s32[]{:T(128)S(6)} %select_n.214, bf16[512,128]{1,0:T(8,128)(2,1)S(1)} %fusion.16, bf16[2,512,1024]{2,1,0:T(8,128)(2,1)S(1)} %bitcast.110, s32[]{:T(128)S(6)} %select_n.279, ...), kind=kOutput, calls=%fused_computation.33 | convolution fusion | flops 67567616 | bytes 1048588 | tf_op jit(solution)/shard_map/dot_general | solution.py:52
  46.0 0.8 %collective-permute-start.10 = (bf16[128,512]{1,0:T(8,128)(2,1)S(1)}, bf16[128,512]{1,0:T(8,128)(2,1)S(1)}, u32[]{:S(2)}, u32[]{:S(2)}) collective-permute-start(bf16[128,512]{1,0:T(8,128)(2,1)S(1)} %fusion.13), channel_id=1, source_target_pairs={{0,4},{2,6},{4,0},{6,2},{8,12},{10,14},{12,8},{14,10},{16,20},{18,... | collective-permute-start | bytes 393224 | tf_op jit(solution)/shard_map/ppermute | solution.py:28
  46.8 3.4 %collective-permute-done.15 = bf16[64,512]{1,0:T(8,128)(2,1)S(1)} collective-permute-done((bf16[64,512]{1,0:T(8,128)(2,1)S(1)}, bf16[64,512]{1,0:T(8,128)(2,1)S(1)}, u32[]{:S(2)}, u32[]{:S(2)}) %collective-permute-start.15) | collective-permute-done | bytes 65568 | tf_op jit(solution)/shard_map/ppermute | solution.py:32
  50.2 0.7 %fusion.23 = f32[64,512]{1,0:T(8,128)} fusion(bf16[64,512]{1,0:T(8,128)(2,1)S(1)} %collective-permute-done.15, f32[4,64,512]{2,1,0:T(8,128)S(1)} %bitcast.118, s32[]{:T(128)S(6)} %select_n.271, bf16[128,512]{1,0:T(8,128)(2,1)S(1)} %collective-permute-done.14), kind=kLoop, calls=%fused_computation.45 | loop fusion | flops 131072 | bytes 393220 | tf_op jit(solution)/shard_map/add | solution.py:42
  51.1 0.7 %fusion.15 = bf16[128,512]{1,0:T(8,128)(2,1)} fusion(f32[512,512]{1,0:T(8,128)S(1)} %get-tuple-element.60, bf16[128,512]{1,0:T(8,128)(2,1)S(1)} %collective-permute-done.10, bf16[256,512]{1,0:T(8,128)(2,1)S(1)} %collective-permute-done.9), kind=kLoop, calls=%fused_computation.24 | loop fusion | flops 327680 | bytes 655360 | tf_op jit(solution)/shard_map/convert_element_type | solution.py:125
  (56 shorter events, 2.9 us)
Async XLA Ops:
  0.6 11.7 %copy-start = (bf16[1024,1024]{1,0:T(8,128)(2,1)S(1)}, bf16[1024,1024]{1,0:T(8,128)(2,1)}, u32[]{:S(2)}) copy-start(bf16[1024,1024]{1,0:T(8,128)(2,1)} %param.8) | copy-start | bytes 6291460
  0.6 11.7 %copy-start.2 = (bf16[128,1024]{1,0:T(8,128)(2,1)S(1)}, bf16[128,1024]{1,0:T(8,128)(2,1)}, u32[]{:S(2)}) copy-start(bf16[128,1024]{1,0:T(8,128)(2,1)} %param.9) | copy-start | bytes 786436
  1.7 19.1 %collective-permute-start.2 = (bf16[128,512]{1,0:T(8,128)(2,1)S(1)}, bf16[128,512]{1,0:T(8,128)(2,1)}, u32[]{:S(2)}, u32[]{:S(2)}) collective-permute-start(bf16[128,512]{1,0:T(8,128)(2,1)S(1)} %dynamic-slice_maximum_fusion), channel_id=1, source_target_pairs={{0,24},{2,26},{4,28},{6,30},{8,16},{10,18},{12,20},{14,22},{16,8},... | collective-permute-start | bytes 393224 | tf_op jit(solution)/shard_map/ppermute | solution.py:32
  6.9 14.6 %collective-permute-start.1 = (bf16[128,512]{1,0:T(8,128)(2,1)S(1)}, bf16[128,512]{1,0:T(8,128)(2,1)}, u32[]{:S(2)}, u32[]{:S(2)}) collective-permute-start(bf16[128,512]{1,0:T(8,128)(2,1)S(1)} %dynamic-slice_maximum_fusion), channel_id=1, source_target_pairs={{0,16},{2,18},{4,20},{6,22},{8,24},{10,26},{12,28},{14,30},{16,0},... | collective-permute-start | bytes 393224 | tf_op jit(solution)/shard_map/ppermute | solution.py:32
  8.7 5.3 %collective-permute-start.5 = (bf16[2,128,128]{2,1,0:T(8,128)(2,1)S(1)}, bf16[2,128,128]{2,1,0:T(8,128)(2,1)S(1)}, u32[]{:S(2)}, u32[]{:S(2)}) collective-permute-start(bf16[2,128,128]{2,1,0:T(8,128)(2,1)S(1)} %get-tuple-element.30), channel_id=1, source_target_pairs={{0,6},{2,4},{4,2},{6,0},{8,14},{10,12},{12,10},{14,8},{16,22},{18,... | collective-permute-start | bytes 196616 | tf_op jit(solution)/shard_map/ppermute | solution.py:28
  11.2 4.3 %collective-permute-start.4 = (bf16[2,128,128]{2,1,0:T(8,128)(2,1)S(1)}, bf16[2,128,128]{2,1,0:T(8,128)(2,1)S(1)}, u32[]{:S(2)}, u32[]{:S(2)}) collective-permute-start(bf16[2,128,128]{2,1,0:T(8,128)(2,1)S(1)} %get-tuple-element.31), channel_id=1, source_target_pairs={{0,4},{2,6},{4,0},{6,2},{8,12},{10,14},{12,8},{14,10},{16,20},{18,... | collective-permute-start | bytes 196616 | tf_op jit(solution)/shard_map/ppermute | solution.py:28
  11.8 5.6 %collective-permute-start.3 = (bf16[2,128,128]{2,1,0:T(8,128)(2,1)S(1)}, bf16[2,128,128]{2,1,0:T(8,128)(2,1)S(1)}, u32[]{:S(2)}, u32[]{:S(2)}) collective-permute-start(bf16[2,128,128]{2,1,0:T(8,128)(2,1)S(1)} %get-tuple-element.32), channel_id=1, source_target_pairs={{0,2},{2,0},{4,6},{6,4},{8,10},{10,8},{12,14},{14,12},{16,18},{18,... | collective-permute-start | bytes 196616 | tf_op jit(solution)/shard_map/ppermute | solution.py:28
  14.1 7.4 %collective-permute-start = (bf16[128,512]{1,0:T(8,128)(2,1)S(1)}, bf16[128,512]{1,0:T(8,128)(2,1)S(1)}, u32[]{:S(2)}, u32[]{:S(2)}) collective-permute-start(bf16[128,512]{1,0:T(8,128)(2,1)S(1)} %dynamic-slice_maximum_fusion), channel_id=1, source_target_pairs={{0,8},{2,10},{4,12},{6,14},{8,0},{10,2},{12,4},{14,6},{16,24},{18,... | collective-permute-start | bytes 393224 | tf_op jit(solution)/shard_map/ppermute | solution.py:32
  15.5 10.7 %collective-permute-start.13 = (bf16[128,512]{1,0:T(8,128)(2,1)S(1)}, bf16[128,512]{1,0:T(8,128)(2,1)S(1)}, u32[]{:S(2)}, u32[]{:S(2)}) collective-permute-start(bf16[128,512]{1,0:T(8,128)(2,1)S(1)} %constant_dynamic-slice_fusion), channel_id=1, source_target_pairs={{0,6},{2,4},{4,2},{6,0},{8,14},{10,12},{12,10},{14,8},{16,22},{18,... | collective-permute-start | bytes 393224 | tf_op jit(solution)/shard_map/ppermute | solution.py:28
  17.3 9.5 %collective-permute-start.12 = (bf16[128,512]{1,0:T(8,128)(2,1)S(1)}, bf16[128,512]{1,0:T(8,128)(2,1)S(1)}, u32[]{:S(2)}, u32[]{:S(2)}) collective-permute-start(bf16[128,512]{1,0:T(8,128)(2,1)S(1)} %constant_dynamic-slice_fusion), channel_id=1, source_target_pairs={{0,4},{2,6},{4,0},{6,2},{8,12},{10,14},{12,8},{14,10},{16,20},{18,... | collective-permute-start | bytes 393224 | tf_op jit(solution)/shard_map/ppermute | solution.py:28
  20.9 6.0 %collective-permute-start.11 = (bf16[128,512]{1,0:T(8,128)(2,1)S(1)}, bf16[128,512]{1,0:T(8,128)(2,1)S(1)}, u32[]{:S(2)}, u32[]{:S(2)}) collective-permute-start(bf16[128,512]{1,0:T(8,128)(2,1)S(1)} %constant_dynamic-slice_fusion), channel_id=1, source_target_pairs={{0,2},{2,0},{4,6},{6,4},{8,10},{10,8},{12,14},{14,12},{16,18},{18,... | collective-permute-start | bytes 393224 | tf_op jit(solution)/shard_map/ppermute | solution.py:28
  23.1 7.5 %collective-permute-start.8 = (bf16[128,512]{1,0:T(8,128)(2,1)S(1)}, bf16[128,512]{1,0:T(8,128)(2,1)S(1)}, u32[]{:S(2)}, u32[]{:S(2)}) collective-permute-start(bf16[128,512]{1,0:T(8,128)(2,1)S(1)} %pad_maximum_fusion.5), channel_id=1, source_target_pairs={{0,6},{2,4},{4,2},{6,0},{8,14},{10,12},{12,10},{14,8},{16,22},{18,... | collective-permute-start | bytes 393224 | tf_op jit(solution)/shard_map/ppermute | solution.py:28
  25.0 7.4 %collective-permute-start.7 = (bf16[128,512]{1,0:T(8,128)(2,1)S(1)}, bf16[128,512]{1,0:T(8,128)(2,1)S(1)}, u32[]{:S(2)}, u32[]{:S(2)}) collective-permute-start(bf16[128,512]{1,0:T(8,128)(2,1)S(1)} %pad_maximum_fusion.4), channel_id=1, source_target_pairs={{0,4},{2,6},{4,0},{6,2},{8,12},{10,14},{12,8},{14,10},{16,20},{18,... | collective-permute-start | bytes 393224 | tf_op jit(solution)/shard_map/ppermute | solution.py:28
  26.2 6.2 %collective-permute-start.6 = (bf16[128,512]{1,0:T(8,128)(2,1)S(1)}, bf16[128,512]{1,0:T(8,128)(2,1)S(1)}, u32[]{:S(2)}, u32[]{:S(2)}) collective-permute-start(bf16[128,512]{1,0:T(8,128)(2,1)S(1)} %pad_maximum_fusion.3), channel_id=1, source_target_pairs={{0,2},{2,0},{4,6},{6,4},{8,10},{10,8},{12,14},{14,12},{16,18},{18,... | collective-permute-start | bytes 393224 | tf_op jit(solution)/shard_map/ppermute | solution.py:28
  27.4 10.3 %collective-permute-start.18 = (bf16[512,128]{1,0:T(8,128)(2,1)S(1)}, bf16[512,128]{1,0:T(8,128)(2,1)S(1)}, u32[]{:S(2)}, u32[]{:S(2)}) collective-permute-start(bf16[512,128]{1,0:T(8,128)(2,1)S(1)} %get-tuple-element.4), channel_id=1, source_target_pairs={{0,24},{2,26},{4,28},{6,30},{8,16},{10,18},{12,20},{14,22},{16,8},... | collective-permute-start | bytes 393224 | tf_op jit(solution)/shard_map/ppermute | solution.py:32
  30.5 11.1 %collective-permute-start.17 = (bf16[512,128]{1,0:T(8,128)(2,1)S(1)}, bf16[512,128]{1,0:T(8,128)(2,1)S(1)}, u32[]{:S(2)}, u32[]{:S(2)}) collective-permute-start(bf16[512,128]{1,0:T(8,128)(2,1)S(1)} %get-tuple-element.5), channel_id=1, source_target_pairs={{0,16},{2,18},{4,20},{6,22},{8,24},{10,26},{12,28},{14,30},{16,0},... | collective-permute-start | bytes 393224 | tf_op jit(solution)/shard_map/ppermute | solution.py:32
  30.5 11.1 %collective-permute-start.16 = (bf16[512,128]{1,0:T(8,128)(2,1)S(1)}, bf16[512,128]{1,0:T(8,128)(2,1)S(1)}, u32[]{:S(2)}, u32[]{:S(2)}) collective-permute-start(bf16[512,128]{1,0:T(8,128)(2,1)S(1)} %get-tuple-element.3), channel_id=1, source_target_pairs={{0,8},{2,10},{4,12},{6,14},{8,0},{10,2},{12,4},{14,6},{16,24},{18,... | collective-permute-start | bytes 393224 | tf_op jit(solution)/shard_map/ppermute | solution.py:32
  34.9 11.2 %collective-permute-start.9 = (bf16[256,512]{1,0:T(8,128)(2,1)S(1)}, bf16[256,512]{1,0:T(8,128)(2,1)S(1)}, u32[]{:S(2)}, u32[]{:S(2)}) collective-permute-start(bf16[256,512]{1,0:T(8,128)(2,1)S(1)} %pad_maximum_fusion.2), channel_id=1, source_target_pairs={{0,2},{2,0},{4,6},{6,4},{8,10},{10,8},{12,14},{14,12},{16,18},{18,... | collective-permute-start | bytes 786440 | tf_op jit(solution)/shard_map/ppermute | solution.py:28
  36.1 8.8 %copy-start.1 = (bf16[128,1024]{1,0:T(8,128)(2,1)S(1)}, bf16[128,1024]{1,0:T(8,128)(2,1)}, u32[]{:S(2)}) copy-start(bf16[128,1024]{1,0:T(8,128)(2,1)} %param.5) | copy-start | bytes 786436
  36.5 7.6 %collective-permute-start.14 = (bf16[128,512]{1,0:T(8,128)(2,1)S(1)}, bf16[128,512]{1,0:T(8,128)(2,1)S(1)}, u32[]{:S(2)}, u32[]{:S(2)}) collective-permute-start(bf16[128,512]{1,0:T(8,128)(2,1)S(1)} %pad_maximum_fusion.6), channel_id=1, source_target_pairs={{0,8},{2,10},{4,12},{6,14},{8,0},{10,2},{12,4},{14,6},{16,24},{18,... | collective-permute-start | bytes 393224 | tf_op jit(solution)/shard_map/ppermute | solution.py:32
  42.1 2.8 %collective-permute-start.19 = (bf16[128,512]{1,0:T(8,128)(2,1)S(1)}, bf16[128,512]{1,0:T(8,128)(2,1)S(1)}, u32[]{:S(2)}, u32[]{:S(2)}) collective-permute-start(bf16[128,512]{1,0:T(8,128)(2,1)S(1)} %convolution_convert_fusion.1), channel_id=1, source_target_pairs={{0,1},{1,0},{2,3},{3,2},{4,5},{5,4},{6,7},{7,6},{8,9},{9,8},{10,11... | collective-permute-start | bytes 393224 | tf_op jit(solution)/shard_map/ppermute | solution.py:49
  44.1 6.1 %collective-permute-start.15 = (bf16[64,512]{1,0:T(8,128)(2,1)S(1)}, bf16[64,512]{1,0:T(8,128)(2,1)S(1)}, u32[]{:S(2)}, u32[]{:S(2)}) collective-permute-start(bf16[64,512]{1,0:T(8,128)(2,1)S(1)} %fusion.22), channel_id=1, source_target_pairs={{0,16},{2,18},{4,20},{6,22},{8,24},{10,26},{12,28},{14,30},{16,0},... | collective-permute-start | bytes 196616 | tf_op jit(solution)/shard_map/ppermute | solution.py:32
  46.0 5.1 %collective-permute-start.10 = (bf16[128,512]{1,0:T(8,128)(2,1)S(1)}, bf16[128,512]{1,0:T(8,128)(2,1)S(1)}, u32[]{:S(2)}, u32[]{:S(2)}) collective-permute-start(bf16[128,512]{1,0:T(8,128)(2,1)S(1)} %fusion.13), channel_id=1, source_target_pairs={{0,4},{2,6},{4,0},{6,2},{8,12},{10,14},{12,8},{14,10},{16,20},{18,... | collective-permute-start | bytes 393224 | tf_op jit(solution)/shard_map/ppermute | solution.py:28

commit v21 on v20

--- a/solution.py
+++ b/solution.py
@@ -37,13 +37,13 @@
         for bit in rising:
             keys = [k for k in parts if not k & bit]
             sent = jnp.concatenate([parts[k ^ bit].astype(bf16) for k in keys], 0)
-            got = move(sent, bit)
+            last = got = move(sent, bit)
             parts = {
                 k: parts[k].astype(jnp.float32)
                 + got[n * size : (n + 1) * size].astype(jnp.float32)
                 for n, k in enumerate(keys)
             }
-        return parts[0]
+        return parts[0], last
 
     def to_other(value):
         return lax.ppermute(value, "rep", [(0, 1), (1, 0)])
@@ -116,13 +116,14 @@
     out_part = dot(mixed_cols, w_share, ((0,), (0,)))
     weight_part = after(dot(mixed_cols, grad_stack, ((1,), (0,))), out_part)
     by_outer = weight_part.reshape(side, rows_here, cols_here)
-    grad_weight = halved(
+    grad_weight, weight_last = halved(
         [lax.dynamic_index_in_dim(by_outer, outer_pos ^ t, 0, keepdims=False) for t in turns],
         along_outer,
     )
-    out_part = halved(
+    out_part, _ = halved(
         [out_part[t * tile_size : (t + 1) * tile_size] for t in turns], along_inner
-    ).astype(bf16)
+    )
+    out_part = out_part.astype(bf16)
 
     back = after(back, weight_part).astype(bf16)
     w_rows = w_out.reshape(rep_count, cols_here, feature_width)
@@ -137,8 +138,7 @@
         back_full = lax.all_gather(back, "rep", axis=0, tiled=True)
         w_mine = lax.dynamic_index_in_dim(w_rows, rep_pos, 0, keepdims=False)
         grad_in = dot(back_full, w_mine, ((0,), (1,)))
-    pre_part = columns_of(hidden_pre, rep_pos)
-    grad_pre = jnp.where(pre_part > 0, grad_in, 0.0).astype(bf16)
+    grad_pre = jnp.where(hidden_part > 0, after(grad_in, weight_last), 0.0).astype(bf16)
     return (out_part, grad_weight, grad_pre)
 
 

time: 52.1 us -> 57.2 us (1.098)
  waiting for transfers between devices: 12.4 us -> 17.8 us
    ppermute x11, waiting for transfers between devices: 3.25 us -> 6.77 us  [along_inner(): return lax.ppermute(value, 'blk', pairs) if turn else value]
    ppermute x8, waiting for transfers between devices: 9.14 us -> 11 us  [along_outer(): return lax.ppermute(value, 'blk', pairs) if turn else value]
    mul x1 -> x2, other arithmetic: 0.02 us -> 0.7 us  [after(): part = other[:height, :width].astype(value.dtype) * 0]
    add x1 -> x0, other arithmetic: 0.68 us -> none  [halved(): parts[k].astype(jnp.float32)]
  transfers between devices with their start and end apart: 20 -> 20, of which waited for: 7 -> 7; matrix products, arithmetic and copies ran while one was open for 14% -> 13% of each run, Pallas kernels for 0% -> 0%
where the time goes in v21:
time: 57.2 us; the launch traced here: 57 us
  starting transfers between devices  24.9 us (44%)
  waiting for transfers between devices  17.8 us (31%)
  blocking collectives  4.18 us (7%)
  matrix products  4.05 us (7%)
  other arithmetic  3.86 us (7%)
  local copies, waits for them, and re-layouts  1.22 us (2%)
  between operations  0.95 us (2%)
    ppermute x11, starting transfers between devices, along_inner(): return lax.ppermute(value, 'blk', pairs) if turn else value  12.5 us
    ppermute x8, starting transfers between devices, along_outer(): return lax.ppermute(value, 'blk', pairs) if turn else value  12.3 us
    ppermute x8, waiting for transfers between devices, along_outer(): return lax.ppermute(value, 'blk', pairs) if turn else value  11 us
    ppermute x11, waiting for transfers between devices, along_inner(): return lax.ppermute(value, 'blk', pairs) if turn else value  6.77 us
    dot_general x6, matrix products, dot(): lax.dot_general(lhs, rhs, (dims, ((), ())), preferred_element_type=jnp.fl...  4.05 us
    all_gather x1, blocking collectives, shards(): everyone = lax.all_gather(jnp.concatenate(arrived, 0), 'rep', axis=0)  2.18 us
    all_gather x1, blocking collectives, shards(): lax.all_gather(mixed_cols.astype(bf16), 'rep', axis=0, tiled=True)  1.99 us
  transfers between devices with their start and end apart: 20, of which 7 were waited for; matrix products, arithmetic and copies ran while one was open for 13% of the time, Pallas kernels for 0%

profile of v21, /device:TPU:0, one launch (start us, length us, event | category | flops | bytes accessed | tf_op | source)
XLA Modules:
  0.0 57.0 jit_solution(7832740320549631253)
XLA Ops:
  0.7 1.1 %dynamic-slice_maximum_fusion = bf16[128,512]{1,0:T(8,128)(2,1)S(1)} fusion(bf16[128,1024]{1,0:T(8,128)(2,1)} %param.5, s32[]{:T(128)S(6)} %select_n.213), kind=kLoop, calls=%fused_computation.51 | loop fusion | flops 262144 | bytes 262148 | tf_op jit(solution)/shard_map/max | solution.py:66
  1.7 5.1 %collective-permute-start.2 = (bf16[128,512]{1,0:T(8,128)(2,1)S(1)}, bf16[128,512]{1,0:T(8,128)(2,1)}, u32[]{:S(2)}, u32[]{:S(2)}) collective-permute-start(bf16[128,512]{1,0:T(8,128)(2,1)S(1)} %dynamic-slice_maximum_fusion), channel_id=1, source_target_pairs={{0,24},{2,26},{4,28},{6,30},{8,16},{10,18},{12,20},{14,22},{16,8},... | collective-permute-start | bytes 393224 | tf_op jit(solution)/shard_map/ppermute | solution.py:32
  6.9 0.7 %add_bitcast_fusion = s32[8]{0:T(128)S(1)} fusion(s32[1,8]{1,0:T(1,128)} %param.7, s32[]{:T(128)S(6)} %shift_right_arithmetic.54, s32[]{:T(128)S(6)} %and.60), kind=kLoop, calls=%fused_computation.97 | loop fusion | flops 56 | bytes 72 | tf_op jit(solution)/shard_map/eq | solution.py:72
  7.6 0.9 %slice_bitcast_fusion.9 = (bf16[128,128]{1,0:T(8,128)(2,1)S(1)}, bf16[128,128]{1,0:T(8,128)(2,1)S(1)}, bf16[128,128]{1,0:T(8,128)(2,1)S(1)}, bf16[128,128]{1,0:T...) fusion(bf16[1,8,128,128]{3,2,1,0:T(8,128)(2,1)} %param.6), kind=kLoop, calls=%fused_computation.78 | loop fusion | bytes 524288 | tf_op jit(solution)/shard_map/jit(_where)/broadcast_in_dim | solution.py:75
  8.7 2.5 %collective-permute-start.5 = (bf16[2,128,128]{2,1,0:T(8,128)(2,1)S(1)}, bf16[2,128,128]{2,1,0:T(8,128)(2,1)S(1)}, u32[]{:S(2)}, u32[]{:S(2)}) collective-permute-start(bf16[2,128,128]{2,1,0:T(8,128)(2,1)S(1)} %get-tuple-element.30), channel_id=1, source_target_pairs={{0,6},{2,4},{4,2},{6,0},{8,14},{10,12},{12,10},{14,8},{16,22},{18,... | collective-permute-start | bytes 196616 | tf_op jit(solution)/shard_map/ppermute | solution.py:28
  11.2 0.5 collective-permute-start.4
  11.8 0.5 collective-permute-start.3
  12.4 1.7 %collective-permute-done.5 = bf16[2,128,128]{2,1,0:T(8,128)(2,1)S(1)} collective-permute-done((bf16[2,128,128]{2,1,0:T(8,128)(2,1)S(1)}, bf16[2,128,128]{2,1,0:T(8,128)(2,1)S(1)}, u32[]{:S(2)}, u32[]{:S(2)}) %collective-permute-start.5) | collective-permute-done | bytes 65568 | tf_op jit(solution)/shard_map/ppermute | solution.py:28
  14.1 0.6 %collective-permute-start = (bf16[128,512]{1,0:T(8,128)(2,1)S(1)}, bf16[128,512]{1,0:T(8,128)(2,1)S(1)}, u32[]{:S(2)}, u32[]{:S(2)}) collective-permute-start(bf16[128,512]{1,0:T(8,128)(2,1)S(1)} %dynamic-slice_maximum_fusion), channel_id=1, source_target_pairs={{0,8},{2,10},{4,12},{6,14},{8,0},{10,2},{12,4},{14,6},{16,24},{18,... | collective-permute-start | bytes 393224 | tf_op jit(solution)/shard_map/ppermute | solution.py:32
  14.7 0.8 %collective-permute-done.4 = bf16[2,128,128]{2,1,0:T(8,128)(2,1)S(1)} collective-permute-done((bf16[2,128,128]{2,1,0:T(8,128)(2,1)S(1)}, bf16[2,128,128]{2,1,0:T(8,128)(2,1)S(1)}, u32[]{:S(2)}, u32[]{:S(2)}) %collective-permute-start.4) | collective-permute-done | bytes 65568 | tf_op jit(solution)/shard_map/ppermute | solution.py:28
  15.5 1.8 %collective-permute-start.13 = (bf16[128,512]{1,0:T(8,128)(2,1)S(1)}, bf16[128,512]{1,0:T(8,128)(2,1)S(1)}, u32[]{:S(2)}, u32[]{:S(2)}) collective-permute-start(bf16[128,512]{1,0:T(8,128)(2,1)S(1)} %constant_dynamic-slice_fusion), channel_id=1, source_target_pairs={{0,6},{2,4},{4,2},{6,0},{8,14},{10,12},{12,10},{14,8},{16,22},{18,... | collective-permute-start | bytes 393224 | tf_op jit(solution)/shard_map/ppermute | solution.py:28
  17.3 1.1 %collective-permute-start.12 = (bf16[128,512]{1,0:T(8,128)(2,1)S(1)}, bf16[128,512]{1,0:T(8,128)(2,1)S(1)}, u32[]{:S(2)}, u32[]{:S(2)}) collective-permute-start(bf16[128,512]{1,0:T(8,128)(2,1)S(1)} %constant_dynamic-slice_fusion), channel_id=1, source_target_pairs={{0,4},{2,6},{4,0},{6,2},{8,12},{10,14},{12,8},{14,10},{16,20},{18,... | collective-permute-start | bytes 393224 | tf_op jit(solution)/shard_map/ppermute | solution.py:28
  18.5 2.2 %all-gather = bf16[16,128,128]{2,1,0:T(8,128)(2,1)S(1)} all-gather(bf16[8,128,128]{2,1,0:T(8,128)(2,1)S(1)} %pad_maximum_fusion.1), channel_id=2, replica_groups=mesh['blk'=16,'rep'=2] {'rep'}, dimensions={0}, use_global_device_ids=true | all-gather | bytes 786432 | tf_op jit(solution)/shard_map/all_gather | solution.py:79
  20.9 0.6 %collective-permute-start.11 = (bf16[128,512]{1,0:T(8,128)(2,1)S(1)}, bf16[128,512]{1,0:T(8,128)(2,1)S(1)}, u32[]{:S(2)}, u32[]{:S(2)}) collective-permute-start(bf16[128,512]{1,0:T(8,128)(2,1)S(1)} %constant_dynamic-slice_fusion), channel_id=1, source_target_pairs={{0,2},{2,0},{4,6},{6,4},{8,10},{10,8},{12,14},{14,12},{16,18},{18,... | collective-permute-start | bytes 393224 | tf_op jit(solution)/shard_map/ppermute | solution.py:28
  21.5 1.5 %convolution_convert_fusion = bf16[512,512]{1,0:T(8,128)(2,1)S(1)} fusion(bf16[512,512]{1,0:T(8,128)(2,1)S(1)} %maximum_maximum_fusion, bf16[128,512]{1,0:T(8,128)(2,1)} %collective-permute-done.2, bf16[128,512]{1,0:T(8,128)(2,1)} %collective-permute-done.1, bf16[128,512]{1,0:T(8,128)(2,1)S(1)} %collective-permute-done, ...), kind=kOutput, calls=%fused_computation.1 | convolution fusion | flops 270794752 | bytes 1572864 | tf_op jit(solution)/shard_map/dot_general | solution.py:52
  23.1 1.9 %collective-permute-start.8 = (bf16[128,512]{1,0:T(8,128)(2,1)S(1)}, bf16[128,512]{1,0:T(8,128)(2,1)S(1)}, u32[]{:S(2)}, u32[]{:S(2)}) collective-permute-start(bf16[128,512]{1,0:T(8,128)(2,1)S(1)} %pad_maximum_fusion.5), channel_id=1, source_target_pairs={{0,6},{2,4},{4,2},{6,0},{8,14},{10,12},{12,10},{14,8},{16,22},{18,... | collective-permute-start | bytes 393224 | tf_op jit(solution)/shard_map/ppermute | solution.py:28
  25.0 1.2 %collective-permute-start.7 = (bf16[128,512]{1,0:T(8,128)(2,1)S(1)}, bf16[128,512]{1,0:T(8,128)(2,1)S(1)}, u32[]{:S(2)}, u32[]{:S(2)}) collective-permute-start(bf16[128,512]{1,0:T(8,128)(2,1)S(1)} %pad_maximum_fusion.4), channel_id=1, source_target_pairs={{0,4},{2,6},{4,0},{6,2},{8,12},{10,14},{12,8},{14,10},{16,20},{18,... | collective-permute-start | bytes 393224 | tf_op jit(solution)/shard_map/ppermute | solution.py:28
  26.2 0.6 %collective-permute-start.6 = (bf16[128,512]{1,0:T(8,128)(2,1)S(1)}, bf16[128,512]{1,0:T(8,128)(2,1)S(1)}, u32[]{:S(2)}, u32[]{:S(2)}) collective-permute-start(bf16[128,512]{1,0:T(8,128)(2,1)S(1)} %pad_maximum_fusion.3), channel_id=1, source_target_pairs={{0,2},{2,0},{4,6},{6,4},{8,10},{10,8},{12,14},{14,12},{16,18},{18,... | collective-permute-start | bytes 393224 | tf_op jit(solution)/shard_map/ppermute | solution.py:28
  27.4 3.1 %collective-permute-start.18 = (bf16[512,128]{1,0:T(8,128)(2,1)S(1)}, bf16[512,128]{1,0:T(8,128)(2,1)S(1)}, u32[]{:S(2)}, u32[]{:S(2)}) collective-permute-start(bf16[512,128]{1,0:T(8,128)(2,1)S(1)} %get-tuple-element.4), channel_id=1, source_target_pairs={{0,24},{2,26},{4,28},{6,30},{8,16},{10,18},{12,20},{14,22},{16,8},... | collective-permute-start | bytes 393224 | tf_op jit(solution)/shard_map/ppermute | solution.py:32
  30.5 1.3 %collective-permute-start.16 = (bf16[512,128]{1,0:T(8,128)(2,1)S(1)}, bf16[512,128]{1,0:T(8,128)(2,1)S(1)}, u32[]{:S(2)}, u32[]{:S(2)}) collective-permute-start(bf16[512,128]{1,0:T(8,128)(2,1)S(1)} %get-tuple-element.3), channel_id=1, source_target_pairs={{0,8},{2,10},{4,12},{6,14},{8,0},{10,2},{12,4},{14,6},{16,24},{18,... | collective-permute-start | bytes 393224 | tf_op jit(solution)/shard_map/ppermute | solution.py:32
  31.9 0.5 collective-permute-done.7
  32.5 2.0 %all_gather.11 = bf16[256,512]{1,0:T(8,128)(2,1)S(1)} all-gather(bf16[128,512]{1,0:T(8,128)(2,1)S(1)} %fusion.21), channel_id=1, replica_groups=mesh['blk'=16,'rep'=2] {'rep'}, dimensions={0}, use_global_device_ids=true | all-gather | bytes 393216 | tf_op jit(solution)/shard_map/all_gather | solution.py:112
  34.9 1.2 %collective-permute-start.9 = (bf16[256,512]{1,0:T(8,128)(2,1)S(1)}, bf16[256,512]{1,0:T(8,128)(2,1)S(1)}, u32[]{:S(2)}, u32[]{:S(2)}) collective-permute-start(bf16[256,512]{1,0:T(8,128)(2,1)S(1)} %pad_maximum_fusion.2), channel_id=1, source_target_pairs={{0,2},{2,0},{4,6},{6,4},{8,10},{10,8},{12,14},{14,12},{16,18},{18,... | collective-permute-start | bytes 786440 | tf_op jit(solution)/shard_map/ppermute | solution.py:28
  36.5 1.2 %collective-permute-start.14 = (bf16[128,512]{1,0:T(8,128)(2,1)S(1)}, bf16[128,512]{1,0:T(8,128)(2,1)S(1)}, u32[]{:S(2)}, u32[]{:S(2)}) collective-permute-start(bf16[128,512]{1,0:T(8,128)(2,1)S(1)} %pad_maximum_fusion.6), channel_id=1, source_target_pairs={{0,8},{2,10},{4,12},{6,14},{8,0},{10,2},{12,4},{14,6},{16,24},{18,... | collective-permute-start | bytes 393224 | tf_op jit(solution)/shard_map/ppermute | solution.py:32
  37.7 3.8 %collective-permute-done.17 = bf16[512,128]{1,0:T(8,128)(2,1)S(1)} collective-permute-done((bf16[512,128]{1,0:T(8,128)(2,1)S(1)}, bf16[512,128]{1,0:T(8,128)(2,1)S(1)}, u32[]{:S(2)}, u32[]{:S(2)}) %collective-permute-start.17) | collective-permute-done | bytes 131104 | tf_op jit(solution)/shard_map/ppermute | solution.py:32
  41.7 2.4 %collective-permute-done.14 = bf16[128,512]{1,0:T(8,128)(2,1)S(1)} collective-permute-done((bf16[128,512]{1,0:T(8,128)(2,1)S(1)}, bf16[128,512]{1,0:T(8,128)(2,1)S(1)}, u32[]{:S(2)}, u32[]{:S(2)}) %collective-permute-start.14) | collective-permute-done | bytes 131104 | tf_op jit(solution)/shard_map/ppermute | solution.py:32
  44.1 0.8 %collective-permute-start.15 = (bf16[64,512]{1,0:T(8,128)(2,1)S(1)}, bf16[64,512]{1,0:T(8,128)(2,1)S(1)}, u32[]{:S(2)}, u32[]{:S(2)}) collective-permute-start(bf16[64,512]{1,0:T(8,128)(2,1)S(1)} %fusion.24), channel_id=1, source_target_pairs={{0,16},{2,18},{4,20},{6,22},{8,24},{10,26},{12,28},{14,30},{16,0},... | collective-permute-start | bytes 196616 | tf_op jit(solution)/shard_map/ppermute | solution.py:32
  45.4 4.8 %collective-permute-done.15 = bf16[64,512]{1,0:T(8,128)(2,1)S(1)} collective-permute-done((bf16[64,512]{1,0:T(8,128)(2,1)S(1)}, bf16[64,512]{1,0:T(8,128)(2,1)S(1)}, u32[]{:S(2)}, u32[]{:S(2)}) %collective-permute-start.15) | collective-permute-done | bytes 65568 | tf_op jit(solution)/shard_map/ppermute | solution.py:32
  50.2 0.7 %convert_multiply_fusion = (f32[64,512]{1,0:T(8,128)S(1)}, f32[64,512]{1,0:T(8,128)}) fusion(bf16[64,512]{1,0:T(8,128)(2,1)S(1)} %collective-permute-done.15, bf16[128,512]{1,0:T(8,128)(2,1)S(1)} %collective-permute-done.14, f32[4,64,512]{2,1,0:T(8,128)S(1)} %bitcast.118, s32[]{:T(128)S(6)} %select_n.270), kind=kLoop, calls=%fused_computation.39 | loop fusion | flops 163840 | bytes 524292 | tf_op jit(solution)/shard_map/mul | solution.py:59
  51.4 1.1 %fusion.18 = bf16[128,512]{1,0:T(8,128)(2,1)} fusion(f32[64,512]{1,0:T(8,128)S(1)} %get-tuple-element.51, bf16[128,512]{1,0:T(8,128)(2,1)S(1)} %collective-permute-done.19, bf16[128,1024]{1,0:T(8,128)(2,1)S(1)} %copy-done.1, s32[]{:T(128)S(6)} %select_n.213, bf16[512,128]{1,0:T(8,128)(2,1)S(1)} %fusion.16, bf16[2,512,1024]{2,1,0:T(8,128)(2,1)S(1)} %bitcast.110, ...), kind=kOutput, calls=%fused_computation.31 | convolution fusion | flops 67698688 | bytes 1179660 | tf_op jit(solution)/shard_map/dot_general | solution.py:52
  52.5 3.7 %collective-permute-done.10 = bf16[128,512]{1,0:T(8,128)(2,1)S(1)} collective-permute-done((bf16[128,512]{1,0:T(8,128)(2,1)S(1)}, bf16[128,512]{1,0:T(8,128)(2,1)S(1)}, u32[]{:S(2)}, u32[]{:S(2)}) %collective-permute-start.10) | collective-permute-done | bytes 131104 | tf_op jit(solution)/shard_map/ppermute | solution.py:28
  56.3 0.7 %fusion.15 = bf16[128,512]{1,0:T(8,128)(2,1)} fusion(f32[512,512]{1,0:T(8,128)S(1)} %get-tuple-element.62, bf16[128,512]{1,0:T(8,128)(2,1)S(1)} %collective-permute-done.10, bf16[256,512]{1,0:T(8,128)(2,1)S(1)} %collective-permute-done.9), kind=kLoop, calls=%fused_computation.24 | loop fusion | flops 327680 | bytes 655360 | tf_op jit(solution)/shard_map/convert_element_type | solution.py:126
  (56 shorter events, 3.2 us)
Async XLA Ops:
  0.6 11.7 %copy-start = (bf16[1024,1024]{1,0:T(8,128)(2,1)S(1)}, bf16[1024,1024]{1,0:T(8,128)(2,1)}, u32[]{:S(2)}) copy-start(bf16[1024,1024]{1,0:T(8,128)(2,1)} %param.8) | copy-start | bytes 6291460
  0.6 11.7 %copy-start.2 = (bf16[128,1024]{1,0:T(8,128)(2,1)S(1)}, bf16[128,1024]{1,0:T(8,128)(2,1)}, u32[]{:S(2)}) copy-start(bf16[128,1024]{1,0:T(8,128)(2,1)} %param.9) | copy-start | bytes 786436
  1.7 19.1 %collective-permute-start.2 = (bf16[128,512]{1,0:T(8,128)(2,1)S(1)}, bf16[128,512]{1,0:T(8,128)(2,1)}, u32[]{:S(2)}, u32[]{:S(2)}) collective-permute-start(bf16[128,512]{1,0:T(8,128)(2,1)S(1)} %dynamic-slice_maximum_fusion), channel_id=1, source_target_pairs={{0,24},{2,26},{4,28},{6,30},{8,16},{10,18},{12,20},{14,22},{16,8},... | collective-permute-start | bytes 393224 | tf_op jit(solution)/shard_map/ppermute | solution.py:32
  6.9 14.6 %collective-permute-start.1 = (bf16[128,512]{1,0:T(8,128)(2,1)S(1)}, bf16[128,512]{1,0:T(8,128)(2,1)}, u32[]{:S(2)}, u32[]{:S(2)}) collective-permute-start(bf16[128,512]{1,0:T(8,128)(2,1)S(1)} %dynamic-slice_maximum_fusion), channel_id=1, source_target_pairs={{0,16},{2,18},{4,20},{6,22},{8,24},{10,26},{12,28},{14,30},{16,0},... | collective-permute-start | bytes 393224 | tf_op jit(solution)/shard_map/ppermute | solution.py:32
  8.7 5.3 %collective-permute-start.5 = (bf16[2,128,128]{2,1,0:T(8,128)(2,1)S(1)}, bf16[2,128,128]{2,1,0:T(8,128)(2,1)S(1)}, u32[]{:S(2)}, u32[]{:S(2)}) collective-permute-start(bf16[2,128,128]{2,1,0:T(8,128)(2,1)S(1)} %get-tuple-element.30), channel_id=1, source_target_pairs={{0,6},{2,4},{4,2},{6,0},{8,14},{10,12},{12,10},{14,8},{16,22},{18,... | collective-permute-start | bytes 196616 | tf_op jit(solution)/shard_map/ppermute | solution.py:28
  11.2 4.3 %collective-permute-start.4 = (bf16[2,128,128]{2,1,0:T(8,128)(2,1)S(1)}, bf16[2,128,128]{2,1,0:T(8,128)(2,1)S(1)}, u32[]{:S(2)}, u32[]{:S(2)}) collective-permute-start(bf16[2,128,128]{2,1,0:T(8,128)(2,1)S(1)} %get-tuple-element.31), channel_id=1, source_target_pairs={{0,4},{2,6},{4,0},{6,2},{8,12},{10,14},{12,8},{14,10},{16,20},{18,... | collective-permute-start | bytes 196616 | tf_op jit(solution)/shard_map/ppermute | solution.py:28
  11.8 5.6 %collective-permute-start.3 = (bf16[2,128,128]{2,1,0:T(8,128)(2,1)S(1)}, bf16[2,128,128]{2,1,0:T(8,128)(2,1)S(1)}, u32[]{:S(2)}, u32[]{:S(2)}) collective-permute-start(bf16[2,128,128]{2,1,0:T(8,128)(2,1)S(1)} %get-tuple-element.32), channel_id=1, source_target_pairs={{0,2},{2,0},{4,6},{6,4},{8,10},{10,8},{12,14},{14,12},{16,18},{18,... | collective-permute-start | bytes 196616 | tf_op jit(solution)/shard_map/ppermute | solution.py:28
  14.1 7.4 %collective-permute-start = (bf16[128,512]{1,0:T(8,128)(2,1)S(1)}, bf16[128,512]{1,0:T(8,128)(2,1)S(1)}, u32[]{:S(2)}, u32[]{:S(2)}) collective-permute-start(bf16[128,512]{1,0:T(8,128)(2,1)S(1)} %dynamic-slice_maximum_fusion), channel_id=1, source_target_pairs={{0,8},{2,10},{4,12},{6,14},{8,0},{10,2},{12,4},{14,6},{16,24},{18,... | collective-permute-start | bytes 393224 | tf_op jit(solution)/shard_map/ppermute | solution.py:32
  15.5 10.7 %collective-permute-start.13 = (bf16[128,512]{1,0:T(8,128)(2,1)S(1)}, bf16[128,512]{1,0:T(8,128)(2,1)S(1)}, u32[]{:S(2)}, u32[]{:S(2)}) collective-permute-start(bf16[128,512]{1,0:T(8,128)(2,1)S(1)} %constant_dynamic-slice_fusion), channel_id=1, source_target_pairs={{0,6},{2,4},{4,2},{6,0},{8,14},{10,12},{12,10},{14,8},{16,22},{18,... | collective-permute-start | bytes 393224 | tf_op jit(solution)/shard_map/ppermute | solution.py:28
  17.3 9.5 %collective-permute-start.12 = (bf16[128,512]{1,0:T(8,128)(2,1)S(1)}, bf16[128,512]{1,0:T(8,128)(2,1)S(1)}, u32[]{:S(2)}, u32[]{:S(2)}) collective-permute-start(bf16[128,512]{1,0:T(8,128)(2,1)S(1)} %constant_dynamic-slice_fusion), channel_id=1, source_target_pairs={{0,4},{2,6},{4,0},{6,2},{8,12},{10,14},{12,8},{14,10},{16,20},{18,... | collective-permute-start | bytes 393224 | tf_op jit(solution)/shard_map/ppermute | solution.py:28
  20.9 6.0 %collective-permute-start.11 = (bf16[128,512]{1,0:T(8,128)(2,1)S(1)}, bf16[128,512]{1,0:T(8,128)(2,1)S(1)}, u32[]{:S(2)}, u32[]{:S(2)}) collective-permute-start(bf16[128,512]{1,0:T(8,128)(2,1)S(1)} %constant_dynamic-slice_fusion), channel_id=1, source_target_pairs={{0,2},{2,0},{4,6},{6,4},{8,10},{10,8},{12,14},{14,12},{16,18},{18,... | collective-permute-start | bytes 393224 | tf_op jit(solution)/shard_map/ppermute | solution.py:28
  23.1 7.5 %collective-permute-start.8 = (bf16[128,512]{1,0:T(8,128)(2,1)S(1)}, bf16[128,512]{1,0:T(8,128)(2,1)S(1)}, u32[]{:S(2)}, u32[]{:S(2)}) collective-permute-start(bf16[128,512]{1,0:T(8,128)(2,1)S(1)} %pad_maximum_fusion.5), channel_id=1, source_target_pairs={{0,6},{2,4},{4,2},{6,0},{8,14},{10,12},{12,10},{14,8},{16,22},{18,... | collective-permute-start | bytes 393224 | tf_op jit(solution)/shard_map/ppermute | solution.py:28
  25.0 7.4 %collective-permute-start.7 = (bf16[128,512]{1,0:T(8,128)(2,1)S(1)}, bf16[128,512]{1,0:T(8,128)(2,1)S(1)}, u32[]{:S(2)}, u32[]{:S(2)}) collective-permute-start(bf16[128,512]{1,0:T(8,128)(2,1)S(1)} %pad_maximum_fusion.4), channel_id=1, source_target_pairs={{0,4},{2,6},{4,0},{6,2},{8,12},{10,14},{12,8},{14,10},{16,20},{18,... | collective-permute-start | bytes 393224 | tf_op jit(solution)/shard_map/ppermute | solution.py:28
  26.2 6.2 %collective-permute-start.6 = (bf16[128,512]{1,0:T(8,128)(2,1)S(1)}, bf16[128,512]{1,0:T(8,128)(2,1)S(1)}, u32[]{:S(2)}, u32[]{:S(2)}) collective-permute-start(bf16[128,512]{1,0:T(8,128)(2,1)S(1)} %pad_maximum_fusion.3), channel_id=1, source_target_pairs={{0,2},{2,0},{4,6},{6,4},{8,10},{10,8},{12,14},{14,12},{16,18},{18,... | collective-permute-start | bytes 393224 | tf_op jit(solution)/shard_map/ppermute | solution.py:28
  27.4 10.3 %collective-permute-start.18 = (bf16[512,128]{1,0:T(8,128)(2,1)S(1)}, bf16[512,128]{1,0:T(8,128)(2,1)S(1)}, u32[]{:S(2)}, u32[]{:S(2)}) collective-permute-start(bf16[512,128]{1,0:T(8,128)(2,1)S(1)} %get-tuple-element.4), channel_id=1, source_target_pairs={{0,24},{2,26},{4,28},{6,30},{8,16},{10,18},{12,20},{14,22},{16,8},... | collective-permute-start | bytes 393224 | tf_op jit(solution)/shard_map/ppermute | solution.py:32
  30.5 11.1 %collective-permute-start.17 = (bf16[512,128]{1,0:T(8,128)(2,1)S(1)}, bf16[512,128]{1,0:T(8,128)(2,1)S(1)}, u32[]{:S(2)}, u32[]{:S(2)}) collective-permute-start(bf16[512,128]{1,0:T(8,128)(2,1)S(1)} %get-tuple-element.5), channel_id=1, source_target_pairs={{0,16},{2,18},{4,20},{6,22},{8,24},{10,26},{12,28},{14,30},{16,0},... | collective-permute-start | bytes 393224 | tf_op jit(solution)/shard_map/ppermute | solution.py:32
  30.5 11.0 %collective-permute-start.16 = (bf16[512,128]{1,0:T(8,128)(2,1)S(1)}, bf16[512,128]{1,0:T(8,128)(2,1)S(1)}, u32[]{:S(2)}, u32[]{:S(2)}) collective-permute-start(bf16[512,128]{1,0:T(8,128)(2,1)S(1)} %get-tuple-element.3), channel_id=1, source_target_pairs={{0,8},{2,10},{4,12},{6,14},{8,0},{10,2},{12,4},{14,6},{16,24},{18,... | collective-permute-start | bytes 393224 | tf_op jit(solution)/shard_map/ppermute | solution.py:32
  34.9 16.1 %collective-permute-start.9 = (bf16[256,512]{1,0:T(8,128)(2,1)S(1)}, bf16[256,512]{1,0:T(8,128)(2,1)S(1)}, u32[]{:S(2)}, u32[]{:S(2)}) collective-permute-start(bf16[256,512]{1,0:T(8,128)(2,1)S(1)} %pad_maximum_fusion.2), channel_id=1, source_target_pairs={{0,2},{2,0},{4,6},{6,4},{8,10},{10,8},{12,14},{14,12},{16,18},{18,... | collective-permute-start | bytes 786440 | tf_op jit(solution)/shard_map/ppermute | solution.py:28
  36.4 15.0 %copy-start.1 = (bf16[128,1024]{1,0:T(8,128)(2,1)S(1)}, bf16[128,1024]{1,0:T(8,128)(2,1)}, u32[]{:S(2)}) copy-start(bf16[128,1024]{1,0:T(8,128)(2,1)} %param.5) | copy-start | bytes 786436
  36.5 7.6 %collective-permute-start.14 = (bf16[128,512]{1,0:T(8,128)(2,1)S(1)}, bf16[128,512]{1,0:T(8,128)(2,1)S(1)}, u32[]{:S(2)}, u32[]{:S(2)}) collective-permute-start(bf16[128,512]{1,0:T(8,128)(2,1)S(1)} %pad_maximum_fusion.6), channel_id=1, source_target_pairs={{0,8},{2,10},{4,12},{6,14},{8,0},{10,2},{12,4},{14,6},{16,24},{18,... | collective-permute-start | bytes 393224 | tf_op jit(solution)/shard_map/ppermute | solution.py:32
  44.1 6.1 %collective-permute-start.15 = (bf16[64,512]{1,0:T(8,128)(2,1)S(1)}, bf16[64,512]{1,0:T(8,128)(2,1)S(1)}, u32[]{:S(2)}, u32[]{:S(2)}) collective-permute-start(bf16[64,512]{1,0:T(8,128)(2,1)S(1)} %fusion.24), channel_id=1, source_target_pairs={{0,16},{2,18},{4,20},{6,22},{8,24},{10,26},{12,28},{14,30},{16,0},... | collective-permute-start | bytes 196616 | tf_op jit(solution)/shard_map/ppermute | solution.py:32
  45.3 6.1 %collective-permute-start.19 = (bf16[128,512]{1,0:T(8,128)(2,1)S(1)}, bf16[128,512]{1,0:T(8,128)(2,1)S(1)}, u32[]{:S(2)}, u32[]{:S(2)}) collective-permute-start(bf16[128,512]{1,0:T(8,128)(2,1)S(1)} %convolution_convert_fusion.1), channel_id=1, source_target_pairs={{0,1},{1,0},{2,3},{3,2},{4,5},{5,4},{6,7},{7,6},{8,9},{9,8},{10,11... | collective-permute-start | bytes 393224 | tf_op jit(solution)/shard_map/ppermute | solution.py:49
  50.9 5.3 %collective-permute-start.10 = (bf16[128,512]{1,0:T(8,128)(2,1)S(1)}, bf16[128,512]{1,0:T(8,128)(2,1)S(1)}, u32[]{:S(2)}, u32[]{:S(2)}) collective-permute-start(bf16[128,512]{1,0:T(8,128)(2,1)S(1)} %fusion.13), channel_id=1, source_target_pairs={{0,4},{2,6},{4,0},{6,2},{8,12},{10,14},{12,8},{14,10},{16,20},{18,... | collective-permute-start | bytes 393224 | tf_op jit(solution)/shard_map/ppermute | solution.py:28

commit v22 on v20

--- a/solution.py
+++ b/solution.py
@@ -76,7 +76,9 @@
     arrived = [
         along_inner(ordered[t * per_core : (t + 1) * per_core], t) for t in turns
     ]
-    everyone = lax.all_gather(jnp.concatenate(arrived, 0), "rep", axis=0)
+    hidden_stack = [along_outer(hidden_part, e) for e in turns]
+    ready = sum(lanes(part, 0) * 0 for part in hidden_stack[2:])
+    everyone = lax.all_gather(jnp.concatenate(arrived, 0) + ready, "rep", axis=0)
     rows = []
     for t in turns:
         row_block = outer_pos * side + (inner_pos ^ t)
@@ -92,7 +94,7 @@
         rows.append(jnp.concatenate(row, 1))
     block = jnp.concatenate(rows, 0)
 
-    hidden_stack = jnp.concatenate([along_outer(hidden_part, e) for e in turns], 0)
+    hidden_stack = jnp.concatenate(hidden_stack, 0)
     grad_part = columns_of(cotangent, rep_pos)
     grad_stack = jnp.concatenate([along_inner(grad_part, t) for t in turns], 0)
 

time: 52.1 us -> 53 us (1.017)
  matrix products: 4.05 us -> 3.08 us
  local copies, waits for them, and re-layouts: 1.22 us -> 2.12 us
  waiting for transfers between devices: 12.4 us -> 13.2 us
    ppermute x8, waiting for transfers between devices: 9.14 us -> 12.5 us  [along_outer(): return lax.ppermute(value, 'blk', pairs) if turn else value]
    ppermute x11, waiting for transfers between devices: 3.25 us -> 0.7 us  [along_inner(): return lax.ppermute(value, 'blk', pairs) if turn else value]
    ppermute x11, starting transfers between devices: 12.8 us -> 13.9 us  [along_inner(): return lax.ppermute(value, 'blk', pairs) if turn else value]
    ppermute x8, starting transfers between devices: 12.3 us -> 11.2 us  [along_outer(): return lax.ppermute(value, 'blk', pairs) if turn else value]
    dot_general x6, matrix products: 4.05 us -> 3.08 us  [dot(): lax.dot_general(lhs, rhs, (dims, ((), ())), preferred_element_type=jnp.fl...]
    dynamic_slice x1, local copies, waits for them, and re-layouts: 0.02 us -> 0.91 us  [columns_of(): return lax.dynamic_slice_in_dim(value, index * cols_here, cols_here, 1)]
where the time goes in v22:
time: 53 us; the launch traced here: 52.7 us
  starting transfers between devices  25.2 us (48%)
  waiting for transfers between devices  13.2 us (25%)
  blocking collectives  4.18 us (8%)
  other arithmetic  3.87 us (7%)
  matrix products  3.08 us (6%)
  local copies, waits for them, and re-layouts  2.12 us (4%)
  between operations  1.04 us (2%)
    ppermute x11, starting transfers between devices, along_inner(): return lax.ppermute(value, 'blk', pairs) if turn else value  13.9 us
    ppermute x8, waiting for transfers between devices, along_outer(): return lax.ppermute(value, 'blk', pairs) if turn else value  12.5 us
    ppermute x8, starting transfers between devices, along_outer(): return lax.ppermute(value, 'blk', pairs) if turn else value  11.2 us
    dot_general x6, matrix products, dot(): lax.dot_general(lhs, rhs, (dims, ((), ())), preferred_element_type=jnp.fl...  3.08 us
    all_gather x1, blocking collectives, shards(): lax.all_gather(jnp.concatenate(arrived, 0) + ready, 'rep', axis=0)  2.18 us
    all_gather x1, blocking collectives, shards(): lax.all_gather(mixed_cols.astype(bf16), 'rep', axis=0, tiled=True)  1.99 us
    max x1, other arithmetic, shards(): hidden_part = jnp.maximum(columns_of(hidden_pre, rep_pos), 0)  1.08 us
  transfers between devices with their start and end apart: 20, of which 7 were waited for; matrix products, arithmetic and copies ran while one was open for 14% of the time, Pallas kernels for 0%

profile of v22, /device:TPU:0, one launch (start us, length us, event | category | flops | bytes accessed | tf_op | source)
XLA Modules:
  0.0 52.7 jit_solution(10604453595680619538)
XLA Ops:
  0.7 1.1 %dynamic-slice_maximum_fusion = bf16[128,512]{1,0:T(8,128)(2,1)S(1)} fusion(bf16[128,1024]{1,0:T(8,128)(2,1)} %param.5, s32[]{:T(128)S(6)} %select_n.214), kind=kLoop, calls=%fused_computation.48 | loop fusion | flops 262144 | bytes 262148 | tf_op jit(solution)/shard_map/max | solution.py:66
  1.7 5.1 %collective-permute-start.2 = (bf16[128,512]{1,0:T(8,128)(2,1)S(1)}, bf16[128,512]{1,0:T(8,128)(2,1)S(1)}, u32[]{:S(2)}, u32[]{:S(2)}) collective-permute-start(bf16[128,512]{1,0:T(8,128)(2,1)S(1)} %dynamic-slice_maximum_fusion), channel_id=1, source_target_pairs={{0,24},{2,26},{4,28},{6,30},{8,16},{10,18},{12,20},{14,22},{16,8},... | collective-permute-start | bytes 393224 | tf_op jit(solution)/shard_map/ppermute | solution.py:32
  6.9 0.6 %collective-permute-start = (bf16[128,512]{1,0:T(8,128)(2,1)S(1)}, bf16[128,512]{1,0:T(8,128)(2,1)S(1)}, u32[]{:S(2)}, u32[]{:S(2)}) collective-permute-start(bf16[128,512]{1,0:T(8,128)(2,1)S(1)} %dynamic-slice_maximum_fusion), channel_id=1, source_target_pairs={{0,8},{2,10},{4,12},{6,14},{8,0},{10,2},{12,4},{14,6},{16,24},{18,... | collective-permute-start | bytes 393224 | tf_op jit(solution)/shard_map/ppermute | solution.py:32
  7.5 0.7 %add_bitcast_fusion = s32[8]{0:T(128)S(1)} fusion(s32[1,8]{1,0:T(1,128)} %param.7, s32[]{:T(128)S(6)} %shift_right_arithmetic.54, s32[]{:T(128)S(6)} %and.60), kind=kLoop, calls=%fused_computation.97 | loop fusion | flops 56 | bytes 72 | tf_op jit(solution)/shard_map/eq | solution.py:72
  8.2 0.9 %slice_bitcast_fusion.10 = (bf16[128,128]{1,0:T(8,128)(2,1)S(1)}, bf16[128,128]{1,0:T(8,128)(2,1)S(1)}, bf16[128,128]{1,0:T(8,128)(2,1)S(1)}, bf16[128,128]{1,0:...) fusion(bf16[1,8,128,128]{3,2,1,0:T(8,128)(2,1)} %param.6), kind=kLoop, calls=%fused_computation.78 | loop fusion | bytes 524288 | tf_op jit(solution)/shard_map/jit(_where)/broadcast_in_dim | solution.py:75
  9.4 2.7 %collective-permute-start.5 = (bf16[2,128,128]{2,1,0:T(8,128)(2,1)S(1)}, bf16[2,128,128]{2,1,0:T(8,128)(2,1)S(1)}, u32[]{:S(2)}, u32[]{:S(2)}) collective-permute-start(bf16[2,128,128]{2,1,0:T(8,128)(2,1)S(1)} %get-tuple-element.30), channel_id=1, source_target_pairs={{0,6},{2,4},{4,2},{6,0},{8,14},{10,12},{12,10},{14,8},{16,22},{18,... | collective-permute-start | bytes 196616 | tf_op jit(solution)/shard_map/ppermute | solution.py:28
  12.0 0.5 collective-permute-start.4
  12.5 0.9 %constant_dynamic-slice_fusion = bf16[128,512]{1,0:T(8,128)(2,1)S(1)} fusion(bf16[128,1024]{1,0:T(8,128)(2,1)} %param.9, s32[]{:T(128)S(6)} %select_n.214), kind=kLoop, calls=%fused_computation.82 | loop fusion | bytes 262148 | tf_op jit(solution)/shard_map/dynamic_slice | solution.py:64
  13.6 0.5 collective-permute-start.3
  14.1 3.8 %collective-permute-done.1 = bf16[128,512]{1,0:T(8,128)(2,1)S(1)} collective-permute-done((bf16[128,512]{1,0:T(8,128)(2,1)S(1)}, bf16[128,512]{1,0:T(8,128)(2,1)S(1)}, u32[]{:S(2)}, u32[]{:S(2)}) %collective-permute-start.1) | collective-permute-done | bytes 131104 | tf_op jit(solution)/shard_map/ppermute | solution.py:32
  17.9 2.4 %collective-permute-start.13 = (bf16[128,512]{1,0:T(8,128)(2,1)S(1)}, bf16[128,512]{1,0:T(8,128)(2,1)S(1)}, u32[]{:S(2)}, u32[]{:S(2)}) collective-permute-start(bf16[128,512]{1,0:T(8,128)(2,1)S(1)} %constant_dynamic-slice_fusion), channel_id=1, source_target_pairs={{0,6},{2,4},{4,2},{6,0},{8,14},{10,12},{12,10},{14,8},{16,22},{18,... | collective-permute-start | bytes 393224 | tf_op jit(solution)/shard_map/ppermute | solution.py:28
  20.4 0.6 %collective-permute-start.12 = (bf16[128,512]{1,0:T(8,128)(2,1)S(1)}, bf16[128,512]{1,0:T(8,128)(2,1)S(1)}, u32[]{:S(2)}, u32[]{:S(2)}) collective-permute-start(bf16[128,512]{1,0:T(8,128)(2,1)S(1)} %constant_dynamic-slice_fusion), channel_id=1, source_target_pairs={{0,4},{2,6},{4,0},{6,2},{8,12},{10,14},{12,8},{14,10},{16,20},{18,... | collective-permute-start | bytes 393224 | tf_op jit(solution)/shard_map/ppermute | solution.py:28
  21.0 0.5 %collective-permute-start.11 = (bf16[128,512]{1,0:T(8,128)(2,1)S(1)}, bf16[128,512]{1,0:T(8,128)(2,1)S(1)}, u32[]{:S(2)}, u32[]{:S(2)}) collective-permute-start(bf16[128,512]{1,0:T(8,128)(2,1)S(1)} %constant_dynamic-slice_fusion), channel_id=1, source_target_pairs={{0,2},{2,0},{4,6},{6,4},{8,10},{10,8},{12,14},{14,12},{16,18},{18,... | collective-permute-start | bytes 393224 | tf_op jit(solution)/shard_map/ppermute | solution.py:28
  21.6 2.2 %all_gather.7 = bf16[2,8,128,128]{3,2,1,0:T(8,128)(2,1)S(1)} all-gather(bf16[1,8,128,128]{3,2,1,0:T(8,128)(2,1)S(1)} %maximum_add_fusion), channel_id=1, replica_groups=mesh['blk'=16,'rep'=2] {'rep'}, dimensions={0}, use_global_device_ids=true | all-gather | bytes 786432 | tf_op jit(solution)/shard_map/all_gather | solution.py:81
  23.9 0.5 convolution_convert_fusion
  24.5 2.5 %collective-permute-start.8 = (bf16[128,512]{1,0:T(8,128)(2,1)S(1)}, bf16[128,512]{1,0:T(8,128)(2,1)S(1)}, u32[]{:S(2)}, u32[]{:S(2)}) collective-permute-start(bf16[128,512]{1,0:T(8,128)(2,1)S(1)} %pad_maximum_fusion.4), channel_id=1, source_target_pairs={{0,6},{2,4},{4,2},{6,0},{8,14},{10,12},{12,10},{14,8},{16,22},{18,... | collective-permute-start | bytes 393224 | tf_op jit(solution)/shard_map/ppermute | solution.py:28
  27.1 0.6 %collective-permute-start.7 = (bf16[128,512]{1,0:T(8,128)(2,1)S(1)}, bf16[128,512]{1,0:T(8,128)(2,1)S(1)}, u32[]{:S(2)}, u32[]{:S(2)}) collective-permute-start(bf16[128,512]{1,0:T(8,128)(2,1)S(1)} %pad_maximum_fusion.3), channel_id=1, source_target_pairs={{0,4},{2,6},{4,0},{6,2},{8,12},{10,14},{12,8},{14,10},{16,20},{18,... | collective-permute-start | bytes 393224 | tf_op jit(solution)/shard_map/ppermute | solution.py:28
  27.7 0.6 %collective-permute-start.6 = (bf16[128,512]{1,0:T(8,128)(2,1)S(1)}, bf16[128,512]{1,0:T(8,128)(2,1)S(1)}, u32[]{:S(2)}, u32[]{:S(2)}) collective-permute-start(bf16[128,512]{1,0:T(8,128)(2,1)S(1)} %pad_maximum_fusion.2), channel_id=1, source_target_pairs={{0,2},{2,0},{4,6},{6,4},{8,10},{10,8},{12,14},{14,12},{16,18},{18,... | collective-permute-start | bytes 393224 | tf_op jit(solution)/shard_map/ppermute | solution.py:28
  28.3 0.5 fusion
  28.9 2.5 %collective-permute-start.18 = (bf16[512,128]{1,0:T(8,128)(2,1)S(1)}, bf16[512,128]{1,0:T(8,128)(2,1)S(1)}, u32[]{:S(2)}, u32[]{:S(2)}) collective-permute-start(bf16[512,128]{1,0:T(8,128)(2,1)S(1)} %get-tuple-element.4), channel_id=1, source_target_pairs={{0,24},{2,26},{4,28},{6,30},{8,16},{10,18},{12,20},{14,22},{16,8},... | collective-permute-start | bytes 393224 | tf_op jit(solution)/shard_map/ppermute | solution.py:32
  31.4 1.9 %collective-permute-start.16 = (bf16[512,128]{1,0:T(8,128)(2,1)S(1)}, bf16[512,128]{1,0:T(8,128)(2,1)S(1)}, u32[]{:S(2)}, u32[]{:S(2)}) collective-permute-start(bf16[512,128]{1,0:T(8,128)(2,1)S(1)} %get-tuple-element.3), channel_id=1, source_target_pairs={{0,8},{2,10},{4,12},{6,14},{8,0},{10,2},{12,4},{14,6},{16,24},{18,... | collective-permute-start | bytes 393224 | tf_op jit(solution)/shard_map/ppermute | solution.py:32
  33.3 0.5 collective-permute-done.7
  34.0 2.0 %all_gather.8 = bf16[256,512]{1,0:T(8,128)(2,1)S(1)} all-gather(bf16[128,512]{1,0:T(8,128)(2,1)S(1)} %fusion.19), channel_id=1, replica_groups=mesh['blk'=16,'rep'=2] {'rep'}, dimensions={0}, use_global_device_ids=true | all-gather | bytes 393216 | tf_op jit(solution)/shard_map/all_gather | solution.py:114
  36.4 1.6 %collective-permute-start.9 = (bf16[256,512]{1,0:T(8,128)(2,1)S(1)}, bf16[256,512]{1,0:T(8,128)(2,1)S(1)}, u32[]{:S(2)}, u32[]{:S(2)}) collective-permute-start(bf16[256,512]{1,0:T(8,128)(2,1)S(1)} %pad_maximum_fusion.1), channel_id=1, source_target_pairs={{0,2},{2,0},{4,6},{6,4},{8,10},{10,8},{12,14},{14,12},{16,18},{18,... | collective-permute-start | bytes 786440 | tf_op jit(solution)/shard_map/ppermute | solution.py:28
  38.5 3.5 %collective-permute-done.17 = bf16[512,128]{1,0:T(8,128)(2,1)S(1)} collective-permute-done((bf16[512,128]{1,0:T(8,128)(2,1)S(1)}, bf16[512,128]{1,0:T(8,128)(2,1)S(1)}, u32[]{:S(2)}, u32[]{:S(2)}) %collective-permute-start.17) | collective-permute-done | bytes 131104 | tf_op jit(solution)/shard_map/ppermute | solution.py:32
  42.6 2.1 %collective-permute-done.14 = bf16[128,512]{1,0:T(8,128)(2,1)S(1)} collective-permute-done((bf16[128,512]{1,0:T(8,128)(2,1)S(1)}, bf16[128,512]{1,0:T(8,128)(2,1)S(1)}, u32[]{:S(2)}, u32[]{:S(2)}) %collective-permute-start.14) | collective-permute-done | bytes 131104 | tf_op jit(solution)/shard_map/ppermute | solution.py:32
  44.8 0.8 %collective-permute-start.15 = (bf16[64,512]{1,0:T(8,128)(2,1)S(1)}, bf16[64,512]{1,0:T(8,128)(2,1)S(1)}, u32[]{:S(2)}, u32[]{:S(2)}) collective-permute-start(bf16[64,512]{1,0:T(8,128)(2,1)S(1)} %fusion.22), channel_id=1, source_target_pairs={{0,16},{2,18},{4,20},{6,22},{8,24},{10,26},{12,28},{14,30},{16,0},... | collective-permute-start | bytes 196616 | tf_op jit(solution)/shard_map/ppermute | solution.py:32
  45.7 1.1 %select_convert_fusion = bf16[128,512]{1,0:T(8,128)(2,1)} fusion(bf16[128,512]{1,0:T(8,128)(2,1)S(1)} %collective-permute-done.19, bf16[128,1024]{1,0:T(8,128)(2,1)S(1)} %copy-done.1, s32[]{:T(128)S(6)} %select_n.214, bf16[512,128]{1,0:T(8,128)(2,1)S(1)} %fusion.16, bf16[2,512,1024]{2,1,0:T(8,128)(2,1)S(1)} %bitcast.114, s32[]{:T(128)S(6)} %select_n.279, ...), kind=kOutput, calls=%fused_computation.33 | convolution fusion | flops 67567616 | bytes 1048588 | tf_op jit(solution)/shard_map/dot_general | solution.py:52
  46.8 1.4 %collective-permute-start.10 = (bf16[128,512]{1,0:T(8,128)(2,1)S(1)}, bf16[128,512]{1,0:T(8,128)(2,1)S(1)}, u32[]{:S(2)}, u32[]{:S(2)}) collective-permute-start(bf16[128,512]{1,0:T(8,128)(2,1)S(1)} %fusion.13), channel_id=1, source_target_pairs={{0,4},{2,6},{4,0},{6,2},{8,12},{10,14},{12,8},{14,10},{16,20},{18,... | collective-permute-start | bytes 393224 | tf_op jit(solution)/shard_map/ppermute | solution.py:28
  48.2 3.0 %collective-permute-done.15 = bf16[64,512]{1,0:T(8,128)(2,1)S(1)} collective-permute-done((bf16[64,512]{1,0:T(8,128)(2,1)S(1)}, bf16[64,512]{1,0:T(8,128)(2,1)S(1)}, u32[]{:S(2)}, u32[]{:S(2)}) %collective-permute-start.15) | collective-permute-done | bytes 65568 | tf_op jit(solution)/shard_map/ppermute | solution.py:32
  51.2 0.7 %fusion.23 = f32[64,512]{1,0:T(8,128)} fusion(bf16[64,512]{1,0:T(8,128)(2,1)S(1)} %collective-permute-done.15, f32[4,64,512]{2,1,0:T(8,128)S(1)} %bitcast.118, s32[]{:T(128)S(6)} %select_n.271, bf16[128,512]{1,0:T(8,128)(2,1)S(1)} %collective-permute-done.14), kind=kLoop, calls=%fused_computation.45 | loop fusion | flops 131072 | bytes 393220 | tf_op jit(solution)/shard_map/add | solution.py:42
  52.0 0.7 %fusion.15 = bf16[128,512]{1,0:T(8,128)(2,1)} fusion(f32[512,512]{1,0:T(8,128)S(1)} %get-tuple-element.60, bf16[128,512]{1,0:T(8,128)(2,1)S(1)} %collective-permute-done.10, bf16[256,512]{1,0:T(8,128)(2,1)S(1)} %collective-permute-done.9), kind=kLoop, calls=%fused_computation.24 | loop fusion | flops 327680 | bytes 655360 | tf_op jit(solution)/shard_map/convert_element_type | solution.py:127
  (55 shorter events, 2.5 us)
Async XLA Ops:
  0.6 12.9 %copy-start = (bf16[1024,1024]{1,0:T(8,128)(2,1)S(1)}, bf16[1024,1024]{1,0:T(8,128)(2,1)}, u32[]{:S(2)}) copy-start(bf16[1024,1024]{1,0:T(8,128)(2,1)} %param.8) | copy-start | bytes 6291460
  1.7 11.9 %collective-permute-start.2 = (bf16[128,512]{1,0:T(8,128)(2,1)S(1)}, bf16[128,512]{1,0:T(8,128)(2,1)S(1)}, u32[]{:S(2)}, u32[]{:S(2)}) collective-permute-start(bf16[128,512]{1,0:T(8,128)(2,1)S(1)} %dynamic-slice_maximum_fusion), channel_id=1, source_target_pairs={{0,24},{2,26},{4,28},{6,30},{8,16},{10,18},{12,20},{14,22},{16,8},... | collective-permute-start | bytes 393224 | tf_op jit(solution)/shard_map/ppermute | solution.py:32
  6.8 11.1 %collective-permute-start.1 = (bf16[128,512]{1,0:T(8,128)(2,1)S(1)}, bf16[128,512]{1,0:T(8,128)(2,1)S(1)}, u32[]{:S(2)}, u32[]{:S(2)}) collective-permute-start(bf16[128,512]{1,0:T(8,128)(2,1)S(1)} %dynamic-slice_maximum_fusion), channel_id=1, source_target_pairs={{0,16},{2,18},{4,20},{6,22},{8,24},{10,26},{12,28},{14,30},{16,0},... | collective-permute-start | bytes 393224 | tf_op jit(solution)/shard_map/ppermute | solution.py:32
  6.9 17.1 %collective-permute-start = (bf16[128,512]{1,0:T(8,128)(2,1)S(1)}, bf16[128,512]{1,0:T(8,128)(2,1)S(1)}, u32[]{:S(2)}, u32[]{:S(2)}) collective-permute-start(bf16[128,512]{1,0:T(8,128)(2,1)S(1)} %dynamic-slice_maximum_fusion), channel_id=1, source_target_pairs={{0,8},{2,10},{4,12},{6,14},{8,0},{10,2},{12,4},{14,6},{16,24},{18,... | collective-permute-start | bytes 393224 | tf_op jit(solution)/shard_map/ppermute | solution.py:32
  9.4 11.0 %collective-permute-start.5 = (bf16[2,128,128]{2,1,0:T(8,128)(2,1)S(1)}, bf16[2,128,128]{2,1,0:T(8,128)(2,1)S(1)}, u32[]{:S(2)}, u32[]{:S(2)}) collective-permute-start(bf16[2,128,128]{2,1,0:T(8,128)(2,1)S(1)} %get-tuple-element.30), channel_id=1, source_target_pairs={{0,6},{2,4},{4,2},{6,0},{8,14},{10,12},{12,10},{14,8},{16,22},{18,... | collective-permute-start | bytes 196616 | tf_op jit(solution)/shard_map/ppermute | solution.py:28
  12.0 9.0 %collective-permute-start.4 = (bf16[2,128,128]{2,1,0:T(8,128)(2,1)S(1)}, bf16[2,128,128]{2,1,0:T(8,128)(2,1)S(1)}, u32[]{:S(2)}, u32[]{:S(2)}) collective-permute-start(bf16[2,128,128]{2,1,0:T(8,128)(2,1)S(1)} %get-tuple-element.31), channel_id=1, source_target_pairs={{0,4},{2,6},{4,0},{6,2},{8,12},{10,14},{12,8},{14,10},{16,20},{18,... | collective-permute-start | bytes 196616 | tf_op jit(solution)/shard_map/ppermute | solution.py:28
  13.6 7.9 %collective-permute-start.3 = (bf16[2,128,128]{2,1,0:T(8,128)(2,1)S(1)}, bf16[2,128,128]{2,1,0:T(8,128)(2,1)S(1)}, u32[]{:S(2)}, u32[]{:S(2)}) collective-permute-start(bf16[2,128,128]{2,1,0:T(8,128)(2,1)S(1)} %get-tuple-element.32), channel_id=1, source_target_pairs={{0,2},{2,0},{4,6},{6,4},{8,10},{10,8},{12,14},{14,12},{16,18},{18,... | collective-permute-start | bytes 196616 | tf_op jit(solution)/shard_map/ppermute | solution.py:28
  17.9 9.8 %collective-permute-start.13 = (bf16[128,512]{1,0:T(8,128)(2,1)S(1)}, bf16[128,512]{1,0:T(8,128)(2,1)S(1)}, u32[]{:S(2)}, u32[]{:S(2)}) collective-permute-start(bf16[128,512]{1,0:T(8,128)(2,1)S(1)} %constant_dynamic-slice_fusion), channel_id=1, source_target_pairs={{0,6},{2,4},{4,2},{6,0},{8,14},{10,12},{12,10},{14,8},{16,22},{18,... | collective-permute-start | bytes 393224 | tf_op jit(solution)/shard_map/ppermute | solution.py:28
  20.4 7.9 %collective-permute-start.12 = (bf16[128,512]{1,0:T(8,128)(2,1)S(1)}, bf16[128,512]{1,0:T(8,128)(2,1)S(1)}, u32[]{:S(2)}, u32[]{:S(2)}) collective-permute-start(bf16[128,512]{1,0:T(8,128)(2,1)S(1)} %constant_dynamic-slice_fusion), channel_id=1, source_target_pairs={{0,4},{2,6},{4,0},{6,2},{8,12},{10,14},{12,8},{14,10},{16,20},{18,... | collective-permute-start | bytes 393224 | tf_op jit(solution)/shard_map/ppermute | solution.py:28
  21.0 7.3 %collective-permute-start.11 = (bf16[128,512]{1,0:T(8,128)(2,1)S(1)}, bf16[128,512]{1,0:T(8,128)(2,1)S(1)}, u32[]{:S(2)}, u32[]{:S(2)}) collective-permute-start(bf16[128,512]{1,0:T(8,128)(2,1)S(1)} %constant_dynamic-slice_fusion), channel_id=1, source_target_pairs={{0,2},{2,0},{4,6},{6,4},{8,10},{10,8},{12,14},{14,12},{16,18},{18,... | collective-permute-start | bytes 393224 | tf_op jit(solution)/shard_map/ppermute | solution.py:28
  24.5 6.9 %collective-permute-start.8 = (bf16[128,512]{1,0:T(8,128)(2,1)S(1)}, bf16[128,512]{1,0:T(8,128)(2,1)S(1)}, u32[]{:S(2)}, u32[]{:S(2)}) collective-permute-start(bf16[128,512]{1,0:T(8,128)(2,1)S(1)} %pad_maximum_fusion.4), channel_id=1, source_target_pairs={{0,6},{2,4},{4,2},{6,0},{8,14},{10,12},{12,10},{14,8},{16,22},{18,... | collective-permute-start | bytes 393224 | tf_op jit(solution)/shard_map/ppermute | solution.py:28
  27.1 6.8 %collective-permute-start.7 = (bf16[128,512]{1,0:T(8,128)(2,1)S(1)}, bf16[128,512]{1,0:T(8,128)(2,1)S(1)}, u32[]{:S(2)}, u32[]{:S(2)}) collective-permute-start(bf16[128,512]{1,0:T(8,128)(2,1)S(1)} %pad_maximum_fusion.3), channel_id=1, source_target_pairs={{0,4},{2,6},{4,0},{6,2},{8,12},{10,14},{12,8},{14,10},{16,20},{18,... | collective-permute-start | bytes 393224 | tf_op jit(solution)/shard_map/ppermute | solution.py:28
  27.7 6.2 %collective-permute-start.6 = (bf16[128,512]{1,0:T(8,128)(2,1)S(1)}, bf16[128,512]{1,0:T(8,128)(2,1)S(1)}, u32[]{:S(2)}, u32[]{:S(2)}) collective-permute-start(bf16[128,512]{1,0:T(8,128)(2,1)S(1)} %pad_maximum_fusion.2), channel_id=1, source_target_pairs={{0,2},{2,0},{4,6},{6,4},{8,10},{10,8},{12,14},{14,12},{16,18},{18,... | collective-permute-start | bytes 393224 | tf_op jit(solution)/shard_map/ppermute | solution.py:28
  28.9 9.7 %collective-permute-start.18 = (bf16[512,128]{1,0:T(8,128)(2,1)S(1)}, bf16[512,128]{1,0:T(8,128)(2,1)S(1)}, u32[]{:S(2)}, u32[]{:S(2)}) collective-permute-start(bf16[512,128]{1,0:T(8,128)(2,1)S(1)} %get-tuple-element.4), channel_id=1, source_target_pairs={{0,24},{2,26},{4,28},{6,30},{8,16},{10,18},{12,20},{14,22},{16,8},... | collective-permute-start | bytes 393224 | tf_op jit(solution)/shard_map/ppermute | solution.py:32
  31.4 10.6 %collective-permute-start.17 = (bf16[512,128]{1,0:T(8,128)(2,1)S(1)}, bf16[512,128]{1,0:T(8,128)(2,1)S(1)}, u32[]{:S(2)}, u32[]{:S(2)}) collective-permute-start(bf16[512,128]{1,0:T(8,128)(2,1)S(1)} %get-tuple-element.5), channel_id=1, source_target_pairs={{0,16},{2,18},{4,20},{6,22},{8,24},{10,26},{12,28},{14,30},{16,0},... | collective-permute-start | bytes 393224 | tf_op jit(solution)/shard_map/ppermute | solution.py:32
  31.4 10.6 %collective-permute-start.16 = (bf16[512,128]{1,0:T(8,128)(2,1)S(1)}, bf16[512,128]{1,0:T(8,128)(2,1)S(1)}, u32[]{:S(2)}, u32[]{:S(2)}) collective-permute-start(bf16[512,128]{1,0:T(8,128)(2,1)S(1)} %get-tuple-element.3), channel_id=1, source_target_pairs={{0,8},{2,10},{4,12},{6,14},{8,0},{10,2},{12,4},{14,6},{16,24},{18,... | collective-permute-start | bytes 393224 | tf_op jit(solution)/shard_map/ppermute | solution.py:32
  36.4 10.4 %collective-permute-start.9 = (bf16[256,512]{1,0:T(8,128)(2,1)S(1)}, bf16[256,512]{1,0:T(8,128)(2,1)S(1)}, u32[]{:S(2)}, u32[]{:S(2)}) collective-permute-start(bf16[256,512]{1,0:T(8,128)(2,1)S(1)} %pad_maximum_fusion.1), channel_id=1, source_target_pairs={{0,2},{2,0},{4,6},{6,4},{8,10},{10,8},{12,14},{14,12},{16,18},{18,... | collective-permute-start | bytes 786440 | tf_op jit(solution)/shard_map/ppermute | solution.py:28
  38.0 7.7 %copy-start.1 = (bf16[128,1024]{1,0:T(8,128)(2,1)S(1)}, bf16[128,1024]{1,0:T(8,128)(2,1)}, u32[]{:S(2)}) copy-start(bf16[128,1024]{1,0:T(8,128)(2,1)} %param.5) | copy-start | bytes 786436
  38.3 6.5 %collective-permute-start.14 = (bf16[128,512]{1,0:T(8,128)(2,1)S(1)}, bf16[128,512]{1,0:T(8,128)(2,1)S(1)}, u32[]{:S(2)}, u32[]{:S(2)}) collective-permute-start(bf16[128,512]{1,0:T(8,128)(2,1)S(1)} %pad_maximum_fusion.5), channel_id=1, source_target_pairs={{0,8},{2,10},{4,12},{6,14},{8,0},{10,2},{12,4},{14,6},{16,24},{18,... | collective-permute-start | bytes 393224 | tf_op jit(solution)/shard_map/ppermute | solution.py:32
  42.6 3.1 %collective-permute-start.19 = (bf16[128,512]{1,0:T(8,128)(2,1)S(1)}, bf16[128,512]{1,0:T(8,128)(2,1)S(1)}, u32[]{:S(2)}, u32[]{:S(2)}) collective-permute-start(bf16[128,512]{1,0:T(8,128)(2,1)S(1)} %convolution_convert_fusion.1), channel_id=1, source_target_pairs={{0,1},{1,0},{2,3},{3,2},{4,5},{5,4},{6,7},{7,6},{8,9},{9,8},{10,11... | collective-permute-start | bytes 393224 | tf_op jit(solution)/shard_map/ppermute | solution.py:49
  44.8 6.4 %collective-permute-start.15 = (bf16[64,512]{1,0:T(8,128)(2,1)S(1)}, bf16[64,512]{1,0:T(8,128)(2,1)S(1)}, u32[]{:S(2)}, u32[]{:S(2)}) collective-permute-start(bf16[64,512]{1,0:T(8,128)(2,1)S(1)} %fusion.22), channel_id=1, source_target_pairs={{0,16},{2,18},{4,20},{6,22},{8,24},{10,26},{12,28},{14,30},{16,0},... | collective-permute-start | bytes 196616 | tf_op jit(solution)/shard_map/ppermute | solution.py:32
  46.8 5.2 %collective-permute-start.10 = (bf16[128,512]{1,0:T(8,128)(2,1)S(1)}, bf16[128,512]{1,0:T(8,128)(2,1)S(1)}, u32[]{:S(2)}, u32[]{:S(2)}) collective-permute-start(bf16[128,512]{1,0:T(8,128)(2,1)S(1)} %fusion.13), channel_id=1, source_target_pairs={{0,4},{2,6},{4,0},{6,2},{8,12},{10,14},{12,8},{14,10},{16,20},{18,... | collective-permute-start | bytes 393224 | tf_op jit(solution)/shard_map/ppermute | solution.py:28

commit v23 on v20

--- a/solution.py
+++ b/solution.py
@@ -113,8 +113,8 @@
     w_share = w_out.reshape(side, side, rows_here, feature_width)
     w_share = lax.dynamic_index_in_dim(w_share, inner_pos, 1, keepdims=False)
     w_share = columns_of(w_share.reshape(side * rows_here, feature_width), rep_pos)
-    out_part = dot(mixed_cols, w_share, ((0,), (0,)))
-    weight_part = after(dot(mixed_cols, grad_stack, ((1,), (0,))), out_part)
+    out_part = dot(mixed_cols, w_share, ((0,), (0,))).astype(bf16)
+    weight_part = after(dot(mixed_cols, grad_stack, ((1,), (0,))), out_part).astype(bf16)
     by_outer = weight_part.reshape(side, rows_here, cols_here)
     grad_weight = halved(
         [lax.dynamic_index_in_dim(by_outer, outer_pos ^ t, 0, keepdims=False) for t in turns],
@@ -137,8 +137,7 @@
         back_full = lax.all_gather(back, "rep", axis=0, tiled=True)
         w_mine = lax.dynamic_index_in_dim(w_rows, rep_pos, 0, keepdims=False)
         grad_in = dot(back_full, w_mine, ((0,), (1,)))
-    pre_part = columns_of(hidden_pre, rep_pos)
-    grad_pre = jnp.where(pre_part > 0, grad_in, 0.0).astype(bf16)
+    grad_pre = jnp.where(hidden_part > 0, grad_in, 0.0).astype(bf16)
     return (out_part, grad_weight, grad_pre)
 
 

time: 52.1 us -> 56.8 us (1.090)
  waiting for transfers between devices: 12.4 us -> 17.1 us
    ppermute x11, waiting for transfers between devices: 3.25 us -> 12.9 us  [along_inner(): return lax.ppermute(value, 'blk', pairs) if turn else value]
    ppermute x8, waiting for transfers between devices: 9.14 us -> 4.11 us  [along_outer(): return lax.ppermute(value, 'blk', pairs) if turn else value]
  transfers between devices with their start and end apart: 20 -> 20, of which waited for: 7 -> 8; matrix products, arithmetic and copies ran while one was open for 14% -> 13% of each run, Pallas kernels for 0% -> 0%
where the time goes in v23:
time: 56.8 us; the launch traced here: 56.6 us
  starting transfers between devices  25.3 us (45%)
  waiting for transfers between devices  17.1 us (30%)
  blocking collectives  4.18 us (7%)
  matrix products  4.05 us (7%)
  other arithmetic  3.87 us (7%)
  local copies, waits for them, and re-layouts  1.21 us (2%)
  between operations  0.95 us (2%)
    ppermute x11, waiting for transfers between devices, along_inner(): return lax.ppermute(value, 'blk', pairs) if turn else value  12.9 us
    ppermute x11, starting transfers between devices, along_inner(): return lax.ppermute(value, 'blk', pairs) if turn else value  12.7 us
    ppermute x8, starting transfers between devices, along_outer(): return lax.ppermute(value, 'blk', pairs) if turn else value  12.5 us
    ppermute x8, waiting for transfers between devices, along_outer(): return lax.ppermute(value, 'blk', pairs) if turn else value  4.11 us
    dot_general x6, matrix products, dot(): lax.dot_general(lhs, rhs, (dims, ((), ())), preferred_element_type=jnp.fl...  4.05 us
    all_gather x1, blocking collectives, shards(): everyone = lax.all_gather(jnp.concatenate(arrived, 0), 'rep', axis=0)  2.18 us
    all_gather x1, blocking collectives, shards(): lax.all_gather(mixed_cols.astype(bf16), 'rep', axis=0, tiled=True)  1.99 us
  transfers between devices with their start and end apart: 20, of which 8 were waited for; matrix products, arithmetic and copies ran while one was open for 13% of the time, Pallas kernels for 0%

profile of v23, /device:TPU:0, one launch (start us, length us, event | category | flops | bytes accessed | tf_op | source)
XLA Modules:
  0.0 56.6 jit_solution(17047784153898143023)
XLA Ops:
  0.7 1.1 %dynamic-slice_maximum_fusion = bf16[128,512]{1,0:T(8,128)(2,1)S(1)} fusion(bf16[128,1024]{1,0:T(8,128)(2,1)} %param.5, s32[]{:T(128)S(6)} %select_n.213), kind=kLoop, calls=%fused_computation.43 | loop fusion | flops 262144 | bytes 262148 | tf_op jit(solution)/shard_map/max | solution.py:66
  1.7 3.1 %collective-permute-start = (bf16[128,512]{1,0:T(8,128)(2,1)S(1)}, bf16[128,512]{1,0:T(8,128)(2,1)}, u32[]{:S(2)}, u32[]{:S(2)}) collective-permute-start(bf16[128,512]{1,0:T(8,128)(2,1)S(1)} %dynamic-slice_maximum_fusion), channel_id=1, source_target_pairs={{0,8},{2,10},{4,12},{6,14},{8,0},{10,2},{12,4},{14,6},{16,24},{18,... | collective-permute-start | bytes 393224 | tf_op jit(solution)/shard_map/ppermute | solution.py:32
  4.8 2.6 %collective-permute-start.1 = (bf16[128,512]{1,0:T(8,128)(2,1)S(1)}, bf16[128,512]{1,0:T(8,128)(2,1)}, u32[]{:S(2)}, u32[]{:S(2)}) collective-permute-start(bf16[128,512]{1,0:T(8,128)(2,1)S(1)} %dynamic-slice_maximum_fusion), channel_id=1, source_target_pairs={{0,16},{2,18},{4,20},{6,22},{8,24},{10,26},{12,28},{14,30},{16,0},... | collective-permute-start | bytes 393224 | tf_op jit(solution)/shard_map/ppermute | solution.py:32
  7.4 0.7 %add_bitcast_fusion = s32[8]{0:T(128)S(1)} fusion(s32[1,8]{1,0:T(1,128)} %param.7, s32[]{:T(128)S(6)} %shift_right_arithmetic.54, s32[]{:T(128)S(6)} %and.60), kind=kLoop, calls=%fused_computation.89 | loop fusion | flops 56 | bytes 72 | tf_op jit(solution)/shard_map/eq | solution.py:72
  8.2 0.9 %slice_bitcast_fusion.9 = (bf16[128,128]{1,0:T(8,128)(2,1)S(1)}, bf16[128,128]{1,0:T(8,128)(2,1)S(1)}, bf16[128,128]{1,0:T(8,128)(2,1)S(1)}, bf16[128,128]{1,0:T...) fusion(bf16[1,8,128,128]{3,2,1,0:T(8,128)(2,1)} %param.6), kind=kLoop, calls=%fused_computation.70 | loop fusion | bytes 524288 | tf_op jit(solution)/shard_map/jit(_where)/broadcast_in_dim | solution.py:75
  9.3 1.6 %collective-permute-start.3 = (bf16[2,128,128]{2,1,0:T(8,128)(2,1)S(1)}, bf16[2,128,128]{2,1,0:T(8,128)(2,1)S(1)}, u32[]{:S(2)}, u32[]{:S(2)}) collective-permute-start(bf16[2,128,128]{2,1,0:T(8,128)(2,1)S(1)} %get-tuple-element.32), channel_id=1, source_target_pairs={{0,2},{2,0},{4,6},{6,4},{8,10},{10,8},{12,14},{14,12},{16,18},{18,... | collective-permute-start | bytes 196616 | tf_op jit(solution)/shard_map/ppermute | solution.py:28
  10.9 1.5 %collective-permute-start.4 = (bf16[2,128,128]{2,1,0:T(8,128)(2,1)S(1)}, bf16[2,128,128]{2,1,0:T(8,128)(2,1)S(1)}, u32[]{:S(2)}, u32[]{:S(2)}) collective-permute-start(bf16[2,128,128]{2,1,0:T(8,128)(2,1)S(1)} %get-tuple-element.31), channel_id=1, source_target_pairs={{0,4},{2,6},{4,0},{6,2},{8,12},{10,14},{12,8},{14,10},{16,20},{18,... | collective-permute-start | bytes 196616 | tf_op jit(solution)/shard_map/ppermute | solution.py:28
  12.9 0.7 %collective-permute-done.3 = bf16[2,128,128]{2,1,0:T(8,128)(2,1)S(1)} collective-permute-done((bf16[2,128,128]{2,1,0:T(8,128)(2,1)S(1)}, bf16[2,128,128]{2,1,0:T(8,128)(2,1)S(1)}, u32[]{:S(2)}, u32[]{:S(2)}) %collective-permute-start.3) | collective-permute-done | bytes 65568 | tf_op jit(solution)/shard_map/ppermute | solution.py:28
  13.6 2.2 %collective-permute-done.4 = bf16[2,128,128]{2,1,0:T(8,128)(2,1)S(1)} collective-permute-done((bf16[2,128,128]{2,1,0:T(8,128)(2,1)S(1)}, bf16[2,128,128]{2,1,0:T(8,128)(2,1)S(1)}, u32[]{:S(2)}, u32[]{:S(2)}) %collective-permute-start.4) | collective-permute-done | bytes 65568 | tf_op jit(solution)/shard_map/ppermute | solution.py:28
  15.8 0.5 collective-permute-start.11
  16.4 1.8 %collective-permute-done.5 = bf16[2,128,128]{2,1,0:T(8,128)(2,1)S(1)} collective-permute-done((bf16[2,128,128]{2,1,0:T(8,128)(2,1)S(1)}, bf16[2,128,128]{2,1,0:T(8,128)(2,1)S(1)}, u32[]{:S(2)}, u32[]{:S(2)}) %collective-permute-start.5) | collective-permute-done | bytes 65568 | tf_op jit(solution)/shard_map/ppermute | solution.py:28
  18.2 0.5 collective-permute-start.12
  18.7 2.2 %all-gather = bf16[16,128,128]{2,1,0:T(8,128)(2,1)S(1)} all-gather(bf16[8,128,128]{2,1,0:T(8,128)(2,1)S(1)} %pad_maximum_fusion.1), channel_id=2, replica_groups=mesh['blk'=16,'rep'=2] {'rep'}, dimensions={0}, use_global_device_ids=true | all-gather | bytes 786432 | tf_op jit(solution)/shard_map/all_gather | solution.py:79
  21.1 1.6 %collective-permute-start.13 = (bf16[128,512]{1,0:T(8,128)(2,1)S(1)}, bf16[128,512]{1,0:T(8,128)(2,1)S(1)}, u32[]{:S(2)}, u32[]{:S(2)}) collective-permute-start(bf16[128,512]{1,0:T(8,128)(2,1)S(1)} %constant_dynamic-slice_fusion), channel_id=1, source_target_pairs={{0,6},{2,4},{4,2},{6,0},{8,14},{10,12},{12,10},{14,8},{16,22},{18,... | collective-permute-start | bytes 393224 | tf_op jit(solution)/shard_map/ppermute | solution.py:28
  22.6 1.5 %convolution_convert_fusion = bf16[512,512]{1,0:T(8,128)(2,1)S(1)} fusion(bf16[512,512]{1,0:T(8,128)(2,1)S(1)} %maximum_maximum_fusion, bf16[128,512]{1,0:T(8,128)(2,1)S(1)} %collective-permute-done.2, bf16[128,512]{1,0:T(8,128)(2,1)} %collective-permute-done.1, bf16[128,512]{1,0:T(8,128)(2,1)} %collective-permute-done, ...), kind=kOutput, calls=%fused_computation.1 | convolution fusion | flops 270794752 | bytes 1572864 | tf_op jit(solution)/shard_map/dot_general | solution.py:52
  24.2 1.6 %collective-permute-start.6 = (bf16[128,512]{1,0:T(8,128)(2,1)S(1)}, bf16[128,512]{1,0:T(8,128)(2,1)S(1)}, u32[]{:S(2)}, u32[]{:S(2)}) collective-permute-start(bf16[128,512]{1,0:T(8,128)(2,1)S(1)} %pad_maximum_fusion.3), channel_id=1, source_target_pairs={{0,2},{2,0},{4,6},{6,4},{8,10},{10,8},{12,14},{14,12},{16,18},{18,... | collective-permute-start | bytes 393224 | tf_op jit(solution)/shard_map/ppermute | solution.py:28
  25.8 0.6 %collective-permute-start.7 = (bf16[128,512]{1,0:T(8,128)(2,1)S(1)}, bf16[128,512]{1,0:T(8,128)(2,1)S(1)}, u32[]{:S(2)}, u32[]{:S(2)}) collective-permute-start(bf16[128,512]{1,0:T(8,128)(2,1)S(1)} %pad_maximum_fusion.4), channel_id=1, source_target_pairs={{0,4},{2,6},{4,0},{6,2},{8,12},{10,14},{12,8},{14,10},{16,20},{18,... | collective-permute-start | bytes 393224 | tf_op jit(solution)/shard_map/ppermute | solution.py:28
  26.4 1.6 %collective-permute-start.8 = (bf16[128,512]{1,0:T(8,128)(2,1)S(1)}, bf16[128,512]{1,0:T(8,128)(2,1)S(1)}, u32[]{:S(2)}, u32[]{:S(2)}) collective-permute-start(bf16[128,512]{1,0:T(8,128)(2,1)S(1)} %pad_maximum_fusion.5), channel_id=1, source_target_pairs={{0,6},{2,4},{4,2},{6,0},{8,14},{10,12},{12,10},{14,8},{16,22},{18,... | collective-permute-start | bytes 393224 | tf_op jit(solution)/shard_map/ppermute | solution.py:28
  28.9 0.5 collective-permute-start.16
  29.4 2.4 %collective-permute-start.17 = (bf16[512,128]{1,0:T(8,128)(2,1)S(1)}, bf16[512,128]{1,0:T(8,128)(2,1)S(1)}, u32[]{:S(2)}, u32[]{:S(2)}) collective-permute-start(bf16[512,128]{1,0:T(8,128)(2,1)S(1)} %get-tuple-element.5), channel_id=1, source_target_pairs={{0,16},{2,18},{4,20},{6,22},{8,24},{10,26},{12,28},{14,30},{16,0},... | collective-permute-start | bytes 393224 | tf_op jit(solution)/shard_map/ppermute | solution.py:32
  31.8 1.6 %collective-permute-start.18 = (bf16[512,128]{1,0:T(8,128)(2,1)S(1)}, bf16[512,128]{1,0:T(8,128)(2,1)S(1)}, u32[]{:S(2)}, u32[]{:S(2)}) collective-permute-start(bf16[512,128]{1,0:T(8,128)(2,1)S(1)} %get-tuple-element.4), channel_id=1, source_target_pairs={{0,24},{2,26},{4,28},{6,30},{8,16},{10,18},{12,20},{14,22},{16,8},... | collective-permute-start | bytes 393224 | tf_op jit(solution)/shard_map/ppermute | solution.py:32
  33.9 2.0 %all_gather.11 = bf16[256,512]{1,0:T(8,128)(2,1)S(1)} all-gather(bf16[128,512]{1,0:T(8,128)(2,1)S(1)} %fusion.17), channel_id=1, replica_groups=mesh['blk'=16,'rep'=2] {'rep'}, dimensions={0}, use_global_device_ids=true | all-gather | bytes 393216 | tf_op jit(solution)/shard_map/all_gather | solution.py:112
  36.6 0.5 collective-permute-start.14
  37.2 4.1 %collective-permute-done.17 = bf16[512,128]{1,0:T(8,128)(2,1)S(1)} collective-permute-done((bf16[512,128]{1,0:T(8,128)(2,1)S(1)}, bf16[512,128]{1,0:T(8,128)(2,1)S(1)}, u32[]{:S(2)}, u32[]{:S(2)}) %collective-permute-start.17) | collective-permute-done | bytes 131104 | tf_op jit(solution)/shard_map/ppermute | solution.py:32
  41.9 1.5 %collective-permute-start.9 = (bf16[256,512]{1,0:T(8,128)(2,1)S(1)}, bf16[256,512]{1,0:T(8,128)(2,1)S(1)}, u32[]{:S(2)}, u32[]{:S(2)}) collective-permute-start(bf16[256,512]{1,0:T(8,128)(2,1)S(1)} %pad_maximum_fusion.2), channel_id=1, source_target_pairs={{0,2},{2,0},{4,6},{6,4},{8,10},{10,8},{12,14},{14,12},{16,18},{18,... | collective-permute-start | bytes 786440 | tf_op jit(solution)/shard_map/ppermute | solution.py:28
  43.4 1.8 %collective-permute-start.15 = (bf16[64,512]{1,0:T(8,128)(2,1)S(1)}, bf16[64,512]{1,0:T(8,128)(2,1)S(1)}, u32[]{:S(2)}, u32[]{:S(2)}) collective-permute-start(bf16[64,512]{1,0:T(8,128)(2,1)S(1)} %fusion.19), channel_id=1, source_target_pairs={{0,16},{2,18},{4,20},{6,22},{8,24},{10,26},{12,28},{14,30},{16,0},... | collective-permute-start | bytes 196616 | tf_op jit(solution)/shard_map/ppermute | solution.py:32
  45.2 1.1 %select_convert_fusion = bf16[128,512]{1,0:T(8,128)(2,1)} fusion(bf16[128,512]{1,0:T(8,128)(2,1)S(1)} %collective-permute-done.19, bf16[128,1024]{1,0:T(8,128)(2,1)S(1)} %copy-done.1, s32[]{:T(128)S(6)} %select_n.213, bf16[512,128]{1,0:T(8,128)(2,1)S(1)} %fusion.14, bf16[2,512,1024]{2,1,0:T(8,128)(2,1)S(1)} %bitcast.108, s32[]{:T(128)S(6)} %select_n.278, ...), kind=kOutput, calls=%fused_computation.29 | convolution fusion | flops 67567616 | bytes 1048588 | tf_op jit(solution)/shard_map/dot_general | solution.py:52
  46.3 4.3 %collective-permute-done.9 = bf16[256,512]{1,0:T(8,128)(2,1)S(1)} collective-permute-done((bf16[256,512]{1,0:T(8,128)(2,1)S(1)}, bf16[256,512]{1,0:T(8,128)(2,1)S(1)}, u32[]{:S(2)}, u32[]{:S(2)}) %collective-permute-start.9) | collective-permute-done | bytes 262176 | tf_op jit(solution)/shard_map/ppermute | solution.py:28
  50.7 1.4 %collective-permute-start.10 = (bf16[128,512]{1,0:T(8,128)(2,1)S(1)}, bf16[128,512]{1,0:T(8,128)(2,1)S(1)}, u32[]{:S(2)}, u32[]{:S(2)}) collective-permute-start(bf16[128,512]{1,0:T(8,128)(2,1)S(1)} %add_convert_fusion.1), channel_id=1, source_target_pairs={{0,4},{2,6},{4,0},{6,2},{8,12},{10,14},{12,8},{14,10},{16,20},{18,... | collective-permute-start | bytes 393224 | tf_op jit(solution)/shard_map/ppermute | solution.py:28
  52.1 0.7 %fusion.20 = f32[64,512]{1,0:T(8,128)} fusion(bf16[64,512]{1,0:T(8,128)(2,1)S(1)} %collective-permute-done.15, bf16[128,512]{1,0:T(8,128)(2,1)S(1)} %collective-permute-done.14, bf16[4,64,512]{2,1,0:T(8,128)(2,1)S(1)} %bitcast.120, s32[]{:T(128)S(6)} %select_n.270), kind=kLoop, calls=%fused_computation.41 | loop fusion | flops 163840 | bytes 327684 | tf_op jit(solution)/shard_map/add | solution.py:42
  52.8 3.1 %collective-permute-done.10 = bf16[128,512]{1,0:T(8,128)(2,1)S(1)} collective-permute-done((bf16[128,512]{1,0:T(8,128)(2,1)S(1)}, bf16[128,512]{1,0:T(8,128)(2,1)S(1)}, u32[]{:S(2)}, u32[]{:S(2)}) %collective-permute-start.10) | collective-permute-done | bytes 131104 | tf_op jit(solution)/shard_map/ppermute | solution.py:28
  55.9 0.7 %add_convert_fusion = bf16[128,512]{1,0:T(8,128)(2,1)} fusion(bf16[128,512]{1,0:T(8,128)(2,1)S(1)} %collective-permute-done.10, bf16[256,512]{1,0:T(8,128)(2,1)S(1)} %collective-permute-done.9, bf16[512,512]{1,0:T(8,128)(2,1)S(1)} %convolution_convert_fusion.1), kind=kLoop, calls=%fused_computation.30 | loop fusion | flops 393216 | bytes 524288 | tf_op jit(solution)/shard_map/convert_element_type | solution.py:125
  (56 shorter events, 4.0 us)
Async XLA Ops:
  0.6 12.2 %copy-start = (bf16[1024,1024]{1,0:T(8,128)(2,1)S(1)}, bf16[1024,1024]{1,0:T(8,128)(2,1)}, u32[]{:S(2)}) copy-start(bf16[1024,1024]{1,0:T(8,128)(2,1)} %param.8) | copy-start | bytes 6291460
  0.6 12.3 %copy-start.2 = (bf16[128,1024]{1,0:T(8,128)(2,1)S(1)}, bf16[128,1024]{1,0:T(8,128)(2,1)}, u32[]{:S(2)}) copy-start(bf16[128,1024]{1,0:T(8,128)(2,1)} %param.9) | copy-start | bytes 786436
  1.7 19.3 %collective-permute-start = (bf16[128,512]{1,0:T(8,128)(2,1)S(1)}, bf16[128,512]{1,0:T(8,128)(2,1)}, u32[]{:S(2)}, u32[]{:S(2)}) collective-permute-start(bf16[128,512]{1,0:T(8,128)(2,1)S(1)} %dynamic-slice_maximum_fusion), channel_id=1, source_target_pairs={{0,8},{2,10},{4,12},{6,14},{8,0},{10,2},{12,4},{14,6},{16,24},{18,... | collective-permute-start | bytes 393224 | tf_op jit(solution)/shard_map/ppermute | solution.py:32
  4.8 17.8 %collective-permute-start.1 = (bf16[128,512]{1,0:T(8,128)(2,1)S(1)}, bf16[128,512]{1,0:T(8,128)(2,1)}, u32[]{:S(2)}, u32[]{:S(2)}) collective-permute-start(bf16[128,512]{1,0:T(8,128)(2,1)S(1)} %dynamic-slice_maximum_fusion), channel_id=1, source_target_pairs={{0,16},{2,18},{4,20},{6,22},{8,24},{10,26},{12,28},{14,30},{16,0},... | collective-permute-start | bytes 393224 | tf_op jit(solution)/shard_map/ppermute | solution.py:32
  9.3 4.3 %collective-permute-start.3 = (bf16[2,128,128]{2,1,0:T(8,128)(2,1)S(1)}, bf16[2,128,128]{2,1,0:T(8,128)(2,1)S(1)}, u32[]{:S(2)}, u32[]{:S(2)}) collective-permute-start(bf16[2,128,128]{2,1,0:T(8,128)(2,1)S(1)} %get-tuple-element.32), channel_id=1, source_target_pairs={{0,2},{2,0},{4,6},{6,4},{8,10},{10,8},{12,14},{14,12},{16,18},{18,... | collective-permute-start | bytes 196616 | tf_op jit(solution)/shard_map/ppermute | solution.py:28
  10.9 5.0 %collective-permute-start.4 = (bf16[2,128,128]{2,1,0:T(8,128)(2,1)S(1)}, bf16[2,128,128]{2,1,0:T(8,128)(2,1)S(1)}, u32[]{:S(2)}, u32[]{:S(2)}) collective-permute-start(bf16[2,128,128]{2,1,0:T(8,128)(2,1)S(1)} %get-tuple-element.31), channel_id=1, source_target_pairs={{0,4},{2,6},{4,0},{6,2},{8,12},{10,14},{12,8},{14,10},{16,20},{18,... | collective-permute-start | bytes 196616 | tf_op jit(solution)/shard_map/ppermute | solution.py:28
  12.4 5.8 %collective-permute-start.5 = (bf16[2,128,128]{2,1,0:T(8,128)(2,1)S(1)}, bf16[2,128,128]{2,1,0:T(8,128)(2,1)S(1)}, u32[]{:S(2)}, u32[]{:S(2)}) collective-permute-start(bf16[2,128,128]{2,1,0:T(8,128)(2,1)S(1)} %get-tuple-element.30), channel_id=1, source_target_pairs={{0,6},{2,4},{4,2},{6,0},{8,14},{10,12},{12,10},{14,8},{16,22},{18,... | collective-permute-start | bytes 196616 | tf_op jit(solution)/shard_map/ppermute | solution.py:28
  13.6 9.0 %collective-permute-start.2 = (bf16[128,512]{1,0:T(8,128)(2,1)S(1)}, bf16[128,512]{1,0:T(8,128)(2,1)S(1)}, u32[]{:S(2)}, u32[]{:S(2)}) collective-permute-start(bf16[128,512]{1,0:T(8,128)(2,1)S(1)} %dynamic-slice_maximum_fusion), channel_id=1, source_target_pairs={{0,24},{2,26},{4,28},{6,30},{8,16},{10,18},{12,20},{14,22},{16,8},... | collective-permute-start | bytes 393224 | tf_op jit(solution)/shard_map/ppermute | solution.py:32
  15.8 10.6 %collective-permute-start.11 = (bf16[128,512]{1,0:T(8,128)(2,1)S(1)}, bf16[128,512]{1,0:T(8,128)(2,1)S(1)}, u32[]{:S(2)}, u32[]{:S(2)}) collective-permute-start(bf16[128,512]{1,0:T(8,128)(2,1)S(1)} %constant_dynamic-slice_fusion), channel_id=1, source_target_pairs={{0,2},{2,0},{4,6},{6,4},{8,10},{10,8},{12,14},{14,12},{16,18},{18,... | collective-permute-start | bytes 393224 | tf_op jit(solution)/shard_map/ppermute | solution.py:28
  18.2 9.8 %collective-permute-start.12 = (bf16[128,512]{1,0:T(8,128)(2,1)S(1)}, bf16[128,512]{1,0:T(8,128)(2,1)S(1)}, u32[]{:S(2)}, u32[]{:S(2)}) collective-permute-start(bf16[128,512]{1,0:T(8,128)(2,1)S(1)} %constant_dynamic-slice_fusion), channel_id=1, source_target_pairs={{0,4},{2,6},{4,0},{6,2},{8,12},{10,14},{12,8},{14,10},{16,20},{18,... | collective-permute-start | bytes 393224 | tf_op jit(solution)/shard_map/ppermute | solution.py:28
  21.1 7.3 %collective-permute-start.13 = (bf16[128,512]{1,0:T(8,128)(2,1)S(1)}, bf16[128,512]{1,0:T(8,128)(2,1)S(1)}, u32[]{:S(2)}, u32[]{:S(2)}) collective-permute-start(bf16[128,512]{1,0:T(8,128)(2,1)S(1)} %constant_dynamic-slice_fusion), channel_id=1, source_target_pairs={{0,6},{2,4},{4,2},{6,0},{8,14},{10,12},{12,10},{14,8},{16,22},{18,... | collective-permute-start | bytes 393224 | tf_op jit(solution)/shard_map/ppermute | solution.py:28
  24.2 7.6 %collective-permute-start.6 = (bf16[128,512]{1,0:T(8,128)(2,1)S(1)}, bf16[128,512]{1,0:T(8,128)(2,1)S(1)}, u32[]{:S(2)}, u32[]{:S(2)}) collective-permute-start(bf16[128,512]{1,0:T(8,128)(2,1)S(1)} %pad_maximum_fusion.3), channel_id=1, source_target_pairs={{0,2},{2,0},{4,6},{6,4},{8,10},{10,8},{12,14},{14,12},{16,18},{18,... | collective-permute-start | bytes 393224 | tf_op jit(solution)/shard_map/ppermute | solution.py:28
  25.8 8.0 %collective-permute-start.7 = (bf16[128,512]{1,0:T(8,128)(2,1)S(1)}, bf16[128,512]{1,0:T(8,128)(2,1)S(1)}, u32[]{:S(2)}, u32[]{:S(2)}) collective-permute-start(bf16[128,512]{1,0:T(8,128)(2,1)S(1)} %pad_maximum_fusion.4), channel_id=1, source_target_pairs={{0,4},{2,6},{4,0},{6,2},{8,12},{10,14},{12,8},{14,10},{16,20},{18,... | collective-permute-start | bytes 393224 | tf_op jit(solution)/shard_map/ppermute | solution.py:28
  26.4 7.4 %collective-permute-start.8 = (bf16[128,512]{1,0:T(8,128)(2,1)S(1)}, bf16[128,512]{1,0:T(8,128)(2,1)S(1)}, u32[]{:S(2)}, u32[]{:S(2)}) collective-permute-start(bf16[128,512]{1,0:T(8,128)(2,1)S(1)} %pad_maximum_fusion.5), channel_id=1, source_target_pairs={{0,6},{2,4},{4,2},{6,0},{8,14},{10,12},{12,10},{14,8},{16,22},{18,... | collective-permute-start | bytes 393224 | tf_op jit(solution)/shard_map/ppermute | solution.py:28
  28.9 8.2 %collective-permute-start.16 = (bf16[512,128]{1,0:T(8,128)(2,1)S(1)}, bf16[512,128]{1,0:T(8,128)(2,1)S(1)}, u32[]{:S(2)}, u32[]{:S(2)}) collective-permute-start(bf16[512,128]{1,0:T(8,128)(2,1)S(1)} %get-tuple-element.3), channel_id=1, source_target_pairs={{0,8},{2,10},{4,12},{6,14},{8,0},{10,2},{12,4},{14,6},{16,24},{18,... | collective-permute-start | bytes 393224 | tf_op jit(solution)/shard_map/ppermute | solution.py:32
  29.4 11.8 %collective-permute-start.17 = (bf16[512,128]{1,0:T(8,128)(2,1)S(1)}, bf16[512,128]{1,0:T(8,128)(2,1)S(1)}, u32[]{:S(2)}, u32[]{:S(2)}) collective-permute-start(bf16[512,128]{1,0:T(8,128)(2,1)S(1)} %get-tuple-element.5), channel_id=1, source_target_pairs={{0,16},{2,18},{4,20},{6,22},{8,24},{10,26},{12,28},{14,30},{16,0},... | collective-permute-start | bytes 393224 | tf_op jit(solution)/shard_map/ppermute | solution.py:32
  31.8 9.4 %collective-permute-start.18 = (bf16[512,128]{1,0:T(8,128)(2,1)S(1)}, bf16[512,128]{1,0:T(8,128)(2,1)S(1)}, u32[]{:S(2)}, u32[]{:S(2)}) collective-permute-start(bf16[512,128]{1,0:T(8,128)(2,1)S(1)} %get-tuple-element.4), channel_id=1, source_target_pairs={{0,24},{2,26},{4,28},{6,30},{8,16},{10,18},{12,20},{14,22},{16,8},... | collective-permute-start | bytes 393224 | tf_op jit(solution)/shard_map/ppermute | solution.py:32
  36.6 8.7 %copy-start.1 = (bf16[128,1024]{1,0:T(8,128)(2,1)S(1)}, bf16[128,1024]{1,0:T(8,128)(2,1)}, u32[]{:S(2)}) copy-start(bf16[128,1024]{1,0:T(8,128)(2,1)} %param.5) | copy-start | bytes 786436
  36.6 6.8 %collective-permute-start.14 = (bf16[128,512]{1,0:T(8,128)(2,1)S(1)}, bf16[128,512]{1,0:T(8,128)(2,1)S(1)}, u32[]{:S(2)}, u32[]{:S(2)}) collective-permute-start(bf16[128,512]{1,0:T(8,128)(2,1)S(1)} %pad_maximum_fusion.6), channel_id=1, source_target_pairs={{0,8},{2,10},{4,12},{6,14},{8,0},{10,2},{12,4},{14,6},{16,24},{18,... | collective-permute-start | bytes 393224 | tf_op jit(solution)/shard_map/ppermute | solution.py:32
  41.8 3.5 %collective-permute-start.19 = (bf16[128,512]{1,0:T(8,128)(2,1)S(1)}, bf16[128,512]{1,0:T(8,128)(2,1)S(1)}, u32[]{:S(2)}, u32[]{:S(2)}) collective-permute-start(bf16[128,512]{1,0:T(8,128)(2,1)S(1)} %convolution_convert_fusion.2), channel_id=1, source_target_pairs={{0,1},{1,0},{2,3},{3,2},{4,5},{5,4},{6,7},{7,6},{8,9},{9,8},{10,11... | collective-permute-start | bytes 393224 | tf_op jit(solution)/shard_map/ppermute | solution.py:49
  41.9 8.8 %collective-permute-start.9 = (bf16[256,512]{1,0:T(8,128)(2,1)S(1)}, bf16[256,512]{1,0:T(8,128)(2,1)S(1)}, u32[]{:S(2)}, u32[]{:S(2)}) collective-permute-start(bf16[256,512]{1,0:T(8,128)(2,1)S(1)} %pad_maximum_fusion.2), channel_id=1, source_target_pairs={{0,2},{2,0},{4,6},{6,4},{8,10},{10,8},{12,14},{14,12},{16,18},{18,... | collective-permute-start | bytes 786440 | tf_op jit(solution)/shard_map/ppermute | solution.py:28
  43.4 8.7 %collective-permute-start.15 = (bf16[64,512]{1,0:T(8,128)(2,1)S(1)}, bf16[64,512]{1,0:T(8,128)(2,1)S(1)}, u32[]{:S(2)}, u32[]{:S(2)}) collective-permute-start(bf16[64,512]{1,0:T(8,128)(2,1)S(1)} %fusion.19), channel_id=1, source_target_pairs={{0,16},{2,18},{4,20},{6,22},{8,24},{10,26},{12,28},{14,30},{16,0},... | collective-permute-start | bytes 196616 | tf_op jit(solution)/shard_map/ppermute | solution.py:32
  50.7 5.2 %collective-permute-start.10 = (bf16[128,512]{1,0:T(8,128)(2,1)S(1)}, bf16[128,512]{1,0:T(8,128)(2,1)S(1)}, u32[]{:S(2)}, u32[]{:S(2)}) collective-permute-start(bf16[128,512]{1,0:T(8,128)(2,1)S(1)} %add_convert_fusion.1), channel_id=1, source_target_pairs={{0,4},{2,6},{4,0},{6,2},{8,12},{10,14},{12,8},{14,10},{16,20},{18,... | collective-permute-start | bytes 393224 | tf_op jit(solution)/shard_map/ppermute | solution.py:28

commit v24 on v20

--- a/solution.py
+++ b/solution.py
@@ -34,16 +34,18 @@
     def halved(parts, move):
         parts = dict(enumerate(parts))
         size = parts[0].shape[0]
+        arrived = []
         for bit in rising:
             keys = [k for k in parts if not k & bit]
             sent = jnp.concatenate([parts[k ^ bit].astype(bf16) for k in keys], 0)
             got = move(sent, bit)
+            arrived.append(got)
             parts = {
                 k: parts[k].astype(jnp.float32)
                 + got[n * size : (n + 1) * size].astype(jnp.float32)
                 for n, k in enumerate(keys)
             }
-        return parts[0]
+        return parts[0], arrived[0]
 
     def to_other(value):
         return lax.ppermute(value, "rep", [(0, 1), (1, 0)])
@@ -116,15 +118,16 @@
     out_part = dot(mixed_cols, w_share, ((0,), (0,)))
     weight_part = after(dot(mixed_cols, grad_stack, ((1,), (0,))), out_part)
     by_outer = weight_part.reshape(side, rows_here, cols_here)
-    grad_weight = halved(
+    grad_weight, _ = halved(
         [lax.dynamic_index_in_dim(by_outer, outer_pos ^ t, 0, keepdims=False) for t in turns],
         along_outer,
     )
-    out_part = halved(
+    out_part, out_first = halved(
         [out_part[t * tile_size : (t + 1) * tile_size] for t in turns], along_inner
-    ).astype(bf16)
+    )
+    out_part = out_part.astype(bf16)
 
-    back = after(back, weight_part).astype(bf16)
+    back = after(back, out_first).astype(bf16)
     w_rows = w_out.reshape(rep_count, cols_here, feature_width)
     if rep_count == 2:
         w_mine = columns_of(lax.dynamic_index_in_dim(w_rows, rep_pos, 0, keepdims=False), rep_pos)

time: 52.1 us -> 60.7 us (1.17)
  waiting for transfers between devices: 12.4 us -> 23.5 us
  starting transfers between devices: 25.2 us -> 22.7 us
    ppermute x11, waiting for transfers between devices: 3.25 us -> 10.1 us  [along_inner(): return lax.ppermute(value, 'blk', pairs) if turn else value]
    ppermute x8, waiting for transfers between devices: 9.14 us -> 12.9 us  [along_outer(): return lax.ppermute(value, 'blk', pairs) if turn else value]
    ppermute x11, starting transfers between devices: 12.8 us -> 11.3 us  [along_inner(): return lax.ppermute(value, 'blk', pairs) if turn else value]
    ppermute x8, starting transfers between devices: 12.3 us -> 11.3 us  [along_outer(): return lax.ppermute(value, 'blk', pairs) if turn else value]
    ppermute x1, waiting for transfers between devices: 0.01 us -> 0.62 us  [to_other(): return lax.ppermute(value, 'rep', [(0, 1), (1, 0)])]
  transfers between devices with their start and end apart: 20 -> 20, of which waited for: 7 -> 11; matrix products, arithmetic and copies ran while one was open for 14% -> 10% of each run, Pallas kernels for 0% -> 0%
where the time goes in v24:
time: 60.7 us; the launch traced here: 60.5 us
  waiting for transfers between devices  23.5 us (39%)
  starting transfers between devices  22.7 us (37%)
  blocking collectives  4.18 us (7%)
  matrix products  4.05 us (7%)
  other arithmetic  3.86 us (6%)
  local copies, waits for them, and re-layouts  1.22 us (2%)
  between operations  0.94 us (2%)
    ppermute x8, waiting for transfers between devices, along_outer(): return lax.ppermute(value, 'blk', pairs) if turn else value  12.9 us
    ppermute x11, starting transfers between devices, along_inner(): return lax.ppermute(value, 'blk', pairs) if turn else value  11.3 us
    ppermute x8, starting transfers between devices, along_outer(): return lax.ppermute(value, 'blk', pairs) if turn else value  11.3 us
    ppermute x11, waiting for transfers between devices, along_inner(): return lax.ppermute(value, 'blk', pairs) if turn else value  10.1 us
    dot_general x6, matrix products, dot(): lax.dot_general(lhs, rhs, (dims, ((), ())), preferred_element_type=jnp.fl...  4.05 us
    all_gather x1, blocking collectives, shards(): everyone = lax.all_gather(jnp.concatenate(arrived, 0), 'rep', axis=0)  2.18 us
    all_gather x1, blocking collectives, shards(): lax.all_gather(mixed_cols.astype(bf16), 'rep', axis=0, tiled=True)  1.99 us
  transfers between devices with their start and end apart: 20, of which 11 were waited for; matrix products, arithmetic and copies ran while one was open for 10% of the time, Pallas kernels for 0%

profile of v24, /device:TPU:0, one launch (start us, length us, event | category | flops | bytes accessed | tf_op | source)
XLA Modules:
  0.0 60.5 jit_solution(7188307479018797668)
XLA Ops:
  0.7 1.1 %dynamic-slice_maximum_fusion = bf16[128,512]{1,0:T(8,128)(2,1)S(1)} fusion(bf16[128,1024]{1,0:T(8,128)(2,1)} %param.5, s32[]{:T(128)S(6)} %select_n.214), kind=kLoop, calls=%fused_computation.48 | loop fusion | flops 262144 | bytes 262148 | tf_op jit(solution)/shard_map/max | solution.py:68
  1.7 3.1 %collective-permute-start = (bf16[128,512]{1,0:T(8,128)(2,1)S(1)}, bf16[128,512]{1,0:T(8,128)(2,1)}, u32[]{:S(2)}, u32[]{:S(2)}) collective-permute-start(bf16[128,512]{1,0:T(8,128)(2,1)S(1)} %dynamic-slice_maximum_fusion), channel_id=1, source_target_pairs={{0,8},{2,10},{4,12},{6,14},{8,0},{10,2},{12,4},{14,6},{16,24},{18,... | collective-permute-start | bytes 393224 | tf_op jit(solution)/shard_map/ppermute | solution.py:32
  4.8 2.6 %collective-permute-start.1 = (bf16[128,512]{1,0:T(8,128)(2,1)S(1)}, bf16[128,512]{1,0:T(8,128)(2,1)}, u32[]{:S(2)}, u32[]{:S(2)}) collective-permute-start(bf16[128,512]{1,0:T(8,128)(2,1)S(1)} %dynamic-slice_maximum_fusion), channel_id=1, source_target_pairs={{0,16},{2,18},{4,20},{6,22},{8,24},{10,26},{12,28},{14,30},{16,0},... | collective-permute-start | bytes 393224 | tf_op jit(solution)/shard_map/ppermute | solution.py:32
  7.4 0.7 %add_bitcast_fusion = s32[8]{0:T(128)S(1)} fusion(s32[1,8]{1,0:T(1,128)} %param.7, s32[]{:T(128)S(6)} %shift_right_arithmetic.54, s32[]{:T(128)S(6)} %and.60), kind=kLoop, calls=%fused_computation.94 | loop fusion | flops 56 | bytes 72 | tf_op jit(solution)/shard_map/eq | solution.py:74
  8.2 0.9 %slice_bitcast_fusion.9 = (bf16[128,128]{1,0:T(8,128)(2,1)S(1)}, bf16[128,128]{1,0:T(8,128)(2,1)S(1)}, bf16[128,128]{1,0:T(8,128)(2,1)S(1)}, bf16[128,128]{1,0:T...) fusion(bf16[1,8,128,128]{3,2,1,0:T(8,128)(2,1)} %param.6), kind=kLoop, calls=%fused_computation.75 | loop fusion | bytes 524288 | tf_op jit(solution)/shard_map/jit(_where)/broadcast_in_dim | solution.py:77
  9.3 1.6 %collective-permute-start.3 = (bf16[2,128,128]{2,1,0:T(8,128)(2,1)S(1)}, bf16[2,128,128]{2,1,0:T(8,128)(2,1)S(1)}, u32[]{:S(2)}, u32[]{:S(2)}) collective-permute-start(bf16[2,128,128]{2,1,0:T(8,128)(2,1)S(1)} %get-tuple-element.32), channel_id=1, source_target_pairs={{0,2},{2,0},{4,6},{6,4},{8,10},{10,8},{12,14},{14,12},{16,18},{18,... | collective-permute-start | bytes 196616 | tf_op jit(solution)/shard_map/ppermute | solution.py:28
  10.9 1.5 %collective-permute-start.4 = (bf16[2,128,128]{2,1,0:T(8,128)(2,1)S(1)}, bf16[2,128,128]{2,1,0:T(8,128)(2,1)S(1)}, u32[]{:S(2)}, u32[]{:S(2)}) collective-permute-start(bf16[2,128,128]{2,1,0:T(8,128)(2,1)S(1)} %get-tuple-element.31), channel_id=1, source_target_pairs={{0,4},{2,6},{4,0},{6,2},{8,12},{10,14},{12,8},{14,10},{16,20},{18,... | collective-permute-start | bytes 196616 | tf_op jit(solution)/shard_map/ppermute | solution.py:28
  12.9 0.7 %collective-permute-done.3 = bf16[2,128,128]{2,1,0:T(8,128)(2,1)S(1)} collective-permute-done((bf16[2,128,128]{2,1,0:T(8,128)(2,1)S(1)}, bf16[2,128,128]{2,1,0:T(8,128)(2,1)S(1)}, u32[]{:S(2)}, u32[]{:S(2)}) %collective-permute-start.3) | collective-permute-done | bytes 65568 | tf_op jit(solution)/shard_map/ppermute | solution.py:28
  13.6 2.2 %collective-permute-done.4 = bf16[2,128,128]{2,1,0:T(8,128)(2,1)S(1)} collective-permute-done((bf16[2,128,128]{2,1,0:T(8,128)(2,1)S(1)}, bf16[2,128,128]{2,1,0:T(8,128)(2,1)S(1)}, u32[]{:S(2)}, u32[]{:S(2)}) %collective-permute-start.4) | collective-permute-done | bytes 65568 | tf_op jit(solution)/shard_map/ppermute | solution.py:28
  15.8 0.5 collective-permute-start.11
  16.4 1.8 %collective-permute-done.5 = bf16[2,128,128]{2,1,0:T(8,128)(2,1)S(1)} collective-permute-done((bf16[2,128,128]{2,1,0:T(8,128)(2,1)S(1)}, bf16[2,128,128]{2,1,0:T(8,128)(2,1)S(1)}, u32[]{:S(2)}, u32[]{:S(2)}) %collective-permute-start.5) | collective-permute-done | bytes 65568 | tf_op jit(solution)/shard_map/ppermute | solution.py:28
  18.7 2.2 %all-gather = bf16[16,128,128]{2,1,0:T(8,128)(2,1)S(1)} all-gather(bf16[8,128,128]{2,1,0:T(8,128)(2,1)S(1)} %pad_maximum_fusion.1), channel_id=2, replica_groups=mesh['blk'=16,'rep'=2] {'rep'}, dimensions={0}, use_global_device_ids=true | all-gather | bytes 786432 | tf_op jit(solution)/shard_map/all_gather | solution.py:81
  21.1 1.6 %collective-permute-start.13 = (bf16[128,512]{1,0:T(8,128)(2,1)S(1)}, bf16[128,512]{1,0:T(8,128)(2,1)S(1)}, u32[]{:S(2)}, u32[]{:S(2)}) collective-permute-start(bf16[128,512]{1,0:T(8,128)(2,1)S(1)} %constant_dynamic-slice_fusion), channel_id=1, source_target_pairs={{0,6},{2,4},{4,2},{6,0},{8,14},{10,12},{12,10},{14,8},{16,22},{18,... | collective-permute-start | bytes 393224 | tf_op jit(solution)/shard_map/ppermute | solution.py:28
  22.6 1.5 %convolution_convert_fusion = bf16[512,512]{1,0:T(8,128)(2,1)S(1)} fusion(bf16[512,512]{1,0:T(8,128)(2,1)S(1)} %maximum_maximum_fusion, bf16[128,512]{1,0:T(8,128)(2,1)S(1)} %collective-permute-done.2, bf16[128,512]{1,0:T(8,128)(2,1)} %collective-permute-done.1, bf16[128,512]{1,0:T(8,128)(2,1)} %collective-permute-done, ...), kind=kOutput, calls=%fused_computation.1 | convolution fusion | flops 270794752 | bytes 1572864 | tf_op jit(solution)/shard_map/dot_general | solution.py:54
  24.2 1.6 %collective-permute-start.6 = (bf16[128,512]{1,0:T(8,128)(2,1)S(1)}, bf16[128,512]{1,0:T(8,128)(2,1)S(1)}, u32[]{:S(2)}, u32[]{:S(2)}) collective-permute-start(bf16[128,512]{1,0:T(8,128)(2,1)S(1)} %pad_maximum_fusion.3), channel_id=1, source_target_pairs={{0,2},{2,0},{4,6},{6,4},{8,10},{10,8},{12,14},{14,12},{16,18},{18,... | collective-permute-start | bytes 393224 | tf_op jit(solution)/shard_map/ppermute | solution.py:28
  25.8 0.6 collective-permute-start.7
  26.4 1.6 %collective-permute-start.8 = (bf16[128,512]{1,0:T(8,128)(2,1)S(1)}, bf16[128,512]{1,0:T(8,128)(2,1)S(1)}, u32[]{:S(2)}, u32[]{:S(2)}) collective-permute-start(bf16[128,512]{1,0:T(8,128)(2,1)S(1)} %pad_maximum_fusion.5), channel_id=1, source_target_pairs={{0,6},{2,4},{4,2},{6,0},{8,14},{10,12},{12,10},{14,8},{16,22},{18,... | collective-permute-start | bytes 393224 | tf_op jit(solution)/shard_map/ppermute | solution.py:28
  28.8 2.4 %collective-permute-done.6 = bf16[128,512]{1,0:T(8,128)(2,1)S(1)} collective-permute-done((bf16[128,512]{1,0:T(8,128)(2,1)S(1)}, bf16[128,512]{1,0:T(8,128)(2,1)S(1)}, u32[]{:S(2)}, u32[]{:S(2)}) %collective-permute-start.6) | collective-permute-done | bytes 131104 | tf_op jit(solution)/shard_map/ppermute | solution.py:28
  31.2 2.6 %collective-permute-done.7 = bf16[128,512]{1,0:T(8,128)(2,1)S(1)} collective-permute-done((bf16[128,512]{1,0:T(8,128)(2,1)S(1)}, bf16[128,512]{1,0:T(8,128)(2,1)S(1)}, u32[]{:S(2)}, u32[]{:S(2)}) %collective-permute-start.7) | collective-permute-done | bytes 131104 | tf_op jit(solution)/shard_map/ppermute | solution.py:28
  33.9 2.0 %all_gather.11 = bf16[256,512]{1,0:T(8,128)(2,1)S(1)} all-gather(bf16[128,512]{1,0:T(8,128)(2,1)S(1)} %fusion.19), channel_id=1, replica_groups=mesh['blk'=16,'rep'=2] {'rep'}, dimensions={0}, use_global_device_ids=true | all-gather | bytes 393216 | tf_op jit(solution)/shard_map/all_gather | solution.py:114
  37.6 4.6 %collective-permute-done.14 = bf16[128,512]{1,0:T(8,128)(2,1)S(1)} collective-permute-done((bf16[128,512]{1,0:T(8,128)(2,1)S(1)}, bf16[128,512]{1,0:T(8,128)(2,1)S(1)}, u32[]{:S(2)}, u32[]{:S(2)}) %collective-permute-start.14) | collective-permute-done | bytes 131104 | tf_op jit(solution)/shard_map/ppermute | solution.py:32
  42.2 0.6 %collective-permute-start.15 = (bf16[64,512]{1,0:T(8,128)(2,1)S(1)}, bf16[64,512]{1,0:T(8,128)(2,1)S(1)}, u32[]{:S(2)}, u32[]{:S(2)}) collective-permute-start(bf16[64,512]{1,0:T(8,128)(2,1)S(1)} %fusion.22), channel_id=1, source_target_pairs={{0,16},{2,18},{4,20},{6,22},{8,24},{10,26},{12,28},{14,30},{16,0},... | collective-permute-start | bytes 196616 | tf_op jit(solution)/shard_map/ppermute | solution.py:32
  42.9 1.8 %collective-permute-start.16 = (bf16[512,128]{1,0:T(8,128)(2,1)S(1)}, bf16[512,128]{1,0:T(8,128)(2,1)S(1)}, u32[]{:S(2)}, u32[]{:S(2)}) collective-permute-start(bf16[512,128]{1,0:T(8,128)(2,1)S(1)} %get-tuple-element.3), channel_id=1, source_target_pairs={{0,8},{2,10},{4,12},{6,14},{8,0},{10,2},{12,4},{14,6},{16,24},{18,... | collective-permute-start | bytes 393224 | tf_op jit(solution)/shard_map/ppermute | solution.py:32
  44.7 1.1 %collective-permute-start.17 = (bf16[512,128]{1,0:T(8,128)(2,1)S(1)}, bf16[512,128]{1,0:T(8,128)(2,1)S(1)}, u32[]{:S(2)}, u32[]{:S(2)}) collective-permute-start(bf16[512,128]{1,0:T(8,128)(2,1)S(1)} %get-tuple-element.5), channel_id=1, source_target_pairs={{0,16},{2,18},{4,20},{6,22},{8,24},{10,26},{12,28},{14,30},{16,0},... | collective-permute-start | bytes 393224 | tf_op jit(solution)/shard_map/ppermute | solution.py:32
  45.8 1.6 %collective-permute-start.18 = (bf16[512,128]{1,0:T(8,128)(2,1)S(1)}, bf16[512,128]{1,0:T(8,128)(2,1)S(1)}, u32[]{:S(2)}, u32[]{:S(2)}) collective-permute-start(bf16[512,128]{1,0:T(8,128)(2,1)S(1)} %get-tuple-element.4), channel_id=1, source_target_pairs={{0,24},{2,26},{4,28},{6,30},{8,16},{10,18},{12,20},{14,22},{16,8},... | collective-permute-start | bytes 393224 | tf_op jit(solution)/shard_map/ppermute | solution.py:32
  47.4 1.4 %collective-permute-done.15 = bf16[64,512]{1,0:T(8,128)(2,1)S(1)} collective-permute-done((bf16[64,512]{1,0:T(8,128)(2,1)S(1)}, bf16[64,512]{1,0:T(8,128)(2,1)S(1)}, u32[]{:S(2)}, u32[]{:S(2)}) %collective-permute-start.15) | collective-permute-done | bytes 65568 | tf_op jit(solution)/shard_map/ppermute | solution.py:32
  48.8 0.7 %fusion.23 = f32[64,512]{1,0:T(8,128)} fusion(bf16[64,512]{1,0:T(8,128)(2,1)S(1)} %collective-permute-done.15, f32[4,64,512]{2,1,0:T(8,128)S(1)} %bitcast.122, s32[]{:T(128)S(6)} %select_n.271, bf16[128,512]{1,0:T(8,128)(2,1)S(1)} %collective-permute-done.14), kind=kLoop, calls=%fused_computation.44 | loop fusion | flops 131072 | bytes 393220 | tf_op jit(solution)/shard_map/add | solution.py:44
  49.5 1.1 %collective-permute-start.10 = (bf16[128,512]{1,0:T(8,128)(2,1)S(1)}, bf16[128,512]{1,0:T(8,128)(2,1)S(1)}, u32[]{:S(2)}, u32[]{:S(2)}) collective-permute-start(bf16[128,512]{1,0:T(8,128)(2,1)S(1)} %fusion.13), channel_id=1, source_target_pairs={{0,4},{2,6},{4,0},{6,2},{8,12},{10,14},{12,8},{14,10},{16,20},{18,... | collective-permute-start | bytes 393224 | tf_op jit(solution)/shard_map/ppermute | solution.py:28
  50.8 6.7 %collective-permute-done.17 = bf16[512,128]{1,0:T(8,128)(2,1)S(1)} collective-permute-done((bf16[512,128]{1,0:T(8,128)(2,1)S(1)}, bf16[512,128]{1,0:T(8,128)(2,1)S(1)}, u32[]{:S(2)}, u32[]{:S(2)}) %collective-permute-start.17) | collective-permute-done | bytes 131104 | tf_op jit(solution)/shard_map/ppermute | solution.py:32
  58.0 0.7 %fusion.15 = bf16[128,512]{1,0:T(8,128)(2,1)} fusion(f32[512,512]{1,0:T(8,128)S(1)} %get-tuple-element.60, bf16[128,512]{1,0:T(8,128)(2,1)S(1)} %collective-permute-done.10, bf16[256,512]{1,0:T(8,128)(2,1)S(1)} %collective-permute-done.9), kind=kLoop, calls=%fused_computation.24 | loop fusion | flops 327680 | bytes 655360 | tf_op jit(solution)/shard_map/convert_element_type | solution.py:128
  58.7 0.6 %collective-permute-done.19 = bf16[128,512]{1,0:T(8,128)(2,1)S(1)} collective-permute-done((bf16[128,512]{1,0:T(8,128)(2,1)S(1)}, bf16[128,512]{1,0:T(8,128)(2,1)S(1)}, u32[]{:S(2)}, u32[]{:S(2)}) %collective-permute-start.19) | collective-permute-done | bytes 131104 | tf_op jit(solution)/shard_map/ppermute | solution.py:51
  59.4 1.1 %select_convert_fusion = bf16[128,512]{1,0:T(8,128)(2,1)} fusion(bf16[128,512]{1,0:T(8,128)(2,1)S(1)} %collective-permute-done.19, bf16[128,1024]{1,0:T(8,128)(2,1)S(1)} %copy-done.1, s32[]{:T(128)S(6)} %select_n.214, bf16[512,128]{1,0:T(8,128)(2,1)S(1)} %fusion.16, bf16[2,512,1024]{2,1,0:T(8,128)(2,1)S(1)} %bitcast.110, s32[]{:T(128)S(6)} %select_n.279, ...), kind=kOutput, calls=%fused_computation.33 | convolution fusion | flops 67567616 | bytes 1048588 | tf_op jit(solution)/shard_map/dot_general | solution.py:54
  (56 shorter events, 5.2 us)
Async XLA Ops:
  0.6 12.2 %copy-start = (bf16[1024,1024]{1,0:T(8,128)(2,1)S(1)}, bf16[1024,1024]{1,0:T(8,128)(2,1)}, u32[]{:S(2)}) copy-start(bf16[1024,1024]{1,0:T(8,128)(2,1)} %param.8) | copy-start | bytes 6291460
  0.6 12.3 %copy-start.2 = (bf16[128,1024]{1,0:T(8,128)(2,1)S(1)}, bf16[128,1024]{1,0:T(8,128)(2,1)}, u32[]{:S(2)}) copy-start(bf16[128,1024]{1,0:T(8,128)(2,1)} %param.9) | copy-start | bytes 786436
  1.7 19.3 %collective-permute-start = (bf16[128,512]{1,0:T(8,128)(2,1)S(1)}, bf16[128,512]{1,0:T(8,128)(2,1)}, u32[]{:S(2)}, u32[]{:S(2)}) collective-permute-start(bf16[128,512]{1,0:T(8,128)(2,1)S(1)} %dynamic-slice_maximum_fusion), channel_id=1, source_target_pairs={{0,8},{2,10},{4,12},{6,14},{8,0},{10,2},{12,4},{14,6},{16,24},{18,... | collective-permute-start | bytes 393224 | tf_op jit(solution)/shard_map/ppermute | solution.py:32
  4.8 17.8 %collective-permute-start.1 = (bf16[128,512]{1,0:T(8,128)(2,1)S(1)}, bf16[128,512]{1,0:T(8,128)(2,1)}, u32[]{:S(2)}, u32[]{:S(2)}) collective-permute-start(bf16[128,512]{1,0:T(8,128)(2,1)S(1)} %dynamic-slice_maximum_fusion), channel_id=1, source_target_pairs={{0,16},{2,18},{4,20},{6,22},{8,24},{10,26},{12,28},{14,30},{16,0},... | collective-permute-start | bytes 393224 | tf_op jit(solution)/shard_map/ppermute | solution.py:32
  9.3 4.3 %collective-permute-start.3 = (bf16[2,128,128]{2,1,0:T(8,128)(2,1)S(1)}, bf16[2,128,128]{2,1,0:T(8,128)(2,1)S(1)}, u32[]{:S(2)}, u32[]{:S(2)}) collective-permute-start(bf16[2,128,128]{2,1,0:T(8,128)(2,1)S(1)} %get-tuple-element.32), channel_id=1, source_target_pairs={{0,2},{2,0},{4,6},{6,4},{8,10},{10,8},{12,14},{14,12},{16,18},{18,... | collective-permute-start | bytes 196616 | tf_op jit(solution)/shard_map/ppermute | solution.py:28
  10.9 5.0 %collective-permute-start.4 = (bf16[2,128,128]{2,1,0:T(8,128)(2,1)S(1)}, bf16[2,128,128]{2,1,0:T(8,128)(2,1)S(1)}, u32[]{:S(2)}, u32[]{:S(2)}) collective-permute-start(bf16[2,128,128]{2,1,0:T(8,128)(2,1)S(1)} %get-tuple-element.31), channel_id=1, source_target_pairs={{0,4},{2,6},{4,0},{6,2},{8,12},{10,14},{12,8},{14,10},{16,20},{18,... | collective-permute-start | bytes 196616 | tf_op jit(solution)/shard_map/ppermute | solution.py:28
  12.4 5.8 %collective-permute-start.5 = (bf16[2,128,128]{2,1,0:T(8,128)(2,1)S(1)}, bf16[2,128,128]{2,1,0:T(8,128)(2,1)S(1)}, u32[]{:S(2)}, u32[]{:S(2)}) collective-permute-start(bf16[2,128,128]{2,1,0:T(8,128)(2,1)S(1)} %get-tuple-element.30), channel_id=1, source_target_pairs={{0,6},{2,4},{4,2},{6,0},{8,14},{10,12},{12,10},{14,8},{16,22},{18,... | collective-permute-start | bytes 196616 | tf_op jit(solution)/shard_map/ppermute | solution.py:28
  13.6 9.0 %collective-permute-start.2 = (bf16[128,512]{1,0:T(8,128)(2,1)S(1)}, bf16[128,512]{1,0:T(8,128)(2,1)S(1)}, u32[]{:S(2)}, u32[]{:S(2)}) collective-permute-start(bf16[128,512]{1,0:T(8,128)(2,1)S(1)} %dynamic-slice_maximum_fusion), channel_id=1, source_target_pairs={{0,24},{2,26},{4,28},{6,30},{8,16},{10,18},{12,20},{14,22},{16,8},... | collective-permute-start | bytes 393224 | tf_op jit(solution)/shard_map/ppermute | solution.py:32
  15.8 10.6 %collective-permute-start.11 = (bf16[128,512]{1,0:T(8,128)(2,1)S(1)}, bf16[128,512]{1,0:T(8,128)(2,1)S(1)}, u32[]{:S(2)}, u32[]{:S(2)}) collective-permute-start(bf16[128,512]{1,0:T(8,128)(2,1)S(1)} %constant_dynamic-slice_fusion), channel_id=1, source_target_pairs={{0,2},{2,0},{4,6},{6,4},{8,10},{10,8},{12,14},{14,12},{16,18},{18,... | collective-permute-start | bytes 393224 | tf_op jit(solution)/shard_map/ppermute | solution.py:28
  18.2 9.8 %collective-permute-start.12 = (bf16[128,512]{1,0:T(8,128)(2,1)S(1)}, bf16[128,512]{1,0:T(8,128)(2,1)S(1)}, u32[]{:S(2)}, u32[]{:S(2)}) collective-permute-start(bf16[128,512]{1,0:T(8,128)(2,1)S(1)} %constant_dynamic-slice_fusion), channel_id=1, source_target_pairs={{0,4},{2,6},{4,0},{6,2},{8,12},{10,14},{12,8},{14,10},{16,20},{18,... | collective-permute-start | bytes 393224 | tf_op jit(solution)/shard_map/ppermute | solution.py:28
  21.1 7.3 %collective-permute-start.13 = (bf16[128,512]{1,0:T(8,128)(2,1)S(1)}, bf16[128,512]{1,0:T(8,128)(2,1)S(1)}, u32[]{:S(2)}, u32[]{:S(2)}) collective-permute-start(bf16[128,512]{1,0:T(8,128)(2,1)S(1)} %constant_dynamic-slice_fusion), channel_id=1, source_target_pairs={{0,6},{2,4},{4,2},{6,0},{8,14},{10,12},{12,10},{14,8},{16,22},{18,... | collective-permute-start | bytes 393224 | tf_op jit(solution)/shard_map/ppermute | solution.py:28
  24.2 7.0 %collective-permute-start.6 = (bf16[128,512]{1,0:T(8,128)(2,1)S(1)}, bf16[128,512]{1,0:T(8,128)(2,1)S(1)}, u32[]{:S(2)}, u32[]{:S(2)}) collective-permute-start(bf16[128,512]{1,0:T(8,128)(2,1)S(1)} %pad_maximum_fusion.3), channel_id=1, source_target_pairs={{0,2},{2,0},{4,6},{6,4},{8,10},{10,8},{12,14},{14,12},{16,18},{18,... | collective-permute-start | bytes 393224 | tf_op jit(solution)/shard_map/ppermute | solution.py:28
  25.8 8.0 %collective-permute-start.7 = (bf16[128,512]{1,0:T(8,128)(2,1)S(1)}, bf16[128,512]{1,0:T(8,128)(2,1)S(1)}, u32[]{:S(2)}, u32[]{:S(2)}) collective-permute-start(bf16[128,512]{1,0:T(8,128)(2,1)S(1)} %pad_maximum_fusion.4), channel_id=1, source_target_pairs={{0,4},{2,6},{4,0},{6,2},{8,12},{10,14},{12,8},{14,10},{16,20},{18,... | collective-permute-start | bytes 393224 | tf_op jit(solution)/shard_map/ppermute | solution.py:28
  26.4 7.4 %collective-permute-start.8 = (bf16[128,512]{1,0:T(8,128)(2,1)S(1)}, bf16[128,512]{1,0:T(8,128)(2,1)S(1)}, u32[]{:S(2)}, u32[]{:S(2)}) collective-permute-start(bf16[128,512]{1,0:T(8,128)(2,1)S(1)} %pad_maximum_fusion.5), channel_id=1, source_target_pairs={{0,6},{2,4},{4,2},{6,0},{8,14},{10,12},{12,10},{14,8},{16,22},{18,... | collective-permute-start | bytes 393224 | tf_op jit(solution)/shard_map/ppermute | solution.py:28
  36.6 5.6 %collective-permute-start.14 = (bf16[128,512]{1,0:T(8,128)(2,1)S(1)}, bf16[128,512]{1,0:T(8,128)(2,1)S(1)}, u32[]{:S(2)}, u32[]{:S(2)}) collective-permute-start(bf16[128,512]{1,0:T(8,128)(2,1)S(1)} %pad_maximum_fusion.6), channel_id=1, source_target_pairs={{0,8},{2,10},{4,12},{6,14},{8,0},{10,2},{12,4},{14,6},{16,24},{18,... | collective-permute-start | bytes 393224 | tf_op jit(solution)/shard_map/ppermute | solution.py:32
  37.2 12.3 %collective-permute-start.9 = (bf16[256,512]{1,0:T(8,128)(2,1)S(1)}, bf16[256,512]{1,0:T(8,128)(2,1)S(1)}, u32[]{:S(2)}, u32[]{:S(2)}) collective-permute-start(bf16[256,512]{1,0:T(8,128)(2,1)S(1)} %pad_maximum_fusion.2), channel_id=1, source_target_pairs={{0,2},{2,0},{4,6},{6,4},{8,10},{10,8},{12,14},{14,12},{16,18},{18,... | collective-permute-start | bytes 786440 | tf_op jit(solution)/shard_map/ppermute | solution.py:28
  42.2 17.1 %copy-start.1 = (bf16[128,1024]{1,0:T(8,128)(2,1)S(1)}, bf16[128,1024]{1,0:T(8,128)(2,1)}, u32[]{:S(2)}) copy-start(bf16[128,1024]{1,0:T(8,128)(2,1)} %param.5) | copy-start | bytes 786436
  42.2 6.5 %collective-permute-start.15 = (bf16[64,512]{1,0:T(8,128)(2,1)S(1)}, bf16[64,512]{1,0:T(8,128)(2,1)S(1)}, u32[]{:S(2)}, u32[]{:S(2)}) collective-permute-start(bf16[64,512]{1,0:T(8,128)(2,1)S(1)} %fusion.22), channel_id=1, source_target_pairs={{0,16},{2,18},{4,20},{6,22},{8,24},{10,26},{12,28},{14,30},{16,0},... | collective-permute-start | bytes 196616 | tf_op jit(solution)/shard_map/ppermute | solution.py:32
  42.9 7.8 %collective-permute-start.16 = (bf16[512,128]{1,0:T(8,128)(2,1)S(1)}, bf16[512,128]{1,0:T(8,128)(2,1)S(1)}, u32[]{:S(2)}, u32[]{:S(2)}) collective-permute-start(bf16[512,128]{1,0:T(8,128)(2,1)S(1)} %get-tuple-element.3), channel_id=1, source_target_pairs={{0,8},{2,10},{4,12},{6,14},{8,0},{10,2},{12,4},{14,6},{16,24},{18,... | collective-permute-start | bytes 393224 | tf_op jit(solution)/shard_map/ppermute | solution.py:32
  44.7 12.7 %collective-permute-start.17 = (bf16[512,128]{1,0:T(8,128)(2,1)S(1)}, bf16[512,128]{1,0:T(8,128)(2,1)S(1)}, u32[]{:S(2)}, u32[]{:S(2)}) collective-permute-start(bf16[512,128]{1,0:T(8,128)(2,1)S(1)} %get-tuple-element.5), channel_id=1, source_target_pairs={{0,16},{2,18},{4,20},{6,22},{8,24},{10,26},{12,28},{14,30},{16,0},... | collective-permute-start | bytes 393224 | tf_op jit(solution)/shard_map/ppermute | solution.py:32
  45.8 11.6 %collective-permute-start.18 = (bf16[512,128]{1,0:T(8,128)(2,1)S(1)}, bf16[512,128]{1,0:T(8,128)(2,1)S(1)}, u32[]{:S(2)}, u32[]{:S(2)}) collective-permute-start(bf16[512,128]{1,0:T(8,128)(2,1)S(1)} %get-tuple-element.4), channel_id=1, source_target_pairs={{0,24},{2,26},{4,28},{6,30},{8,16},{10,18},{12,20},{14,22},{16,8},... | collective-permute-start | bytes 393224 | tf_op jit(solution)/shard_map/ppermute | solution.py:32
  49.5 8.6 %collective-permute-start.10 = (bf16[128,512]{1,0:T(8,128)(2,1)S(1)}, bf16[128,512]{1,0:T(8,128)(2,1)S(1)}, u32[]{:S(2)}, u32[]{:S(2)}) collective-permute-start(bf16[128,512]{1,0:T(8,128)(2,1)S(1)} %fusion.13), channel_id=1, source_target_pairs={{0,4},{2,6},{4,0},{6,2},{8,12},{10,14},{12,8},{14,10},{16,20},{18,... | collective-permute-start | bytes 393224 | tf_op jit(solution)/shard_map/ppermute | solution.py:28
  58.0 1.4 %collective-permute-start.19 = (bf16[128,512]{1,0:T(8,128)(2,1)S(1)}, bf16[128,512]{1,0:T(8,128)(2,1)S(1)}, u32[]{:S(2)}, u32[]{:S(2)}) collective-permute-start(bf16[128,512]{1,0:T(8,128)(2,1)S(1)} %convolution_convert_fusion.1), channel_id=1, source_target_pairs={{0,1},{1,0},{2,3},{3,2},{4,5},{5,4},{6,7},{7,6},{8,9},{9,8},{10,11... | collective-permute-start | bytes 393224 | tf_op jit(solution)/shard_map/ppermute | solution.py:51

commit v25 on v22

--- a/solution.py
+++ b/solution.py
@@ -77,8 +77,14 @@
         along_inner(ordered[t * per_core : (t + 1) * per_core], t) for t in turns
     ]
     hidden_stack = [along_outer(hidden_part, e) for e in turns]
-    ready = sum(lanes(part, 0) * 0 for part in hidden_stack[2:])
-    everyone = lax.all_gather(jnp.concatenate(arrived, 0) + ready, "rep", axis=0)
+    arrived = jnp.concatenate(arrived, 0)
+    if rep_count == 2:
+        ready = sum(lanes(part, 0) * 0 for part in hidden_stack[2:])
+        everyone = [arrived, to_other(arrived + ready)]
+        first_holder = rep_pos
+    else:
+        everyone = lax.all_gather(arrived, "rep", axis=0)
+        first_holder = 0
     rows = []
     for t in turns:
         row_block = outer_pos * side + (inner_pos ^ t)
@@ -87,9 +93,9 @@
             column_block = (outer_pos ^ e) * side + inner_pos
             holder = ((row_block - column_block) & (blk_count - 1)) >> span_bits
             index = t * per_core + e % per_core
-            piece = everyone[0, index]
+            piece = everyone[0][index]
             for r in range(1, rep_count):
-                piece = jnp.where(holder == r, everyone[r, index], piece)
+                piece = jnp.where(holder ^ first_holder == r, everyone[r][index], piece)
             row.append(piece)
         rows.append(jnp.concatenate(row, 1))
     block = jnp.concatenate(rows, 0)

time: 53 us -> 56 us (1.057)
  waiting for transfers between devices: 13.2 us -> 16.4 us
  matrix products: 3.08 us -> 6.09 us
  blocking collectives: 4.18 us -> 1.99 us
  starting transfers between devices: 25.2 us -> 24.5 us
    ppermute x8, waiting for transfers between devices: 12.5 us -> 16.3 us  [along_outer(): return lax.ppermute(value, 'blk', pairs) if turn else value]
    dot_general x6, matrix products: 3.08 us -> 6.09 us  [dot(): lax.dot_general(lhs, rhs, (dims, ((), ())), preferred_element_type=jnp.fl...]
    all_gather x1 -> x0, blocking collectives: 2.18 us -> none  [shards(): lax.all_gather(jnp.concatenate(arrived, 0) + ready, 'rep', axis=0)]
    dynamic_slice x1, local copies, waits for them, and re-layouts: 0.91 us -> 0.02 us  [columns_of(): return lax.dynamic_slice_in_dim(value, index * cols_here, cols_here, 1)]
    ppermute x8, starting transfers between devices: 11.2 us -> 10.4 us  [along_outer(): return lax.ppermute(value, 'blk', pairs) if turn else value]
    unnamed x4 -> x10, local copies, waits for them, and re-layouts: 0.01 us -> 0.63 us
    ppermute x11, waiting for transfers between devices: 0.7 us -> 0.09 us  [along_inner(): return lax.ppermute(value, 'blk', pairs) if turn else value]
  transfers between devices with their start and end apart: 20 -> 21, of which waited for: 7 -> 6; matrix products, arithmetic and copies ran while one was open for 14% -> 17% of each run, Pallas kernels for 0% -> 0%
where the time goes in v25:
time: 56 us; the launch traced here: 55.7 us
  starting transfers between devices  24.5 us (44%)
  waiting for transfers between devices  16.4 us (29%)
  matrix products  6.09 us (11%)
  other arithmetic  3.9 us (7%)
  blocking collectives  1.99 us (4%)
  local copies, waits for them, and re-layouts  1.83 us (3%)
  between operations  0.96 us (2%)
    ppermute x8, waiting for transfers between devices, along_outer(): return lax.ppermute(value, 'blk', pairs) if turn else value  16.3 us
    ppermute x11, starting transfers between devices, along_inner(): return lax.ppermute(value, 'blk', pairs) if turn else value  13.9 us
    ppermute x8, starting transfers between devices, along_outer(): return lax.ppermute(value, 'blk', pairs) if turn else value  10.4 us
    dot_general x6, matrix products, dot(): lax.dot_general(lhs, rhs, (dims, ((), ())), preferred_element_type=jnp.fl...  6.09 us
    all_gather x1, blocking collectives, shards(): lax.all_gather(mixed_cols.astype(bf16), 'rep', axis=0, tiled=True)  1.99 us
  transfers between devices with their start and end apart: 21, of which 6 were waited for; matrix products, arithmetic and copies ran while one was open for 17% of the time, Pallas kernels for 0%

profile of v25, /device:TPU:0, one launch (start us, length us, event | category | flops | bytes accessed | tf_op | source)
XLA Modules:
  0.0 55.7 jit_solution(13615781809195600073)
XLA Ops:
  0.7 1.1 %dynamic-slice_maximum_fusion = bf16[128,512]{1,0:T(8,128)(2,1)S(1)} fusion(bf16[128,1024]{1,0:T(8,128)(2,1)} %param.5, s32[]{:T(128)S(6)} %select_n.224), kind=kLoop, calls=%fused_computation.48 | loop fusion | flops 262144 | bytes 262148 | tf_op jit(solution)/shard_map/max | solution.py:66
  1.7 5.1 %collective-permute-start.2 = (bf16[128,512]{1,0:T(8,128)(2,1)S(1)}, bf16[128,512]{1,0:T(8,128)(2,1)S(1)}, u32[]{:S(2)}, u32[]{:S(2)}) collective-permute-start(bf16[128,512]{1,0:T(8,128)(2,1)S(1)} %dynamic-slice_maximum_fusion), channel_id=1, source_target_pairs={{0,24},{2,26},{4,28},{6,30},{8,16},{10,18},{12,20},{14,22},{16,8},... | collective-permute-start | bytes 393224 | tf_op jit(solution)/shard_map/ppermute | solution.py:32
  6.9 0.7 %add_bitcast_fusion = s32[8]{0:T(128)S(1)} fusion(s32[1,8]{1,0:T(1,128)} %param.7, s32[]{:T(128)S(6)} %shift_right_arithmetic.54, s32[]{:T(128)S(6)} %and.60), kind=kLoop, calls=%fused_computation.95 | loop fusion | flops 56 | bytes 72 | tf_op jit(solution)/shard_map/eq | solution.py:72
  7.6 0.9 %slice_bitcast_fusion.7 = (bf16[128,128]{1,0:T(8,128)(2,1)S(1)}, bf16[128,128]{1,0:T(8,128)(2,1)S(1)}, bf16[128,128]{1,0:T(8,128)(2,1)S(1)}, bf16[128,128]{1,0:T...) fusion(bf16[1,8,128,128]{3,2,1,0:T(8,128)(2,1)} %param.6), kind=kLoop, calls=%fused_computation.76 | loop fusion | bytes 524288 | tf_op jit(solution)/shard_map/jit(_where)/broadcast_in_dim | solution.py:75
  8.8 2.5 %collective-permute-start.5 = (bf16[2,128,128]{2,1,0:T(8,128)(2,1)S(1)}, bf16[2,128,128]{2,1,0:T(8,128)(2,1)S(1)}, u32[]{:S(2)}, u32[]{:S(2)}) collective-permute-start(bf16[2,128,128]{2,1,0:T(8,128)(2,1)S(1)} %get-tuple-element.31), channel_id=1, source_target_pairs={{0,6},{2,4},{4,2},{6,0},{8,14},{10,12},{12,10},{14,8},{16,22},{18,... | collective-permute-start | bytes 196616 | tf_op jit(solution)/shard_map/ppermute | solution.py:28
  11.3 0.5 collective-permute-start.4
  11.8 0.5 collective-permute-start.3
  12.3 5.6 %collective-permute-done.1 = bf16[128,512]{1,0:T(8,128)(2,1)S(1)} collective-permute-done((bf16[128,512]{1,0:T(8,128)(2,1)S(1)}, bf16[128,512]{1,0:T(8,128)(2,1)S(1)}, u32[]{:S(2)}, u32[]{:S(2)}) %collective-permute-start.1) | collective-permute-done | bytes 131104 | tf_op jit(solution)/shard_map/ppermute | solution.py:32
  18.0 0.6 %copy-done.3 = bf16[128,512]{1,0:T(8,128)(2,1)} copy-done((bf16[128,512]{1,0:T(8,128)(2,1)}, bf16[128,512]{1,0:T(8,128)(2,1)S(1)}, u32[]{:S(2)}) %copy-start.3) | copy-done | bytes 131096
  18.8 2.5 %collective-permute-start.14 = (bf16[128,512]{1,0:T(8,128)(2,1)S(1)}, bf16[128,512]{1,0:T(8,128)(2,1)}, u32[]{:S(2)}, u32[]{:S(2)}) collective-permute-start(bf16[128,512]{1,0:T(8,128)(2,1)S(1)} %constant_dynamic-slice_fusion), channel_id=1, source_target_pairs={{0,6},{2,4},{4,2},{6,0},{8,14},{10,12},{12,10},{14,8},{16,22},{18,... | collective-permute-start | bytes 393224 | tf_op jit(solution)/shard_map/ppermute | solution.py:28
  21.3 0.5 collective-permute-start.13
  21.8 0.5 collective-permute-start.12
  22.6 2.1 %collective-permute-done = bf16[128,512]{1,0:T(8,128)(2,1)} collective-permute-done((bf16[128,512]{1,0:T(8,128)(2,1)S(1)}, bf16[128,512]{1,0:T(8,128)(2,1)}, u32[]{:S(2)}, u32[]{:S(2)}) %collective-permute-start) | collective-permute-done | bytes 131104 | tf_op jit(solution)/shard_map/ppermute | solution.py:32
  24.7 1.4 %convolution_convert_fusion = bf16[512,512]{1,0:T(8,128)(2,1)S(1)} fusion(bf16[512,512]{1,0:T(8,128)(2,1)S(1)} %maximum_maximum_fusion, bf16[128,512]{1,0:T(8,128)(2,1)S(1)} %collective-permute-done.2, bf16[128,512]{1,0:T(8,128)(2,1)S(1)} %copy-done.4, bf16[128,512]{1,0:T(8,128)(2,1)} %collective-permute-done, bf16[128,512]{1,0:T(8,128)(2,1)S(1)} %dynamic-slice_maximum_fusion), kind=kOutput, calls=%fused_computation.1 | convolution fusion | flops 270794752 | bytes 1572864 | tf_op jit(solution)/shard_map/dot_general | solution.py:52
  26.2 2.5 %collective-permute-start.9 = (bf16[128,512]{1,0:T(8,128)(2,1)S(1)}, bf16[128,512]{1,0:T(8,128)(2,1)S(1)}, u32[]{:S(2)}, u32[]{:S(2)}) collective-permute-start(bf16[128,512]{1,0:T(8,128)(2,1)S(1)} %pad_maximum_fusion.4), channel_id=1, source_target_pairs={{0,6},{2,4},{4,2},{6,0},{8,14},{10,12},{12,10},{14,8},{16,22},{18,... | collective-permute-start | bytes 393224 | tf_op jit(solution)/shard_map/ppermute | solution.py:28
  28.8 0.6 %collective-permute-start.8 = (bf16[128,512]{1,0:T(8,128)(2,1)S(1)}, bf16[128,512]{1,0:T(8,128)(2,1)S(1)}, u32[]{:S(2)}, u32[]{:S(2)}) collective-permute-start(bf16[128,512]{1,0:T(8,128)(2,1)S(1)} %pad_maximum_fusion.3), channel_id=1, source_target_pairs={{0,4},{2,6},{4,0},{6,2},{8,12},{10,14},{12,8},{14,10},{16,20},{18,... | collective-permute-start | bytes 393224 | tf_op jit(solution)/shard_map/ppermute | solution.py:28
  29.4 0.6 %collective-permute-start.7 = (bf16[128,512]{1,0:T(8,128)(2,1)S(1)}, bf16[128,512]{1,0:T(8,128)(2,1)S(1)}, u32[]{:S(2)}, u32[]{:S(2)}) collective-permute-start(bf16[128,512]{1,0:T(8,128)(2,1)S(1)} %pad_maximum_fusion.2), channel_id=1, source_target_pairs={{0,2},{2,0},{4,6},{6,4},{8,10},{10,8},{12,14},{14,12},{16,18},{18,... | collective-permute-start | bytes 393224 | tf_op jit(solution)/shard_map/ppermute | solution.py:28
  30.0 1.5 %fusion = bf16[512,512]{1,0:T(8,128)(2,1)S(1)} fusion(bf16[512,512]{1,0:T(8,128)(2,1)S(1)} %maximum_maximum_fusion, bf16[512,512]{1,0:T(8,128)(2,1)S(1)} %convolution_convert_fusion, bf16[128,512]{1,0:T(8,128)(2,1)} %collective-permute-done.14, bf16[128,512]{1,0:T(8,128)(2,1)} %collective-permute-done.13, bf16[128,512]{1,0:T(8,128)(2,1)} %collective-permute-done.12, ...), kind=kOutput, calls=%fused_computation.2 | convolution fusion | flops 271581184 | bytes 2097152 | tf_op jit(solution)/shard_map/dot_general | solution.py:52
  31.6 2.5 %collective-permute-start.19 = (bf16[512,128]{1,0:T(8,128)(2,1)S(1)}, bf16[512,128]{1,0:T(8,128)(2,1)S(1)}, u32[]{:S(2)}, u32[]{:S(2)}) collective-permute-start(bf16[512,128]{1,0:T(8,128)(2,1)S(1)} %get-tuple-element.4), channel_id=1, source_target_pairs={{0,24},{2,26},{4,28},{6,30},{8,16},{10,18},{12,20},{14,22},{16,8},... | collective-permute-start | bytes 393224 | tf_op jit(solution)/shard_map/ppermute | solution.py:32
  34.1 1.9 %collective-permute-start.17 = (bf16[512,128]{1,0:T(8,128)(2,1)S(1)}, bf16[512,128]{1,0:T(8,128)(2,1)S(1)}, u32[]{:S(2)}, u32[]{:S(2)}) collective-permute-start(bf16[512,128]{1,0:T(8,128)(2,1)S(1)} %get-tuple-element.3), channel_id=1, source_target_pairs={{0,8},{2,10},{4,12},{6,14},{8,0},{10,2},{12,4},{14,6},{16,24},{18,... | collective-permute-start | bytes 393224 | tf_op jit(solution)/shard_map/ppermute | solution.py:32
  36.1 2.0 %all_gather.3 = bf16[256,512]{1,0:T(8,128)(2,1)S(1)} all-gather(bf16[128,512]{1,0:T(8,128)(2,1)S(1)} %fusion.19), channel_id=1, replica_groups=mesh['blk'=16,'rep'=2] {'rep'}, dimensions={0}, use_global_device_ids=true | all-gather | bytes 393216 | tf_op jit(solution)/shard_map/all_gather | solution.py:120
  38.5 1.6 %collective-permute-start.10 = (bf16[256,512]{1,0:T(8,128)(2,1)S(1)}, bf16[256,512]{1,0:T(8,128)(2,1)S(1)}, u32[]{:S(2)}, u32[]{:S(2)}) collective-permute-start(bf16[256,512]{1,0:T(8,128)(2,1)S(1)} %pad_maximum_fusion.1), channel_id=1, source_target_pairs={{0,2},{2,0},{4,6},{6,4},{8,10},{10,8},{12,14},{14,12},{16,18},{18,... | collective-permute-start | bytes 786440 | tf_op jit(solution)/shard_map/ppermute | solution.py:28
  40.1 1.4 %convolution_add_fusion.1 = f32[256,512]{1,0:T(8,128)S(1)} fusion(bf16[256,512]{1,0:T(8,128)(2,1)S(1)} %all_gather.3, f32[512,512]{1,0:T(8,128)S(1)} %get-tuple-element.61, bf16[128,512]{1,0:T(8,128)(2,1)} %collective-permute-done.14, bf16[128,512]{1,0:T(8,128)(2,1)} %collective-permute-done.13, bf16[128,512]{1,0:T(8,128)(2,1)} %collective-permute-done.12, ...), kind=kOutput, calls=%fused_computation.3 | convolution fusion | flops 136577024 | bytes 1835008 | tf_op jit(solution)/shard_map/dot_general | solution.py:52
  41.7 3.6 %collective-permute-done.18 = bf16[512,128]{1,0:T(8,128)(2,1)S(1)} collective-permute-done((bf16[512,128]{1,0:T(8,128)(2,1)S(1)}, bf16[512,128]{1,0:T(8,128)(2,1)S(1)}, u32[]{:S(2)}, u32[]{:S(2)}) %collective-permute-start.18) | collective-permute-done | bytes 131104 | tf_op jit(solution)/shard_map/ppermute | solution.py:32
  45.4 0.4 convolution_convert_fusion.1
  46.0 2.1 %collective-permute-done.15 = bf16[128,512]{1,0:T(8,128)(2,1)S(1)} collective-permute-done((bf16[128,512]{1,0:T(8,128)(2,1)S(1)}, bf16[128,512]{1,0:T(8,128)(2,1)S(1)}, u32[]{:S(2)}, u32[]{:S(2)}) %collective-permute-start.15) | collective-permute-done | bytes 131104 | tf_op jit(solution)/shard_map/ppermute | solution.py:32
  48.1 0.6 %collective-permute-start.16 = (bf16[64,512]{1,0:T(8,128)(2,1)S(1)}, bf16[64,512]{1,0:T(8,128)(2,1)S(1)}, u32[]{:S(2)}, u32[]{:S(2)}) collective-permute-start(bf16[64,512]{1,0:T(8,128)(2,1)S(1)} %fusion.22), channel_id=1, source_target_pairs={{0,16},{2,18},{4,20},{6,22},{8,24},{10,26},{12,28},{14,30},{16,0},... | collective-permute-start | bytes 196616 | tf_op jit(solution)/shard_map/ppermute | solution.py:32
  48.7 1.1 %select_convert_fusion = bf16[128,512]{1,0:T(8,128)(2,1)} fusion(bf16[128,512]{1,0:T(8,128)(2,1)S(1)} %collective-permute-done.20, bf16[128,1024]{1,0:T(8,128)(2,1)S(1)} %copy-done.1, s32[]{:T(128)S(6)} %select_n.224, bf16[512,128]{1,0:T(8,128)(2,1)S(1)} %fusion.16, bf16[2,512,1024]{2,1,0:T(8,128)(2,1)S(1)} %bitcast.105, s32[]{:T(128)S(6)} %select_n.293, ...), kind=kOutput, calls=%fused_computation.33 | convolution fusion | flops 67567616 | bytes 1048588 | tf_op jit(solution)/shard_map/dot_general | solution.py:52
  49.8 1.6 %collective-permute-start.11 = (bf16[128,512]{1,0:T(8,128)(2,1)S(1)}, bf16[128,512]{1,0:T(8,128)(2,1)S(1)}, u32[]{:S(2)}, u32[]{:S(2)}) collective-permute-start(bf16[128,512]{1,0:T(8,128)(2,1)S(1)} %fusion.13), channel_id=1, source_target_pairs={{0,4},{2,6},{4,0},{6,2},{8,12},{10,14},{12,8},{14,10},{16,20},{18,... | collective-permute-start | bytes 393224 | tf_op jit(solution)/shard_map/ppermute | solution.py:28
  51.4 2.9 %collective-permute-done.16 = bf16[64,512]{1,0:T(8,128)(2,1)S(1)} collective-permute-done((bf16[64,512]{1,0:T(8,128)(2,1)S(1)}, bf16[64,512]{1,0:T(8,128)(2,1)S(1)}, u32[]{:S(2)}, u32[]{:S(2)}) %collective-permute-start.16) | collective-permute-done | bytes 65568 | tf_op jit(solution)/shard_map/ppermute | solution.py:32
  54.3 0.7 %fusion.23 = f32[64,512]{1,0:T(8,128)} fusion(bf16[64,512]{1,0:T(8,128)(2,1)S(1)} %collective-permute-done.16, f32[4,64,512]{2,1,0:T(8,128)S(1)} %bitcast.109, s32[]{:T(128)S(6)} %select_n.285, bf16[128,512]{1,0:T(8,128)(2,1)S(1)} %collective-permute-done.15), kind=kLoop, calls=%fused_computation.45 | loop fusion | flops 131072 | bytes 393220 | tf_op jit(solution)/shard_map/add | solution.py:42
  55.0 0.7 %fusion.15 = bf16[128,512]{1,0:T(8,128)(2,1)} fusion(f32[512,512]{1,0:T(8,128)S(1)} %get-tuple-element.61, bf16[128,512]{1,0:T(8,128)(2,1)S(1)} %collective-permute-done.11, bf16[256,512]{1,0:T(8,128)(2,1)S(1)} %collective-permute-done.10), kind=kLoop, calls=%fused_computation.24 | loop fusion | flops 327680 | bytes 655360 | tf_op jit(solution)/shard_map/convert_element_type | solution.py:133
  (62 shorter events, 1.9 us)
Async XLA Ops:
  0.6 21.7 %copy-start = (bf16[1024,1024]{1,0:T(8,128)(2,1)S(1)}, bf16[1024,1024]{1,0:T(8,128)(2,1)}, u32[]{:S(2)}) copy-start(bf16[1024,1024]{1,0:T(8,128)(2,1)} %param.8) | copy-start | bytes 6291460
  1.7 10.6 %collective-permute-start.2 = (bf16[128,512]{1,0:T(8,128)(2,1)S(1)}, bf16[128,512]{1,0:T(8,128)(2,1)S(1)}, u32[]{:S(2)}, u32[]{:S(2)}) collective-permute-start(bf16[128,512]{1,0:T(8,128)(2,1)S(1)} %dynamic-slice_maximum_fusion), channel_id=1, source_target_pairs={{0,24},{2,26},{4,28},{6,30},{8,16},{10,18},{12,20},{14,22},{16,8},... | collective-permute-start | bytes 393224 | tf_op jit(solution)/shard_map/ppermute | solution.py:32
  6.8 11.1 %collective-permute-start.1 = (bf16[128,512]{1,0:T(8,128)(2,1)S(1)}, bf16[128,512]{1,0:T(8,128)(2,1)S(1)}, u32[]{:S(2)}, u32[]{:S(2)}) collective-permute-start(bf16[128,512]{1,0:T(8,128)(2,1)S(1)} %dynamic-slice_maximum_fusion), channel_id=1, source_target_pairs={{0,16},{2,18},{4,20},{6,22},{8,24},{10,26},{12,28},{14,30},{16,0},... | collective-permute-start | bytes 393224 | tf_op jit(solution)/shard_map/ppermute | solution.py:32
  6.9 11.9 %copy-start.2 = (bf16[128,1024]{1,0:T(8,128)(2,1)S(1)}, bf16[128,1024]{1,0:T(8,128)(2,1)}, u32[]{:S(2)}) copy-start(bf16[128,1024]{1,0:T(8,128)(2,1)} %param.9) | copy-start | bytes 786436
  8.8 9.2 %collective-permute-start.5 = (bf16[2,128,128]{2,1,0:T(8,128)(2,1)S(1)}, bf16[2,128,128]{2,1,0:T(8,128)(2,1)S(1)}, u32[]{:S(2)}, u32[]{:S(2)}) collective-permute-start(bf16[2,128,128]{2,1,0:T(8,128)(2,1)S(1)} %get-tuple-element.31), channel_id=1, source_target_pairs={{0,6},{2,4},{4,2},{6,0},{8,14},{10,12},{12,10},{14,8},{16,22},{18,... | collective-permute-start | bytes 196616 | tf_op jit(solution)/shard_map/ppermute | solution.py:28
  11.3 6.7 %collective-permute-start.4 = (bf16[2,128,128]{2,1,0:T(8,128)(2,1)S(1)}, bf16[2,128,128]{2,1,0:T(8,128)(2,1)S(1)}, u32[]{:S(2)}, u32[]{:S(2)}) collective-permute-start(bf16[2,128,128]{2,1,0:T(8,128)(2,1)S(1)} %get-tuple-element.32), channel_id=1, source_target_pairs={{0,4},{2,6},{4,0},{6,2},{8,12},{10,14},{12,8},{14,10},{16,20},{18,... | collective-permute-start | bytes 196616 | tf_op jit(solution)/shard_map/ppermute | solution.py:28
  11.8 6.2 %collective-permute-start.3 = (bf16[2,128,128]{2,1,0:T(8,128)(2,1)S(1)}, bf16[2,128,128]{2,1,0:T(8,128)(2,1)S(1)}, u32[]{:S(2)}, u32[]{:S(2)}) collective-permute-start(bf16[2,128,128]{2,1,0:T(8,128)(2,1)S(1)} %get-tuple-element.33), channel_id=1, source_target_pairs={{0,2},{2,0},{4,6},{6,4},{8,10},{10,8},{12,14},{14,12},{16,18},{18,... | collective-permute-start | bytes 196616 | tf_op jit(solution)/shard_map/ppermute | solution.py:28
  17.9 0.7 %copy-start.3 = (bf16[128,512]{1,0:T(8,128)(2,1)}, bf16[128,512]{1,0:T(8,128)(2,1)S(1)}, u32[]{:S(2)}) copy-start(bf16[128,512]{1,0:T(8,128)(2,1)S(1)} %collective-permute-done.1) | copy-start | bytes 393220
  18.6 3.8 %collective-permute-start.6 = (bf16[8,128,128]{2,1,0:T(8,128)(2,1)S(1)}, bf16[8,128,128]{2,1,0:T(8,128)(2,1)S(1)}, u32[]{:S(2)}, u32[]{:S(2)}) collective-permute-start(bf16[8,128,128]{2,1,0:T(8,128)(2,1)S(1)} %maximum_add_fusion), channel_id=1, source_target_pairs={{0,1},{1,0},{2,3},{3,2},{4,5},{5,4},{6,7},{7,6},{8,9},{9,8},{10,11... | collective-permute-start | bytes 786440 | tf_op jit(solution)/shard_map/ppermute | solution.py:49
  18.7 6.0 %collective-permute-start = (bf16[128,512]{1,0:T(8,128)(2,1)S(1)}, bf16[128,512]{1,0:T(8,128)(2,1)}, u32[]{:S(2)}, u32[]{:S(2)}) collective-permute-start(bf16[128,512]{1,0:T(8,128)(2,1)S(1)} %dynamic-slice_maximum_fusion), channel_id=1, source_target_pairs={{0,8},{2,10},{4,12},{6,14},{8,0},{10,2},{12,4},{14,6},{16,24},{18,... | collective-permute-start | bytes 393224 | tf_op jit(solution)/shard_map/ppermute | solution.py:32
  18.8 10.6 %collective-permute-start.14 = (bf16[128,512]{1,0:T(8,128)(2,1)S(1)}, bf16[128,512]{1,0:T(8,128)(2,1)}, u32[]{:S(2)}, u32[]{:S(2)}) collective-permute-start(bf16[128,512]{1,0:T(8,128)(2,1)S(1)} %constant_dynamic-slice_fusion), channel_id=1, source_target_pairs={{0,6},{2,4},{4,2},{6,0},{8,14},{10,12},{12,10},{14,8},{16,22},{18,... | collective-permute-start | bytes 393224 | tf_op jit(solution)/shard_map/ppermute | solution.py:28
  21.3 8.7 %collective-permute-start.13 = (bf16[128,512]{1,0:T(8,128)(2,1)S(1)}, bf16[128,512]{1,0:T(8,128)(2,1)}, u32[]{:S(2)}, u32[]{:S(2)}) collective-permute-start(bf16[128,512]{1,0:T(8,128)(2,1)S(1)} %constant_dynamic-slice_fusion), channel_id=1, source_target_pairs={{0,4},{2,6},{4,0},{6,2},{8,12},{10,14},{12,8},{14,10},{16,20},{18,... | collective-permute-start | bytes 393224 | tf_op jit(solution)/shard_map/ppermute | solution.py:28
  21.8 8.2 %collective-permute-start.12 = (bf16[128,512]{1,0:T(8,128)(2,1)S(1)}, bf16[128,512]{1,0:T(8,128)(2,1)}, u32[]{:S(2)}, u32[]{:S(2)}) collective-permute-start(bf16[128,512]{1,0:T(8,128)(2,1)S(1)} %constant_dynamic-slice_fusion), channel_id=1, source_target_pairs={{0,2},{2,0},{4,6},{6,4},{8,10},{10,8},{12,14},{14,12},{16,18},{18,... | collective-permute-start | bytes 393224 | tf_op jit(solution)/shard_map/ppermute | solution.py:28
  22.4 2.3 %copy-start.4 = (bf16[128,512]{1,0:T(8,128)(2,1)S(1)}, bf16[128,512]{1,0:T(8,128)(2,1)}, u32[]{:S(2)}) copy-start(bf16[128,512]{1,0:T(8,128)(2,1)} %copy-done.3) | copy-start | bytes 393220
  26.2 7.9 %collective-permute-start.9 = (bf16[128,512]{1,0:T(8,128)(2,1)S(1)}, bf16[128,512]{1,0:T(8,128)(2,1)S(1)}, u32[]{:S(2)}, u32[]{:S(2)}) collective-permute-start(bf16[128,512]{1,0:T(8,128)(2,1)S(1)} %pad_maximum_fusion.4), channel_id=1, source_target_pairs={{0,6},{2,4},{4,2},{6,0},{8,14},{10,12},{12,10},{14,8},{16,22},{18,... | collective-permute-start | bytes 393224 | tf_op jit(solution)/shard_map/ppermute | solution.py:28
  28.8 7.3 %collective-permute-start.8 = (bf16[128,512]{1,0:T(8,128)(2,1)S(1)}, bf16[128,512]{1,0:T(8,128)(2,1)S(1)}, u32[]{:S(2)}, u32[]{:S(2)}) collective-permute-start(bf16[128,512]{1,0:T(8,128)(2,1)S(1)} %pad_maximum_fusion.3), channel_id=1, source_target_pairs={{0,4},{2,6},{4,0},{6,2},{8,12},{10,14},{12,8},{14,10},{16,20},{18,... | collective-permute-start | bytes 393224 | tf_op jit(solution)/shard_map/ppermute | solution.py:28
  29.4 6.7 %collective-permute-start.7 = (bf16[128,512]{1,0:T(8,128)(2,1)S(1)}, bf16[128,512]{1,0:T(8,128)(2,1)S(1)}, u32[]{:S(2)}, u32[]{:S(2)}) collective-permute-start(bf16[128,512]{1,0:T(8,128)(2,1)S(1)} %pad_maximum_fusion.2), channel_id=1, source_target_pairs={{0,2},{2,0},{4,6},{6,4},{8,10},{10,8},{12,14},{14,12},{16,18},{18,... | collective-permute-start | bytes 393224 | tf_op jit(solution)/shard_map/ppermute | solution.py:28
  31.6 10.1 %collective-permute-start.19 = (bf16[512,128]{1,0:T(8,128)(2,1)S(1)}, bf16[512,128]{1,0:T(8,128)(2,1)S(1)}, u32[]{:S(2)}, u32[]{:S(2)}) collective-permute-start(bf16[512,128]{1,0:T(8,128)(2,1)S(1)} %get-tuple-element.4), channel_id=1, source_target_pairs={{0,24},{2,26},{4,28},{6,30},{8,16},{10,18},{12,20},{14,22},{16,8},... | collective-permute-start | bytes 393224 | tf_op jit(solution)/shard_map/ppermute | solution.py:32
  34.1 11.2 %collective-permute-start.18 = (bf16[512,128]{1,0:T(8,128)(2,1)S(1)}, bf16[512,128]{1,0:T(8,128)(2,1)S(1)}, u32[]{:S(2)}, u32[]{:S(2)}) collective-permute-start(bf16[512,128]{1,0:T(8,128)(2,1)S(1)} %get-tuple-element.5), channel_id=1, source_target_pairs={{0,16},{2,18},{4,20},{6,22},{8,24},{10,26},{12,28},{14,30},{16,0},... | collective-permute-start | bytes 393224 | tf_op jit(solution)/shard_map/ppermute | solution.py:32
  34.1 11.2 %collective-permute-start.17 = (bf16[512,128]{1,0:T(8,128)(2,1)S(1)}, bf16[512,128]{1,0:T(8,128)(2,1)S(1)}, u32[]{:S(2)}, u32[]{:S(2)}) collective-permute-start(bf16[512,128]{1,0:T(8,128)(2,1)S(1)} %get-tuple-element.3), channel_id=1, source_target_pairs={{0,8},{2,10},{4,12},{6,14},{8,0},{10,2},{12,4},{14,6},{16,24},{18,... | collective-permute-start | bytes 393224 | tf_op jit(solution)/shard_map/ppermute | solution.py:32
  38.5 11.3 %collective-permute-start.10 = (bf16[256,512]{1,0:T(8,128)(2,1)S(1)}, bf16[256,512]{1,0:T(8,128)(2,1)S(1)}, u32[]{:S(2)}, u32[]{:S(2)}) collective-permute-start(bf16[256,512]{1,0:T(8,128)(2,1)S(1)} %pad_maximum_fusion.1), channel_id=1, source_target_pairs={{0,2},{2,0},{4,6},{6,4},{8,10},{10,8},{12,14},{14,12},{16,18},{18,... | collective-permute-start | bytes 786440 | tf_op jit(solution)/shard_map/ppermute | solution.py:28
  40.1 8.6 %copy-start.1 = (bf16[128,1024]{1,0:T(8,128)(2,1)S(1)}, bf16[128,1024]{1,0:T(8,128)(2,1)}, u32[]{:S(2)}) copy-start(bf16[128,1024]{1,0:T(8,128)(2,1)} %param.5) | copy-start | bytes 786436
  41.5 6.5 %collective-permute-start.15 = (bf16[128,512]{1,0:T(8,128)(2,1)S(1)}, bf16[128,512]{1,0:T(8,128)(2,1)S(1)}, u32[]{:S(2)}, u32[]{:S(2)}) collective-permute-start(bf16[128,512]{1,0:T(8,128)(2,1)S(1)} %pad_maximum_fusion.5), channel_id=1, source_target_pairs={{0,8},{2,10},{4,12},{6,14},{8,0},{10,2},{12,4},{14,6},{16,24},{18,... | collective-permute-start | bytes 393224 | tf_op jit(solution)/shard_map/ppermute | solution.py:32
  45.9 2.8 %collective-permute-start.20 = (bf16[128,512]{1,0:T(8,128)(2,1)S(1)}, bf16[128,512]{1,0:T(8,128)(2,1)S(1)}, u32[]{:S(2)}, u32[]{:S(2)}) collective-permute-start(bf16[128,512]{1,0:T(8,128)(2,1)S(1)} %convolution_convert_fusion.1), channel_id=1, source_target_pairs={{0,1},{1,0},{2,3},{3,2},{4,5},{5,4},{6,7},{7,6},{8,9},{9,8},{10,11... | collective-permute-start | bytes 393224 | tf_op jit(solution)/shard_map/ppermute | solution.py:49
  48.1 6.2 %collective-permute-start.16 = (bf16[64,512]{1,0:T(8,128)(2,1)S(1)}, bf16[64,512]{1,0:T(8,128)(2,1)S(1)}, u32[]{:S(2)}, u32[]{:S(2)}) collective-permute-start(bf16[64,512]{1,0:T(8,128)(2,1)S(1)} %fusion.22), channel_id=1, source_target_pairs={{0,16},{2,18},{4,20},{6,22},{8,24},{10,26},{12,28},{14,30},{16,0},... | collective-permute-start | bytes 196616 | tf_op jit(solution)/shard_map/ppermute | solution.py:32
  49.8 5.2 %collective-permute-start.11 = (bf16[128,512]{1,0:T(8,128)(2,1)S(1)}, bf16[128,512]{1,0:T(8,128)(2,1)S(1)}, u32[]{:S(2)}, u32[]{:S(2)}) collective-permute-start(bf16[128,512]{1,0:T(8,128)(2,1)S(1)} %fusion.13), channel_id=1, source_target_pairs={{0,4},{2,6},{4,0},{6,2},{8,12},{10,14},{12,8},{14,10},{16,20},{18,... | collective-permute-start | bytes 393224 | tf_op jit(solution)/shard_map/ppermute | solution.py:28

commit v26 on v20

--- a/solution.py
+++ b/solution.py
@@ -31,12 +31,15 @@
         pairs = [(o * side + i, (o ^ turn) * side + i) for o in turns for i in turns]
         return lax.ppermute(value, "blk", pairs) if turn else value
 
-    def halved(parts, move):
+    def halved(parts, move, late):
         parts = dict(enumerate(parts))
         size = parts[0].shape[0]
         for bit in rising:
             keys = [k for k in parts if not k & bit]
             sent = jnp.concatenate([parts[k ^ bit].astype(bf16) for k in keys], 0)
+            if bit == rising[-1]:
+                for other in late:
+                    sent = after(sent, other)
             got = move(sent, bit)
             parts = {
                 k: parts[k].astype(jnp.float32)
@@ -114,15 +117,18 @@
     w_share = lax.dynamic_index_in_dim(w_share, inner_pos, 1, keepdims=False)
     w_share = columns_of(w_share.reshape(side * rows_here, feature_width), rep_pos)
     out_part = dot(mixed_cols, w_share, ((0,), (0,)))
+    out_part = out_part.astype(bf16)
+    out_got = [
+        along_inner(out_part[t * tile_size : (t + 1) * tile_size], t) for t in turns
+    ]
     weight_part = after(dot(mixed_cols, grad_stack, ((1,), (0,))), out_part)
     by_outer = weight_part.reshape(side, rows_here, cols_here)
     grad_weight = halved(
         [lax.dynamic_index_in_dim(by_outer, outer_pos ^ t, 0, keepdims=False) for t in turns],
         along_outer,
+        out_got[1:],
     )
-    out_part = halved(
-        [out_part[t * tile_size : (t + 1) * tile_size] for t in turns], along_inner
-    ).astype(bf16)
+    out_part = sum(part.astype(jnp.float32) for part in out_got).astype(bf16)
 
     back = after(back, weight_part).astype(bf16)
     w_rows = w_out.reshape(rep_count, cols_here, feature_width)

time: 52.1 us -> 53.5 us (1.027)
  starting transfers between devices: 25.2 us -> 28.5 us
  matrix products: 4.05 us -> 3.09 us
  waiting for transfers between devices: 12.4 us -> 11.5 us
    ppermute x8, waiting for transfers between devices: 9.14 us -> 3.47 us  [along_outer(): return lax.ppermute(value, 'blk', pairs) if turn else value]
    ppermute x11 -> x12, waiting for transfers between devices: 3.25 us -> 7.98 us  [along_inner(): return lax.ppermute(value, 'blk', pairs) if turn else value]
    ppermute x8, starting transfers between devices: 12.3 us -> 14.1 us  [along_outer(): return lax.ppermute(value, 'blk', pairs) if turn else value]
    ppermute x11 -> x12, starting transfers between devices: 12.8 us -> 14.3 us  [along_inner(): return lax.ppermute(value, 'blk', pairs) if turn else value]
    dot_general x6, matrix products: 4.05 us -> 3.09 us  [dot(): lax.dot_general(lhs, rhs, (dims, ((), ())), preferred_element_type=jnp.fl...]
  transfers between devices with their start and end apart: 20 -> 21, of which waited for: 7 -> 9; matrix products, arithmetic and copies ran while one was open for 14% -> 12% of each run, Pallas kernels for 0% -> 0%
where the time goes in v26:
time: 53.5 us; the launch traced here: 53.3 us
  starting transfers between devices  28.5 us (53%)
  waiting for transfers between devices  11.5 us (21%)
  blocking collectives  4.18 us (8%)
  other arithmetic  3.86 us (7%)
  matrix products  3.09 us (6%)
  local copies, waits for them, and re-layouts  1.24 us (2%)
  between operations  0.92 us (2%)
    ppermute x12, starting transfers between devices, along_inner(): return lax.ppermute(value, 'blk', pairs) if turn else value  14.3 us
    ppermute x8, starting transfers between devices, along_outer(): return lax.ppermute(value, 'blk', pairs) if turn else value  14.1 us
    ppermute x12, waiting for transfers between devices, along_inner(): return lax.ppermute(value, 'blk', pairs) if turn else value  7.98 us
    ppermute x8, waiting for transfers between devices, along_outer(): return lax.ppermute(value, 'blk', pairs) if turn else value  3.47 us
    dot_general x6, matrix products, dot(): lax.dot_general(lhs, rhs, (dims, ((), ())), preferred_element_type=jnp.fl...  3.09 us
    all_gather x1, blocking collectives, shards(): everyone = lax.all_gather(jnp.concatenate(arrived, 0), 'rep', axis=0)  2.18 us
    all_gather x1, blocking collectives, shards(): lax.all_gather(mixed_cols.astype(bf16), 'rep', axis=0, tiled=True)  1.99 us
    max x1, other arithmetic, shards(): hidden_part = jnp.maximum(columns_of(hidden_pre, rep_pos), 0)  1.08 us
  transfers between devices with their start and end apart: 21, of which 9 were waited for; matrix products, arithmetic and copies ran while one was open for 12% of the time, Pallas kernels for 0%

profile of v26, /device:TPU:0, one launch (start us, length us, event | category | flops | bytes accessed | tf_op | source)
XLA Modules:
  0.0 53.3 jit_solution(3606946698410720159)
XLA Ops:
  0.7 1.1 %dynamic-slice_maximum_fusion = bf16[128,512]{1,0:T(8,128)(2,1)S(1)} fusion(bf16[128,1024]{1,0:T(8,128)(2,1)} %param.5, s32[]{:T(128)S(6)} %select_n.214), kind=kLoop, calls=%fused_computation.42 | loop fusion | flops 262144 | bytes 262148 | tf_op jit(solution)/shard_map/max | solution.py:69
  1.7 5.1 %collective-permute-start.2 = (bf16[128,512]{1,0:T(8,128)(2,1)S(1)}, bf16[128,512]{1,0:T(8,128)(2,1)S(1)}, u32[]{:S(2)}, u32[]{:S(2)}) collective-permute-start(bf16[128,512]{1,0:T(8,128)(2,1)S(1)} %dynamic-slice_maximum_fusion), channel_id=1, source_target_pairs={{0,24},{2,26},{4,28},{6,30},{8,16},{10,18},{12,20},{14,22},{16,8},... | collective-permute-start | bytes 393224 | tf_op jit(solution)/shard_map/ppermute | solution.py:32
  6.9 0.7 %add_bitcast_fusion = s32[8]{0:T(128)S(1)} fusion(s32[1,8]{1,0:T(1,128)} %param.7, s32[]{:T(128)S(6)} %shift_right_arithmetic.54, s32[]{:T(128)S(6)} %and.60), kind=kLoop, calls=%fused_computation.94 | loop fusion | flops 56 | bytes 72 | tf_op jit(solution)/shard_map/eq | solution.py:75
  7.6 0.9 %slice_bitcast_fusion.9 = (bf16[128,128]{1,0:T(8,128)(2,1)S(1)}, bf16[128,128]{1,0:T(8,128)(2,1)S(1)}, bf16[128,128]{1,0:T(8,128)(2,1)S(1)}, bf16[128,128]{1,0:T...) fusion(bf16[1,8,128,128]{3,2,1,0:T(8,128)(2,1)} %param.6), kind=kLoop, calls=%fused_computation.75 | loop fusion | bytes 524288 | tf_op jit(solution)/shard_map/jit(_where)/broadcast_in_dim | solution.py:78
  8.7 2.5 %collective-permute-start.5 = (bf16[2,128,128]{2,1,0:T(8,128)(2,1)S(1)}, bf16[2,128,128]{2,1,0:T(8,128)(2,1)S(1)}, u32[]{:S(2)}, u32[]{:S(2)}) collective-permute-start(bf16[2,128,128]{2,1,0:T(8,128)(2,1)S(1)} %get-tuple-element.31), channel_id=1, source_target_pairs={{0,6},{2,4},{4,2},{6,0},{8,14},{10,12},{12,10},{14,8},{16,22},{18,... | collective-permute-start | bytes 196616 | tf_op jit(solution)/shard_map/ppermute | solution.py:28
  12.4 1.7 %collective-permute-done.5 = bf16[2,128,128]{2,1,0:T(8,128)(2,1)S(1)} collective-permute-done((bf16[2,128,128]{2,1,0:T(8,128)(2,1)S(1)}, bf16[2,128,128]{2,1,0:T(8,128)(2,1)S(1)}, u32[]{:S(2)}, u32[]{:S(2)}) %collective-permute-start.5) | collective-permute-done | bytes 65568 | tf_op jit(solution)/shard_map/ppermute | solution.py:28
  14.1 0.6 %collective-permute-start = (bf16[128,512]{1,0:T(8,128)(2,1)S(1)}, bf16[128,512]{1,0:T(8,128)(2,1)S(1)}, u32[]{:S(2)}, u32[]{:S(2)}) collective-permute-start(bf16[128,512]{1,0:T(8,128)(2,1)S(1)} %dynamic-slice_maximum_fusion), channel_id=1, source_target_pairs={{0,8},{2,10},{4,12},{6,14},{8,0},{10,2},{12,4},{14,6},{16,24},{18,... | collective-permute-start | bytes 393224 | tf_op jit(solution)/shard_map/ppermute | solution.py:32
  14.7 0.8 %collective-permute-done.4 = bf16[2,128,128]{2,1,0:T(8,128)(2,1)S(1)} collective-permute-done((bf16[2,128,128]{2,1,0:T(8,128)(2,1)S(1)}, bf16[2,128,128]{2,1,0:T(8,128)(2,1)S(1)}, u32[]{:S(2)}, u32[]{:S(2)}) %collective-permute-start.4) | collective-permute-done | bytes 65568 | tf_op jit(solution)/shard_map/ppermute | solution.py:28
  15.5 1.8 %collective-permute-start.14 = (bf16[128,512]{1,0:T(8,128)(2,1)S(1)}, bf16[128,512]{1,0:T(8,128)(2,1)S(1)}, u32[]{:S(2)}, u32[]{:S(2)}) collective-permute-start(bf16[128,512]{1,0:T(8,128)(2,1)S(1)} %constant_dynamic-slice_fusion), channel_id=1, source_target_pairs={{0,6},{2,4},{4,2},{6,0},{8,14},{10,12},{12,10},{14,8},{16,22},{18,... | collective-permute-start | bytes 393224 | tf_op jit(solution)/shard_map/ppermute | solution.py:28
  17.3 1.1 %collective-permute-start.13 = (bf16[128,512]{1,0:T(8,128)(2,1)S(1)}, bf16[128,512]{1,0:T(8,128)(2,1)S(1)}, u32[]{:S(2)}, u32[]{:S(2)}) collective-permute-start(bf16[128,512]{1,0:T(8,128)(2,1)S(1)} %constant_dynamic-slice_fusion), channel_id=1, source_target_pairs={{0,4},{2,6},{4,0},{6,2},{8,12},{10,14},{12,8},{14,10},{16,20},{18,... | collective-permute-start | bytes 393224 | tf_op jit(solution)/shard_map/ppermute | solution.py:28
  18.5 2.2 %all-gather = bf16[16,128,128]{2,1,0:T(8,128)(2,1)S(1)} all-gather(bf16[8,128,128]{2,1,0:T(8,128)(2,1)S(1)} %pad_maximum_fusion.1), channel_id=2, replica_groups=mesh['blk'=16,'rep'=2] {'rep'}, dimensions={0}, use_global_device_ids=true | all-gather | bytes 786432 | tf_op jit(solution)/shard_map/all_gather | solution.py:82
  20.9 0.6 %collective-permute-start.12 = (bf16[128,512]{1,0:T(8,128)(2,1)S(1)}, bf16[128,512]{1,0:T(8,128)(2,1)S(1)}, u32[]{:S(2)}, u32[]{:S(2)}) collective-permute-start(bf16[128,512]{1,0:T(8,128)(2,1)S(1)} %constant_dynamic-slice_fusion), channel_id=1, source_target_pairs={{0,2},{2,0},{4,6},{6,4},{8,10},{10,8},{12,14},{14,12},{16,18},{18,... | collective-permute-start | bytes 393224 | tf_op jit(solution)/shard_map/ppermute | solution.py:28
  22.1 1.5 %collective-permute-start.7 = (bf16[128,512]{1,0:T(8,128)(2,1)S(1)}, bf16[128,512]{1,0:T(8,128)(2,1)S(1)}, u32[]{:S(2)}, u32[]{:S(2)}) collective-permute-start(bf16[128,512]{1,0:T(8,128)(2,1)S(1)} %pad_maximum_fusion.3), channel_id=1, source_target_pairs={{0,4},{2,6},{4,0},{6,2},{8,12},{10,14},{12,8},{14,10},{16,20},{18,... | collective-permute-start | bytes 393224 | tf_op jit(solution)/shard_map/ppermute | solution.py:28
  23.7 1.0 %collective-permute-start.6 = (bf16[128,512]{1,0:T(8,128)(2,1)S(1)}, bf16[128,512]{1,0:T(8,128)(2,1)S(1)}, u32[]{:S(2)}, u32[]{:S(2)}) collective-permute-start(bf16[128,512]{1,0:T(8,128)(2,1)S(1)} %pad_maximum_fusion.2), channel_id=1, source_target_pairs={{0,2},{2,0},{4,6},{6,4},{8,10},{10,8},{12,14},{14,12},{16,18},{18,... | collective-permute-start | bytes 393224 | tf_op jit(solution)/shard_map/ppermute | solution.py:28
  24.7 1.2 %collective-permute-start.8 = (bf16[128,512]{1,0:T(8,128)(2,1)S(1)}, bf16[128,512]{1,0:T(8,128)(2,1)S(1)}, u32[]{:S(2)}, u32[]{:S(2)}) collective-permute-start(bf16[128,512]{1,0:T(8,128)(2,1)S(1)} %pad_maximum_fusion.4), channel_id=1, source_target_pairs={{0,6},{2,4},{4,2},{6,0},{8,14},{10,12},{12,10},{14,8},{16,22},{18,... | collective-permute-start | bytes 393224 | tf_op jit(solution)/shard_map/ppermute | solution.py:28
  25.9 1.1 %collective-permute-done.12 = bf16[128,512]{1,0:T(8,128)(2,1)S(1)} collective-permute-done((bf16[128,512]{1,0:T(8,128)(2,1)S(1)}, bf16[128,512]{1,0:T(8,128)(2,1)S(1)}, u32[]{:S(2)}, u32[]{:S(2)}) %collective-permute-start.12) | collective-permute-done | bytes 131104 | tf_op jit(solution)/shard_map/ppermute | solution.py:28
  27.5 1.0 %collective-permute-start.17 = (bf16[512,128]{1,0:T(8,128)(2,1)S(1)}, bf16[512,128]{1,0:T(8,128)(2,1)S(1)}, u32[]{:S(2)}, u32[]{:S(2)}) collective-permute-start(bf16[512,128]{1,0:T(8,128)(2,1)S(1)} %get-tuple-element.3), channel_id=1, source_target_pairs={{0,8},{2,10},{4,12},{6,14},{8,0},{10,2},{12,4},{14,6},{16,24},{18,... | collective-permute-start | bytes 393224 | tf_op jit(solution)/shard_map/ppermute | solution.py:32
  28.6 2.8 %collective-permute-start.19 = (bf16[512,128]{1,0:T(8,128)(2,1)S(1)}, bf16[512,128]{1,0:T(8,128)(2,1)S(1)}, u32[]{:S(2)}, u32[]{:S(2)}) collective-permute-start(bf16[512,128]{1,0:T(8,128)(2,1)S(1)} %get-tuple-element.4), channel_id=1, source_target_pairs={{0,24},{2,26},{4,28},{6,30},{8,16},{10,18},{12,20},{14,22},{16,8},... | collective-permute-start | bytes 393224 | tf_op jit(solution)/shard_map/ppermute | solution.py:32
  31.6 0.8 %collective-permute-done.8 = bf16[128,512]{1,0:T(8,128)(2,1)S(1)} collective-permute-done((bf16[128,512]{1,0:T(8,128)(2,1)S(1)}, bf16[128,512]{1,0:T(8,128)(2,1)S(1)}, u32[]{:S(2)}, u32[]{:S(2)}) %collective-permute-start.8) | collective-permute-done | bytes 131104 | tf_op jit(solution)/shard_map/ppermute | solution.py:28
  32.5 2.0 %all_gather.11 = bf16[256,512]{1,0:T(8,128)(2,1)S(1)} all-gather(bf16[128,512]{1,0:T(8,128)(2,1)S(1)} %fusion.16), channel_id=1, replica_groups=mesh['blk'=16,'rep'=2] {'rep'}, dimensions={0}, use_global_device_ids=true | all-gather | bytes 393216 | tf_op jit(solution)/shard_map/all_gather | solution.py:115
  35.2 1.3 %collective-permute-start.15 = (bf16[128,512]{1,0:T(8,128)(2,1)S(1)}, bf16[128,512]{1,0:T(8,128)(2,1)S(1)}, u32[]{:S(2)}, u32[]{:S(2)}) collective-permute-start(bf16[128,512]{1,0:T(8,128)(2,1)S(1)} %pad_maximum_fusion.5), channel_id=1, source_target_pairs={{0,8},{2,10},{4,12},{6,14},{8,0},{10,2},{12,4},{14,6},{16,24},{18,... | collective-permute-start | bytes 393224 | tf_op jit(solution)/shard_map/ppermute | solution.py:32
  36.5 1.1 %collective-permute-start.9 = (bf16[128,512]{1,0:T(8,128)(2,1)S(1)}, bf16[128,512]{1,0:T(8,128)(2,1)S(1)}, u32[]{:S(2)}, u32[]{:S(2)}) collective-permute-start(bf16[128,512]{1,0:T(8,128)(2,1)S(1)} %get-tuple-element.8), channel_id=1, source_target_pairs={{0,2},{2,0},{4,6},{6,4},{8,10},{10,8},{12,14},{14,12},{16,18},{18,... | collective-permute-start | bytes 393224 | tf_op jit(solution)/shard_map/ppermute | solution.py:28
  37.7 1.4 %collective-permute-start.11 = (bf16[128,512]{1,0:T(8,128)(2,1)S(1)}, bf16[128,512]{1,0:T(8,128)(2,1)S(1)}, u32[]{:S(2)}, u32[]{:S(2)}) collective-permute-start(bf16[128,512]{1,0:T(8,128)(2,1)S(1)} %get-tuple-element.9), channel_id=1, source_target_pairs={{0,6},{2,4},{4,2},{6,0},{8,14},{10,12},{12,10},{14,8},{16,22},{18,... | collective-permute-start | bytes 393224 | tf_op jit(solution)/shard_map/ppermute | solution.py:28
  39.1 1.0 %collective-permute-start.10 = (bf16[128,512]{1,0:T(8,128)(2,1)S(1)}, bf16[128,512]{1,0:T(8,128)(2,1)S(1)}, u32[]{:S(2)}, u32[]{:S(2)}) collective-permute-start(bf16[128,512]{1,0:T(8,128)(2,1)S(1)} %get-tuple-element.10), channel_id=1, source_target_pairs={{0,4},{2,6},{4,0},{6,2},{8,12},{10,14},{12,8},{14,10},{16,20},{18,... | collective-permute-start | bytes 393224 | tf_op jit(solution)/shard_map/ppermute | solution.py:28
  40.1 2.2 %collective-permute-done.18 = bf16[512,128]{1,0:T(8,128)(2,1)S(1)} collective-permute-done((bf16[512,128]{1,0:T(8,128)(2,1)S(1)}, bf16[512,128]{1,0:T(8,128)(2,1)S(1)}, u32[]{:S(2)}, u32[]{:S(2)}) %collective-permute-start.18) | collective-permute-done | bytes 131104 | tf_op jit(solution)/shard_map/ppermute | solution.py:32
  43.0 2.1 %collective-permute-done.11 = bf16[128,512]{1,0:T(8,128)(2,1)S(1)} collective-permute-done((bf16[128,512]{1,0:T(8,128)(2,1)S(1)}, bf16[128,512]{1,0:T(8,128)(2,1)S(1)}, u32[]{:S(2)}, u32[]{:S(2)}) %collective-permute-start.11) | collective-permute-done | bytes 131104 | tf_op jit(solution)/shard_map/ppermute | solution.py:28
  45.2 1.5 %collective-permute-done.10 = bf16[128,512]{1,0:T(8,128)(2,1)S(1)} collective-permute-done((bf16[128,512]{1,0:T(8,128)(2,1)S(1)}, bf16[128,512]{1,0:T(8,128)(2,1)S(1)}, u32[]{:S(2)}, u32[]{:S(2)}) %collective-permute-start.10) | collective-permute-done | bytes 131104 | tf_op jit(solution)/shard_map/ppermute | solution.py:28
  46.7 3.0 %collective-permute-start.16 = (bf16[64,512]{1,0:T(8,128)(2,1)S(1)}, bf16[64,512]{1,0:T(8,128)(2,1)S(1)}, u32[]{:S(2)}, u32[]{:S(2)}) collective-permute-start(bf16[64,512]{1,0:T(8,128)(2,1)S(1)} %fusion.24), channel_id=1, source_target_pairs={{0,16},{2,18},{4,20},{6,22},{8,24},{10,26},{12,28},{14,30},{16,0},... | collective-permute-start | bytes 196616 | tf_op jit(solution)/shard_map/ppermute | solution.py:32
  49.6 0.7 %add_convert_fusion = bf16[128,512]{1,0:T(8,128)(2,1)} fusion(bf16[128,512]{1,0:T(8,128)(2,1)S(1)} %collective-permute-done.11, bf16[128,512]{1,0:T(8,128)(2,1)S(1)} %collective-permute-done.10, bf16[128,512]{1,0:T(8,128)(2,1)S(1)} %collective-permute-done.9, bf16[512,512]{1,0:T(8,128)(2,1)S(1)} %convolution_convert_fusion.1), kind=kLoop, calls=%fused_computation.28 | loop fusion | flops 524288 | bytes 655360 | tf_op jit(solution)/shard_map/convert_element_type | solution.py:131
  50.4 1.1 %select_convert_fusion = bf16[128,512]{1,0:T(8,128)(2,1)} fusion(bf16[128,512]{1,0:T(8,128)(2,1)S(1)} %collective-permute-done.20, bf16[128,1024]{1,0:T(8,128)(2,1)S(1)} %copy-done.1, s32[]{:T(128)S(6)} %select_n.214, bf16[512,128]{1,0:T(8,128)(2,1)S(1)} %fusion.13, bf16[2,512,1024]{2,1,0:T(8,128)(2,1)S(1)} %bitcast.116, s32[]{:T(128)S(6)} %select_n.279, ...), kind=kOutput, calls=%fused_computation.27 | convolution fusion | flops 67567616 | bytes 1048588 | tf_op jit(solution)/shard_map/dot_general | solution.py:55
  51.5 1.1 %collective-permute-done.16 = bf16[64,512]{1,0:T(8,128)(2,1)S(1)} collective-permute-done((bf16[64,512]{1,0:T(8,128)(2,1)S(1)}, bf16[64,512]{1,0:T(8,128)(2,1)S(1)}, u32[]{:S(2)}, u32[]{:S(2)}) %collective-permute-start.16) | collective-permute-done | bytes 65568 | tf_op jit(solution)/shard_map/ppermute | solution.py:32
  52.6 0.7 %fusion.19 = f32[64,512]{1,0:T(8,128)} fusion(bf16[64,512]{1,0:T(8,128)(2,1)S(1)} %collective-permute-done.16, f32[4,64,512]{2,1,0:T(8,128)S(1)} %bitcast.124, s32[]{:T(128)S(6)} %select_n.271, bf16[128,512]{1,0:T(8,128)(2,1)S(1)} %collective-permute-done.15), kind=kLoop, calls=%fused_computation.39 | loop fusion | flops 131072 | bytes 393220 | tf_op jit(solution)/shard_map/add | solution.py:45
  (56 shorter events, 4.5 us)
Async XLA Ops:
  0.6 11.7 %copy-start = (bf16[1024,1024]{1,0:T(8,128)(2,1)S(1)}, bf16[1024,1024]{1,0:T(8,128)(2,1)}, u32[]{:S(2)}) copy-start(bf16[1024,1024]{1,0:T(8,128)(2,1)} %param.8) | copy-start | bytes 6291460
  0.6 11.7 %copy-start.2 = (bf16[128,1024]{1,0:T(8,128)(2,1)S(1)}, bf16[128,1024]{1,0:T(8,128)(2,1)}, u32[]{:S(2)}) copy-start(bf16[128,1024]{1,0:T(8,128)(2,1)} %param.9) | copy-start | bytes 786436
  1.7 19.1 %collective-permute-start.2 = (bf16[128,512]{1,0:T(8,128)(2,1)S(1)}, bf16[128,512]{1,0:T(8,128)(2,1)S(1)}, u32[]{:S(2)}, u32[]{:S(2)}) collective-permute-start(bf16[128,512]{1,0:T(8,128)(2,1)S(1)} %dynamic-slice_maximum_fusion), channel_id=1, source_target_pairs={{0,24},{2,26},{4,28},{6,30},{8,16},{10,18},{12,20},{14,22},{16,8},... | collective-permute-start | bytes 393224 | tf_op jit(solution)/shard_map/ppermute | solution.py:32
  6.9 14.6 %collective-permute-start.1 = (bf16[128,512]{1,0:T(8,128)(2,1)S(1)}, bf16[128,512]{1,0:T(8,128)(2,1)S(1)}, u32[]{:S(2)}, u32[]{:S(2)}) collective-permute-start(bf16[128,512]{1,0:T(8,128)(2,1)S(1)} %dynamic-slice_maximum_fusion), channel_id=1, source_target_pairs={{0,16},{2,18},{4,20},{6,22},{8,24},{10,26},{12,28},{14,30},{16,0},... | collective-permute-start | bytes 393224 | tf_op jit(solution)/shard_map/ppermute | solution.py:32
  8.7 5.3 %collective-permute-start.5 = (bf16[2,128,128]{2,1,0:T(8,128)(2,1)S(1)}, bf16[2,128,128]{2,1,0:T(8,128)(2,1)S(1)}, u32[]{:S(2)}, u32[]{:S(2)}) collective-permute-start(bf16[2,128,128]{2,1,0:T(8,128)(2,1)S(1)} %get-tuple-element.31), channel_id=1, source_target_pairs={{0,6},{2,4},{4,2},{6,0},{8,14},{10,12},{12,10},{14,8},{16,22},{18,... | collective-permute-start | bytes 196616 | tf_op jit(solution)/shard_map/ppermute | solution.py:28
  11.2 4.3 %collective-permute-start.4 = (bf16[2,128,128]{2,1,0:T(8,128)(2,1)S(1)}, bf16[2,128,128]{2,1,0:T(8,128)(2,1)S(1)}, u32[]{:S(2)}, u32[]{:S(2)}) collective-permute-start(bf16[2,128,128]{2,1,0:T(8,128)(2,1)S(1)} %get-tuple-element.32), channel_id=1, source_target_pairs={{0,4},{2,6},{4,0},{6,2},{8,12},{10,14},{12,8},{14,10},{16,20},{18,... | collective-permute-start | bytes 196616 | tf_op jit(solution)/shard_map/ppermute | solution.py:28
  11.8 5.6 %collective-permute-start.3 = (bf16[2,128,128]{2,1,0:T(8,128)(2,1)S(1)}, bf16[2,128,128]{2,1,0:T(8,128)(2,1)S(1)}, u32[]{:S(2)}, u32[]{:S(2)}) collective-permute-start(bf16[2,128,128]{2,1,0:T(8,128)(2,1)S(1)} %get-tuple-element.33), channel_id=1, source_target_pairs={{0,2},{2,0},{4,6},{6,4},{8,10},{10,8},{12,14},{14,12},{16,18},{18,... | collective-permute-start | bytes 196616 | tf_op jit(solution)/shard_map/ppermute | solution.py:28
  14.1 7.4 %collective-permute-start = (bf16[128,512]{1,0:T(8,128)(2,1)S(1)}, bf16[128,512]{1,0:T(8,128)(2,1)S(1)}, u32[]{:S(2)}, u32[]{:S(2)}) collective-permute-start(bf16[128,512]{1,0:T(8,128)(2,1)S(1)} %dynamic-slice_maximum_fusion), channel_id=1, source_target_pairs={{0,8},{2,10},{4,12},{6,14},{8,0},{10,2},{12,4},{14,6},{16,24},{18,... | collective-permute-start | bytes 393224 | tf_op jit(solution)/shard_map/ppermute | solution.py:32
  15.5 9.2 %collective-permute-start.14 = (bf16[128,512]{1,0:T(8,128)(2,1)S(1)}, bf16[128,512]{1,0:T(8,128)(2,1)S(1)}, u32[]{:S(2)}, u32[]{:S(2)}) collective-permute-start(bf16[128,512]{1,0:T(8,128)(2,1)S(1)} %constant_dynamic-slice_fusion), channel_id=1, source_target_pairs={{0,6},{2,4},{4,2},{6,0},{8,14},{10,12},{12,10},{14,8},{16,22},{18,... | collective-permute-start | bytes 393224 | tf_op jit(solution)/shard_map/ppermute | solution.py:28
  17.3 8.6 %collective-permute-start.13 = (bf16[128,512]{1,0:T(8,128)(2,1)S(1)}, bf16[128,512]{1,0:T(8,128)(2,1)S(1)}, u32[]{:S(2)}, u32[]{:S(2)}) collective-permute-start(bf16[128,512]{1,0:T(8,128)(2,1)S(1)} %constant_dynamic-slice_fusion), channel_id=1, source_target_pairs={{0,4},{2,6},{4,0},{6,2},{8,12},{10,14},{12,8},{14,10},{16,20},{18,... | collective-permute-start | bytes 393224 | tf_op jit(solution)/shard_map/ppermute | solution.py:28
  20.9 6.1 %collective-permute-start.12 = (bf16[128,512]{1,0:T(8,128)(2,1)S(1)}, bf16[128,512]{1,0:T(8,128)(2,1)S(1)}, u32[]{:S(2)}, u32[]{:S(2)}) collective-permute-start(bf16[128,512]{1,0:T(8,128)(2,1)S(1)} %constant_dynamic-slice_fusion), channel_id=1, source_target_pairs={{0,2},{2,0},{4,6},{6,4},{8,10},{10,8},{12,14},{14,12},{16,18},{18,... | collective-permute-start | bytes 393224 | tf_op jit(solution)/shard_map/ppermute | solution.py:28
  22.1 9.2 %collective-permute-start.7 = (bf16[128,512]{1,0:T(8,128)(2,1)S(1)}, bf16[128,512]{1,0:T(8,128)(2,1)S(1)}, u32[]{:S(2)}, u32[]{:S(2)}) collective-permute-start(bf16[128,512]{1,0:T(8,128)(2,1)S(1)} %pad_maximum_fusion.3), channel_id=1, source_target_pairs={{0,4},{2,6},{4,0},{6,2},{8,12},{10,14},{12,8},{14,10},{16,20},{18,... | collective-permute-start | bytes 393224 | tf_op jit(solution)/shard_map/ppermute | solution.py:28
  23.7 7.9 %collective-permute-start.6 = (bf16[128,512]{1,0:T(8,128)(2,1)S(1)}, bf16[128,512]{1,0:T(8,128)(2,1)S(1)}, u32[]{:S(2)}, u32[]{:S(2)}) collective-permute-start(bf16[128,512]{1,0:T(8,128)(2,1)S(1)} %pad_maximum_fusion.2), channel_id=1, source_target_pairs={{0,2},{2,0},{4,6},{6,4},{8,10},{10,8},{12,14},{14,12},{16,18},{18,... | collective-permute-start | bytes 393224 | tf_op jit(solution)/shard_map/ppermute | solution.py:28
  24.7 7.7 %collective-permute-start.8 = (bf16[128,512]{1,0:T(8,128)(2,1)S(1)}, bf16[128,512]{1,0:T(8,128)(2,1)S(1)}, u32[]{:S(2)}, u32[]{:S(2)}) collective-permute-start(bf16[128,512]{1,0:T(8,128)(2,1)S(1)} %pad_maximum_fusion.4), channel_id=1, source_target_pairs={{0,6},{2,4},{4,2},{6,0},{8,14},{10,12},{12,10},{14,8},{16,22},{18,... | collective-permute-start | bytes 393224 | tf_op jit(solution)/shard_map/ppermute | solution.py:28
  27.5 10.1 %collective-permute-start.17 = (bf16[512,128]{1,0:T(8,128)(2,1)S(1)}, bf16[512,128]{1,0:T(8,128)(2,1)S(1)}, u32[]{:S(2)}, u32[]{:S(2)}) collective-permute-start(bf16[512,128]{1,0:T(8,128)(2,1)S(1)} %get-tuple-element.3), channel_id=1, source_target_pairs={{0,8},{2,10},{4,12},{6,14},{8,0},{10,2},{12,4},{14,6},{16,24},{18,... | collective-permute-start | bytes 393224 | tf_op jit(solution)/shard_map/ppermute | solution.py:32
  28.6 10.5 %collective-permute-start.19 = (bf16[512,128]{1,0:T(8,128)(2,1)S(1)}, bf16[512,128]{1,0:T(8,128)(2,1)S(1)}, u32[]{:S(2)}, u32[]{:S(2)}) collective-permute-start(bf16[512,128]{1,0:T(8,128)(2,1)S(1)} %get-tuple-element.4), channel_id=1, source_target_pairs={{0,24},{2,26},{4,28},{6,30},{8,16},{10,18},{12,20},{14,22},{16,8},... | collective-permute-start | bytes 393224 | tf_op jit(solution)/shard_map/ppermute | solution.py:32
  31.4 10.9 %collective-permute-start.18 = (bf16[512,128]{1,0:T(8,128)(2,1)S(1)}, bf16[512,128]{1,0:T(8,128)(2,1)S(1)}, u32[]{:S(2)}, u32[]{:S(2)}) collective-permute-start(bf16[512,128]{1,0:T(8,128)(2,1)S(1)} %get-tuple-element.5), channel_id=1, source_target_pairs={{0,16},{2,18},{4,20},{6,22},{8,24},{10,26},{12,28},{14,30},{16,0},... | collective-permute-start | bytes 393224 | tf_op jit(solution)/shard_map/ppermute | solution.py:32
  35.1 15.2 %copy-start.1 = (bf16[128,1024]{1,0:T(8,128)(2,1)S(1)}, bf16[128,1024]{1,0:T(8,128)(2,1)}, u32[]{:S(2)}) copy-start(bf16[128,1024]{1,0:T(8,128)(2,1)} %param.5) | copy-start | bytes 786436
  35.2 7.8 %collective-permute-start.15 = (bf16[128,512]{1,0:T(8,128)(2,1)S(1)}, bf16[128,512]{1,0:T(8,128)(2,1)S(1)}, u32[]{:S(2)}, u32[]{:S(2)}) collective-permute-start(bf16[128,512]{1,0:T(8,128)(2,1)S(1)} %pad_maximum_fusion.5), channel_id=1, source_target_pairs={{0,8},{2,10},{4,12},{6,14},{8,0},{10,2},{12,4},{14,6},{16,24},{18,... | collective-permute-start | bytes 393224 | tf_op jit(solution)/shard_map/ppermute | solution.py:32
  36.5 6.5 %collective-permute-start.9 = (bf16[128,512]{1,0:T(8,128)(2,1)S(1)}, bf16[128,512]{1,0:T(8,128)(2,1)S(1)}, u32[]{:S(2)}, u32[]{:S(2)}) collective-permute-start(bf16[128,512]{1,0:T(8,128)(2,1)S(1)} %get-tuple-element.8), channel_id=1, source_target_pairs={{0,2},{2,0},{4,6},{6,4},{8,10},{10,8},{12,14},{14,12},{16,18},{18,... | collective-permute-start | bytes 393224 | tf_op jit(solution)/shard_map/ppermute | solution.py:28
  37.7 7.5 %collective-permute-start.11 = (bf16[128,512]{1,0:T(8,128)(2,1)S(1)}, bf16[128,512]{1,0:T(8,128)(2,1)S(1)}, u32[]{:S(2)}, u32[]{:S(2)}) collective-permute-start(bf16[128,512]{1,0:T(8,128)(2,1)S(1)} %get-tuple-element.9), channel_id=1, source_target_pairs={{0,6},{2,4},{4,2},{6,0},{8,14},{10,12},{12,10},{14,8},{16,22},{18,... | collective-permute-start | bytes 393224 | tf_op jit(solution)/shard_map/ppermute | solution.py:28
  39.1 7.5 %collective-permute-start.10 = (bf16[128,512]{1,0:T(8,128)(2,1)S(1)}, bf16[128,512]{1,0:T(8,128)(2,1)S(1)}, u32[]{:S(2)}, u32[]{:S(2)}) collective-permute-start(bf16[128,512]{1,0:T(8,128)(2,1)S(1)} %get-tuple-element.10), channel_id=1, source_target_pairs={{0,4},{2,6},{4,0},{6,2},{8,12},{10,14},{12,8},{14,10},{16,20},{18,... | collective-permute-start | bytes 393224 | tf_op jit(solution)/shard_map/ppermute | solution.py:28
  42.8 7.5 %collective-permute-start.20 = (bf16[128,512]{1,0:T(8,128)(2,1)S(1)}, bf16[128,512]{1,0:T(8,128)(2,1)S(1)}, u32[]{:S(2)}, u32[]{:S(2)}) collective-permute-start(bf16[128,512]{1,0:T(8,128)(2,1)S(1)} %convolution_convert_fusion.2), channel_id=1, source_target_pairs={{0,1},{1,0},{2,3},{3,2},{4,5},{5,4},{6,7},{7,6},{8,9},{9,8},{10,11... | collective-permute-start | bytes 393224 | tf_op jit(solution)/shard_map/ppermute | solution.py:52
  46.7 5.9 %collective-permute-start.16 = (bf16[64,512]{1,0:T(8,128)(2,1)S(1)}, bf16[64,512]{1,0:T(8,128)(2,1)S(1)}, u32[]{:S(2)}, u32[]{:S(2)}) collective-permute-start(bf16[64,512]{1,0:T(8,128)(2,1)S(1)} %fusion.24), channel_id=1, source_target_pairs={{0,16},{2,18},{4,20},{6,22},{8,24},{10,26},{12,28},{14,30},{16,0},... | collective-permute-start | bytes 196616 | tf_op jit(solution)/shard_map/ppermute | solution.py:32

commit v27 on v26

--- a/solution.py
+++ b/solution.py
@@ -126,7 +126,7 @@
     grad_weight = halved(
         [lax.dynamic_index_in_dim(by_outer, outer_pos ^ t, 0, keepdims=False) for t in turns],
         along_outer,
-        out_got[1:],
+        out_got[1:2],
     )
     out_part = sum(part.astype(jnp.float32) for part in out_got).astype(bf16)
 

time: 53.5 us -> 55.3 us (1.034)
  waiting for transfers between devices: 11.5 us -> 16.1 us
  starting transfers between devices: 28.5 us -> 25.6 us
    ppermute x12, waiting for transfers between devices: 7.98 us -> 11.5 us  [along_inner(): return lax.ppermute(value, 'blk', pairs) if turn else value]
    ppermute x8, starting transfers between devices: 14.1 us -> 11.2 us  [along_outer(): return lax.ppermute(value, 'blk', pairs) if turn else value]
    ppermute x8, waiting for transfers between devices: 3.47 us -> 4.67 us  [along_outer(): return lax.ppermute(value, 'blk', pairs) if turn else value]
  transfers between devices with their start and end apart: 21 -> 21, of which waited for: 9 -> 8; matrix products, arithmetic and copies ran while one was open for 12% -> 12% of each run, Pallas kernels for 0% -> 0%
where the time goes in v27:
time: 55.3 us; the launch traced here: 55 us
  starting transfers between devices  25.6 us (46%)
  waiting for transfers between devices  16.1 us (29%)
  blocking collectives  4.18 us (8%)
  other arithmetic  3.86 us (7%)
  matrix products  3.09 us (6%)
  local copies, waits for them, and re-layouts  1.24 us (2%)
  between operations  0.93 us (2%)
    ppermute x12, starting transfers between devices, along_inner(): return lax.ppermute(value, 'blk', pairs) if turn else value  14.3 us
    ppermute x12, waiting for transfers between devices, along_inner(): return lax.ppermute(value, 'blk', pairs) if turn else value  11.5 us
    ppermute x8, starting transfers between devices, along_outer(): return lax.ppermute(value, 'blk', pairs) if turn else value  11.2 us
    ppermute x8, waiting for transfers between devices, along_outer(): return lax.ppermute(value, 'blk', pairs) if turn else value  4.67 us
    dot_general x6, matrix products, dot(): lax.dot_general(lhs, rhs, (dims, ((), ())), preferred_element_type=jnp.fl...  3.09 us
    all_gather x1, blocking collectives, shards(): everyone = lax.all_gather(jnp.concatenate(arrived, 0), 'rep', axis=0)  2.18 us
    all_gather x1, blocking collectives, shards(): lax.all_gather(mixed_cols.astype(bf16), 'rep', axis=0, tiled=True)  1.99 us
  transfers between devices with their start and end apart: 21, of which 8 were waited for; matrix products, arithmetic and copies ran while one was open for 12% of the time, Pallas kernels for 0%

profile of v27, /device:TPU:0, one launch (start us, length us, event | category | flops | bytes accessed | tf_op | source)
XLA Modules:
  0.0 55.0 jit_solution(11771117559196055665)
XLA Ops:
  0.7 1.1 %dynamic-slice_maximum_fusion = bf16[128,512]{1,0:T(8,128)(2,1)S(1)} fusion(bf16[128,1024]{1,0:T(8,128)(2,1)} %param.5, s32[]{:T(128)S(6)} %select_n.214), kind=kLoop, calls=%fused_computation.42 | loop fusion | flops 262144 | bytes 262148 | tf_op jit(solution)/shard_map/max | solution.py:69
  1.7 5.1 %collective-permute-start.2 = (bf16[128,512]{1,0:T(8,128)(2,1)S(1)}, bf16[128,512]{1,0:T(8,128)(2,1)S(1)}, u32[]{:S(2)}, u32[]{:S(2)}) collective-permute-start(bf16[128,512]{1,0:T(8,128)(2,1)S(1)} %dynamic-slice_maximum_fusion), channel_id=1, source_target_pairs={{0,24},{2,26},{4,28},{6,30},{8,16},{10,18},{12,20},{14,22},{16,8},... | collective-permute-start | bytes 393224 | tf_op jit(solution)/shard_map/ppermute | solution.py:32
  6.9 0.7 %add_bitcast_fusion = s32[8]{0:T(128)S(1)} fusion(s32[1,8]{1,0:T(1,128)} %param.7, s32[]{:T(128)S(6)} %shift_right_arithmetic.54, s32[]{:T(128)S(6)} %and.60), kind=kLoop, calls=%fused_computation.90 | loop fusion | flops 56 | bytes 72 | tf_op jit(solution)/shard_map/eq | solution.py:75
  7.6 0.9 %slice_bitcast_fusion.9 = (bf16[128,128]{1,0:T(8,128)(2,1)S(1)}, bf16[128,128]{1,0:T(8,128)(2,1)S(1)}, bf16[128,128]{1,0:T(8,128)(2,1)S(1)}, bf16[128,128]{1,0:T...) fusion(bf16[1,8,128,128]{3,2,1,0:T(8,128)(2,1)} %param.6), kind=kLoop, calls=%fused_computation.71 | loop fusion | bytes 524288 | tf_op jit(solution)/shard_map/jit(_where)/broadcast_in_dim | solution.py:78
  8.7 2.5 %collective-permute-start.5 = (bf16[2,128,128]{2,1,0:T(8,128)(2,1)S(1)}, bf16[2,128,128]{2,1,0:T(8,128)(2,1)S(1)}, u32[]{:S(2)}, u32[]{:S(2)}) collective-permute-start(bf16[2,128,128]{2,1,0:T(8,128)(2,1)S(1)} %get-tuple-element.31), channel_id=1, source_target_pairs={{0,6},{2,4},{4,2},{6,0},{8,14},{10,12},{12,10},{14,8},{16,22},{18,... | collective-permute-start | bytes 196616 | tf_op jit(solution)/shard_map/ppermute | solution.py:28
  11.2 0.5 collective-permute-start.4
  11.8 0.5 collective-permute-start.3
  12.4 1.7 %collective-permute-done.5 = bf16[2,128,128]{2,1,0:T(8,128)(2,1)S(1)} collective-permute-done((bf16[2,128,128]{2,1,0:T(8,128)(2,1)S(1)}, bf16[2,128,128]{2,1,0:T(8,128)(2,1)S(1)}, u32[]{:S(2)}, u32[]{:S(2)}) %collective-permute-start.5) | collective-permute-done | bytes 65568 | tf_op jit(solution)/shard_map/ppermute | solution.py:28
  14.1 0.6 %collective-permute-start = (bf16[128,512]{1,0:T(8,128)(2,1)S(1)}, bf16[128,512]{1,0:T(8,128)(2,1)S(1)}, u32[]{:S(2)}, u32[]{:S(2)}) collective-permute-start(bf16[128,512]{1,0:T(8,128)(2,1)S(1)} %dynamic-slice_maximum_fusion), channel_id=1, source_target_pairs={{0,8},{2,10},{4,12},{6,14},{8,0},{10,2},{12,4},{14,6},{16,24},{18,... | collective-permute-start | bytes 393224 | tf_op jit(solution)/shard_map/ppermute | solution.py:32
  14.7 0.8 %collective-permute-done.4 = bf16[2,128,128]{2,1,0:T(8,128)(2,1)S(1)} collective-permute-done((bf16[2,128,128]{2,1,0:T(8,128)(2,1)S(1)}, bf16[2,128,128]{2,1,0:T(8,128)(2,1)S(1)}, u32[]{:S(2)}, u32[]{:S(2)}) %collective-permute-start.4) | collective-permute-done | bytes 65568 | tf_op jit(solution)/shard_map/ppermute | solution.py:28
  15.5 1.8 %collective-permute-start.14 = (bf16[128,512]{1,0:T(8,128)(2,1)S(1)}, bf16[128,512]{1,0:T(8,128)(2,1)S(1)}, u32[]{:S(2)}, u32[]{:S(2)}) collective-permute-start(bf16[128,512]{1,0:T(8,128)(2,1)S(1)} %constant_dynamic-slice_fusion), channel_id=1, source_target_pairs={{0,6},{2,4},{4,2},{6,0},{8,14},{10,12},{12,10},{14,8},{16,22},{18,... | collective-permute-start | bytes 393224 | tf_op jit(solution)/shard_map/ppermute | solution.py:28
  17.3 1.1 %collective-permute-start.13 = (bf16[128,512]{1,0:T(8,128)(2,1)S(1)}, bf16[128,512]{1,0:T(8,128)(2,1)S(1)}, u32[]{:S(2)}, u32[]{:S(2)}) collective-permute-start(bf16[128,512]{1,0:T(8,128)(2,1)S(1)} %constant_dynamic-slice_fusion), channel_id=1, source_target_pairs={{0,4},{2,6},{4,0},{6,2},{8,12},{10,14},{12,8},{14,10},{16,20},{18,... | collective-permute-start | bytes 393224 | tf_op jit(solution)/shard_map/ppermute | solution.py:28
  18.5 2.2 %all-gather = bf16[16,128,128]{2,1,0:T(8,128)(2,1)S(1)} all-gather(bf16[8,128,128]{2,1,0:T(8,128)(2,1)S(1)} %pad_maximum_fusion.1), channel_id=2, replica_groups=mesh['blk'=16,'rep'=2] {'rep'}, dimensions={0}, use_global_device_ids=true | all-gather | bytes 786432 | tf_op jit(solution)/shard_map/all_gather | solution.py:82
  20.9 0.6 %collective-permute-start.12 = (bf16[128,512]{1,0:T(8,128)(2,1)S(1)}, bf16[128,512]{1,0:T(8,128)(2,1)S(1)}, u32[]{:S(2)}, u32[]{:S(2)}) collective-permute-start(bf16[128,512]{1,0:T(8,128)(2,1)S(1)} %constant_dynamic-slice_fusion), channel_id=1, source_target_pairs={{0,2},{2,0},{4,6},{6,4},{8,10},{10,8},{12,14},{14,12},{16,18},{18,... | collective-permute-start | bytes 393224 | tf_op jit(solution)/shard_map/ppermute | solution.py:28
  22.1 1.5 %collective-permute-start.7 = (bf16[128,512]{1,0:T(8,128)(2,1)S(1)}, bf16[128,512]{1,0:T(8,128)(2,1)S(1)}, u32[]{:S(2)}, u32[]{:S(2)}) collective-permute-start(bf16[128,512]{1,0:T(8,128)(2,1)S(1)} %pad_maximum_fusion.3), channel_id=1, source_target_pairs={{0,4},{2,6},{4,0},{6,2},{8,12},{10,14},{12,8},{14,10},{16,20},{18,... | collective-permute-start | bytes 393224 | tf_op jit(solution)/shard_map/ppermute | solution.py:28
  23.7 1.0 %collective-permute-start.6 = (bf16[128,512]{1,0:T(8,128)(2,1)S(1)}, bf16[128,512]{1,0:T(8,128)(2,1)S(1)}, u32[]{:S(2)}, u32[]{:S(2)}) collective-permute-start(bf16[128,512]{1,0:T(8,128)(2,1)S(1)} %pad_maximum_fusion.2), channel_id=1, source_target_pairs={{0,2},{2,0},{4,6},{6,4},{8,10},{10,8},{12,14},{14,12},{16,18},{18,... | collective-permute-start | bytes 393224 | tf_op jit(solution)/shard_map/ppermute | solution.py:28
  24.7 1.2 %collective-permute-start.8 = (bf16[128,512]{1,0:T(8,128)(2,1)S(1)}, bf16[128,512]{1,0:T(8,128)(2,1)S(1)}, u32[]{:S(2)}, u32[]{:S(2)}) collective-permute-start(bf16[128,512]{1,0:T(8,128)(2,1)S(1)} %pad_maximum_fusion.4), channel_id=1, source_target_pairs={{0,6},{2,4},{4,2},{6,0},{8,14},{10,12},{12,10},{14,8},{16,22},{18,... | collective-permute-start | bytes 393224 | tf_op jit(solution)/shard_map/ppermute | solution.py:28
  25.9 1.1 %collective-permute-done.12 = bf16[128,512]{1,0:T(8,128)(2,1)S(1)} collective-permute-done((bf16[128,512]{1,0:T(8,128)(2,1)S(1)}, bf16[128,512]{1,0:T(8,128)(2,1)S(1)}, u32[]{:S(2)}, u32[]{:S(2)}) %collective-permute-start.12) | collective-permute-done | bytes 131104 | tf_op jit(solution)/shard_map/ppermute | solution.py:28
  27.5 1.0 %collective-permute-start.17 = (bf16[512,128]{1,0:T(8,128)(2,1)S(1)}, bf16[512,128]{1,0:T(8,128)(2,1)S(1)}, u32[]{:S(2)}, u32[]{:S(2)}) collective-permute-start(bf16[512,128]{1,0:T(8,128)(2,1)S(1)} %get-tuple-element.3), channel_id=1, source_target_pairs={{0,8},{2,10},{4,12},{6,14},{8,0},{10,2},{12,4},{14,6},{16,24},{18,... | collective-permute-start | bytes 393224 | tf_op jit(solution)/shard_map/ppermute | solution.py:32
  28.6 2.8 %collective-permute-start.19 = (bf16[512,128]{1,0:T(8,128)(2,1)S(1)}, bf16[512,128]{1,0:T(8,128)(2,1)S(1)}, u32[]{:S(2)}, u32[]{:S(2)}) collective-permute-start(bf16[512,128]{1,0:T(8,128)(2,1)S(1)} %get-tuple-element.4), channel_id=1, source_target_pairs={{0,24},{2,26},{4,28},{6,30},{8,16},{10,18},{12,20},{14,22},{16,8},... | collective-permute-start | bytes 393224 | tf_op jit(solution)/shard_map/ppermute | solution.py:32
  31.6 0.8 %collective-permute-done.8 = bf16[128,512]{1,0:T(8,128)(2,1)S(1)} collective-permute-done((bf16[128,512]{1,0:T(8,128)(2,1)S(1)}, bf16[128,512]{1,0:T(8,128)(2,1)S(1)}, u32[]{:S(2)}, u32[]{:S(2)}) %collective-permute-start.8) | collective-permute-done | bytes 131104 | tf_op jit(solution)/shard_map/ppermute | solution.py:28
  32.5 2.0 %all_gather.11 = bf16[256,512]{1,0:T(8,128)(2,1)S(1)} all-gather(bf16[128,512]{1,0:T(8,128)(2,1)S(1)} %fusion.16), channel_id=1, replica_groups=mesh['blk'=16,'rep'=2] {'rep'}, dimensions={0}, use_global_device_ids=true | all-gather | bytes 393216 | tf_op jit(solution)/shard_map/all_gather | solution.py:115
  35.2 1.3 %collective-permute-start.15 = (bf16[128,512]{1,0:T(8,128)(2,1)S(1)}, bf16[128,512]{1,0:T(8,128)(2,1)S(1)}, u32[]{:S(2)}, u32[]{:S(2)}) collective-permute-start(bf16[128,512]{1,0:T(8,128)(2,1)S(1)} %pad_maximum_fusion.5), channel_id=1, source_target_pairs={{0,8},{2,10},{4,12},{6,14},{8,0},{10,2},{12,4},{14,6},{16,24},{18,... | collective-permute-start | bytes 393224 | tf_op jit(solution)/shard_map/ppermute | solution.py:32
  36.5 1.1 %collective-permute-start.9 = (bf16[128,512]{1,0:T(8,128)(2,1)S(1)}, bf16[128,512]{1,0:T(8,128)(2,1)S(1)}, u32[]{:S(2)}, u32[]{:S(2)}) collective-permute-start(bf16[128,512]{1,0:T(8,128)(2,1)S(1)} %get-tuple-element.8), channel_id=1, source_target_pairs={{0,2},{2,0},{4,6},{6,4},{8,10},{10,8},{12,14},{14,12},{16,18},{18,... | collective-permute-start | bytes 393224 | tf_op jit(solution)/shard_map/ppermute | solution.py:28
  37.8 4.5 %collective-permute-done.18 = bf16[512,128]{1,0:T(8,128)(2,1)S(1)} collective-permute-done((bf16[512,128]{1,0:T(8,128)(2,1)S(1)}, bf16[512,128]{1,0:T(8,128)(2,1)S(1)}, u32[]{:S(2)}, u32[]{:S(2)}) %collective-permute-start.18) | collective-permute-done | bytes 131104 | tf_op jit(solution)/shard_map/ppermute | solution.py:32
  42.9 1.5 %collective-permute-start.11 = (bf16[128,512]{1,0:T(8,128)(2,1)S(1)}, bf16[128,512]{1,0:T(8,128)(2,1)S(1)}, u32[]{:S(2)}, u32[]{:S(2)}) collective-permute-start(bf16[128,512]{1,0:T(8,128)(2,1)S(1)} %get-tuple-element.9), channel_id=1, source_target_pairs={{0,6},{2,4},{4,2},{6,0},{8,14},{10,12},{12,10},{14,8},{16,22},{18,... | collective-permute-start | bytes 393224 | tf_op jit(solution)/shard_map/ppermute | solution.py:28
  44.4 0.9 %collective-permute-start.10 = (bf16[128,512]{1,0:T(8,128)(2,1)S(1)}, bf16[128,512]{1,0:T(8,128)(2,1)S(1)}, u32[]{:S(2)}, u32[]{:S(2)}) collective-permute-start(bf16[128,512]{1,0:T(8,128)(2,1)S(1)} %get-tuple-element.10), channel_id=1, source_target_pairs={{0,4},{2,6},{4,0},{6,2},{8,12},{10,14},{12,8},{14,10},{16,20},{18,... | collective-permute-start | bytes 393224 | tf_op jit(solution)/shard_map/ppermute | solution.py:28
  45.5 4.4 %collective-permute-done.11 = bf16[128,512]{1,0:T(8,128)(2,1)S(1)} collective-permute-done((bf16[128,512]{1,0:T(8,128)(2,1)S(1)}, bf16[128,512]{1,0:T(8,128)(2,1)S(1)}, u32[]{:S(2)}, u32[]{:S(2)}) %collective-permute-start.11) | collective-permute-done | bytes 131104 | tf_op jit(solution)/shard_map/ppermute | solution.py:28
  49.8 2.7 %collective-permute-done.10 = bf16[128,512]{1,0:T(8,128)(2,1)S(1)} collective-permute-done((bf16[128,512]{1,0:T(8,128)(2,1)S(1)}, bf16[128,512]{1,0:T(8,128)(2,1)S(1)}, u32[]{:S(2)}, u32[]{:S(2)}) %collective-permute-start.10) | collective-permute-done | bytes 131104 | tf_op jit(solution)/shard_map/ppermute | solution.py:28
  52.5 0.7 %add_convert_fusion = bf16[128,512]{1,0:T(8,128)(2,1)} fusion(bf16[128,512]{1,0:T(8,128)(2,1)S(1)} %collective-permute-done.11, bf16[128,512]{1,0:T(8,128)(2,1)S(1)} %collective-permute-done.10, bf16[128,512]{1,0:T(8,128)(2,1)S(1)} %collective-permute-done.9, bf16[512,512]{1,0:T(8,128)(2,1)S(1)} %convolution_convert_fusion.1), kind=kLoop, calls=%fused_computation.28 | loop fusion | flops 524288 | bytes 655360 | tf_op jit(solution)/shard_map/convert_element_type | solution.py:131
  53.3 1.1 %select_convert_fusion = bf16[128,512]{1,0:T(8,128)(2,1)} fusion(bf16[128,512]{1,0:T(8,128)(2,1)S(1)} %collective-permute-done.20, bf16[128,1024]{1,0:T(8,128)(2,1)S(1)} %copy-done.1, s32[]{:T(128)S(6)} %select_n.214, bf16[512,128]{1,0:T(8,128)(2,1)S(1)} %fusion.13, bf16[2,512,1024]{2,1,0:T(8,128)(2,1)S(1)} %bitcast.112, s32[]{:T(128)S(6)} %select_n.279, ...), kind=kOutput, calls=%fused_computation.27 | convolution fusion | flops 67567616 | bytes 1048588 | tf_op jit(solution)/shard_map/dot_general | solution.py:55
  54.4 0.7 %fusion.19 = f32[64,512]{1,0:T(8,128)} fusion(bf16[64,512]{1,0:T(8,128)(2,1)S(1)} %collective-permute-done.16, f32[4,64,512]{2,1,0:T(8,128)S(1)} %bitcast.120, s32[]{:T(128)S(6)} %select_n.271, bf16[128,512]{1,0:T(8,128)(2,1)S(1)} %collective-permute-done.15), kind=kLoop, calls=%fused_computation.39 | loop fusion | flops 131072 | bytes 393220 | tf_op jit(solution)/shard_map/add | solution.py:45
  (56 shorter events, 3.6 us)
Async XLA Ops:
  0.6 11.7 %copy-start = (bf16[1024,1024]{1,0:T(8,128)(2,1)S(1)}, bf16[1024,1024]{1,0:T(8,128)(2,1)}, u32[]{:S(2)}) copy-start(bf16[1024,1024]{1,0:T(8,128)(2,1)} %param.8) | copy-start | bytes 6291460
  0.6 11.7 %copy-start.2 = (bf16[128,1024]{1,0:T(8,128)(2,1)S(1)}, bf16[128,1024]{1,0:T(8,128)(2,1)}, u32[]{:S(2)}) copy-start(bf16[128,1024]{1,0:T(8,128)(2,1)} %param.9) | copy-start | bytes 786436
  1.7 19.1 %collective-permute-start.2 = (bf16[128,512]{1,0:T(8,128)(2,1)S(1)}, bf16[128,512]{1,0:T(8,128)(2,1)S(1)}, u32[]{:S(2)}, u32[]{:S(2)}) collective-permute-start(bf16[128,512]{1,0:T(8,128)(2,1)S(1)} %dynamic-slice_maximum_fusion), channel_id=1, source_target_pairs={{0,24},{2,26},{4,28},{6,30},{8,16},{10,18},{12,20},{14,22},{16,8},... | collective-permute-start | bytes 393224 | tf_op jit(solution)/shard_map/ppermute | solution.py:32
  6.9 14.6 %collective-permute-start.1 = (bf16[128,512]{1,0:T(8,128)(2,1)S(1)}, bf16[128,512]{1,0:T(8,128)(2,1)S(1)}, u32[]{:S(2)}, u32[]{:S(2)}) collective-permute-start(bf16[128,512]{1,0:T(8,128)(2,1)S(1)} %dynamic-slice_maximum_fusion), channel_id=1, source_target_pairs={{0,16},{2,18},{4,20},{6,22},{8,24},{10,26},{12,28},{14,30},{16,0},... | collective-permute-start | bytes 393224 | tf_op jit(solution)/shard_map/ppermute | solution.py:32
  8.7 5.3 %collective-permute-start.5 = (bf16[2,128,128]{2,1,0:T(8,128)(2,1)S(1)}, bf16[2,128,128]{2,1,0:T(8,128)(2,1)S(1)}, u32[]{:S(2)}, u32[]{:S(2)}) collective-permute-start(bf16[2,128,128]{2,1,0:T(8,128)(2,1)S(1)} %get-tuple-element.31), channel_id=1, source_target_pairs={{0,6},{2,4},{4,2},{6,0},{8,14},{10,12},{12,10},{14,8},{16,22},{18,... | collective-permute-start | bytes 196616 | tf_op jit(solution)/shard_map/ppermute | solution.py:28
  11.2 4.3 %collective-permute-start.4 = (bf16[2,128,128]{2,1,0:T(8,128)(2,1)S(1)}, bf16[2,128,128]{2,1,0:T(8,128)(2,1)S(1)}, u32[]{:S(2)}, u32[]{:S(2)}) collective-permute-start(bf16[2,128,128]{2,1,0:T(8,128)(2,1)S(1)} %get-tuple-element.32), channel_id=1, source_target_pairs={{0,4},{2,6},{4,0},{6,2},{8,12},{10,14},{12,8},{14,10},{16,20},{18,... | collective-permute-start | bytes 196616 | tf_op jit(solution)/shard_map/ppermute | solution.py:28
  11.8 5.6 %collective-permute-start.3 = (bf16[2,128,128]{2,1,0:T(8,128)(2,1)S(1)}, bf16[2,128,128]{2,1,0:T(8,128)(2,1)S(1)}, u32[]{:S(2)}, u32[]{:S(2)}) collective-permute-start(bf16[2,128,128]{2,1,0:T(8,128)(2,1)S(1)} %get-tuple-element.33), channel_id=1, source_target_pairs={{0,2},{2,0},{4,6},{6,4},{8,10},{10,8},{12,14},{14,12},{16,18},{18,... | collective-permute-start | bytes 196616 | tf_op jit(solution)/shard_map/ppermute | solution.py:28
  14.1 7.4 %collective-permute-start = (bf16[128,512]{1,0:T(8,128)(2,1)S(1)}, bf16[128,512]{1,0:T(8,128)(2,1)S(1)}, u32[]{:S(2)}, u32[]{:S(2)}) collective-permute-start(bf16[128,512]{1,0:T(8,128)(2,1)S(1)} %dynamic-slice_maximum_fusion), channel_id=1, source_target_pairs={{0,8},{2,10},{4,12},{6,14},{8,0},{10,2},{12,4},{14,6},{16,24},{18,... | collective-permute-start | bytes 393224 | tf_op jit(solution)/shard_map/ppermute | solution.py:32
  15.5 9.2 %collective-permute-start.14 = (bf16[128,512]{1,0:T(8,128)(2,1)S(1)}, bf16[128,512]{1,0:T(8,128)(2,1)S(1)}, u32[]{:S(2)}, u32[]{:S(2)}) collective-permute-start(bf16[128,512]{1,0:T(8,128)(2,1)S(1)} %constant_dynamic-slice_fusion), channel_id=1, source_target_pairs={{0,6},{2,4},{4,2},{6,0},{8,14},{10,12},{12,10},{14,8},{16,22},{18,... | collective-permute-start | bytes 393224 | tf_op jit(solution)/shard_map/ppermute | solution.py:28
  17.3 8.6 %collective-permute-start.13 = (bf16[128,512]{1,0:T(8,128)(2,1)S(1)}, bf16[128,512]{1,0:T(8,128)(2,1)S(1)}, u32[]{:S(2)}, u32[]{:S(2)}) collective-permute-start(bf16[128,512]{1,0:T(8,128)(2,1)S(1)} %constant_dynamic-slice_fusion), channel_id=1, source_target_pairs={{0,4},{2,6},{4,0},{6,2},{8,12},{10,14},{12,8},{14,10},{16,20},{18,... | collective-permute-start | bytes 393224 | tf_op jit(solution)/shard_map/ppermute | solution.py:28
  20.9 6.1 %collective-permute-start.12 = (bf16[128,512]{1,0:T(8,128)(2,1)S(1)}, bf16[128,512]{1,0:T(8,128)(2,1)S(1)}, u32[]{:S(2)}, u32[]{:S(2)}) collective-permute-start(bf16[128,512]{1,0:T(8,128)(2,1)S(1)} %constant_dynamic-slice_fusion), channel_id=1, source_target_pairs={{0,2},{2,0},{4,6},{6,4},{8,10},{10,8},{12,14},{14,12},{16,18},{18,... | collective-permute-start | bytes 393224 | tf_op jit(solution)/shard_map/ppermute | solution.py:28
  22.1 9.2 %collective-permute-start.7 = (bf16[128,512]{1,0:T(8,128)(2,1)S(1)}, bf16[128,512]{1,0:T(8,128)(2,1)S(1)}, u32[]{:S(2)}, u32[]{:S(2)}) collective-permute-start(bf16[128,512]{1,0:T(8,128)(2,1)S(1)} %pad_maximum_fusion.3), channel_id=1, source_target_pairs={{0,4},{2,6},{4,0},{6,2},{8,12},{10,14},{12,8},{14,10},{16,20},{18,... | collective-permute-start | bytes 393224 | tf_op jit(solution)/shard_map/ppermute | solution.py:28
  23.7 7.9 %collective-permute-start.6 = (bf16[128,512]{1,0:T(8,128)(2,1)S(1)}, bf16[128,512]{1,0:T(8,128)(2,1)S(1)}, u32[]{:S(2)}, u32[]{:S(2)}) collective-permute-start(bf16[128,512]{1,0:T(8,128)(2,1)S(1)} %pad_maximum_fusion.2), channel_id=1, source_target_pairs={{0,2},{2,0},{4,6},{6,4},{8,10},{10,8},{12,14},{14,12},{16,18},{18,... | collective-permute-start | bytes 393224 | tf_op jit(solution)/shard_map/ppermute | solution.py:28
  24.7 7.7 %collective-permute-start.8 = (bf16[128,512]{1,0:T(8,128)(2,1)S(1)}, bf16[128,512]{1,0:T(8,128)(2,1)S(1)}, u32[]{:S(2)}, u32[]{:S(2)}) collective-permute-start(bf16[128,512]{1,0:T(8,128)(2,1)S(1)} %pad_maximum_fusion.4), channel_id=1, source_target_pairs={{0,6},{2,4},{4,2},{6,0},{8,14},{10,12},{12,10},{14,8},{16,22},{18,... | collective-permute-start | bytes 393224 | tf_op jit(solution)/shard_map/ppermute | solution.py:28
  27.5 10.1 %collective-permute-start.17 = (bf16[512,128]{1,0:T(8,128)(2,1)S(1)}, bf16[512,128]{1,0:T(8,128)(2,1)S(1)}, u32[]{:S(2)}, u32[]{:S(2)}) collective-permute-start(bf16[512,128]{1,0:T(8,128)(2,1)S(1)} %get-tuple-element.3), channel_id=1, source_target_pairs={{0,8},{2,10},{4,12},{6,14},{8,0},{10,2},{12,4},{14,6},{16,24},{18,... | collective-permute-start | bytes 393224 | tf_op jit(solution)/shard_map/ppermute | solution.py:32
  28.6 9.3 %collective-permute-start.19 = (bf16[512,128]{1,0:T(8,128)(2,1)S(1)}, bf16[512,128]{1,0:T(8,128)(2,1)S(1)}, u32[]{:S(2)}, u32[]{:S(2)}) collective-permute-start(bf16[512,128]{1,0:T(8,128)(2,1)S(1)} %get-tuple-element.4), channel_id=1, source_target_pairs={{0,24},{2,26},{4,28},{6,30},{8,16},{10,18},{12,20},{14,22},{16,8},... | collective-permute-start | bytes 393224 | tf_op jit(solution)/shard_map/ppermute | solution.py:32
  31.4 10.9 %collective-permute-start.18 = (bf16[512,128]{1,0:T(8,128)(2,1)S(1)}, bf16[512,128]{1,0:T(8,128)(2,1)S(1)}, u32[]{:S(2)}, u32[]{:S(2)}) collective-permute-start(bf16[512,128]{1,0:T(8,128)(2,1)S(1)} %get-tuple-element.5), channel_id=1, source_target_pairs={{0,16},{2,18},{4,20},{6,22},{8,24},{10,26},{12,28},{14,30},{16,0},... | collective-permute-start | bytes 393224 | tf_op jit(solution)/shard_map/ppermute | solution.py:32
  35.1 18.1 %copy-start.1 = (bf16[128,1024]{1,0:T(8,128)(2,1)S(1)}, bf16[128,1024]{1,0:T(8,128)(2,1)}, u32[]{:S(2)}) copy-start(bf16[128,1024]{1,0:T(8,128)(2,1)} %param.5) | copy-start | bytes 786436
  35.2 10.1 %collective-permute-start.15 = (bf16[128,512]{1,0:T(8,128)(2,1)S(1)}, bf16[128,512]{1,0:T(8,128)(2,1)S(1)}, u32[]{:S(2)}, u32[]{:S(2)}) collective-permute-start(bf16[128,512]{1,0:T(8,128)(2,1)S(1)} %pad_maximum_fusion.5), channel_id=1, source_target_pairs={{0,8},{2,10},{4,12},{6,14},{8,0},{10,2},{12,4},{14,6},{16,24},{18,... | collective-permute-start | bytes 393224 | tf_op jit(solution)/shard_map/ppermute | solution.py:32
  36.5 8.8 %collective-permute-start.9 = (bf16[128,512]{1,0:T(8,128)(2,1)S(1)}, bf16[128,512]{1,0:T(8,128)(2,1)S(1)}, u32[]{:S(2)}, u32[]{:S(2)}) collective-permute-start(bf16[128,512]{1,0:T(8,128)(2,1)S(1)} %get-tuple-element.8), channel_id=1, source_target_pairs={{0,2},{2,0},{4,6},{6,4},{8,10},{10,8},{12,14},{14,12},{16,18},{18,... | collective-permute-start | bytes 393224 | tf_op jit(solution)/shard_map/ppermute | solution.py:28
  42.8 10.4 %collective-permute-start.20 = (bf16[128,512]{1,0:T(8,128)(2,1)S(1)}, bf16[128,512]{1,0:T(8,128)(2,1)S(1)}, u32[]{:S(2)}, u32[]{:S(2)}) collective-permute-start(bf16[128,512]{1,0:T(8,128)(2,1)S(1)} %convolution_convert_fusion.2), channel_id=1, source_target_pairs={{0,1},{1,0},{2,3},{3,2},{4,5},{5,4},{6,7},{7,6},{8,9},{9,8},{10,11... | collective-permute-start | bytes 393224 | tf_op jit(solution)/shard_map/ppermute | solution.py:52
  42.9 6.9 %collective-permute-start.11 = (bf16[128,512]{1,0:T(8,128)(2,1)S(1)}, bf16[128,512]{1,0:T(8,128)(2,1)S(1)}, u32[]{:S(2)}, u32[]{:S(2)}) collective-permute-start(bf16[128,512]{1,0:T(8,128)(2,1)S(1)} %get-tuple-element.9), channel_id=1, source_target_pairs={{0,6},{2,4},{4,2},{6,0},{8,14},{10,12},{12,10},{14,8},{16,22},{18,... | collective-permute-start | bytes 393224 | tf_op jit(solution)/shard_map/ppermute | solution.py:28
  44.4 8.1 %collective-permute-start.10 = (bf16[128,512]{1,0:T(8,128)(2,1)S(1)}, bf16[128,512]{1,0:T(8,128)(2,1)S(1)}, u32[]{:S(2)}, u32[]{:S(2)}) collective-permute-start(bf16[128,512]{1,0:T(8,128)(2,1)S(1)} %get-tuple-element.10), channel_id=1, source_target_pairs={{0,4},{2,6},{4,0},{6,2},{8,12},{10,14},{12,8},{14,10},{16,20},{18,... | collective-permute-start | bytes 393224 | tf_op jit(solution)/shard_map/ppermute | solution.py:28
  45.4 9.0 %collective-permute-start.16 = (bf16[64,512]{1,0:T(8,128)(2,1)S(1)}, bf16[64,512]{1,0:T(8,128)(2,1)S(1)}, u32[]{:S(2)}, u32[]{:S(2)}) collective-permute-start(bf16[64,512]{1,0:T(8,128)(2,1)S(1)} %fusion.22), channel_id=1, source_target_pairs={{0,16},{2,18},{4,20},{6,22},{8,24},{10,26},{12,28},{14,30},{16,0},... | collective-permute-start | bytes 196616 | tf_op jit(solution)/shard_map/ppermute | solution.py:32

commit v28 on v20

--- a/solution.py
+++ b/solution.py
@@ -93,9 +93,6 @@
     block = jnp.concatenate(rows, 0)
 
     hidden_stack = jnp.concatenate([along_outer(hidden_part, e) for e in turns], 0)
-    grad_part = columns_of(cotangent, rep_pos)
-    grad_stack = jnp.concatenate([along_inner(grad_part, t) for t in turns], 0)
-
     mixed = dot(hidden_stack, block, ((0,), (1,))).astype(bf16)
     share = cols_here // side
     by_owner = mixed.reshape(share // rows_here, side, rows_here, side * tile_size)
@@ -106,7 +103,9 @@
         chosen = jnp.concatenate([lanes(chosen, u ^ t) for u in turns], 1)
         mixed_cols = mixed_cols + along_inner(chosen, t).astype(jnp.float32)
 
-    back = after(dot(grad_stack, block, ((0,), (0,))), mixed).astype(bf16)
+    grad_part = after(columns_of(cotangent, rep_pos), mixed)
+    grad_stack = jnp.concatenate([along_inner(grad_part, t) for t in turns], 0)
+    back = dot(grad_stack, block, ((0,), (0,))).astype(bf16)
     back = sum(along_outer(lanes(back, e), e).astype(jnp.float32) for e in turns)
 
     mixed_cols = lax.all_gather(mixed_cols.astype(bf16), "rep", axis=0, tiled=True)

time: 52.1 us -> 62.1 us (1.19)
  waiting for transfers between devices: 12.4 us -> 20.6 us
  starting transfers between devices: 25.2 us -> 28 us
  matrix products: 4.05 us -> 3.07 us
    ppermute x11, waiting for transfers between devices: 3.25 us -> 8.76 us  [along_inner(): return lax.ppermute(value, 'blk', pairs) if turn else value]
    ppermute x8, waiting for transfers between devices: 9.14 us -> 11.8 us  [along_outer(): return lax.ppermute(value, 'blk', pairs) if turn else value]
    ppermute x11, starting transfers between devices: 12.8 us -> 15.1 us  [along_inner(): return lax.ppermute(value, 'blk', pairs) if turn else value]
    dot_general x6, matrix products: 4.05 us -> 3.07 us  [dot(): lax.dot_general(lhs, rhs, (dims, ((), ())), preferred_element_type=jnp.fl...]
  transfers between devices with their start and end apart: 20 -> 20, of which waited for: 7 -> 10; matrix products, arithmetic and copies ran while one was open for 14% -> 9% of each run, Pallas kernels for 0% -> 0%
where the time goes in v28:
time: 62.1 us; the launch traced here: 61.8 us
  starting transfers between devices  28 us (45%)
  waiting for transfers between devices  20.6 us (33%)
  blocking collectives  4.18 us (7%)
  other arithmetic  3.89 us (6%)
  matrix products  3.07 us (5%)
  local copies, waits for them, and re-layouts  1.2 us (2%)
  between operations  0.91 us (1%)
    ppermute x11, starting transfers between devices, along_inner(): return lax.ppermute(value, 'blk', pairs) if turn else value  15.1 us
    ppermute x8, starting transfers between devices, along_outer(): return lax.ppermute(value, 'blk', pairs) if turn else value  12.8 us
    ppermute x8, waiting for transfers between devices, along_outer(): return lax.ppermute(value, 'blk', pairs) if turn else value  11.8 us
    ppermute x11, waiting for transfers between devices, along_inner(): return lax.ppermute(value, 'blk', pairs) if turn else value  8.76 us
    dot_general x6, matrix products, dot(): lax.dot_general(lhs, rhs, (dims, ((), ())), preferred_element_type=jnp.fl...  3.07 us
    all_gather x1, blocking collectives, shards(): everyone = lax.all_gather(jnp.concatenate(arrived, 0), 'rep', axis=0)  2.18 us
    all_gather x1, blocking collectives, shards(): lax.all_gather(mixed_cols.astype(bf16), 'rep', axis=0, tiled=True)  1.99 us
  transfers between devices with their start and end apart: 20, of which 10 were waited for; matrix products, arithmetic and copies ran while one was open for 9% of the time, Pallas kernels for 0%

profile of v28, /device:TPU:0, one launch (start us, length us, event | category | flops | bytes accessed | tf_op | source)
XLA Modules:
  0.0 61.8 jit_solution(7807552261588449021)
XLA Ops:
  0.7 1.1 %dynamic-slice_maximum_fusion = bf16[128,512]{1,0:T(8,128)(2,1)S(1)} fusion(bf16[128,1024]{1,0:T(8,128)(2,1)} %param.5, s32[]{:T(128)S(6)} %select_n.214), kind=kLoop, calls=%fused_computation.49 | loop fusion | flops 262144 | bytes 262148 | tf_op jit(solution)/shard_map/max | solution.py:66
  1.7 5.1 %collective-permute-start.2 = (bf16[128,512]{1,0:T(8,128)(2,1)S(1)}, bf16[128,512]{1,0:T(8,128)(2,1)S(1)}, u32[]{:S(2)}, u32[]{:S(2)}) collective-permute-start(bf16[128,512]{1,0:T(8,128)(2,1)S(1)} %dynamic-slice_maximum_fusion), channel_id=1, source_target_pairs={{0,24},{2,26},{4,28},{6,30},{8,16},{10,18},{12,20},{14,22},{16,8},... | collective-permute-start | bytes 393224 | tf_op jit(solution)/shard_map/ppermute | solution.py:32
  6.9 0.7 %add_bitcast_fusion = s32[8]{0:T(128)S(1)} fusion(s32[1,8]{1,0:T(1,128)} %param.7, s32[]{:T(128)S(6)} %shift_right_arithmetic.54, s32[]{:T(128)S(6)} %and.60), kind=kLoop, calls=%fused_computation.94 | loop fusion | flops 56 | bytes 72 | tf_op jit(solution)/shard_map/eq | solution.py:72
  7.6 0.9 %slice_bitcast_fusion.9 = (bf16[128,128]{1,0:T(8,128)(2,1)S(1)}, bf16[128,128]{1,0:T(8,128)(2,1)S(1)}, bf16[128,128]{1,0:T(8,128)(2,1)S(1)}, bf16[128,128]{1,0:T...) fusion(bf16[1,8,128,128]{3,2,1,0:T(8,128)(2,1)} %param.6), kind=kLoop, calls=%fused_computation.76 | loop fusion | bytes 524288 | tf_op jit(solution)/shard_map/jit(_where)/broadcast_in_dim | solution.py:75
  8.7 2.5 %collective-permute-start.5 = (bf16[2,128,128]{2,1,0:T(8,128)(2,1)S(1)}, bf16[2,128,128]{2,1,0:T(8,128)(2,1)S(1)}, u32[]{:S(2)}, u32[]{:S(2)}) collective-permute-start(bf16[2,128,128]{2,1,0:T(8,128)(2,1)S(1)} %get-tuple-element.30), channel_id=1, source_target_pairs={{0,6},{2,4},{4,2},{6,0},{8,14},{10,12},{12,10},{14,8},{16,22},{18,... | collective-permute-start | bytes 196616 | tf_op jit(solution)/shard_map/ppermute | solution.py:28
  11.2 0.5 collective-permute-start.4
  11.7 0.5 collective-permute-start.3
  12.3 1.7 %collective-permute-done.5 = bf16[2,128,128]{2,1,0:T(8,128)(2,1)S(1)} collective-permute-done((bf16[2,128,128]{2,1,0:T(8,128)(2,1)S(1)}, bf16[2,128,128]{2,1,0:T(8,128)(2,1)S(1)}, u32[]{:S(2)}, u32[]{:S(2)}) %collective-permute-start.5) | collective-permute-done | bytes 65568 | tf_op jit(solution)/shard_map/ppermute | solution.py:28
  14.1 0.6 %collective-permute-start = (bf16[128,512]{1,0:T(8,128)(2,1)S(1)}, bf16[128,512]{1,0:T(8,128)(2,1)S(1)}, u32[]{:S(2)}, u32[]{:S(2)}) collective-permute-start(bf16[128,512]{1,0:T(8,128)(2,1)S(1)} %dynamic-slice_maximum_fusion), channel_id=1, source_target_pairs={{0,8},{2,10},{4,12},{6,14},{8,0},{10,2},{12,4},{14,6},{16,24},{18,... | collective-permute-start | bytes 393224 | tf_op jit(solution)/shard_map/ppermute | solution.py:32
  14.7 0.8 %collective-permute-done.4 = bf16[2,128,128]{2,1,0:T(8,128)(2,1)S(1)} collective-permute-done((bf16[2,128,128]{2,1,0:T(8,128)(2,1)S(1)}, bf16[2,128,128]{2,1,0:T(8,128)(2,1)S(1)}, u32[]{:S(2)}, u32[]{:S(2)}) %collective-permute-start.4) | collective-permute-done | bytes 65568 | tf_op jit(solution)/shard_map/ppermute | solution.py:28
  16.0 2.2 %all-gather = bf16[16,128,128]{2,1,0:T(8,128)(2,1)S(1)} all-gather(bf16[8,128,128]{2,1,0:T(8,128)(2,1)S(1)} %pad_maximum_fusion.1), channel_id=2, replica_groups=mesh['blk'=16,'rep'=2] {'rep'}, dimensions={0}, use_global_device_ids=true | all-gather | bytes 786432 | tf_op jit(solution)/shard_map/all_gather | solution.py:79
  18.4 1.7 %collective-permute-done = bf16[128,512]{1,0:T(8,128)(2,1)S(1)} collective-permute-done((bf16[128,512]{1,0:T(8,128)(2,1)S(1)}, bf16[128,512]{1,0:T(8,128)(2,1)S(1)}, u32[]{:S(2)}, u32[]{:S(2)}) %collective-permute-start) | collective-permute-done | bytes 131104 | tf_op jit(solution)/shard_map/ppermute | solution.py:32
  20.8 2.5 %collective-permute-start.8 = (bf16[128,512]{1,0:T(8,128)(2,1)S(1)}, bf16[128,512]{1,0:T(8,128)(2,1)S(1)}, u32[]{:S(2)}, u32[]{:S(2)}) collective-permute-start(bf16[128,512]{1,0:T(8,128)(2,1)S(1)} %pad_maximum_fusion.5), channel_id=1, source_target_pairs={{0,6},{2,4},{4,2},{6,0},{8,14},{10,12},{12,10},{14,8},{16,22},{18,... | collective-permute-start | bytes 393224 | tf_op jit(solution)/shard_map/ppermute | solution.py:28
  23.3 0.6 collective-permute-start.7
  24.0 0.6 collective-permute-start.6
  24.6 2.5 %collective-permute-start.13 = (bf16[128,512]{1,0:T(8,128)(2,1)S(1)}, bf16[128,512]{1,0:T(8,128)(2,1)S(1)}, u32[]{:S(2)}, u32[]{:S(2)}) collective-permute-start(bf16[128,512]{1,0:T(8,128)(2,1)S(1)} %fusion.21), channel_id=1, source_target_pairs={{0,6},{2,4},{4,2},{6,0},{8,14},{10,12},{12,10},{14,8},{16,22},{18,... | collective-permute-start | bytes 393224 | tf_op jit(solution)/shard_map/ppermute | solution.py:28
  27.1 0.5 collective-permute-start.12
  27.6 2.0 %collective-permute-start.11 = (bf16[128,512]{1,0:T(8,128)(2,1)S(1)}, bf16[128,512]{1,0:T(8,128)(2,1)S(1)}, u32[]{:S(2)}, u32[]{:S(2)}) collective-permute-start(bf16[128,512]{1,0:T(8,128)(2,1)S(1)} %fusion.21), channel_id=1, source_target_pairs={{0,2},{2,0},{4,6},{6,4},{8,10},{10,8},{12,14},{14,12},{16,18},{18,... | collective-permute-start | bytes 393224 | tf_op jit(solution)/shard_map/ppermute | solution.py:28
  29.6 1.6 %collective-permute-done.7 = bf16[128,512]{1,0:T(8,128)(2,1)S(1)} collective-permute-done((bf16[128,512]{1,0:T(8,128)(2,1)S(1)}, bf16[128,512]{1,0:T(8,128)(2,1)S(1)}, u32[]{:S(2)}, u32[]{:S(2)}) %collective-permute-start.7) | collective-permute-done | bytes 131104 | tf_op jit(solution)/shard_map/ppermute | solution.py:28
  31.3 2.0 %all_gather.11 = bf16[256,512]{1,0:T(8,128)(2,1)S(1)} all-gather(bf16[128,512]{1,0:T(8,128)(2,1)S(1)} %fusion.18), channel_id=1, replica_groups=mesh['blk'=16,'rep'=2] {'rep'}, dimensions={0}, use_global_device_ids=true | all-gather | bytes 393216 | tf_op jit(solution)/shard_map/all_gather | solution.py:111
  33.7 2.0 %collective-permute-start.9 = (bf16[256,512]{1,0:T(8,128)(2,1)S(1)}, bf16[256,512]{1,0:T(8,128)(2,1)S(1)}, u32[]{:S(2)}, u32[]{:S(2)}) collective-permute-start(bf16[256,512]{1,0:T(8,128)(2,1)S(1)} %pad_maximum_fusion.2), channel_id=1, source_target_pairs={{0,2},{2,0},{4,6},{6,4},{8,10},{10,8},{12,14},{14,12},{16,18},{18,... | collective-permute-start | bytes 786440 | tf_op jit(solution)/shard_map/ppermute | solution.py:28
  37.0 2.8 %collective-permute-start.18 = (bf16[512,128]{1,0:T(8,128)(2,1)S(1)}, bf16[512,128]{1,0:T(8,128)(2,1)S(1)}, u32[]{:S(2)}, u32[]{:S(2)}) collective-permute-start(bf16[512,128]{1,0:T(8,128)(2,1)S(1)} %get-tuple-element.4), channel_id=1, source_target_pairs={{0,24},{2,26},{4,28},{6,30},{8,16},{10,18},{12,20},{14,22},{16,8},... | collective-permute-start | bytes 393224 | tf_op jit(solution)/shard_map/ppermute | solution.py:32
  39.7 0.6 collective-permute-start.17
  40.3 1.1 %collective-permute-start.16 = (bf16[512,128]{1,0:T(8,128)(2,1)S(1)}, bf16[512,128]{1,0:T(8,128)(2,1)S(1)}, u32[]{:S(2)}, u32[]{:S(2)}) collective-permute-start(bf16[512,128]{1,0:T(8,128)(2,1)S(1)} %get-tuple-element.3), channel_id=1, source_target_pairs={{0,8},{2,10},{4,12},{6,14},{8,0},{10,2},{12,4},{14,6},{16,24},{18,... | collective-permute-start | bytes 393224 | tf_op jit(solution)/shard_map/ppermute | solution.py:32
  41.7 2.4 %collective-permute-start.15 = (bf16[64,512]{1,0:T(8,128)(2,1)S(1)}, bf16[64,512]{1,0:T(8,128)(2,1)S(1)}, u32[]{:S(2)}, u32[]{:S(2)}) collective-permute-start(bf16[64,512]{1,0:T(8,128)(2,1)S(1)} %fusion.22), channel_id=1, source_target_pairs={{0,16},{2,18},{4,20},{6,22},{8,24},{10,26},{12,28},{14,30},{16,0},... | collective-permute-start | bytes 196616 | tf_op jit(solution)/shard_map/ppermute | solution.py:32
  44.1 2.3 %collective-permute-done.18 = bf16[512,128]{1,0:T(8,128)(2,1)S(1)} collective-permute-done((bf16[512,128]{1,0:T(8,128)(2,1)S(1)}, bf16[512,128]{1,0:T(8,128)(2,1)S(1)}, u32[]{:S(2)}, u32[]{:S(2)}) %collective-permute-start.18) | collective-permute-done | bytes 131104 | tf_op jit(solution)/shard_map/ppermute | solution.py:32
  46.4 7.4 %collective-permute-done.17 = bf16[512,128]{1,0:T(8,128)(2,1)S(1)} collective-permute-done((bf16[512,128]{1,0:T(8,128)(2,1)S(1)}, bf16[512,128]{1,0:T(8,128)(2,1)S(1)}, u32[]{:S(2)}, u32[]{:S(2)}) %collective-permute-start.17) | collective-permute-done | bytes 131104 | tf_op jit(solution)/shard_map/ppermute | solution.py:32
  54.5 0.7 %fusion.23 = f32[64,512]{1,0:T(8,128)} fusion(bf16[64,512]{1,0:T(8,128)(2,1)S(1)} %collective-permute-done.15, f32[4,64,512]{2,1,0:T(8,128)S(1)} %bitcast.119, s32[]{:T(128)S(6)} %select_n.271, bf16[128,512]{1,0:T(8,128)(2,1)S(1)} %collective-permute-done.14), kind=kLoop, calls=%fused_computation.46 | loop fusion | flops 131072 | bytes 393220 | tf_op jit(solution)/shard_map/add | solution.py:42
  55.2 0.7 %collective-permute-start.10 = (bf16[128,512]{1,0:T(8,128)(2,1)S(1)}, bf16[128,512]{1,0:T(8,128)(2,1)S(1)}, u32[]{:S(2)}, u32[]{:S(2)}) collective-permute-start(bf16[128,512]{1,0:T(8,128)(2,1)S(1)} %fusion.12), channel_id=1, source_target_pairs={{0,4},{2,6},{4,0},{6,2},{8,12},{10,14},{12,8},{14,10},{16,20},{18,... | collective-permute-start | bytes 393224 | tf_op jit(solution)/shard_map/ppermute | solution.py:28
  56.0 1.1 %select_convert_fusion = bf16[128,512]{1,0:T(8,128)(2,1)} fusion(bf16[128,512]{1,0:T(8,128)(2,1)S(1)} %collective-permute-done.19, bf16[128,1024]{1,0:T(8,128)(2,1)S(1)} %copy-done.1, s32[]{:T(128)S(6)} %select_n.214, bf16[512,128]{1,0:T(8,128)(2,1)S(1)} %fusion.15, bf16[2,512,1024]{2,1,0:T(8,128)(2,1)S(1)} %bitcast.110, s32[]{:T(128)S(6)} %select_n.279, ...), kind=kOutput, calls=%fused_computation.32 | convolution fusion | flops 67567616 | bytes 1048588 | tf_op jit(solution)/shard_map/dot_general | solution.py:52
  57.1 4.1 %collective-permute-done.10 = bf16[128,512]{1,0:T(8,128)(2,1)S(1)} collective-permute-done((bf16[128,512]{1,0:T(8,128)(2,1)S(1)}, bf16[128,512]{1,0:T(8,128)(2,1)S(1)}, u32[]{:S(2)}, u32[]{:S(2)}) %collective-permute-start.10) | collective-permute-done | bytes 131104 | tf_op jit(solution)/shard_map/ppermute | solution.py:28
  61.1 0.7 %fusion.14 = bf16[128,512]{1,0:T(8,128)(2,1)} fusion(f32[512,512]{1,0:T(8,128)S(1)} %get-tuple-element.60, bf16[128,512]{1,0:T(8,128)(2,1)S(1)} %collective-permute-done.10, bf16[256,512]{1,0:T(8,128)(2,1)S(1)} %collective-permute-done.9), kind=kLoop, calls=%fused_computation.23 | loop fusion | flops 327680 | bytes 655360 | tf_op jit(solution)/shard_map/convert_element_type | solution.py:124
  (56 shorter events, 4.3 us)
Async XLA Ops:
  0.6 11.6 %copy-start = (bf16[1024,1024]{1,0:T(8,128)(2,1)S(1)}, bf16[1024,1024]{1,0:T(8,128)(2,1)}, u32[]{:S(2)}) copy-start(bf16[1024,1024]{1,0:T(8,128)(2,1)} %param.8) | copy-start | bytes 6291460
  1.7 16.7 %collective-permute-start.2 = (bf16[128,512]{1,0:T(8,128)(2,1)S(1)}, bf16[128,512]{1,0:T(8,128)(2,1)S(1)}, u32[]{:S(2)}, u32[]{:S(2)}) collective-permute-start(bf16[128,512]{1,0:T(8,128)(2,1)S(1)} %dynamic-slice_maximum_fusion), channel_id=1, source_target_pairs={{0,24},{2,26},{4,28},{6,30},{8,16},{10,18},{12,20},{14,22},{16,8},... | collective-permute-start | bytes 393224 | tf_op jit(solution)/shard_map/ppermute | solution.py:32
  6.8 11.6 %collective-permute-start.1 = (bf16[128,512]{1,0:T(8,128)(2,1)S(1)}, bf16[128,512]{1,0:T(8,128)(2,1)S(1)}, u32[]{:S(2)}, u32[]{:S(2)}) collective-permute-start(bf16[128,512]{1,0:T(8,128)(2,1)S(1)} %dynamic-slice_maximum_fusion), channel_id=1, source_target_pairs={{0,16},{2,18},{4,20},{6,22},{8,24},{10,26},{12,28},{14,30},{16,0},... | collective-permute-start | bytes 393224 | tf_op jit(solution)/shard_map/ppermute | solution.py:32
  8.7 5.3 %collective-permute-start.5 = (bf16[2,128,128]{2,1,0:T(8,128)(2,1)S(1)}, bf16[2,128,128]{2,1,0:T(8,128)(2,1)S(1)}, u32[]{:S(2)}, u32[]{:S(2)}) collective-permute-start(bf16[2,128,128]{2,1,0:T(8,128)(2,1)S(1)} %get-tuple-element.30), channel_id=1, source_target_pairs={{0,6},{2,4},{4,2},{6,0},{8,14},{10,12},{12,10},{14,8},{16,22},{18,... | collective-permute-start | bytes 196616 | tf_op jit(solution)/shard_map/ppermute | solution.py:28
  11.2 4.3 %collective-permute-start.4 = (bf16[2,128,128]{2,1,0:T(8,128)(2,1)S(1)}, bf16[2,128,128]{2,1,0:T(8,128)(2,1)S(1)}, u32[]{:S(2)}, u32[]{:S(2)}) collective-permute-start(bf16[2,128,128]{2,1,0:T(8,128)(2,1)S(1)} %get-tuple-element.31), channel_id=1, source_target_pairs={{0,4},{2,6},{4,0},{6,2},{8,12},{10,14},{12,8},{14,10},{16,20},{18,... | collective-permute-start | bytes 196616 | tf_op jit(solution)/shard_map/ppermute | solution.py:28
  11.7 4.3 %collective-permute-start.3 = (bf16[2,128,128]{2,1,0:T(8,128)(2,1)S(1)}, bf16[2,128,128]{2,1,0:T(8,128)(2,1)S(1)}, u32[]{:S(2)}, u32[]{:S(2)}) collective-permute-start(bf16[2,128,128]{2,1,0:T(8,128)(2,1)S(1)} %get-tuple-element.32), channel_id=1, source_target_pairs={{0,2},{2,0},{4,6},{6,4},{8,10},{10,8},{12,14},{14,12},{16,18},{18,... | collective-permute-start | bytes 196616 | tf_op jit(solution)/shard_map/ppermute | solution.py:28
  14.1 6.1 %collective-permute-start = (bf16[128,512]{1,0:T(8,128)(2,1)S(1)}, bf16[128,512]{1,0:T(8,128)(2,1)S(1)}, u32[]{:S(2)}, u32[]{:S(2)}) collective-permute-start(bf16[128,512]{1,0:T(8,128)(2,1)S(1)} %dynamic-slice_maximum_fusion), channel_id=1, source_target_pairs={{0,8},{2,10},{4,12},{6,14},{8,0},{10,2},{12,4},{14,6},{16,24},{18,... | collective-permute-start | bytes 393224 | tf_op jit(solution)/shard_map/ppermute | solution.py:32
  18.4 6.1 %copy-start.2 = (bf16[128,1024]{1,0:T(8,128)(2,1)S(1)}, bf16[128,1024]{1,0:T(8,128)(2,1)}, u32[]{:S(2)}) copy-start(bf16[128,1024]{1,0:T(8,128)(2,1)} %param.9) | copy-start | bytes 786436
  20.8 6.9 %collective-permute-start.8 = (bf16[128,512]{1,0:T(8,128)(2,1)S(1)}, bf16[128,512]{1,0:T(8,128)(2,1)S(1)}, u32[]{:S(2)}, u32[]{:S(2)}) collective-permute-start(bf16[128,512]{1,0:T(8,128)(2,1)S(1)} %pad_maximum_fusion.5), channel_id=1, source_target_pairs={{0,6},{2,4},{4,2},{6,0},{8,14},{10,12},{12,10},{14,8},{16,22},{18,... | collective-permute-start | bytes 393224 | tf_op jit(solution)/shard_map/ppermute | solution.py:28
  23.3 7.9 %collective-permute-start.7 = (bf16[128,512]{1,0:T(8,128)(2,1)S(1)}, bf16[128,512]{1,0:T(8,128)(2,1)S(1)}, u32[]{:S(2)}, u32[]{:S(2)}) collective-permute-start(bf16[128,512]{1,0:T(8,128)(2,1)S(1)} %pad_maximum_fusion.4), channel_id=1, source_target_pairs={{0,4},{2,6},{4,0},{6,2},{8,12},{10,14},{12,8},{14,10},{16,20},{18,... | collective-permute-start | bytes 393224 | tf_op jit(solution)/shard_map/ppermute | solution.py:28
  24.0 7.3 %collective-permute-start.6 = (bf16[128,512]{1,0:T(8,128)(2,1)S(1)}, bf16[128,512]{1,0:T(8,128)(2,1)S(1)}, u32[]{:S(2)}, u32[]{:S(2)}) collective-permute-start(bf16[128,512]{1,0:T(8,128)(2,1)S(1)} %pad_maximum_fusion.3), channel_id=1, source_target_pairs={{0,2},{2,0},{4,6},{6,4},{8,10},{10,8},{12,14},{14,12},{16,18},{18,... | collective-permute-start | bytes 393224 | tf_op jit(solution)/shard_map/ppermute | solution.py:28
  24.6 11.2 %collective-permute-start.13 = (bf16[128,512]{1,0:T(8,128)(2,1)S(1)}, bf16[128,512]{1,0:T(8,128)(2,1)S(1)}, u32[]{:S(2)}, u32[]{:S(2)}) collective-permute-start(bf16[128,512]{1,0:T(8,128)(2,1)S(1)} %fusion.21), channel_id=1, source_target_pairs={{0,6},{2,4},{4,2},{6,0},{8,14},{10,12},{12,10},{14,8},{16,22},{18,... | collective-permute-start | bytes 393224 | tf_op jit(solution)/shard_map/ppermute | solution.py:28
  27.1 8.7 %collective-permute-start.12 = (bf16[128,512]{1,0:T(8,128)(2,1)S(1)}, bf16[128,512]{1,0:T(8,128)(2,1)S(1)}, u32[]{:S(2)}, u32[]{:S(2)}) collective-permute-start(bf16[128,512]{1,0:T(8,128)(2,1)S(1)} %fusion.21), channel_id=1, source_target_pairs={{0,4},{2,6},{4,0},{6,2},{8,12},{10,14},{12,8},{14,10},{16,20},{18,... | collective-permute-start | bytes 393224 | tf_op jit(solution)/shard_map/ppermute | solution.py:28
  27.6 8.1 %collective-permute-start.11 = (bf16[128,512]{1,0:T(8,128)(2,1)S(1)}, bf16[128,512]{1,0:T(8,128)(2,1)S(1)}, u32[]{:S(2)}, u32[]{:S(2)}) collective-permute-start(bf16[128,512]{1,0:T(8,128)(2,1)S(1)} %fusion.21), channel_id=1, source_target_pairs={{0,2},{2,0},{4,6},{6,4},{8,10},{10,8},{12,14},{14,12},{16,18},{18,... | collective-permute-start | bytes 393224 | tf_op jit(solution)/shard_map/ppermute | solution.py:28
  33.7 21.5 %collective-permute-start.9 = (bf16[256,512]{1,0:T(8,128)(2,1)S(1)}, bf16[256,512]{1,0:T(8,128)(2,1)S(1)}, u32[]{:S(2)}, u32[]{:S(2)}) collective-permute-start(bf16[256,512]{1,0:T(8,128)(2,1)S(1)} %pad_maximum_fusion.2), channel_id=1, source_target_pairs={{0,2},{2,0},{4,6},{6,4},{8,10},{10,8},{12,14},{14,12},{16,18},{18,... | collective-permute-start | bytes 786440 | tf_op jit(solution)/shard_map/ppermute | solution.py:28
  36.1 5.6 %collective-permute-start.14 = (bf16[128,512]{1,0:T(8,128)(2,1)S(1)}, bf16[128,512]{1,0:T(8,128)(2,1)S(1)}, u32[]{:S(2)}, u32[]{:S(2)}) collective-permute-start(bf16[128,512]{1,0:T(8,128)(2,1)S(1)} %pad_maximum_fusion.6), channel_id=1, source_target_pairs={{0,8},{2,10},{4,12},{6,14},{8,0},{10,2},{12,4},{14,6},{16,24},{18,... | collective-permute-start | bytes 393224 | tf_op jit(solution)/shard_map/ppermute | solution.py:32
  36.9 19.1 %copy-start.1 = (bf16[128,1024]{1,0:T(8,128)(2,1)S(1)}, bf16[128,1024]{1,0:T(8,128)(2,1)}, u32[]{:S(2)}) copy-start(bf16[128,1024]{1,0:T(8,128)(2,1)} %param.5) | copy-start | bytes 786436
  37.0 9.4 %collective-permute-start.18 = (bf16[512,128]{1,0:T(8,128)(2,1)S(1)}, bf16[512,128]{1,0:T(8,128)(2,1)S(1)}, u32[]{:S(2)}, u32[]{:S(2)}) collective-permute-start(bf16[512,128]{1,0:T(8,128)(2,1)S(1)} %get-tuple-element.4), channel_id=1, source_target_pairs={{0,24},{2,26},{4,28},{6,30},{8,16},{10,18},{12,20},{14,22},{16,8},... | collective-permute-start | bytes 393224 | tf_op jit(solution)/shard_map/ppermute | solution.py:32
  39.7 14.1 %collective-permute-start.17 = (bf16[512,128]{1,0:T(8,128)(2,1)S(1)}, bf16[512,128]{1,0:T(8,128)(2,1)S(1)}, u32[]{:S(2)}, u32[]{:S(2)}) collective-permute-start(bf16[512,128]{1,0:T(8,128)(2,1)S(1)} %get-tuple-element.5), channel_id=1, source_target_pairs={{0,16},{2,18},{4,20},{6,22},{8,24},{10,26},{12,28},{14,30},{16,0},... | collective-permute-start | bytes 393224 | tf_op jit(solution)/shard_map/ppermute | solution.py:32
  40.3 13.5 %collective-permute-start.16 = (bf16[512,128]{1,0:T(8,128)(2,1)S(1)}, bf16[512,128]{1,0:T(8,128)(2,1)S(1)}, u32[]{:S(2)}, u32[]{:S(2)}) collective-permute-start(bf16[512,128]{1,0:T(8,128)(2,1)S(1)} %get-tuple-element.3), channel_id=1, source_target_pairs={{0,8},{2,10},{4,12},{6,14},{8,0},{10,2},{12,4},{14,6},{16,24},{18,... | collective-permute-start | bytes 393224 | tf_op jit(solution)/shard_map/ppermute | solution.py:32
  41.7 12.8 %collective-permute-start.15 = (bf16[64,512]{1,0:T(8,128)(2,1)S(1)}, bf16[64,512]{1,0:T(8,128)(2,1)S(1)}, u32[]{:S(2)}, u32[]{:S(2)}) collective-permute-start(bf16[64,512]{1,0:T(8,128)(2,1)S(1)} %fusion.22), channel_id=1, source_target_pairs={{0,16},{2,18},{4,20},{6,22},{8,24},{10,26},{12,28},{14,30},{16,0},... | collective-permute-start | bytes 196616 | tf_op jit(solution)/shard_map/ppermute | solution.py:32
  54.3 1.6 %collective-permute-start.19 = (bf16[128,512]{1,0:T(8,128)(2,1)S(1)}, bf16[128,512]{1,0:T(8,128)(2,1)S(1)}, u32[]{:S(2)}, u32[]{:S(2)}) collective-permute-start(bf16[128,512]{1,0:T(8,128)(2,1)S(1)} %convolution_convert_fusion.2), channel_id=1, source_target_pairs={{0,1},{1,0},{2,3},{3,2},{4,5},{5,4},{6,7},{7,6},{8,9},{9,8},{10,11... | collective-permute-start | bytes 393224 | tf_op jit(solution)/shard_map/ppermute | solution.py:49
  55.2 5.9 %collective-permute-start.10 = (bf16[128,512]{1,0:T(8,128)(2,1)S(1)}, bf16[128,512]{1,0:T(8,128)(2,1)S(1)}, u32[]{:S(2)}, u32[]{:S(2)}) collective-permute-start(bf16[128,512]{1,0:T(8,128)(2,1)S(1)} %fusion.12), channel_id=1, source_target_pairs={{0,4},{2,6},{4,0},{6,2},{8,12},{10,14},{12,8},{14,10},{16,20},{18,... | collective-permute-start | bytes 393224 | tf_op jit(solution)/shard_map/ppermute | solution.py:28

commit v29 on v27

--- a/solution.py
+++ b/solution.py
@@ -126,7 +126,7 @@
     grad_weight = halved(
         [lax.dynamic_index_in_dim(by_outer, outer_pos ^ t, 0, keepdims=False) for t in turns],
         along_outer,
-        out_got[1:2],
+        out_got[1::2],
     )
     out_part = sum(part.astype(jnp.float32) for part in out_got).astype(bf16)
 

time: 55.3 us -> 52 us (0.940)
  waiting for transfers between devices: 16.1 us -> 9.8 us
  starting transfers between devices: 25.6 us -> 28.7 us
    ppermute x12, waiting for transfers between devices: 11.5 us -> 6.11 us  [along_inner(): return lax.ppermute(value, 'blk', pairs) if turn else value]
    ppermute x8, starting transfers between devices: 11.2 us -> 14.2 us  [along_outer(): return lax.ppermute(value, 'blk', pairs) if turn else value]
    ppermute x8, waiting for transfers between devices: 4.67 us -> 3.69 us  [along_outer(): return lax.ppermute(value, 'blk', pairs) if turn else value]
where the time goes in v29:
time: 52 us; the launch traced here: 51.8 us
  starting transfers between devices  28.7 us (55%)
  waiting for transfers between devices  9.8 us (19%)
  blocking collectives  4.18 us (8%)
  other arithmetic  3.85 us (7%)
  matrix products  3.09 us (6%)
  local copies, waits for them, and re-layouts  1.24 us (2%)
  between operations  0.92 us (2%)
    ppermute x12, starting transfers between devices, along_inner(): return lax.ppermute(value, 'blk', pairs) if turn else value  14.4 us
    ppermute x8, starting transfers between devices, along_outer(): return lax.ppermute(value, 'blk', pairs) if turn else value  14.2 us
    ppermute x12, waiting for transfers between devices, along_inner(): return lax.ppermute(value, 'blk', pairs) if turn else value  6.11 us
    ppermute x8, waiting for transfers between devices, along_outer(): return lax.ppermute(value, 'blk', pairs) if turn else value  3.69 us
    dot_general x6, matrix products, dot(): lax.dot_general(lhs, rhs, (dims, ((), ())), preferred_element_type=jnp.fl...  3.09 us
    all_gather x1, blocking collectives, shards(): everyone = lax.all_gather(jnp.concatenate(arrived, 0), 'rep', axis=0)  2.18 us
    all_gather x1, blocking collectives, shards(): lax.all_gather(mixed_cols.astype(bf16), 'rep', axis=0, tiled=True)  1.99 us
    max x1, other arithmetic, shards(): hidden_part = jnp.maximum(columns_of(hidden_pre, rep_pos), 0)  1.08 us
  transfers between devices with their start and end apart: 21, of which 8 were waited for; matrix products, arithmetic and copies ran while one was open for 12% of the time, Pallas kernels for 0%

profile of v29, /device:TPU:0, one launch (start us, length us, event | category | flops | bytes accessed | tf_op | source)
XLA Modules:
  0.0 51.8 jit_solution(2562871512436976519)
XLA Ops:
  0.7 1.1 %dynamic-slice_maximum_fusion = bf16[128,512]{1,0:T(8,128)(2,1)S(1)} fusion(bf16[128,1024]{1,0:T(8,128)(2,1)} %param.5, s32[]{:T(128)S(6)} %select_n.214), kind=kLoop, calls=%fused_computation.42 | loop fusion | flops 262144 | bytes 262148 | tf_op jit(solution)/shard_map/max | solution.py:69
  1.7 5.1 %collective-permute-start.2 = (bf16[128,512]{1,0:T(8,128)(2,1)S(1)}, bf16[128,512]{1,0:T(8,128)(2,1)S(1)}, u32[]{:S(2)}, u32[]{:S(2)}) collective-permute-start(bf16[128,512]{1,0:T(8,128)(2,1)S(1)} %dynamic-slice_maximum_fusion), channel_id=1, source_target_pairs={{0,24},{2,26},{4,28},{6,30},{8,16},{10,18},{12,20},{14,22},{16,8},... | collective-permute-start | bytes 393224 | tf_op jit(solution)/shard_map/ppermute | solution.py:32
  6.9 0.7 %add_bitcast_fusion = s32[8]{0:T(128)S(1)} fusion(s32[1,8]{1,0:T(1,128)} %param.7, s32[]{:T(128)S(6)} %shift_right_arithmetic.54, s32[]{:T(128)S(6)} %and.60), kind=kLoop, calls=%fused_computation.92 | loop fusion | flops 56 | bytes 72 | tf_op jit(solution)/shard_map/eq | solution.py:75
  7.6 0.9 %slice_bitcast_fusion.9 = (bf16[128,128]{1,0:T(8,128)(2,1)S(1)}, bf16[128,128]{1,0:T(8,128)(2,1)S(1)}, bf16[128,128]{1,0:T(8,128)(2,1)S(1)}, bf16[128,128]{1,0:T...) fusion(bf16[1,8,128,128]{3,2,1,0:T(8,128)(2,1)} %param.6), kind=kLoop, calls=%fused_computation.73 | loop fusion | bytes 524288 | tf_op jit(solution)/shard_map/jit(_where)/broadcast_in_dim | solution.py:78
  8.7 2.5 %collective-permute-start.5 = (bf16[2,128,128]{2,1,0:T(8,128)(2,1)S(1)}, bf16[2,128,128]{2,1,0:T(8,128)(2,1)S(1)}, u32[]{:S(2)}, u32[]{:S(2)}) collective-permute-start(bf16[2,128,128]{2,1,0:T(8,128)(2,1)S(1)} %get-tuple-element.31), channel_id=1, source_target_pairs={{0,6},{2,4},{4,2},{6,0},{8,14},{10,12},{12,10},{14,8},{16,22},{18,... | collective-permute-start | bytes 196616 | tf_op jit(solution)/shard_map/ppermute | solution.py:28
  11.8 0.5 %collective-permute-start.3 = (bf16[2,128,128]{2,1,0:T(8,128)(2,1)S(1)}, bf16[2,128,128]{2,1,0:T(8,128)(2,1)S(1)}, u32[]{:S(2)}, u32[]{:S(2)}) collective-permute-start(bf16[2,128,128]{2,1,0:T(8,128)(2,1)S(1)} %get-tuple-element.33), channel_id=1, source_target_pairs={{0,2},{2,0},{4,6},{6,4},{8,10},{10,8},{12,14},{14,12},{16,18},{18,... | collective-permute-start | bytes 196616 | tf_op jit(solution)/shard_map/ppermute | solution.py:28
  12.4 1.7 %collective-permute-done.5 = bf16[2,128,128]{2,1,0:T(8,128)(2,1)S(1)} collective-permute-done((bf16[2,128,128]{2,1,0:T(8,128)(2,1)S(1)}, bf16[2,128,128]{2,1,0:T(8,128)(2,1)S(1)}, u32[]{:S(2)}, u32[]{:S(2)}) %collective-permute-start.5) | collective-permute-done | bytes 65568 | tf_op jit(solution)/shard_map/ppermute | solution.py:28
  14.1 0.6 %collective-permute-start = (bf16[128,512]{1,0:T(8,128)(2,1)S(1)}, bf16[128,512]{1,0:T(8,128)(2,1)S(1)}, u32[]{:S(2)}, u32[]{:S(2)}) collective-permute-start(bf16[128,512]{1,0:T(8,128)(2,1)S(1)} %dynamic-slice_maximum_fusion), channel_id=1, source_target_pairs={{0,8},{2,10},{4,12},{6,14},{8,0},{10,2},{12,4},{14,6},{16,24},{18,... | collective-permute-start | bytes 393224 | tf_op jit(solution)/shard_map/ppermute | solution.py:32
  14.7 0.8 %collective-permute-done.4 = bf16[2,128,128]{2,1,0:T(8,128)(2,1)S(1)} collective-permute-done((bf16[2,128,128]{2,1,0:T(8,128)(2,1)S(1)}, bf16[2,128,128]{2,1,0:T(8,128)(2,1)S(1)}, u32[]{:S(2)}, u32[]{:S(2)}) %collective-permute-start.4) | collective-permute-done | bytes 65568 | tf_op jit(solution)/shard_map/ppermute | solution.py:28
  15.5 1.8 %collective-permute-start.14 = (bf16[128,512]{1,0:T(8,128)(2,1)S(1)}, bf16[128,512]{1,0:T(8,128)(2,1)S(1)}, u32[]{:S(2)}, u32[]{:S(2)}) collective-permute-start(bf16[128,512]{1,0:T(8,128)(2,1)S(1)} %constant_dynamic-slice_fusion), channel_id=1, source_target_pairs={{0,6},{2,4},{4,2},{6,0},{8,14},{10,12},{12,10},{14,8},{16,22},{18,... | collective-permute-start | bytes 393224 | tf_op jit(solution)/shard_map/ppermute | solution.py:28
  17.3 1.1 %collective-permute-start.13 = (bf16[128,512]{1,0:T(8,128)(2,1)S(1)}, bf16[128,512]{1,0:T(8,128)(2,1)S(1)}, u32[]{:S(2)}, u32[]{:S(2)}) collective-permute-start(bf16[128,512]{1,0:T(8,128)(2,1)S(1)} %constant_dynamic-slice_fusion), channel_id=1, source_target_pairs={{0,4},{2,6},{4,0},{6,2},{8,12},{10,14},{12,8},{14,10},{16,20},{18,... | collective-permute-start | bytes 393224 | tf_op jit(solution)/shard_map/ppermute | solution.py:28
  18.5 2.2 %all-gather = bf16[16,128,128]{2,1,0:T(8,128)(2,1)S(1)} all-gather(bf16[8,128,128]{2,1,0:T(8,128)(2,1)S(1)} %pad_maximum_fusion.1), channel_id=2, replica_groups=mesh['blk'=16,'rep'=2] {'rep'}, dimensions={0}, use_global_device_ids=true | all-gather | bytes 786432 | tf_op jit(solution)/shard_map/all_gather | solution.py:82
  20.9 0.6 %collective-permute-start.12 = (bf16[128,512]{1,0:T(8,128)(2,1)S(1)}, bf16[128,512]{1,0:T(8,128)(2,1)S(1)}, u32[]{:S(2)}, u32[]{:S(2)}) collective-permute-start(bf16[128,512]{1,0:T(8,128)(2,1)S(1)} %constant_dynamic-slice_fusion), channel_id=1, source_target_pairs={{0,2},{2,0},{4,6},{6,4},{8,10},{10,8},{12,14},{14,12},{16,18},{18,... | collective-permute-start | bytes 393224 | tf_op jit(solution)/shard_map/ppermute | solution.py:28
  22.1 1.5 %collective-permute-start.7 = (bf16[128,512]{1,0:T(8,128)(2,1)S(1)}, bf16[128,512]{1,0:T(8,128)(2,1)S(1)}, u32[]{:S(2)}, u32[]{:S(2)}) collective-permute-start(bf16[128,512]{1,0:T(8,128)(2,1)S(1)} %pad_maximum_fusion.3), channel_id=1, source_target_pairs={{0,4},{2,6},{4,0},{6,2},{8,12},{10,14},{12,8},{14,10},{16,20},{18,... | collective-permute-start | bytes 393224 | tf_op jit(solution)/shard_map/ppermute | solution.py:28
  23.7 1.0 %collective-permute-start.6 = (bf16[128,512]{1,0:T(8,128)(2,1)S(1)}, bf16[128,512]{1,0:T(8,128)(2,1)S(1)}, u32[]{:S(2)}, u32[]{:S(2)}) collective-permute-start(bf16[128,512]{1,0:T(8,128)(2,1)S(1)} %pad_maximum_fusion.2), channel_id=1, source_target_pairs={{0,2},{2,0},{4,6},{6,4},{8,10},{10,8},{12,14},{14,12},{16,18},{18,... | collective-permute-start | bytes 393224 | tf_op jit(solution)/shard_map/ppermute | solution.py:28
  24.7 1.2 %collective-permute-start.8 = (bf16[128,512]{1,0:T(8,128)(2,1)S(1)}, bf16[128,512]{1,0:T(8,128)(2,1)S(1)}, u32[]{:S(2)}, u32[]{:S(2)}) collective-permute-start(bf16[128,512]{1,0:T(8,128)(2,1)S(1)} %pad_maximum_fusion.4), channel_id=1, source_target_pairs={{0,6},{2,4},{4,2},{6,0},{8,14},{10,12},{12,10},{14,8},{16,22},{18,... | collective-permute-start | bytes 393224 | tf_op jit(solution)/shard_map/ppermute | solution.py:28
  25.9 1.1 %collective-permute-done.12 = bf16[128,512]{1,0:T(8,128)(2,1)S(1)} collective-permute-done((bf16[128,512]{1,0:T(8,128)(2,1)S(1)}, bf16[128,512]{1,0:T(8,128)(2,1)S(1)}, u32[]{:S(2)}, u32[]{:S(2)}) %collective-permute-start.12) | collective-permute-done | bytes 131104 | tf_op jit(solution)/shard_map/ppermute | solution.py:28
  27.5 1.0 %collective-permute-start.17 = (bf16[512,128]{1,0:T(8,128)(2,1)S(1)}, bf16[512,128]{1,0:T(8,128)(2,1)S(1)}, u32[]{:S(2)}, u32[]{:S(2)}) collective-permute-start(bf16[512,128]{1,0:T(8,128)(2,1)S(1)} %get-tuple-element.3), channel_id=1, source_target_pairs={{0,8},{2,10},{4,12},{6,14},{8,0},{10,2},{12,4},{14,6},{16,24},{18,... | collective-permute-start | bytes 393224 | tf_op jit(solution)/shard_map/ppermute | solution.py:32
  28.6 2.8 %collective-permute-start.19 = (bf16[512,128]{1,0:T(8,128)(2,1)S(1)}, bf16[512,128]{1,0:T(8,128)(2,1)S(1)}, u32[]{:S(2)}, u32[]{:S(2)}) collective-permute-start(bf16[512,128]{1,0:T(8,128)(2,1)S(1)} %get-tuple-element.4), channel_id=1, source_target_pairs={{0,24},{2,26},{4,28},{6,30},{8,16},{10,18},{12,20},{14,22},{16,8},... | collective-permute-start | bytes 393224 | tf_op jit(solution)/shard_map/ppermute | solution.py:32
  31.6 0.8 %collective-permute-done.8 = bf16[128,512]{1,0:T(8,128)(2,1)S(1)} collective-permute-done((bf16[128,512]{1,0:T(8,128)(2,1)S(1)}, bf16[128,512]{1,0:T(8,128)(2,1)S(1)}, u32[]{:S(2)}, u32[]{:S(2)}) %collective-permute-start.8) | collective-permute-done | bytes 131104 | tf_op jit(solution)/shard_map/ppermute | solution.py:28
  32.5 2.0 %all_gather.11 = bf16[256,512]{1,0:T(8,128)(2,1)S(1)} all-gather(bf16[128,512]{1,0:T(8,128)(2,1)S(1)} %fusion.16), channel_id=1, replica_groups=mesh['blk'=16,'rep'=2] {'rep'}, dimensions={0}, use_global_device_ids=true | all-gather | bytes 393216 | tf_op jit(solution)/shard_map/all_gather | solution.py:115
  35.2 1.3 %collective-permute-start.15 = (bf16[128,512]{1,0:T(8,128)(2,1)S(1)}, bf16[128,512]{1,0:T(8,128)(2,1)S(1)}, u32[]{:S(2)}, u32[]{:S(2)}) collective-permute-start(bf16[128,512]{1,0:T(8,128)(2,1)S(1)} %pad_maximum_fusion.5), channel_id=1, source_target_pairs={{0,8},{2,10},{4,12},{6,14},{8,0},{10,2},{12,4},{14,6},{16,24},{18,... | collective-permute-start | bytes 393224 | tf_op jit(solution)/shard_map/ppermute | solution.py:32
  36.5 1.1 %collective-permute-start.9 = (bf16[128,512]{1,0:T(8,128)(2,1)S(1)}, bf16[128,512]{1,0:T(8,128)(2,1)S(1)}, u32[]{:S(2)}, u32[]{:S(2)}) collective-permute-start(bf16[128,512]{1,0:T(8,128)(2,1)S(1)} %get-tuple-element.8), channel_id=1, source_target_pairs={{0,2},{2,0},{4,6},{6,4},{8,10},{10,8},{12,14},{14,12},{16,18},{18,... | collective-permute-start | bytes 393224 | tf_op jit(solution)/shard_map/ppermute | solution.py:28
  37.7 1.4 %collective-permute-start.11 = (bf16[128,512]{1,0:T(8,128)(2,1)S(1)}, bf16[128,512]{1,0:T(8,128)(2,1)S(1)}, u32[]{:S(2)}, u32[]{:S(2)}) collective-permute-start(bf16[128,512]{1,0:T(8,128)(2,1)S(1)} %get-tuple-element.9), channel_id=1, source_target_pairs={{0,6},{2,4},{4,2},{6,0},{8,14},{10,12},{12,10},{14,8},{16,22},{18,... | collective-permute-start | bytes 393224 | tf_op jit(solution)/shard_map/ppermute | solution.py:28
  39.1 3.2 %collective-permute-done.18 = bf16[512,128]{1,0:T(8,128)(2,1)S(1)} collective-permute-done((bf16[512,128]{1,0:T(8,128)(2,1)S(1)}, bf16[512,128]{1,0:T(8,128)(2,1)S(1)}, u32[]{:S(2)}, u32[]{:S(2)}) %collective-permute-start.18) | collective-permute-done | bytes 131104 | tf_op jit(solution)/shard_map/ppermute | solution.py:32
  42.9 1.1 %collective-permute-start.10 = (bf16[128,512]{1,0:T(8,128)(2,1)S(1)}, bf16[128,512]{1,0:T(8,128)(2,1)S(1)}, u32[]{:S(2)}, u32[]{:S(2)}) collective-permute-start(bf16[128,512]{1,0:T(8,128)(2,1)S(1)} %get-tuple-element.10), channel_id=1, source_target_pairs={{0,4},{2,6},{4,0},{6,2},{8,12},{10,14},{12,8},{14,10},{16,20},{18,... | collective-permute-start | bytes 393224 | tf_op jit(solution)/shard_map/ppermute | solution.py:28
  44.0 1.1 %collective-permute-done.11 = bf16[128,512]{1,0:T(8,128)(2,1)S(1)} collective-permute-done((bf16[128,512]{1,0:T(8,128)(2,1)S(1)}, bf16[128,512]{1,0:T(8,128)(2,1)S(1)}, u32[]{:S(2)}, u32[]{:S(2)}) %collective-permute-start.11) | collective-permute-done | bytes 131104 | tf_op jit(solution)/shard_map/ppermute | solution.py:28
  45.1 3.1 %collective-permute-start.16 = (bf16[64,512]{1,0:T(8,128)(2,1)S(1)}, bf16[64,512]{1,0:T(8,128)(2,1)S(1)}, u32[]{:S(2)}, u32[]{:S(2)}) collective-permute-start(bf16[64,512]{1,0:T(8,128)(2,1)S(1)} %fusion.23), channel_id=1, source_target_pairs={{0,16},{2,18},{4,20},{6,22},{8,24},{10,26},{12,28},{14,30},{16,0},... | collective-permute-start | bytes 196616 | tf_op jit(solution)/shard_map/ppermute | solution.py:32
  48.2 0.7 %collective-permute-done.10 = bf16[128,512]{1,0:T(8,128)(2,1)S(1)} collective-permute-done((bf16[128,512]{1,0:T(8,128)(2,1)S(1)}, bf16[128,512]{1,0:T(8,128)(2,1)S(1)}, u32[]{:S(2)}, u32[]{:S(2)}) %collective-permute-start.10) | collective-permute-done | bytes 131104 | tf_op jit(solution)/shard_map/ppermute | solution.py:28
  48.8 0.7 %add_convert_fusion = bf16[128,512]{1,0:T(8,128)(2,1)} fusion(bf16[128,512]{1,0:T(8,128)(2,1)S(1)} %collective-permute-done.11, bf16[128,512]{1,0:T(8,128)(2,1)S(1)} %collective-permute-done.10, bf16[128,512]{1,0:T(8,128)(2,1)S(1)} %collective-permute-done.9, bf16[512,512]{1,0:T(8,128)(2,1)S(1)} %convolution_convert_fusion.1), kind=kLoop, calls=%fused_computation.28 | loop fusion | flops 524288 | bytes 655360 | tf_op jit(solution)/shard_map/convert_element_type | solution.py:131
  49.6 1.1 %select_convert_fusion = bf16[128,512]{1,0:T(8,128)(2,1)} fusion(bf16[128,512]{1,0:T(8,128)(2,1)S(1)} %collective-permute-done.20, bf16[128,1024]{1,0:T(8,128)(2,1)S(1)} %copy-done.1, s32[]{:T(128)S(6)} %select_n.214, bf16[512,128]{1,0:T(8,128)(2,1)S(1)} %fusion.13, bf16[2,512,1024]{2,1,0:T(8,128)(2,1)S(1)} %bitcast.114, s32[]{:T(128)S(6)} %select_n.279, ...), kind=kOutput, calls=%fused_computation.27 | convolution fusion | flops 67567616 | bytes 1048588 | tf_op jit(solution)/shard_map/dot_general | solution.py:55
  51.1 0.7 %fusion.19 = f32[64,512]{1,0:T(8,128)} fusion(bf16[64,512]{1,0:T(8,128)(2,1)S(1)} %collective-permute-done.16, f32[4,64,512]{2,1,0:T(8,128)S(1)} %bitcast.122, s32[]{:T(128)S(6)} %select_n.271, bf16[128,512]{1,0:T(8,128)(2,1)S(1)} %collective-permute-done.15), kind=kLoop, calls=%fused_computation.39 | loop fusion | flops 131072 | bytes 393220 | tf_op jit(solution)/shard_map/add | solution.py:45
  (56 shorter events, 4.4 us)
Async XLA Ops:
  0.6 11.7 %copy-start = (bf16[1024,1024]{1,0:T(8,128)(2,1)S(1)}, bf16[1024,1024]{1,0:T(8,128)(2,1)}, u32[]{:S(2)}) copy-start(bf16[1024,1024]{1,0:T(8,128)(2,1)} %param.8) | copy-start | bytes 6291460
  0.6 11.7 %copy-start.2 = (bf16[128,1024]{1,0:T(8,128)(2,1)S(1)}, bf16[128,1024]{1,0:T(8,128)(2,1)}, u32[]{:S(2)}) copy-start(bf16[128,1024]{1,0:T(8,128)(2,1)} %param.9) | copy-start | bytes 786436
  1.7 19.1 %collective-permute-start.2 = (bf16[128,512]{1,0:T(8,128)(2,1)S(1)}, bf16[128,512]{1,0:T(8,128)(2,1)S(1)}, u32[]{:S(2)}, u32[]{:S(2)}) collective-permute-start(bf16[128,512]{1,0:T(8,128)(2,1)S(1)} %dynamic-slice_maximum_fusion), channel_id=1, source_target_pairs={{0,24},{2,26},{4,28},{6,30},{8,16},{10,18},{12,20},{14,22},{16,8},... | collective-permute-start | bytes 393224 | tf_op jit(solution)/shard_map/ppermute | solution.py:32
  6.9 14.6 %collective-permute-start.1 = (bf16[128,512]{1,0:T(8,128)(2,1)S(1)}, bf16[128,512]{1,0:T(8,128)(2,1)S(1)}, u32[]{:S(2)}, u32[]{:S(2)}) collective-permute-start(bf16[128,512]{1,0:T(8,128)(2,1)S(1)} %dynamic-slice_maximum_fusion), channel_id=1, source_target_pairs={{0,16},{2,18},{4,20},{6,22},{8,24},{10,26},{12,28},{14,30},{16,0},... | collective-permute-start | bytes 393224 | tf_op jit(solution)/shard_map/ppermute | solution.py:32
  8.7 5.3 %collective-permute-start.5 = (bf16[2,128,128]{2,1,0:T(8,128)(2,1)S(1)}, bf16[2,128,128]{2,1,0:T(8,128)(2,1)S(1)}, u32[]{:S(2)}, u32[]{:S(2)}) collective-permute-start(bf16[2,128,128]{2,1,0:T(8,128)(2,1)S(1)} %get-tuple-element.31), channel_id=1, source_target_pairs={{0,6},{2,4},{4,2},{6,0},{8,14},{10,12},{12,10},{14,8},{16,22},{18,... | collective-permute-start | bytes 196616 | tf_op jit(solution)/shard_map/ppermute | solution.py:28
  11.2 4.3 %collective-permute-start.4 = (bf16[2,128,128]{2,1,0:T(8,128)(2,1)S(1)}, bf16[2,128,128]{2,1,0:T(8,128)(2,1)S(1)}, u32[]{:S(2)}, u32[]{:S(2)}) collective-permute-start(bf16[2,128,128]{2,1,0:T(8,128)(2,1)S(1)} %get-tuple-element.32), channel_id=1, source_target_pairs={{0,4},{2,6},{4,0},{6,2},{8,12},{10,14},{12,8},{14,10},{16,20},{18,... | collective-permute-start | bytes 196616 | tf_op jit(solution)/shard_map/ppermute | solution.py:28
  11.8 5.6 %collective-permute-start.3 = (bf16[2,128,128]{2,1,0:T(8,128)(2,1)S(1)}, bf16[2,128,128]{2,1,0:T(8,128)(2,1)S(1)}, u32[]{:S(2)}, u32[]{:S(2)}) collective-permute-start(bf16[2,128,128]{2,1,0:T(8,128)(2,1)S(1)} %get-tuple-element.33), channel_id=1, source_target_pairs={{0,2},{2,0},{4,6},{6,4},{8,10},{10,8},{12,14},{14,12},{16,18},{18,... | collective-permute-start | bytes 196616 | tf_op jit(solution)/shard_map/ppermute | solution.py:28
  14.1 7.4 %collective-permute-start = (bf16[128,512]{1,0:T(8,128)(2,1)S(1)}, bf16[128,512]{1,0:T(8,128)(2,1)S(1)}, u32[]{:S(2)}, u32[]{:S(2)}) collective-permute-start(bf16[128,512]{1,0:T(8,128)(2,1)S(1)} %dynamic-slice_maximum_fusion), channel_id=1, source_target_pairs={{0,8},{2,10},{4,12},{6,14},{8,0},{10,2},{12,4},{14,6},{16,24},{18,... | collective-permute-start | bytes 393224 | tf_op jit(solution)/shard_map/ppermute | solution.py:32
  15.5 9.2 %collective-permute-start.14 = (bf16[128,512]{1,0:T(8,128)(2,1)S(1)}, bf16[128,512]{1,0:T(8,128)(2,1)S(1)}, u32[]{:S(2)}, u32[]{:S(2)}) collective-permute-start(bf16[128,512]{1,0:T(8,128)(2,1)S(1)} %constant_dynamic-slice_fusion), channel_id=1, source_target_pairs={{0,6},{2,4},{4,2},{6,0},{8,14},{10,12},{12,10},{14,8},{16,22},{18,... | collective-permute-start | bytes 393224 | tf_op jit(solution)/shard_map/ppermute | solution.py:28
  17.3 8.6 %collective-permute-start.13 = (bf16[128,512]{1,0:T(8,128)(2,1)S(1)}, bf16[128,512]{1,0:T(8,128)(2,1)S(1)}, u32[]{:S(2)}, u32[]{:S(2)}) collective-permute-start(bf16[128,512]{1,0:T(8,128)(2,1)S(1)} %constant_dynamic-slice_fusion), channel_id=1, source_target_pairs={{0,4},{2,6},{4,0},{6,2},{8,12},{10,14},{12,8},{14,10},{16,20},{18,... | collective-permute-start | bytes 393224 | tf_op jit(solution)/shard_map/ppermute | solution.py:28
  20.9 6.1 %collective-permute-start.12 = (bf16[128,512]{1,0:T(8,128)(2,1)S(1)}, bf16[128,512]{1,0:T(8,128)(2,1)S(1)}, u32[]{:S(2)}, u32[]{:S(2)}) collective-permute-start(bf16[128,512]{1,0:T(8,128)(2,1)S(1)} %constant_dynamic-slice_fusion), channel_id=1, source_target_pairs={{0,2},{2,0},{4,6},{6,4},{8,10},{10,8},{12,14},{14,12},{16,18},{18,... | collective-permute-start | bytes 393224 | tf_op jit(solution)/shard_map/ppermute | solution.py:28
  22.1 9.2 %collective-permute-start.7 = (bf16[128,512]{1,0:T(8,128)(2,1)S(1)}, bf16[128,512]{1,0:T(8,128)(2,1)S(1)}, u32[]{:S(2)}, u32[]{:S(2)}) collective-permute-start(bf16[128,512]{1,0:T(8,128)(2,1)S(1)} %pad_maximum_fusion.3), channel_id=1, source_target_pairs={{0,4},{2,6},{4,0},{6,2},{8,12},{10,14},{12,8},{14,10},{16,20},{18,... | collective-permute-start | bytes 393224 | tf_op jit(solution)/shard_map/ppermute | solution.py:28
  23.7 7.9 %collective-permute-start.6 = (bf16[128,512]{1,0:T(8,128)(2,1)S(1)}, bf16[128,512]{1,0:T(8,128)(2,1)S(1)}, u32[]{:S(2)}, u32[]{:S(2)}) collective-permute-start(bf16[128,512]{1,0:T(8,128)(2,1)S(1)} %pad_maximum_fusion.2), channel_id=1, source_target_pairs={{0,2},{2,0},{4,6},{6,4},{8,10},{10,8},{12,14},{14,12},{16,18},{18,... | collective-permute-start | bytes 393224 | tf_op jit(solution)/shard_map/ppermute | solution.py:28
  24.7 7.7 %collective-permute-start.8 = (bf16[128,512]{1,0:T(8,128)(2,1)S(1)}, bf16[128,512]{1,0:T(8,128)(2,1)S(1)}, u32[]{:S(2)}, u32[]{:S(2)}) collective-permute-start(bf16[128,512]{1,0:T(8,128)(2,1)S(1)} %pad_maximum_fusion.4), channel_id=1, source_target_pairs={{0,6},{2,4},{4,2},{6,0},{8,14},{10,12},{12,10},{14,8},{16,22},{18,... | collective-permute-start | bytes 393224 | tf_op jit(solution)/shard_map/ppermute | solution.py:28
  27.5 10.1 %collective-permute-start.17 = (bf16[512,128]{1,0:T(8,128)(2,1)S(1)}, bf16[512,128]{1,0:T(8,128)(2,1)S(1)}, u32[]{:S(2)}, u32[]{:S(2)}) collective-permute-start(bf16[512,128]{1,0:T(8,128)(2,1)S(1)} %get-tuple-element.3), channel_id=1, source_target_pairs={{0,8},{2,10},{4,12},{6,14},{8,0},{10,2},{12,4},{14,6},{16,24},{18,... | collective-permute-start | bytes 393224 | tf_op jit(solution)/shard_map/ppermute | solution.py:32
  28.6 10.5 %collective-permute-start.19 = (bf16[512,128]{1,0:T(8,128)(2,1)S(1)}, bf16[512,128]{1,0:T(8,128)(2,1)S(1)}, u32[]{:S(2)}, u32[]{:S(2)}) collective-permute-start(bf16[512,128]{1,0:T(8,128)(2,1)S(1)} %get-tuple-element.4), channel_id=1, source_target_pairs={{0,24},{2,26},{4,28},{6,30},{8,16},{10,18},{12,20},{14,22},{16,8},... | collective-permute-start | bytes 393224 | tf_op jit(solution)/shard_map/ppermute | solution.py:32
  31.4 10.9 %collective-permute-start.18 = (bf16[512,128]{1,0:T(8,128)(2,1)S(1)}, bf16[512,128]{1,0:T(8,128)(2,1)S(1)}, u32[]{:S(2)}, u32[]{:S(2)}) collective-permute-start(bf16[512,128]{1,0:T(8,128)(2,1)S(1)} %get-tuple-element.5), channel_id=1, source_target_pairs={{0,16},{2,18},{4,20},{6,22},{8,24},{10,26},{12,28},{14,30},{16,0},... | collective-permute-start | bytes 393224 | tf_op jit(solution)/shard_map/ppermute | solution.py:32
  35.1 14.4 %copy-start.1 = (bf16[128,1024]{1,0:T(8,128)(2,1)S(1)}, bf16[128,1024]{1,0:T(8,128)(2,1)}, u32[]{:S(2)}) copy-start(bf16[128,1024]{1,0:T(8,128)(2,1)} %param.5) | copy-start | bytes 786436
  35.2 8.8 %collective-permute-start.15 = (bf16[128,512]{1,0:T(8,128)(2,1)S(1)}, bf16[128,512]{1,0:T(8,128)(2,1)S(1)}, u32[]{:S(2)}, u32[]{:S(2)}) collective-permute-start(bf16[128,512]{1,0:T(8,128)(2,1)S(1)} %pad_maximum_fusion.5), channel_id=1, source_target_pairs={{0,8},{2,10},{4,12},{6,14},{8,0},{10,2},{12,4},{14,6},{16,24},{18,... | collective-permute-start | bytes 393224 | tf_op jit(solution)/shard_map/ppermute | solution.py:32
  36.5 7.5 %collective-permute-start.9 = (bf16[128,512]{1,0:T(8,128)(2,1)S(1)}, bf16[128,512]{1,0:T(8,128)(2,1)S(1)}, u32[]{:S(2)}, u32[]{:S(2)}) collective-permute-start(bf16[128,512]{1,0:T(8,128)(2,1)S(1)} %get-tuple-element.8), channel_id=1, source_target_pairs={{0,2},{2,0},{4,6},{6,4},{8,10},{10,8},{12,14},{14,12},{16,18},{18,... | collective-permute-start | bytes 393224 | tf_op jit(solution)/shard_map/ppermute | solution.py:28
  37.7 7.4 %collective-permute-start.11 = (bf16[128,512]{1,0:T(8,128)(2,1)S(1)}, bf16[128,512]{1,0:T(8,128)(2,1)S(1)}, u32[]{:S(2)}, u32[]{:S(2)}) collective-permute-start(bf16[128,512]{1,0:T(8,128)(2,1)S(1)} %get-tuple-element.9), channel_id=1, source_target_pairs={{0,6},{2,4},{4,2},{6,0},{8,14},{10,12},{12,10},{14,8},{16,22},{18,... | collective-permute-start | bytes 393224 | tf_op jit(solution)/shard_map/ppermute | solution.py:28
  42.8 6.7 %collective-permute-start.20 = (bf16[128,512]{1,0:T(8,128)(2,1)S(1)}, bf16[128,512]{1,0:T(8,128)(2,1)S(1)}, u32[]{:S(2)}, u32[]{:S(2)}) collective-permute-start(bf16[128,512]{1,0:T(8,128)(2,1)S(1)} %convolution_convert_fusion.2), channel_id=1, source_target_pairs={{0,1},{1,0},{2,3},{3,2},{4,5},{5,4},{6,7},{7,6},{8,9},{9,8},{10,11... | collective-permute-start | bytes 393224 | tf_op jit(solution)/shard_map/ppermute | solution.py:52
  42.9 5.9 %collective-permute-start.10 = (bf16[128,512]{1,0:T(8,128)(2,1)S(1)}, bf16[128,512]{1,0:T(8,128)(2,1)S(1)}, u32[]{:S(2)}, u32[]{:S(2)}) collective-permute-start(bf16[128,512]{1,0:T(8,128)(2,1)S(1)} %get-tuple-element.10), channel_id=1, source_target_pairs={{0,4},{2,6},{4,0},{6,2},{8,12},{10,14},{12,8},{14,10},{16,20},{18,... | collective-permute-start | bytes 393224 | tf_op jit(solution)/shard_map/ppermute | solution.py:28
  45.1 6.0 %collective-permute-start.16 = (bf16[64,512]{1,0:T(8,128)(2,1)S(1)}, bf16[64,512]{1,0:T(8,128)(2,1)S(1)}, u32[]{:S(2)}, u32[]{:S(2)}) collective-permute-start(bf16[64,512]{1,0:T(8,128)(2,1)S(1)} %fusion.23), channel_id=1, source_target_pairs={{0,16},{2,18},{4,20},{6,22},{8,24},{10,26},{12,28},{14,30},{16,0},... | collective-permute-start | bytes 196616 | tf_op jit(solution)/shard_map/ppermute | solution.py:32

commit v30 on v29

--- a/solution.py
+++ b/solution.py
@@ -138,13 +138,12 @@
             lax.dynamic_index_in_dim(w_rows, 1 - rep_pos, 0, keepdims=False), rep_pos
         )
         grad_in = to_other(dot(back, w_other, ((0,), (1,))).astype(bf16)).astype(jnp.float32)
-        grad_in = grad_in + dot(back, w_mine, ((0,), (1,)))
+        grad_in = grad_in + lax.optimization_barrier(dot(back, w_mine, ((0,), (1,))))
     else:
         back_full = lax.all_gather(back, "rep", axis=0, tiled=True)
         w_mine = lax.dynamic_index_in_dim(w_rows, rep_pos, 0, keepdims=False)
         grad_in = dot(back_full, w_mine, ((0,), (1,)))
-    pre_part = columns_of(hidden_pre, rep_pos)
-    grad_pre = jnp.where(pre_part > 0, grad_in, 0.0).astype(bf16)
+    grad_pre = jnp.where(hidden_part > 0, grad_in, 0.0).astype(bf16)
     return (out_part, grad_weight, grad_pre)
 
 

time: 52 us -> 56.3 us (1.083)
  waiting for transfers between devices: 9.8 us -> 15.4 us
  starting transfers between devices: 28.7 us -> 27.3 us
  other arithmetic: 3.85 us -> 4.56 us
  matrix products: 3.09 us -> 2.42 us
    ppermute x8, waiting for transfers between devices: 3.69 us -> 8.74 us  [along_outer(): return lax.ppermute(value, 'blk', pairs) if turn else value]
    ppermute x8, starting transfers between devices: 14.2 us -> 12.8 us  [along_outer(): return lax.ppermute(value, 'blk', pairs) if turn else value]
    convert_element_type x0 -> x1, other arithmetic: none -> 0.71 us  [shards(): grad_pre = jnp.where(hidden_part > 0, grad_in, 0.0).astype(bf16)]
    dot_general x6, matrix products: 3.09 us -> 2.42 us  [dot(): lax.dot_general(lhs, rhs, (dims, ((), ())), preferred_element_type=jnp.fl...]
    ppermute x12, waiting for transfers between devices: 6.11 us -> 6.7 us  [along_inner(): return lax.ppermute(value, 'blk', pairs) if turn else value]
  transfers between devices with their start and end apart: 21 -> 21, of which waited for: 8 -> 10; matrix products, arithmetic and copies ran while one was open for 12% -> 11% of each run, Pallas kernels for 0% -> 0%
where the time goes in v30:
time: 56.3 us; the launch traced here: 56.1 us
  starting transfers between devices  27.3 us (48%)
  waiting for transfers between devices  15.4 us (27%)
  other arithmetic  4.56 us (8%)
  blocking collectives  4.18 us (7%)
  matrix products  2.42 us (4%)
  local copies, waits for them, and re-layouts  1.24 us (2%)
  between operations  0.94 us (2%)
    ppermute x12, starting transfers between devices, along_inner(): return lax.ppermute(value, 'blk', pairs) if turn else value  14.4 us
    ppermute x8, starting transfers between devices, along_outer(): return lax.ppermute(value, 'blk', pairs) if turn else value  12.8 us
    ppermute x8, waiting for transfers between devices, along_outer(): return lax.ppermute(value, 'blk', pairs) if turn else value  8.74 us
    ppermute x12, waiting for transfers between devices, along_inner(): return lax.ppermute(value, 'blk', pairs) if turn else value  6.7 us
    dot_general x6, matrix products, dot(): lax.dot_general(lhs, rhs, (dims, ((), ())), preferred_element_type=jnp.fl...  2.42 us
    all_gather x1, blocking collectives, shards(): everyone = lax.all_gather(jnp.concatenate(arrived, 0), 'rep', axis=0)  2.18 us
    all_gather x1, blocking collectives, shards(): lax.all_gather(mixed_cols.astype(bf16), 'rep', axis=0, tiled=True)  1.99 us
  transfers between devices with their start and end apart: 21, of which 10 were waited for; matrix products, arithmetic and copies ran while one was open for 11% of the time, Pallas kernels for 0%

profile of v30, /device:TPU:0, one launch (start us, length us, event | category | flops | bytes accessed | tf_op | source)
XLA Modules:
  0.0 56.1 jit_solution(17626549482707404580)
XLA Ops:
  0.7 1.1 %dynamic-slice_maximum_fusion = bf16[128,512]{1,0:T(8,128)(2,1)S(1)} fusion(bf16[128,1024]{1,0:T(8,128)(2,1)} %param.5, s32[]{:T(128)S(6)} %select_n.213), kind=kLoop, calls=%fused_computation.42 | loop fusion | flops 262144 | bytes 262148 | tf_op jit(solution)/shard_map/max | solution.py:69
  1.7 5.1 %collective-permute-start.2 = (bf16[128,512]{1,0:T(8,128)(2,1)S(1)}, bf16[128,512]{1,0:T(8,128)(2,1)S(1)}, u32[]{:S(2)}, u32[]{:S(2)}) collective-permute-start(bf16[128,512]{1,0:T(8,128)(2,1)S(1)} %dynamic-slice_maximum_fusion), channel_id=1, source_target_pairs={{0,24},{2,26},{4,28},{6,30},{8,16},{10,18},{12,20},{14,22},{16,8},... | collective-permute-start | bytes 393224 | tf_op jit(solution)/shard_map/ppermute | solution.py:32
  6.9 0.7 %add_bitcast_fusion = s32[8]{0:T(128)S(1)} fusion(s32[1,8]{1,0:T(1,128)} %param.7, s32[]{:T(128)S(6)} %shift_right_arithmetic.54, s32[]{:T(128)S(6)} %and.60), kind=kLoop, calls=%fused_computation.92 | loop fusion | flops 56 | bytes 72 | tf_op jit(solution)/shard_map/eq | solution.py:75
  7.6 0.9 %slice_bitcast_fusion.9 = (bf16[128,128]{1,0:T(8,128)(2,1)S(1)}, bf16[128,128]{1,0:T(8,128)(2,1)S(1)}, bf16[128,128]{1,0:T(8,128)(2,1)S(1)}, bf16[128,128]{1,0:T...) fusion(bf16[1,8,128,128]{3,2,1,0:T(8,128)(2,1)} %param.6), kind=kLoop, calls=%fused_computation.73 | loop fusion | bytes 524288 | tf_op jit(solution)/shard_map/jit(_where)/broadcast_in_dim | solution.py:78
  8.7 2.5 %collective-permute-start.5 = (bf16[2,128,128]{2,1,0:T(8,128)(2,1)S(1)}, bf16[2,128,128]{2,1,0:T(8,128)(2,1)S(1)}, u32[]{:S(2)}, u32[]{:S(2)}) collective-permute-start(bf16[2,128,128]{2,1,0:T(8,128)(2,1)S(1)} %get-tuple-element.31), channel_id=1, source_target_pairs={{0,6},{2,4},{4,2},{6,0},{8,14},{10,12},{12,10},{14,8},{16,22},{18,... | collective-permute-start | bytes 196616 | tf_op jit(solution)/shard_map/ppermute | solution.py:28
  12.4 1.7 %collective-permute-done.5 = bf16[2,128,128]{2,1,0:T(8,128)(2,1)S(1)} collective-permute-done((bf16[2,128,128]{2,1,0:T(8,128)(2,1)S(1)}, bf16[2,128,128]{2,1,0:T(8,128)(2,1)S(1)}, u32[]{:S(2)}, u32[]{:S(2)}) %collective-permute-start.5) | collective-permute-done | bytes 65568 | tf_op jit(solution)/shard_map/ppermute | solution.py:28
  14.1 0.6 %collective-permute-start = (bf16[128,512]{1,0:T(8,128)(2,1)S(1)}, bf16[128,512]{1,0:T(8,128)(2,1)S(1)}, u32[]{:S(2)}, u32[]{:S(2)}) collective-permute-start(bf16[128,512]{1,0:T(8,128)(2,1)S(1)} %dynamic-slice_maximum_fusion), channel_id=1, source_target_pairs={{0,8},{2,10},{4,12},{6,14},{8,0},{10,2},{12,4},{14,6},{16,24},{18,... | collective-permute-start | bytes 393224 | tf_op jit(solution)/shard_map/ppermute | solution.py:32
  14.7 0.8 %collective-permute-done.4 = bf16[2,128,128]{2,1,0:T(8,128)(2,1)S(1)} collective-permute-done((bf16[2,128,128]{2,1,0:T(8,128)(2,1)S(1)}, bf16[2,128,128]{2,1,0:T(8,128)(2,1)S(1)}, u32[]{:S(2)}, u32[]{:S(2)}) %collective-permute-start.4) | collective-permute-done | bytes 65568 | tf_op jit(solution)/shard_map/ppermute | solution.py:28
  15.5 1.8 %collective-permute-start.14 = (bf16[128,512]{1,0:T(8,128)(2,1)S(1)}, bf16[128,512]{1,0:T(8,128)(2,1)S(1)}, u32[]{:S(2)}, u32[]{:S(2)}) collective-permute-start(bf16[128,512]{1,0:T(8,128)(2,1)S(1)} %constant_dynamic-slice_fusion), channel_id=1, source_target_pairs={{0,6},{2,4},{4,2},{6,0},{8,14},{10,12},{12,10},{14,8},{16,22},{18,... | collective-permute-start | bytes 393224 | tf_op jit(solution)/shard_map/ppermute | solution.py:28
  17.3 1.1 %collective-permute-start.13 = (bf16[128,512]{1,0:T(8,128)(2,1)S(1)}, bf16[128,512]{1,0:T(8,128)(2,1)S(1)}, u32[]{:S(2)}, u32[]{:S(2)}) collective-permute-start(bf16[128,512]{1,0:T(8,128)(2,1)S(1)} %constant_dynamic-slice_fusion), channel_id=1, source_target_pairs={{0,4},{2,6},{4,0},{6,2},{8,12},{10,14},{12,8},{14,10},{16,20},{18,... | collective-permute-start | bytes 393224 | tf_op jit(solution)/shard_map/ppermute | solution.py:28
  18.5 2.2 %all-gather = bf16[16,128,128]{2,1,0:T(8,128)(2,1)S(1)} all-gather(bf16[8,128,128]{2,1,0:T(8,128)(2,1)S(1)} %pad_maximum_fusion.1), channel_id=2, replica_groups=mesh['blk'=16,'rep'=2] {'rep'}, dimensions={0}, use_global_device_ids=true | all-gather | bytes 786432 | tf_op jit(solution)/shard_map/all_gather | solution.py:82
  22.1 1.5 %collective-permute-start.7 = (bf16[128,512]{1,0:T(8,128)(2,1)S(1)}, bf16[128,512]{1,0:T(8,128)(2,1)S(1)}, u32[]{:S(2)}, u32[]{:S(2)}) collective-permute-start(bf16[128,512]{1,0:T(8,128)(2,1)S(1)} %pad_maximum_fusion.3), channel_id=1, source_target_pairs={{0,4},{2,6},{4,0},{6,2},{8,12},{10,14},{12,8},{14,10},{16,20},{18,... | collective-permute-start | bytes 393224 | tf_op jit(solution)/shard_map/ppermute | solution.py:28
  23.7 1.0 %collective-permute-start.6 = (bf16[128,512]{1,0:T(8,128)(2,1)S(1)}, bf16[128,512]{1,0:T(8,128)(2,1)S(1)}, u32[]{:S(2)}, u32[]{:S(2)}) collective-permute-start(bf16[128,512]{1,0:T(8,128)(2,1)S(1)} %pad_maximum_fusion.2), channel_id=1, source_target_pairs={{0,2},{2,0},{4,6},{6,4},{8,10},{10,8},{12,14},{14,12},{16,18},{18,... | collective-permute-start | bytes 393224 | tf_op jit(solution)/shard_map/ppermute | solution.py:28
  24.7 1.2 %collective-permute-start.8 = (bf16[128,512]{1,0:T(8,128)(2,1)S(1)}, bf16[128,512]{1,0:T(8,128)(2,1)S(1)}, u32[]{:S(2)}, u32[]{:S(2)}) collective-permute-start(bf16[128,512]{1,0:T(8,128)(2,1)S(1)} %pad_maximum_fusion.4), channel_id=1, source_target_pairs={{0,6},{2,4},{4,2},{6,0},{8,14},{10,12},{12,10},{14,8},{16,22},{18,... | collective-permute-start | bytes 393224 | tf_op jit(solution)/shard_map/ppermute | solution.py:28
  25.9 1.1 %collective-permute-done.12 = bf16[128,512]{1,0:T(8,128)(2,1)S(1)} collective-permute-done((bf16[128,512]{1,0:T(8,128)(2,1)S(1)}, bf16[128,512]{1,0:T(8,128)(2,1)S(1)}, u32[]{:S(2)}, u32[]{:S(2)}) %collective-permute-start.12) | collective-permute-done | bytes 131104 | tf_op jit(solution)/shard_map/ppermute | solution.py:28
  27.5 1.0 %collective-permute-start.17 = (bf16[512,128]{1,0:T(8,128)(2,1)S(1)}, bf16[512,128]{1,0:T(8,128)(2,1)S(1)}, u32[]{:S(2)}, u32[]{:S(2)}) collective-permute-start(bf16[512,128]{1,0:T(8,128)(2,1)S(1)} %get-tuple-element.3), channel_id=1, source_target_pairs={{0,8},{2,10},{4,12},{6,14},{8,0},{10,2},{12,4},{14,6},{16,24},{18,... | collective-permute-start | bytes 393224 | tf_op jit(solution)/shard_map/ppermute | solution.py:32
  28.6 2.8 %collective-permute-start.19 = (bf16[512,128]{1,0:T(8,128)(2,1)S(1)}, bf16[512,128]{1,0:T(8,128)(2,1)S(1)}, u32[]{:S(2)}, u32[]{:S(2)}) collective-permute-start(bf16[512,128]{1,0:T(8,128)(2,1)S(1)} %get-tuple-element.4), channel_id=1, source_target_pairs={{0,24},{2,26},{4,28},{6,30},{8,16},{10,18},{12,20},{14,22},{16,8},... | collective-permute-start | bytes 393224 | tf_op jit(solution)/shard_map/ppermute | solution.py:32
  31.6 0.8 %collective-permute-done.8 = bf16[128,512]{1,0:T(8,128)(2,1)S(1)} collective-permute-done((bf16[128,512]{1,0:T(8,128)(2,1)S(1)}, bf16[128,512]{1,0:T(8,128)(2,1)S(1)}, u32[]{:S(2)}, u32[]{:S(2)}) %collective-permute-start.8) | collective-permute-done | bytes 131104 | tf_op jit(solution)/shard_map/ppermute | solution.py:28
  32.5 2.0 %all_gather.11 = bf16[256,512]{1,0:T(8,128)(2,1)S(1)} all-gather(bf16[128,512]{1,0:T(8,128)(2,1)S(1)} %fusion.16), channel_id=1, replica_groups=mesh['blk'=16,'rep'=2] {'rep'}, dimensions={0}, use_global_device_ids=true | all-gather | bytes 393216 | tf_op jit(solution)/shard_map/all_gather | solution.py:115
  35.2 2.6 %collective-permute-done.19 = bf16[512,128]{1,0:T(8,128)(2,1)S(1)} collective-permute-done((bf16[512,128]{1,0:T(8,128)(2,1)S(1)}, bf16[512,128]{1,0:T(8,128)(2,1)S(1)}, u32[]{:S(2)}, u32[]{:S(2)}) %collective-permute-start.19) | collective-permute-done | bytes 131104 | tf_op jit(solution)/shard_map/ppermute | solution.py:32
  37.8 4.4 %collective-permute-done.18 = bf16[512,128]{1,0:T(8,128)(2,1)S(1)} collective-permute-done((bf16[512,128]{1,0:T(8,128)(2,1)S(1)}, bf16[512,128]{1,0:T(8,128)(2,1)S(1)}, u32[]{:S(2)}, u32[]{:S(2)}) %collective-permute-start.18) | collective-permute-done | bytes 131104 | tf_op jit(solution)/shard_map/ppermute | solution.py:32
  42.9 1.0 %collective-permute-start.9 = (bf16[128,512]{1,0:T(8,128)(2,1)S(1)}, bf16[128,512]{1,0:T(8,128)(2,1)S(1)}, u32[]{:S(2)}, u32[]{:S(2)}) collective-permute-start(bf16[128,512]{1,0:T(8,128)(2,1)S(1)} %get-tuple-element.8), channel_id=1, source_target_pairs={{0,2},{2,0},{4,6},{6,4},{8,10},{10,8},{12,14},{14,12},{16,18},{18,... | collective-permute-start | bytes 393224 | tf_op jit(solution)/shard_map/ppermute | solution.py:28
  43.8 1.6 %collective-permute-start.11 = (bf16[128,512]{1,0:T(8,128)(2,1)S(1)}, bf16[128,512]{1,0:T(8,128)(2,1)S(1)}, u32[]{:S(2)}, u32[]{:S(2)}) collective-permute-start(bf16[128,512]{1,0:T(8,128)(2,1)S(1)} %get-tuple-element.9), channel_id=1, source_target_pairs={{0,6},{2,4},{4,2},{6,0},{8,14},{10,12},{12,10},{14,8},{16,22},{18,... | collective-permute-start | bytes 393224 | tf_op jit(solution)/shard_map/ppermute | solution.py:28
  45.9 1.1 %collective-permute-start.10 = (bf16[128,512]{1,0:T(8,128)(2,1)S(1)}, bf16[128,512]{1,0:T(8,128)(2,1)S(1)}, u32[]{:S(2)}, u32[]{:S(2)}) collective-permute-start(bf16[128,512]{1,0:T(8,128)(2,1)S(1)} %get-tuple-element.10), channel_id=1, source_target_pairs={{0,4},{2,6},{4,0},{6,2},{8,12},{10,14},{12,8},{14,10},{16,20},{18,... | collective-permute-start | bytes 393224 | tf_op jit(solution)/shard_map/ppermute | solution.py:28
  47.0 0.8 %collective-permute-done.15 = bf16[128,512]{1,0:T(8,128)(2,1)S(1)} collective-permute-done((bf16[128,512]{1,0:T(8,128)(2,1)S(1)}, bf16[128,512]{1,0:T(8,128)(2,1)S(1)}, u32[]{:S(2)}, u32[]{:S(2)}) %collective-permute-start.15) | collective-permute-done | bytes 131104 | tf_op jit(solution)/shard_map/ppermute | solution.py:32
  47.8 0.6 %collective-permute-done.9 = bf16[128,512]{1,0:T(8,128)(2,1)S(1)} collective-permute-done((bf16[128,512]{1,0:T(8,128)(2,1)S(1)}, bf16[128,512]{1,0:T(8,128)(2,1)S(1)}, u32[]{:S(2)}, u32[]{:S(2)}) %collective-permute-start.9) | collective-permute-done | bytes 131104 | tf_op jit(solution)/shard_map/ppermute | solution.py:28
  48.5 1.7 %collective-permute-done.11 = bf16[128,512]{1,0:T(8,128)(2,1)S(1)} collective-permute-done((bf16[128,512]{1,0:T(8,128)(2,1)S(1)}, bf16[128,512]{1,0:T(8,128)(2,1)S(1)}, u32[]{:S(2)}, u32[]{:S(2)}) %collective-permute-start.11) | collective-permute-done | bytes 131104 | tf_op jit(solution)/shard_map/ppermute | solution.py:28
  50.2 2.9 %collective-permute-start.16 = (bf16[64,512]{1,0:T(8,128)(2,1)S(1)}, bf16[64,512]{1,0:T(8,128)(2,1)S(1)}, u32[]{:S(2)}, u32[]{:S(2)}) collective-permute-start(bf16[64,512]{1,0:T(8,128)(2,1)S(1)} %fusion.23), channel_id=1, source_target_pairs={{0,16},{2,18},{4,20},{6,22},{8,24},{10,26},{12,28},{14,30},{16,0},... | collective-permute-start | bytes 196616 | tf_op jit(solution)/shard_map/ppermute | solution.py:32
  53.1 0.7 %add_convert_fusion = bf16[128,512]{1,0:T(8,128)(2,1)} fusion(bf16[128,512]{1,0:T(8,128)(2,1)S(1)} %collective-permute-done.11, bf16[128,512]{1,0:T(8,128)(2,1)S(1)} %collective-permute-done.10, bf16[128,512]{1,0:T(8,128)(2,1)S(1)} %collective-permute-done.9, bf16[512,512]{1,0:T(8,128)(2,1)S(1)} %convolution_convert_fusion.1), kind=kLoop, calls=%fused_computation.28 | loop fusion | flops 524288 | bytes 655360 | tf_op jit(solution)/shard_map/convert_element_type | solution.py:131
  53.8 0.7 %select_convert_fusion = bf16[128,512]{1,0:T(8,128)(2,1)} fusion(f32[128,512]{1,0:T(8,128)S(1)} %fusion.8, bf16[128,512]{1,0:T(8,128)(2,1)S(1)} %collective-permute-done.20, bf16[128,1024]{1,0:T(8,128)(2,1)S(1)} %copy-done.1, s32[]{:T(128)S(6)} %select_n.213), kind=kLoop, calls=%fused_computation.27 | loop fusion | flops 458752 | bytes 655364 | tf_op jit(solution)/shard_map/convert_element_type | solution.py:146
  54.5 0.9 %collective-permute-done.16 = bf16[64,512]{1,0:T(8,128)(2,1)S(1)} collective-permute-done((bf16[64,512]{1,0:T(8,128)(2,1)S(1)}, bf16[64,512]{1,0:T(8,128)(2,1)S(1)}, u32[]{:S(2)}, u32[]{:S(2)}) %collective-permute-start.16) | collective-permute-done | bytes 65568 | tf_op jit(solution)/shard_map/ppermute | solution.py:32
  55.4 0.7 %fusion.19 = f32[64,512]{1,0:T(8,128)} fusion(bf16[64,512]{1,0:T(8,128)(2,1)S(1)} %collective-permute-done.16, f32[4,64,512]{2,1,0:T(8,128)S(1)} %bitcast.120, s32[]{:T(128)S(6)} %select_n.270, bf16[128,512]{1,0:T(8,128)(2,1)S(1)} %collective-permute-done.15), kind=kLoop, calls=%fused_computation.39 | loop fusion | flops 131072 | bytes 393220 | tf_op jit(solution)/shard_map/add | solution.py:45
  (57 shorter events, 5.5 us)
Async XLA Ops:
  0.6 11.7 %copy-start = (bf16[1024,1024]{1,0:T(8,128)(2,1)S(1)}, bf16[1024,1024]{1,0:T(8,128)(2,1)}, u32[]{:S(2)}) copy-start(bf16[1024,1024]{1,0:T(8,128)(2,1)} %param.8) | copy-start | bytes 6291460
  0.6 11.7 %copy-start.2 = (bf16[128,1024]{1,0:T(8,128)(2,1)S(1)}, bf16[128,1024]{1,0:T(8,128)(2,1)}, u32[]{:S(2)}) copy-start(bf16[128,1024]{1,0:T(8,128)(2,1)} %param.9) | copy-start | bytes 786436
  1.7 19.1 %collective-permute-start.2 = (bf16[128,512]{1,0:T(8,128)(2,1)S(1)}, bf16[128,512]{1,0:T(8,128)(2,1)S(1)}, u32[]{:S(2)}, u32[]{:S(2)}) collective-permute-start(bf16[128,512]{1,0:T(8,128)(2,1)S(1)} %dynamic-slice_maximum_fusion), channel_id=1, source_target_pairs={{0,24},{2,26},{4,28},{6,30},{8,16},{10,18},{12,20},{14,22},{16,8},... | collective-permute-start | bytes 393224 | tf_op jit(solution)/shard_map/ppermute | solution.py:32
  6.9 14.6 %collective-permute-start.1 = (bf16[128,512]{1,0:T(8,128)(2,1)S(1)}, bf16[128,512]{1,0:T(8,128)(2,1)S(1)}, u32[]{:S(2)}, u32[]{:S(2)}) collective-permute-start(bf16[128,512]{1,0:T(8,128)(2,1)S(1)} %dynamic-slice_maximum_fusion), channel_id=1, source_target_pairs={{0,16},{2,18},{4,20},{6,22},{8,24},{10,26},{12,28},{14,30},{16,0},... | collective-permute-start | bytes 393224 | tf_op jit(solution)/shard_map/ppermute | solution.py:32
  8.7 5.3 %collective-permute-start.5 = (bf16[2,128,128]{2,1,0:T(8,128)(2,1)S(1)}, bf16[2,128,128]{2,1,0:T(8,128)(2,1)S(1)}, u32[]{:S(2)}, u32[]{:S(2)}) collective-permute-start(bf16[2,128,128]{2,1,0:T(8,128)(2,1)S(1)} %get-tuple-element.31), channel_id=1, source_target_pairs={{0,6},{2,4},{4,2},{6,0},{8,14},{10,12},{12,10},{14,8},{16,22},{18,... | collective-permute-start | bytes 196616 | tf_op jit(solution)/shard_map/ppermute | solution.py:28
  11.2 4.3 %collective-permute-start.4 = (bf16[2,128,128]{2,1,0:T(8,128)(2,1)S(1)}, bf16[2,128,128]{2,1,0:T(8,128)(2,1)S(1)}, u32[]{:S(2)}, u32[]{:S(2)}) collective-permute-start(bf16[2,128,128]{2,1,0:T(8,128)(2,1)S(1)} %get-tuple-element.32), channel_id=1, source_target_pairs={{0,4},{2,6},{4,0},{6,2},{8,12},{10,14},{12,8},{14,10},{16,20},{18,... | collective-permute-start | bytes 196616 | tf_op jit(solution)/shard_map/ppermute | solution.py:28
  11.8 5.6 %collective-permute-start.3 = (bf16[2,128,128]{2,1,0:T(8,128)(2,1)S(1)}, bf16[2,128,128]{2,1,0:T(8,128)(2,1)S(1)}, u32[]{:S(2)}, u32[]{:S(2)}) collective-permute-start(bf16[2,128,128]{2,1,0:T(8,128)(2,1)S(1)} %get-tuple-element.33), channel_id=1, source_target_pairs={{0,2},{2,0},{4,6},{6,4},{8,10},{10,8},{12,14},{14,12},{16,18},{18,... | collective-permute-start | bytes 196616 | tf_op jit(solution)/shard_map/ppermute | solution.py:28
  14.1 7.4 %collective-permute-start = (bf16[128,512]{1,0:T(8,128)(2,1)S(1)}, bf16[128,512]{1,0:T(8,128)(2,1)S(1)}, u32[]{:S(2)}, u32[]{:S(2)}) collective-permute-start(bf16[128,512]{1,0:T(8,128)(2,1)S(1)} %dynamic-slice_maximum_fusion), channel_id=1, source_target_pairs={{0,8},{2,10},{4,12},{6,14},{8,0},{10,2},{12,4},{14,6},{16,24},{18,... | collective-permute-start | bytes 393224 | tf_op jit(solution)/shard_map/ppermute | solution.py:32
  15.5 9.2 %collective-permute-start.14 = (bf16[128,512]{1,0:T(8,128)(2,1)S(1)}, bf16[128,512]{1,0:T(8,128)(2,1)S(1)}, u32[]{:S(2)}, u32[]{:S(2)}) collective-permute-start(bf16[128,512]{1,0:T(8,128)(2,1)S(1)} %constant_dynamic-slice_fusion), channel_id=1, source_target_pairs={{0,6},{2,4},{4,2},{6,0},{8,14},{10,12},{12,10},{14,8},{16,22},{18,... | collective-permute-start | bytes 393224 | tf_op jit(solution)/shard_map/ppermute | solution.py:28
  17.3 8.6 %collective-permute-start.13 = (bf16[128,512]{1,0:T(8,128)(2,1)S(1)}, bf16[128,512]{1,0:T(8,128)(2,1)S(1)}, u32[]{:S(2)}, u32[]{:S(2)}) collective-permute-start(bf16[128,512]{1,0:T(8,128)(2,1)S(1)} %constant_dynamic-slice_fusion), channel_id=1, source_target_pairs={{0,4},{2,6},{4,0},{6,2},{8,12},{10,14},{12,8},{14,10},{16,20},{18,... | collective-permute-start | bytes 393224 | tf_op jit(solution)/shard_map/ppermute | solution.py:28
  20.9 6.1 %collective-permute-start.12 = (bf16[128,512]{1,0:T(8,128)(2,1)S(1)}, bf16[128,512]{1,0:T(8,128)(2,1)S(1)}, u32[]{:S(2)}, u32[]{:S(2)}) collective-permute-start(bf16[128,512]{1,0:T(8,128)(2,1)S(1)} %constant_dynamic-slice_fusion), channel_id=1, source_target_pairs={{0,2},{2,0},{4,6},{6,4},{8,10},{10,8},{12,14},{14,12},{16,18},{18,... | collective-permute-start | bytes 393224 | tf_op jit(solution)/shard_map/ppermute | solution.py:28
  22.1 9.2 %collective-permute-start.7 = (bf16[128,512]{1,0:T(8,128)(2,1)S(1)}, bf16[128,512]{1,0:T(8,128)(2,1)S(1)}, u32[]{:S(2)}, u32[]{:S(2)}) collective-permute-start(bf16[128,512]{1,0:T(8,128)(2,1)S(1)} %pad_maximum_fusion.3), channel_id=1, source_target_pairs={{0,4},{2,6},{4,0},{6,2},{8,12},{10,14},{12,8},{14,10},{16,20},{18,... | collective-permute-start | bytes 393224 | tf_op jit(solution)/shard_map/ppermute | solution.py:28
  23.7 7.9 %collective-permute-start.6 = (bf16[128,512]{1,0:T(8,128)(2,1)S(1)}, bf16[128,512]{1,0:T(8,128)(2,1)S(1)}, u32[]{:S(2)}, u32[]{:S(2)}) collective-permute-start(bf16[128,512]{1,0:T(8,128)(2,1)S(1)} %pad_maximum_fusion.2), channel_id=1, source_target_pairs={{0,2},{2,0},{4,6},{6,4},{8,10},{10,8},{12,14},{14,12},{16,18},{18,... | collective-permute-start | bytes 393224 | tf_op jit(solution)/shard_map/ppermute | solution.py:28
  24.7 7.7 %collective-permute-start.8 = (bf16[128,512]{1,0:T(8,128)(2,1)S(1)}, bf16[128,512]{1,0:T(8,128)(2,1)S(1)}, u32[]{:S(2)}, u32[]{:S(2)}) collective-permute-start(bf16[128,512]{1,0:T(8,128)(2,1)S(1)} %pad_maximum_fusion.4), channel_id=1, source_target_pairs={{0,6},{2,4},{4,2},{6,0},{8,14},{10,12},{12,10},{14,8},{16,22},{18,... | collective-permute-start | bytes 393224 | tf_op jit(solution)/shard_map/ppermute | solution.py:28
  27.5 7.7 %collective-permute-start.17 = (bf16[512,128]{1,0:T(8,128)(2,1)S(1)}, bf16[512,128]{1,0:T(8,128)(2,1)S(1)}, u32[]{:S(2)}, u32[]{:S(2)}) collective-permute-start(bf16[512,128]{1,0:T(8,128)(2,1)S(1)} %get-tuple-element.3), channel_id=1, source_target_pairs={{0,8},{2,10},{4,12},{6,14},{8,0},{10,2},{12,4},{14,6},{16,24},{18,... | collective-permute-start | bytes 393224 | tf_op jit(solution)/shard_map/ppermute | solution.py:32
  28.6 9.3 %collective-permute-start.19 = (bf16[512,128]{1,0:T(8,128)(2,1)S(1)}, bf16[512,128]{1,0:T(8,128)(2,1)S(1)}, u32[]{:S(2)}, u32[]{:S(2)}) collective-permute-start(bf16[512,128]{1,0:T(8,128)(2,1)S(1)} %get-tuple-element.4), channel_id=1, source_target_pairs={{0,24},{2,26},{4,28},{6,30},{8,16},{10,18},{12,20},{14,22},{16,8},... | collective-permute-start | bytes 393224 | tf_op jit(solution)/shard_map/ppermute | solution.py:32
  31.4 10.8 %collective-permute-start.18 = (bf16[512,128]{1,0:T(8,128)(2,1)S(1)}, bf16[512,128]{1,0:T(8,128)(2,1)S(1)}, u32[]{:S(2)}, u32[]{:S(2)}) collective-permute-start(bf16[512,128]{1,0:T(8,128)(2,1)S(1)} %get-tuple-element.5), channel_id=1, source_target_pairs={{0,16},{2,18},{4,20},{6,22},{8,24},{10,26},{12,28},{14,30},{16,0},... | collective-permute-start | bytes 393224 | tf_op jit(solution)/shard_map/ppermute | solution.py:32
  35.2 18.6 %copy-start.1 = (bf16[128,1024]{1,0:T(8,128)(2,1)S(1)}, bf16[128,1024]{1,0:T(8,128)(2,1)}, u32[]{:S(2)}) copy-start(bf16[128,1024]{1,0:T(8,128)(2,1)} %param.5) | copy-start | bytes 786436
  42.8 5.0 %collective-permute-start.15 = (bf16[128,512]{1,0:T(8,128)(2,1)S(1)}, bf16[128,512]{1,0:T(8,128)(2,1)S(1)}, u32[]{:S(2)}, u32[]{:S(2)}) collective-permute-start(bf16[128,512]{1,0:T(8,128)(2,1)S(1)} %pad_maximum_fusion.5), channel_id=1, source_target_pairs={{0,8},{2,10},{4,12},{6,14},{8,0},{10,2},{12,4},{14,6},{16,24},{18,... | collective-permute-start | bytes 393224 | tf_op jit(solution)/shard_map/ppermute | solution.py:32
  42.9 5.6 %collective-permute-start.9 = (bf16[128,512]{1,0:T(8,128)(2,1)S(1)}, bf16[128,512]{1,0:T(8,128)(2,1)S(1)}, u32[]{:S(2)}, u32[]{:S(2)}) collective-permute-start(bf16[128,512]{1,0:T(8,128)(2,1)S(1)} %get-tuple-element.8), channel_id=1, source_target_pairs={{0,2},{2,0},{4,6},{6,4},{8,10},{10,8},{12,14},{14,12},{16,18},{18,... | collective-permute-start | bytes 393224 | tf_op jit(solution)/shard_map/ppermute | solution.py:28
  43.8 6.3 %collective-permute-start.11 = (bf16[128,512]{1,0:T(8,128)(2,1)S(1)}, bf16[128,512]{1,0:T(8,128)(2,1)S(1)}, u32[]{:S(2)}, u32[]{:S(2)}) collective-permute-start(bf16[128,512]{1,0:T(8,128)(2,1)S(1)} %get-tuple-element.9), channel_id=1, source_target_pairs={{0,6},{2,4},{4,2},{6,0},{8,14},{10,12},{12,10},{14,8},{16,22},{18,... | collective-permute-start | bytes 393224 | tf_op jit(solution)/shard_map/ppermute | solution.py:28
  45.8 7.9 %collective-permute-start.20 = (bf16[128,512]{1,0:T(8,128)(2,1)S(1)}, bf16[128,512]{1,0:T(8,128)(2,1)S(1)}, u32[]{:S(2)}, u32[]{:S(2)}) collective-permute-start(bf16[128,512]{1,0:T(8,128)(2,1)S(1)} %convolution_convert_fusion.2), channel_id=1, source_target_pairs={{0,1},{1,0},{2,3},{3,2},{4,5},{5,4},{6,7},{7,6},{8,9},{9,8},{10,11... | collective-permute-start | bytes 393224 | tf_op jit(solution)/shard_map/ppermute | solution.py:52
  45.9 7.1 %collective-permute-start.10 = (bf16[128,512]{1,0:T(8,128)(2,1)S(1)}, bf16[128,512]{1,0:T(8,128)(2,1)S(1)}, u32[]{:S(2)}, u32[]{:S(2)}) collective-permute-start(bf16[128,512]{1,0:T(8,128)(2,1)S(1)} %get-tuple-element.10), channel_id=1, source_target_pairs={{0,4},{2,6},{4,0},{6,2},{8,12},{10,14},{12,8},{14,10},{16,20},{18,... | collective-permute-start | bytes 393224 | tf_op jit(solution)/shard_map/ppermute | solution.py:28
  50.2 5.2 %collective-permute-start.16 = (bf16[64,512]{1,0:T(8,128)(2,1)S(1)}, bf16[64,512]{1,0:T(8,128)(2,1)S(1)}, u32[]{:S(2)}, u32[]{:S(2)}) collective-permute-start(bf16[64,512]{1,0:T(8,128)(2,1)S(1)} %fusion.23), channel_id=1, source_target_pairs={{0,16},{2,18},{4,20},{6,22},{8,24},{10,26},{12,28},{14,30},{16,0},... | collective-permute-start | bytes 196616 | tf_op jit(solution)/shard_map/ppermute | solution.py:32

commit v31 on v29

--- a/solution.py
+++ b/solution.py
@@ -30,6 +30,15 @@
     def along_outer(value, turn):
         pairs = [(o * side + i, (o ^ turn) * side + i) for o in turns for i in turns]
         return lax.ppermute(value, "blk", pairs) if turn else value
+
+    def from_two(value, turn):
+        pairs = [
+            ((o * side + i) * 2 + r, ((o ^ (turn + r)) * side + i) * 2 + r)
+            for o in turns
+            for i in turns
+            for r in range(2)
+        ]
+        return lax.ppermute(value, ("blk", "rep"), pairs)
 
     def halved(parts, move, late):
         parts = dict(enumerate(parts))
@@ -66,6 +75,8 @@
     def columns_of(value, index):
         return lax.dynamic_slice_in_dim(value, index * cols_here, cols_here, 1)
 
+    pair_up = rep_count == 2 and side == 4
+    far = from_two(hidden_pre, 2) if pair_up else None
     hidden_part = jnp.maximum(columns_of(hidden_pre, rep_pos), 0)
 
     columns = adj_cols[0]
@@ -79,6 +90,10 @@
     arrived = [
         along_inner(ordered[t * per_core : (t + 1) * per_core], t) for t in turns
     ]
+    if pair_up:
+        other = columns_of(far, 1 - rep_pos)
+        blocks = cols_here // tile_size
+        arrived.append(jnp.stack([lanes(other, n) for n in range(blocks)]))
     everyone = lax.all_gather(jnp.concatenate(arrived, 0), "rep", axis=0)
     rows = []
     for t in turns:
@@ -95,7 +110,15 @@
         rows.append(jnp.concatenate(row, 1))
     block = jnp.concatenate(rows, 0)
 
-    hidden_stack = jnp.concatenate([along_outer(hidden_part, e) for e in turns], 0)
+    direct = turns[:2] if pair_up else turns
+    hidden_stack = [along_outer(hidden_part, e) for e in direct]
+    if pair_up:
+        mine = columns_of(far, rep_pos)
+        other = jnp.where(rep_pos == 0, everyone[1, section_span:], everyone[0, section_span:])
+        other = jnp.concatenate([other[n] for n in range(blocks)], 1)
+        second, third = jnp.where(rep_pos == 0, mine, other), jnp.where(rep_pos == 0, other, mine)
+        hidden_stack.extend([jnp.maximum(second, 0), jnp.maximum(third, 0)])
+    hidden_stack = jnp.concatenate(hidden_stack, 0)
     grad_part = columns_of(cotangent, rep_pos)
     grad_stack = jnp.concatenate([along_inner(grad_part, t) for t in turns], 0)
 

time: 52 us -> 61 us (1.17)
  starting transfers between devices: 28.7 us -> 33 us
  local copies, waits for them, and re-layouts: 1.24 us -> 4.6 us
  matrix products: 3.09 us -> 5.27 us
  other arithmetic: 3.85 us -> 2.88 us
    ppermute x12, starting transfers between devices: 14.4 us -> 19.2 us  [along_inner(): return lax.ppermute(value, 'blk', pairs) if turn else value]
    ppermute x8 -> x6, starting transfers between devices: 14.2 us -> 11.1 us  [along_outer(): return lax.ppermute(value, 'blk', pairs) if turn else value]
    ppermute x0 -> x1, starting transfers between devices: none -> 2.59 us  [from_two(): return lax.ppermute(value, ('blk', 'rep'), pairs)]
    dot_general x6, matrix products: 3.09 us -> 5.27 us  [dot(): lax.dot_general(lhs, rhs, (dims, ((), ())), preferred_element_type=jnp.fl...]
    dynamic_slice x1, local copies, waits for them, and re-layouts: 0.02 us -> 1.72 us  [columns_of(): return lax.dynamic_slice_in_dim(value, index * cols_here, cols_here, 1)]
    ppermute x8 -> x6, waiting for transfers between devices: 3.69 us -> 2.48 us  [along_outer(): return lax.ppermute(value, 'blk', pairs) if turn else value]
    max x1, other arithmetic: 1.08 us -> 0.03 us  [shards(): hidden_part = jnp.maximum(columns_of(hidden_pre, rep_pos), 0)]
    ppermute x12, waiting for transfers between devices: 6.11 us -> 7.07 us  [along_inner(): return lax.ppermute(value, 'blk', pairs) if turn else value]
  transfers between devices with their start and end apart: 21 -> 20, of which waited for: 8 -> 7; matrix products, arithmetic and copies ran while one was open for 12% -> 17% of each run, Pallas kernels for 0% -> 0%
where the time goes in v31:
time: 61 us; the launch traced here: 60.6 us
  starting transfers between devices  33 us (54%)
  waiting for transfers between devices  9.55 us (16%)
  matrix products  5.27 us (9%)
  local copies, waits for them, and re-layouts  4.6 us (8%)
  blocking collectives  4.36 us (7%)
  other arithmetic  2.88 us (5%)
  between operations  0.96 us (2%)
    ppermute x12, starting transfers between devices, along_inner(): return lax.ppermute(value, 'blk', pairs) if turn else value  19.2 us
    ppermute x6, starting transfers between devices, along_outer(): return lax.ppermute(value, 'blk', pairs) if turn else value  11.1 us
    ppermute x12, waiting for transfers between devices, along_inner(): return lax.ppermute(value, 'blk', pairs) if turn else value  7.07 us
    dot_general x6, matrix products, dot(): lax.dot_general(lhs, rhs, (dims, ((), ())), preferred_element_type=jnp.fl...  5.27 us
    ppermute x1, starting transfers between devices, from_two(): return lax.ppermute(value, ('blk', 'rep'), pairs)  2.59 us
    ppermute x6, waiting for transfers between devices, along_outer(): return lax.ppermute(value, 'blk', pairs) if turn else value  2.48 us
    all_gather x1, blocking collectives, shards(): everyone = lax.all_gather(jnp.concatenate(arrived, 0), 'rep', axis=0)  2.37 us
    all_gather x1, blocking collectives, shards(): lax.all_gather(mixed_cols.astype(bf16), 'rep', axis=0, tiled=True)  1.99 us
  transfers between devices with their start and end apart: 20, of which 7 were waited for; matrix products, arithmetic and copies ran while one was open for 17% of the time, Pallas kernels for 0%

profile of v31, /device:TPU:0, one launch (start us, length us, event | category | flops | bytes accessed | tf_op | source)
XLA Modules:
  0.0 60.6 jit_solution(6950243283929730676)
XLA Ops:
  0.7 1.7 %constant_dynamic-slice_fusion = bf16[128,512]{1,0:T(8,128)(2,1)} fusion(bf16[128,1024]{1,0:T(8,128)(2,1)} %param.9, s32[]{:T(128)S(6)} %select_n.239), kind=kLoop, calls=%fused_computation.95 | loop fusion | bytes 262148 | tf_op jit(solution)/shard_map/dynamic_slice | solution.py:76
  2.4 2.9 %collective-permute-start.11 = (bf16[128,512]{1,0:T(8,128)(2,1)}, bf16[128,512]{1,0:T(8,128)(2,1)}, u32[]{:S(2)}, u32[]{:S(2)}) collective-permute-start(bf16[128,512]{1,0:T(8,128)(2,1)} %constant_dynamic-slice_fusion), channel_id=1, source_target_pairs={{0,2},{2,0},{4,6},{6,4},{8,10},{10,8},{12,14},{14,12},{16,18},{18,... | collective-permute-start | bytes 393224 | tf_op jit(solution)/shard_map/ppermute | solution.py:28
  5.3 1.5 %collective-permute-start.12 = (bf16[128,512]{1,0:T(8,128)(2,1)}, bf16[128,512]{1,0:T(8,128)(2,1)}, u32[]{:S(2)}, u32[]{:S(2)}) collective-permute-start(bf16[128,512]{1,0:T(8,128)(2,1)} %constant_dynamic-slice_fusion), channel_id=1, source_target_pairs={{0,4},{2,6},{4,0},{6,2},{8,12},{10,14},{12,8},{14,10},{16,20},{18,... | collective-permute-start | bytes 393224 | tf_op jit(solution)/shard_map/ppermute | solution.py:28
  7.6 0.9 %slice_bitcast_fusion.13 = (bf16[128,128]{1,0:T(8,128)(2,1)S(1)}, bf16[128,128]{1,0:T(8,128)(2,1)S(1)}, bf16[128,128]{1,0:T(8,128)(2,1)S(1)}, bf16[128,128]{1,0:...) fusion(bf16[1,8,128,128]{3,2,1,0:T(8,128)(2,1)} %param.6), kind=kLoop, calls=%fused_computation.89 | loop fusion | bytes 524288 | tf_op jit(solution)/shard_map/jit(_where)/broadcast_in_dim | solution.py:89
  8.7 0.7 %fusion.39 = (bf16[2,128,128]{2,1,0:T(8,128)(2,1)}, bf16[2,128,128]{2,1,0:T(8,128)(2,1)}, bf16[2,128,128]{2,1,0:T(8,128)(2,1)}, bf16[12,128,128]{2,1,0:T(8,128)(2,1)S(1)}) fusion(bf16[8,128,128]{2,1,0:T(8,128)(2,1)S(1)} %select_select_fusion), kind=kLoop, calls=%fused_computation.117 | loop fusion | bytes 524288 | tf_op jit(solution)/shard_map/slice | solution.py:91
  9.4 2.0 %collective-permute-start.2 = (bf16[2,128,128]{2,1,0:T(8,128)(2,1)}, bf16[2,128,128]{2,1,0:T(8,128)(2,1)}, u32[]{:S(2)}, u32[]{:S(2)}) collective-permute-start(bf16[2,128,128]{2,1,0:T(8,128)(2,1)} %get-tuple-element.34), channel_id=1, source_target_pairs={{0,2},{2,0},{4,6},{6,4},{8,10},{10,8},{12,14},{14,12},{16,18},{18,... | collective-permute-start | bytes 196616 | tf_op jit(solution)/shard_map/ppermute | solution.py:28
  11.3 2.6 %collective-permute-start.1 = (bf16[128,1024]{1,0:T(8,128)(2,1)}, bf16[128,1024]{1,0:T(8,128)(2,1)S(1)}, u32[]{:S(2)}, u32[]{:S(2)}) collective-permute-start(bf16[128,1024]{1,0:T(8,128)(2,1)} %param.5), channel_id=1, source_target_pairs={{0,16},{1,25},{2,18},{3,27},{4,20},{5,29},{6,22},{7,31},{8,24},{9,... | collective-permute-start | bytes 786440 | tf_op jit(solution)/shard_map/ppermute | solution.py:41
  14.0 1.9 %collective-permute-start.3 = (bf16[2,128,128]{2,1,0:T(8,128)(2,1)}, bf16[2,128,128]{2,1,0:T(8,128)(2,1)S(1)}, u32[]{:S(2)}, u32[]{:S(2)}) collective-permute-start(bf16[2,128,128]{2,1,0:T(8,128)(2,1)} %get-tuple-element.33), channel_id=1, source_target_pairs={{0,4},{2,6},{4,0},{6,2},{8,12},{10,14},{12,8},{14,10},{16,20},{18,... | collective-permute-start | bytes 196616 | tf_op jit(solution)/shard_map/ppermute | solution.py:28
  15.9 0.9 %constant_dynamic-update-slice_fusion.2 = bf16[12,128,128]{2,1,0:T(8,128)(2,1)S(1)} fusion(bf16[12,128,128]{2,1,0:T(8,128)(2,1)S(1)} %get-tuple-element.35, bf16[2,128,128]{2,1,0:T(8,128)(2,1)} %collective-permute-done.2), kind=kLoop, calls=%fused_computation.92 | loop fusion | bytes 131072
  16.8 1.8 %collective-permute-done.3 = bf16[2,128,128]{2,1,0:T(8,128)(2,1)S(1)} collective-permute-done((bf16[2,128,128]{2,1,0:T(8,128)(2,1)}, bf16[2,128,128]{2,1,0:T(8,128)(2,1)S(1)}, u32[]{:S(2)}, u32[]{:S(2)}) %collective-permute-start.3) | collective-permute-done | bytes 65568 | tf_op jit(solution)/shard_map/ppermute | solution.py:28
  18.6 2.8 %collective-permute-start.4 = (bf16[2,128,128]{2,1,0:T(8,128)(2,1)}, bf16[2,128,128]{2,1,0:T(8,128)(2,1)S(1)}, u32[]{:S(2)}, u32[]{:S(2)}) collective-permute-start(bf16[2,128,128]{2,1,0:T(8,128)(2,1)} %get-tuple-element.32), channel_id=1, source_target_pairs={{0,6},{2,4},{4,2},{6,0},{8,14},{10,12},{12,10},{14,8},{16,22},{18,... | collective-permute-start | bytes 196616 | tf_op jit(solution)/shard_map/ppermute | solution.py:28
  21.4 2.6 %collective-permute-done.4 = bf16[2,128,128]{2,1,0:T(8,128)(2,1)S(1)} collective-permute-done((bf16[2,128,128]{2,1,0:T(8,128)(2,1)}, bf16[2,128,128]{2,1,0:T(8,128)(2,1)S(1)}, u32[]{:S(2)}, u32[]{:S(2)}) %collective-permute-start.4) | collective-permute-done | bytes 65568 | tf_op jit(solution)/shard_map/ppermute | solution.py:28
  24.0 1.9 %collective-permute-start = (bf16[128,512]{1,0:T(8,128)(2,1)S(1)}, bf16[128,512]{1,0:T(8,128)(2,1)S(1)}, u32[]{:S(2)}, u32[]{:S(2)}) collective-permute-start(bf16[128,512]{1,0:T(8,128)(2,1)S(1)} %dynamic-slice_maximum_fusion), channel_id=1, source_target_pairs={{0,8},{2,10},{4,12},{6,14},{8,0},{10,2},{12,4},{14,6},{16,24},{18,... | collective-permute-start | bytes 393224 | tf_op jit(solution)/shard_map/ppermute | solution.py:32
  26.0 2.4 %all-gather = bf16[24,128,128]{2,1,0:T(8,128)(2,1)S(1)} all-gather(bf16[12,128,128]{2,1,0:T(8,128)(2,1)S(1)} %fusion.25), channel_id=2, replica_groups=mesh['blk'=16,'rep'=2] {'rep'}, dimensions={0}, use_global_device_ids=true | all-gather | bytes 1179648 | tf_op jit(solution)/shard_map/all_gather | solution.py:97
  29.5 1.9 %collective-permute-start.5 = (bf16[128,512]{1,0:T(8,128)(2,1)S(1)}, bf16[128,512]{1,0:T(8,128)(2,1)S(1)}, u32[]{:S(2)}, u32[]{:S(2)}) collective-permute-start(bf16[128,512]{1,0:T(8,128)(2,1)S(1)} %pad_maximum_fusion.2), channel_id=1, source_target_pairs={{0,2},{2,0},{4,6},{6,4},{8,10},{10,8},{12,14},{14,12},{16,18},{18,... | collective-permute-start | bytes 393224 | tf_op jit(solution)/shard_map/ppermute | solution.py:28
  31.4 1.6 %collective-permute-start.6 = (bf16[128,512]{1,0:T(8,128)(2,1)S(1)}, bf16[128,512]{1,0:T(8,128)(2,1)S(1)}, u32[]{:S(2)}, u32[]{:S(2)}) collective-permute-start(bf16[128,512]{1,0:T(8,128)(2,1)S(1)} %pad_maximum_fusion.3), channel_id=1, source_target_pairs={{0,4},{2,6},{4,0},{6,2},{8,12},{10,14},{12,8},{14,10},{16,20},{18,... | collective-permute-start | bytes 393224 | tf_op jit(solution)/shard_map/ppermute | solution.py:28
  33.3 1.6 %fusion = bf16[512,512]{1,0:T(8,128)(2,1)S(1)} fusion(bf16[512,512]{1,0:T(8,128)(2,1)S(1)} %maximum_maximum_fusion, bf16[512,512]{1,0:T(8,128)(2,1)S(1)} %convolution_convert_fusion, bf16[128,512]{1,0:T(8,128)(2,1)} %collective-permute-done.13, bf16[128,512]{1,0:T(8,128)(2,1)} %collective-permute-done.12, bf16[128,512]{1,0:T(8,128)(2,1)} %collective-permute-done.11, ...), kind=kOutput, calls=%fused_computation.3 | convolution fusion | flops 271581184 | bytes 2097152 | tf_op jit(solution)/shard_map/dot_general | solution.py:64
  35.0 2.0 %collective-permute-start.16 = (bf16[512,128]{1,0:T(8,128)(2,1)S(1)}, bf16[512,128]{1,0:T(8,128)(2,1)S(1)}, u32[]{:S(2)}, u32[]{:S(2)}) collective-permute-start(bf16[512,128]{1,0:T(8,128)(2,1)S(1)} %get-tuple-element.18), channel_id=1, source_target_pairs={{0,8},{2,10},{4,12},{6,14},{8,0},{10,2},{12,4},{14,6},{16,24},{18,... | collective-permute-start | bytes 393224 | tf_op jit(solution)/shard_map/ppermute | solution.py:32
  36.9 2.6 %collective-permute-start.17 = (bf16[512,128]{1,0:T(8,128)(2,1)S(1)}, bf16[512,128]{1,0:T(8,128)(2,1)S(1)}, u32[]{:S(2)}, u32[]{:S(2)}) collective-permute-start(bf16[512,128]{1,0:T(8,128)(2,1)S(1)} %get-tuple-element.20), channel_id=1, source_target_pairs={{0,16},{2,18},{4,20},{6,22},{8,24},{10,26},{12,28},{14,30},{16,0},... | collective-permute-start | bytes 393224 | tf_op jit(solution)/shard_map/ppermute | solution.py:32
  39.9 2.0 %all_gather.11 = bf16[256,512]{1,0:T(8,128)(2,1)S(1)} all-gather(bf16[128,512]{1,0:T(8,128)(2,1)S(1)} %fusion.16), channel_id=1, replica_groups=mesh['blk'=16,'rep'=2] {'rep'}, dimensions={0}, use_global_device_ids=true | all-gather | bytes 393216 | tf_op jit(solution)/shard_map/all_gather | solution.py:138
  42.2 1.4 %convolution_add_fusion.1 = f32[256,512]{1,0:T(8,128)S(1)} fusion(bf16[256,512]{1,0:T(8,128)(2,1)S(1)} %all_gather.11, bf16[512,512]{1,0:T(8,128)(2,1)S(1)} %convolution_convert_fusion.1, bf16[128,512]{1,0:T(8,128)(2,1)} %collective-permute-done.13, bf16[128,512]{1,0:T(8,128)(2,1)} %collective-permute-done.12, bf16[128,512]{1,0:T(8,128)(2,1)} %collective-permute-done.11, ...), kind=kOutput, calls=%fused_computation.4 | convolution fusion | flops 136708096 | bytes 1572864 | tf_op jit(solution)/shard_map/dot_general | solution.py:64
  43.7 0.9 %collective-permute-start.14 = (bf16[128,512]{1,0:T(8,128)(2,1)S(1)}, bf16[128,512]{1,0:T(8,128)(2,1)S(1)}, u32[]{:S(2)}, u32[]{:S(2)}) collective-permute-start(bf16[128,512]{1,0:T(8,128)(2,1)S(1)} %pad_maximum_fusion.5), channel_id=1, source_target_pairs={{0,8},{2,10},{4,12},{6,14},{8,0},{10,2},{12,4},{14,6},{16,24},{18,... | collective-permute-start | bytes 393224 | tf_op jit(solution)/shard_map/ppermute | solution.py:32
  44.6 2.3 %collective-permute-start.10 = (bf16[128,512]{1,0:T(8,128)(2,1)S(1)}, bf16[128,512]{1,0:T(8,128)(2,1)S(1)}, u32[]{:S(2)}, u32[]{:S(2)}) collective-permute-start(bf16[128,512]{1,0:T(8,128)(2,1)S(1)} %get-tuple-element.24), channel_id=1, source_target_pairs={{0,6},{2,4},{4,2},{6,0},{8,14},{10,12},{12,10},{14,8},{16,22},{18,... | collective-permute-start | bytes 393224 | tf_op jit(solution)/shard_map/ppermute | solution.py:28
  47.5 1.1 %collective-permute-done.17 = bf16[512,128]{1,0:T(8,128)(2,1)S(1)} collective-permute-done((bf16[512,128]{1,0:T(8,128)(2,1)S(1)}, bf16[512,128]{1,0:T(8,128)(2,1)S(1)}, u32[]{:S(2)}, u32[]{:S(2)}) %collective-permute-start.17) | collective-permute-done | bytes 131104 | tf_op jit(solution)/shard_map/ppermute | solution.py:32
  49.2 1.6 %collective-permute-start.9 = (bf16[128,512]{1,0:T(8,128)(2,1)S(1)}, bf16[128,512]{1,0:T(8,128)(2,1)S(1)}, u32[]{:S(2)}, u32[]{:S(2)}) collective-permute-start(bf16[128,512]{1,0:T(8,128)(2,1)S(1)} %get-tuple-element.25), channel_id=1, source_target_pairs={{0,4},{2,6},{4,0},{6,2},{8,12},{10,14},{12,8},{14,10},{16,20},{18,... | collective-permute-start | bytes 393224 | tf_op jit(solution)/shard_map/ppermute | solution.py:28
  50.8 1.1 %collective-permute-done.10 = bf16[128,512]{1,0:T(8,128)(2,1)S(1)} collective-permute-done((bf16[128,512]{1,0:T(8,128)(2,1)S(1)}, bf16[128,512]{1,0:T(8,128)(2,1)S(1)}, u32[]{:S(2)}, u32[]{:S(2)}) %collective-permute-start.10) | collective-permute-done | bytes 131104 | tf_op jit(solution)/shard_map/ppermute | solution.py:28
  51.8 1.6 %collective-permute-done.8 = bf16[128,512]{1,0:T(8,128)(2,1)S(1)} collective-permute-done((bf16[128,512]{1,0:T(8,128)(2,1)S(1)}, bf16[128,512]{1,0:T(8,128)(2,1)S(1)}, u32[]{:S(2)}, u32[]{:S(2)}) %collective-permute-start.8) | collective-permute-done | bytes 131104 | tf_op jit(solution)/shard_map/ppermute | solution.py:28
  53.5 3.6 %collective-permute-start.15 = (bf16[64,512]{1,0:T(8,128)(2,1)S(1)}, bf16[64,512]{1,0:T(8,128)(2,1)S(1)}, u32[]{:S(2)}, u32[]{:S(2)}) collective-permute-start(bf16[64,512]{1,0:T(8,128)(2,1)S(1)} %fusion.23), channel_id=1, source_target_pairs={{0,16},{2,18},{4,20},{6,22},{8,24},{10,26},{12,28},{14,30},{16,0},... | collective-permute-start | bytes 196616 | tf_op jit(solution)/shard_map/ppermute | solution.py:32
  57.0 0.7 %add_convert_fusion = bf16[128,512]{1,0:T(8,128)(2,1)} fusion(bf16[128,512]{1,0:T(8,128)(2,1)S(1)} %collective-permute-done.10, bf16[128,512]{1,0:T(8,128)(2,1)S(1)} %collective-permute-done.9, bf16[128,512]{1,0:T(8,128)(2,1)S(1)} %collective-permute-done.8, bf16[512,512]{1,0:T(8,128)(2,1)S(1)} %convolution_convert_fusion.1), kind=kLoop, calls=%fused_computation.27 | loop fusion | flops 524288 | bytes 655360 | tf_op jit(solution)/shard_map/convert_element_type | solution.py:154
  57.7 1.1 %select_convert_fusion = bf16[128,512]{1,0:T(8,128)(2,1)} fusion(bf16[128,512]{1,0:T(8,128)(2,1)S(1)} %collective-permute-done.19, bf16[128,1024]{1,0:T(8,128)(2,1)S(1)} %copy-done.1, s32[]{:T(128)S(6)} %select_n.239, bf16[512,128]{1,0:T(8,128)(2,1)S(1)} %fusion.13, bf16[2,512,1024]{2,1,0:T(8,128)(2,1)S(1)} %bitcast.138, s32[]{:T(128)S(6)} %select_n.310, ...), kind=kOutput, calls=%fused_computation.26 | convolution fusion | flops 67567616 | bytes 1048588 | tf_op jit(solution)/shard_map/dot_general | solution.py:64
  58.8 1.1 %collective-permute-done.15 = bf16[64,512]{1,0:T(8,128)(2,1)S(1)} collective-permute-done((bf16[64,512]{1,0:T(8,128)(2,1)S(1)}, bf16[64,512]{1,0:T(8,128)(2,1)S(1)}, u32[]{:S(2)}, u32[]{:S(2)}) %collective-permute-start.15) | collective-permute-done | bytes 65568 | tf_op jit(solution)/shard_map/ppermute | solution.py:32
  60.0 0.7 %fusion.19 = f32[64,512]{1,0:T(8,128)} fusion(bf16[64,512]{1,0:T(8,128)(2,1)S(1)} %collective-permute-done.15, f32[4,64,512]{2,1,0:T(8,128)S(1)} %bitcast.147, s32[]{:T(128)S(6)} %select_n.302, bf16[128,512]{1,0:T(8,128)(2,1)S(1)} %collective-permute-done.14), kind=kLoop, calls=%fused_computation.40 | loop fusion | flops 131072 | bytes 393220 | tf_op jit(solution)/shard_map/add | solution.py:54
  (61 shorter events, 4.6 us)
Async XLA Ops:
  0.6 13.3 %copy-start = (bf16[1024,1024]{1,0:T(8,128)(2,1)S(1)}, bf16[1024,1024]{1,0:T(8,128)(2,1)}, u32[]{:S(2)}) copy-start(bf16[1024,1024]{1,0:T(8,128)(2,1)} %param.8) | copy-start | bytes 6291460
  0.6 13.3 %copy-start.1 = (bf16[128,1024]{1,0:T(8,128)(2,1)S(1)}, bf16[128,1024]{1,0:T(8,128)(2,1)}, u32[]{:S(2)}) copy-start(bf16[128,1024]{1,0:T(8,128)(2,1)} %param.5) | copy-start | bytes 786436
  2.4 30.7 %collective-permute-start.11 = (bf16[128,512]{1,0:T(8,128)(2,1)}, bf16[128,512]{1,0:T(8,128)(2,1)}, u32[]{:S(2)}, u32[]{:S(2)}) collective-permute-start(bf16[128,512]{1,0:T(8,128)(2,1)} %constant_dynamic-slice_fusion), channel_id=1, source_target_pairs={{0,2},{2,0},{4,6},{6,4},{8,10},{10,8},{12,14},{14,12},{16,18},{18,... | collective-permute-start | bytes 393224 | tf_op jit(solution)/shard_map/ppermute | solution.py:28
  5.3 28.0 %collective-permute-start.12 = (bf16[128,512]{1,0:T(8,128)(2,1)}, bf16[128,512]{1,0:T(8,128)(2,1)}, u32[]{:S(2)}, u32[]{:S(2)}) collective-permute-start(bf16[128,512]{1,0:T(8,128)(2,1)} %constant_dynamic-slice_fusion), channel_id=1, source_target_pairs={{0,4},{2,6},{4,0},{6,2},{8,12},{10,14},{12,8},{14,10},{16,20},{18,... | collective-permute-start | bytes 393224 | tf_op jit(solution)/shard_map/ppermute | solution.py:28
  6.8 26.5 %collective-permute-start.13 = (bf16[128,512]{1,0:T(8,128)(2,1)}, bf16[128,512]{1,0:T(8,128)(2,1)}, u32[]{:S(2)}, u32[]{:S(2)}) collective-permute-start(bf16[128,512]{1,0:T(8,128)(2,1)} %constant_dynamic-slice_fusion), channel_id=1, source_target_pairs={{0,6},{2,4},{4,2},{6,0},{8,14},{10,12},{12,10},{14,8},{16,22},{18,... | collective-permute-start | bytes 393224 | tf_op jit(solution)/shard_map/ppermute | solution.py:28
  9.4 4.7 %collective-permute-start.2 = (bf16[2,128,128]{2,1,0:T(8,128)(2,1)}, bf16[2,128,128]{2,1,0:T(8,128)(2,1)}, u32[]{:S(2)}, u32[]{:S(2)}) collective-permute-start(bf16[2,128,128]{2,1,0:T(8,128)(2,1)} %get-tuple-element.34), channel_id=1, source_target_pairs={{0,2},{2,0},{4,6},{6,4},{8,10},{10,8},{12,14},{14,12},{16,18},{18,... | collective-permute-start | bytes 196616 | tf_op jit(solution)/shard_map/ppermute | solution.py:28
  11.3 14.5 %collective-permute-start.1 = (bf16[128,1024]{1,0:T(8,128)(2,1)}, bf16[128,1024]{1,0:T(8,128)(2,1)S(1)}, u32[]{:S(2)}, u32[]{:S(2)}) collective-permute-start(bf16[128,1024]{1,0:T(8,128)(2,1)} %param.5), channel_id=1, source_target_pairs={{0,16},{1,25},{2,18},{3,27},{4,20},{5,29},{6,22},{7,31},{8,24},{9,... | collective-permute-start | bytes 786440 | tf_op jit(solution)/shard_map/ppermute | solution.py:41
  14.0 4.5 %collective-permute-start.3 = (bf16[2,128,128]{2,1,0:T(8,128)(2,1)}, bf16[2,128,128]{2,1,0:T(8,128)(2,1)S(1)}, u32[]{:S(2)}, u32[]{:S(2)}) collective-permute-start(bf16[2,128,128]{2,1,0:T(8,128)(2,1)} %get-tuple-element.33), channel_id=1, source_target_pairs={{0,4},{2,6},{4,0},{6,2},{8,12},{10,14},{12,8},{14,10},{16,20},{18,... | collective-permute-start | bytes 196616 | tf_op jit(solution)/shard_map/ppermute | solution.py:28
  18.6 5.4 %collective-permute-start.4 = (bf16[2,128,128]{2,1,0:T(8,128)(2,1)}, bf16[2,128,128]{2,1,0:T(8,128)(2,1)S(1)}, u32[]{:S(2)}, u32[]{:S(2)}) collective-permute-start(bf16[2,128,128]{2,1,0:T(8,128)(2,1)} %get-tuple-element.32), channel_id=1, source_target_pairs={{0,6},{2,4},{4,2},{6,0},{8,14},{10,12},{12,10},{14,8},{16,22},{18,... | collective-permute-start | bytes 196616 | tf_op jit(solution)/shard_map/ppermute | solution.py:28
  24.0 5.0 %collective-permute-start = (bf16[128,512]{1,0:T(8,128)(2,1)S(1)}, bf16[128,512]{1,0:T(8,128)(2,1)S(1)}, u32[]{:S(2)}, u32[]{:S(2)}) collective-permute-start(bf16[128,512]{1,0:T(8,128)(2,1)S(1)} %dynamic-slice_maximum_fusion), channel_id=1, source_target_pairs={{0,8},{2,10},{4,12},{6,14},{8,0},{10,2},{12,4},{14,6},{16,24},{18,... | collective-permute-start | bytes 393224 | tf_op jit(solution)/shard_map/ppermute | solution.py:32
  29.5 10.0 %collective-permute-start.5 = (bf16[128,512]{1,0:T(8,128)(2,1)S(1)}, bf16[128,512]{1,0:T(8,128)(2,1)S(1)}, u32[]{:S(2)}, u32[]{:S(2)}) collective-permute-start(bf16[128,512]{1,0:T(8,128)(2,1)S(1)} %pad_maximum_fusion.2), channel_id=1, source_target_pairs={{0,2},{2,0},{4,6},{6,4},{8,10},{10,8},{12,14},{14,12},{16,18},{18,... | collective-permute-start | bytes 393224 | tf_op jit(solution)/shard_map/ppermute | solution.py:28
  31.4 8.3 %collective-permute-start.6 = (bf16[128,512]{1,0:T(8,128)(2,1)S(1)}, bf16[128,512]{1,0:T(8,128)(2,1)S(1)}, u32[]{:S(2)}, u32[]{:S(2)}) collective-permute-start(bf16[128,512]{1,0:T(8,128)(2,1)S(1)} %pad_maximum_fusion.3), channel_id=1, source_target_pairs={{0,4},{2,6},{4,0},{6,2},{8,12},{10,14},{12,8},{14,10},{16,20},{18,... | collective-permute-start | bytes 393224 | tf_op jit(solution)/shard_map/ppermute | solution.py:28
  33.1 6.7 %collective-permute-start.7 = (bf16[128,512]{1,0:T(8,128)(2,1)S(1)}, bf16[128,512]{1,0:T(8,128)(2,1)S(1)}, u32[]{:S(2)}, u32[]{:S(2)}) collective-permute-start(bf16[128,512]{1,0:T(8,128)(2,1)S(1)} %pad_maximum_fusion.4), channel_id=1, source_target_pairs={{0,6},{2,4},{4,2},{6,0},{8,14},{10,12},{12,10},{14,8},{16,22},{18,... | collective-permute-start | bytes 393224 | tf_op jit(solution)/shard_map/ppermute | solution.py:28
  35.0 11.9 %collective-permute-start.16 = (bf16[512,128]{1,0:T(8,128)(2,1)S(1)}, bf16[512,128]{1,0:T(8,128)(2,1)S(1)}, u32[]{:S(2)}, u32[]{:S(2)}) collective-permute-start(bf16[512,128]{1,0:T(8,128)(2,1)S(1)} %get-tuple-element.18), channel_id=1, source_target_pairs={{0,8},{2,10},{4,12},{6,14},{8,0},{10,2},{12,4},{14,6},{16,24},{18,... | collective-permute-start | bytes 393224 | tf_op jit(solution)/shard_map/ppermute | solution.py:32
  36.9 11.6 %collective-permute-start.17 = (bf16[512,128]{1,0:T(8,128)(2,1)S(1)}, bf16[512,128]{1,0:T(8,128)(2,1)S(1)}, u32[]{:S(2)}, u32[]{:S(2)}) collective-permute-start(bf16[512,128]{1,0:T(8,128)(2,1)S(1)} %get-tuple-element.20), channel_id=1, source_target_pairs={{0,16},{2,18},{4,20},{6,22},{8,24},{10,26},{12,28},{14,30},{16,0},... | collective-permute-start | bytes 393224 | tf_op jit(solution)/shard_map/ppermute | solution.py:32
  39.5 9.1 %collective-permute-start.18 = (bf16[512,128]{1,0:T(8,128)(2,1)S(1)}, bf16[512,128]{1,0:T(8,128)(2,1)S(1)}, u32[]{:S(2)}, u32[]{:S(2)}) collective-permute-start(bf16[512,128]{1,0:T(8,128)(2,1)S(1)} %get-tuple-element.19), channel_id=1, source_target_pairs={{0,24},{2,26},{4,28},{6,30},{8,16},{10,18},{12,20},{14,22},{16,8},... | collective-permute-start | bytes 393224 | tf_op jit(solution)/shard_map/ppermute | solution.py:32
  43.7 7.1 %collective-permute-start.14 = (bf16[128,512]{1,0:T(8,128)(2,1)S(1)}, bf16[128,512]{1,0:T(8,128)(2,1)S(1)}, u32[]{:S(2)}, u32[]{:S(2)}) collective-permute-start(bf16[128,512]{1,0:T(8,128)(2,1)S(1)} %pad_maximum_fusion.5), channel_id=1, source_target_pairs={{0,8},{2,10},{4,12},{6,14},{8,0},{10,2},{12,4},{14,6},{16,24},{18,... | collective-permute-start | bytes 393224 | tf_op jit(solution)/shard_map/ppermute | solution.py:32
  44.6 7.3 %collective-permute-start.10 = (bf16[128,512]{1,0:T(8,128)(2,1)S(1)}, bf16[128,512]{1,0:T(8,128)(2,1)S(1)}, u32[]{:S(2)}, u32[]{:S(2)}) collective-permute-start(bf16[128,512]{1,0:T(8,128)(2,1)S(1)} %get-tuple-element.24), channel_id=1, source_target_pairs={{0,6},{2,4},{4,2},{6,0},{8,14},{10,12},{12,10},{14,8},{16,22},{18,... | collective-permute-start | bytes 393224 | tf_op jit(solution)/shard_map/ppermute | solution.py:28
  46.9 6.6 %collective-permute-start.8 = (bf16[128,512]{1,0:T(8,128)(2,1)S(1)}, bf16[128,512]{1,0:T(8,128)(2,1)S(1)}, u32[]{:S(2)}, u32[]{:S(2)}) collective-permute-start(bf16[128,512]{1,0:T(8,128)(2,1)S(1)} %get-tuple-element.23), channel_id=1, source_target_pairs={{0,2},{2,0},{4,6},{6,4},{8,10},{10,8},{12,14},{14,12},{16,18},{18,... | collective-permute-start | bytes 393224 | tf_op jit(solution)/shard_map/ppermute | solution.py:28
  49.1 8.6 %collective-permute-start.19 = (bf16[128,512]{1,0:T(8,128)(2,1)S(1)}, bf16[128,512]{1,0:T(8,128)(2,1)S(1)}, u32[]{:S(2)}, u32[]{:S(2)}) collective-permute-start(bf16[128,512]{1,0:T(8,128)(2,1)S(1)} %convolution_convert_fusion.2), channel_id=1, source_target_pairs={{0,1},{1,0},{2,3},{3,2},{4,5},{5,4},{6,7},{7,6},{8,9},{9,8},{10,11... | collective-permute-start | bytes 393224 | tf_op jit(solution)/shard_map/ppermute | solution.py:61
  49.2 7.8 %collective-permute-start.9 = (bf16[128,512]{1,0:T(8,128)(2,1)S(1)}, bf16[128,512]{1,0:T(8,128)(2,1)S(1)}, u32[]{:S(2)}, u32[]{:S(2)}) collective-permute-start(bf16[128,512]{1,0:T(8,128)(2,1)S(1)} %get-tuple-element.25), channel_id=1, source_target_pairs={{0,4},{2,6},{4,0},{6,2},{8,12},{10,14},{12,8},{14,10},{16,20},{18,... | collective-permute-start | bytes 393224 | tf_op jit(solution)/shard_map/ppermute | solution.py:28
  53.5 6.5 %collective-permute-start.15 = (bf16[64,512]{1,0:T(8,128)(2,1)S(1)}, bf16[64,512]{1,0:T(8,128)(2,1)S(1)}, u32[]{:S(2)}, u32[]{:S(2)}) collective-permute-start(bf16[64,512]{1,0:T(8,128)(2,1)S(1)} %fusion.23), channel_id=1, source_target_pairs={{0,16},{2,18},{4,20},{6,22},{8,24},{10,26},{12,28},{14,30},{16,0},... | collective-permute-start | bytes 196616 | tf_op jit(solution)/shard_map/ppermute | solution.py:32

commit v32 on v29

--- a/solution.py
+++ b/solution.py
@@ -110,7 +110,7 @@
         mixed_cols = mixed_cols + along_inner(chosen, t).astype(jnp.float32)
 
     back = after(dot(grad_stack, block, ((0,), (0,))), mixed).astype(bf16)
-    back = sum(along_outer(lanes(back, e), e).astype(jnp.float32) for e in turns)
+    back = halved([lanes(back, e) for e in turns], along_outer, [])
 
     mixed_cols = lax.all_gather(mixed_cols.astype(bf16), "rep", axis=0, tiled=True)
     w_share = w_out.reshape(side, side, rows_here, feature_width)

time: 52 us -> 53.5 us (1.029)
  waiting for transfers between devices: 9.8 us -> 15 us
  starting transfers between devices: 28.7 us -> 24 us
  matrix products: 3.09 us -> 4.06 us
    ppermute x12, waiting for transfers between devices: 6.11 us -> 12.5 us  [along_inner(): return lax.ppermute(value, 'blk', pairs) if turn else value]
    ppermute x8 -> x7, starting transfers between devices: 14.2 us -> 10.6 us  [along_outer(): return lax.ppermute(value, 'blk', pairs) if turn else value]
    ppermute x8 -> x7, waiting for transfers between devices: 3.69 us -> 2.09 us  [along_outer(): return lax.ppermute(value, 'blk', pairs) if turn else value]
    ppermute x12, starting transfers between devices: 14.4 us -> 13.3 us  [along_inner(): return lax.ppermute(value, 'blk', pairs) if turn else value]
    dot_general x6, matrix products: 3.09 us -> 4.06 us  [dot(): lax.dot_general(lhs, rhs, (dims, ((), ())), preferred_element_type=jnp.fl...]
  transfers between devices with their start and end apart: 21 -> 20, of which waited for: 8 -> 11; matrix products, arithmetic and copies ran while one was open for 12% -> 13% of each run, Pallas kernels for 0% -> 0%
where the time goes in v32:
time: 53.5 us; the launch traced here: 53.2 us
  starting transfers between devices  24 us (45%)
  waiting for transfers between devices  15 us (28%)
  blocking collectives  4.18 us (8%)
  matrix products  4.06 us (8%)
  other arithmetic  3.9 us (7%)
  local copies, waits for them, and re-layouts  1.19 us (2%)
  between operations  0.95 us (2%)
    ppermute x12, starting transfers between devices, along_inner(): return lax.ppermute(value, 'blk', pairs) if turn else value  13.3 us
    ppermute x12, waiting for transfers between devices, along_inner(): return lax.ppermute(value, 'blk', pairs) if turn else value  12.5 us
    ppermute x7, starting transfers between devices, along_outer(): return lax.ppermute(value, 'blk', pairs) if turn else value  10.6 us
    dot_general x6, matrix products, dot(): lax.dot_general(lhs, rhs, (dims, ((), ())), preferred_element_type=jnp.fl...  4.06 us
    all_gather x1, blocking collectives, shards(): everyone = lax.all_gather(jnp.concatenate(arrived, 0), 'rep', axis=0)  2.18 us
    ppermute x7, waiting for transfers between devices, along_outer(): return lax.ppermute(value, 'blk', pairs) if turn else value  2.09 us
    all_gather x1, blocking collectives, shards(): lax.all_gather(mixed_cols.astype(bf16), 'rep', axis=0, tiled=True)  1.99 us
    max x1, other arithmetic, shards(): hidden_part = jnp.maximum(columns_of(hidden_pre, rep_pos), 0)  1.08 us
  transfers between devices with their start and end apart: 20, of which 11 were waited for; matrix products, arithmetic and copies ran while one was open for 13% of the time, Pallas kernels for 0%

profile of v32, /device:TPU:0, one launch (start us, length us, event | category | flops | bytes accessed | tf_op | source)
XLA Modules:
  0.0 53.2 jit_solution(12349277941195425893)
XLA Ops:
  0.7 1.1 %dynamic-slice_maximum_fusion = bf16[128,512]{1,0:T(8,128)(2,1)S(1)} fusion(bf16[128,1024]{1,0:T(8,128)(2,1)} %param.5, s32[]{:T(128)S(6)} %select_n.214), kind=kLoop, calls=%fused_computation.44 | loop fusion | flops 262144 | bytes 262148 | tf_op jit(solution)/shard_map/max | solution.py:69
  1.7 3.1 %collective-permute-start = (bf16[128,512]{1,0:T(8,128)(2,1)S(1)}, bf16[128,512]{1,0:T(8,128)(2,1)}, u32[]{:S(2)}, u32[]{:S(2)}) collective-permute-start(bf16[128,512]{1,0:T(8,128)(2,1)S(1)} %dynamic-slice_maximum_fusion), channel_id=1, source_target_pairs={{0,8},{2,10},{4,12},{6,14},{8,0},{10,2},{12,4},{14,6},{16,24},{18,... | collective-permute-start | bytes 393224 | tf_op jit(solution)/shard_map/ppermute | solution.py:32
  4.8 2.6 %collective-permute-start.1 = (bf16[128,512]{1,0:T(8,128)(2,1)S(1)}, bf16[128,512]{1,0:T(8,128)(2,1)}, u32[]{:S(2)}, u32[]{:S(2)}) collective-permute-start(bf16[128,512]{1,0:T(8,128)(2,1)S(1)} %dynamic-slice_maximum_fusion), channel_id=1, source_target_pairs={{0,16},{2,18},{4,20},{6,22},{8,24},{10,26},{12,28},{14,30},{16,0},... | collective-permute-start | bytes 393224 | tf_op jit(solution)/shard_map/ppermute | solution.py:32
  7.4 0.7 %add_bitcast_fusion = s32[8]{0:T(128)S(1)} fusion(s32[1,8]{1,0:T(1,128)} %param.7, s32[]{:T(128)S(6)} %shift_right_arithmetic.54, s32[]{:T(128)S(6)} %and.60), kind=kLoop, calls=%fused_computation.94 | loop fusion | flops 56 | bytes 72 | tf_op jit(solution)/shard_map/eq | solution.py:75
  8.2 0.9 %slice_bitcast_fusion.9 = (bf16[128,128]{1,0:T(8,128)(2,1)S(1)}, bf16[128,128]{1,0:T(8,128)(2,1)S(1)}, bf16[128,128]{1,0:T(8,128)(2,1)S(1)}, bf16[128,128]{1,0:T...) fusion(bf16[1,8,128,128]{3,2,1,0:T(8,128)(2,1)} %param.6), kind=kLoop, calls=%fused_computation.75 | loop fusion | bytes 524288 | tf_op jit(solution)/shard_map/jit(_where)/broadcast_in_dim | solution.py:78
  9.3 1.6 %collective-permute-start.3 = (bf16[2,128,128]{2,1,0:T(8,128)(2,1)S(1)}, bf16[2,128,128]{2,1,0:T(8,128)(2,1)S(1)}, u32[]{:S(2)}, u32[]{:S(2)}) collective-permute-start(bf16[2,128,128]{2,1,0:T(8,128)(2,1)S(1)} %get-tuple-element.32), channel_id=1, source_target_pairs={{0,2},{2,0},{4,6},{6,4},{8,10},{10,8},{12,14},{14,12},{16,18},{18,... | collective-permute-start | bytes 196616 | tf_op jit(solution)/shard_map/ppermute | solution.py:28
  10.9 1.5 %collective-permute-start.4 = (bf16[2,128,128]{2,1,0:T(8,128)(2,1)S(1)}, bf16[2,128,128]{2,1,0:T(8,128)(2,1)S(1)}, u32[]{:S(2)}, u32[]{:S(2)}) collective-permute-start(bf16[2,128,128]{2,1,0:T(8,128)(2,1)S(1)} %get-tuple-element.31), channel_id=1, source_target_pairs={{0,4},{2,6},{4,0},{6,2},{8,12},{10,14},{12,8},{14,10},{16,20},{18,... | collective-permute-start | bytes 196616 | tf_op jit(solution)/shard_map/ppermute | solution.py:28
  12.9 0.7 %collective-permute-done.3 = bf16[2,128,128]{2,1,0:T(8,128)(2,1)S(1)} collective-permute-done((bf16[2,128,128]{2,1,0:T(8,128)(2,1)S(1)}, bf16[2,128,128]{2,1,0:T(8,128)(2,1)S(1)}, u32[]{:S(2)}, u32[]{:S(2)}) %collective-permute-start.3) | collective-permute-done | bytes 65568 | tf_op jit(solution)/shard_map/ppermute | solution.py:28
  13.6 2.2 %collective-permute-done.4 = bf16[2,128,128]{2,1,0:T(8,128)(2,1)S(1)} collective-permute-done((bf16[2,128,128]{2,1,0:T(8,128)(2,1)S(1)}, bf16[2,128,128]{2,1,0:T(8,128)(2,1)S(1)}, u32[]{:S(2)}, u32[]{:S(2)}) %collective-permute-start.4) | collective-permute-done | bytes 65568 | tf_op jit(solution)/shard_map/ppermute | solution.py:28
  15.8 0.5 %collective-permute-start.12 = (bf16[128,512]{1,0:T(8,128)(2,1)S(1)}, bf16[128,512]{1,0:T(8,128)(2,1)S(1)}, u32[]{:S(2)}, u32[]{:S(2)}) collective-permute-start(bf16[128,512]{1,0:T(8,128)(2,1)S(1)} %constant_dynamic-slice_fusion), channel_id=1, source_target_pairs={{0,2},{2,0},{4,6},{6,4},{8,10},{10,8},{12,14},{14,12},{16,18},{18,... | collective-permute-start | bytes 393224 | tf_op jit(solution)/shard_map/ppermute | solution.py:28
  16.4 1.8 %collective-permute-done.5 = bf16[2,128,128]{2,1,0:T(8,128)(2,1)S(1)} collective-permute-done((bf16[2,128,128]{2,1,0:T(8,128)(2,1)S(1)}, bf16[2,128,128]{2,1,0:T(8,128)(2,1)S(1)}, u32[]{:S(2)}, u32[]{:S(2)}) %collective-permute-start.5) | collective-permute-done | bytes 65568 | tf_op jit(solution)/shard_map/ppermute | solution.py:28
  18.7 2.2 %all-gather = bf16[16,128,128]{2,1,0:T(8,128)(2,1)S(1)} all-gather(bf16[8,128,128]{2,1,0:T(8,128)(2,1)S(1)} %pad_maximum_fusion.1), channel_id=2, replica_groups=mesh['blk'=16,'rep'=2] {'rep'}, dimensions={0}, use_global_device_ids=true | all-gather | bytes 786432 | tf_op jit(solution)/shard_map/all_gather | solution.py:82
  21.1 1.6 %collective-permute-start.14 = (bf16[128,512]{1,0:T(8,128)(2,1)S(1)}, bf16[128,512]{1,0:T(8,128)(2,1)S(1)}, u32[]{:S(2)}, u32[]{:S(2)}) collective-permute-start(bf16[128,512]{1,0:T(8,128)(2,1)S(1)} %constant_dynamic-slice_fusion), channel_id=1, source_target_pairs={{0,6},{2,4},{4,2},{6,0},{8,14},{10,12},{12,10},{14,8},{16,22},{18,... | collective-permute-start | bytes 393224 | tf_op jit(solution)/shard_map/ppermute | solution.py:28
  22.6 1.5 %convolution_convert_fusion = bf16[512,512]{1,0:T(8,128)(2,1)S(1)} fusion(bf16[512,512]{1,0:T(8,128)(2,1)S(1)} %maximum_maximum_fusion, bf16[128,512]{1,0:T(8,128)(2,1)S(1)} %collective-permute-done.2, bf16[128,512]{1,0:T(8,128)(2,1)} %collective-permute-done.1, bf16[128,512]{1,0:T(8,128)(2,1)} %collective-permute-done, ...), kind=kOutput, calls=%fused_computation.1 | convolution fusion | flops 270794752 | bytes 1572864 | tf_op jit(solution)/shard_map/dot_general | solution.py:55
  24.2 1.6 %collective-permute-start.6 = (bf16[128,512]{1,0:T(8,128)(2,1)S(1)}, bf16[128,512]{1,0:T(8,128)(2,1)S(1)}, u32[]{:S(2)}, u32[]{:S(2)}) collective-permute-start(bf16[128,512]{1,0:T(8,128)(2,1)S(1)} %pad_maximum_fusion.3), channel_id=1, source_target_pairs={{0,2},{2,0},{4,6},{6,4},{8,10},{10,8},{12,14},{14,12},{16,18},{18,... | collective-permute-start | bytes 393224 | tf_op jit(solution)/shard_map/ppermute | solution.py:28
  25.8 0.6 %collective-permute-start.7 = (bf16[128,512]{1,0:T(8,128)(2,1)S(1)}, bf16[128,512]{1,0:T(8,128)(2,1)S(1)}, u32[]{:S(2)}, u32[]{:S(2)}) collective-permute-start(bf16[128,512]{1,0:T(8,128)(2,1)S(1)} %pad_maximum_fusion.4), channel_id=1, source_target_pairs={{0,4},{2,6},{4,0},{6,2},{8,12},{10,14},{12,8},{14,10},{16,20},{18,... | collective-permute-start | bytes 393224 | tf_op jit(solution)/shard_map/ppermute | solution.py:28
  26.4 1.6 %collective-permute-start.8 = (bf16[128,512]{1,0:T(8,128)(2,1)S(1)}, bf16[128,512]{1,0:T(8,128)(2,1)S(1)}, u32[]{:S(2)}, u32[]{:S(2)}) collective-permute-start(bf16[128,512]{1,0:T(8,128)(2,1)S(1)} %pad_maximum_fusion.5), channel_id=1, source_target_pairs={{0,6},{2,4},{4,2},{6,0},{8,14},{10,12},{12,10},{14,8},{16,22},{18,... | collective-permute-start | bytes 393224 | tf_op jit(solution)/shard_map/ppermute | solution.py:28
  28.9 0.5 collective-permute-start.17
  29.4 1.8 %collective-permute-done.6 = bf16[128,512]{1,0:T(8,128)(2,1)S(1)} collective-permute-done((bf16[128,512]{1,0:T(8,128)(2,1)S(1)}, bf16[128,512]{1,0:T(8,128)(2,1)S(1)}, u32[]{:S(2)}, u32[]{:S(2)}) %collective-permute-start.6) | collective-permute-done | bytes 131104 | tf_op jit(solution)/shard_map/ppermute | solution.py:28
  31.2 2.6 %collective-permute-done.7 = bf16[128,512]{1,0:T(8,128)(2,1)S(1)} collective-permute-done((bf16[128,512]{1,0:T(8,128)(2,1)S(1)}, bf16[128,512]{1,0:T(8,128)(2,1)S(1)}, u32[]{:S(2)}, u32[]{:S(2)}) %collective-permute-start.7) | collective-permute-done | bytes 131104 | tf_op jit(solution)/shard_map/ppermute | solution.py:28
  33.9 2.0 %all_gather.11 = bf16[256,512]{1,0:T(8,128)(2,1)S(1)} all-gather(bf16[128,512]{1,0:T(8,128)(2,1)S(1)} %fusion.16), channel_id=1, replica_groups=mesh['blk'=16,'rep'=2] {'rep'}, dimensions={0}, use_global_device_ids=true | all-gather | bytes 393216 | tf_op jit(solution)/shard_map/all_gather | solution.py:115
  37.2 0.9 %collective-permute-start.11 = (bf16[128,512]{1,0:T(8,128)(2,1)S(1)}, bf16[128,512]{1,0:T(8,128)(2,1)S(1)}, u32[]{:S(2)}, u32[]{:S(2)}) collective-permute-start(bf16[128,512]{1,0:T(8,128)(2,1)S(1)} %get-tuple-element.8), channel_id=1, source_target_pairs={{0,6},{2,4},{4,2},{6,0},{8,14},{10,12},{12,10},{14,8},{16,22},{18,... | collective-permute-start | bytes 393224 | tf_op jit(solution)/shard_map/ppermute | solution.py:28
  38.1 1.6 %collective-permute-start.9 = (bf16[128,512]{1,0:T(8,128)(2,1)S(1)}, bf16[128,512]{1,0:T(8,128)(2,1)S(1)}, u32[]{:S(2)}, u32[]{:S(2)}) collective-permute-start(bf16[128,512]{1,0:T(8,128)(2,1)S(1)} %get-tuple-element.7), channel_id=1, source_target_pairs={{0,2},{2,0},{4,6},{6,4},{8,10},{10,8},{12,14},{14,12},{16,18},{18,... | collective-permute-start | bytes 393224 | tf_op jit(solution)/shard_map/ppermute | solution.py:28
  39.6 1.0 %collective-permute-start.10 = (bf16[128,512]{1,0:T(8,128)(2,1)S(1)}, bf16[128,512]{1,0:T(8,128)(2,1)S(1)}, u32[]{:S(2)}, u32[]{:S(2)}) collective-permute-start(bf16[128,512]{1,0:T(8,128)(2,1)S(1)} %get-tuple-element.9), channel_id=1, source_target_pairs={{0,4},{2,6},{4,0},{6,2},{8,12},{10,14},{12,8},{14,10},{16,20},{18,... | collective-permute-start | bytes 393224 | tf_op jit(solution)/shard_map/ppermute | solution.py:28
  40.7 1.9 %collective-permute-start.18 = (bf16[512,128]{1,0:T(8,128)(2,1)S(1)}, bf16[512,128]{1,0:T(8,128)(2,1)S(1)}, u32[]{:S(2)}, u32[]{:S(2)}) collective-permute-start(bf16[512,128]{1,0:T(8,128)(2,1)S(1)} %add_convert_fusion), channel_id=1, source_target_pairs={{0,16},{2,18},{4,20},{6,22},{8,24},{10,26},{12,28},{14,30},{16,0},... | collective-permute-start | bytes 393224 | tf_op jit(solution)/shard_map/ppermute | solution.py:32
  42.7 1.8 %collective-permute-done.11 = bf16[128,512]{1,0:T(8,128)(2,1)S(1)} collective-permute-done((bf16[128,512]{1,0:T(8,128)(2,1)S(1)}, bf16[128,512]{1,0:T(8,128)(2,1)S(1)}, u32[]{:S(2)}, u32[]{:S(2)}) %collective-permute-start.11) | collective-permute-done | bytes 131104 | tf_op jit(solution)/shard_map/ppermute | solution.py:28
  44.4 1.3 %collective-permute-done.9 = bf16[128,512]{1,0:T(8,128)(2,1)S(1)} collective-permute-done((bf16[128,512]{1,0:T(8,128)(2,1)S(1)}, bf16[128,512]{1,0:T(8,128)(2,1)S(1)}, u32[]{:S(2)}, u32[]{:S(2)}) %collective-permute-start.9) | collective-permute-done | bytes 131104 | tf_op jit(solution)/shard_map/ppermute | solution.py:28
  45.7 1.9 %collective-permute-start.16 = (bf16[64,512]{1,0:T(8,128)(2,1)S(1)}, bf16[64,512]{1,0:T(8,128)(2,1)S(1)}, u32[]{:S(2)}, u32[]{:S(2)}) collective-permute-start(bf16[64,512]{1,0:T(8,128)(2,1)S(1)} %fusion.23), channel_id=1, source_target_pairs={{0,16},{2,18},{4,20},{6,22},{8,24},{10,26},{12,28},{14,30},{16,0},... | collective-permute-start | bytes 196616 | tf_op jit(solution)/shard_map/ppermute | solution.py:32
  47.7 0.7 %add_convert_fusion.1 = bf16[128,512]{1,0:T(8,128)(2,1)} fusion(bf16[128,512]{1,0:T(8,128)(2,1)S(1)} %collective-permute-done.11, bf16[128,512]{1,0:T(8,128)(2,1)S(1)} %collective-permute-done.10, bf16[128,512]{1,0:T(8,128)(2,1)S(1)} %collective-permute-done.9, bf16[512,512]{1,0:T(8,128)(2,1)S(1)} %convolution_convert_fusion.1), kind=kLoop, calls=%fused_computation.30 | loop fusion | flops 524288 | bytes 655360 | tf_op jit(solution)/shard_map/convert_element_type | solution.py:131
  48.4 1.8 %collective-permute-done.18 = bf16[512,128]{1,0:T(8,128)(2,1)S(1)} collective-permute-done((bf16[512,128]{1,0:T(8,128)(2,1)S(1)}, bf16[512,128]{1,0:T(8,128)(2,1)S(1)}, u32[]{:S(2)}, u32[]{:S(2)}) %collective-permute-start.18) | collective-permute-done | bytes 131104 | tf_op jit(solution)/shard_map/ppermute | solution.py:32
  51.0 0.7 %fusion.19 = f32[64,512]{1,0:T(8,128)} fusion(bf16[64,512]{1,0:T(8,128)(2,1)S(1)} %collective-permute-done.16, f32[4,64,512]{2,1,0:T(8,128)S(1)} %bitcast.122, s32[]{:T(128)S(6)} %select_n.271, bf16[128,512]{1,0:T(8,128)(2,1)S(1)} %collective-permute-done.15), kind=kLoop, calls=%fused_computation.41 | loop fusion | flops 131072 | bytes 393220 | tf_op jit(solution)/shard_map/add | solution.py:45
  52.1 1.1 %select_convert_fusion = bf16[128,512]{1,0:T(8,128)(2,1)} fusion(bf16[128,512]{1,0:T(8,128)(2,1)S(1)} %collective-permute-done.19, bf16[128,1024]{1,0:T(8,128)(2,1)S(1)} %copy-done.1, s32[]{:T(128)S(6)} %select_n.214, bf16[512,128]{1,0:T(8,128)(2,1)S(1)} %fusion.13, bf16[2,512,1024]{2,1,0:T(8,128)(2,1)S(1)} %bitcast.114, s32[]{:T(128)S(6)} %select_n.279, ...), kind=kOutput, calls=%fused_computation.28 | convolution fusion | flops 67567616 | bytes 1048588 | tf_op jit(solution)/shard_map/dot_general | solution.py:55
  (56 shorter events, 5.2 us)
Async XLA Ops:
  0.6 12.2 %copy-start = (bf16[1024,1024]{1,0:T(8,128)(2,1)S(1)}, bf16[1024,1024]{1,0:T(8,128)(2,1)}, u32[]{:S(2)}) copy-start(bf16[1024,1024]{1,0:T(8,128)(2,1)} %param.8) | copy-start | bytes 6291460
  0.6 12.3 %copy-start.2 = (bf16[128,1024]{1,0:T(8,128)(2,1)S(1)}, bf16[128,1024]{1,0:T(8,128)(2,1)}, u32[]{:S(2)}) copy-start(bf16[128,1024]{1,0:T(8,128)(2,1)} %param.9) | copy-start | bytes 786436
  1.7 19.3 %collective-permute-start = (bf16[128,512]{1,0:T(8,128)(2,1)S(1)}, bf16[128,512]{1,0:T(8,128)(2,1)}, u32[]{:S(2)}, u32[]{:S(2)}) collective-permute-start(bf16[128,512]{1,0:T(8,128)(2,1)S(1)} %dynamic-slice_maximum_fusion), channel_id=1, source_target_pairs={{0,8},{2,10},{4,12},{6,14},{8,0},{10,2},{12,4},{14,6},{16,24},{18,... | collective-permute-start | bytes 393224 | tf_op jit(solution)/shard_map/ppermute | solution.py:32
  4.8 17.8 %collective-permute-start.1 = (bf16[128,512]{1,0:T(8,128)(2,1)S(1)}, bf16[128,512]{1,0:T(8,128)(2,1)}, u32[]{:S(2)}, u32[]{:S(2)}) collective-permute-start(bf16[128,512]{1,0:T(8,128)(2,1)S(1)} %dynamic-slice_maximum_fusion), channel_id=1, source_target_pairs={{0,16},{2,18},{4,20},{6,22},{8,24},{10,26},{12,28},{14,30},{16,0},... | collective-permute-start | bytes 393224 | tf_op jit(solution)/shard_map/ppermute | solution.py:32
  9.3 4.3 %collective-permute-start.3 = (bf16[2,128,128]{2,1,0:T(8,128)(2,1)S(1)}, bf16[2,128,128]{2,1,0:T(8,128)(2,1)S(1)}, u32[]{:S(2)}, u32[]{:S(2)}) collective-permute-start(bf16[2,128,128]{2,1,0:T(8,128)(2,1)S(1)} %get-tuple-element.32), channel_id=1, source_target_pairs={{0,2},{2,0},{4,6},{6,4},{8,10},{10,8},{12,14},{14,12},{16,18},{18,... | collective-permute-start | bytes 196616 | tf_op jit(solution)/shard_map/ppermute | solution.py:28
  10.9 5.0 %collective-permute-start.4 = (bf16[2,128,128]{2,1,0:T(8,128)(2,1)S(1)}, bf16[2,128,128]{2,1,0:T(8,128)(2,1)S(1)}, u32[]{:S(2)}, u32[]{:S(2)}) collective-permute-start(bf16[2,128,128]{2,1,0:T(8,128)(2,1)S(1)} %get-tuple-element.31), channel_id=1, source_target_pairs={{0,4},{2,6},{4,0},{6,2},{8,12},{10,14},{12,8},{14,10},{16,20},{18,... | collective-permute-start | bytes 196616 | tf_op jit(solution)/shard_map/ppermute | solution.py:28
  12.4 5.8 %collective-permute-start.5 = (bf16[2,128,128]{2,1,0:T(8,128)(2,1)S(1)}, bf16[2,128,128]{2,1,0:T(8,128)(2,1)S(1)}, u32[]{:S(2)}, u32[]{:S(2)}) collective-permute-start(bf16[2,128,128]{2,1,0:T(8,128)(2,1)S(1)} %get-tuple-element.30), channel_id=1, source_target_pairs={{0,6},{2,4},{4,2},{6,0},{8,14},{10,12},{12,10},{14,8},{16,22},{18,... | collective-permute-start | bytes 196616 | tf_op jit(solution)/shard_map/ppermute | solution.py:28
  13.6 9.0 %collective-permute-start.2 = (bf16[128,512]{1,0:T(8,128)(2,1)S(1)}, bf16[128,512]{1,0:T(8,128)(2,1)S(1)}, u32[]{:S(2)}, u32[]{:S(2)}) collective-permute-start(bf16[128,512]{1,0:T(8,128)(2,1)S(1)} %dynamic-slice_maximum_fusion), channel_id=1, source_target_pairs={{0,24},{2,26},{4,28},{6,30},{8,16},{10,18},{12,20},{14,22},{16,8},... | collective-permute-start | bytes 393224 | tf_op jit(solution)/shard_map/ppermute | solution.py:32
  15.8 10.6 %collective-permute-start.12 = (bf16[128,512]{1,0:T(8,128)(2,1)S(1)}, bf16[128,512]{1,0:T(8,128)(2,1)S(1)}, u32[]{:S(2)}, u32[]{:S(2)}) collective-permute-start(bf16[128,512]{1,0:T(8,128)(2,1)S(1)} %constant_dynamic-slice_fusion), channel_id=1, source_target_pairs={{0,2},{2,0},{4,6},{6,4},{8,10},{10,8},{12,14},{14,12},{16,18},{18,... | collective-permute-start | bytes 393224 | tf_op jit(solution)/shard_map/ppermute | solution.py:28
  18.2 9.8 %collective-permute-start.13 = (bf16[128,512]{1,0:T(8,128)(2,1)S(1)}, bf16[128,512]{1,0:T(8,128)(2,1)S(1)}, u32[]{:S(2)}, u32[]{:S(2)}) collective-permute-start(bf16[128,512]{1,0:T(8,128)(2,1)S(1)} %constant_dynamic-slice_fusion), channel_id=1, source_target_pairs={{0,4},{2,6},{4,0},{6,2},{8,12},{10,14},{12,8},{14,10},{16,20},{18,... | collective-permute-start | bytes 393224 | tf_op jit(solution)/shard_map/ppermute | solution.py:28
  21.1 7.3 %collective-permute-start.14 = (bf16[128,512]{1,0:T(8,128)(2,1)S(1)}, bf16[128,512]{1,0:T(8,128)(2,1)S(1)}, u32[]{:S(2)}, u32[]{:S(2)}) collective-permute-start(bf16[128,512]{1,0:T(8,128)(2,1)S(1)} %constant_dynamic-slice_fusion), channel_id=1, source_target_pairs={{0,6},{2,4},{4,2},{6,0},{8,14},{10,12},{12,10},{14,8},{16,22},{18,... | collective-permute-start | bytes 393224 | tf_op jit(solution)/shard_map/ppermute | solution.py:28
  24.2 7.0 %collective-permute-start.6 = (bf16[128,512]{1,0:T(8,128)(2,1)S(1)}, bf16[128,512]{1,0:T(8,128)(2,1)S(1)}, u32[]{:S(2)}, u32[]{:S(2)}) collective-permute-start(bf16[128,512]{1,0:T(8,128)(2,1)S(1)} %pad_maximum_fusion.3), channel_id=1, source_target_pairs={{0,2},{2,0},{4,6},{6,4},{8,10},{10,8},{12,14},{14,12},{16,18},{18,... | collective-permute-start | bytes 393224 | tf_op jit(solution)/shard_map/ppermute | solution.py:28
  25.8 8.0 %collective-permute-start.7 = (bf16[128,512]{1,0:T(8,128)(2,1)S(1)}, bf16[128,512]{1,0:T(8,128)(2,1)S(1)}, u32[]{:S(2)}, u32[]{:S(2)}) collective-permute-start(bf16[128,512]{1,0:T(8,128)(2,1)S(1)} %pad_maximum_fusion.4), channel_id=1, source_target_pairs={{0,4},{2,6},{4,0},{6,2},{8,12},{10,14},{12,8},{14,10},{16,20},{18,... | collective-permute-start | bytes 393224 | tf_op jit(solution)/shard_map/ppermute | solution.py:28
  26.4 7.4 %collective-permute-start.8 = (bf16[128,512]{1,0:T(8,128)(2,1)S(1)}, bf16[128,512]{1,0:T(8,128)(2,1)S(1)}, u32[]{:S(2)}, u32[]{:S(2)}) collective-permute-start(bf16[128,512]{1,0:T(8,128)(2,1)S(1)} %pad_maximum_fusion.5), channel_id=1, source_target_pairs={{0,6},{2,4},{4,2},{6,0},{8,14},{10,12},{12,10},{14,8},{16,22},{18,... | collective-permute-start | bytes 393224 | tf_op jit(solution)/shard_map/ppermute | solution.py:28
  28.9 11.8 %collective-permute-start.17 = (bf16[1024,128]{1,0:T(8,128)(2,1)S(1)}, bf16[1024,128]{1,0:T(8,128)(2,1)S(1)}, u32[]{:S(2)}, u32[]{:S(2)}) collective-permute-start(bf16[1024,128]{1,0:T(8,128)(2,1)S(1)} %pad_maximum_fusion.2), channel_id=1, source_target_pairs={{0,8},{2,10},{4,12},{6,14},{8,0},{10,2},{12,4},{14,6},{16,24},{18,... | collective-permute-start | bytes 786440 | tf_op jit(solution)/shard_map/ppermute | solution.py:32
  36.6 15.6 %copy-start.1 = (bf16[128,1024]{1,0:T(8,128)(2,1)S(1)}, bf16[128,1024]{1,0:T(8,128)(2,1)}, u32[]{:S(2)}) copy-start(bf16[128,1024]{1,0:T(8,128)(2,1)} %param.5) | copy-start | bytes 786436
  36.7 6.0 %collective-permute-start.15 = (bf16[128,512]{1,0:T(8,128)(2,1)S(1)}, bf16[128,512]{1,0:T(8,128)(2,1)S(1)}, u32[]{:S(2)}, u32[]{:S(2)}) collective-permute-start(bf16[128,512]{1,0:T(8,128)(2,1)S(1)} %pad_maximum_fusion.6), channel_id=1, source_target_pairs={{0,8},{2,10},{4,12},{6,14},{8,0},{10,2},{12,4},{14,6},{16,24},{18,... | collective-permute-start | bytes 393224 | tf_op jit(solution)/shard_map/ppermute | solution.py:32
  37.2 7.3 %collective-permute-start.11 = (bf16[128,512]{1,0:T(8,128)(2,1)S(1)}, bf16[128,512]{1,0:T(8,128)(2,1)S(1)}, u32[]{:S(2)}, u32[]{:S(2)}) collective-permute-start(bf16[128,512]{1,0:T(8,128)(2,1)S(1)} %get-tuple-element.8), channel_id=1, source_target_pairs={{0,6},{2,4},{4,2},{6,0},{8,14},{10,12},{12,10},{14,8},{16,22},{18,... | collective-permute-start | bytes 393224 | tf_op jit(solution)/shard_map/ppermute | solution.py:28
  38.1 7.6 %collective-permute-start.9 = (bf16[128,512]{1,0:T(8,128)(2,1)S(1)}, bf16[128,512]{1,0:T(8,128)(2,1)S(1)}, u32[]{:S(2)}, u32[]{:S(2)}) collective-permute-start(bf16[128,512]{1,0:T(8,128)(2,1)S(1)} %get-tuple-element.7), channel_id=1, source_target_pairs={{0,2},{2,0},{4,6},{6,4},{8,10},{10,8},{12,14},{14,12},{16,18},{18,... | collective-permute-start | bytes 393224 | tf_op jit(solution)/shard_map/ppermute | solution.py:28
  39.6 8.0 %collective-permute-start.10 = (bf16[128,512]{1,0:T(8,128)(2,1)S(1)}, bf16[128,512]{1,0:T(8,128)(2,1)S(1)}, u32[]{:S(2)}, u32[]{:S(2)}) collective-permute-start(bf16[128,512]{1,0:T(8,128)(2,1)S(1)} %get-tuple-element.9), channel_id=1, source_target_pairs={{0,4},{2,6},{4,0},{6,2},{8,12},{10,14},{12,8},{14,10},{16,20},{18,... | collective-permute-start | bytes 393224 | tf_op jit(solution)/shard_map/ppermute | solution.py:28
  40.7 9.5 %collective-permute-start.18 = (bf16[512,128]{1,0:T(8,128)(2,1)S(1)}, bf16[512,128]{1,0:T(8,128)(2,1)S(1)}, u32[]{:S(2)}, u32[]{:S(2)}) collective-permute-start(bf16[512,128]{1,0:T(8,128)(2,1)S(1)} %add_convert_fusion), channel_id=1, source_target_pairs={{0,16},{2,18},{4,20},{6,22},{8,24},{10,26},{12,28},{14,30},{16,0},... | collective-permute-start | bytes 393224 | tf_op jit(solution)/shard_map/ppermute | solution.py:32
  45.7 5.3 %collective-permute-start.16 = (bf16[64,512]{1,0:T(8,128)(2,1)S(1)}, bf16[64,512]{1,0:T(8,128)(2,1)S(1)}, u32[]{:S(2)}, u32[]{:S(2)}) collective-permute-start(bf16[64,512]{1,0:T(8,128)(2,1)S(1)} %fusion.23), channel_id=1, source_target_pairs={{0,16},{2,18},{4,20},{6,22},{8,24},{10,26},{12,28},{14,30},{16,0},... | collective-permute-start | bytes 196616 | tf_op jit(solution)/shard_map/ppermute | solution.py:32
  50.7 1.4 %collective-permute-start.19 = (bf16[128,512]{1,0:T(8,128)(2,1)S(1)}, bf16[128,512]{1,0:T(8,128)(2,1)S(1)}, u32[]{:S(2)}, u32[]{:S(2)}) collective-permute-start(bf16[128,512]{1,0:T(8,128)(2,1)S(1)} %convolution_convert_fusion.2), channel_id=1, source_target_pairs={{0,1},{1,0},{2,3},{3,2},{4,5},{5,4},{6,7},{7,6},{8,9},{9,8},{10,11... | collective-permute-start | bytes 393224 | tf_op jit(solution)/shard_map/ppermute | solution.py:52

commit v33 on v29

--- a/solution.py
+++ b/solution.py
@@ -128,7 +128,6 @@
         along_outer,
         out_got[1::2],
     )
-    out_part = sum(part.astype(jnp.float32) for part in out_got).astype(bf16)
 
     back = after(back, weight_part).astype(bf16)
     w_rows = w_out.reshape(rep_count, cols_here, feature_width)
@@ -145,6 +144,8 @@
         grad_in = dot(back_full, w_mine, ((0,), (1,)))
     pre_part = columns_of(hidden_pre, rep_pos)
     grad_pre = jnp.where(pre_part > 0, grad_in, 0.0).astype(bf16)
+    out_part = sum(part.astype(jnp.float32) for part in out_got)
+    out_part = after(out_part, grad_pre).astype(bf16)
     return (out_part, grad_weight, grad_pre)
 
 

time: 52 us -> 52 us (level)
  other arithmetic: 3.85 us -> 3.11 us
  waiting for transfers between devices: 9.8 us -> 10.5 us
    convert_element_type x1 -> x0, other arithmetic: 0.72 us -> none  [shards(): out_part = sum((part.astype(jnp.float32) for part in out_got)).astype(bf16)]
    ppermute x8, waiting for transfers between devices: 3.69 us -> 4.35 us  [along_outer(): return lax.ppermute(value, 'blk', pairs) if turn else value]
  transfers between devices with their start and end apart: 21 -> 21, of which waited for: 8 -> 8; matrix products, arithmetic and copies ran while one was open for 12% -> 11% of each run, Pallas kernels for 0% -> 0%
where the time goes in v33:
time: 52 us; the launch traced here: 51.8 us
  starting transfers between devices  28.7 us (55%)
  waiting for transfers between devices  10.5 us (20%)
  blocking collectives  4.18 us (8%)
  matrix products  3.15 us (6%)
  other arithmetic  3.11 us (6%)
  local copies, waits for them, and re-layouts  1.23 us (2%)
  between operations  0.92 us (2%)
    ppermute x12, starting transfers between devices, along_inner(): return lax.ppermute(value, 'blk', pairs) if turn else value  14.4 us
    ppermute x8, starting transfers between devices, along_outer(): return lax.ppermute(value, 'blk', pairs) if turn else value  14.2 us
    ppermute x12, waiting for transfers between devices, along_inner(): return lax.ppermute(value, 'blk', pairs) if turn else value  6.11 us
    ppermute x8, waiting for transfers between devices, along_outer(): return lax.ppermute(value, 'blk', pairs) if turn else value  4.35 us
    dot_general x6, matrix products, dot(): lax.dot_general(lhs, rhs, (dims, ((), ())), preferred_element_type=jnp.fl...  3.15 us
    all_gather x1, blocking collectives, shards(): everyone = lax.all_gather(jnp.concatenate(arrived, 0), 'rep', axis=0)  2.18 us
    all_gather x1, blocking collectives, shards(): lax.all_gather(mixed_cols.astype(bf16), 'rep', axis=0, tiled=True)  1.99 us
    max x1, other arithmetic, shards(): hidden_part = jnp.maximum(columns_of(hidden_pre, rep_pos), 0)  1.08 us
  transfers between devices with their start and end apart: 21, of which 8 were waited for; matrix products, arithmetic and copies ran while one was open for 11% of the time, Pallas kernels for 0%

profile of v33, /device:TPU:0, one launch (start us, length us, event | category | flops | bytes accessed | tf_op | source)
XLA Modules:
  0.0 51.8 jit_solution(2866357421659179576)
XLA Ops:
  0.7 1.1 %dynamic-slice_maximum_fusion = bf16[128,512]{1,0:T(8,128)(2,1)S(1)} fusion(bf16[128,1024]{1,0:T(8,128)(2,1)} %param.5, s32[]{:T(128)S(6)} %select_n.214), kind=kLoop, calls=%fused_computation.42 | loop fusion | flops 262144 | bytes 262148 | tf_op jit(solution)/shard_map/max | solution.py:69
  1.7 5.1 %collective-permute-start.2 = (bf16[128,512]{1,0:T(8,128)(2,1)S(1)}, bf16[128,512]{1,0:T(8,128)(2,1)S(1)}, u32[]{:S(2)}, u32[]{:S(2)}) collective-permute-start(bf16[128,512]{1,0:T(8,128)(2,1)S(1)} %dynamic-slice_maximum_fusion), channel_id=1, source_target_pairs={{0,24},{2,26},{4,28},{6,30},{8,16},{10,18},{12,20},{14,22},{16,8},... | collective-permute-start | bytes 393224 | tf_op jit(solution)/shard_map/ppermute | solution.py:32
  6.9 0.7 %add_bitcast_fusion = s32[8]{0:T(128)S(1)} fusion(s32[1,8]{1,0:T(1,128)} %param.7, s32[]{:T(128)S(6)} %shift_right_arithmetic.54, s32[]{:T(128)S(6)} %and.60), kind=kLoop, calls=%fused_computation.92 | loop fusion | flops 56 | bytes 72 | tf_op jit(solution)/shard_map/eq | solution.py:75
  7.6 0.9 %slice_bitcast_fusion.9 = (bf16[128,128]{1,0:T(8,128)(2,1)S(1)}, bf16[128,128]{1,0:T(8,128)(2,1)S(1)}, bf16[128,128]{1,0:T(8,128)(2,1)S(1)}, bf16[128,128]{1,0:T...) fusion(bf16[1,8,128,128]{3,2,1,0:T(8,128)(2,1)} %param.6), kind=kLoop, calls=%fused_computation.73 | loop fusion | bytes 524288 | tf_op jit(solution)/shard_map/jit(_where)/broadcast_in_dim | solution.py:78
  8.7 2.5 %collective-permute-start.5 = (bf16[2,128,128]{2,1,0:T(8,128)(2,1)S(1)}, bf16[2,128,128]{2,1,0:T(8,128)(2,1)S(1)}, u32[]{:S(2)}, u32[]{:S(2)}) collective-permute-start(bf16[2,128,128]{2,1,0:T(8,128)(2,1)S(1)} %get-tuple-element.31), channel_id=1, source_target_pairs={{0,6},{2,4},{4,2},{6,0},{8,14},{10,12},{12,10},{14,8},{16,22},{18,... | collective-permute-start | bytes 196616 | tf_op jit(solution)/shard_map/ppermute | solution.py:28
  11.8 0.5 %collective-permute-start.3 = (bf16[2,128,128]{2,1,0:T(8,128)(2,1)S(1)}, bf16[2,128,128]{2,1,0:T(8,128)(2,1)S(1)}, u32[]{:S(2)}, u32[]{:S(2)}) collective-permute-start(bf16[2,128,128]{2,1,0:T(8,128)(2,1)S(1)} %get-tuple-element.33), channel_id=1, source_target_pairs={{0,2},{2,0},{4,6},{6,4},{8,10},{10,8},{12,14},{14,12},{16,18},{18,... | collective-permute-start | bytes 196616 | tf_op jit(solution)/shard_map/ppermute | solution.py:28
  12.4 1.7 %collective-permute-done.5 = bf16[2,128,128]{2,1,0:T(8,128)(2,1)S(1)} collective-permute-done((bf16[2,128,128]{2,1,0:T(8,128)(2,1)S(1)}, bf16[2,128,128]{2,1,0:T(8,128)(2,1)S(1)}, u32[]{:S(2)}, u32[]{:S(2)}) %collective-permute-start.5) | collective-permute-done | bytes 65568 | tf_op jit(solution)/shard_map/ppermute | solution.py:28
  14.1 0.6 %collective-permute-start = (bf16[128,512]{1,0:T(8,128)(2,1)S(1)}, bf16[128,512]{1,0:T(8,128)(2,1)S(1)}, u32[]{:S(2)}, u32[]{:S(2)}) collective-permute-start(bf16[128,512]{1,0:T(8,128)(2,1)S(1)} %dynamic-slice_maximum_fusion), channel_id=1, source_target_pairs={{0,8},{2,10},{4,12},{6,14},{8,0},{10,2},{12,4},{14,6},{16,24},{18,... | collective-permute-start | bytes 393224 | tf_op jit(solution)/shard_map/ppermute | solution.py:32
  14.7 0.8 %collective-permute-done.4 = bf16[2,128,128]{2,1,0:T(8,128)(2,1)S(1)} collective-permute-done((bf16[2,128,128]{2,1,0:T(8,128)(2,1)S(1)}, bf16[2,128,128]{2,1,0:T(8,128)(2,1)S(1)}, u32[]{:S(2)}, u32[]{:S(2)}) %collective-permute-start.4) | collective-permute-done | bytes 65568 | tf_op jit(solution)/shard_map/ppermute | solution.py:28
  15.5 1.8 %collective-permute-start.14 = (bf16[128,512]{1,0:T(8,128)(2,1)S(1)}, bf16[128,512]{1,0:T(8,128)(2,1)S(1)}, u32[]{:S(2)}, u32[]{:S(2)}) collective-permute-start(bf16[128,512]{1,0:T(8,128)(2,1)S(1)} %constant_dynamic-slice_fusion), channel_id=1, source_target_pairs={{0,6},{2,4},{4,2},{6,0},{8,14},{10,12},{12,10},{14,8},{16,22},{18,... | collective-permute-start | bytes 393224 | tf_op jit(solution)/shard_map/ppermute | solution.py:28
  17.3 1.1 %collective-permute-start.13 = (bf16[128,512]{1,0:T(8,128)(2,1)S(1)}, bf16[128,512]{1,0:T(8,128)(2,1)S(1)}, u32[]{:S(2)}, u32[]{:S(2)}) collective-permute-start(bf16[128,512]{1,0:T(8,128)(2,1)S(1)} %constant_dynamic-slice_fusion), channel_id=1, source_target_pairs={{0,4},{2,6},{4,0},{6,2},{8,12},{10,14},{12,8},{14,10},{16,20},{18,... | collective-permute-start | bytes 393224 | tf_op jit(solution)/shard_map/ppermute | solution.py:28
  18.5 2.2 %all-gather = bf16[16,128,128]{2,1,0:T(8,128)(2,1)S(1)} all-gather(bf16[8,128,128]{2,1,0:T(8,128)(2,1)S(1)} %pad_maximum_fusion.1), channel_id=2, replica_groups=mesh['blk'=16,'rep'=2] {'rep'}, dimensions={0}, use_global_device_ids=true | all-gather | bytes 786432 | tf_op jit(solution)/shard_map/all_gather | solution.py:82
  20.9 0.6 %collective-permute-start.12 = (bf16[128,512]{1,0:T(8,128)(2,1)S(1)}, bf16[128,512]{1,0:T(8,128)(2,1)S(1)}, u32[]{:S(2)}, u32[]{:S(2)}) collective-permute-start(bf16[128,512]{1,0:T(8,128)(2,1)S(1)} %constant_dynamic-slice_fusion), channel_id=1, source_target_pairs={{0,2},{2,0},{4,6},{6,4},{8,10},{10,8},{12,14},{14,12},{16,18},{18,... | collective-permute-start | bytes 393224 | tf_op jit(solution)/shard_map/ppermute | solution.py:28
  22.1 1.5 %collective-permute-start.7 = (bf16[128,512]{1,0:T(8,128)(2,1)S(1)}, bf16[128,512]{1,0:T(8,128)(2,1)S(1)}, u32[]{:S(2)}, u32[]{:S(2)}) collective-permute-start(bf16[128,512]{1,0:T(8,128)(2,1)S(1)} %pad_maximum_fusion.3), channel_id=1, source_target_pairs={{0,4},{2,6},{4,0},{6,2},{8,12},{10,14},{12,8},{14,10},{16,20},{18,... | collective-permute-start | bytes 393224 | tf_op jit(solution)/shard_map/ppermute | solution.py:28
  23.7 1.0 %collective-permute-start.6 = (bf16[128,512]{1,0:T(8,128)(2,1)S(1)}, bf16[128,512]{1,0:T(8,128)(2,1)S(1)}, u32[]{:S(2)}, u32[]{:S(2)}) collective-permute-start(bf16[128,512]{1,0:T(8,128)(2,1)S(1)} %pad_maximum_fusion.2), channel_id=1, source_target_pairs={{0,2},{2,0},{4,6},{6,4},{8,10},{10,8},{12,14},{14,12},{16,18},{18,... | collective-permute-start | bytes 393224 | tf_op jit(solution)/shard_map/ppermute | solution.py:28
  24.7 1.2 %collective-permute-start.8 = (bf16[128,512]{1,0:T(8,128)(2,1)S(1)}, bf16[128,512]{1,0:T(8,128)(2,1)S(1)}, u32[]{:S(2)}, u32[]{:S(2)}) collective-permute-start(bf16[128,512]{1,0:T(8,128)(2,1)S(1)} %pad_maximum_fusion.4), channel_id=1, source_target_pairs={{0,6},{2,4},{4,2},{6,0},{8,14},{10,12},{12,10},{14,8},{16,22},{18,... | collective-permute-start | bytes 393224 | tf_op jit(solution)/shard_map/ppermute | solution.py:28
  25.9 1.1 %collective-permute-done.12 = bf16[128,512]{1,0:T(8,128)(2,1)S(1)} collective-permute-done((bf16[128,512]{1,0:T(8,128)(2,1)S(1)}, bf16[128,512]{1,0:T(8,128)(2,1)S(1)}, u32[]{:S(2)}, u32[]{:S(2)}) %collective-permute-start.12) | collective-permute-done | bytes 131104 | tf_op jit(solution)/shard_map/ppermute | solution.py:28
  27.5 1.1 %collective-permute-start.15 = (bf16[512,128]{1,0:T(8,128)(2,1)S(1)}, bf16[512,128]{1,0:T(8,128)(2,1)S(1)}, u32[]{:S(2)}, u32[]{:S(2)}) collective-permute-start(bf16[512,128]{1,0:T(8,128)(2,1)S(1)} %get-tuple-element.8), channel_id=1, source_target_pairs={{0,8},{2,10},{4,12},{6,14},{8,0},{10,2},{12,4},{14,6},{16,24},{18,... | collective-permute-start | bytes 393224 | tf_op jit(solution)/shard_map/ppermute | solution.py:32
  28.6 2.8 %collective-permute-start.17 = (bf16[512,128]{1,0:T(8,128)(2,1)S(1)}, bf16[512,128]{1,0:T(8,128)(2,1)S(1)}, u32[]{:S(2)}, u32[]{:S(2)}) collective-permute-start(bf16[512,128]{1,0:T(8,128)(2,1)S(1)} %get-tuple-element.9), channel_id=1, source_target_pairs={{0,24},{2,26},{4,28},{6,30},{8,16},{10,18},{12,20},{14,22},{16,8},... | collective-permute-start | bytes 393224 | tf_op jit(solution)/shard_map/ppermute | solution.py:32
  31.6 0.8 %collective-permute-done.8 = bf16[128,512]{1,0:T(8,128)(2,1)S(1)} collective-permute-done((bf16[128,512]{1,0:T(8,128)(2,1)S(1)}, bf16[128,512]{1,0:T(8,128)(2,1)S(1)}, u32[]{:S(2)}, u32[]{:S(2)}) %collective-permute-start.8) | collective-permute-done | bytes 131104 | tf_op jit(solution)/shard_map/ppermute | solution.py:28
  32.5 2.0 %all_gather.11 = bf16[256,512]{1,0:T(8,128)(2,1)S(1)} all-gather(bf16[128,512]{1,0:T(8,128)(2,1)S(1)} %fusion.16), channel_id=1, replica_groups=mesh['blk'=16,'rep'=2] {'rep'}, dimensions={0}, use_global_device_ids=true | all-gather | bytes 393216 | tf_op jit(solution)/shard_map/all_gather | solution.py:115
  35.2 1.3 %collective-permute-start.19 = (bf16[128,512]{1,0:T(8,128)(2,1)S(1)}, bf16[128,512]{1,0:T(8,128)(2,1)S(1)}, u32[]{:S(2)}, u32[]{:S(2)}) collective-permute-start(bf16[128,512]{1,0:T(8,128)(2,1)S(1)} %pad_maximum_fusion.5), channel_id=1, source_target_pairs={{0,8},{2,10},{4,12},{6,14},{8,0},{10,2},{12,4},{14,6},{16,24},{18,... | collective-permute-start | bytes 393224 | tf_op jit(solution)/shard_map/ppermute | solution.py:32
  36.5 1.1 %collective-permute-start.9 = (bf16[128,512]{1,0:T(8,128)(2,1)S(1)}, bf16[128,512]{1,0:T(8,128)(2,1)S(1)}, u32[]{:S(2)}, u32[]{:S(2)}) collective-permute-start(bf16[128,512]{1,0:T(8,128)(2,1)S(1)} %get-tuple-element.5), channel_id=1, source_target_pairs={{0,2},{2,0},{4,6},{6,4},{8,10},{10,8},{12,14},{14,12},{16,18},{18,... | collective-permute-start | bytes 393224 | tf_op jit(solution)/shard_map/ppermute | solution.py:28
  37.7 1.4 %collective-permute-start.11 = (bf16[128,512]{1,0:T(8,128)(2,1)S(1)}, bf16[128,512]{1,0:T(8,128)(2,1)S(1)}, u32[]{:S(2)}, u32[]{:S(2)}) collective-permute-start(bf16[128,512]{1,0:T(8,128)(2,1)S(1)} %get-tuple-element.6), channel_id=1, source_target_pairs={{0,6},{2,4},{4,2},{6,0},{8,14},{10,12},{12,10},{14,8},{16,22},{18,... | collective-permute-start | bytes 393224 | tf_op jit(solution)/shard_map/ppermute | solution.py:28
  39.1 3.2 %collective-permute-done.16 = bf16[512,128]{1,0:T(8,128)(2,1)S(1)} collective-permute-done((bf16[512,128]{1,0:T(8,128)(2,1)S(1)}, bf16[512,128]{1,0:T(8,128)(2,1)S(1)}, u32[]{:S(2)}, u32[]{:S(2)}) %collective-permute-start.16) | collective-permute-done | bytes 131104 | tf_op jit(solution)/shard_map/ppermute | solution.py:32
  42.9 1.1 %collective-permute-start.10 = (bf16[128,512]{1,0:T(8,128)(2,1)S(1)}, bf16[128,512]{1,0:T(8,128)(2,1)S(1)}, u32[]{:S(2)}, u32[]{:S(2)}) collective-permute-start(bf16[128,512]{1,0:T(8,128)(2,1)S(1)} %get-tuple-element.7), channel_id=1, source_target_pairs={{0,4},{2,6},{4,0},{6,2},{8,12},{10,14},{12,8},{14,10},{16,20},{18,... | collective-permute-start | bytes 393224 | tf_op jit(solution)/shard_map/ppermute | solution.py:28
  44.0 1.1 %collective-permute-done.11 = bf16[128,512]{1,0:T(8,128)(2,1)S(1)} collective-permute-done((bf16[128,512]{1,0:T(8,128)(2,1)S(1)}, bf16[128,512]{1,0:T(8,128)(2,1)S(1)}, u32[]{:S(2)}, u32[]{:S(2)}) %collective-permute-start.11) | collective-permute-done | bytes 131104 | tf_op jit(solution)/shard_map/ppermute | solution.py:28
  45.1 3.1 %collective-permute-start.20 = (bf16[64,512]{1,0:T(8,128)(2,1)S(1)}, bf16[64,512]{1,0:T(8,128)(2,1)S(1)}, u32[]{:S(2)}, u32[]{:S(2)}) collective-permute-start(bf16[64,512]{1,0:T(8,128)(2,1)S(1)} %fusion.23), channel_id=1, source_target_pairs={{0,16},{2,18},{4,20},{6,22},{8,24},{10,26},{12,28},{14,30},{16,0},... | collective-permute-start | bytes 196616 | tf_op jit(solution)/shard_map/ppermute | solution.py:32
  48.2 0.7 %collective-permute-done.10 = bf16[128,512]{1,0:T(8,128)(2,1)S(1)} collective-permute-done((bf16[128,512]{1,0:T(8,128)(2,1)S(1)}, bf16[128,512]{1,0:T(8,128)(2,1)S(1)}, u32[]{:S(2)}, u32[]{:S(2)}) %collective-permute-start.10) | collective-permute-done | bytes 131104 | tf_op jit(solution)/shard_map/ppermute | solution.py:28
  48.8 1.2 %add_convert_fusion = (bf16[128,512]{1,0:T(8,128)(2,1)}, bf16[128,512]{1,0:T(8,128)(2,1)}) fusion(bf16[128,512]{1,0:T(8,128)(2,1)S(1)} %collective-permute-done.11, bf16[128,512]{1,0:T(8,128)(2,1)S(1)} %collective-permute-done.10, bf16[128,512]{1,0:T(8,128)(2,1)S(1)} %collective-permute-done.9, bf16[512,512]{1,0:T(8,128)(2,1)S(1)} %convolution_convert_fusion.1, ...), kind=kOutput, calls=%fused_computation.27 | convolution fusion | flops 68288512 | bytes 1703948 | tf_op jit(solution)/shard_map/dot_general | solution.py:55
  50.0 1.1 %collective-permute-done.20 = bf16[64,512]{1,0:T(8,128)(2,1)S(1)} collective-permute-done((bf16[64,512]{1,0:T(8,128)(2,1)S(1)}, bf16[64,512]{1,0:T(8,128)(2,1)S(1)}, u32[]{:S(2)}, u32[]{:S(2)}) %collective-permute-start.20) | collective-permute-done | bytes 65568 | tf_op jit(solution)/shard_map/ppermute | solution.py:32
  51.1 0.7 %fusion.19 = f32[64,512]{1,0:T(8,128)} fusion(bf16[64,512]{1,0:T(8,128)(2,1)S(1)} %collective-permute-done.20, f32[4,64,512]{2,1,0:T(8,128)S(1)} %bitcast.124, s32[]{:T(128)S(6)} %select_n.277, bf16[128,512]{1,0:T(8,128)(2,1)S(1)} %collective-permute-done.19), kind=kLoop, calls=%fused_computation.39 | loop fusion | flops 131072 | bytes 393220 | tf_op jit(solution)/shard_map/add | solution.py:45
  (55 shorter events, 3.9 us)
Async XLA Ops:
  0.6 11.7 %copy-start = (bf16[1024,1024]{1,0:T(8,128)(2,1)S(1)}, bf16[1024,1024]{1,0:T(8,128)(2,1)}, u32[]{:S(2)}) copy-start(bf16[1024,1024]{1,0:T(8,128)(2,1)} %param.8) | copy-start | bytes 6291460
  0.6 11.7 %copy-start.2 = (bf16[128,1024]{1,0:T(8,128)(2,1)S(1)}, bf16[128,1024]{1,0:T(8,128)(2,1)}, u32[]{:S(2)}) copy-start(bf16[128,1024]{1,0:T(8,128)(2,1)} %param.9) | copy-start | bytes 786436
  1.7 19.1 %collective-permute-start.2 = (bf16[128,512]{1,0:T(8,128)(2,1)S(1)}, bf16[128,512]{1,0:T(8,128)(2,1)S(1)}, u32[]{:S(2)}, u32[]{:S(2)}) collective-permute-start(bf16[128,512]{1,0:T(8,128)(2,1)S(1)} %dynamic-slice_maximum_fusion), channel_id=1, source_target_pairs={{0,24},{2,26},{4,28},{6,30},{8,16},{10,18},{12,20},{14,22},{16,8},... | collective-permute-start | bytes 393224 | tf_op jit(solution)/shard_map/ppermute | solution.py:32
  6.9 14.6 %collective-permute-start.1 = (bf16[128,512]{1,0:T(8,128)(2,1)S(1)}, bf16[128,512]{1,0:T(8,128)(2,1)S(1)}, u32[]{:S(2)}, u32[]{:S(2)}) collective-permute-start(bf16[128,512]{1,0:T(8,128)(2,1)S(1)} %dynamic-slice_maximum_fusion), channel_id=1, source_target_pairs={{0,16},{2,18},{4,20},{6,22},{8,24},{10,26},{12,28},{14,30},{16,0},... | collective-permute-start | bytes 393224 | tf_op jit(solution)/shard_map/ppermute | solution.py:32
  8.7 5.3 %collective-permute-start.5 = (bf16[2,128,128]{2,1,0:T(8,128)(2,1)S(1)}, bf16[2,128,128]{2,1,0:T(8,128)(2,1)S(1)}, u32[]{:S(2)}, u32[]{:S(2)}) collective-permute-start(bf16[2,128,128]{2,1,0:T(8,128)(2,1)S(1)} %get-tuple-element.31), channel_id=1, source_target_pairs={{0,6},{2,4},{4,2},{6,0},{8,14},{10,12},{12,10},{14,8},{16,22},{18,... | collective-permute-start | bytes 196616 | tf_op jit(solution)/shard_map/ppermute | solution.py:28
  11.2 4.3 %collective-permute-start.4 = (bf16[2,128,128]{2,1,0:T(8,128)(2,1)S(1)}, bf16[2,128,128]{2,1,0:T(8,128)(2,1)S(1)}, u32[]{:S(2)}, u32[]{:S(2)}) collective-permute-start(bf16[2,128,128]{2,1,0:T(8,128)(2,1)S(1)} %get-tuple-element.32), channel_id=1, source_target_pairs={{0,4},{2,6},{4,0},{6,2},{8,12},{10,14},{12,8},{14,10},{16,20},{18,... | collective-permute-start | bytes 196616 | tf_op jit(solution)/shard_map/ppermute | solution.py:28
  11.8 5.6 %collective-permute-start.3 = (bf16[2,128,128]{2,1,0:T(8,128)(2,1)S(1)}, bf16[2,128,128]{2,1,0:T(8,128)(2,1)S(1)}, u32[]{:S(2)}, u32[]{:S(2)}) collective-permute-start(bf16[2,128,128]{2,1,0:T(8,128)(2,1)S(1)} %get-tuple-element.33), channel_id=1, source_target_pairs={{0,2},{2,0},{4,6},{6,4},{8,10},{10,8},{12,14},{14,12},{16,18},{18,... | collective-permute-start | bytes 196616 | tf_op jit(solution)/shard_map/ppermute | solution.py:28
  14.1 7.4 %collective-permute-start = (bf16[128,512]{1,0:T(8,128)(2,1)S(1)}, bf16[128,512]{1,0:T(8,128)(2,1)S(1)}, u32[]{:S(2)}, u32[]{:S(2)}) collective-permute-start(bf16[128,512]{1,0:T(8,128)(2,1)S(1)} %dynamic-slice_maximum_fusion), channel_id=1, source_target_pairs={{0,8},{2,10},{4,12},{6,14},{8,0},{10,2},{12,4},{14,6},{16,24},{18,... | collective-permute-start | bytes 393224 | tf_op jit(solution)/shard_map/ppermute | solution.py:32
  15.5 9.1 %collective-permute-start.14 = (bf16[128,512]{1,0:T(8,128)(2,1)S(1)}, bf16[128,512]{1,0:T(8,128)(2,1)S(1)}, u32[]{:S(2)}, u32[]{:S(2)}) collective-permute-start(bf16[128,512]{1,0:T(8,128)(2,1)S(1)} %constant_dynamic-slice_fusion), channel_id=1, source_target_pairs={{0,6},{2,4},{4,2},{6,0},{8,14},{10,12},{12,10},{14,8},{16,22},{18,... | collective-permute-start | bytes 393224 | tf_op jit(solution)/shard_map/ppermute | solution.py:28
  17.3 8.6 %collective-permute-start.13 = (bf16[128,512]{1,0:T(8,128)(2,1)S(1)}, bf16[128,512]{1,0:T(8,128)(2,1)S(1)}, u32[]{:S(2)}, u32[]{:S(2)}) collective-permute-start(bf16[128,512]{1,0:T(8,128)(2,1)S(1)} %constant_dynamic-slice_fusion), channel_id=1, source_target_pairs={{0,4},{2,6},{4,0},{6,2},{8,12},{10,14},{12,8},{14,10},{16,20},{18,... | collective-permute-start | bytes 393224 | tf_op jit(solution)/shard_map/ppermute | solution.py:28
  20.9 6.1 %collective-permute-start.12 = (bf16[128,512]{1,0:T(8,128)(2,1)S(1)}, bf16[128,512]{1,0:T(8,128)(2,1)S(1)}, u32[]{:S(2)}, u32[]{:S(2)}) collective-permute-start(bf16[128,512]{1,0:T(8,128)(2,1)S(1)} %constant_dynamic-slice_fusion), channel_id=1, source_target_pairs={{0,2},{2,0},{4,6},{6,4},{8,10},{10,8},{12,14},{14,12},{16,18},{18,... | collective-permute-start | bytes 393224 | tf_op jit(solution)/shard_map/ppermute | solution.py:28
  22.1 9.3 %collective-permute-start.7 = (bf16[128,512]{1,0:T(8,128)(2,1)S(1)}, bf16[128,512]{1,0:T(8,128)(2,1)S(1)}, u32[]{:S(2)}, u32[]{:S(2)}) collective-permute-start(bf16[128,512]{1,0:T(8,128)(2,1)S(1)} %pad_maximum_fusion.3), channel_id=1, source_target_pairs={{0,4},{2,6},{4,0},{6,2},{8,12},{10,14},{12,8},{14,10},{16,20},{18,... | collective-permute-start | bytes 393224 | tf_op jit(solution)/shard_map/ppermute | solution.py:28
  23.7 8.0 %collective-permute-start.6 = (bf16[128,512]{1,0:T(8,128)(2,1)S(1)}, bf16[128,512]{1,0:T(8,128)(2,1)S(1)}, u32[]{:S(2)}, u32[]{:S(2)}) collective-permute-start(bf16[128,512]{1,0:T(8,128)(2,1)S(1)} %pad_maximum_fusion.2), channel_id=1, source_target_pairs={{0,2},{2,0},{4,6},{6,4},{8,10},{10,8},{12,14},{14,12},{16,18},{18,... | collective-permute-start | bytes 393224 | tf_op jit(solution)/shard_map/ppermute | solution.py:28
  24.7 7.7 %collective-permute-start.8 = (bf16[128,512]{1,0:T(8,128)(2,1)S(1)}, bf16[128,512]{1,0:T(8,128)(2,1)S(1)}, u32[]{:S(2)}, u32[]{:S(2)}) collective-permute-start(bf16[128,512]{1,0:T(8,128)(2,1)S(1)} %pad_maximum_fusion.4), channel_id=1, source_target_pairs={{0,6},{2,4},{4,2},{6,0},{8,14},{10,12},{12,10},{14,8},{16,22},{18,... | collective-permute-start | bytes 393224 | tf_op jit(solution)/shard_map/ppermute | solution.py:28
  27.5 10.1 %collective-permute-start.15 = (bf16[512,128]{1,0:T(8,128)(2,1)S(1)}, bf16[512,128]{1,0:T(8,128)(2,1)S(1)}, u32[]{:S(2)}, u32[]{:S(2)}) collective-permute-start(bf16[512,128]{1,0:T(8,128)(2,1)S(1)} %get-tuple-element.8), channel_id=1, source_target_pairs={{0,8},{2,10},{4,12},{6,14},{8,0},{10,2},{12,4},{14,6},{16,24},{18,... | collective-permute-start | bytes 393224 | tf_op jit(solution)/shard_map/ppermute | solution.py:32
  28.6 10.5 %collective-permute-start.17 = (bf16[512,128]{1,0:T(8,128)(2,1)S(1)}, bf16[512,128]{1,0:T(8,128)(2,1)S(1)}, u32[]{:S(2)}, u32[]{:S(2)}) collective-permute-start(bf16[512,128]{1,0:T(8,128)(2,1)S(1)} %get-tuple-element.9), channel_id=1, source_target_pairs={{0,24},{2,26},{4,28},{6,30},{8,16},{10,18},{12,20},{14,22},{16,8},... | collective-permute-start | bytes 393224 | tf_op jit(solution)/shard_map/ppermute | solution.py:32
  31.4 10.9 %collective-permute-start.16 = (bf16[512,128]{1,0:T(8,128)(2,1)S(1)}, bf16[512,128]{1,0:T(8,128)(2,1)S(1)}, u32[]{:S(2)}, u32[]{:S(2)}) collective-permute-start(bf16[512,128]{1,0:T(8,128)(2,1)S(1)} %get-tuple-element.10), channel_id=1, source_target_pairs={{0,16},{2,18},{4,20},{6,22},{8,24},{10,26},{12,28},{14,30},{16,0},... | collective-permute-start | bytes 393224 | tf_op jit(solution)/shard_map/ppermute | solution.py:32
  34.8 14.0 %copy-start.1 = (bf16[128,1024]{1,0:T(8,128)(2,1)S(1)}, bf16[128,1024]{1,0:T(8,128)(2,1)}, u32[]{:S(2)}) copy-start(bf16[128,1024]{1,0:T(8,128)(2,1)} %param.5) | copy-start | bytes 786436
  35.2 8.8 %collective-permute-start.19 = (bf16[128,512]{1,0:T(8,128)(2,1)S(1)}, bf16[128,512]{1,0:T(8,128)(2,1)S(1)}, u32[]{:S(2)}, u32[]{:S(2)}) collective-permute-start(bf16[128,512]{1,0:T(8,128)(2,1)S(1)} %pad_maximum_fusion.5), channel_id=1, source_target_pairs={{0,8},{2,10},{4,12},{6,14},{8,0},{10,2},{12,4},{14,6},{16,24},{18,... | collective-permute-start | bytes 393224 | tf_op jit(solution)/shard_map/ppermute | solution.py:32
  36.5 7.5 %collective-permute-start.9 = (bf16[128,512]{1,0:T(8,128)(2,1)S(1)}, bf16[128,512]{1,0:T(8,128)(2,1)S(1)}, u32[]{:S(2)}, u32[]{:S(2)}) collective-permute-start(bf16[128,512]{1,0:T(8,128)(2,1)S(1)} %get-tuple-element.5), channel_id=1, source_target_pairs={{0,2},{2,0},{4,6},{6,4},{8,10},{10,8},{12,14},{14,12},{16,18},{18,... | collective-permute-start | bytes 393224 | tf_op jit(solution)/shard_map/ppermute | solution.py:28
  37.7 7.4 %collective-permute-start.11 = (bf16[128,512]{1,0:T(8,128)(2,1)S(1)}, bf16[128,512]{1,0:T(8,128)(2,1)S(1)}, u32[]{:S(2)}, u32[]{:S(2)}) collective-permute-start(bf16[128,512]{1,0:T(8,128)(2,1)S(1)} %get-tuple-element.6), channel_id=1, source_target_pairs={{0,6},{2,4},{4,2},{6,0},{8,14},{10,12},{12,10},{14,8},{16,22},{18,... | collective-permute-start | bytes 393224 | tf_op jit(solution)/shard_map/ppermute | solution.py:28
  42.8 5.3 %collective-permute-start.18 = (bf16[128,512]{1,0:T(8,128)(2,1)S(1)}, bf16[128,512]{1,0:T(8,128)(2,1)S(1)}, u32[]{:S(2)}, u32[]{:S(2)}) collective-permute-start(bf16[128,512]{1,0:T(8,128)(2,1)S(1)} %convolution_convert_fusion.2), channel_id=1, source_target_pairs={{0,1},{1,0},{2,3},{3,2},{4,5},{5,4},{6,7},{7,6},{8,9},{9,8},{10,11... | collective-permute-start | bytes 393224 | tf_op jit(solution)/shard_map/ppermute | solution.py:52
  42.9 5.9 %collective-permute-start.10 = (bf16[128,512]{1,0:T(8,128)(2,1)S(1)}, bf16[128,512]{1,0:T(8,128)(2,1)S(1)}, u32[]{:S(2)}, u32[]{:S(2)}) collective-permute-start(bf16[128,512]{1,0:T(8,128)(2,1)S(1)} %get-tuple-element.7), channel_id=1, source_target_pairs={{0,4},{2,6},{4,0},{6,2},{8,12},{10,14},{12,8},{14,10},{16,20},{18,... | collective-permute-start | bytes 393224 | tf_op jit(solution)/shard_map/ppermute | solution.py:28
  45.1 6.0 %collective-permute-start.20 = (bf16[64,512]{1,0:T(8,128)(2,1)S(1)}, bf16[64,512]{1,0:T(8,128)(2,1)S(1)}, u32[]{:S(2)}, u32[]{:S(2)}) collective-permute-start(bf16[64,512]{1,0:T(8,128)(2,1)S(1)} %fusion.23), channel_id=1, source_target_pairs={{0,16},{2,18},{4,20},{6,22},{8,24},{10,26},{12,28},{14,30},{16,0},... | collective-permute-start | bytes 196616 | tf_op jit(solution)/shard_map/ppermute | solution.py:32

commit v34 on v33

--- a/solution.py
+++ b/solution.py
@@ -145,7 +145,7 @@
     pre_part = columns_of(hidden_pre, rep_pos)
     grad_pre = jnp.where(pre_part > 0, grad_in, 0.0).astype(bf16)
     out_part = sum(part.astype(jnp.float32) for part in out_got)
-    out_part = after(out_part, grad_pre).astype(bf16)
+    out_part = after(out_part, lax.optimization_barrier(grad_pre)).astype(bf16)
     return (out_part, grad_weight, grad_pre)
 
 

time: 52 us -> 58.7 us (1.13)
  waiting for transfers between devices: 10.5 us -> 18.5 us
  starting transfers between devices: 28.7 us -> 27.3 us
  other arithmetic: 3.11 us -> 3.87 us
  matrix products: 3.15 us -> 2.43 us
    ppermute x8, waiting for transfers between devices: 4.35 us -> 10.6 us  [along_outer(): return lax.ppermute(value, 'blk', pairs) if turn else value]
    ppermute x12, waiting for transfers between devices: 6.11 us -> 7.87 us  [along_inner(): return lax.ppermute(value, 'blk', pairs) if turn else value]
    ppermute x8, starting transfers between devices: 14.2 us -> 12.9 us  [along_outer(): return lax.ppermute(value, 'blk', pairs) if turn else value]
    convert_element_type x0 -> x1, other arithmetic: none -> 0.75 us  [shards(): out_part = after(out_part, lax.optimization_barrier(grad_pre)).astype(bf16)]
    dot_general x6, matrix products: 3.15 us -> 2.43 us  [dot(): lax.dot_general(lhs, rhs, (dims, ((), ())), preferred_element_type=jnp.fl...]
  transfers between devices with their start and end apart: 21 -> 21, of which waited for: 8 -> 10; matrix products, arithmetic and copies ran while one was open for 11% -> 9% of each run, Pallas kernels for 0% -> 0%
where the time goes in v34:
time: 58.7 us; the launch traced here: 58.4 us
  starting transfers between devices  27.3 us (47%)
  waiting for transfers between devices  18.5 us (32%)
  blocking collectives  4.18 us (7%)
  other arithmetic  3.87 us (7%)
  matrix products  2.43 us (4%)
  local copies, waits for them, and re-layouts  1.25 us (2%)
  between operations  0.94 us (2%)
    ppermute x12, starting transfers between devices, along_inner(): return lax.ppermute(value, 'blk', pairs) if turn else value  14.3 us
    ppermute x8, starting transfers between devices, along_outer(): return lax.ppermute(value, 'blk', pairs) if turn else value  12.9 us
    ppermute x8, waiting for transfers between devices, along_outer(): return lax.ppermute(value, 'blk', pairs) if turn else value  10.6 us
    ppermute x12, waiting for transfers between devices, along_inner(): return lax.ppermute(value, 'blk', pairs) if turn else value  7.87 us
    dot_general x6, matrix products, dot(): lax.dot_general(lhs, rhs, (dims, ((), ())), preferred_element_type=jnp.fl...  2.43 us
    all_gather x1, blocking collectives, shards(): everyone = lax.all_gather(jnp.concatenate(arrived, 0), 'rep', axis=0)  2.18 us
    all_gather x1, blocking collectives, shards(): lax.all_gather(mixed_cols.astype(bf16), 'rep', axis=0, tiled=True)  1.99 us
  transfers between devices with their start and end apart: 21, of which 10 were waited for; matrix products, arithmetic and copies ran while one was open for 9% of the time, Pallas kernels for 0%

profile of v34, /device:TPU:0, one launch (start us, length us, event | category | flops | bytes accessed | tf_op | source)
XLA Modules:
  0.0 58.4 jit_solution(9762881428670389932)
XLA Ops:
  0.7 1.1 %dynamic-slice_maximum_fusion = bf16[128,512]{1,0:T(8,128)(2,1)S(1)} fusion(bf16[128,1024]{1,0:T(8,128)(2,1)} %param.5, s32[]{:T(128)S(6)} %select_n.214), kind=kLoop, calls=%fused_computation.42 | loop fusion | flops 262144 | bytes 262148 | tf_op jit(solution)/shard_map/max | solution.py:69
  1.7 5.1 %collective-permute-start.2 = (bf16[128,512]{1,0:T(8,128)(2,1)S(1)}, bf16[128,512]{1,0:T(8,128)(2,1)S(1)}, u32[]{:S(2)}, u32[]{:S(2)}) collective-permute-start(bf16[128,512]{1,0:T(8,128)(2,1)S(1)} %dynamic-slice_maximum_fusion), channel_id=1, source_target_pairs={{0,24},{2,26},{4,28},{6,30},{8,16},{10,18},{12,20},{14,22},{16,8},... | collective-permute-start | bytes 393224 | tf_op jit(solution)/shard_map/ppermute | solution.py:32
  6.9 0.7 %add_bitcast_fusion = s32[8]{0:T(128)S(1)} fusion(s32[1,8]{1,0:T(1,128)} %param.7, s32[]{:T(128)S(6)} %shift_right_arithmetic.54, s32[]{:T(128)S(6)} %and.60), kind=kLoop, calls=%fused_computation.92 | loop fusion | flops 56 | bytes 72 | tf_op jit(solution)/shard_map/eq | solution.py:75
  7.6 0.9 %slice_bitcast_fusion.9 = (bf16[128,128]{1,0:T(8,128)(2,1)S(1)}, bf16[128,128]{1,0:T(8,128)(2,1)S(1)}, bf16[128,128]{1,0:T(8,128)(2,1)S(1)}, bf16[128,128]{1,0:T...) fusion(bf16[1,8,128,128]{3,2,1,0:T(8,128)(2,1)} %param.6), kind=kLoop, calls=%fused_computation.73 | loop fusion | bytes 524288 | tf_op jit(solution)/shard_map/jit(_where)/broadcast_in_dim | solution.py:78
  8.7 2.5 %collective-permute-start.5 = (bf16[2,128,128]{2,1,0:T(8,128)(2,1)S(1)}, bf16[2,128,128]{2,1,0:T(8,128)(2,1)S(1)}, u32[]{:S(2)}, u32[]{:S(2)}) collective-permute-start(bf16[2,128,128]{2,1,0:T(8,128)(2,1)S(1)} %get-tuple-element.31), channel_id=1, source_target_pairs={{0,6},{2,4},{4,2},{6,0},{8,14},{10,12},{12,10},{14,8},{16,22},{18,... | collective-permute-start | bytes 196616 | tf_op jit(solution)/shard_map/ppermute | solution.py:28
  11.8 0.5 collective-permute-start.3
  12.4 1.7 %collective-permute-done.5 = bf16[2,128,128]{2,1,0:T(8,128)(2,1)S(1)} collective-permute-done((bf16[2,128,128]{2,1,0:T(8,128)(2,1)S(1)}, bf16[2,128,128]{2,1,0:T(8,128)(2,1)S(1)}, u32[]{:S(2)}, u32[]{:S(2)}) %collective-permute-start.5) | collective-permute-done | bytes 65568 | tf_op jit(solution)/shard_map/ppermute | solution.py:28
  14.1 0.6 %collective-permute-start = (bf16[128,512]{1,0:T(8,128)(2,1)S(1)}, bf16[128,512]{1,0:T(8,128)(2,1)S(1)}, u32[]{:S(2)}, u32[]{:S(2)}) collective-permute-start(bf16[128,512]{1,0:T(8,128)(2,1)S(1)} %dynamic-slice_maximum_fusion), channel_id=1, source_target_pairs={{0,8},{2,10},{4,12},{6,14},{8,0},{10,2},{12,4},{14,6},{16,24},{18,... | collective-permute-start | bytes 393224 | tf_op jit(solution)/shard_map/ppermute | solution.py:32
  14.7 0.8 %collective-permute-done.4 = bf16[2,128,128]{2,1,0:T(8,128)(2,1)S(1)} collective-permute-done((bf16[2,128,128]{2,1,0:T(8,128)(2,1)S(1)}, bf16[2,128,128]{2,1,0:T(8,128)(2,1)S(1)}, u32[]{:S(2)}, u32[]{:S(2)}) %collective-permute-start.4) | collective-permute-done | bytes 65568 | tf_op jit(solution)/shard_map/ppermute | solution.py:28
  15.5 1.8 %collective-permute-start.14 = (bf16[128,512]{1,0:T(8,128)(2,1)S(1)}, bf16[128,512]{1,0:T(8,128)(2,1)S(1)}, u32[]{:S(2)}, u32[]{:S(2)}) collective-permute-start(bf16[128,512]{1,0:T(8,128)(2,1)S(1)} %constant_dynamic-slice_fusion), channel_id=1, source_target_pairs={{0,6},{2,4},{4,2},{6,0},{8,14},{10,12},{12,10},{14,8},{16,22},{18,... | collective-permute-start | bytes 393224 | tf_op jit(solution)/shard_map/ppermute | solution.py:28
  17.3 1.1 %collective-permute-start.13 = (bf16[128,512]{1,0:T(8,128)(2,1)S(1)}, bf16[128,512]{1,0:T(8,128)(2,1)S(1)}, u32[]{:S(2)}, u32[]{:S(2)}) collective-permute-start(bf16[128,512]{1,0:T(8,128)(2,1)S(1)} %constant_dynamic-slice_fusion), channel_id=1, source_target_pairs={{0,4},{2,6},{4,0},{6,2},{8,12},{10,14},{12,8},{14,10},{16,20},{18,... | collective-permute-start | bytes 393224 | tf_op jit(solution)/shard_map/ppermute | solution.py:28
  18.5 2.2 %all-gather = bf16[16,128,128]{2,1,0:T(8,128)(2,1)S(1)} all-gather(bf16[8,128,128]{2,1,0:T(8,128)(2,1)S(1)} %pad_maximum_fusion.1), channel_id=2, replica_groups=mesh['blk'=16,'rep'=2] {'rep'}, dimensions={0}, use_global_device_ids=true | all-gather | bytes 786432 | tf_op jit(solution)/shard_map/all_gather | solution.py:82
  20.9 0.6 %collective-permute-start.12 = (bf16[128,512]{1,0:T(8,128)(2,1)S(1)}, bf16[128,512]{1,0:T(8,128)(2,1)S(1)}, u32[]{:S(2)}, u32[]{:S(2)}) collective-permute-start(bf16[128,512]{1,0:T(8,128)(2,1)S(1)} %constant_dynamic-slice_fusion), channel_id=1, source_target_pairs={{0,2},{2,0},{4,6},{6,4},{8,10},{10,8},{12,14},{14,12},{16,18},{18,... | collective-permute-start | bytes 393224 | tf_op jit(solution)/shard_map/ppermute | solution.py:28
  22.1 1.5 %collective-permute-start.7 = (bf16[128,512]{1,0:T(8,128)(2,1)S(1)}, bf16[128,512]{1,0:T(8,128)(2,1)S(1)}, u32[]{:S(2)}, u32[]{:S(2)}) collective-permute-start(bf16[128,512]{1,0:T(8,128)(2,1)S(1)} %pad_maximum_fusion.3), channel_id=1, source_target_pairs={{0,4},{2,6},{4,0},{6,2},{8,12},{10,14},{12,8},{14,10},{16,20},{18,... | collective-permute-start | bytes 393224 | tf_op jit(solution)/shard_map/ppermute | solution.py:28
  23.7 1.0 %collective-permute-start.6 = (bf16[128,512]{1,0:T(8,128)(2,1)S(1)}, bf16[128,512]{1,0:T(8,128)(2,1)S(1)}, u32[]{:S(2)}, u32[]{:S(2)}) collective-permute-start(bf16[128,512]{1,0:T(8,128)(2,1)S(1)} %pad_maximum_fusion.2), channel_id=1, source_target_pairs={{0,2},{2,0},{4,6},{6,4},{8,10},{10,8},{12,14},{14,12},{16,18},{18,... | collective-permute-start | bytes 393224 | tf_op jit(solution)/shard_map/ppermute | solution.py:28
  24.7 1.2 %collective-permute-start.8 = (bf16[128,512]{1,0:T(8,128)(2,1)S(1)}, bf16[128,512]{1,0:T(8,128)(2,1)S(1)}, u32[]{:S(2)}, u32[]{:S(2)}) collective-permute-start(bf16[128,512]{1,0:T(8,128)(2,1)S(1)} %pad_maximum_fusion.4), channel_id=1, source_target_pairs={{0,6},{2,4},{4,2},{6,0},{8,14},{10,12},{12,10},{14,8},{16,22},{18,... | collective-permute-start | bytes 393224 | tf_op jit(solution)/shard_map/ppermute | solution.py:28
  25.9 1.1 %collective-permute-done.12 = bf16[128,512]{1,0:T(8,128)(2,1)S(1)} collective-permute-done((bf16[128,512]{1,0:T(8,128)(2,1)S(1)}, bf16[128,512]{1,0:T(8,128)(2,1)S(1)}, u32[]{:S(2)}, u32[]{:S(2)}) %collective-permute-start.12) | collective-permute-done | bytes 131104 | tf_op jit(solution)/shard_map/ppermute | solution.py:28
  27.5 1.0 %collective-permute-start.15 = (bf16[512,128]{1,0:T(8,128)(2,1)S(1)}, bf16[512,128]{1,0:T(8,128)(2,1)S(1)}, u32[]{:S(2)}, u32[]{:S(2)}) collective-permute-start(bf16[512,128]{1,0:T(8,128)(2,1)S(1)} %get-tuple-element.8), channel_id=1, source_target_pairs={{0,8},{2,10},{4,12},{6,14},{8,0},{10,2},{12,4},{14,6},{16,24},{18,... | collective-permute-start | bytes 393224 | tf_op jit(solution)/shard_map/ppermute | solution.py:32
  28.6 2.8 %collective-permute-start.17 = (bf16[512,128]{1,0:T(8,128)(2,1)S(1)}, bf16[512,128]{1,0:T(8,128)(2,1)S(1)}, u32[]{:S(2)}, u32[]{:S(2)}) collective-permute-start(bf16[512,128]{1,0:T(8,128)(2,1)S(1)} %get-tuple-element.9), channel_id=1, source_target_pairs={{0,24},{2,26},{4,28},{6,30},{8,16},{10,18},{12,20},{14,22},{16,8},... | collective-permute-start | bytes 393224 | tf_op jit(solution)/shard_map/ppermute | solution.py:32
  31.6 0.8 %collective-permute-done.8 = bf16[128,512]{1,0:T(8,128)(2,1)S(1)} collective-permute-done((bf16[128,512]{1,0:T(8,128)(2,1)S(1)}, bf16[128,512]{1,0:T(8,128)(2,1)S(1)}, u32[]{:S(2)}, u32[]{:S(2)}) %collective-permute-start.8) | collective-permute-done | bytes 131104 | tf_op jit(solution)/shard_map/ppermute | solution.py:28
  32.5 2.0 %all_gather.11 = bf16[256,512]{1,0:T(8,128)(2,1)S(1)} all-gather(bf16[128,512]{1,0:T(8,128)(2,1)S(1)} %fusion.16), channel_id=1, replica_groups=mesh['blk'=16,'rep'=2] {'rep'}, dimensions={0}, use_global_device_ids=true | all-gather | bytes 393216 | tf_op jit(solution)/shard_map/all_gather | solution.py:115
  35.2 2.6 %collective-permute-done.17 = bf16[512,128]{1,0:T(8,128)(2,1)S(1)} collective-permute-done((bf16[512,128]{1,0:T(8,128)(2,1)S(1)}, bf16[512,128]{1,0:T(8,128)(2,1)S(1)}, u32[]{:S(2)}, u32[]{:S(2)}) %collective-permute-start.17) | collective-permute-done | bytes 131104 | tf_op jit(solution)/shard_map/ppermute | solution.py:32
  37.8 4.4 %collective-permute-done.16 = bf16[512,128]{1,0:T(8,128)(2,1)S(1)} collective-permute-done((bf16[512,128]{1,0:T(8,128)(2,1)S(1)}, bf16[512,128]{1,0:T(8,128)(2,1)S(1)}, u32[]{:S(2)}, u32[]{:S(2)}) %collective-permute-start.16) | collective-permute-done | bytes 131104 | tf_op jit(solution)/shard_map/ppermute | solution.py:32
  43.0 1.0 %collective-permute-start.9 = (bf16[128,512]{1,0:T(8,128)(2,1)S(1)}, bf16[128,512]{1,0:T(8,128)(2,1)S(1)}, u32[]{:S(2)}, u32[]{:S(2)}) collective-permute-start(bf16[128,512]{1,0:T(8,128)(2,1)S(1)} %get-tuple-element.5), channel_id=1, source_target_pairs={{0,2},{2,0},{4,6},{6,4},{8,10},{10,8},{12,14},{14,12},{16,18},{18,... | collective-permute-start | bytes 393224 | tf_op jit(solution)/shard_map/ppermute | solution.py:28
  43.9 1.6 %collective-permute-start.11 = (bf16[128,512]{1,0:T(8,128)(2,1)S(1)}, bf16[128,512]{1,0:T(8,128)(2,1)S(1)}, u32[]{:S(2)}, u32[]{:S(2)}) collective-permute-start(bf16[128,512]{1,0:T(8,128)(2,1)S(1)} %get-tuple-element.6), channel_id=1, source_target_pairs={{0,6},{2,4},{4,2},{6,0},{8,14},{10,12},{12,10},{14,8},{16,22},{18,... | collective-permute-start | bytes 393224 | tf_op jit(solution)/shard_map/ppermute | solution.py:28
  45.5 1.0 %collective-permute-start.10 = (bf16[128,512]{1,0:T(8,128)(2,1)S(1)}, bf16[128,512]{1,0:T(8,128)(2,1)S(1)}, u32[]{:S(2)}, u32[]{:S(2)}) collective-permute-start(bf16[128,512]{1,0:T(8,128)(2,1)S(1)} %get-tuple-element.7), channel_id=1, source_target_pairs={{0,4},{2,6},{4,0},{6,2},{8,12},{10,14},{12,8},{14,10},{16,20},{18,... | collective-permute-start | bytes 393224 | tf_op jit(solution)/shard_map/ppermute | solution.py:28
  47.0 1.8 %collective-permute-done.19 = bf16[128,512]{1,0:T(8,128)(2,1)S(1)} collective-permute-done((bf16[128,512]{1,0:T(8,128)(2,1)S(1)}, bf16[128,512]{1,0:T(8,128)(2,1)S(1)}, u32[]{:S(2)}, u32[]{:S(2)}) %collective-permute-start.19) | collective-permute-done | bytes 131104 | tf_op jit(solution)/shard_map/ppermute | solution.py:32
  49.3 3.0 %collective-permute-done.11 = bf16[128,512]{1,0:T(8,128)(2,1)S(1)} collective-permute-done((bf16[128,512]{1,0:T(8,128)(2,1)S(1)}, bf16[128,512]{1,0:T(8,128)(2,1)S(1)}, u32[]{:S(2)}, u32[]{:S(2)}) %collective-permute-start.11) | collective-permute-done | bytes 131104 | tf_op jit(solution)/shard_map/ppermute | solution.py:28
  52.3 3.0 %collective-permute-start.20 = (bf16[64,512]{1,0:T(8,128)(2,1)S(1)}, bf16[64,512]{1,0:T(8,128)(2,1)S(1)}, u32[]{:S(2)}, u32[]{:S(2)}) collective-permute-start(bf16[64,512]{1,0:T(8,128)(2,1)S(1)} %fusion.23), channel_id=1, source_target_pairs={{0,16},{2,18},{4,20},{6,22},{8,24},{10,26},{12,28},{14,30},{16,0},... | collective-permute-start | bytes 196616 | tf_op jit(solution)/shard_map/ppermute | solution.py:32
  55.3 0.8 %add_convert_fusion = bf16[128,512]{1,0:T(8,128)(2,1)} fusion(bf16[128,512]{1,0:T(8,128)(2,1)S(1)} %select_convert_fusion, bf16[128,512]{1,0:T(8,128)(2,1)S(1)} %collective-permute-done.11, bf16[128,512]{1,0:T(8,128)(2,1)S(1)} %collective-permute-done.10, bf16[128,512]{1,0:T(8,128)(2,1)S(1)} %collective-permute-done.9, ...), kind=kLoop, calls=%fused_computation.27 | loop fusion | flops 720896 | bytes 786432 | tf_op jit(solution)/shard_map/convert_element_type | solution.py:148
  56.1 1.7 %collective-permute-done.20 = bf16[64,512]{1,0:T(8,128)(2,1)S(1)} collective-permute-done((bf16[64,512]{1,0:T(8,128)(2,1)S(1)}, bf16[64,512]{1,0:T(8,128)(2,1)S(1)}, u32[]{:S(2)}, u32[]{:S(2)}) %collective-permute-start.20) | collective-permute-done | bytes 65568 | tf_op jit(solution)/shard_map/ppermute | solution.py:32
  57.8 0.7 %fusion.19 = f32[64,512]{1,0:T(8,128)} fusion(bf16[64,512]{1,0:T(8,128)(2,1)S(1)} %collective-permute-done.20, f32[4,64,512]{2,1,0:T(8,128)S(1)} %bitcast.122, s32[]{:T(128)S(6)} %select_n.277, bf16[128,512]{1,0:T(8,128)(2,1)S(1)} %collective-permute-done.19), kind=kLoop, calls=%fused_computation.39 | loop fusion | flops 131072 | bytes 393220 | tf_op jit(solution)/shard_map/add | solution.py:45
  (58 shorter events, 4.9 us)
Async XLA Ops:
  0.6 11.7 %copy-start = (bf16[1024,1024]{1,0:T(8,128)(2,1)S(1)}, bf16[1024,1024]{1,0:T(8,128)(2,1)}, u32[]{:S(2)}) copy-start(bf16[1024,1024]{1,0:T(8,128)(2,1)} %param.8) | copy-start | bytes 6291460
  0.6 11.7 %copy-start.3 = (bf16[128,1024]{1,0:T(8,128)(2,1)S(1)}, bf16[128,1024]{1,0:T(8,128)(2,1)}, u32[]{:S(2)}) copy-start(bf16[128,1024]{1,0:T(8,128)(2,1)} %param.9) | copy-start | bytes 786436
  1.7 19.1 %collective-permute-start.2 = (bf16[128,512]{1,0:T(8,128)(2,1)S(1)}, bf16[128,512]{1,0:T(8,128)(2,1)S(1)}, u32[]{:S(2)}, u32[]{:S(2)}) collective-permute-start(bf16[128,512]{1,0:T(8,128)(2,1)S(1)} %dynamic-slice_maximum_fusion), channel_id=1, source_target_pairs={{0,24},{2,26},{4,28},{6,30},{8,16},{10,18},{12,20},{14,22},{16,8},... | collective-permute-start | bytes 393224 | tf_op jit(solution)/shard_map/ppermute | solution.py:32
  6.9 14.6 %collective-permute-start.1 = (bf16[128,512]{1,0:T(8,128)(2,1)S(1)}, bf16[128,512]{1,0:T(8,128)(2,1)S(1)}, u32[]{:S(2)}, u32[]{:S(2)}) collective-permute-start(bf16[128,512]{1,0:T(8,128)(2,1)S(1)} %dynamic-slice_maximum_fusion), channel_id=1, source_target_pairs={{0,16},{2,18},{4,20},{6,22},{8,24},{10,26},{12,28},{14,30},{16,0},... | collective-permute-start | bytes 393224 | tf_op jit(solution)/shard_map/ppermute | solution.py:32
  8.7 5.3 %collective-permute-start.5 = (bf16[2,128,128]{2,1,0:T(8,128)(2,1)S(1)}, bf16[2,128,128]{2,1,0:T(8,128)(2,1)S(1)}, u32[]{:S(2)}, u32[]{:S(2)}) collective-permute-start(bf16[2,128,128]{2,1,0:T(8,128)(2,1)S(1)} %get-tuple-element.31), channel_id=1, source_target_pairs={{0,6},{2,4},{4,2},{6,0},{8,14},{10,12},{12,10},{14,8},{16,22},{18,... | collective-permute-start | bytes 196616 | tf_op jit(solution)/shard_map/ppermute | solution.py:28
  11.2 4.3 %collective-permute-start.4 = (bf16[2,128,128]{2,1,0:T(8,128)(2,1)S(1)}, bf16[2,128,128]{2,1,0:T(8,128)(2,1)S(1)}, u32[]{:S(2)}, u32[]{:S(2)}) collective-permute-start(bf16[2,128,128]{2,1,0:T(8,128)(2,1)S(1)} %get-tuple-element.32), channel_id=1, source_target_pairs={{0,4},{2,6},{4,0},{6,2},{8,12},{10,14},{12,8},{14,10},{16,20},{18,... | collective-permute-start | bytes 196616 | tf_op jit(solution)/shard_map/ppermute | solution.py:28
  11.8 5.6 %collective-permute-start.3 = (bf16[2,128,128]{2,1,0:T(8,128)(2,1)S(1)}, bf16[2,128,128]{2,1,0:T(8,128)(2,1)S(1)}, u32[]{:S(2)}, u32[]{:S(2)}) collective-permute-start(bf16[2,128,128]{2,1,0:T(8,128)(2,1)S(1)} %get-tuple-element.33), channel_id=1, source_target_pairs={{0,2},{2,0},{4,6},{6,4},{8,10},{10,8},{12,14},{14,12},{16,18},{18,... | collective-permute-start | bytes 196616 | tf_op jit(solution)/shard_map/ppermute | solution.py:28
  14.1 7.4 %collective-permute-start = (bf16[128,512]{1,0:T(8,128)(2,1)S(1)}, bf16[128,512]{1,0:T(8,128)(2,1)S(1)}, u32[]{:S(2)}, u32[]{:S(2)}) collective-permute-start(bf16[128,512]{1,0:T(8,128)(2,1)S(1)} %dynamic-slice_maximum_fusion), channel_id=1, source_target_pairs={{0,8},{2,10},{4,12},{6,14},{8,0},{10,2},{12,4},{14,6},{16,24},{18,... | collective-permute-start | bytes 393224 | tf_op jit(solution)/shard_map/ppermute | solution.py:32
  15.5 9.2 %collective-permute-start.14 = (bf16[128,512]{1,0:T(8,128)(2,1)S(1)}, bf16[128,512]{1,0:T(8,128)(2,1)S(1)}, u32[]{:S(2)}, u32[]{:S(2)}) collective-permute-start(bf16[128,512]{1,0:T(8,128)(2,1)S(1)} %constant_dynamic-slice_fusion), channel_id=1, source_target_pairs={{0,6},{2,4},{4,2},{6,0},{8,14},{10,12},{12,10},{14,8},{16,22},{18,... | collective-permute-start | bytes 393224 | tf_op jit(solution)/shard_map/ppermute | solution.py:28
  17.3 8.6 %collective-permute-start.13 = (bf16[128,512]{1,0:T(8,128)(2,1)S(1)}, bf16[128,512]{1,0:T(8,128)(2,1)S(1)}, u32[]{:S(2)}, u32[]{:S(2)}) collective-permute-start(bf16[128,512]{1,0:T(8,128)(2,1)S(1)} %constant_dynamic-slice_fusion), channel_id=1, source_target_pairs={{0,4},{2,6},{4,0},{6,2},{8,12},{10,14},{12,8},{14,10},{16,20},{18,... | collective-permute-start | bytes 393224 | tf_op jit(solution)/shard_map/ppermute | solution.py:28
  20.9 6.1 %collective-permute-start.12 = (bf16[128,512]{1,0:T(8,128)(2,1)S(1)}, bf16[128,512]{1,0:T(8,128)(2,1)S(1)}, u32[]{:S(2)}, u32[]{:S(2)}) collective-permute-start(bf16[128,512]{1,0:T(8,128)(2,1)S(1)} %constant_dynamic-slice_fusion), channel_id=1, source_target_pairs={{0,2},{2,0},{4,6},{6,4},{8,10},{10,8},{12,14},{14,12},{16,18},{18,... | collective-permute-start | bytes 393224 | tf_op jit(solution)/shard_map/ppermute | solution.py:28
  22.1 9.2 %collective-permute-start.7 = (bf16[128,512]{1,0:T(8,128)(2,1)S(1)}, bf16[128,512]{1,0:T(8,128)(2,1)S(1)}, u32[]{:S(2)}, u32[]{:S(2)}) collective-permute-start(bf16[128,512]{1,0:T(8,128)(2,1)S(1)} %pad_maximum_fusion.3), channel_id=1, source_target_pairs={{0,4},{2,6},{4,0},{6,2},{8,12},{10,14},{12,8},{14,10},{16,20},{18,... | collective-permute-start | bytes 393224 | tf_op jit(solution)/shard_map/ppermute | solution.py:28
  23.7 7.9 %collective-permute-start.6 = (bf16[128,512]{1,0:T(8,128)(2,1)S(1)}, bf16[128,512]{1,0:T(8,128)(2,1)S(1)}, u32[]{:S(2)}, u32[]{:S(2)}) collective-permute-start(bf16[128,512]{1,0:T(8,128)(2,1)S(1)} %pad_maximum_fusion.2), channel_id=1, source_target_pairs={{0,2},{2,0},{4,6},{6,4},{8,10},{10,8},{12,14},{14,12},{16,18},{18,... | collective-permute-start | bytes 393224 | tf_op jit(solution)/shard_map/ppermute | solution.py:28
  24.7 7.7 %collective-permute-start.8 = (bf16[128,512]{1,0:T(8,128)(2,1)S(1)}, bf16[128,512]{1,0:T(8,128)(2,1)S(1)}, u32[]{:S(2)}, u32[]{:S(2)}) collective-permute-start(bf16[128,512]{1,0:T(8,128)(2,1)S(1)} %pad_maximum_fusion.4), channel_id=1, source_target_pairs={{0,6},{2,4},{4,2},{6,0},{8,14},{10,12},{12,10},{14,8},{16,22},{18,... | collective-permute-start | bytes 393224 | tf_op jit(solution)/shard_map/ppermute | solution.py:28
  27.5 7.6 %collective-permute-start.15 = (bf16[512,128]{1,0:T(8,128)(2,1)S(1)}, bf16[512,128]{1,0:T(8,128)(2,1)S(1)}, u32[]{:S(2)}, u32[]{:S(2)}) collective-permute-start(bf16[512,128]{1,0:T(8,128)(2,1)S(1)} %get-tuple-element.8), channel_id=1, source_target_pairs={{0,8},{2,10},{4,12},{6,14},{8,0},{10,2},{12,4},{14,6},{16,24},{18,... | collective-permute-start | bytes 393224 | tf_op jit(solution)/shard_map/ppermute | solution.py:32
  28.6 9.3 %collective-permute-start.17 = (bf16[512,128]{1,0:T(8,128)(2,1)S(1)}, bf16[512,128]{1,0:T(8,128)(2,1)S(1)}, u32[]{:S(2)}, u32[]{:S(2)}) collective-permute-start(bf16[512,128]{1,0:T(8,128)(2,1)S(1)} %get-tuple-element.9), channel_id=1, source_target_pairs={{0,24},{2,26},{4,28},{6,30},{8,16},{10,18},{12,20},{14,22},{16,8},... | collective-permute-start | bytes 393224 | tf_op jit(solution)/shard_map/ppermute | solution.py:32
  31.4 10.8 %collective-permute-start.16 = (bf16[512,128]{1,0:T(8,128)(2,1)S(1)}, bf16[512,128]{1,0:T(8,128)(2,1)S(1)}, u32[]{:S(2)}, u32[]{:S(2)}) collective-permute-start(bf16[512,128]{1,0:T(8,128)(2,1)S(1)} %get-tuple-element.10), channel_id=1, source_target_pairs={{0,16},{2,18},{4,20},{6,22},{8,24},{10,26},{12,28},{14,30},{16,0},... | collective-permute-start | bytes 393224 | tf_op jit(solution)/shard_map/ppermute | solution.py:32
  35.1 11.4 %copy-start.2 = (bf16[128,1024]{1,0:T(8,128)(2,1)S(1)}, bf16[128,1024]{1,0:T(8,128)(2,1)}, u32[]{:S(2)}) copy-start(bf16[128,1024]{1,0:T(8,128)(2,1)} %param.5) | copy-start | bytes 786436
  42.7 3.8 %collective-permute-start.18 = (bf16[128,512]{1,0:T(8,128)(2,1)S(1)}, bf16[128,512]{1,0:T(8,128)(2,1)S(1)}, u32[]{:S(2)}, u32[]{:S(2)}) collective-permute-start(bf16[128,512]{1,0:T(8,128)(2,1)S(1)} %convolution_convert_fusion.2), channel_id=1, source_target_pairs={{0,1},{1,0},{2,3},{3,2},{4,5},{5,4},{6,7},{7,6},{8,9},{9,8},{10,11... | collective-permute-start | bytes 393224 | tf_op jit(solution)/shard_map/ppermute | solution.py:52
  42.9 6.0 %collective-permute-start.19 = (bf16[128,512]{1,0:T(8,128)(2,1)S(1)}, bf16[128,512]{1,0:T(8,128)(2,1)S(1)}, u32[]{:S(2)}, u32[]{:S(2)}) collective-permute-start(bf16[128,512]{1,0:T(8,128)(2,1)S(1)} %pad_maximum_fusion.5), channel_id=1, source_target_pairs={{0,8},{2,10},{4,12},{6,14},{8,0},{10,2},{12,4},{14,6},{16,24},{18,... | collective-permute-start | bytes 393224 | tf_op jit(solution)/shard_map/ppermute | solution.py:32
  43.0 6.4 %collective-permute-start.9 = (bf16[128,512]{1,0:T(8,128)(2,1)S(1)}, bf16[128,512]{1,0:T(8,128)(2,1)S(1)}, u32[]{:S(2)}, u32[]{:S(2)}) collective-permute-start(bf16[128,512]{1,0:T(8,128)(2,1)S(1)} %get-tuple-element.5), channel_id=1, source_target_pairs={{0,2},{2,0},{4,6},{6,4},{8,10},{10,8},{12,14},{14,12},{16,18},{18,... | collective-permute-start | bytes 393224 | tf_op jit(solution)/shard_map/ppermute | solution.py:28
  43.9 8.3 %collective-permute-start.11 = (bf16[128,512]{1,0:T(8,128)(2,1)S(1)}, bf16[128,512]{1,0:T(8,128)(2,1)S(1)}, u32[]{:S(2)}, u32[]{:S(2)}) collective-permute-start(bf16[128,512]{1,0:T(8,128)(2,1)S(1)} %get-tuple-element.6), channel_id=1, source_target_pairs={{0,6},{2,4},{4,2},{6,0},{8,14},{10,12},{12,10},{14,8},{16,22},{18,... | collective-permute-start | bytes 393224 | tf_op jit(solution)/shard_map/ppermute | solution.py:28
  45.5 9.8 %collective-permute-start.10 = (bf16[128,512]{1,0:T(8,128)(2,1)S(1)}, bf16[128,512]{1,0:T(8,128)(2,1)S(1)}, u32[]{:S(2)}, u32[]{:S(2)}) collective-permute-start(bf16[128,512]{1,0:T(8,128)(2,1)S(1)} %get-tuple-element.7), channel_id=1, source_target_pairs={{0,4},{2,6},{4,0},{6,2},{8,12},{10,14},{12,8},{14,10},{16,20},{18,... | collective-permute-start | bytes 393224 | tf_op jit(solution)/shard_map/ppermute | solution.py:28
  47.0 11.5 %copy-start.1 = (bf16[128,512]{1,0:T(8,128)(2,1)}, bf16[128,512]{1,0:T(8,128)(2,1)S(1)}, u32[]{:S(2)}) copy-start(bf16[128,512]{1,0:T(8,128)(2,1)S(1)} %select_convert_fusion) | copy-start | bytes 393220
  52.3 5.4 %collective-permute-start.20 = (bf16[64,512]{1,0:T(8,128)(2,1)S(1)}, bf16[64,512]{1,0:T(8,128)(2,1)S(1)}, u32[]{:S(2)}, u32[]{:S(2)}) collective-permute-start(bf16[64,512]{1,0:T(8,128)(2,1)S(1)} %fusion.23), channel_id=1, source_target_pairs={{0,16},{2,18},{4,20},{6,22},{8,24},{10,26},{12,28},{14,30},{16,0},... | collective-permute-start | bytes 196616 | tf_op jit(solution)/shard_map/ppermute | solution.py:32

commit v35 on v33

--- a/solution.py
+++ b/solution.py
@@ -126,7 +126,7 @@
     grad_weight = halved(
         [lax.dynamic_index_in_dim(by_outer, outer_pos ^ t, 0, keepdims=False) for t in turns],
         along_outer,
-        out_got[1::2],
+        out_got[2:],
     )
 
     back = after(back, weight_part).astype(bf16)

time: 52 us -> 52.8 us (1.015)
  waiting for transfers between devices: 10.5 us -> 11.5 us
    ppermute x8, waiting for transfers between devices: 4.35 us -> 5.04 us  [along_outer(): return lax.ppermute(value, 'blk', pairs) if turn else value]
where the time goes in v35:
time: 52.8 us; the launch traced here: 52.6 us
  starting transfers between devices  28.5 us (54%)
  waiting for transfers between devices  11.5 us (22%)
  blocking collectives  4.18 us (8%)
  matrix products  3.15 us (6%)
  other arithmetic  3.11 us (6%)
  local copies, waits for them, and re-layouts  1.23 us (2%)
  between operations  0.92 us (2%)
    ppermute x12, starting transfers between devices, along_inner(): return lax.ppermute(value, 'blk', pairs) if turn else value  14.4 us
    ppermute x8, starting transfers between devices, along_outer(): return lax.ppermute(value, 'blk', pairs) if turn else value  14 us
    ppermute x12, waiting for transfers between devices, along_inner(): return lax.ppermute(value, 'blk', pairs) if turn else value  6.46 us
    ppermute x8, waiting for transfers between devices, along_outer(): return lax.ppermute(value, 'blk', pairs) if turn else value  5.04 us
    dot_general x6, matrix products, dot(): lax.dot_general(lhs, rhs, (dims, ((), ())), preferred_element_type=jnp.fl...  3.15 us
    all_gather x1, blocking collectives, shards(): everyone = lax.all_gather(jnp.concatenate(arrived, 0), 'rep', axis=0)  2.18 us
    all_gather x1, blocking collectives, shards(): lax.all_gather(mixed_cols.astype(bf16), 'rep', axis=0, tiled=True)  1.99 us
    max x1, other arithmetic, shards(): hidden_part = jnp.maximum(columns_of(hidden_pre, rep_pos), 0)  1.08 us
  transfers between devices with their start and end apart: 21, of which 8 were waited for; matrix products, arithmetic and copies ran while one was open for 11% of the time, Pallas kernels for 0%

profile of v35, /device:TPU:0, one launch (start us, length us, event | category | flops | bytes accessed | tf_op | source)
XLA Modules:
  0.0 52.6 jit_solution(8510335361841177468)
XLA Ops:
  0.7 1.1 %dynamic-slice_maximum_fusion = bf16[128,512]{1,0:T(8,128)(2,1)S(1)} fusion(bf16[128,1024]{1,0:T(8,128)(2,1)} %param.5, s32[]{:T(128)S(6)} %select_n.214), kind=kLoop, calls=%fused_computation.42 | loop fusion | flops 262144 | bytes 262148 | tf_op jit(solution)/shard_map/max | solution.py:69
  1.7 5.1 %collective-permute-start.2 = (bf16[128,512]{1,0:T(8,128)(2,1)S(1)}, bf16[128,512]{1,0:T(8,128)(2,1)S(1)}, u32[]{:S(2)}, u32[]{:S(2)}) collective-permute-start(bf16[128,512]{1,0:T(8,128)(2,1)S(1)} %dynamic-slice_maximum_fusion), channel_id=1, source_target_pairs={{0,24},{2,26},{4,28},{6,30},{8,16},{10,18},{12,20},{14,22},{16,8},... | collective-permute-start | bytes 393224 | tf_op jit(solution)/shard_map/ppermute | solution.py:32
  6.9 0.7 %add_bitcast_fusion = s32[8]{0:T(128)S(1)} fusion(s32[1,8]{1,0:T(1,128)} %param.7, s32[]{:T(128)S(6)} %shift_right_arithmetic.54, s32[]{:T(128)S(6)} %and.60), kind=kLoop, calls=%fused_computation.92 | loop fusion | flops 56 | bytes 72 | tf_op jit(solution)/shard_map/eq | solution.py:75
  7.6 0.9 %slice_bitcast_fusion.9 = (bf16[128,128]{1,0:T(8,128)(2,1)S(1)}, bf16[128,128]{1,0:T(8,128)(2,1)S(1)}, bf16[128,128]{1,0:T(8,128)(2,1)S(1)}, bf16[128,128]{1,0:T...) fusion(bf16[1,8,128,128]{3,2,1,0:T(8,128)(2,1)} %param.6), kind=kLoop, calls=%fused_computation.73 | loop fusion | bytes 524288 | tf_op jit(solution)/shard_map/jit(_where)/broadcast_in_dim | solution.py:78
  8.7 2.5 %collective-permute-start.5 = (bf16[2,128,128]{2,1,0:T(8,128)(2,1)S(1)}, bf16[2,128,128]{2,1,0:T(8,128)(2,1)S(1)}, u32[]{:S(2)}, u32[]{:S(2)}) collective-permute-start(bf16[2,128,128]{2,1,0:T(8,128)(2,1)S(1)} %get-tuple-element.31), channel_id=1, source_target_pairs={{0,6},{2,4},{4,2},{6,0},{8,14},{10,12},{12,10},{14,8},{16,22},{18,... | collective-permute-start | bytes 196616 | tf_op jit(solution)/shard_map/ppermute | solution.py:28
  11.2 0.5 collective-permute-start.4
  11.8 0.5 %collective-permute-start.3 = (bf16[2,128,128]{2,1,0:T(8,128)(2,1)S(1)}, bf16[2,128,128]{2,1,0:T(8,128)(2,1)S(1)}, u32[]{:S(2)}, u32[]{:S(2)}) collective-permute-start(bf16[2,128,128]{2,1,0:T(8,128)(2,1)S(1)} %get-tuple-element.33), channel_id=1, source_target_pairs={{0,2},{2,0},{4,6},{6,4},{8,10},{10,8},{12,14},{14,12},{16,18},{18,... | collective-permute-start | bytes 196616 | tf_op jit(solution)/shard_map/ppermute | solution.py:28
  12.4 1.7 %collective-permute-done.5 = bf16[2,128,128]{2,1,0:T(8,128)(2,1)S(1)} collective-permute-done((bf16[2,128,128]{2,1,0:T(8,128)(2,1)S(1)}, bf16[2,128,128]{2,1,0:T(8,128)(2,1)S(1)}, u32[]{:S(2)}, u32[]{:S(2)}) %collective-permute-start.5) | collective-permute-done | bytes 65568 | tf_op jit(solution)/shard_map/ppermute | solution.py:28
  14.1 0.6 %collective-permute-start = (bf16[128,512]{1,0:T(8,128)(2,1)S(1)}, bf16[128,512]{1,0:T(8,128)(2,1)S(1)}, u32[]{:S(2)}, u32[]{:S(2)}) collective-permute-start(bf16[128,512]{1,0:T(8,128)(2,1)S(1)} %dynamic-slice_maximum_fusion), channel_id=1, source_target_pairs={{0,8},{2,10},{4,12},{6,14},{8,0},{10,2},{12,4},{14,6},{16,24},{18,... | collective-permute-start | bytes 393224 | tf_op jit(solution)/shard_map/ppermute | solution.py:32
  14.7 0.8 %collective-permute-done.4 = bf16[2,128,128]{2,1,0:T(8,128)(2,1)S(1)} collective-permute-done((bf16[2,128,128]{2,1,0:T(8,128)(2,1)S(1)}, bf16[2,128,128]{2,1,0:T(8,128)(2,1)S(1)}, u32[]{:S(2)}, u32[]{:S(2)}) %collective-permute-start.4) | collective-permute-done | bytes 65568 | tf_op jit(solution)/shard_map/ppermute | solution.py:28
  15.5 1.8 %collective-permute-start.14 = (bf16[128,512]{1,0:T(8,128)(2,1)S(1)}, bf16[128,512]{1,0:T(8,128)(2,1)S(1)}, u32[]{:S(2)}, u32[]{:S(2)}) collective-permute-start(bf16[128,512]{1,0:T(8,128)(2,1)S(1)} %constant_dynamic-slice_fusion), channel_id=1, source_target_pairs={{0,6},{2,4},{4,2},{6,0},{8,14},{10,12},{12,10},{14,8},{16,22},{18,... | collective-permute-start | bytes 393224 | tf_op jit(solution)/shard_map/ppermute | solution.py:28
  17.3 1.1 %collective-permute-start.13 = (bf16[128,512]{1,0:T(8,128)(2,1)S(1)}, bf16[128,512]{1,0:T(8,128)(2,1)S(1)}, u32[]{:S(2)}, u32[]{:S(2)}) collective-permute-start(bf16[128,512]{1,0:T(8,128)(2,1)S(1)} %constant_dynamic-slice_fusion), channel_id=1, source_target_pairs={{0,4},{2,6},{4,0},{6,2},{8,12},{10,14},{12,8},{14,10},{16,20},{18,... | collective-permute-start | bytes 393224 | tf_op jit(solution)/shard_map/ppermute | solution.py:28
  18.5 2.2 %all-gather = bf16[16,128,128]{2,1,0:T(8,128)(2,1)S(1)} all-gather(bf16[8,128,128]{2,1,0:T(8,128)(2,1)S(1)} %pad_maximum_fusion.1), channel_id=2, replica_groups=mesh['blk'=16,'rep'=2] {'rep'}, dimensions={0}, use_global_device_ids=true | all-gather | bytes 786432 | tf_op jit(solution)/shard_map/all_gather | solution.py:82
  20.9 0.6 %collective-permute-start.12 = (bf16[128,512]{1,0:T(8,128)(2,1)S(1)}, bf16[128,512]{1,0:T(8,128)(2,1)S(1)}, u32[]{:S(2)}, u32[]{:S(2)}) collective-permute-start(bf16[128,512]{1,0:T(8,128)(2,1)S(1)} %constant_dynamic-slice_fusion), channel_id=1, source_target_pairs={{0,2},{2,0},{4,6},{6,4},{8,10},{10,8},{12,14},{14,12},{16,18},{18,... | collective-permute-start | bytes 393224 | tf_op jit(solution)/shard_map/ppermute | solution.py:28
  22.1 1.5 %collective-permute-start.7 = (bf16[128,512]{1,0:T(8,128)(2,1)S(1)}, bf16[128,512]{1,0:T(8,128)(2,1)S(1)}, u32[]{:S(2)}, u32[]{:S(2)}) collective-permute-start(bf16[128,512]{1,0:T(8,128)(2,1)S(1)} %pad_maximum_fusion.3), channel_id=1, source_target_pairs={{0,4},{2,6},{4,0},{6,2},{8,12},{10,14},{12,8},{14,10},{16,20},{18,... | collective-permute-start | bytes 393224 | tf_op jit(solution)/shard_map/ppermute | solution.py:28
  23.7 1.0 %collective-permute-start.6 = (bf16[128,512]{1,0:T(8,128)(2,1)S(1)}, bf16[128,512]{1,0:T(8,128)(2,1)S(1)}, u32[]{:S(2)}, u32[]{:S(2)}) collective-permute-start(bf16[128,512]{1,0:T(8,128)(2,1)S(1)} %pad_maximum_fusion.2), channel_id=1, source_target_pairs={{0,2},{2,0},{4,6},{6,4},{8,10},{10,8},{12,14},{14,12},{16,18},{18,... | collective-permute-start | bytes 393224 | tf_op jit(solution)/shard_map/ppermute | solution.py:28
  24.7 1.2 %collective-permute-start.8 = (bf16[128,512]{1,0:T(8,128)(2,1)S(1)}, bf16[128,512]{1,0:T(8,128)(2,1)S(1)}, u32[]{:S(2)}, u32[]{:S(2)}) collective-permute-start(bf16[128,512]{1,0:T(8,128)(2,1)S(1)} %pad_maximum_fusion.4), channel_id=1, source_target_pairs={{0,6},{2,4},{4,2},{6,0},{8,14},{10,12},{12,10},{14,8},{16,22},{18,... | collective-permute-start | bytes 393224 | tf_op jit(solution)/shard_map/ppermute | solution.py:28
  25.9 1.1 %collective-permute-done.12 = bf16[128,512]{1,0:T(8,128)(2,1)S(1)} collective-permute-done((bf16[128,512]{1,0:T(8,128)(2,1)S(1)}, bf16[128,512]{1,0:T(8,128)(2,1)S(1)}, u32[]{:S(2)}, u32[]{:S(2)}) %collective-permute-start.12) | collective-permute-done | bytes 131104 | tf_op jit(solution)/shard_map/ppermute | solution.py:28
  27.5 1.1 %collective-permute-start.15 = (bf16[512,128]{1,0:T(8,128)(2,1)S(1)}, bf16[512,128]{1,0:T(8,128)(2,1)S(1)}, u32[]{:S(2)}, u32[]{:S(2)}) collective-permute-start(bf16[512,128]{1,0:T(8,128)(2,1)S(1)} %get-tuple-element.8), channel_id=1, source_target_pairs={{0,8},{2,10},{4,12},{6,14},{8,0},{10,2},{12,4},{14,6},{16,24},{18,... | collective-permute-start | bytes 393224 | tf_op jit(solution)/shard_map/ppermute | solution.py:32
  28.6 2.8 %collective-permute-start.17 = (bf16[512,128]{1,0:T(8,128)(2,1)S(1)}, bf16[512,128]{1,0:T(8,128)(2,1)S(1)}, u32[]{:S(2)}, u32[]{:S(2)}) collective-permute-start(bf16[512,128]{1,0:T(8,128)(2,1)S(1)} %get-tuple-element.9), channel_id=1, source_target_pairs={{0,24},{2,26},{4,28},{6,30},{8,16},{10,18},{12,20},{14,22},{16,8},... | collective-permute-start | bytes 393224 | tf_op jit(solution)/shard_map/ppermute | solution.py:32
  31.6 0.8 %collective-permute-done.8 = bf16[128,512]{1,0:T(8,128)(2,1)S(1)} collective-permute-done((bf16[128,512]{1,0:T(8,128)(2,1)S(1)}, bf16[128,512]{1,0:T(8,128)(2,1)S(1)}, u32[]{:S(2)}, u32[]{:S(2)}) %collective-permute-start.8) | collective-permute-done | bytes 131104 | tf_op jit(solution)/shard_map/ppermute | solution.py:28
  32.5 2.0 %all_gather.11 = bf16[256,512]{1,0:T(8,128)(2,1)S(1)} all-gather(bf16[128,512]{1,0:T(8,128)(2,1)S(1)} %fusion.16), channel_id=1, replica_groups=mesh['blk'=16,'rep'=2] {'rep'}, dimensions={0}, use_global_device_ids=true | all-gather | bytes 393216 | tf_op jit(solution)/shard_map/all_gather | solution.py:115
  35.2 1.3 %collective-permute-start.19 = (bf16[128,512]{1,0:T(8,128)(2,1)S(1)}, bf16[128,512]{1,0:T(8,128)(2,1)S(1)}, u32[]{:S(2)}, u32[]{:S(2)}) collective-permute-start(bf16[128,512]{1,0:T(8,128)(2,1)S(1)} %pad_maximum_fusion.5), channel_id=1, source_target_pairs={{0,8},{2,10},{4,12},{6,14},{8,0},{10,2},{12,4},{14,6},{16,24},{18,... | collective-permute-start | bytes 393224 | tf_op jit(solution)/shard_map/ppermute | solution.py:32
  36.5 1.1 %collective-permute-start.11 = (bf16[128,512]{1,0:T(8,128)(2,1)S(1)}, bf16[128,512]{1,0:T(8,128)(2,1)S(1)}, u32[]{:S(2)}, u32[]{:S(2)}) collective-permute-start(bf16[128,512]{1,0:T(8,128)(2,1)S(1)} %get-tuple-element.6), channel_id=1, source_target_pairs={{0,6},{2,4},{4,2},{6,0},{8,14},{10,12},{12,10},{14,8},{16,22},{18,... | collective-permute-start | bytes 393224 | tf_op jit(solution)/shard_map/ppermute | solution.py:28
  37.6 1.6 %collective-permute-start.10 = (bf16[128,512]{1,0:T(8,128)(2,1)S(1)}, bf16[128,512]{1,0:T(8,128)(2,1)S(1)}, u32[]{:S(2)}, u32[]{:S(2)}) collective-permute-start(bf16[128,512]{1,0:T(8,128)(2,1)S(1)} %get-tuple-element.7), channel_id=1, source_target_pairs={{0,4},{2,6},{4,0},{6,2},{8,12},{10,14},{12,8},{14,10},{16,20},{18,... | collective-permute-start | bytes 393224 | tf_op jit(solution)/shard_map/ppermute | solution.py:28
  39.2 3.1 %collective-permute-done.16 = bf16[512,128]{1,0:T(8,128)(2,1)S(1)} collective-permute-done((bf16[512,128]{1,0:T(8,128)(2,1)S(1)}, bf16[512,128]{1,0:T(8,128)(2,1)S(1)}, u32[]{:S(2)}, u32[]{:S(2)}) %collective-permute-start.16) | collective-permute-done | bytes 131104 | tf_op jit(solution)/shard_map/ppermute | solution.py:32
  42.9 1.0 %collective-permute-start.9 = (bf16[128,512]{1,0:T(8,128)(2,1)S(1)}, bf16[128,512]{1,0:T(8,128)(2,1)S(1)}, u32[]{:S(2)}, u32[]{:S(2)}) collective-permute-start(bf16[128,512]{1,0:T(8,128)(2,1)S(1)} %get-tuple-element.5), channel_id=1, source_target_pairs={{0,2},{2,0},{4,6},{6,4},{8,10},{10,8},{12,14},{14,12},{16,18},{18,... | collective-permute-start | bytes 393224 | tf_op jit(solution)/shard_map/ppermute | solution.py:28
  43.9 1.6 %collective-permute-done.10 = bf16[128,512]{1,0:T(8,128)(2,1)S(1)} collective-permute-done((bf16[128,512]{1,0:T(8,128)(2,1)S(1)}, bf16[128,512]{1,0:T(8,128)(2,1)S(1)}, u32[]{:S(2)}, u32[]{:S(2)}) %collective-permute-start.10) | collective-permute-done | bytes 131104 | tf_op jit(solution)/shard_map/ppermute | solution.py:28
  45.5 2.8 %collective-permute-start.20 = (bf16[64,512]{1,0:T(8,128)(2,1)S(1)}, bf16[64,512]{1,0:T(8,128)(2,1)S(1)}, u32[]{:S(2)}, u32[]{:S(2)}) collective-permute-start(bf16[64,512]{1,0:T(8,128)(2,1)S(1)} %fusion.23), channel_id=1, source_target_pairs={{0,16},{2,18},{4,20},{6,22},{8,24},{10,26},{12,28},{14,30},{16,0},... | collective-permute-start | bytes 196616 | tf_op jit(solution)/shard_map/ppermute | solution.py:32
  48.8 1.2 %add_convert_fusion = (bf16[128,512]{1,0:T(8,128)(2,1)}, bf16[128,512]{1,0:T(8,128)(2,1)}) fusion(bf16[128,512]{1,0:T(8,128)(2,1)S(1)} %collective-permute-done.11, bf16[128,512]{1,0:T(8,128)(2,1)S(1)} %collective-permute-done.10, bf16[128,512]{1,0:T(8,128)(2,1)S(1)} %collective-permute-done.9, bf16[512,512]{1,0:T(8,128)(2,1)S(1)} %convolution_convert_fusion.1, ...), kind=kOutput, calls=%fused_computation.27 | convolution fusion | flops 68288512 | bytes 1703948 | tf_op jit(solution)/shard_map/dot_general | solution.py:55
  50.0 1.9 %collective-permute-done.20 = bf16[64,512]{1,0:T(8,128)(2,1)S(1)} collective-permute-done((bf16[64,512]{1,0:T(8,128)(2,1)S(1)}, bf16[64,512]{1,0:T(8,128)(2,1)S(1)}, u32[]{:S(2)}, u32[]{:S(2)}) %collective-permute-start.20) | collective-permute-done | bytes 65568 | tf_op jit(solution)/shard_map/ppermute | solution.py:32
  51.9 0.7 %fusion.19 = f32[64,512]{1,0:T(8,128)} fusion(bf16[64,512]{1,0:T(8,128)(2,1)S(1)} %collective-permute-done.20, f32[4,64,512]{2,1,0:T(8,128)S(1)} %bitcast.124, s32[]{:T(128)S(6)} %select_n.277, bf16[128,512]{1,0:T(8,128)(2,1)S(1)} %collective-permute-done.19), kind=kLoop, calls=%fused_computation.39 | loop fusion | flops 131072 | bytes 393220 | tf_op jit(solution)/shard_map/add | solution.py:45
  (55 shorter events, 3.8 us)
Async XLA Ops:
  0.6 11.7 %copy-start = (bf16[1024,1024]{1,0:T(8,128)(2,1)S(1)}, bf16[1024,1024]{1,0:T(8,128)(2,1)}, u32[]{:S(2)}) copy-start(bf16[1024,1024]{1,0:T(8,128)(2,1)} %param.8) | copy-start | bytes 6291460
  0.6 11.7 %copy-start.2 = (bf16[128,1024]{1,0:T(8,128)(2,1)S(1)}, bf16[128,1024]{1,0:T(8,128)(2,1)}, u32[]{:S(2)}) copy-start(bf16[128,1024]{1,0:T(8,128)(2,1)} %param.9) | copy-start | bytes 786436
  1.7 19.1 %collective-permute-start.2 = (bf16[128,512]{1,0:T(8,128)(2,1)S(1)}, bf16[128,512]{1,0:T(8,128)(2,1)S(1)}, u32[]{:S(2)}, u32[]{:S(2)}) collective-permute-start(bf16[128,512]{1,0:T(8,128)(2,1)S(1)} %dynamic-slice_maximum_fusion), channel_id=1, source_target_pairs={{0,24},{2,26},{4,28},{6,30},{8,16},{10,18},{12,20},{14,22},{16,8},... | collective-permute-start | bytes 393224 | tf_op jit(solution)/shard_map/ppermute | solution.py:32
  6.9 14.6 %collective-permute-start.1 = (bf16[128,512]{1,0:T(8,128)(2,1)S(1)}, bf16[128,512]{1,0:T(8,128)(2,1)S(1)}, u32[]{:S(2)}, u32[]{:S(2)}) collective-permute-start(bf16[128,512]{1,0:T(8,128)(2,1)S(1)} %dynamic-slice_maximum_fusion), channel_id=1, source_target_pairs={{0,16},{2,18},{4,20},{6,22},{8,24},{10,26},{12,28},{14,30},{16,0},... | collective-permute-start | bytes 393224 | tf_op jit(solution)/shard_map/ppermute | solution.py:32
  8.7 5.3 %collective-permute-start.5 = (bf16[2,128,128]{2,1,0:T(8,128)(2,1)S(1)}, bf16[2,128,128]{2,1,0:T(8,128)(2,1)S(1)}, u32[]{:S(2)}, u32[]{:S(2)}) collective-permute-start(bf16[2,128,128]{2,1,0:T(8,128)(2,1)S(1)} %get-tuple-element.31), channel_id=1, source_target_pairs={{0,6},{2,4},{4,2},{6,0},{8,14},{10,12},{12,10},{14,8},{16,22},{18,... | collective-permute-start | bytes 196616 | tf_op jit(solution)/shard_map/ppermute | solution.py:28
  11.2 4.3 %collective-permute-start.4 = (bf16[2,128,128]{2,1,0:T(8,128)(2,1)S(1)}, bf16[2,128,128]{2,1,0:T(8,128)(2,1)S(1)}, u32[]{:S(2)}, u32[]{:S(2)}) collective-permute-start(bf16[2,128,128]{2,1,0:T(8,128)(2,1)S(1)} %get-tuple-element.32), channel_id=1, source_target_pairs={{0,4},{2,6},{4,0},{6,2},{8,12},{10,14},{12,8},{14,10},{16,20},{18,... | collective-permute-start | bytes 196616 | tf_op jit(solution)/shard_map/ppermute | solution.py:28
  11.8 5.6 %collective-permute-start.3 = (bf16[2,128,128]{2,1,0:T(8,128)(2,1)S(1)}, bf16[2,128,128]{2,1,0:T(8,128)(2,1)S(1)}, u32[]{:S(2)}, u32[]{:S(2)}) collective-permute-start(bf16[2,128,128]{2,1,0:T(8,128)(2,1)S(1)} %get-tuple-element.33), channel_id=1, source_target_pairs={{0,2},{2,0},{4,6},{6,4},{8,10},{10,8},{12,14},{14,12},{16,18},{18,... | collective-permute-start | bytes 196616 | tf_op jit(solution)/shard_map/ppermute | solution.py:28
  14.1 7.4 %collective-permute-start = (bf16[128,512]{1,0:T(8,128)(2,1)S(1)}, bf16[128,512]{1,0:T(8,128)(2,1)S(1)}, u32[]{:S(2)}, u32[]{:S(2)}) collective-permute-start(bf16[128,512]{1,0:T(8,128)(2,1)S(1)} %dynamic-slice_maximum_fusion), channel_id=1, source_target_pairs={{0,8},{2,10},{4,12},{6,14},{8,0},{10,2},{12,4},{14,6},{16,24},{18,... | collective-permute-start | bytes 393224 | tf_op jit(solution)/shard_map/ppermute | solution.py:32
  15.5 9.1 %collective-permute-start.14 = (bf16[128,512]{1,0:T(8,128)(2,1)S(1)}, bf16[128,512]{1,0:T(8,128)(2,1)S(1)}, u32[]{:S(2)}, u32[]{:S(2)}) collective-permute-start(bf16[128,512]{1,0:T(8,128)(2,1)S(1)} %constant_dynamic-slice_fusion), channel_id=1, source_target_pairs={{0,6},{2,4},{4,2},{6,0},{8,14},{10,12},{12,10},{14,8},{16,22},{18,... | collective-permute-start | bytes 393224 | tf_op jit(solution)/shard_map/ppermute | solution.py:28
  17.3 8.6 %collective-permute-start.13 = (bf16[128,512]{1,0:T(8,128)(2,1)S(1)}, bf16[128,512]{1,0:T(8,128)(2,1)S(1)}, u32[]{:S(2)}, u32[]{:S(2)}) collective-permute-start(bf16[128,512]{1,0:T(8,128)(2,1)S(1)} %constant_dynamic-slice_fusion), channel_id=1, source_target_pairs={{0,4},{2,6},{4,0},{6,2},{8,12},{10,14},{12,8},{14,10},{16,20},{18,... | collective-permute-start | bytes 393224 | tf_op jit(solution)/shard_map/ppermute | solution.py:28
  20.9 6.1 %collective-permute-start.12 = (bf16[128,512]{1,0:T(8,128)(2,1)S(1)}, bf16[128,512]{1,0:T(8,128)(2,1)S(1)}, u32[]{:S(2)}, u32[]{:S(2)}) collective-permute-start(bf16[128,512]{1,0:T(8,128)(2,1)S(1)} %constant_dynamic-slice_fusion), channel_id=1, source_target_pairs={{0,2},{2,0},{4,6},{6,4},{8,10},{10,8},{12,14},{14,12},{16,18},{18,... | collective-permute-start | bytes 393224 | tf_op jit(solution)/shard_map/ppermute | solution.py:28
  22.1 9.3 %collective-permute-start.7 = (bf16[128,512]{1,0:T(8,128)(2,1)S(1)}, bf16[128,512]{1,0:T(8,128)(2,1)S(1)}, u32[]{:S(2)}, u32[]{:S(2)}) collective-permute-start(bf16[128,512]{1,0:T(8,128)(2,1)S(1)} %pad_maximum_fusion.3), channel_id=1, source_target_pairs={{0,4},{2,6},{4,0},{6,2},{8,12},{10,14},{12,8},{14,10},{16,20},{18,... | collective-permute-start | bytes 393224 | tf_op jit(solution)/shard_map/ppermute | solution.py:28
  23.7 8.0 %collective-permute-start.6 = (bf16[128,512]{1,0:T(8,128)(2,1)S(1)}, bf16[128,512]{1,0:T(8,128)(2,1)S(1)}, u32[]{:S(2)}, u32[]{:S(2)}) collective-permute-start(bf16[128,512]{1,0:T(8,128)(2,1)S(1)} %pad_maximum_fusion.2), channel_id=1, source_target_pairs={{0,2},{2,0},{4,6},{6,4},{8,10},{10,8},{12,14},{14,12},{16,18},{18,... | collective-permute-start | bytes 393224 | tf_op jit(solution)/shard_map/ppermute | solution.py:28
  24.7 7.7 %collective-permute-start.8 = (bf16[128,512]{1,0:T(8,128)(2,1)S(1)}, bf16[128,512]{1,0:T(8,128)(2,1)S(1)}, u32[]{:S(2)}, u32[]{:S(2)}) collective-permute-start(bf16[128,512]{1,0:T(8,128)(2,1)S(1)} %pad_maximum_fusion.4), channel_id=1, source_target_pairs={{0,6},{2,4},{4,2},{6,0},{8,14},{10,12},{12,10},{14,8},{16,22},{18,... | collective-permute-start | bytes 393224 | tf_op jit(solution)/shard_map/ppermute | solution.py:28
  27.5 10.1 %collective-permute-start.15 = (bf16[512,128]{1,0:T(8,128)(2,1)S(1)}, bf16[512,128]{1,0:T(8,128)(2,1)S(1)}, u32[]{:S(2)}, u32[]{:S(2)}) collective-permute-start(bf16[512,128]{1,0:T(8,128)(2,1)S(1)} %get-tuple-element.8), channel_id=1, source_target_pairs={{0,8},{2,10},{4,12},{6,14},{8,0},{10,2},{12,4},{14,6},{16,24},{18,... | collective-permute-start | bytes 393224 | tf_op jit(solution)/shard_map/ppermute | solution.py:32
  28.6 10.6 %collective-permute-start.17 = (bf16[512,128]{1,0:T(8,128)(2,1)S(1)}, bf16[512,128]{1,0:T(8,128)(2,1)S(1)}, u32[]{:S(2)}, u32[]{:S(2)}) collective-permute-start(bf16[512,128]{1,0:T(8,128)(2,1)S(1)} %get-tuple-element.9), channel_id=1, source_target_pairs={{0,24},{2,26},{4,28},{6,30},{8,16},{10,18},{12,20},{14,22},{16,8},... | collective-permute-start | bytes 393224 | tf_op jit(solution)/shard_map/ppermute | solution.py:32
  31.4 10.9 %collective-permute-start.16 = (bf16[512,128]{1,0:T(8,128)(2,1)S(1)}, bf16[512,128]{1,0:T(8,128)(2,1)S(1)}, u32[]{:S(2)}, u32[]{:S(2)}) collective-permute-start(bf16[512,128]{1,0:T(8,128)(2,1)S(1)} %get-tuple-element.10), channel_id=1, source_target_pairs={{0,16},{2,18},{4,20},{6,22},{8,24},{10,26},{12,28},{14,30},{16,0},... | collective-permute-start | bytes 393224 | tf_op jit(solution)/shard_map/ppermute | solution.py:32
  34.8 14.0 %copy-start.1 = (bf16[128,1024]{1,0:T(8,128)(2,1)S(1)}, bf16[128,1024]{1,0:T(8,128)(2,1)}, u32[]{:S(2)}) copy-start(bf16[128,1024]{1,0:T(8,128)(2,1)} %param.5) | copy-start | bytes 786436
  35.2 8.7 %collective-permute-start.19 = (bf16[128,512]{1,0:T(8,128)(2,1)S(1)}, bf16[128,512]{1,0:T(8,128)(2,1)S(1)}, u32[]{:S(2)}, u32[]{:S(2)}) collective-permute-start(bf16[128,512]{1,0:T(8,128)(2,1)S(1)} %pad_maximum_fusion.5), channel_id=1, source_target_pairs={{0,8},{2,10},{4,12},{6,14},{8,0},{10,2},{12,4},{14,6},{16,24},{18,... | collective-permute-start | bytes 393224 | tf_op jit(solution)/shard_map/ppermute | solution.py:32
  36.5 7.4 %collective-permute-start.11 = (bf16[128,512]{1,0:T(8,128)(2,1)S(1)}, bf16[128,512]{1,0:T(8,128)(2,1)S(1)}, u32[]{:S(2)}, u32[]{:S(2)}) collective-permute-start(bf16[128,512]{1,0:T(8,128)(2,1)S(1)} %get-tuple-element.6), channel_id=1, source_target_pairs={{0,6},{2,4},{4,2},{6,0},{8,14},{10,12},{12,10},{14,8},{16,22},{18,... | collective-permute-start | bytes 393224 | tf_op jit(solution)/shard_map/ppermute | solution.py:28
  37.6 7.9 %collective-permute-start.10 = (bf16[128,512]{1,0:T(8,128)(2,1)S(1)}, bf16[128,512]{1,0:T(8,128)(2,1)S(1)}, u32[]{:S(2)}, u32[]{:S(2)}) collective-permute-start(bf16[128,512]{1,0:T(8,128)(2,1)S(1)} %get-tuple-element.7), channel_id=1, source_target_pairs={{0,4},{2,6},{4,0},{6,2},{8,12},{10,14},{12,8},{14,10},{16,20},{18,... | collective-permute-start | bytes 393224 | tf_op jit(solution)/shard_map/ppermute | solution.py:28
  42.8 5.5 %collective-permute-start.18 = (bf16[128,512]{1,0:T(8,128)(2,1)S(1)}, bf16[128,512]{1,0:T(8,128)(2,1)S(1)}, u32[]{:S(2)}, u32[]{:S(2)}) collective-permute-start(bf16[128,512]{1,0:T(8,128)(2,1)S(1)} %convolution_convert_fusion.2), channel_id=1, source_target_pairs={{0,1},{1,0},{2,3},{3,2},{4,5},{5,4},{6,7},{7,6},{8,9},{9,8},{10,11... | collective-permute-start | bytes 393224 | tf_op jit(solution)/shard_map/ppermute | solution.py:52
  42.9 5.9 %collective-permute-start.9 = (bf16[128,512]{1,0:T(8,128)(2,1)S(1)}, bf16[128,512]{1,0:T(8,128)(2,1)S(1)}, u32[]{:S(2)}, u32[]{:S(2)}) collective-permute-start(bf16[128,512]{1,0:T(8,128)(2,1)S(1)} %get-tuple-element.5), channel_id=1, source_target_pairs={{0,2},{2,0},{4,6},{6,4},{8,10},{10,8},{12,14},{14,12},{16,18},{18,... | collective-permute-start | bytes 393224 | tf_op jit(solution)/shard_map/ppermute | solution.py:28
  45.5 6.4 %collective-permute-start.20 = (bf16[64,512]{1,0:T(8,128)(2,1)S(1)}, bf16[64,512]{1,0:T(8,128)(2,1)S(1)}, u32[]{:S(2)}, u32[]{:S(2)}) collective-permute-start(bf16[64,512]{1,0:T(8,128)(2,1)S(1)} %fusion.23), channel_id=1, source_target_pairs={{0,16},{2,18},{4,20},{6,22},{8,24},{10,26},{12,28},{14,30},{16,0},... | collective-permute-start | bytes 196616 | tf_op jit(solution)/shard_map/ppermute | solution.py:32

commit v36 on v33

--- a/solution.py
+++ b/solution.py
@@ -142,8 +142,7 @@
         back_full = lax.all_gather(back, "rep", axis=0, tiled=True)
         w_mine = lax.dynamic_index_in_dim(w_rows, rep_pos, 0, keepdims=False)
         grad_in = dot(back_full, w_mine, ((0,), (1,)))
-    pre_part = columns_of(hidden_pre, rep_pos)
-    grad_pre = jnp.where(pre_part > 0, grad_in, 0.0).astype(bf16)
+    grad_pre = jnp.where(hidden_part > 0, grad_in, 0.0).astype(bf16)
     out_part = sum(part.astype(jnp.float32) for part in out_got)
     out_part = after(out_part, grad_pre).astype(bf16)
     return (out_part, grad_weight, grad_pre)

time: 52 us -> 52 us (level)
  no operation moved by 1% of the time
where the time goes in v36:
time: 52 us; the launch traced here: 51.8 us
  starting transfers between devices  28.7 us (55%)
  waiting for transfers between devices  10.5 us (20%)
  blocking collectives  4.18 us (8%)
  matrix products  3.15 us (6%)
  other arithmetic  3.11 us (6%)
  local copies, waits for them, and re-layouts  1.23 us (2%)
  between operations  0.92 us (2%)
    ppermute x12, starting transfers between devices, along_inner(): return lax.ppermute(value, 'blk', pairs) if turn else value  14.4 us
    ppermute x8, starting transfers between devices, along_outer(): return lax.ppermute(value, 'blk', pairs) if turn else value  14.2 us
    ppermute x12, waiting for transfers between devices, along_inner(): return lax.ppermute(value, 'blk', pairs) if turn else value  6.11 us
    ppermute x8, waiting for transfers between devices, along_outer(): return lax.ppermute(value, 'blk', pairs) if turn else value  4.35 us
    dot_general x6, matrix products, dot(): lax.dot_general(lhs, rhs, (dims, ((), ())), preferred_element_type=jnp.fl...  3.15 us
    all_gather x1, blocking collectives, shards(): everyone = lax.all_gather(jnp.concatenate(arrived, 0), 'rep', axis=0)  2.18 us
    all_gather x1, blocking collectives, shards(): lax.all_gather(mixed_cols.astype(bf16), 'rep', axis=0, tiled=True)  1.99 us
    max x1, other arithmetic, shards(): hidden_part = jnp.maximum(columns_of(hidden_pre, rep_pos), 0)  1.08 us
  transfers between devices with their start and end apart: 21, of which 8 were waited for; matrix products, arithmetic and copies ran while one was open for 11% of the time, Pallas kernels for 0%

profile of v36, /device:TPU:0, one launch (start us, length us, event | category | flops | bytes accessed | tf_op | source)
XLA Modules:
  0.0 51.8 jit_solution(2866357421659179576)
XLA Ops:
  0.7 1.1 %dynamic-slice_maximum_fusion = bf16[128,512]{1,0:T(8,128)(2,1)S(1)} fusion(bf16[128,1024]{1,0:T(8,128)(2,1)} %param.5, s32[]{:T(128)S(6)} %select_n.213), kind=kLoop, calls=%fused_computation.42 | loop fusion | flops 262144 | bytes 262148 | tf_op jit(solution)/shard_map/max | solution.py:69
  1.7 5.1 %collective-permute-start.2 = (bf16[128,512]{1,0:T(8,128)(2,1)S(1)}, bf16[128,512]{1,0:T(8,128)(2,1)S(1)}, u32[]{:S(2)}, u32[]{:S(2)}) collective-permute-start(bf16[128,512]{1,0:T(8,128)(2,1)S(1)} %dynamic-slice_maximum_fusion), channel_id=1, source_target_pairs={{0,24},{2,26},{4,28},{6,30},{8,16},{10,18},{12,20},{14,22},{16,8},... | collective-permute-start | bytes 393224 | tf_op jit(solution)/shard_map/ppermute | solution.py:32
  6.9 0.7 %add_bitcast_fusion = s32[8]{0:T(128)S(1)} fusion(s32[1,8]{1,0:T(1,128)} %param.7, s32[]{:T(128)S(6)} %shift_right_arithmetic.54, s32[]{:T(128)S(6)} %and.60), kind=kLoop, calls=%fused_computation.92 | loop fusion | flops 56 | bytes 72 | tf_op jit(solution)/shard_map/eq | solution.py:75
  7.6 0.9 %slice_bitcast_fusion.9 = (bf16[128,128]{1,0:T(8,128)(2,1)S(1)}, bf16[128,128]{1,0:T(8,128)(2,1)S(1)}, bf16[128,128]{1,0:T(8,128)(2,1)S(1)}, bf16[128,128]{1,0:T...) fusion(bf16[1,8,128,128]{3,2,1,0:T(8,128)(2,1)} %param.6), kind=kLoop, calls=%fused_computation.73 | loop fusion | bytes 524288 | tf_op jit(solution)/shard_map/jit(_where)/broadcast_in_dim | solution.py:78
  8.7 2.5 %collective-permute-start.5 = (bf16[2,128,128]{2,1,0:T(8,128)(2,1)S(1)}, bf16[2,128,128]{2,1,0:T(8,128)(2,1)S(1)}, u32[]{:S(2)}, u32[]{:S(2)}) collective-permute-start(bf16[2,128,128]{2,1,0:T(8,128)(2,1)S(1)} %get-tuple-element.31), channel_id=1, source_target_pairs={{0,6},{2,4},{4,2},{6,0},{8,14},{10,12},{12,10},{14,8},{16,22},{18,... | collective-permute-start | bytes 196616 | tf_op jit(solution)/shard_map/ppermute | solution.py:28
  11.8 0.5 %collective-permute-start.3 = (bf16[2,128,128]{2,1,0:T(8,128)(2,1)S(1)}, bf16[2,128,128]{2,1,0:T(8,128)(2,1)S(1)}, u32[]{:S(2)}, u32[]{:S(2)}) collective-permute-start(bf16[2,128,128]{2,1,0:T(8,128)(2,1)S(1)} %get-tuple-element.33), channel_id=1, source_target_pairs={{0,2},{2,0},{4,6},{6,4},{8,10},{10,8},{12,14},{14,12},{16,18},{18,... | collective-permute-start | bytes 196616 | tf_op jit(solution)/shard_map/ppermute | solution.py:28
  12.4 1.7 %collective-permute-done.5 = bf16[2,128,128]{2,1,0:T(8,128)(2,1)S(1)} collective-permute-done((bf16[2,128,128]{2,1,0:T(8,128)(2,1)S(1)}, bf16[2,128,128]{2,1,0:T(8,128)(2,1)S(1)}, u32[]{:S(2)}, u32[]{:S(2)}) %collective-permute-start.5) | collective-permute-done | bytes 65568 | tf_op jit(solution)/shard_map/ppermute | solution.py:28
  14.1 0.6 %collective-permute-start = (bf16[128,512]{1,0:T(8,128)(2,1)S(1)}, bf16[128,512]{1,0:T(8,128)(2,1)S(1)}, u32[]{:S(2)}, u32[]{:S(2)}) collective-permute-start(bf16[128,512]{1,0:T(8,128)(2,1)S(1)} %dynamic-slice_maximum_fusion), channel_id=1, source_target_pairs={{0,8},{2,10},{4,12},{6,14},{8,0},{10,2},{12,4},{14,6},{16,24},{18,... | collective-permute-start | bytes 393224 | tf_op jit(solution)/shard_map/ppermute | solution.py:32
  14.7 0.8 %collective-permute-done.4 = bf16[2,128,128]{2,1,0:T(8,128)(2,1)S(1)} collective-permute-done((bf16[2,128,128]{2,1,0:T(8,128)(2,1)S(1)}, bf16[2,128,128]{2,1,0:T(8,128)(2,1)S(1)}, u32[]{:S(2)}, u32[]{:S(2)}) %collective-permute-start.4) | collective-permute-done | bytes 65568 | tf_op jit(solution)/shard_map/ppermute | solution.py:28
  15.5 1.8 %collective-permute-start.14 = (bf16[128,512]{1,0:T(8,128)(2,1)S(1)}, bf16[128,512]{1,0:T(8,128)(2,1)S(1)}, u32[]{:S(2)}, u32[]{:S(2)}) collective-permute-start(bf16[128,512]{1,0:T(8,128)(2,1)S(1)} %constant_dynamic-slice_fusion), channel_id=1, source_target_pairs={{0,6},{2,4},{4,2},{6,0},{8,14},{10,12},{12,10},{14,8},{16,22},{18,... | collective-permute-start | bytes 393224 | tf_op jit(solution)/shard_map/ppermute | solution.py:28
  17.3 1.1 %collective-permute-start.13 = (bf16[128,512]{1,0:T(8,128)(2,1)S(1)}, bf16[128,512]{1,0:T(8,128)(2,1)S(1)}, u32[]{:S(2)}, u32[]{:S(2)}) collective-permute-start(bf16[128,512]{1,0:T(8,128)(2,1)S(1)} %constant_dynamic-slice_fusion), channel_id=1, source_target_pairs={{0,4},{2,6},{4,0},{6,2},{8,12},{10,14},{12,8},{14,10},{16,20},{18,... | collective-permute-start | bytes 393224 | tf_op jit(solution)/shard_map/ppermute | solution.py:28
  18.5 2.2 %all-gather = bf16[16,128,128]{2,1,0:T(8,128)(2,1)S(1)} all-gather(bf16[8,128,128]{2,1,0:T(8,128)(2,1)S(1)} %pad_maximum_fusion.1), channel_id=2, replica_groups=mesh['blk'=16,'rep'=2] {'rep'}, dimensions={0}, use_global_device_ids=true | all-gather | bytes 786432 | tf_op jit(solution)/shard_map/all_gather | solution.py:82
  20.9 0.6 %collective-permute-start.12 = (bf16[128,512]{1,0:T(8,128)(2,1)S(1)}, bf16[128,512]{1,0:T(8,128)(2,1)S(1)}, u32[]{:S(2)}, u32[]{:S(2)}) collective-permute-start(bf16[128,512]{1,0:T(8,128)(2,1)S(1)} %constant_dynamic-slice_fusion), channel_id=1, source_target_pairs={{0,2},{2,0},{4,6},{6,4},{8,10},{10,8},{12,14},{14,12},{16,18},{18,... | collective-permute-start | bytes 393224 | tf_op jit(solution)/shard_map/ppermute | solution.py:28
  22.1 1.5 %collective-permute-start.7 = (bf16[128,512]{1,0:T(8,128)(2,1)S(1)}, bf16[128,512]{1,0:T(8,128)(2,1)S(1)}, u32[]{:S(2)}, u32[]{:S(2)}) collective-permute-start(bf16[128,512]{1,0:T(8,128)(2,1)S(1)} %pad_maximum_fusion.3), channel_id=1, source_target_pairs={{0,4},{2,6},{4,0},{6,2},{8,12},{10,14},{12,8},{14,10},{16,20},{18,... | collective-permute-start | bytes 393224 | tf_op jit(solution)/shard_map/ppermute | solution.py:28
  23.7 1.0 %collective-permute-start.6 = (bf16[128,512]{1,0:T(8,128)(2,1)S(1)}, bf16[128,512]{1,0:T(8,128)(2,1)S(1)}, u32[]{:S(2)}, u32[]{:S(2)}) collective-permute-start(bf16[128,512]{1,0:T(8,128)(2,1)S(1)} %pad_maximum_fusion.2), channel_id=1, source_target_pairs={{0,2},{2,0},{4,6},{6,4},{8,10},{10,8},{12,14},{14,12},{16,18},{18,... | collective-permute-start | bytes 393224 | tf_op jit(solution)/shard_map/ppermute | solution.py:28
  24.7 1.2 %collective-permute-start.8 = (bf16[128,512]{1,0:T(8,128)(2,1)S(1)}, bf16[128,512]{1,0:T(8,128)(2,1)S(1)}, u32[]{:S(2)}, u32[]{:S(2)}) collective-permute-start(bf16[128,512]{1,0:T(8,128)(2,1)S(1)} %pad_maximum_fusion.4), channel_id=1, source_target_pairs={{0,6},{2,4},{4,2},{6,0},{8,14},{10,12},{12,10},{14,8},{16,22},{18,... | collective-permute-start | bytes 393224 | tf_op jit(solution)/shard_map/ppermute | solution.py:28
  25.9 1.1 %collective-permute-done.12 = bf16[128,512]{1,0:T(8,128)(2,1)S(1)} collective-permute-done((bf16[128,512]{1,0:T(8,128)(2,1)S(1)}, bf16[128,512]{1,0:T(8,128)(2,1)S(1)}, u32[]{:S(2)}, u32[]{:S(2)}) %collective-permute-start.12) | collective-permute-done | bytes 131104 | tf_op jit(solution)/shard_map/ppermute | solution.py:28
  27.5 1.1 %collective-permute-start.15 = (bf16[512,128]{1,0:T(8,128)(2,1)S(1)}, bf16[512,128]{1,0:T(8,128)(2,1)S(1)}, u32[]{:S(2)}, u32[]{:S(2)}) collective-permute-start(bf16[512,128]{1,0:T(8,128)(2,1)S(1)} %get-tuple-element.8), channel_id=1, source_target_pairs={{0,8},{2,10},{4,12},{6,14},{8,0},{10,2},{12,4},{14,6},{16,24},{18,... | collective-permute-start | bytes 393224 | tf_op jit(solution)/shard_map/ppermute | solution.py:32
  28.6 2.8 %collective-permute-start.17 = (bf16[512,128]{1,0:T(8,128)(2,1)S(1)}, bf16[512,128]{1,0:T(8,128)(2,1)S(1)}, u32[]{:S(2)}, u32[]{:S(2)}) collective-permute-start(bf16[512,128]{1,0:T(8,128)(2,1)S(1)} %get-tuple-element.9), channel_id=1, source_target_pairs={{0,24},{2,26},{4,28},{6,30},{8,16},{10,18},{12,20},{14,22},{16,8},... | collective-permute-start | bytes 393224 | tf_op jit(solution)/shard_map/ppermute | solution.py:32
  31.6 0.8 %collective-permute-done.8 = bf16[128,512]{1,0:T(8,128)(2,1)S(1)} collective-permute-done((bf16[128,512]{1,0:T(8,128)(2,1)S(1)}, bf16[128,512]{1,0:T(8,128)(2,1)S(1)}, u32[]{:S(2)}, u32[]{:S(2)}) %collective-permute-start.8) | collective-permute-done | bytes 131104 | tf_op jit(solution)/shard_map/ppermute | solution.py:28
  32.5 2.0 %all_gather.11 = bf16[256,512]{1,0:T(8,128)(2,1)S(1)} all-gather(bf16[128,512]{1,0:T(8,128)(2,1)S(1)} %fusion.16), channel_id=1, replica_groups=mesh['blk'=16,'rep'=2] {'rep'}, dimensions={0}, use_global_device_ids=true | all-gather | bytes 393216 | tf_op jit(solution)/shard_map/all_gather | solution.py:115
  35.2 1.3 %collective-permute-start.19 = (bf16[128,512]{1,0:T(8,128)(2,1)S(1)}, bf16[128,512]{1,0:T(8,128)(2,1)S(1)}, u32[]{:S(2)}, u32[]{:S(2)}) collective-permute-start(bf16[128,512]{1,0:T(8,128)(2,1)S(1)} %pad_maximum_fusion.5), channel_id=1, source_target_pairs={{0,8},{2,10},{4,12},{6,14},{8,0},{10,2},{12,4},{14,6},{16,24},{18,... | collective-permute-start | bytes 393224 | tf_op jit(solution)/shard_map/ppermute | solution.py:32
  36.5 1.1 %collective-permute-start.9 = (bf16[128,512]{1,0:T(8,128)(2,1)S(1)}, bf16[128,512]{1,0:T(8,128)(2,1)S(1)}, u32[]{:S(2)}, u32[]{:S(2)}) collective-permute-start(bf16[128,512]{1,0:T(8,128)(2,1)S(1)} %get-tuple-element.5), channel_id=1, source_target_pairs={{0,2},{2,0},{4,6},{6,4},{8,10},{10,8},{12,14},{14,12},{16,18},{18,... | collective-permute-start | bytes 393224 | tf_op jit(solution)/shard_map/ppermute | solution.py:28
  37.7 1.4 %collective-permute-start.11 = (bf16[128,512]{1,0:T(8,128)(2,1)S(1)}, bf16[128,512]{1,0:T(8,128)(2,1)S(1)}, u32[]{:S(2)}, u32[]{:S(2)}) collective-permute-start(bf16[128,512]{1,0:T(8,128)(2,1)S(1)} %get-tuple-element.6), channel_id=1, source_target_pairs={{0,6},{2,4},{4,2},{6,0},{8,14},{10,12},{12,10},{14,8},{16,22},{18,... | collective-permute-start | bytes 393224 | tf_op jit(solution)/shard_map/ppermute | solution.py:28
  39.1 3.2 %collective-permute-done.16 = bf16[512,128]{1,0:T(8,128)(2,1)S(1)} collective-permute-done((bf16[512,128]{1,0:T(8,128)(2,1)S(1)}, bf16[512,128]{1,0:T(8,128)(2,1)S(1)}, u32[]{:S(2)}, u32[]{:S(2)}) %collective-permute-start.16) | collective-permute-done | bytes 131104 | tf_op jit(solution)/shard_map/ppermute | solution.py:32
  42.9 1.1 %collective-permute-start.10 = (bf16[128,512]{1,0:T(8,128)(2,1)S(1)}, bf16[128,512]{1,0:T(8,128)(2,1)S(1)}, u32[]{:S(2)}, u32[]{:S(2)}) collective-permute-start(bf16[128,512]{1,0:T(8,128)(2,1)S(1)} %get-tuple-element.7), channel_id=1, source_target_pairs={{0,4},{2,6},{4,0},{6,2},{8,12},{10,14},{12,8},{14,10},{16,20},{18,... | collective-permute-start | bytes 393224 | tf_op jit(solution)/shard_map/ppermute | solution.py:28
  44.0 1.1 %collective-permute-done.11 = bf16[128,512]{1,0:T(8,128)(2,1)S(1)} collective-permute-done((bf16[128,512]{1,0:T(8,128)(2,1)S(1)}, bf16[128,512]{1,0:T(8,128)(2,1)S(1)}, u32[]{:S(2)}, u32[]{:S(2)}) %collective-permute-start.11) | collective-permute-done | bytes 131104 | tf_op jit(solution)/shard_map/ppermute | solution.py:28
  45.1 3.1 %collective-permute-start.20 = (bf16[64,512]{1,0:T(8,128)(2,1)S(1)}, bf16[64,512]{1,0:T(8,128)(2,1)S(1)}, u32[]{:S(2)}, u32[]{:S(2)}) collective-permute-start(bf16[64,512]{1,0:T(8,128)(2,1)S(1)} %fusion.23), channel_id=1, source_target_pairs={{0,16},{2,18},{4,20},{6,22},{8,24},{10,26},{12,28},{14,30},{16,0},... | collective-permute-start | bytes 196616 | tf_op jit(solution)/shard_map/ppermute | solution.py:32
  48.2 0.7 %collective-permute-done.10 = bf16[128,512]{1,0:T(8,128)(2,1)S(1)} collective-permute-done((bf16[128,512]{1,0:T(8,128)(2,1)S(1)}, bf16[128,512]{1,0:T(8,128)(2,1)S(1)}, u32[]{:S(2)}, u32[]{:S(2)}) %collective-permute-start.10) | collective-permute-done | bytes 131104 | tf_op jit(solution)/shard_map/ppermute | solution.py:28
  48.8 1.2 %add_convert_fusion = (bf16[128,512]{1,0:T(8,128)(2,1)}, bf16[128,512]{1,0:T(8,128)(2,1)}) fusion(bf16[128,512]{1,0:T(8,128)(2,1)S(1)} %collective-permute-done.11, bf16[128,512]{1,0:T(8,128)(2,1)S(1)} %collective-permute-done.10, bf16[128,512]{1,0:T(8,128)(2,1)S(1)} %collective-permute-done.9, bf16[512,512]{1,0:T(8,128)(2,1)S(1)} %convolution_convert_fusion.1, ...), kind=kOutput, calls=%fused_computation.27 | convolution fusion | flops 68288512 | bytes 1703948 | tf_op jit(solution)/shard_map/dot_general | solution.py:55
  50.0 1.1 %collective-permute-done.20 = bf16[64,512]{1,0:T(8,128)(2,1)S(1)} collective-permute-done((bf16[64,512]{1,0:T(8,128)(2,1)S(1)}, bf16[64,512]{1,0:T(8,128)(2,1)S(1)}, u32[]{:S(2)}, u32[]{:S(2)}) %collective-permute-start.20) | collective-permute-done | bytes 65568 | tf_op jit(solution)/shard_map/ppermute | solution.py:32
  51.1 0.7 %fusion.19 = f32[64,512]{1,0:T(8,128)} fusion(bf16[64,512]{1,0:T(8,128)(2,1)S(1)} %collective-permute-done.20, f32[4,64,512]{2,1,0:T(8,128)S(1)} %bitcast.124, s32[]{:T(128)S(6)} %select_n.276, bf16[128,512]{1,0:T(8,128)(2,1)S(1)} %collective-permute-done.19), kind=kLoop, calls=%fused_computation.39 | loop fusion | flops 131072 | bytes 393220 | tf_op jit(solution)/shard_map/add | solution.py:45
  (55 shorter events, 3.9 us)
Async XLA Ops:
  0.6 11.7 %copy-start = (bf16[1024,1024]{1,0:T(8,128)(2,1)S(1)}, bf16[1024,1024]{1,0:T(8,128)(2,1)}, u32[]{:S(2)}) copy-start(bf16[1024,1024]{1,0:T(8,128)(2,1)} %param.8) | copy-start | bytes 6291460
  0.6 11.7 %copy-start.2 = (bf16[128,1024]{1,0:T(8,128)(2,1)S(1)}, bf16[128,1024]{1,0:T(8,128)(2,1)}, u32[]{:S(2)}) copy-start(bf16[128,1024]{1,0:T(8,128)(2,1)} %param.9) | copy-start | bytes 786436
  1.7 19.1 %collective-permute-start.2 = (bf16[128,512]{1,0:T(8,128)(2,1)S(1)}, bf16[128,512]{1,0:T(8,128)(2,1)S(1)}, u32[]{:S(2)}, u32[]{:S(2)}) collective-permute-start(bf16[128,512]{1,0:T(8,128)(2,1)S(1)} %dynamic-slice_maximum_fusion), channel_id=1, source_target_pairs={{0,24},{2,26},{4,28},{6,30},{8,16},{10,18},{12,20},{14,22},{16,8},... | collective-permute-start | bytes 393224 | tf_op jit(solution)/shard_map/ppermute | solution.py:32
  6.9 14.6 %collective-permute-start.1 = (bf16[128,512]{1,0:T(8,128)(2,1)S(1)}, bf16[128,512]{1,0:T(8,128)(2,1)S(1)}, u32[]{:S(2)}, u32[]{:S(2)}) collective-permute-start(bf16[128,512]{1,0:T(8,128)(2,1)S(1)} %dynamic-slice_maximum_fusion), channel_id=1, source_target_pairs={{0,16},{2,18},{4,20},{6,22},{8,24},{10,26},{12,28},{14,30},{16,0},... | collective-permute-start | bytes 393224 | tf_op jit(solution)/shard_map/ppermute | solution.py:32
  8.7 5.3 %collective-permute-start.5 = (bf16[2,128,128]{2,1,0:T(8,128)(2,1)S(1)}, bf16[2,128,128]{2,1,0:T(8,128)(2,1)S(1)}, u32[]{:S(2)}, u32[]{:S(2)}) collective-permute-start(bf16[2,128,128]{2,1,0:T(8,128)(2,1)S(1)} %get-tuple-element.31), channel_id=1, source_target_pairs={{0,6},{2,4},{4,2},{6,0},{8,14},{10,12},{12,10},{14,8},{16,22},{18,... | collective-permute-start | bytes 196616 | tf_op jit(solution)/shard_map/ppermute | solution.py:28
  11.2 4.3 %collective-permute-start.4 = (bf16[2,128,128]{2,1,0:T(8,128)(2,1)S(1)}, bf16[2,128,128]{2,1,0:T(8,128)(2,1)S(1)}, u32[]{:S(2)}, u32[]{:S(2)}) collective-permute-start(bf16[2,128,128]{2,1,0:T(8,128)(2,1)S(1)} %get-tuple-element.32), channel_id=1, source_target_pairs={{0,4},{2,6},{4,0},{6,2},{8,12},{10,14},{12,8},{14,10},{16,20},{18,... | collective-permute-start | bytes 196616 | tf_op jit(solution)/shard_map/ppermute | solution.py:28
  11.8 5.6 %collective-permute-start.3 = (bf16[2,128,128]{2,1,0:T(8,128)(2,1)S(1)}, bf16[2,128,128]{2,1,0:T(8,128)(2,1)S(1)}, u32[]{:S(2)}, u32[]{:S(2)}) collective-permute-start(bf16[2,128,128]{2,1,0:T(8,128)(2,1)S(1)} %get-tuple-element.33), channel_id=1, source_target_pairs={{0,2},{2,0},{4,6},{6,4},{8,10},{10,8},{12,14},{14,12},{16,18},{18,... | collective-permute-start | bytes 196616 | tf_op jit(solution)/shard_map/ppermute | solution.py:28
  14.1 7.4 %collective-permute-start = (bf16[128,512]{1,0:T(8,128)(2,1)S(1)}, bf16[128,512]{1,0:T(8,128)(2,1)S(1)}, u32[]{:S(2)}, u32[]{:S(2)}) collective-permute-start(bf16[128,512]{1,0:T(8,128)(2,1)S(1)} %dynamic-slice_maximum_fusion), channel_id=1, source_target_pairs={{0,8},{2,10},{4,12},{6,14},{8,0},{10,2},{12,4},{14,6},{16,24},{18,... | collective-permute-start | bytes 393224 | tf_op jit(solution)/shard_map/ppermute | solution.py:32
  15.5 9.1 %collective-permute-start.14 = (bf16[128,512]{1,0:T(8,128)(2,1)S(1)}, bf16[128,512]{1,0:T(8,128)(2,1)S(1)}, u32[]{:S(2)}, u32[]{:S(2)}) collective-permute-start(bf16[128,512]{1,0:T(8,128)(2,1)S(1)} %constant_dynamic-slice_fusion), channel_id=1, source_target_pairs={{0,6},{2,4},{4,2},{6,0},{8,14},{10,12},{12,10},{14,8},{16,22},{18,... | collective-permute-start | bytes 393224 | tf_op jit(solution)/shard_map/ppermute | solution.py:28
  17.3 8.6 %collective-permute-start.13 = (bf16[128,512]{1,0:T(8,128)(2,1)S(1)}, bf16[128,512]{1,0:T(8,128)(2,1)S(1)}, u32[]{:S(2)}, u32[]{:S(2)}) collective-permute-start(bf16[128,512]{1,0:T(8,128)(2,1)S(1)} %constant_dynamic-slice_fusion), channel_id=1, source_target_pairs={{0,4},{2,6},{4,0},{6,2},{8,12},{10,14},{12,8},{14,10},{16,20},{18,... | collective-permute-start | bytes 393224 | tf_op jit(solution)/shard_map/ppermute | solution.py:28
  20.9 6.1 %collective-permute-start.12 = (bf16[128,512]{1,0:T(8,128)(2,1)S(1)}, bf16[128,512]{1,0:T(8,128)(2,1)S(1)}, u32[]{:S(2)}, u32[]{:S(2)}) collective-permute-start(bf16[128,512]{1,0:T(8,128)(2,1)S(1)} %constant_dynamic-slice_fusion), channel_id=1, source_target_pairs={{0,2},{2,0},{4,6},{6,4},{8,10},{10,8},{12,14},{14,12},{16,18},{18,... | collective-permute-start | bytes 393224 | tf_op jit(solution)/shard_map/ppermute | solution.py:28
  22.1 9.3 %collective-permute-start.7 = (bf16[128,512]{1,0:T(8,128)(2,1)S(1)}, bf16[128,512]{1,0:T(8,128)(2,1)S(1)}, u32[]{:S(2)}, u32[]{:S(2)}) collective-permute-start(bf16[128,512]{1,0:T(8,128)(2,1)S(1)} %pad_maximum_fusion.3), channel_id=1, source_target_pairs={{0,4},{2,6},{4,0},{6,2},{8,12},{10,14},{12,8},{14,10},{16,20},{18,... | collective-permute-start | bytes 393224 | tf_op jit(solution)/shard_map/ppermute | solution.py:28
  23.7 8.0 %collective-permute-start.6 = (bf16[128,512]{1,0:T(8,128)(2,1)S(1)}, bf16[128,512]{1,0:T(8,128)(2,1)S(1)}, u32[]{:S(2)}, u32[]{:S(2)}) collective-permute-start(bf16[128,512]{1,0:T(8,128)(2,1)S(1)} %pad_maximum_fusion.2), channel_id=1, source_target_pairs={{0,2},{2,0},{4,6},{6,4},{8,10},{10,8},{12,14},{14,12},{16,18},{18,... | collective-permute-start | bytes 393224 | tf_op jit(solution)/shard_map/ppermute | solution.py:28
  24.7 7.7 %collective-permute-start.8 = (bf16[128,512]{1,0:T(8,128)(2,1)S(1)}, bf16[128,512]{1,0:T(8,128)(2,1)S(1)}, u32[]{:S(2)}, u32[]{:S(2)}) collective-permute-start(bf16[128,512]{1,0:T(8,128)(2,1)S(1)} %pad_maximum_fusion.4), channel_id=1, source_target_pairs={{0,6},{2,4},{4,2},{6,0},{8,14},{10,12},{12,10},{14,8},{16,22},{18,... | collective-permute-start | bytes 393224 | tf_op jit(solution)/shard_map/ppermute | solution.py:28
  27.5 10.1 %collective-permute-start.15 = (bf16[512,128]{1,0:T(8,128)(2,1)S(1)}, bf16[512,128]{1,0:T(8,128)(2,1)S(1)}, u32[]{:S(2)}, u32[]{:S(2)}) collective-permute-start(bf16[512,128]{1,0:T(8,128)(2,1)S(1)} %get-tuple-element.8), channel_id=1, source_target_pairs={{0,8},{2,10},{4,12},{6,14},{8,0},{10,2},{12,4},{14,6},{16,24},{18,... | collective-permute-start | bytes 393224 | tf_op jit(solution)/shard_map/ppermute | solution.py:32
  28.6 10.5 %collective-permute-start.17 = (bf16[512,128]{1,0:T(8,128)(2,1)S(1)}, bf16[512,128]{1,0:T(8,128)(2,1)S(1)}, u32[]{:S(2)}, u32[]{:S(2)}) collective-permute-start(bf16[512,128]{1,0:T(8,128)(2,1)S(1)} %get-tuple-element.9), channel_id=1, source_target_pairs={{0,24},{2,26},{4,28},{6,30},{8,16},{10,18},{12,20},{14,22},{16,8},... | collective-permute-start | bytes 393224 | tf_op jit(solution)/shard_map/ppermute | solution.py:32
  31.4 10.9 %collective-permute-start.16 = (bf16[512,128]{1,0:T(8,128)(2,1)S(1)}, bf16[512,128]{1,0:T(8,128)(2,1)S(1)}, u32[]{:S(2)}, u32[]{:S(2)}) collective-permute-start(bf16[512,128]{1,0:T(8,128)(2,1)S(1)} %get-tuple-element.10), channel_id=1, source_target_pairs={{0,16},{2,18},{4,20},{6,22},{8,24},{10,26},{12,28},{14,30},{16,0},... | collective-permute-start | bytes 393224 | tf_op jit(solution)/shard_map/ppermute | solution.py:32
  34.8 14.0 %copy-start.1 = (bf16[128,1024]{1,0:T(8,128)(2,1)S(1)}, bf16[128,1024]{1,0:T(8,128)(2,1)}, u32[]{:S(2)}) copy-start(bf16[128,1024]{1,0:T(8,128)(2,1)} %param.5) | copy-start | bytes 786436
  35.2 8.8 %collective-permute-start.19 = (bf16[128,512]{1,0:T(8,128)(2,1)S(1)}, bf16[128,512]{1,0:T(8,128)(2,1)S(1)}, u32[]{:S(2)}, u32[]{:S(2)}) collective-permute-start(bf16[128,512]{1,0:T(8,128)(2,1)S(1)} %pad_maximum_fusion.5), channel_id=1, source_target_pairs={{0,8},{2,10},{4,12},{6,14},{8,0},{10,2},{12,4},{14,6},{16,24},{18,... | collective-permute-start | bytes 393224 | tf_op jit(solution)/shard_map/ppermute | solution.py:32
  36.5 7.5 %collective-permute-start.9 = (bf16[128,512]{1,0:T(8,128)(2,1)S(1)}, bf16[128,512]{1,0:T(8,128)(2,1)S(1)}, u32[]{:S(2)}, u32[]{:S(2)}) collective-permute-start(bf16[128,512]{1,0:T(8,128)(2,1)S(1)} %get-tuple-element.5), channel_id=1, source_target_pairs={{0,2},{2,0},{4,6},{6,4},{8,10},{10,8},{12,14},{14,12},{16,18},{18,... | collective-permute-start | bytes 393224 | tf_op jit(solution)/shard_map/ppermute | solution.py:28
  37.7 7.4 %collective-permute-start.11 = (bf16[128,512]{1,0:T(8,128)(2,1)S(1)}, bf16[128,512]{1,0:T(8,128)(2,1)S(1)}, u32[]{:S(2)}, u32[]{:S(2)}) collective-permute-start(bf16[128,512]{1,0:T(8,128)(2,1)S(1)} %get-tuple-element.6), channel_id=1, source_target_pairs={{0,6},{2,4},{4,2},{6,0},{8,14},{10,12},{12,10},{14,8},{16,22},{18,... | collective-permute-start | bytes 393224 | tf_op jit(solution)/shard_map/ppermute | solution.py:28
  42.8 5.3 %collective-permute-start.18 = (bf16[128,512]{1,0:T(8,128)(2,1)S(1)}, bf16[128,512]{1,0:T(8,128)(2,1)S(1)}, u32[]{:S(2)}, u32[]{:S(2)}) collective-permute-start(bf16[128,512]{1,0:T(8,128)(2,1)S(1)} %convolution_convert_fusion.2), channel_id=1, source_target_pairs={{0,1},{1,0},{2,3},{3,2},{4,5},{5,4},{6,7},{7,6},{8,9},{9,8},{10,11... | collective-permute-start | bytes 393224 | tf_op jit(solution)/shard_map/ppermute | solution.py:52
  42.9 5.9 %collective-permute-start.10 = (bf16[128,512]{1,0:T(8,128)(2,1)S(1)}, bf16[128,512]{1,0:T(8,128)(2,1)S(1)}, u32[]{:S(2)}, u32[]{:S(2)}) collective-permute-start(bf16[128,512]{1,0:T(8,128)(2,1)S(1)} %get-tuple-element.7), channel_id=1, source_target_pairs={{0,4},{2,6},{4,0},{6,2},{8,12},{10,14},{12,8},{14,10},{16,20},{18,... | collective-permute-start | bytes 393224 | tf_op jit(solution)/shard_map/ppermute | solution.py:28
  45.1 6.0 %collective-permute-start.20 = (bf16[64,512]{1,0:T(8,128)(2,1)S(1)}, bf16[64,512]{1,0:T(8,128)(2,1)S(1)}, u32[]{:S(2)}, u32[]{:S(2)}) collective-permute-start(bf16[64,512]{1,0:T(8,128)(2,1)S(1)} %fusion.23), channel_id=1, source_target_pairs={{0,16},{2,18},{4,20},{6,22},{8,24},{10,26},{12,28},{14,30},{16,0},... | collective-permute-start | bytes 196616 | tf_op jit(solution)/shard_map/ppermute | solution.py:32

commit v37 on v33

--- a/solution.py
+++ b/solution.py
@@ -129,7 +129,7 @@
         out_got[1::2],
     )
 
-    back = after(back, weight_part).astype(bf16)
+    back = back.astype(bf16)
     w_rows = w_out.reshape(rep_count, cols_here, feature_width)
     if rep_count == 2:
         w_mine = columns_of(lax.dynamic_index_in_dim(w_rows, rep_pos, 0, keepdims=False), rep_pos)

time: 52 us -> 52.1 us (level)
  no operation moved by 1% of the time
where the time goes in v37:
time: 52.1 us; the launch traced here: 51.8 us
  starting transfers between devices  28.7 us (55%)
  waiting for transfers between devices  10.6 us (20%)
  blocking collectives  4.18 us (8%)
  matrix products  3.15 us (6%)
  other arithmetic  3.09 us (6%)
  local copies, waits for them, and re-layouts  1.23 us (2%)
  between operations  0.9 us (2%)
    ppermute x12, starting transfers between devices, along_inner(): return lax.ppermute(value, 'blk', pairs) if turn else value  14.4 us
    ppermute x8, starting transfers between devices, along_outer(): return lax.ppermute(value, 'blk', pairs) if turn else value  14.2 us
    ppermute x12, waiting for transfers between devices, along_inner(): return lax.ppermute(value, 'blk', pairs) if turn else value  6.12 us
    ppermute x8, waiting for transfers between devices, along_outer(): return lax.ppermute(value, 'blk', pairs) if turn else value  4.45 us
    dot_general x6, matrix products, dot(): lax.dot_general(lhs, rhs, (dims, ((), ())), preferred_element_type=jnp.fl...  3.15 us
    all_gather x1, blocking collectives, shards(): everyone = lax.all_gather(jnp.concatenate(arrived, 0), 'rep', axis=0)  2.18 us
    all_gather x1, blocking collectives, shards(): lax.all_gather(mixed_cols.astype(bf16), 'rep', axis=0, tiled=True)  1.99 us
    max x1, other arithmetic, shards(): hidden_part = jnp.maximum(columns_of(hidden_pre, rep_pos), 0)  1.08 us
  transfers between devices with their start and end apart: 21, of which 8 were waited for; matrix products, arithmetic and copies ran while one was open for 11% of the time, Pallas kernels for 0%

profile of v37, /device:TPU:0, one launch (start us, length us, event | category | flops | bytes accessed | tf_op | source)
XLA Modules:
  0.0 51.8 jit_solution(16682317430916987970)
XLA Ops:
  0.7 1.1 %dynamic-slice_maximum_fusion = bf16[128,512]{1,0:T(8,128)(2,1)S(1)} fusion(bf16[128,1024]{1,0:T(8,128)(2,1)} %param.5, s32[]{:T(128)S(6)} %select_n.214), kind=kLoop, calls=%fused_computation.40 | loop fusion | flops 262144 | bytes 262148 | tf_op jit(solution)/shard_map/max | solution.py:69
  1.7 5.1 %collective-permute-start.2 = (bf16[128,512]{1,0:T(8,128)(2,1)S(1)}, bf16[128,512]{1,0:T(8,128)(2,1)S(1)}, u32[]{:S(2)}, u32[]{:S(2)}) collective-permute-start(bf16[128,512]{1,0:T(8,128)(2,1)S(1)} %dynamic-slice_maximum_fusion), channel_id=1, source_target_pairs={{0,24},{2,26},{4,28},{6,30},{8,16},{10,18},{12,20},{14,22},{16,8},... | collective-permute-start | bytes 393224 | tf_op jit(solution)/shard_map/ppermute | solution.py:32
  6.9 0.7 %add_bitcast_fusion = s32[8]{0:T(128)S(1)} fusion(s32[1,8]{1,0:T(1,128)} %param.7, s32[]{:T(128)S(6)} %shift_right_arithmetic.54, s32[]{:T(128)S(6)} %and.60), kind=kLoop, calls=%fused_computation.90 | loop fusion | flops 56 | bytes 72 | tf_op jit(solution)/shard_map/eq | solution.py:75
  7.6 0.9 %slice_bitcast_fusion.9 = (bf16[128,128]{1,0:T(8,128)(2,1)S(1)}, bf16[128,128]{1,0:T(8,128)(2,1)S(1)}, bf16[128,128]{1,0:T(8,128)(2,1)S(1)}, bf16[128,128]{1,0:T...) fusion(bf16[1,8,128,128]{3,2,1,0:T(8,128)(2,1)} %param.6), kind=kLoop, calls=%fused_computation.71 | loop fusion | bytes 524288 | tf_op jit(solution)/shard_map/jit(_where)/broadcast_in_dim | solution.py:78
  8.7 2.5 %collective-permute-start.5 = (bf16[2,128,128]{2,1,0:T(8,128)(2,1)S(1)}, bf16[2,128,128]{2,1,0:T(8,128)(2,1)S(1)}, u32[]{:S(2)}, u32[]{:S(2)}) collective-permute-start(bf16[2,128,128]{2,1,0:T(8,128)(2,1)S(1)} %get-tuple-element.31), channel_id=1, source_target_pairs={{0,6},{2,4},{4,2},{6,0},{8,14},{10,12},{12,10},{14,8},{16,22},{18,... | collective-permute-start | bytes 196616 | tf_op jit(solution)/shard_map/ppermute | solution.py:28
  11.8 0.5 %collective-permute-start.3 = (bf16[2,128,128]{2,1,0:T(8,128)(2,1)S(1)}, bf16[2,128,128]{2,1,0:T(8,128)(2,1)S(1)}, u32[]{:S(2)}, u32[]{:S(2)}) collective-permute-start(bf16[2,128,128]{2,1,0:T(8,128)(2,1)S(1)} %get-tuple-element.33), channel_id=1, source_target_pairs={{0,2},{2,0},{4,6},{6,4},{8,10},{10,8},{12,14},{14,12},{16,18},{18,... | collective-permute-start | bytes 196616 | tf_op jit(solution)/shard_map/ppermute | solution.py:28
  12.4 1.7 %collective-permute-done.5 = bf16[2,128,128]{2,1,0:T(8,128)(2,1)S(1)} collective-permute-done((bf16[2,128,128]{2,1,0:T(8,128)(2,1)S(1)}, bf16[2,128,128]{2,1,0:T(8,128)(2,1)S(1)}, u32[]{:S(2)}, u32[]{:S(2)}) %collective-permute-start.5) | collective-permute-done | bytes 65568 | tf_op jit(solution)/shard_map/ppermute | solution.py:28
  14.1 0.6 %collective-permute-start = (bf16[128,512]{1,0:T(8,128)(2,1)S(1)}, bf16[128,512]{1,0:T(8,128)(2,1)S(1)}, u32[]{:S(2)}, u32[]{:S(2)}) collective-permute-start(bf16[128,512]{1,0:T(8,128)(2,1)S(1)} %dynamic-slice_maximum_fusion), channel_id=1, source_target_pairs={{0,8},{2,10},{4,12},{6,14},{8,0},{10,2},{12,4},{14,6},{16,24},{18,... | collective-permute-start | bytes 393224 | tf_op jit(solution)/shard_map/ppermute | solution.py:32
  14.7 0.8 %collective-permute-done.4 = bf16[2,128,128]{2,1,0:T(8,128)(2,1)S(1)} collective-permute-done((bf16[2,128,128]{2,1,0:T(8,128)(2,1)S(1)}, bf16[2,128,128]{2,1,0:T(8,128)(2,1)S(1)}, u32[]{:S(2)}, u32[]{:S(2)}) %collective-permute-start.4) | collective-permute-done | bytes 65568 | tf_op jit(solution)/shard_map/ppermute | solution.py:28
  15.5 1.8 %collective-permute-start.14 = (bf16[128,512]{1,0:T(8,128)(2,1)S(1)}, bf16[128,512]{1,0:T(8,128)(2,1)S(1)}, u32[]{:S(2)}, u32[]{:S(2)}) collective-permute-start(bf16[128,512]{1,0:T(8,128)(2,1)S(1)} %constant_dynamic-slice_fusion), channel_id=1, source_target_pairs={{0,6},{2,4},{4,2},{6,0},{8,14},{10,12},{12,10},{14,8},{16,22},{18,... | collective-permute-start | bytes 393224 | tf_op jit(solution)/shard_map/ppermute | solution.py:28
  17.3 1.1 %collective-permute-start.13 = (bf16[128,512]{1,0:T(8,128)(2,1)S(1)}, bf16[128,512]{1,0:T(8,128)(2,1)S(1)}, u32[]{:S(2)}, u32[]{:S(2)}) collective-permute-start(bf16[128,512]{1,0:T(8,128)(2,1)S(1)} %constant_dynamic-slice_fusion), channel_id=1, source_target_pairs={{0,4},{2,6},{4,0},{6,2},{8,12},{10,14},{12,8},{14,10},{16,20},{18,... | collective-permute-start | bytes 393224 | tf_op jit(solution)/shard_map/ppermute | solution.py:28
  18.5 2.2 %all-gather = bf16[16,128,128]{2,1,0:T(8,128)(2,1)S(1)} all-gather(bf16[8,128,128]{2,1,0:T(8,128)(2,1)S(1)} %pad_maximum_fusion.1), channel_id=2, replica_groups=mesh['blk'=16,'rep'=2] {'rep'}, dimensions={0}, use_global_device_ids=true | all-gather | bytes 786432 | tf_op jit(solution)/shard_map/all_gather | solution.py:82
  20.9 0.6 %collective-permute-start.12 = (bf16[128,512]{1,0:T(8,128)(2,1)S(1)}, bf16[128,512]{1,0:T(8,128)(2,1)S(1)}, u32[]{:S(2)}, u32[]{:S(2)}) collective-permute-start(bf16[128,512]{1,0:T(8,128)(2,1)S(1)} %constant_dynamic-slice_fusion), channel_id=1, source_target_pairs={{0,2},{2,0},{4,6},{6,4},{8,10},{10,8},{12,14},{14,12},{16,18},{18,... | collective-permute-start | bytes 393224 | tf_op jit(solution)/shard_map/ppermute | solution.py:28
  22.1 1.5 %collective-permute-start.7 = (bf16[128,512]{1,0:T(8,128)(2,1)S(1)}, bf16[128,512]{1,0:T(8,128)(2,1)S(1)}, u32[]{:S(2)}, u32[]{:S(2)}) collective-permute-start(bf16[128,512]{1,0:T(8,128)(2,1)S(1)} %pad_maximum_fusion.3), channel_id=1, source_target_pairs={{0,4},{2,6},{4,0},{6,2},{8,12},{10,14},{12,8},{14,10},{16,20},{18,... | collective-permute-start | bytes 393224 | tf_op jit(solution)/shard_map/ppermute | solution.py:28
  23.7 1.0 %collective-permute-start.6 = (bf16[128,512]{1,0:T(8,128)(2,1)S(1)}, bf16[128,512]{1,0:T(8,128)(2,1)S(1)}, u32[]{:S(2)}, u32[]{:S(2)}) collective-permute-start(bf16[128,512]{1,0:T(8,128)(2,1)S(1)} %pad_maximum_fusion.2), channel_id=1, source_target_pairs={{0,2},{2,0},{4,6},{6,4},{8,10},{10,8},{12,14},{14,12},{16,18},{18,... | collective-permute-start | bytes 393224 | tf_op jit(solution)/shard_map/ppermute | solution.py:28
  24.7 1.2 %collective-permute-start.8 = (bf16[128,512]{1,0:T(8,128)(2,1)S(1)}, bf16[128,512]{1,0:T(8,128)(2,1)S(1)}, u32[]{:S(2)}, u32[]{:S(2)}) collective-permute-start(bf16[128,512]{1,0:T(8,128)(2,1)S(1)} %pad_maximum_fusion.4), channel_id=1, source_target_pairs={{0,6},{2,4},{4,2},{6,0},{8,14},{10,12},{12,10},{14,8},{16,22},{18,... | collective-permute-start | bytes 393224 | tf_op jit(solution)/shard_map/ppermute | solution.py:28
  25.9 1.1 %collective-permute-done.12 = bf16[128,512]{1,0:T(8,128)(2,1)S(1)} collective-permute-done((bf16[128,512]{1,0:T(8,128)(2,1)S(1)}, bf16[128,512]{1,0:T(8,128)(2,1)S(1)}, u32[]{:S(2)}, u32[]{:S(2)}) %collective-permute-start.12) | collective-permute-done | bytes 131104 | tf_op jit(solution)/shard_map/ppermute | solution.py:28
  27.5 1.1 %collective-permute-start.15 = (bf16[512,128]{1,0:T(8,128)(2,1)S(1)}, bf16[512,128]{1,0:T(8,128)(2,1)S(1)}, u32[]{:S(2)}, u32[]{:S(2)}) collective-permute-start(bf16[512,128]{1,0:T(8,128)(2,1)S(1)} %get-tuple-element.12), channel_id=1, source_target_pairs={{0,8},{2,10},{4,12},{6,14},{8,0},{10,2},{12,4},{14,6},{16,24},{18,... | collective-permute-start | bytes 393224 | tf_op jit(solution)/shard_map/ppermute | solution.py:32
  28.6 2.8 %collective-permute-start.17 = (bf16[512,128]{1,0:T(8,128)(2,1)S(1)}, bf16[512,128]{1,0:T(8,128)(2,1)S(1)}, u32[]{:S(2)}, u32[]{:S(2)}) collective-permute-start(bf16[512,128]{1,0:T(8,128)(2,1)S(1)} %get-tuple-element.13), channel_id=1, source_target_pairs={{0,24},{2,26},{4,28},{6,30},{8,16},{10,18},{12,20},{14,22},{16,8},... | collective-permute-start | bytes 393224 | tf_op jit(solution)/shard_map/ppermute | solution.py:32
  31.6 0.8 %collective-permute-done.8 = bf16[128,512]{1,0:T(8,128)(2,1)S(1)} collective-permute-done((bf16[128,512]{1,0:T(8,128)(2,1)S(1)}, bf16[128,512]{1,0:T(8,128)(2,1)S(1)}, u32[]{:S(2)}, u32[]{:S(2)}) %collective-permute-start.8) | collective-permute-done | bytes 131104 | tf_op jit(solution)/shard_map/ppermute | solution.py:28
  32.5 2.0 %all_gather.11 = bf16[256,512]{1,0:T(8,128)(2,1)S(1)} all-gather(bf16[128,512]{1,0:T(8,128)(2,1)S(1)} %fusion.15), channel_id=1, replica_groups=mesh['blk'=16,'rep'=2] {'rep'}, dimensions={0}, use_global_device_ids=true | all-gather | bytes 393216 | tf_op jit(solution)/shard_map/all_gather | solution.py:115
  35.2 1.3 %collective-permute-start.19 = (bf16[128,512]{1,0:T(8,128)(2,1)S(1)}, bf16[128,512]{1,0:T(8,128)(2,1)S(1)}, u32[]{:S(2)}, u32[]{:S(2)}) collective-permute-start(bf16[128,512]{1,0:T(8,128)(2,1)S(1)} %pad_maximum_fusion.5), channel_id=1, source_target_pairs={{0,8},{2,10},{4,12},{6,14},{8,0},{10,2},{12,4},{14,6},{16,24},{18,... | collective-permute-start | bytes 393224 | tf_op jit(solution)/shard_map/ppermute | solution.py:32
  36.5 1.2 %collective-permute-start.9 = (bf16[128,512]{1,0:T(8,128)(2,1)S(1)}, bf16[128,512]{1,0:T(8,128)(2,1)S(1)}, u32[]{:S(2)}, u32[]{:S(2)}) collective-permute-start(bf16[128,512]{1,0:T(8,128)(2,1)S(1)} %get-tuple-element.5), channel_id=1, source_target_pairs={{0,2},{2,0},{4,6},{6,4},{8,10},{10,8},{12,14},{14,12},{16,18},{18,... | collective-permute-start | bytes 393224 | tf_op jit(solution)/shard_map/ppermute | solution.py:28
  37.7 1.4 %collective-permute-start.11 = (bf16[128,512]{1,0:T(8,128)(2,1)S(1)}, bf16[128,512]{1,0:T(8,128)(2,1)S(1)}, u32[]{:S(2)}, u32[]{:S(2)}) collective-permute-start(bf16[128,512]{1,0:T(8,128)(2,1)S(1)} %get-tuple-element.6), channel_id=1, source_target_pairs={{0,6},{2,4},{4,2},{6,0},{8,14},{10,12},{12,10},{14,8},{16,22},{18,... | collective-permute-start | bytes 393224 | tf_op jit(solution)/shard_map/ppermute | solution.py:28
  39.1 3.3 %collective-permute-done.16 = bf16[512,128]{1,0:T(8,128)(2,1)S(1)} collective-permute-done((bf16[512,128]{1,0:T(8,128)(2,1)S(1)}, bf16[512,128]{1,0:T(8,128)(2,1)S(1)}, u32[]{:S(2)}, u32[]{:S(2)}) %collective-permute-start.16) | collective-permute-done | bytes 131104 | tf_op jit(solution)/shard_map/ppermute | solution.py:32
  42.9 1.1 %collective-permute-start.10 = (bf16[128,512]{1,0:T(8,128)(2,1)S(1)}, bf16[128,512]{1,0:T(8,128)(2,1)S(1)}, u32[]{:S(2)}, u32[]{:S(2)}) collective-permute-start(bf16[128,512]{1,0:T(8,128)(2,1)S(1)} %get-tuple-element.7), channel_id=1, source_target_pairs={{0,4},{2,6},{4,0},{6,2},{8,12},{10,14},{12,8},{14,10},{16,20},{18,... | collective-permute-start | bytes 393224 | tf_op jit(solution)/shard_map/ppermute | solution.py:28
  44.0 1.1 %collective-permute-done.11 = bf16[128,512]{1,0:T(8,128)(2,1)S(1)} collective-permute-done((bf16[128,512]{1,0:T(8,128)(2,1)S(1)}, bf16[128,512]{1,0:T(8,128)(2,1)S(1)}, u32[]{:S(2)}, u32[]{:S(2)}) %collective-permute-start.11) | collective-permute-done | bytes 131104 | tf_op jit(solution)/shard_map/ppermute | solution.py:28
  45.1 3.1 %collective-permute-start.20 = (bf16[64,512]{1,0:T(8,128)(2,1)S(1)}, bf16[64,512]{1,0:T(8,128)(2,1)S(1)}, u32[]{:S(2)}, u32[]{:S(2)}) collective-permute-start(bf16[64,512]{1,0:T(8,128)(2,1)S(1)} %fusion.22), channel_id=1, source_target_pairs={{0,16},{2,18},{4,20},{6,22},{8,24},{10,26},{12,28},{14,30},{16,0},... | collective-permute-start | bytes 196616 | tf_op jit(solution)/shard_map/ppermute | solution.py:32
  48.2 0.6 %collective-permute-done.10 = bf16[128,512]{1,0:T(8,128)(2,1)S(1)} collective-permute-done((bf16[128,512]{1,0:T(8,128)(2,1)S(1)}, bf16[128,512]{1,0:T(8,128)(2,1)S(1)}, u32[]{:S(2)}, u32[]{:S(2)}) %collective-permute-start.10) | collective-permute-done | bytes 131104 | tf_op jit(solution)/shard_map/ppermute | solution.py:28
  48.8 1.2 %add_convert_fusion = (bf16[128,512]{1,0:T(8,128)(2,1)}, bf16[128,512]{1,0:T(8,128)(2,1)}) fusion(bf16[128,512]{1,0:T(8,128)(2,1)S(1)} %collective-permute-done.11, bf16[128,512]{1,0:T(8,128)(2,1)S(1)} %collective-permute-done.10, bf16[128,512]{1,0:T(8,128)(2,1)S(1)} %collective-permute-done.9, bf16[512,512]{1,0:T(8,128)(2,1)S(1)} %convolution_convert_fusion.1, ...), kind=kOutput, calls=%fused_computation.25 | convolution fusion | flops 68288512 | bytes 1703948 | tf_op jit(solution)/shard_map/dot_general | solution.py:55
  50.0 1.2 %collective-permute-done.20 = bf16[64,512]{1,0:T(8,128)(2,1)S(1)} collective-permute-done((bf16[64,512]{1,0:T(8,128)(2,1)S(1)}, bf16[64,512]{1,0:T(8,128)(2,1)S(1)}, u32[]{:S(2)}, u32[]{:S(2)}) %collective-permute-start.20) | collective-permute-done | bytes 65568 | tf_op jit(solution)/shard_map/ppermute | solution.py:32
  51.2 0.7 %fusion.18 = f32[64,512]{1,0:T(8,128)} fusion(bf16[64,512]{1,0:T(8,128)(2,1)S(1)} %collective-permute-done.20, f32[4,64,512]{2,1,0:T(8,128)S(1)} %bitcast.128, s32[]{:T(128)S(6)} %select_n.277, bf16[128,512]{1,0:T(8,128)(2,1)S(1)} %collective-permute-done.19), kind=kLoop, calls=%fused_computation.37 | loop fusion | flops 131072 | bytes 393220 | tf_op jit(solution)/shard_map/add | solution.py:45
  (54 shorter events, 3.8 us)
Async XLA Ops:
  0.6 11.7 %copy-start = (bf16[1024,1024]{1,0:T(8,128)(2,1)S(1)}, bf16[1024,1024]{1,0:T(8,128)(2,1)}, u32[]{:S(2)}) copy-start(bf16[1024,1024]{1,0:T(8,128)(2,1)} %param.8) | copy-start | bytes 6291460
  0.6 11.7 %copy-start.2 = (bf16[128,1024]{1,0:T(8,128)(2,1)S(1)}, bf16[128,1024]{1,0:T(8,128)(2,1)}, u32[]{:S(2)}) copy-start(bf16[128,1024]{1,0:T(8,128)(2,1)} %param.9) | copy-start | bytes 786436
  1.7 19.1 %collective-permute-start.2 = (bf16[128,512]{1,0:T(8,128)(2,1)S(1)}, bf16[128,512]{1,0:T(8,128)(2,1)S(1)}, u32[]{:S(2)}, u32[]{:S(2)}) collective-permute-start(bf16[128,512]{1,0:T(8,128)(2,1)S(1)} %dynamic-slice_maximum_fusion), channel_id=1, source_target_pairs={{0,24},{2,26},{4,28},{6,30},{8,16},{10,18},{12,20},{14,22},{16,8},... | collective-permute-start | bytes 393224 | tf_op jit(solution)/shard_map/ppermute | solution.py:32
  6.9 14.6 %collective-permute-start.1 = (bf16[128,512]{1,0:T(8,128)(2,1)S(1)}, bf16[128,512]{1,0:T(8,128)(2,1)S(1)}, u32[]{:S(2)}, u32[]{:S(2)}) collective-permute-start(bf16[128,512]{1,0:T(8,128)(2,1)S(1)} %dynamic-slice_maximum_fusion), channel_id=1, source_target_pairs={{0,16},{2,18},{4,20},{6,22},{8,24},{10,26},{12,28},{14,30},{16,0},... | collective-permute-start | bytes 393224 | tf_op jit(solution)/shard_map/ppermute | solution.py:32
  8.7 5.3 %collective-permute-start.5 = (bf16[2,128,128]{2,1,0:T(8,128)(2,1)S(1)}, bf16[2,128,128]{2,1,0:T(8,128)(2,1)S(1)}, u32[]{:S(2)}, u32[]{:S(2)}) collective-permute-start(bf16[2,128,128]{2,1,0:T(8,128)(2,1)S(1)} %get-tuple-element.31), channel_id=1, source_target_pairs={{0,6},{2,4},{4,2},{6,0},{8,14},{10,12},{12,10},{14,8},{16,22},{18,... | collective-permute-start | bytes 196616 | tf_op jit(solution)/shard_map/ppermute | solution.py:28
  11.2 4.3 %collective-permute-start.4 = (bf16[2,128,128]{2,1,0:T(8,128)(2,1)S(1)}, bf16[2,128,128]{2,1,0:T(8,128)(2,1)S(1)}, u32[]{:S(2)}, u32[]{:S(2)}) collective-permute-start(bf16[2,128,128]{2,1,0:T(8,128)(2,1)S(1)} %get-tuple-element.32), channel_id=1, source_target_pairs={{0,4},{2,6},{4,0},{6,2},{8,12},{10,14},{12,8},{14,10},{16,20},{18,... | collective-permute-start | bytes 196616 | tf_op jit(solution)/shard_map/ppermute | solution.py:28
  11.8 5.6 %collective-permute-start.3 = (bf16[2,128,128]{2,1,0:T(8,128)(2,1)S(1)}, bf16[2,128,128]{2,1,0:T(8,128)(2,1)S(1)}, u32[]{:S(2)}, u32[]{:S(2)}) collective-permute-start(bf16[2,128,128]{2,1,0:T(8,128)(2,1)S(1)} %get-tuple-element.33), channel_id=1, source_target_pairs={{0,2},{2,0},{4,6},{6,4},{8,10},{10,8},{12,14},{14,12},{16,18},{18,... | collective-permute-start | bytes 196616 | tf_op jit(solution)/shard_map/ppermute | solution.py:28
  14.1 7.4 %collective-permute-start = (bf16[128,512]{1,0:T(8,128)(2,1)S(1)}, bf16[128,512]{1,0:T(8,128)(2,1)S(1)}, u32[]{:S(2)}, u32[]{:S(2)}) collective-permute-start(bf16[128,512]{1,0:T(8,128)(2,1)S(1)} %dynamic-slice_maximum_fusion), channel_id=1, source_target_pairs={{0,8},{2,10},{4,12},{6,14},{8,0},{10,2},{12,4},{14,6},{16,24},{18,... | collective-permute-start | bytes 393224 | tf_op jit(solution)/shard_map/ppermute | solution.py:32
  15.5 9.1 %collective-permute-start.14 = (bf16[128,512]{1,0:T(8,128)(2,1)S(1)}, bf16[128,512]{1,0:T(8,128)(2,1)S(1)}, u32[]{:S(2)}, u32[]{:S(2)}) collective-permute-start(bf16[128,512]{1,0:T(8,128)(2,1)S(1)} %constant_dynamic-slice_fusion), channel_id=1, source_target_pairs={{0,6},{2,4},{4,2},{6,0},{8,14},{10,12},{12,10},{14,8},{16,22},{18,... | collective-permute-start | bytes 393224 | tf_op jit(solution)/shard_map/ppermute | solution.py:28
  17.3 8.6 %collective-permute-start.13 = (bf16[128,512]{1,0:T(8,128)(2,1)S(1)}, bf16[128,512]{1,0:T(8,128)(2,1)S(1)}, u32[]{:S(2)}, u32[]{:S(2)}) collective-permute-start(bf16[128,512]{1,0:T(8,128)(2,1)S(1)} %constant_dynamic-slice_fusion), channel_id=1, source_target_pairs={{0,4},{2,6},{4,0},{6,2},{8,12},{10,14},{12,8},{14,10},{16,20},{18,... | collective-permute-start | bytes 393224 | tf_op jit(solution)/shard_map/ppermute | solution.py:28
  20.9 6.1 %collective-permute-start.12 = (bf16[128,512]{1,0:T(8,128)(2,1)S(1)}, bf16[128,512]{1,0:T(8,128)(2,1)S(1)}, u32[]{:S(2)}, u32[]{:S(2)}) collective-permute-start(bf16[128,512]{1,0:T(8,128)(2,1)S(1)} %constant_dynamic-slice_fusion), channel_id=1, source_target_pairs={{0,2},{2,0},{4,6},{6,4},{8,10},{10,8},{12,14},{14,12},{16,18},{18,... | collective-permute-start | bytes 393224 | tf_op jit(solution)/shard_map/ppermute | solution.py:28
  22.1 9.3 %collective-permute-start.7 = (bf16[128,512]{1,0:T(8,128)(2,1)S(1)}, bf16[128,512]{1,0:T(8,128)(2,1)S(1)}, u32[]{:S(2)}, u32[]{:S(2)}) collective-permute-start(bf16[128,512]{1,0:T(8,128)(2,1)S(1)} %pad_maximum_fusion.3), channel_id=1, source_target_pairs={{0,4},{2,6},{4,0},{6,2},{8,12},{10,14},{12,8},{14,10},{16,20},{18,... | collective-permute-start | bytes 393224 | tf_op jit(solution)/shard_map/ppermute | solution.py:28
  23.7 8.0 %collective-permute-start.6 = (bf16[128,512]{1,0:T(8,128)(2,1)S(1)}, bf16[128,512]{1,0:T(8,128)(2,1)S(1)}, u32[]{:S(2)}, u32[]{:S(2)}) collective-permute-start(bf16[128,512]{1,0:T(8,128)(2,1)S(1)} %pad_maximum_fusion.2), channel_id=1, source_target_pairs={{0,2},{2,0},{4,6},{6,4},{8,10},{10,8},{12,14},{14,12},{16,18},{18,... | collective-permute-start | bytes 393224 | tf_op jit(solution)/shard_map/ppermute | solution.py:28
  24.7 7.7 %collective-permute-start.8 = (bf16[128,512]{1,0:T(8,128)(2,1)S(1)}, bf16[128,512]{1,0:T(8,128)(2,1)S(1)}, u32[]{:S(2)}, u32[]{:S(2)}) collective-permute-start(bf16[128,512]{1,0:T(8,128)(2,1)S(1)} %pad_maximum_fusion.4), channel_id=1, source_target_pairs={{0,6},{2,4},{4,2},{6,0},{8,14},{10,12},{12,10},{14,8},{16,22},{18,... | collective-permute-start | bytes 393224 | tf_op jit(solution)/shard_map/ppermute | solution.py:28
  27.5 10.2 %collective-permute-start.15 = (bf16[512,128]{1,0:T(8,128)(2,1)S(1)}, bf16[512,128]{1,0:T(8,128)(2,1)S(1)}, u32[]{:S(2)}, u32[]{:S(2)}) collective-permute-start(bf16[512,128]{1,0:T(8,128)(2,1)S(1)} %get-tuple-element.12), channel_id=1, source_target_pairs={{0,8},{2,10},{4,12},{6,14},{8,0},{10,2},{12,4},{14,6},{16,24},{18,... | collective-permute-start | bytes 393224 | tf_op jit(solution)/shard_map/ppermute | solution.py:32
  28.6 10.5 %collective-permute-start.17 = (bf16[512,128]{1,0:T(8,128)(2,1)S(1)}, bf16[512,128]{1,0:T(8,128)(2,1)S(1)}, u32[]{:S(2)}, u32[]{:S(2)}) collective-permute-start(bf16[512,128]{1,0:T(8,128)(2,1)S(1)} %get-tuple-element.13), channel_id=1, source_target_pairs={{0,24},{2,26},{4,28},{6,30},{8,16},{10,18},{12,20},{14,22},{16,8},... | collective-permute-start | bytes 393224 | tf_op jit(solution)/shard_map/ppermute | solution.py:32
  31.4 10.9 %collective-permute-start.16 = (bf16[512,128]{1,0:T(8,128)(2,1)S(1)}, bf16[512,128]{1,0:T(8,128)(2,1)S(1)}, u32[]{:S(2)}, u32[]{:S(2)}) collective-permute-start(bf16[512,128]{1,0:T(8,128)(2,1)S(1)} %get-tuple-element.14), channel_id=1, source_target_pairs={{0,16},{2,18},{4,20},{6,22},{8,24},{10,26},{12,28},{14,30},{16,0},... | collective-permute-start | bytes 393224 | tf_op jit(solution)/shard_map/ppermute | solution.py:32
  35.1 13.7 %copy-start.1 = (bf16[128,1024]{1,0:T(8,128)(2,1)S(1)}, bf16[128,1024]{1,0:T(8,128)(2,1)}, u32[]{:S(2)}) copy-start(bf16[128,1024]{1,0:T(8,128)(2,1)} %param.5) | copy-start | bytes 786436
  35.2 8.8 %collective-permute-start.19 = (bf16[128,512]{1,0:T(8,128)(2,1)S(1)}, bf16[128,512]{1,0:T(8,128)(2,1)S(1)}, u32[]{:S(2)}, u32[]{:S(2)}) collective-permute-start(bf16[128,512]{1,0:T(8,128)(2,1)S(1)} %pad_maximum_fusion.5), channel_id=1, source_target_pairs={{0,8},{2,10},{4,12},{6,14},{8,0},{10,2},{12,4},{14,6},{16,24},{18,... | collective-permute-start | bytes 393224 | tf_op jit(solution)/shard_map/ppermute | solution.py:32
  36.5 7.5 %collective-permute-start.9 = (bf16[128,512]{1,0:T(8,128)(2,1)S(1)}, bf16[128,512]{1,0:T(8,128)(2,1)S(1)}, u32[]{:S(2)}, u32[]{:S(2)}) collective-permute-start(bf16[128,512]{1,0:T(8,128)(2,1)S(1)} %get-tuple-element.5), channel_id=1, source_target_pairs={{0,2},{2,0},{4,6},{6,4},{8,10},{10,8},{12,14},{14,12},{16,18},{18,... | collective-permute-start | bytes 393224 | tf_op jit(solution)/shard_map/ppermute | solution.py:28
  37.7 7.4 %collective-permute-start.11 = (bf16[128,512]{1,0:T(8,128)(2,1)S(1)}, bf16[128,512]{1,0:T(8,128)(2,1)S(1)}, u32[]{:S(2)}, u32[]{:S(2)}) collective-permute-start(bf16[128,512]{1,0:T(8,128)(2,1)S(1)} %get-tuple-element.6), channel_id=1, source_target_pairs={{0,6},{2,4},{4,2},{6,0},{8,14},{10,12},{12,10},{14,8},{16,22},{18,... | collective-permute-start | bytes 393224 | tf_op jit(solution)/shard_map/ppermute | solution.py:28
  42.8 5.4 %collective-permute-start.18 = (bf16[128,512]{1,0:T(8,128)(2,1)S(1)}, bf16[128,512]{1,0:T(8,128)(2,1)S(1)}, u32[]{:S(2)}, u32[]{:S(2)}) collective-permute-start(bf16[128,512]{1,0:T(8,128)(2,1)S(1)} %convolution_convert_fusion.2), channel_id=1, source_target_pairs={{0,1},{1,0},{2,3},{3,2},{4,5},{5,4},{6,7},{7,6},{8,9},{9,8},{10,11... | collective-permute-start | bytes 393224 | tf_op jit(solution)/shard_map/ppermute | solution.py:52
  42.9 5.9 %collective-permute-start.10 = (bf16[128,512]{1,0:T(8,128)(2,1)S(1)}, bf16[128,512]{1,0:T(8,128)(2,1)S(1)}, u32[]{:S(2)}, u32[]{:S(2)}) collective-permute-start(bf16[128,512]{1,0:T(8,128)(2,1)S(1)} %get-tuple-element.7), channel_id=1, source_target_pairs={{0,4},{2,6},{4,0},{6,2},{8,12},{10,14},{12,8},{14,10},{16,20},{18,... | collective-permute-start | bytes 393224 | tf_op jit(solution)/shard_map/ppermute | solution.py:28
  45.1 6.0 %collective-permute-start.20 = (bf16[64,512]{1,0:T(8,128)(2,1)S(1)}, bf16[64,512]{1,0:T(8,128)(2,1)S(1)}, u32[]{:S(2)}, u32[]{:S(2)}) collective-permute-start(bf16[64,512]{1,0:T(8,128)(2,1)S(1)} %fusion.22), channel_id=1, source_target_pairs={{0,16},{2,18},{4,20},{6,22},{8,24},{10,26},{12,28},{14,30},{16,0},... | collective-permute-start | bytes 196616 | tf_op jit(solution)/shard_map/ppermute | solution.py:32
